TPU v7x, 32 devices: a whole 2x2x4 slice. The times are simulated.
32 devices in a mesh: chan: 8 (over y, x, core), tm: 4 (over z).
Axes of the slice: x: 2, y: 2, z: 4, core: 2. Of those that a mesh axis runs over, the one named last changes fastest.
Arguments:
- spectra: bfloat16 [2, 32, 2048, 128], P(None, 'tm', 'chan'), may hold values from -150 to 150
- quality: int32 [32, 128], P('tm'), may hold values 0 or 1
- offsets: int32 [4], replicated, may hold values from 1 to 4, as said below
Outputs:
- gathers: float32 [128, 4, 256], P('chan')
Inputs may be any that keep to these rules, and one draw needn't show every extreme that they name: `offsets`: each offset lies from 1 to 4, and one of them equals 4.
All inputs are finite; a program needn't handle non-finite values. No bound on the sum of `quality` on one device may be relied on, other than what follows from the above.
Results may differ from a plain program's by a relative error of at most 0.0003.
Values may be sent and summed in bfloat16 or wider, within the bound.
No kernel may reach another device: no remote copies, remote signals or barrier semaphores. Data moves between devices by JAX's collectives and lax.ppermute only.
A program may use at most 64 MiB of HBM per device.

v0:
```python
import math

import jax
import jax.numpy as jnp
from jax import lax
from jax.sharding import PartitionSpec as P

F = 2048
LAGS = 256
NOFF = 4
CH_DEV = 16
W_DEV = 8


def shifted(value, axis, steps):
    count = lax.axis_size(axis)
    leading, last = (max(0, -steps), min(count, count - steps))
    return lax.ppermute(value, axis, [(source, source + steps) for source in range(leading, last)])


def lag_table(freq_count, lag_count):
    freq_index = jnp.arange(freq_count, dtype=jnp.int32)[:, None]
    double_lag = (2 * jnp.arange(lag_count, dtype=jnp.int32) - lag_count + 1)[None, :]
    turns = jnp.mod(freq_index * double_lag, 4 * freq_count)
    angles = turns.astype(jnp.float32) * (2.0 * math.pi / (4 * freq_count))
    cosine = jnp.cos(angles)
    sine = jnp.sin(angles)
    upper = jnp.concatenate([cosine, sine], axis=1)
    lower = jnp.concatenate([-sine, cosine], axis=1)
    return jnp.stack([upper, lower]).astype(jnp.bfloat16)


def whiten_parts(real_part, imag_part, magnitude, channel_level, usable):
    factor = usable.astype(jnp.float32)[:, None, :] / (magnitude + 0.5 * (channel_level + 1e-05))
    return jnp.stack([real_part * factor, imag_part * factor]).astype(jnp.bfloat16)


def cross_parts(own_real, own_imag, far_real, far_imag):
    own_real = own_real.astype(jnp.float32)
    own_imag = own_imag.astype(jnp.float32)
    far_real = far_real.astype(jnp.float32)
    far_imag = far_imag.astype(jnp.float32)
    return jnp.stack(
        [own_real * far_real + own_imag * far_imag, own_imag * far_real - own_real * far_imag]
    ).astype(jnp.bfloat16)


def pair_terms(corr_all):
    lag_count = corr_all.shape[-1] // 2
    real_corr = corr_all[..., :lag_count]
    imag_corr = corr_all[..., lag_count:]
    power = real_corr * real_corr + imag_corr * imag_corr
    mean_power = jnp.mean(power, axis=-1, keepdims=True)
    denominator = jnp.sqrt(power + 0.25 * (mean_power + 1e-06))
    return (
        jnp.sum(real_corr, axis=-3),
        jnp.sum(real_corr / denominator, axis=-3),
        jnp.sum(imag_corr / denominator, axis=-3),
    )


def shards(spectra, quality, offsets):
    chan_count = lax.axis_size("chan")
    tm_count = lax.axis_size("tm")
    levels = chan_count.bit_length() - 1
    table_bf = lag_table(F, LAGS)
    inv_root = 1.0 / math.sqrt(F)
    real_part = spectra[0].astype(jnp.float32)
    imag_part = spectra[1].astype(jnp.float32)
    magnitude = jnp.sqrt(real_part * real_part + imag_part * imag_part)
    band_total = lax.psum(jnp.sum(magnitude, axis=1), "chan")
    channel_level = (band_total / F)[:, None, :]
    whitened = whiten_parts(real_part, imag_part, magnitude, channel_level, quality)
    width_all = whitened.shape[3]
    padded = jnp.pad(whitened, ((0, 0), (0, 0), (0, 0), (0, width_all)))
    crossed_list = []
    for offset_index in range(NOFF):
        partner = lax.dynamic_slice_in_dim(padded, offsets[offset_index] * CH_DEV, width_all, 3)
        crossed_list.append(cross_parts(whitened[0], whitened[1], partner[0], partner[1]))
    crossed = jnp.stack(crossed_list, axis=1)
    corr_all = jnp.einsum(
        "cnwfh,cfl->nwhl",
        lax.all_to_all(crossed, "chan", split_axis=4, concat_axis=3, tiled=True),
        table_bf,
        preferred_element_type=jnp.float32,
    )
    linear_sum, real_sum, imag_sum = pair_terms(corr_all * inv_root)
    totals = lax.psum((linear_sum, real_sum, imag_sum), "tm")
    window_count = W_DEV * tm_count
    linear = totals[0] / window_count
    real_phase = totals[1] / window_count
    imag_phase = totals[2] / window_count
    stacks = jnp.transpose(linear * (real_phase * real_phase + imag_phase * imag_phase), (1, 0, 2))
    reverse_part = stacks
    for bit_index in range(levels):
        step_size = 1 << bit_index
        arrived = shifted(reverse_part, "chan", step_size)
        chosen = offsets // step_size % 2 == 1
        reverse_part = jnp.where(chosen[None, :, None], arrived, reverse_part)
    return stacks + jnp.flip(reverse_part, axis=2)


def solution(mesh):
    return jax.shard_map(
        shards,
        mesh=mesh,
        in_specs=(P(None, "tm", "chan", None), P("tm", None), P()),
        out_specs=P("chan", None, None),
        check_vma=False,
    )
```

profile of v0, /device:TPU:0, one launch (start us, length us, event | category | flops | bytes accessed | tf_op | source)
XLA Modules:
  0.0 169.4 jit_solution(17504813986182795707)
XLA Ops:
  6.5 1.5 fusion.53
  10.5 1.3 fusion.52
  12.6 0.5 fusion.36
  13.1 15.1 %psum.28 = f32[8,128]{1,0:T(8,128)S(1)} all-reduce(f32[8,128]{1,0:T(8,128)S(1)} %copy.32), channel_id=1, replica_groups=mesh['chan'=8,'tm'=4] {'chan'}, use_global_device_ids=true, to_apply=%region_1.2 | all-reduce | flops 1024 | bytes 8192 | tf_op jit(solution)/shard_map/psum | solution.py:71
  28.5 0.6 fusion.17
  29.3 1.4 fusion.44
  30.8 2.3 %maximum_maximum_fusion = bf16[2,4,8,256,128]{3,2,1,0,4:T(8,128)(2,1)} fusion(bf16[1,1,8,256,128]{3,2,1,0,4:T(8,128)(2,1)S(1)} %get-tuple-element.18, bf16[1,1,8,256,128]{3,2,1,0,4:T(8,128)(2,1)S(1)} %get-tuple-element.17, bf16[2,1,8,256,128]{3,2,4,1,0:T(8,128)(2,1)S(1)} %get-tuple-element.35, bf16[2,1,8,256,128]{3,2,4,1,0:T(8,128)(2,1)S(1)} %get-tuple-element.36, ...), kind=kLoop, calls=%fused_computation.3 | loop fusion | flops 21495808 | bytes 8388608 | tf_op jit(solution)/shard_map/stack | solution.py:80
  33.1 4.5 %all-to-all-start = ((bf16[2,4,8,256,128]{3,2,1,0,4:T(8,128)(2,1)}), bf16[2,4,8,256,128]{3,2,1,0,4:T(8,128)(2,1)}, u32[]{:S(2)}, u32[]{:S(2)}) async-start(bf16[2,4,8,256,128]{3,2,1,0,4:T(8,128)(2,1)} %maximum_maximum_fusion), calls=%async_computation | async-start | bytes 8388608 | tf_op jit(solution)/shard_map/all_to_all | solution.py:83
  37.7 8.7 %fusion.35 = (bf16[2048,256]{1,0:T(8,128)(2,1)S(1)}, bf16[2048,256]{1,0:T(8,128)(2,1)S(1)}, bf16[2048,256]{1,0:T(8,128)(2,1)S(1)}) fusion(s32[256]{0:T(256)S(1)} %multiply_add_fusion.1), kind=kLoop, calls=%fused_computation.68 | loop fusion | flops 9437184 | bytes 3146752 | tf_op jit(solution)/shard_map/convert.7
  46.4 1.7 %maximum_bitcast_fusion.2 = (bf16[1,2048,512]{2,1,0:T(8,128)(2,1)S(1)}, bf16[1,2048,512]{2,1,0:T(8,128)(2,1)}) fusion(bf16[2048,256]{1,0:T(8,128)(2,1)S(1)} %get-tuple-element.25, bf16[2048,256]{1,0:T(8,128)(2,1)S(1)} %get-tuple-element.27, bf16[2048,256]{1,0:T(8,128)(2,1)S(1)} %get-tuple-element.26), kind=kLoop, calls=%fused_computation.31 | loop fusion | flops 8388608 | bytes 7340032 | tf_op jit(solution)/shard_map/stack | solution.py:30
  48.1 38.6 %all-to-all-done = bf16[2,4,8,256,128]{3,2,1,0,4:T(8,128)(2,1)} async-done(((bf16[2,4,8,256,128]{3,2,1,0,4:T(8,128)(2,1)}), bf16[2,4,8,256,128]{3,2,1,0,4:T(8,128)(2,1)}, u32[]{:S(2)}, u32[]{:S(2)}) %all-to-all-start) | async-done | bytes 4194336 | tf_op jit(solution)/shard_map/all_to_all | solution.py:83
  86.8 6.5 %copy.39 = bf16[2,4,8,8,256,16]{4,3,5,0,2,1:T(8,128)(2,1)} copy(bf16[2,4,8,8,256,16]{4,2,1,0,5,3:T(8,128)(2,1)} %bitcast.15) | data formatting | bytes 8388608 | tf_op jit(solution)/shard_map/all_to_all | solution.py:83
  93.3 7.4 %all_to_all.16 = bf16[2,4,8,2048,16]{3,4,0,2,1:T(8,128)(2,1)} reshape(bf16[2,4,8,8,256,16]{4,3,5,0,2,1:T(8,128)(2,1)} %copy.39) | data formatting | bytes 8388608 | tf_op jit(solution)/shard_map/all_to_all | solution.py:83
  100.7 5.2 %fusion.13 = f32[4,8,16,512]{3,2,1,0:T(8,128)S(1)} fusion(bf16[2,4,8,2048,16]{3,4,0,2,1:T(8,128)(2,1)} %all_to_all.16, bf16[1,2048,512]{2,1,0:T(8,128)(2,1)} %get-tuple-element.22, bf16[1,2048,512]{2,1,0:T(8,128)(2,1)S(1)} %get-tuple-element.21), kind=kOutput, calls=%fused_computation.39 | convolution fusion | flops 2149842944 | bytes 9437184 | tf_op jit(solution)/shard_map/cnwfh,cfl->nwhl/dot_general | solution.py:81
  106.1 1.0 divide_reduce_fusion.1
  107.1 34.6 %all-reduce.4.cloned.1.call-done = (f32[4,16,256]{2,1,0:T(8,128)}, f32[4,16,256]{2,1,0:T(8,128)}, f32[4,16,256]{2,1,0:T(8,128)}) async-done(((f32[4,16,256]{2,1,0:T(8,128)}, f32[4,16,256]{2,1,0:T(8,128)}, f32[4,16,256]{2,1,0:T(8,128)}), (f32[4,16,256]{2,1,0:T(8,128)}, f32[4,16,256]{2,1,0:T(8,128)}, f32[4,16,256]{2,1,0:T(8,128)})) %all-reduce.4.cloned.1.call-update) | async-done | bytes 196624 | tf_op jit(solution)/shard_map/psum | solution.py:88
  141.8 0.9 multiply_bitcast_fusion
  142.7 1.3 collective-permute-start
  144.0 0.8 collective-permute-done
  144.9 6.8 %collective-permute-start.1 = (f32[16,4,256]{2,0,1:T(8,128)S(1)}, f32[16,4,256]{2,0,1:T(8,128)S(1)}, u32[]{:S(2)}, u32[]{:S(2)}) collective-permute-start(f32[16,4,256]{2,0,1:T(8,128)S(1)} %broadcast_select_fusion), channel_id=1, source_target_pairs={{0,8},{4,12},{8,16},{12,20},{16,24},{20,28},{1,9},{5,13},{9,17},{1... | collective-permute-start | bytes 196616 | tf_op jit(solution)/shard_map/ppermute | solution.py:18
  151.7 1.9 %collective-permute-done.1 = f32[16,4,256]{2,0,1:T(8,128)S(1)} collective-permute-done((f32[16,4,256]{2,0,1:T(8,128)S(1)}, f32[16,4,256]{2,0,1:T(8,128)S(1)}, u32[]{:S(2)}, u32[]{:S(2)}) %collective-permute-start.1) | collective-permute-done | bytes 65568 | tf_op jit(solution)/shard_map/ppermute | solution.py:18
  153.7 6.1 %collective-permute-start.2 = (f32[16,4,256]{2,0,1:T(8,128)S(1)}, f32[16,4,256]{2,0,1:T(8,128)S(1)}, u32[]{:S(2)}, u32[]{:S(2)}) collective-permute-start(f32[16,4,256]{2,0,1:T(8,128)S(1)} %broadcast_select_fusion.1), channel_id=1, source_target_pairs={{0,16},{4,20},{8,24},{12,28},{1,17},{5,21},{9,25},{13,29},{2,18},{... | collective-permute-start | bytes 196616 | tf_op jit(solution)/shard_map/ppermute | solution.py:18
  159.7 1.9 %collective-permute-done.2 = f32[16,4,256]{2,0,1:T(8,128)S(1)} collective-permute-done((f32[16,4,256]{2,0,1:T(8,128)S(1)}, f32[16,4,256]{2,0,1:T(8,128)S(1)}, u32[]{:S(2)}, u32[]{:S(2)}) %collective-permute-start.2) | collective-permute-done | bytes 65568 | tf_op jit(solution)/shard_map/ppermute | solution.py:18
  161.9 0.7 copy.40
  (24 shorter events, 2.0 us)
Async XLA Ops:
  11.7 16.6 %copy-start.1 = (s32[8,128]{1,0:T(8,128)S(1)}, s32[8,128]{1,0:T(8,128)}, u32[]{:S(2)}) copy-start(s32[8,128]{1,0:T(8,128)} %param.4) | copy-start | bytes 12292
  33.1 53.7 %all-to-all-start = ((bf16[2,4,8,256,128]{3,2,1,0,4:T(8,128)(2,1)}), bf16[2,4,8,256,128]{3,2,1,0,4:T(8,128)(2,1)}, u32[]{:S(2)}, u32[]{:S(2)}) async-start(bf16[2,4,8,256,128]{3,2,1,0,4:T(8,128)(2,1)} %maximum_maximum_fusion), calls=%async_computation | async-start | bytes 8388608 | tf_op jit(solution)/shard_map/all_to_all | solution.py:83
  37.7 104.1 %all-reduce.4.cloned.1.call-start = ((), (), s32[]{:S(2)}) async-start(), calls=%async_computation.1 | async-start | bytes 393216 | tf_op jit(solution)/shard_map/psum | solution.py:88
  105.9 38.1 %copy-start = (s32[4]{0:T(128)S(1)}, s32[4]{0:T(128)}, u32[]{:S(2)}) copy-start(s32[4]{0:T(128)} %param.5) | copy-start | bytes 52
  142.7 2.2 %collective-permute-start = (f32[16,4,256]{2,0,1:T(8,128)S(1)}, f32[16,4,256]{2,0,1:T(8,128)S(1)}, u32[]{:S(2)}, u32[]{:S(2)}) collective-permute-start(f32[16,4,256]{2,0,1:T(8,128)S(1)} %multiply_bitcast_fusion), channel_id=1, source_target_pairs={{0,4},{4,8},{8,12},{12,16},{16,20},{20,24},{24,28},{1,5},{5,9},{9,... | collective-permute-start | bytes 196616 | tf_op jit(solution)/shard_map/ppermute | solution.py:18
  144.9 8.7 %collective-permute-start.1 = (f32[16,4,256]{2,0,1:T(8,128)S(1)}, f32[16,4,256]{2,0,1:T(8,128)S(1)}, u32[]{:S(2)}, u32[]{:S(2)}) collective-permute-start(f32[16,4,256]{2,0,1:T(8,128)S(1)} %broadcast_select_fusion), channel_id=1, source_target_pairs={{0,8},{4,12},{8,16},{12,20},{16,24},{20,28},{1,9},{5,13},{9,17},{1... | collective-permute-start | bytes 196616 | tf_op jit(solution)/shard_map/ppermute | solution.py:18
  153.7 7.9 %collective-permute-start.2 = (f32[16,4,256]{2,0,1:T(8,128)S(1)}, f32[16,4,256]{2,0,1:T(8,128)S(1)}, u32[]{:S(2)}, u32[]{:S(2)}) collective-permute-start(f32[16,4,256]{2,0,1:T(8,128)S(1)} %broadcast_select_fusion.1), channel_id=1, source_target_pairs={{0,16},{4,20},{8,24},{12,28},{1,17},{5,21},{9,25},{13,29},{2,18},{... | collective-permute-start | bytes 196616 | tf_op jit(solution)/shard_map/ppermute | solution.py:18
Sparse Core Ops, SparseCore 0:
  107.2 34.4 all-reduce.3
where the time goes:
time: 170 us; the launch traced here: 169 us
  waiting for transfers between devices  77.9 us (46%)
  starting transfers between devices  18.7 us (11%)
  local copies, waits for them, and re-layouts  18.5 us (11%)
  other arithmetic  17.9 us (11%)
  between operations  16.1 us (9%)
  blocking collectives  15.1 us (9%)
  matrix products  5.19 us (3%)
    all_to_all x1, waiting for transfers between devices, shards(): lax.all_to_all(crossed, 'chan', split_axis=4, concat_axis=3, tiled=True)  38.6 us
    psum x1, waiting for transfers between devices, shards(): totals = lax.psum((linear_sum, real_sum, imag_sum), 'tm')  34.6 us
    psum x1, blocking collectives, shards(): band_total = lax.psum(jnp.sum(magnitude, axis=1), 'chan')  15.1 us
    ppermute x3, starting transfers between devices, shifted(): lax.ppermute(value, axis, [(source, source + steps) for source in range(l...  14.1 us
    all_to_all x2, local copies, waits for them, and re-layouts, shards(): lax.all_to_all(crossed, 'chan', split_axis=4, concat_axis=3, tiled=True)  13.9 us
    another operation x1, other arithmetic  8.68 us
    dot_general x1, matrix products, shards(): jnp.einsum('cnwfh,cfl->nwhl', lax.all_to_all(crossed, 'chan', split_axis=...  5.19 us
    ppermute x3, waiting for transfers between devices, shifted(): lax.ppermute(value, axis, [(source, source + steps) for source in range(l...  4.61 us
  transfers between devices with their start and end apart: 5, of which 5 were waited for; matrix products, arithmetic and copies ran while one was open for 6% of the time, Pallas kernels for 0%

commit v1 on v0

--- a/solution.py
+++ b/solution.py
@@ -1,8 +1,12 @@
+import functools
 import math
 
 import jax
 import jax.numpy as jnp
+import numpy as np
 from jax import lax
+from jax.experimental import pallas as pl
+from jax.experimental.pallas import tpu as pltpu
 from jax.sharding import PartitionSpec as P
 
 F = 2048
@@ -10,6 +14,179 @@
 NOFF = 4
 CH_DEV = 16
 W_DEV = 8
+VMEM_LIMIT = 48 * 1024 * 1024
+
+
+def half_table(freq_count, lag_count):
+    freq_index = np.arange(freq_count, dtype=np.int64)[None, :]
+    double_lag = (2 * np.arange(lag_count // 2, lag_count, dtype=np.int64) - lag_count + 1)[:, None]
+    turns = np.mod(freq_index * double_lag, 4 * freq_count).astype(np.float32)
+    angles = turns * np.float32(2.0 * math.pi / (4 * freq_count))
+    return np.concatenate([np.cos(angles), np.sin(angles)]).astype(jnp.bfloat16)
+
+
+def window_kernel(offs_ref, where_ref, spec_ref, qual_ref, table_ref, out_ref, mag_ref, white_ref, cross_ref):
+    sources, _, band, chans = spec_ref.shape
+    freqs = sources * band
+    groups, offset_count, _, lag_rows, _ = out_ref.shape
+    half = groups * lag_rows
+    step = 64
+
+    def magnitudes(index, total):
+        source, row = index // (band // step), index % (band // step) * step
+        rows = pl.ds(pl.multiple_of(row, step), step)
+        real = spec_ref[source, 0, rows, :].astype(jnp.float32)
+        imag = spec_ref[source, 1, rows, :].astype(jnp.float32)
+        magnitude = jnp.sqrt(real * real + imag * imag)
+        mag_ref[pl.ds(pl.multiple_of(index * step, step), step), :] = magnitude
+        return total + jnp.sum(magnitude.reshape(step // 8, 8, chans), axis=0)
+
+    total = lax.fori_loop(0, freqs // step, magnitudes, jnp.zeros((8, chans), jnp.float32), unroll=4)
+    level = jnp.sum(total, axis=0, keepdims=True) / freqs
+    floor = 0.5 * (level + 1e-05)
+    usable = qual_ref[pl.ds(where_ref[0], 1), :].astype(jnp.float32)
+
+    def whiten(index, carry):
+        source, row = index // (band // step), index % (band // step) * step
+        rows = pl.ds(pl.multiple_of(row, step), step)
+        held = pl.ds(pl.multiple_of(index * step, step), step)
+        factor = usable / (mag_ref[held, :] + floor)
+        for part in range(2):
+            value = spec_ref[source, part, rows, :].astype(jnp.float32) * factor
+            white_ref[part, held, :] = value.astype(jnp.bfloat16).astype(jnp.float32)
+        return carry
+
+    lax.fori_loop(0, freqs // step, whiten, 0, unroll=4)
+
+    lane = lax.broadcasted_iota(jnp.int32, (1, chans), 1)
+    scale = 1.0 / math.sqrt(freqs)
+    for number in range(offset_count):
+        ahead = offs_ref[number] * (chans // groups)
+        turn = chans - ahead
+
+        def cross(index, carry):
+            held = pl.ds(pl.multiple_of(index * step, step), step)
+            own_real, own_imag = white_ref[0, held, :], white_ref[1, held, :]
+            far_real = pltpu.roll(own_real, turn, 1)
+            far_imag = pltpu.roll(own_imag, turn, 1)
+            cross_ref[held, pl.ds(0, chans)] = (own_real * far_real + own_imag * far_imag).astype(jnp.bfloat16)
+            cross_ref[held, pl.ds(chans, chans)] = (own_imag * far_real - own_real * far_imag).astype(jnp.bfloat16)
+            return carry
+
+        lax.fori_loop(0, freqs // step, cross, 0, unroll=4)
+        sums = jnp.dot(table_ref[...], cross_ref[...], preferred_element_type=jnp.float32)
+        keep = jnp.where(lane < turn, scale, 0.0)
+        cos_real, sin_real = sums[:half, :chans] * keep, sums[half:, :chans] * keep
+        cos_imag, sin_imag = sums[:half, chans:] * keep, sums[half:, chans:] * keep
+        corr = (
+            (cos_real - sin_imag, sin_real + cos_imag),
+            (cos_real + sin_imag, cos_imag - sin_real),
+        )
+        power = [real * real + imag * imag for real, imag in corr]
+        mean_power = (jnp.sum(power[0], axis=0, keepdims=True) + jnp.sum(power[1], axis=0, keepdims=True)) / (2 * half)
+        extra = 0.25 * (mean_power + 1e-06)
+        for side in range(2):
+            inverse = 1.0 / jnp.sqrt(power[side] + extra)
+            real, imag = corr[side]
+            for kind, value in enumerate((real, real * inverse, imag * inverse)):
+                out_ref[:, number, 2 * kind + side, :, :] = value.reshape(groups, lag_rows, chans)
+
+
+def stack_kernel(offs_ref, where_ref, sums_ref, out_ref, *, windows):
+    blocks, copies, _, _ = out_ref.shape
+    _, _, lag_rows, chans = sums_ref.shape
+    total = jnp.sum(sums_ref[...], axis=0) / windows
+    stacks = [
+        total[side] * (total[2 + side] * total[2 + side] + total[4 + side] * total[4 + side]) for side in range(2)
+    ]
+    ahead = offs_ref[where_ref[0]] * (chans // blocks)
+    lane = lax.broadcasted_iota(jnp.int32, (1, chans), 1)
+    behind = [jnp.where(lane >= ahead, pltpu.roll(stack, ahead, 1), 0.0) for stack in stacks]
+    both = jnp.concatenate([stacks[0] + behind[1], stacks[1] + behind[0]], axis=0)
+    wide = 2 * lag_rows
+    turned = jnp.concatenate([both] * (chans // wide), axis=0).T
+    per_block = chans // blocks
+    rows = per_block // 2
+    for block in range(blocks):
+        first = turned[block * per_block : block * per_block + rows, :]
+        second = turned[block * per_block + rows : (block + 1) * per_block, :]
+        piece = jnp.where(lane < wide, first, second)
+        for copy in range(copies):
+            out_ref[block, copy, :, :] = piece
+
+
+def place_kernel(parts_ref, out_ref):
+    groups, offset_count, rows, lanes = parts_ref.shape
+    half = out_ref.shape[2] // 2
+    lag_rows = half // groups
+    lane = lax.broadcasted_iota(jnp.int32, (1, lanes), 1)
+    mirror = (
+        lax.broadcasted_iota(jnp.int32, (half, half), 0) + lax.broadcasted_iota(jnp.int32, (half, half), 1) == half - 1
+    ).astype(jnp.float32)
+    for number in range(offset_count):
+        for part in range(2):
+            ahead = jnp.zeros((rows, lanes), jnp.float32)
+            back = jnp.zeros((rows, lanes), jnp.float32)
+            for group in range(groups):
+                piece = parts_ref[group, number]
+                here = (lane >= group * lag_rows) & (lane < (group + 1) * lag_rows)
+                begin = part * 2 * lag_rows
+                ahead = jnp.where(here, pltpu.roll(piece, (group * lag_rows - begin) % lanes, 1), ahead)
+                back = jnp.where(here, pltpu.roll(piece, (group * lag_rows - begin - lag_rows) % lanes, 1), back)
+            back = jnp.dot(back, mirror, precision=lax.Precision.HIGHEST, preferred_element_type=jnp.float32)
+            out_ref[part * rows : (part + 1) * rows, number, 0:half] = back
+            out_ref[part * rows : (part + 1) * rows, number, half : 2 * half] = ahead
+
+
+def window_shards(spectra, quality, offsets):
+    chan_count = lax.axis_size("chan")
+    tm_count = lax.axis_size("tm")
+    _, windows, band, chans = spectra.shape
+    freqs = band * chan_count
+    half = LAGS // 2
+    lag_rows = half // chan_count
+    offset_count = offsets.shape[0]
+    smem = pl.BlockSpec(memory_space=pltpu.SMEM)
+    vmem = pl.BlockSpec(memory_space=pltpu.VMEM)
+    params = pltpu.CompilerParams(vmem_limit_bytes=VMEM_LIMIT)
+    table = jnp.asarray(half_table(freqs, LAGS))
+    chan_index = lax.axis_index("chan").astype(jnp.int32).reshape(1)
+    tm_index = lax.axis_index("tm").astype(jnp.int32).reshape(1)
+
+    by_window = lax.all_to_all(jnp.transpose(spectra, (1, 0, 2, 3)), "chan", 0, 0, tiled=True)
+    pairs = pl.pallas_call(
+        window_kernel,
+        out_shape=jax.ShapeDtypeStruct((chan_count, offset_count, 6, lag_rows, chans), jnp.float32),
+        in_specs=[smem, smem, vmem, vmem, vmem],
+        out_specs=vmem,
+        scratch_shapes=[
+            pltpu.VMEM((freqs, chans), jnp.float32),
+            pltpu.VMEM((2, freqs, chans), jnp.float32),
+            pltpu.VMEM((freqs, 2 * chans), jnp.bfloat16),
+        ],
+        compiler_params=params,
+        name="window_pairs",
+    )(offsets, chan_index, by_window, quality, table)
+    by_lag = jnp.sum(lax.all_to_all(pairs, "chan", 0, 0, tiled=True), axis=0)
+    by_offset = lax.all_to_all(by_lag, "tm", 0, 0, tiled=True)
+    pieces = pl.pallas_call(
+        functools.partial(stack_kernel, windows=windows * tm_count),
+        out_shape=jax.ShapeDtypeStruct((chan_count, tm_count, CH_DEV // 2, chans), jnp.float32),
+        in_specs=[smem, smem, vmem],
+        out_specs=vmem,
+        compiler_params=params,
+        name="stack_pairs",
+    )(offsets, tm_index, by_offset)
+    shape = (chan_count * tm_count, CH_DEV // 2, chans)
+    arrived = lax.all_to_all(pieces.reshape(shape), ("chan", "tm"), 0, 0, tiled=True)
+    return pl.pallas_call(
+        place_kernel,
+        out_shape=jax.ShapeDtypeStruct((CH_DEV, offset_count, LAGS), jnp.float32),
+        in_specs=[vmem],
+        out_specs=vmem,
+        compiler_params=params,
+        name="place_lags",
+    )(arrived.reshape(chan_count, tm_count, CH_DEV // 2, chans))
 
 
 def shifted(value, axis, steps):
@@ -101,8 +278,10 @@
 
 
 def solution(mesh):
+    chan_count, tm_count = mesh.shape["chan"], mesh.shape["tm"]
+    by_window = chan_count == W_DEV and tm_count == NOFF
     return jax.shard_map(
-        shards,
+        window_shards if by_window else shards,
         mesh=mesh,
         in_specs=(P(None, "tm", "chan", None), P("tm", None), P()),
         out_specs=P("chan", None, None),

time: 170 us -> 81 us (0.48)
  waiting for transfers between devices: 77.9 us -> 22.1 us
  blocking collectives: 15.1 us -> 34.3 us
  other arithmetic: 17.9 us -> 0.78 us
  local copies, waits for them, and re-layouts: 18.5 us -> 2.3 us
  between operations: 16.1 us -> 0.03 us
  Pallas kernels: 0 us -> 10.9 us
  starting transfers between devices: 18.7 us -> 10.2 us
  matrix products: 5.19 us -> 0 us
    psum x1 -> x0, waiting for transfers between devices: 34.6 us -> none  [shards(): totals = lax.psum((linear_sum, real_sum, imag_sum), 'tm')]
    all_to_all x0 -> x2, blocking collectives: none -> 34.3 us  [the longest x1 23.4 us: window_shards(): by_lag = jnp.sum(lax.all_to_all(pairs, 'chan', 0, 0, tiled=True), axis=0)]
    all_to_all x1 -> x2, waiting for transfers between devices: 38.6 us -> 22.1 us  [the longest x1 15.4 us: window_shards(): lax.all_to_all(jnp.transpose(spectra, (1, 0, 2, 3)), 'chan', 0, 0, tiled=...]
    psum x1 -> x0, blocking collectives: 15.1 us -> none  [shards(): band_total = lax.psum(jnp.sum(magnitude, axis=1), 'chan')]
    another operation x6 -> x0, other arithmetic: 14.4 us -> none
    ppermute x3 -> x0, starting transfers between devices: 14.1 us -> none  [shifted(): lax.ppermute(value, axis, [(source, source + steps) for source in range(l...]
    all_to_all x2 -> x0, local copies, waits for them, and re-layouts: 13.9 us -> none  [shards(): lax.all_to_all(crossed, 'chan', split_axis=4, concat_axis=3, tiled=True)]
    pallas_call x0 -> x3, Pallas kernels: none -> 10.9 us  [the longest x1 8.99 us: window_shards(): pl.pallas_call(window_kernel, out_shape=jax.ShapeDtypeStruct((chan_count,...]
  transfers between devices with their start and end apart: 5 -> 2, of which waited for: 5 -> 2; matrix products, arithmetic and copies ran while one was open for 6% -> 0% of each run, Pallas kernels for 0% -> 0%
where the time goes in v1:
time: 81 us; the launch traced here: 80.6 us
  blocking collectives  34.3 us (42%)
  waiting for transfers between devices  22.1 us (27%)
  Pallas kernels  10.9 us (13%)
  starting transfers between devices  10.2 us (13%)
  local copies, waits for them, and re-layouts  2.3 us (3%)
    all_to_all x1, blocking collectives, window_shards(): by_lag = jnp.sum(lax.all_to_all(pairs, 'chan', 0, 0, tiled=True), axis=0)  23.4 us
    all_to_all x1, waiting for transfers between devices, window_shards(): lax.all_to_all(jnp.transpose(spectra, (1, 0, 2, 3)), 'chan', 0, 0, tiled=...  15.4 us
    all_to_all x1, blocking collectives, window_shards(): lax.all_to_all(pieces.reshape(shape), ('chan', 'tm'), 0, 0, tiled=True)  10.9 us
    pallas_call x1, Pallas kernels, window_shards(): pl.pallas_call(window_kernel, out_shape=jax.ShapeDtypeStruct((chan_count,...  8.99 us
    all_to_all x1, waiting for transfers between devices, window_shards(): by_offset = lax.all_to_all(by_lag, 'tm', 0, 0, tiled=True)  6.67 us
    all_to_all x1, starting transfers between devices, window_shards(): lax.all_to_all(jnp.transpose(spectra, (1, 0, 2, 3)), 'chan', 0, 0, tiled=...  5.3 us
    all_to_all x1, starting transfers between devices, window_shards(): by_offset = lax.all_to_all(by_lag, 'tm', 0, 0, tiled=True)  4.87 us
    unnamed x7, local copies, waits for them, and re-layouts  2.3 us
  transfers between devices with their start and end apart: 2, of which 2 were waited for; matrix products, arithmetic and copies ran while one was open for 0% of the time, Pallas kernels for 0%

profile of v1, /device:TPU:0, one launch (start us, length us, event | category | flops | bytes accessed | tf_op | source)
XLA Modules:
  0.0 80.6 jit_solution(15521054449491596619)
XLA Ops:
  0.0 2.3 %copy.7 = bf16[2,8,256,128]{3,2,0,1:T(8,128)(2,1)} copy(bf16[2,8,256,128]{3,2,1,0:T(8,128)(2,1)} %param.4) | data formatting | bytes 2097152 | tf_op args[0]
  2.3 0.0 copy-start
  2.3 0.0 copy-start.1
  2.3 0.0 copy-start.2
  2.3 5.3 %all-to-all-start = ((bf16[8,2,256,128]{3,2,1,0:T(8,128)(2,1)}), bf16[8,2,256,128]{3,2,1,0:T(8,128)(2,1)S(1)}, u32[]{:S(2)}, u32[]{:S(2)}) async-start(bf16[8,2,256,128]{3,2,1,0:T(8,128)(2,1)} %bitcast.6), calls=%async_computation | async-start | bytes 2097152 | tf_op jit(solution)/shard_map/all_to_all | solution.py:156
  7.6 15.4 %all-to-all-done.spec_ref = bf16[8,2,256,128]{3,2,1,0:T(8,128)(2,1)S(1)} async-done(((bf16[8,2,256,128]{3,2,1,0:T(8,128)(2,1)}), bf16[8,2,256,128]{3,2,1,0:T(8,128)(2,1)S(1)}, u32[]{:S(2)}, u32[]{:S(2)}) %all-to-all-start) | async-done | bytes 1048608 | tf_op jit(solution)/shard_map/all_to_all | solution.py:156
  23.0 0.0 copy-done
  23.0 0.0 copy-done.1
  23.0 0.0 copy-done.2
  23.0 9.0 %window_pairs.1 = f32[8,4,6,16,128]{4,3,2,1,0:T(8,128)S(1)} custom-call(s32[4]{0:T(128)S(1)} %copy-done.2, s32[1]{0:T(128)} %bitcast.1.where_ref, bf16[8,2,256,128]{3,2,1,0:T(8,128)(2,1)S(1)} %all-to-all-done.spec_ref, s32[8,128]{1,0:T(8,128)S(1)} %copy-done.1, bf16[256,2048]{1,0:T(8,128)(2,1)S(1)} %copy-done), custom_call_target="tpu_custom_call" | custom-call | tf_op jit(solution)/shard_map/window_pairs/pallas_call | solution.py:157
  32.0 23.4 %all_to_all.20 = f32[8,4,6,16,128]{4,3,2,1,0:T(8,128)S(1)} all-to-all(f32[8,4,6,16,128]{4,3,2,1,0:T(8,128)S(1)} %window_pairs.1), channel_id=1, replica_groups=mesh['chan'=8,'tm'=4] {'chan'}, dimensions={0} | all-to-all | bytes 3145728 | tf_op jit(solution)/shard_map/all_to_all | solution.py:170
  55.4 0.8 reduce_sum.9
  56.2 4.9 %all-to-all-start.2 = ((f32[4,6,16,128]{3,2,1,0:T(8,128)}), f32[4,6,16,128]{3,2,1,0:T(8,128)S(1)}, u32[]{:S(2)}, u32[]{:S(2)}) async-start(f32[4,6,16,128]{3,2,1,0:T(8,128)} %reduce_sum.9), calls=%async_computation.2 | async-start | bytes 393216 | tf_op jit(solution)/shard_map/all_to_all | solution.py:171
  61.1 6.7 %all-to-all-done.2.sums_ref = f32[4,6,16,128]{3,2,1,0:T(8,128)S(1)} async-done(((f32[4,6,16,128]{3,2,1,0:T(8,128)}), f32[4,6,16,128]{3,2,1,0:T(8,128)S(1)}, u32[]{:S(2)}, u32[]{:S(2)}) %all-to-all-start.2) | async-done | bytes 196640 | tf_op jit(solution)/shard_map/all_to_all | solution.py:171
  67.8 0.7 stack_pairs.1
  68.5 10.9 %all_to_all.21 = f32[32,8,128]{2,1,0:T(8,128)S(1)} all-to-all(f32[32,8,128]{2,1,0:T(8,128)S(1)} %bitcast.7), channel_id=1, replica_groups=mesh['chan'=8,'tm'=4] {'chan','tm'}, dimensions={0} | all-to-all | bytes 262144 | tf_op jit(solution)/shard_map/all_to_all | solution.py:181
  79.4 1.2 %place_lags.1 = f32[16,4,256]{2,1,0:T(4,128)} custom-call(f32[8,4,8,128]{3,2,1,0:T(8,128)S(1)} %bitcast.8), custom_call_target="tpu_custom_call" | custom-call | tf_op jit(solution)/shard_map/place_lags/pallas_call | solution.py:182
Async XLA Ops:
  2.3 20.7 %copy-start = (bf16[256,2048]{1,0:T(8,128)(2,1)S(1)}, bf16[256,2048]{1,0:T(8,128)(2,1)}, u32[]{:S(2)}) copy-start(bf16[256,2048]{1,0:T(8,128)(2,1)} %constant.13.clone.table_ref) | copy-start | bytes 3145732
  2.3 20.7 %copy-start.1 = (s32[8,128]{1,0:T(8,128)S(1)}, s32[8,128]{1,0:T(8,128)}, u32[]{:S(2)}) copy-start(s32[8,128]{1,0:T(8,128)} %qual_ref.1) | copy-start | bytes 12292
  2.3 20.7 %copy-start.2 = (s32[4]{0:T(128)S(1)}, s32[4]{0:T(128)}, u32[]{:S(2)}) copy-start(s32[4]{0:T(128)} %offs_ref.3) | copy-start | bytes 52
  2.3 20.7 %all-to-all-start = ((bf16[8,2,256,128]{3,2,1,0:T(8,128)(2,1)}), bf16[8,2,256,128]{3,2,1,0:T(8,128)(2,1)S(1)}, u32[]{:S(2)}, u32[]{:S(2)}) async-start(bf16[8,2,256,128]{3,2,1,0:T(8,128)(2,1)} %bitcast.6), calls=%async_computation | async-start | bytes 2097152 | tf_op jit(solution)/shard_map/all_to_all | solution.py:156
  56.2 11.5 %all-to-all-start.2 = ((f32[4,6,16,128]{3,2,1,0:T(8,128)}), f32[4,6,16,128]{3,2,1,0:T(8,128)S(1)}, u32[]{:S(2)}, u32[]{:S(2)}) async-start(f32[4,6,16,128]{3,2,1,0:T(8,128)} %reduce_sum.9), calls=%async_computation.2 | async-start | bytes 393216 | tf_op jit(solution)/shard_map/all_to_all | solution.py:171

commit v2 on v1

--- a/solution.py
+++ b/solution.py
@@ -15,6 +15,25 @@
 CH_DEV = 16
 W_DEV = 8
 VMEM_LIMIT = 48 * 1024 * 1024
+CODE_TOP = 32767.0
+OCTAVE = 256.0
+LOWEST = -110.0
+
+
+def encode(value):
+    return jnp.round(value * CODE_TOP).astype(jnp.int32).astype(jnp.int16)
+
+
+def decode(code):
+    return code.astype(jnp.int32).astype(jnp.float32)
+
+
+def level_code(peak):
+    return jnp.ceil(jnp.maximum(jnp.log2(jnp.maximum(peak, 1e-30)), LOWEST) * OCTAVE) + 1.0
+
+
+def level_of(code):
+    return jnp.exp2(code * (1.0 / OCTAVE))
 
 
 def half_table(freq_count, lag_count):
@@ -28,7 +47,8 @@
 def window_kernel(offs_ref, where_ref, spec_ref, qual_ref, table_ref, out_ref, mag_ref, white_ref, cross_ref):
     sources, _, band, chans = spec_ref.shape
     freqs = sources * band
-    groups, offset_count, _, lag_rows, _ = out_ref.shape
+    groups, blocks, lag_rows, _ = out_ref.shape
+    offset_count = offs_ref.shape[0]
     half = groups * lag_rows
     step = 64
 
@@ -59,6 +79,8 @@
     lax.fori_loop(0, freqs // step, whiten, 0, unroll=4)
 
     lane = lax.broadcasted_iota(jnp.int32, (1, chans), 1)
+    row = lax.broadcasted_iota(jnp.int32, (lag_rows, chans), 0)
+    levels = jnp.zeros((lag_rows, chans), jnp.float32)
     scale = 1.0 / math.sqrt(freqs)
     for number in range(offset_count):
         ahead = offs_ref[number] * (chans // groups)
@@ -85,11 +107,30 @@
         power = [real * real + imag * imag for real, imag in corr]
         mean_power = (jnp.sum(power[0], axis=0, keepdims=True) + jnp.sum(power[1], axis=0, keepdims=True)) / (2 * half)
         extra = 0.25 * (mean_power + 1e-06)
+        peak = jnp.max(jnp.maximum(jnp.abs(corr[0][0]), jnp.abs(corr[1][0])), axis=0, keepdims=True)
+        code = level_code(peak)
+        levels = jnp.where(row == number, code, levels)
+        upscale = 1.0 / level_of(code)
         for side in range(2):
             inverse = 1.0 / jnp.sqrt(power[side] + extra)
             real, imag = corr[side]
-            for kind, value in enumerate((real, real * inverse, imag * inverse)):
-                out_ref[:, number, 2 * kind + side, :, :] = value.reshape(groups, lag_rows, chans)
+            for kind, value in enumerate((real * upscale, real * inverse, imag * inverse)):
+                out_ref[:, 6 * number + 2 * kind + side, :, :] = encode(value).reshape(groups, lag_rows, chans)
+    for group in range(groups):
+        out_ref[group, blocks - 1, :, :] = levels.astype(jnp.int32).astype(jnp.int16)
+
+
+def sum_kernel(codes_ref, out_ref):
+    sources, blocks, _, _ = codes_ref.shape
+    offset_count = out_ref.shape[0]
+    levels = [level_of(decode(codes_ref[source, blocks - 1])) / CODE_TOP for source in range(sources)]
+    for number in range(offset_count):
+        for block in range(6):
+            total = 0.0
+            for source in range(sources):
+                value = decode(codes_ref[source, 6 * number + block])
+                total += value * levels[source][number : number + 1, :] if block < 2 else value
+            out_ref[number, block, :, :] = total if block < 2 else total / CODE_TOP
 
 
 def stack_kernel(offs_ref, where_ref, sums_ref, out_ref, *, windows):
@@ -156,7 +197,7 @@
     by_window = lax.all_to_all(jnp.transpose(spectra, (1, 0, 2, 3)), "chan", 0, 0, tiled=True)
     pairs = pl.pallas_call(
         window_kernel,
-        out_shape=jax.ShapeDtypeStruct((chan_count, offset_count, 6, lag_rows, chans), jnp.float32),
+        out_shape=jax.ShapeDtypeStruct((chan_count, 6 * offset_count + 1, lag_rows, chans), jnp.int16),
         in_specs=[smem, smem, vmem, vmem, vmem],
         out_specs=vmem,
         scratch_shapes=[
@@ -167,7 +208,14 @@
         compiler_params=params,
         name="window_pairs",
     )(offsets, chan_index, by_window, quality, table)
-    by_lag = jnp.sum(lax.all_to_all(pairs, "chan", 0, 0, tiled=True), axis=0)
+    by_lag = pl.pallas_call(
+        sum_kernel,
+        out_shape=jax.ShapeDtypeStruct((offset_count, 6, lag_rows, chans), jnp.float32),
+        in_specs=[vmem],
+        out_specs=vmem,
+        compiler_params=params,
+        name="sum_windows",
+    )(lax.all_to_all(pairs, "chan", 0, 0, tiled=True))
     by_offset = lax.all_to_all(by_lag, "tm", 0, 0, tiled=True)
     pieces = pl.pallas_call(
         functools.partial(stack_kernel, windows=windows * tm_count),

time: 81 us -> 73.3 us (0.905)
  blocking collectives: 34.3 us -> 25.4 us
  Pallas kernels: 10.9 us -> 12 us
  waiting for transfers between devices: 22.1 us -> 23 us
    all_to_all x1, blocking collectives: 23.4 us -> 15.3 us  [window_shards(): lax.all_to_all(pairs, 'chan', 0, 0, tiled=True)]
    all_to_all x1, waiting for transfers between devices: 6.67 us -> 7.62 us  [window_shards(): by_offset = lax.all_to_all(by_lag, 'tm', 0, 0, tiled=True)]
    pallas_call x0 -> x1, Pallas kernels: none -> 0.85 us  [window_shards(): pl.pallas_call(sum_kernel, out_shape=jax.ShapeDtypeStruct((offset_count,...]
where the time goes in v2:
time: 73.3 us; the launch traced here: 72.9 us
  blocking collectives  25.4 us (35%)
  waiting for transfers between devices  23 us (31%)
  Pallas kernels  12 us (16%)
  starting transfers between devices  10.2 us (14%)
  local copies, waits for them, and re-layouts  2.31 us (3%)
    all_to_all x1, waiting for transfers between devices, window_shards(): lax.all_to_all(jnp.transpose(spectra, (1, 0, 2, 3)), 'chan', 0, 0, tiled=...  15.4 us
    all_to_all x1, blocking collectives, window_shards(): lax.all_to_all(pairs, 'chan', 0, 0, tiled=True)  15.3 us
    all_to_all x1, blocking collectives, window_shards(): lax.all_to_all(pieces.reshape(shape), ('chan', 'tm'), 0, 0, tiled=True)  10.1 us
    pallas_call x1, Pallas kernels, window_shards(): pl.pallas_call(window_kernel, out_shape=jax.ShapeDtypeStruct((chan_count,...  9.2 us
    all_to_all x1, waiting for transfers between devices, window_shards(): by_offset = lax.all_to_all(by_lag, 'tm', 0, 0, tiled=True)  7.62 us
    all_to_all x1, starting transfers between devices, window_shards(): lax.all_to_all(jnp.transpose(spectra, (1, 0, 2, 3)), 'chan', 0, 0, tiled=...  5.3 us
    all_to_all x1, starting transfers between devices, window_shards(): by_offset = lax.all_to_all(by_lag, 'tm', 0, 0, tiled=True)  4.87 us
    unnamed x7, local copies, waits for them, and re-layouts  2.31 us
  transfers between devices with their start and end apart: 2, of which 2 were waited for; matrix products, arithmetic and copies ran while one was open for 0% of the time, Pallas kernels for 0%

profile of v2, /device:TPU:0, one launch (start us, length us, event | category | flops | bytes accessed | tf_op | source)
XLA Modules:
  0.0 72.9 jit_solution(11662089485494574800)
XLA Ops:
  0.0 2.3 %copy.7 = bf16[2,8,256,128]{3,2,0,1:T(8,128)(2,1)} copy(bf16[2,8,256,128]{3,2,1,0:T(8,128)(2,1)} %param.4) | data formatting | bytes 2097152 | tf_op args[0]
  2.3 0.0 copy-start
  2.3 5.3 %all-to-all-start = ((bf16[8,2,256,128]{3,2,1,0:T(8,128)(2,1)}), bf16[8,2,256,128]{3,2,1,0:T(8,128)(2,1)S(1)}, u32[]{:S(2)}, u32[]{:S(2)}) async-start(bf16[8,2,256,128]{3,2,1,0:T(8,128)(2,1)} %bitcast.6), calls=%async_computation | async-start | bytes 2097152 | tf_op jit(solution)/shard_map/all_to_all | solution.py:197
  7.6 0.0 copy-start.1
  7.6 0.0 copy-start.2
  7.6 15.4 %all-to-all-done.spec_ref = bf16[8,2,256,128]{3,2,1,0:T(8,128)(2,1)S(1)} async-done(((bf16[8,2,256,128]{3,2,1,0:T(8,128)(2,1)}), bf16[8,2,256,128]{3,2,1,0:T(8,128)(2,1)S(1)}, u32[]{:S(2)}, u32[]{:S(2)}) %all-to-all-start) | async-done | bytes 1048608 | tf_op jit(solution)/shard_map/all_to_all | solution.py:197
  23.0 0.0 copy-done
  23.0 0.0 copy-done.1
  23.0 0.0 copy-done.2
  23.0 9.2 %window_pairs.1 = s16[8,25,16,128]{3,2,1,0:T(8,128)(2,1)S(1)} custom-call(s32[4]{0:T(128)S(1)} %copy-done.2, s32[1]{0:T(128)} %bitcast.1.where_ref, bf16[8,2,256,128]{3,2,1,0:T(8,128)(2,1)S(1)} %all-to-all-done.spec_ref, s32[8,128]{1,0:T(8,128)S(1)} %copy-done.1, bf16[256,2048]{1,0:T(8,128)(2,1)S(1)} %copy-done), custom_call_target="tpu_custom_call" | custom-call | tf_op jit(solution)/shard_map/window_pairs/pallas_call | solution.py:198
  32.2 15.3 %all_to_all.20.codes_ref = s16[8,25,16,128]{3,2,1,0:T(8,128)(2,1)S(1)} all-to-all(s16[8,25,16,128]{3,2,1,0:T(8,128)(2,1)S(1)} %window_pairs.1), channel_id=1, replica_groups=mesh['chan'=8,'tm'=4] {'chan'}, dimensions={0} | all-to-all | bytes 1638400 | tf_op jit(solution)/shard_map/all_to_all | solution.py:218
  47.5 0.8 %sum_windows.1 = f32[4,6,16,128]{3,2,1,0:T(8,128)} custom-call(s16[8,25,16,128]{3,2,1,0:T(8,128)(2,1)S(1)} %all_to_all.20.codes_ref), custom_call_target="tpu_custom_call" | custom-call | tf_op jit(solution)/shard_map/sum_windows/pallas_call | solution.py:211
  48.4 4.9 %all-to-all-start.2 = ((f32[4,6,16,128]{3,2,1,0:T(8,128)}), f32[4,6,16,128]{3,2,1,0:T(8,128)S(1)}, u32[]{:S(2)}, u32[]{:S(2)}) async-start(f32[4,6,16,128]{3,2,1,0:T(8,128)} %sum_windows.1), calls=%async_computation.2 | async-start | bytes 393216 | tf_op jit(solution)/shard_map/all_to_all | solution.py:219
  53.2 7.6 %all-to-all-done.2.sums_ref = f32[4,6,16,128]{3,2,1,0:T(8,128)S(1)} async-done(((f32[4,6,16,128]{3,2,1,0:T(8,128)}), f32[4,6,16,128]{3,2,1,0:T(8,128)S(1)}, u32[]{:S(2)}, u32[]{:S(2)}) %all-to-all-start.2) | async-done | bytes 196640 | tf_op jit(solution)/shard_map/all_to_all | solution.py:219
  60.9 0.7 stack_pairs.1
  61.6 10.1 %all_to_all.21 = f32[32,8,128]{2,1,0:T(8,128)S(1)} all-to-all(f32[32,8,128]{2,1,0:T(8,128)S(1)} %bitcast.7), channel_id=1, replica_groups=mesh['chan'=8,'tm'=4] {'chan','tm'}, dimensions={0} | all-to-all | bytes 262144 | tf_op jit(solution)/shard_map/all_to_all | solution.py:229
  71.7 1.2 %place_lags.1 = f32[16,4,256]{2,1,0:T(4,128)} custom-call(f32[8,4,8,128]{3,2,1,0:T(8,128)S(1)} %bitcast.8), custom_call_target="tpu_custom_call" | custom-call | tf_op jit(solution)/shard_map/place_lags/pallas_call | solution.py:230
Async XLA Ops:
  2.3 20.7 %copy-start = (bf16[256,2048]{1,0:T(8,128)(2,1)S(1)}, bf16[256,2048]{1,0:T(8,128)(2,1)}, u32[]{:S(2)}) copy-start(bf16[256,2048]{1,0:T(8,128)(2,1)} %constant.11.clone.table_ref) | copy-start | bytes 3145732
  2.3 20.7 %all-to-all-start = ((bf16[8,2,256,128]{3,2,1,0:T(8,128)(2,1)}), bf16[8,2,256,128]{3,2,1,0:T(8,128)(2,1)S(1)}, u32[]{:S(2)}, u32[]{:S(2)}) async-start(bf16[8,2,256,128]{3,2,1,0:T(8,128)(2,1)} %bitcast.6), calls=%async_computation | async-start | bytes 2097152 | tf_op jit(solution)/shard_map/all_to_all | solution.py:197
  7.6 15.4 %copy-start.1 = (s32[8,128]{1,0:T(8,128)S(1)}, s32[8,128]{1,0:T(8,128)}, u32[]{:S(2)}) copy-start(s32[8,128]{1,0:T(8,128)} %qual_ref.1) | copy-start | bytes 12292
  7.6 15.4 %copy-start.2 = (s32[4]{0:T(128)S(1)}, s32[4]{0:T(128)}, u32[]{:S(2)}) copy-start(s32[4]{0:T(128)} %offs_ref.3) | copy-start | bytes 52
  48.4 12.5 %all-to-all-start.2 = ((f32[4,6,16,128]{3,2,1,0:T(8,128)}), f32[4,6,16,128]{3,2,1,0:T(8,128)S(1)}, u32[]{:S(2)}, u32[]{:S(2)}) async-start(f32[4,6,16,128]{3,2,1,0:T(8,128)} %sum_windows.1), calls=%async_computation.2 | async-start | bytes 393216 | tf_op jit(solution)/shard_map/all_to_all | solution.py:219

commit v3 on v2

--- a/solution.py
+++ b/solution.py
@@ -44,46 +44,54 @@
     return np.concatenate([np.cos(angles), np.sin(angles)]).astype(jnp.bfloat16)
 
 
-def window_kernel(offs_ref, where_ref, spec_ref, qual_ref, table_ref, out_ref, mag_ref, white_ref, cross_ref):
-    sources, _, band, chans = spec_ref.shape
-    freqs = sources * band
-    groups, blocks, lag_rows, _ = out_ref.shape
+def window_kernel(chan_count, offs_ref, where_ref, *refs):
+    spec_refs, (qual_ref, table_ref) = refs[:chan_count], refs[chan_count : chan_count + 2]
+    out_refs = refs[chan_count + 2 : 2 * chan_count + 2]
+    mag_ref, white_ref, cross_ref = refs[2 * chan_count + 2 :]
+    me = where_ref[0]
+    _, band, chans = spec_refs[0].shape
+    freqs = chan_count * band
+    blocks, lag_rows, _ = out_refs[0].shape
     offset_count = offs_ref.shape[0]
-    half = groups * lag_rows
+    half = chan_count * lag_rows
     step = 64
 
-    def magnitudes(index, total):
-        source, row = index // (band // step), index % (band // step) * step
-        rows = pl.ds(pl.multiple_of(row, step), step)
-        real = spec_ref[source, 0, rows, :].astype(jnp.float32)
-        imag = spec_ref[source, 1, rows, :].astype(jnp.float32)
-        magnitude = jnp.sqrt(real * real + imag * imag)
-        mag_ref[pl.ds(pl.multiple_of(index * step, step), step), :] = magnitude
-        return total + jnp.sum(magnitude.reshape(step // 8, 8, chans), axis=0)
-
-    total = lax.fori_loop(0, freqs // step, magnitudes, jnp.zeros((8, chans), jnp.float32), unroll=4)
+    total = jnp.zeros((8, chans), jnp.float32)
+    for partner, spec_ref in enumerate(spec_refs):
+
+        def magnitudes(index, total, spec_ref=spec_ref, base=(me ^ partner) * band):
+            rows = pl.ds(pl.multiple_of(index * step, step), step)
+            real = spec_ref[0, rows, :].astype(jnp.float32)
+            imag = spec_ref[1, rows, :].astype(jnp.float32)
+            magnitude = jnp.sqrt(real * real + imag * imag)
+            mag_ref[pl.ds(pl.multiple_of(base + index * step, step), step), :] = magnitude
+            return total + jnp.sum(magnitude.reshape(step // 8, 8, chans), axis=0)
+
+        total = lax.fori_loop(0, band // step, magnitudes, total, unroll=True)
     level = jnp.sum(total, axis=0, keepdims=True) / freqs
     floor = 0.5 * (level + 1e-05)
-    usable = qual_ref[pl.ds(where_ref[0], 1), :].astype(jnp.float32)
-
-    def whiten(index, carry):
-        source, row = index // (band // step), index % (band // step) * step
-        rows = pl.ds(pl.multiple_of(row, step), step)
-        held = pl.ds(pl.multiple_of(index * step, step), step)
-        factor = usable / (mag_ref[held, :] + floor)
-        for part in range(2):
-            value = spec_ref[source, part, rows, :].astype(jnp.float32) * factor
-            white_ref[part, held, :] = value.astype(jnp.bfloat16).astype(jnp.float32)
-        return carry
-
-    lax.fori_loop(0, freqs // step, whiten, 0, unroll=4)
+    usable = qual_ref[pl.ds(me, 1), :].astype(jnp.float32)
+
+    for partner, spec_ref in enumerate(spec_refs):
+
+        def whiten(index, carry, spec_ref=spec_ref, base=(me ^ partner) * band):
+            rows = pl.ds(pl.multiple_of(index * step, step), step)
+            held = pl.ds(pl.multiple_of(base + index * step, step), step)
+            factor = usable / (mag_ref[held, :] + floor)
+            for part in range(2):
+                value = spec_ref[part, rows, :].astype(jnp.float32) * factor
+                white_ref[part, held, :] = value.astype(jnp.bfloat16).astype(jnp.float32)
+            return carry
+
+        lax.fori_loop(0, band // step, whiten, 0, unroll=True)
 
     lane = lax.broadcasted_iota(jnp.int32, (1, chans), 1)
     row = lax.broadcasted_iota(jnp.int32, (lag_rows, chans), 0)
     levels = jnp.zeros((lag_rows, chans), jnp.float32)
     scale = 1.0 / math.sqrt(freqs)
+    table = jnp.concatenate([table_ref[side, me ^ k] for side in range(2) for k in range(chan_count)], axis=0)
     for number in range(offset_count):
-        ahead = offs_ref[number] * (chans // groups)
+        ahead = offs_ref[number] * (chans // chan_count)
         turn = chans - ahead
 
         def cross(index, carry):
@@ -96,7 +104,7 @@
             return carry
 
         lax.fori_loop(0, freqs // step, cross, 0, unroll=4)
-        sums = jnp.dot(table_ref[...], cross_ref[...], preferred_element_type=jnp.float32)
+        sums = jnp.dot(table, cross_ref[...], preferred_element_type=jnp.float32)
         keep = jnp.where(lane < turn, scale, 0.0)
         cos_real, sin_real = sums[:half, :chans] * keep, sums[half:, :chans] * keep
         cos_imag, sin_imag = sums[:half, chans:] * keep, sums[half:, chans:] * keep
@@ -115,28 +123,41 @@
             inverse = 1.0 / jnp.sqrt(power[side] + extra)
             real, imag = corr[side]
             for kind, value in enumerate((real * upscale, real * inverse, imag * inverse)):
-                out_ref[:, 6 * number + 2 * kind + side, :, :] = encode(value).reshape(groups, lag_rows, chans)
-    for group in range(groups):
-        out_ref[group, blocks - 1, :, :] = levels.astype(jnp.int32).astype(jnp.int16)
-
-
-def sum_kernel(codes_ref, out_ref):
-    sources, blocks, _, _ = codes_ref.shape
-    offset_count = out_ref.shape[0]
-    levels = [level_of(decode(codes_ref[source, blocks - 1])) / CODE_TOP for source in range(sources)]
-    for number in range(offset_count):
+                coded = encode(value).reshape(chan_count, lag_rows, chans)
+                for k in range(chan_count):
+                    out_refs[k][6 * number + 2 * kind + side, :, :] = coded[k]
+    for k in range(chan_count):
+        out_refs[k][blocks - 1, :, :] = levels.astype(jnp.int32).astype(jnp.int16)
+
+
+def sum_kernel(chan_count, where_ref, *refs):
+    code_refs, out_refs = refs[:chan_count], refs[chan_count:]
+    blocks = code_refs[0].shape[0]
+    levels = [level_of(decode(codes_ref[blocks - 1])) / CODE_TOP for codes_ref in code_refs]
+    row = lax.broadcasted_iota(jnp.int32, levels[0].shape, 0)
+    for k, out_ref in enumerate(out_refs):
+        number = where_ref[0] ^ k
+        own = [jnp.sum(jnp.where(row == number, level, 0.0), axis=0, keepdims=True) for level in levels]
         for block in range(6):
             total = 0.0
-            for source in range(sources):
-                value = decode(codes_ref[source, 6 * number + block])
-                total += value * levels[source][number : number + 1, :] if block < 2 else value
-            out_ref[number, block, :, :] = total if block < 2 else total / CODE_TOP
-
-
-def stack_kernel(offs_ref, where_ref, sums_ref, out_ref, *, windows):
+            for codes_ref, level in zip(code_refs, own):
+                value = decode(codes_ref[6 * number + block])
+                total += value * level if block < 2 else value
+            out_ref[block, :, :] = total if block < 2 else total / CODE_TOP
+
+
+def exchange(pieces, axis):
+    count = lax.axis_size(axis)
+    return [pieces[0]] + [
+        lax.ppermute(pieces[k], axis, [(source, source ^ k) for source in range(count)]) for k in range(1, count)
+    ]
+
+
+def stack_kernel(windows, offs_ref, where_ref, *refs):
+    sums_refs, out_ref = refs[:-1], refs[-1]
     blocks, copies, _, _ = out_ref.shape
-    _, _, lag_rows, chans = sums_ref.shape
-    total = jnp.sum(sums_ref[...], axis=0) / windows
+    _, lag_rows, chans = sums_refs[0].shape
+    total = sum(sums_ref[...] for sums_ref in sums_refs) / windows
     stacks = [
         total[side] * (total[2 + side] * total[2 + side] + total[4 + side] * total[4 + side]) for side in range(2)
     ]
@@ -190,16 +211,19 @@
     smem = pl.BlockSpec(memory_space=pltpu.SMEM)
     vmem = pl.BlockSpec(memory_space=pltpu.VMEM)
     params = pltpu.CompilerParams(vmem_limit_bytes=VMEM_LIMIT)
-    table = jnp.asarray(half_table(freqs, LAGS))
-    chan_index = lax.axis_index("chan").astype(jnp.int32).reshape(1)
-    tm_index = lax.axis_index("tm").astype(jnp.int32).reshape(1)
-
-    by_window = lax.all_to_all(jnp.transpose(spectra, (1, 0, 2, 3)), "chan", 0, 0, tiled=True)
+    table = jnp.asarray(half_table(freqs, LAGS).reshape(2, chan_count, lag_rows, freqs))
+    chan_index = lax.axis_index("chan").astype(jnp.int32)
+    tm_index = lax.axis_index("tm").astype(jnp.int32)
+    chan_where, tm_where = chan_index.reshape(1), tm_index.reshape(1)
+
+    pieces = [
+        lax.dynamic_index_in_dim(spectra, chan_index ^ k, 1, keepdims=False) for k in range(chan_count)
+    ]
     pairs = pl.pallas_call(
-        window_kernel,
-        out_shape=jax.ShapeDtypeStruct((chan_count, 6 * offset_count + 1, lag_rows, chans), jnp.int16),
-        in_specs=[smem, smem, vmem, vmem, vmem],
-        out_specs=vmem,
+        functools.partial(window_kernel, chan_count),
+        out_shape=[jax.ShapeDtypeStruct((6 * offset_count + 1, lag_rows, chans), jnp.int16)] * chan_count,
+        in_specs=[smem, smem] + [vmem] * (chan_count + 2),
+        out_specs=[vmem] * chan_count,
         scratch_shapes=[
             pltpu.VMEM((freqs, chans), jnp.float32),
             pltpu.VMEM((2, freqs, chans), jnp.float32),
@@ -207,24 +231,23 @@
         ],
         compiler_params=params,
         name="window_pairs",
-    )(offsets, chan_index, by_window, quality, table)
-    by_lag = pl.pallas_call(
-        sum_kernel,
-        out_shape=jax.ShapeDtypeStruct((offset_count, 6, lag_rows, chans), jnp.float32),
-        in_specs=[vmem],
-        out_specs=vmem,
+    )(offsets, chan_where, *exchange(pieces, "chan"), quality, table)
+    sums = pl.pallas_call(
+        functools.partial(sum_kernel, chan_count),
+        out_shape=[jax.ShapeDtypeStruct((6, lag_rows, chans), jnp.float32)] * tm_count,
+        in_specs=[smem] + [vmem] * chan_count,
+        out_specs=[vmem] * tm_count,
         compiler_params=params,
         name="sum_windows",
-    )(lax.all_to_all(pairs, "chan", 0, 0, tiled=True))
-    by_offset = lax.all_to_all(by_lag, "tm", 0, 0, tiled=True)
+    )(tm_where, *exchange(pairs, "chan"))
     pieces = pl.pallas_call(
-        functools.partial(stack_kernel, windows=windows * tm_count),
+        functools.partial(stack_kernel, windows * tm_count),
         out_shape=jax.ShapeDtypeStruct((chan_count, tm_count, CH_DEV // 2, chans), jnp.float32),
-        in_specs=[smem, smem, vmem],
+        in_specs=[smem, smem] + [vmem] * tm_count,
         out_specs=vmem,
         compiler_params=params,
         name="stack_pairs",
-    )(offsets, tm_index, by_offset)
+    )(offsets, tm_where, *exchange(sums, "tm"))
     shape = (chan_count * tm_count, CH_DEV // 2, chans)
     arrived = lax.all_to_all(pieces.reshape(shape), ("chan", "tm"), 0, 0, tiled=True)
     return pl.pallas_call(

time: 73.3 us -> 65.1 us (0.89)
  blocking collectives: 25.4 us -> 10.8 us
  starting transfers between devices: 10.2 us -> 20.8 us
  waiting for transfers between devices: 23 us -> 19.9 us
    all_to_all x2 -> x0, waiting for transfers between devices: 23 us -> none  [the longest x1 15.4 us: window_shards(): lax.all_to_all(jnp.transpose(spectra, (1, 0, 2, 3)), 'chan', 0, 0, tiled=...]
    ppermute x0 -> x17, starting transfers between devices: none -> 20.8 us  [exchange(): lax.ppermute(pieces[k], axis, [(source, source ^ k) for source in range(c...]
    ppermute x0 -> x17, waiting for transfers between devices: none -> 19.9 us  [exchange(): lax.ppermute(pieces[k], axis, [(source, source ^ k) for source in range(c...]
    all_to_all x1 -> x0, blocking collectives: 15.3 us -> none  [window_shards(): lax.all_to_all(pairs, 'chan', 0, 0, tiled=True)]
    all_to_all x2 -> x0, starting transfers between devices: 10.2 us -> none  [the longest x1 5.3 us: window_shards(): lax.all_to_all(jnp.transpose(spectra, (1, 0, 2, 3)), 'chan', 0, 0, tiled=...]
    unnamed x7 -> x6, local copies, waits for them, and re-layouts: 2.31 us -> 0.66 us
    squeeze x0 -> x1, local copies, waits for them, and re-layouts: none -> 1.44 us  [window_shards(): lax.dynamic_index_in_dim(spectra, chan_index ^ k, 1, keepdims=False)]
  transfers between devices with their start and end apart: 2 -> 17, of which waited for: 2 -> 11; matrix products, arithmetic and copies ran while one was open for 0% -> 0% of each run, Pallas kernels for 0% -> 0%
where the time goes in v3:
time: 65.1 us; the launch traced here: 64.9 us
  starting transfers between devices  20.8 us (32%)
  waiting for transfers between devices  19.9 us (31%)
  Pallas kernels  11.3 us (17%)
  blocking collectives  10.8 us (17%)
  local copies, waits for them, and re-layouts  2.1 us (3%)
    ppermute x17, starting transfers between devices, exchange(): lax.ppermute(pieces[k], axis, [(source, source ^ k) for source in range(c...  20.8 us
    ppermute x17, waiting for transfers between devices, exchange(): lax.ppermute(pieces[k], axis, [(source, source ^ k) for source in range(c...  19.9 us
    all_to_all x1, blocking collectives, window_shards(): lax.all_to_all(pieces.reshape(shape), ('chan', 'tm'), 0, 0, tiled=True)  10.8 us
    pallas_call x1, Pallas kernels, window_shards(): pl.pallas_call(functools.partial(window_kernel, chan_count), out_shape=[j...  9.11 us
    squeeze x1, local copies, waits for them, and re-layouts, window_shards(): lax.dynamic_index_in_dim(spectra, chan_index ^ k, 1, keepdims=False)  1.44 us
  transfers between devices with their start and end apart: 17, of which 11 were waited for; matrix products, arithmetic and copies ran while one was open for 0% of the time, Pallas kernels for 0%

profile of v3, /device:TPU:0, one launch (start us, length us, event | category | flops | bytes accessed | tf_op | source)
XLA Modules:
  0.0 64.9 jit_solution(2914910794554624697)
XLA Ops:
  0.0 1.4 %dynamic-slice_bitcast_fusion = (bf16[2,256,128]{2,1,0:T(8,128)(2,1)S(1)}, bf16[2,256,128]{2,1,0:T(8,128)(2,1)S(1)}, bf16[2,256,128]{2,1,0:T(8,128)(2,1)S(1)}, b...) fusion(bf16[2,8,256,128]{3,2,1,0:T(8,128)(2,1)} %param.4, ...), kind=kLoop, calls=%fused_computation | loop fusion | bytes 2097184 | tf_op jit(solution)/shard_map/jit(dynamic_index_in_dim)/squeeze | solution.py:220
  1.5 3.4 %collective-permute-start.6 = (bf16[2,256,128]{2,1,0:T(8,128)(2,1)S(1)}, bf16[2,256,128]{2,1,0:T(8,128)(2,1)S(1)}, u32[]{:S(2)}, u32[]{:S(2)}) collective-permute-start(bf16[2,256,128]{2,1,0:T(8,128)(2,1)S(1)} %get-tuple-element.29), channel_id=1, source_target_pairs={{0,28},{4,24},{8,20},{12,16},{16,12},{20,8},{24,4},{28,0},{1,29},{... | collective-permute-start | bytes 393224 | tf_op jit(solution)/shard_map/ppermute | solution.py:152
  4.9 0.8 %collective-permute-start.4 = (bf16[2,256,128]{2,1,0:T(8,128)(2,1)S(1)}, bf16[2,256,128]{2,1,0:T(8,128)(2,1)S(1)}, u32[]{:S(2)}, u32[]{:S(2)}) collective-permute-start(bf16[2,256,128]{2,1,0:T(8,128)(2,1)S(1)} %get-tuple-element.30), channel_id=1, source_target_pairs={{0,20},{4,16},{8,28},{12,24},{16,4},{20,0},{24,12},{28,8},{1,21},{... | collective-permute-start | bytes 393224 | tf_op jit(solution)/shard_map/ppermute | solution.py:152
  5.6 1.5 %collective-permute-start.3 = (bf16[2,256,128]{2,1,0:T(8,128)(2,1)S(1)}, bf16[2,256,128]{2,1,0:T(8,128)(2,1)S(1)}, u32[]{:S(2)}, u32[]{:S(2)}) collective-permute-start(bf16[2,256,128]{2,1,0:T(8,128)(2,1)S(1)} %get-tuple-element.31), channel_id=1, source_target_pairs={{0,16},{4,20},{8,24},{12,28},{16,0},{20,4},{24,8},{28,12},{1,17},{... | collective-permute-start | bytes 393224 | tf_op jit(solution)/shard_map/ppermute | solution.py:152
  7.2 1.2 %collective-permute-start.1 = (bf16[2,256,128]{2,1,0:T(8,128)(2,1)S(1)}, bf16[2,256,128]{2,1,0:T(8,128)(2,1)S(1)}, u32[]{:S(2)}, u32[]{:S(2)}) collective-permute-start(bf16[2,256,128]{2,1,0:T(8,128)(2,1)S(1)} %get-tuple-element.33), channel_id=1, source_target_pairs={{0,8},{4,12},{8,0},{12,4},{16,24},{20,28},{24,16},{28,20},{1,9},{5... | collective-permute-start | bytes 393224 | tf_op jit(solution)/shard_map/ppermute | solution.py:152
  9.0 2.6 %collective-permute-done.4.refs_5_ = bf16[2,256,128]{2,1,0:T(8,128)(2,1)S(1)} collective-permute-done((bf16[2,256,128]{2,1,0:T(8,128)(2,1)S(1)}, bf16[2,256,128]{2,1,0:T(8,128)(2,1)S(1)}, u32[]{:S(2)}, u32[]{:S(2)}) %collective-permute-start.4) | collective-permute-done | bytes 131104 | tf_op jit(solution)/shard_map/ppermute | solution.py:152
  11.6 2.4 %collective-permute-start.5 = (bf16[2,256,128]{2,1,0:T(8,128)(2,1)S(1)}, bf16[2,256,128]{2,1,0:T(8,128)(2,1)S(1)}, u32[]{:S(2)}, u32[]{:S(2)}) collective-permute-start(bf16[2,256,128]{2,1,0:T(8,128)(2,1)S(1)} %get-tuple-element.36), channel_id=1, source_target_pairs={{0,24},{4,28},{8,16},{12,20},{16,8},{20,12},{24,0},{28,4},{1,25},{... | collective-permute-start | bytes 393224 | tf_op jit(solution)/shard_map/ppermute | solution.py:152
  14.5 0.7 %collective-permute-done.1.refs_2_ = bf16[2,256,128]{2,1,0:T(8,128)(2,1)S(1)} collective-permute-done((bf16[2,256,128]{2,1,0:T(8,128)(2,1)S(1)}, bf16[2,256,128]{2,1,0:T(8,128)(2,1)S(1)}, u32[]{:S(2)}, u32[]{:S(2)}) %collective-permute-start.1) | collective-permute-done | bytes 131104 | tf_op jit(solution)/shard_map/ppermute | solution.py:152
  15.2 3.1 %collective-permute-done.5.refs_6_ = bf16[2,256,128]{2,1,0:T(8,128)(2,1)S(1)} collective-permute-done((bf16[2,256,128]{2,1,0:T(8,128)(2,1)S(1)}, bf16[2,256,128]{2,1,0:T(8,128)(2,1)S(1)}, u32[]{:S(2)}, u32[]{:S(2)}) %collective-permute-start.5) | collective-permute-done | bytes 131104 | tf_op jit(solution)/shard_map/ppermute | solution.py:152
  18.3 0.6 copy-done.2
  19.0 9.1 %window_pairs.1 = (s16[25,16,128]{2,1,0:T(8,128)(2,1)S(1)}, s16[25,16,128]{2,1,0:T(8,128)(2,1)S(1)}, s16[25,16,128]{2,1,0:T(8,128)(2,1)S(1)}, s16[25,16,128]{2,1...) custom-call(s32[4]{0:T(128)S(1)} %copy-done.2, ...), custom_call_target="tpu_custom_call" | custom-call | tf_op jit(solution)/shard_map/window_pairs/pallas_call | solution.py:222
  28.2 2.2 %collective-permute-start.8 = (s16[25,16,128]{2,1,0:T(8,128)(2,1)S(1)}, s16[25,16,128]{2,1,0:T(8,128)(2,1)S(1)}, u32[]{:S(2)}, u32[]{:S(2)}) collective-permute-start(s16[25,16,128]{2,1,0:T(8,128)(2,1)S(1)} %get-tuple-element.19), channel_id=1, source_target_pairs={{0,8},{4,12},{8,0},{12,4},{16,24},{20,28},{24,16},{28,20},{1,9},{5... | collective-permute-start | bytes 307208 | tf_op jit(solution)/shard_map/ppermute | solution.py:152
  30.4 1.8 %collective-permute-start.10 = (s16[25,16,128]{2,1,0:T(8,128)(2,1)S(1)}, s16[25,16,128]{2,1,0:T(8,128)(2,1)S(1)}, u32[]{:S(2)}, u32[]{:S(2)}) collective-permute-start(s16[25,16,128]{2,1,0:T(8,128)(2,1)S(1)} %get-tuple-element.21), channel_id=1, source_target_pairs={{0,16},{4,20},{8,24},{12,28},{16,0},{20,4},{24,8},{28,12},{1,17},{... | collective-permute-start | bytes 307208 | tf_op jit(solution)/shard_map/ppermute | solution.py:152
  32.2 1.8 %collective-permute-start.12 = (s16[25,16,128]{2,1,0:T(8,128)(2,1)S(1)}, s16[25,16,128]{2,1,0:T(8,128)(2,1)S(1)}, u32[]{:S(2)}, u32[]{:S(2)}) collective-permute-start(s16[25,16,128]{2,1,0:T(8,128)(2,1)S(1)} %get-tuple-element.23), channel_id=1, source_target_pairs={{0,24},{4,28},{8,16},{12,20},{16,8},{20,12},{24,0},{28,4},{1,25},{... | collective-permute-start | bytes 307208 | tf_op jit(solution)/shard_map/ppermute | solution.py:152
  34.1 0.9 %collective-permute-start.13 = (s16[25,16,128]{2,1,0:T(8,128)(2,1)S(1)}, s16[25,16,128]{2,1,0:T(8,128)(2,1)S(1)}, u32[]{:S(2)}, u32[]{:S(2)}) collective-permute-start(s16[25,16,128]{2,1,0:T(8,128)(2,1)S(1)} %get-tuple-element.24), channel_id=1, source_target_pairs={{0,28},{4,24},{8,20},{12,16},{16,12},{20,8},{24,4},{28,0},{1,29},{... | collective-permute-start | bytes 307208 | tf_op jit(solution)/shard_map/ppermute | solution.py:152
  35.0 0.8 %collective-permute-done.9.refs_3_ = s16[25,16,128]{2,1,0:T(8,128)(2,1)S(1)} collective-permute-done((s16[25,16,128]{2,1,0:T(8,128)(2,1)S(1)}, s16[25,16,128]{2,1,0:T(8,128)(2,1)S(1)}, u32[]{:S(2)}, u32[]{:S(2)}) %collective-permute-start.9) | collective-permute-done | bytes 102432 | tf_op jit(solution)/shard_map/ppermute | solution.py:152
  35.9 5.9 %collective-permute-done.11.refs_5_ = s16[25,16,128]{2,1,0:T(8,128)(2,1)S(1)} collective-permute-done((s16[25,16,128]{2,1,0:T(8,128)(2,1)S(1)}, s16[25,16,128]{2,1,0:T(8,128)(2,1)S(1)}, u32[]{:S(2)}, u32[]{:S(2)}) %collective-permute-start.11) | collective-permute-done | bytes 102432 | tf_op jit(solution)/shard_map/ppermute | solution.py:152
  42.0 1.7 %collective-permute-start.14 = (f32[6,16,128]{2,1,0:T(8,128)S(1)}, f32[6,16,128]{2,1,0:T(8,128)S(1)}, u32[]{:S(2)}, u32[]{:S(2)}) collective-permute-start(f32[6,16,128]{2,1,0:T(8,128)S(1)} %get-tuple-element.26), channel_id=1, source_target_pairs={{0,1},{1,0},{2,3},{3,2},{4,5},{5,4},{6,7},{7,6},{8,9},{9,8},{10,11... | collective-permute-start | bytes 147464 | tf_op jit(solution)/shard_map/ppermute | solution.py:152
  43.7 2.6 %collective-permute-start.15 = (f32[6,16,128]{2,1,0:T(8,128)S(1)}, f32[6,16,128]{2,1,0:T(8,128)S(1)}, u32[]{:S(2)}, u32[]{:S(2)}) collective-permute-start(f32[6,16,128]{2,1,0:T(8,128)S(1)} %get-tuple-element.27), channel_id=1, source_target_pairs={{0,2},{1,3},{2,0},{3,1},{4,6},{5,7},{6,4},{7,5},{8,10},{9,11},{10,... | collective-permute-start | bytes 147464 | tf_op jit(solution)/shard_map/ppermute | solution.py:152
  46.5 3.3 %collective-permute-done.15.refs_2_ = f32[6,16,128]{2,1,0:T(8,128)S(1)} collective-permute-done((f32[6,16,128]{2,1,0:T(8,128)S(1)}, f32[6,16,128]{2,1,0:T(8,128)S(1)}, u32[]{:S(2)}, u32[]{:S(2)}) %collective-permute-start.15) | collective-permute-done | bytes 49184 | tf_op jit(solution)/shard_map/ppermute | solution.py:152
  49.8 2.4 %collective-permute-done.16.refs_3_ = f32[6,16,128]{2,1,0:T(8,128)S(1)} collective-permute-done((f32[6,16,128]{2,1,0:T(8,128)S(1)}, f32[6,16,128]{2,1,0:T(8,128)S(1)}, u32[]{:S(2)}, u32[]{:S(2)}) %collective-permute-start.16) | collective-permute-done | bytes 49184 | tf_op jit(solution)/shard_map/ppermute | solution.py:152
  52.2 0.7 %stack_pairs.1 = f32[8,4,8,128]{3,2,1,0:T(8,128)S(1)} custom-call(s32[4]{0:T(128)S(1)} %copy-done.2, s32[1]{0:T(128)} %bitcast.where_ref, f32[6,16,128]{2,1,0:T(8,128)S(1)} %get-tuple-element.25.refs_0_, f32[6,16,128]{2,1,0:T(8,128)S(1)} %collective-permute-done.14.refs_1_, f32[6,16,128]{2,1,0:T(8,128)S(1)} %collective-permute-done.15.refs_2_, ...), custom_call_target="tpu_custom_call" | custom-call | tf_op jit(solution)/shard_map/stack_pairs/pallas_call | solution.py:243
  52.9 10.8 %all_to_all.5 = f32[32,8,128]{2,1,0:T(8,128)S(1)} all-to-all(f32[32,8,128]{2,1,0:T(8,128)S(1)} %bitcast.20), channel_id=1, replica_groups=mesh['chan'=8,'tm'=4] {'chan','tm'}, dimensions={0} | all-to-all | bytes 262144 | tf_op jit(solution)/shard_map/all_to_all | solution.py:252
  63.7 1.2 %place_lags.1 = f32[16,4,256]{2,1,0:T(4,128)} custom-call(f32[8,4,8,128]{3,2,1,0:T(8,128)S(1)} %bitcast.21), custom_call_target="tpu_custom_call" | custom-call | tf_op jit(solution)/shard_map/place_lags/pallas_call | solution.py:253
  (22 shorter events, 2.0 us)
Async XLA Ops:
  0.0 18.3 %copy-start = (bf16[2,8,16,2048]{3,2,1,0:T(8,128)(2,1)S(1)}, bf16[2,8,16,2048]{3,2,1,0:T(8,128)(2,1)}, u32[]{:S(2)}) copy-start(bf16[2,8,16,2048]{3,2,1,0:T(8,128)(2,1)} %constant.45.clone.refs_9_) | copy-start | bytes 3145732
  1.5 7.3 %collective-permute-start.6 = (bf16[2,256,128]{2,1,0:T(8,128)(2,1)S(1)}, bf16[2,256,128]{2,1,0:T(8,128)(2,1)S(1)}, u32[]{:S(2)}, u32[]{:S(2)}) collective-permute-start(bf16[2,256,128]{2,1,0:T(8,128)(2,1)S(1)} %get-tuple-element.29), channel_id=1, source_target_pairs={{0,28},{4,24},{8,20},{12,16},{16,12},{20,8},{24,4},{28,0},{1,29},{... | collective-permute-start | bytes 393224 | tf_op jit(solution)/shard_map/ppermute | solution.py:152
  4.9 6.8 %collective-permute-start.4 = (bf16[2,256,128]{2,1,0:T(8,128)(2,1)S(1)}, bf16[2,256,128]{2,1,0:T(8,128)(2,1)S(1)}, u32[]{:S(2)}, u32[]{:S(2)}) collective-permute-start(bf16[2,256,128]{2,1,0:T(8,128)(2,1)S(1)} %get-tuple-element.30), channel_id=1, source_target_pairs={{0,20},{4,16},{8,28},{12,24},{16,4},{20,0},{24,12},{28,8},{1,21},{... | collective-permute-start | bytes 393224 | tf_op jit(solution)/shard_map/ppermute | solution.py:152
  5.6 8.9 %collective-permute-start.3 = (bf16[2,256,128]{2,1,0:T(8,128)(2,1)S(1)}, bf16[2,256,128]{2,1,0:T(8,128)(2,1)S(1)}, u32[]{:S(2)}, u32[]{:S(2)}) collective-permute-start(bf16[2,256,128]{2,1,0:T(8,128)(2,1)S(1)} %get-tuple-element.31), channel_id=1, source_target_pairs={{0,16},{4,20},{8,24},{12,28},{16,0},{20,4},{24,8},{28,12},{1,17},{... | collective-permute-start | bytes 393224 | tf_op jit(solution)/shard_map/ppermute | solution.py:152
  7.2 7.4 %collective-permute-start.2 = (bf16[2,256,128]{2,1,0:T(8,128)(2,1)S(1)}, bf16[2,256,128]{2,1,0:T(8,128)(2,1)S(1)}, u32[]{:S(2)}, u32[]{:S(2)}) collective-permute-start(bf16[2,256,128]{2,1,0:T(8,128)(2,1)S(1)} %get-tuple-element.32), channel_id=1, source_target_pairs={{0,12},{4,8},{8,4},{12,0},{16,28},{20,24},{24,20},{28,16},{1,13},{... | collective-permute-start | bytes 393224 | tf_op jit(solution)/shard_map/ppermute | solution.py:152
  7.2 11.2 %copy-start.1 = (s32[8,128]{1,0:T(8,128)S(1)}, s32[8,128]{1,0:T(8,128)}, u32[]{:S(2)}) copy-start(s32[8,128]{1,0:T(8,128)} %refs_8_.1) | copy-start | bytes 12292
  7.2 8.1 %collective-permute-start.1 = (bf16[2,256,128]{2,1,0:T(8,128)(2,1)S(1)}, bf16[2,256,128]{2,1,0:T(8,128)(2,1)S(1)}, u32[]{:S(2)}, u32[]{:S(2)}) collective-permute-start(bf16[2,256,128]{2,1,0:T(8,128)(2,1)S(1)} %get-tuple-element.33), channel_id=1, source_target_pairs={{0,8},{4,12},{8,0},{12,4},{16,24},{20,28},{24,16},{28,20},{1,9},{5... | collective-permute-start | bytes 393224 | tf_op jit(solution)/shard_map/ppermute | solution.py:152
  8.8 6.4 %collective-permute-start = (bf16[2,256,128]{2,1,0:T(8,128)(2,1)S(1)}, bf16[2,256,128]{2,1,0:T(8,128)(2,1)S(1)}, u32[]{:S(2)}, u32[]{:S(2)}) collective-permute-start(bf16[2,256,128]{2,1,0:T(8,128)(2,1)S(1)} %get-tuple-element.34), channel_id=1, source_target_pairs={{0,4},{4,0},{8,12},{12,8},{16,20},{20,16},{24,28},{28,24},{1,5},{5... | collective-permute-start | bytes 393224 | tf_op jit(solution)/shard_map/ppermute | solution.py:152
  11.6 6.7 %collective-permute-start.5 = (bf16[2,256,128]{2,1,0:T(8,128)(2,1)S(1)}, bf16[2,256,128]{2,1,0:T(8,128)(2,1)S(1)}, u32[]{:S(2)}, u32[]{:S(2)}) collective-permute-start(bf16[2,256,128]{2,1,0:T(8,128)(2,1)S(1)} %get-tuple-element.36), channel_id=1, source_target_pairs={{0,24},{4,28},{8,16},{12,20},{16,8},{20,12},{24,0},{28,4},{1,25},{... | collective-permute-start | bytes 393224 | tf_op jit(solution)/shard_map/ppermute | solution.py:152
  18.3 0.7 %copy-start.2 = (s32[4]{0:T(128)S(1)}, s32[4]{0:T(128)}, u32[]{:S(2)}) copy-start(s32[4]{0:T(128)} %offs_ref.3) | copy-start | bytes 52
  28.1 4.1 %collective-permute-start.7 = (s16[25,16,128]{2,1,0:T(8,128)(2,1)S(1)}, s16[25,16,128]{2,1,0:T(8,128)(2,1)S(1)}, u32[]{:S(2)}, u32[]{:S(2)}) collective-permute-start(s16[25,16,128]{2,1,0:T(8,128)(2,1)S(1)} %get-tuple-element.18), channel_id=1, source_target_pairs={{0,4},{4,0},{8,12},{12,8},{16,20},{20,16},{24,28},{28,24},{1,5},{5... | collective-permute-start | bytes 307208 | tf_op jit(solution)/shard_map/ppermute | solution.py:152
  28.2 5.9 %collective-permute-start.8 = (s16[25,16,128]{2,1,0:T(8,128)(2,1)S(1)}, s16[25,16,128]{2,1,0:T(8,128)(2,1)S(1)}, u32[]{:S(2)}, u32[]{:S(2)}) collective-permute-start(s16[25,16,128]{2,1,0:T(8,128)(2,1)S(1)} %get-tuple-element.19), channel_id=1, source_target_pairs={{0,8},{4,12},{8,0},{12,4},{16,24},{20,28},{24,16},{28,20},{1,9},{5... | collective-permute-start | bytes 307208 | tf_op jit(solution)/shard_map/ppermute | solution.py:152
  30.4 5.4 %collective-permute-start.9 = (s16[25,16,128]{2,1,0:T(8,128)(2,1)S(1)}, s16[25,16,128]{2,1,0:T(8,128)(2,1)S(1)}, u32[]{:S(2)}, u32[]{:S(2)}) collective-permute-start(s16[25,16,128]{2,1,0:T(8,128)(2,1)S(1)} %get-tuple-element.20), channel_id=1, source_target_pairs={{0,12},{4,8},{8,4},{12,0},{16,28},{20,24},{24,20},{28,16},{1,13},{... | collective-permute-start | bytes 307208 | tf_op jit(solution)/shard_map/ppermute | solution.py:152
  30.4 5.5 %collective-permute-start.10 = (s16[25,16,128]{2,1,0:T(8,128)(2,1)S(1)}, s16[25,16,128]{2,1,0:T(8,128)(2,1)S(1)}, u32[]{:S(2)}, u32[]{:S(2)}) collective-permute-start(s16[25,16,128]{2,1,0:T(8,128)(2,1)S(1)} %get-tuple-element.21), channel_id=1, source_target_pairs={{0,16},{4,20},{8,24},{12,28},{16,0},{20,4},{24,8},{28,12},{1,17},{... | collective-permute-start | bytes 307208 | tf_op jit(solution)/shard_map/ppermute | solution.py:152
  32.2 9.6 %collective-permute-start.11 = (s16[25,16,128]{2,1,0:T(8,128)(2,1)S(1)}, s16[25,16,128]{2,1,0:T(8,128)(2,1)S(1)}, u32[]{:S(2)}, u32[]{:S(2)}) collective-permute-start(s16[25,16,128]{2,1,0:T(8,128)(2,1)S(1)} %get-tuple-element.22), channel_id=1, source_target_pairs={{0,20},{4,16},{8,28},{12,24},{16,4},{20,0},{24,12},{28,8},{1,21},{... | collective-permute-start | bytes 307208 | tf_op jit(solution)/shard_map/ppermute | solution.py:152
  32.2 9.6 %collective-permute-start.12 = (s16[25,16,128]{2,1,0:T(8,128)(2,1)S(1)}, s16[25,16,128]{2,1,0:T(8,128)(2,1)S(1)}, u32[]{:S(2)}, u32[]{:S(2)}) collective-permute-start(s16[25,16,128]{2,1,0:T(8,128)(2,1)S(1)} %get-tuple-element.23), channel_id=1, source_target_pairs={{0,24},{4,28},{8,16},{12,20},{16,8},{20,12},{24,0},{28,4},{1,25},{... | collective-permute-start | bytes 307208 | tf_op jit(solution)/shard_map/ppermute | solution.py:152
  34.1 7.7 %collective-permute-start.13 = (s16[25,16,128]{2,1,0:T(8,128)(2,1)S(1)}, s16[25,16,128]{2,1,0:T(8,128)(2,1)S(1)}, u32[]{:S(2)}, u32[]{:S(2)}) collective-permute-start(s16[25,16,128]{2,1,0:T(8,128)(2,1)S(1)} %get-tuple-element.24), channel_id=1, source_target_pairs={{0,28},{4,24},{8,20},{12,16},{16,12},{20,8},{24,4},{28,0},{1,29},{... | collective-permute-start | bytes 307208 | tf_op jit(solution)/shard_map/ppermute | solution.py:152
  42.0 4.5 %collective-permute-start.14 = (f32[6,16,128]{2,1,0:T(8,128)S(1)}, f32[6,16,128]{2,1,0:T(8,128)S(1)}, u32[]{:S(2)}, u32[]{:S(2)}) collective-permute-start(f32[6,16,128]{2,1,0:T(8,128)S(1)} %get-tuple-element.26), channel_id=1, source_target_pairs={{0,1},{1,0},{2,3},{3,2},{4,5},{5,4},{6,7},{7,6},{8,9},{9,8},{10,11... | collective-permute-start | bytes 147464 | tf_op jit(solution)/shard_map/ppermute | solution.py:152
  43.7 6.1 %collective-permute-start.15 = (f32[6,16,128]{2,1,0:T(8,128)S(1)}, f32[6,16,128]{2,1,0:T(8,128)S(1)}, u32[]{:S(2)}, u32[]{:S(2)}) collective-permute-start(f32[6,16,128]{2,1,0:T(8,128)S(1)} %get-tuple-element.27), channel_id=1, source_target_pairs={{0,2},{1,3},{2,0},{3,1},{4,6},{5,7},{6,4},{7,5},{8,10},{9,11},{10,... | collective-permute-start | bytes 147464 | tf_op jit(solution)/shard_map/ppermute | solution.py:152
  46.3 5.9 %collective-permute-start.16 = (f32[6,16,128]{2,1,0:T(8,128)S(1)}, f32[6,16,128]{2,1,0:T(8,128)S(1)}, u32[]{:S(2)}, u32[]{:S(2)}) collective-permute-start(f32[6,16,128]{2,1,0:T(8,128)S(1)} %get-tuple-element.28), channel_id=1, source_target_pairs={{0,3},{1,2},{2,1},{3,0},{4,7},{5,6},{6,5},{7,4},{8,11},{9,10},{10,... | collective-permute-start | bytes 147464 | tf_op jit(solution)/shard_map/ppermute | solution.py:152

commit v4 on v3

--- a/solution.py
+++ b/solution.py
@@ -44,7 +44,8 @@
     return np.concatenate([np.cos(angles), np.sin(angles)]).astype(jnp.bfloat16)
 
 
-def window_kernel(chan_count, offs_ref, where_ref, *refs):
+def window_kernel(order, offs_ref, where_ref, *refs):
+    chan_count = len(order)
     spec_refs, (qual_ref, table_ref) = refs[:chan_count], refs[chan_count : chan_count + 2]
     out_refs = refs[chan_count + 2 : 2 * chan_count + 2]
     mag_ref, white_ref, cross_ref = refs[2 * chan_count + 2 :]
@@ -57,7 +58,7 @@
     step = 64
 
     total = jnp.zeros((8, chans), jnp.float32)
-    for partner, spec_ref in enumerate(spec_refs):
+    for partner, spec_ref in zip(order, spec_refs):
 
         def magnitudes(index, total, spec_ref=spec_ref, base=(me ^ partner) * band):
             rows = pl.ds(pl.multiple_of(index * step, step), step)
@@ -72,7 +73,7 @@
     floor = 0.5 * (level + 1e-05)
     usable = qual_ref[pl.ds(me, 1), :].astype(jnp.float32)
 
-    for partner, spec_ref in enumerate(spec_refs):
+    for partner, spec_ref in zip(order, spec_refs):
 
         def whiten(index, carry, spec_ref=spec_ref, base=(me ^ partner) * band):
             rows = pl.ds(pl.multiple_of(index * step, step), step)
@@ -89,7 +90,7 @@
     row = lax.broadcasted_iota(jnp.int32, (lag_rows, chans), 0)
     levels = jnp.zeros((lag_rows, chans), jnp.float32)
     scale = 1.0 / math.sqrt(freqs)
-    table = jnp.concatenate([table_ref[side, me ^ k] for side in range(2) for k in range(chan_count)], axis=0)
+    table = jnp.concatenate([table_ref[side, me ^ k] for side in range(2) for k in order], axis=0)
     for number in range(offset_count):
         ahead = offs_ref[number] * (chans // chan_count)
         turn = chans - ahead
@@ -130,12 +131,12 @@
         out_refs[k][blocks - 1, :, :] = levels.astype(jnp.int32).astype(jnp.int16)
 
 
-def sum_kernel(chan_count, where_ref, *refs):
-    code_refs, out_refs = refs[:chan_count], refs[chan_count:]
+def sum_kernel(order, where_ref, *refs):
+    code_refs, out_refs = refs[: -len(order)], refs[-len(order) :]
     blocks = code_refs[0].shape[0]
     levels = [level_of(decode(codes_ref[blocks - 1])) / CODE_TOP for codes_ref in code_refs]
     row = lax.broadcasted_iota(jnp.int32, levels[0].shape, 0)
-    for k, out_ref in enumerate(out_refs):
+    for k, out_ref in zip(order, out_refs):
         number = where_ref[0] ^ k
         own = [jnp.sum(jnp.where(row == number, level, 0.0), axis=0, keepdims=True) for level in levels]
         for block in range(6):
@@ -146,11 +147,28 @@
             out_ref[block, :, :] = total if block < 2 else total / CODE_TOP
 
 
+def partners(count):
+    return sorted(range(1, count), key=lambda k: (-(k >> 1).bit_count(), k & 1, k)) + [0]
+
+
 def exchange(pieces, axis):
     count = lax.axis_size(axis)
-    return [pieces[0]] + [
-        lax.ppermute(pieces[k], axis, [(source, source ^ k) for source in range(count)]) for k in range(1, count)
+    return [
+        lax.ppermute(piece, axis, [(source, source ^ k) for source in range(count)]) if k else piece
+        for k, piece in zip(partners(count), pieces)
     ]
+
+
+def split_kernel(order, where_ref, spec_ref, *refs):
+    out_refs, sems = refs[:-1], refs[-1]
+    copies = [
+        pltpu.make_async_copy(spec_ref.at[:, where_ref[0] ^ k], out_ref, sems.at[number])
+        for number, (k, out_ref) in enumerate(zip(order, out_refs))
+    ]
+    for copy in copies:
+        copy.start()
+    for copy in copies:
+        copy.wait()
 
 
 def stack_kernel(windows, offs_ref, where_ref, *refs):
@@ -216,11 +234,18 @@
     tm_index = lax.axis_index("tm").astype(jnp.int32)
     chan_where, tm_where = chan_index.reshape(1), tm_index.reshape(1)
 
-    pieces = [
-        lax.dynamic_index_in_dim(spectra, chan_index ^ k, 1, keepdims=False) for k in range(chan_count)
-    ]
+    chan_order, tm_order = partners(chan_count), partners(tm_count)
+    pieces = pl.pallas_call(
+        functools.partial(split_kernel, chan_order),
+        out_shape=[jax.ShapeDtypeStruct((2, band, chans), spectra.dtype)] * chan_count,
+        in_specs=[smem, pl.BlockSpec(memory_space=pl.ANY)],
+        out_specs=[pl.BlockSpec(memory_space=pl.ANY)] * chan_count,
+        scratch_shapes=[pltpu.SemaphoreType.DMA((chan_count,))],
+        compiler_params=params,
+        name="split_windows",
+    )(chan_where, spectra)
     pairs = pl.pallas_call(
-        functools.partial(window_kernel, chan_count),
+        functools.partial(window_kernel, chan_order),
         out_shape=[jax.ShapeDtypeStruct((6 * offset_count + 1, lag_rows, chans), jnp.int16)] * chan_count,
         in_specs=[smem, smem] + [vmem] * (chan_count + 2),
         out_specs=[vmem] * chan_count,
@@ -233,7 +258,7 @@
         name="window_pairs",
     )(offsets, chan_where, *exchange(pieces, "chan"), quality, table)
     sums = pl.pallas_call(
-        functools.partial(sum_kernel, chan_count),
+        functools.partial(sum_kernel, tm_order),
         out_shape=[jax.ShapeDtypeStruct((6, lag_rows, chans), jnp.float32)] * tm_count,
         in_specs=[smem] + [vmem] * chan_count,
         out_specs=[vmem] * tm_count,

time: 65.1 us -> 63.7 us (0.978)
  starting transfers between devices: 20.8 us -> 17.7 us
  blocking collectives: 10.8 us -> 12.6 us
  local copies, waits for them, and re-layouts: 2.1 us -> 1.24 us
  Pallas kernels: 11.3 us -> 12 us
    ppermute x17, starting transfers between devices: 20.8 us -> 17.7 us  [exchange(): lax.ppermute(piece, axis, [(source, source ^ k) for source in range(count)])]
    all_to_all x1, blocking collectives: 10.8 us -> 12.6 us  [window_shards(): lax.all_to_all(pieces.reshape(shape), ('chan', 'tm'), 0, 0, tiled=True)]
    squeeze x1 -> x0, local copies, waits for them, and re-layouts: 1.44 us -> none  [window_shards(): lax.dynamic_index_in_dim(spectra, chan_index ^ k, 1, keepdims=False)]
    pallas_call x2 -> x3, Pallas kernels: 9.34 us -> 10.1 us  [the longest x1 9.13 us: window_shards(): pl.pallas_call(functools.partial(window_kernel, chan_order), out_shape=[j...]
  transfers between devices with their start and end apart: 17 -> 17, of which waited for: 11 -> 12; matrix products, arithmetic and copies ran while one was open for 0% -> 0% of each run, Pallas kernels for 0% -> 0%
where the time goes in v4:
time: 63.7 us; the launch traced here: 63.5 us
  waiting for transfers between devices  19.8 us (31%)
  starting transfers between devices  17.7 us (28%)
  blocking collectives  12.6 us (20%)
  Pallas kernels  12 us (19%)
  local copies, waits for them, and re-layouts  1.24 us (2%)
    ppermute x17, waiting for transfers between devices, exchange(): lax.ppermute(piece, axis, [(source, source ^ k) for source in range(count)])  19.8 us
    ppermute x17, starting transfers between devices, exchange(): lax.ppermute(piece, axis, [(source, source ^ k) for source in range(count)])  17.7 us
    all_to_all x1, blocking collectives, window_shards(): lax.all_to_all(pieces.reshape(shape), ('chan', 'tm'), 0, 0, tiled=True)  12.6 us
    pallas_call x1, Pallas kernels, window_shards(): pl.pallas_call(functools.partial(window_kernel, chan_order), out_shape=[j...  9.13 us
  transfers between devices with their start and end apart: 17, of which 12 were waited for; matrix products, arithmetic and copies ran while one was open for 0% of the time, Pallas kernels for 0%

profile of v4, /device:TPU:0, one launch (start us, length us, event | category | flops | bytes accessed | tf_op | source)
XLA Modules:
  0.0 63.5 jit_solution(9539856622320803865)
XLA Ops:
  0.0 1.2 %copy-done = bf16[2,8,256,128]{3,2,1,0:T(8,128)(2,1)S(1)} copy-done((bf16[2,8,256,128]{3,2,1,0:T(8,128)(2,1)S(1)}, bf16[2,8,256,128]{3,2,1,0:T(8,128)(2,1)}, u32[]{:S(2)}) %copy-start) | copy-done | bytes 1048600
  1.2 0.7 %split_windows.1 = (bf16[2,256,128]{2,1,0:T(8,128)(2,1)S(1)}, bf16[2,256,128]{2,1,0:T(8,128)(2,1)S(1)}, bf16[2,256,128]{2,1,0:T(8,128)(2,1)S(1)}, bf16[2,256,128...) custom-call(s32[1]{0:T(128)} %bitcast.1.where_ref, ...), custom_call_target="tpu_custom_call" | custom-call | tf_op jit(solution)/shard_map/split_windows/pallas_call | solution.py:238
  2.0 4.0 %collective-permute-start = (bf16[2,256,128]{2,1,0:T(8,128)(2,1)S(1)}, bf16[2,256,128]{2,1,0:T(8,128)(2,1)S(1)}, u32[]{:S(2)}, u32[]{:S(2)}) collective-permute-start(bf16[2,256,128]{2,1,0:T(8,128)(2,1)S(1)} %get-tuple-element.25), channel_id=1, source_target_pairs={{0,24},{4,28},{8,16},{12,20},{16,8},{20,12},{24,0},{28,4},{1,25},{... | collective-permute-start | bytes 393224 | tf_op jit(solution)/shard_map/ppermute | solution.py:157
  5.9 1.1 %collective-permute-start.2 = (bf16[2,256,128]{2,1,0:T(8,128)(2,1)S(1)}, bf16[2,256,128]{2,1,0:T(8,128)(2,1)S(1)}, u32[]{:S(2)}, u32[]{:S(2)}) collective-permute-start(bf16[2,256,128]{2,1,0:T(8,128)(2,1)S(1)} %get-tuple-element.27), channel_id=1, source_target_pairs={{0,8},{4,12},{8,0},{12,4},{16,24},{20,28},{24,16},{28,20},{1,9},{5... | collective-permute-start | bytes 393224 | tf_op jit(solution)/shard_map/ppermute | solution.py:157
  7.1 1.5 %collective-permute-start.3 = (bf16[2,256,128]{2,1,0:T(8,128)(2,1)S(1)}, bf16[2,256,128]{2,1,0:T(8,128)(2,1)S(1)}, u32[]{:S(2)}, u32[]{:S(2)}) collective-permute-start(bf16[2,256,128]{2,1,0:T(8,128)(2,1)S(1)} %get-tuple-element.28), channel_id=1, source_target_pairs={{0,16},{4,20},{8,24},{12,28},{16,0},{20,4},{24,8},{28,12},{1,17},{... | collective-permute-start | bytes 393224 | tf_op jit(solution)/shard_map/ppermute | solution.py:157
  9.8 2.8 %collective-permute-done.1.refs_1_ = bf16[2,256,128]{2,1,0:T(8,128)(2,1)S(1)} collective-permute-done((bf16[2,256,128]{2,1,0:T(8,128)(2,1)S(1)}, bf16[2,256,128]{2,1,0:T(8,128)(2,1)S(1)}, u32[]{:S(2)}, u32[]{:S(2)}) %collective-permute-start.1) | collective-permute-done | bytes 131104 | tf_op jit(solution)/shard_map/ppermute | solution.py:157
  12.7 3.4 %collective-permute-done.2.refs_2_ = bf16[2,256,128]{2,1,0:T(8,128)(2,1)S(1)} collective-permute-done((bf16[2,256,128]{2,1,0:T(8,128)(2,1)S(1)}, bf16[2,256,128]{2,1,0:T(8,128)(2,1)S(1)}, u32[]{:S(2)}, u32[]{:S(2)}) %collective-permute-start.2) | collective-permute-done | bytes 131104 | tf_op jit(solution)/shard_map/ppermute | solution.py:157
  16.1 1.1 %collective-permute-done.4.refs_4_ = bf16[2,256,128]{2,1,0:T(8,128)(2,1)S(1)} collective-permute-done((bf16[2,256,128]{2,1,0:T(8,128)(2,1)S(1)}, bf16[2,256,128]{2,1,0:T(8,128)(2,1)S(1)}, u32[]{:S(2)}, u32[]{:S(2)}) %collective-permute-start.4) | collective-permute-done | bytes 131104 | tf_op jit(solution)/shard_map/ppermute | solution.py:157
  17.3 0.7 %collective-permute-done.5.refs_5_ = bf16[2,256,128]{2,1,0:T(8,128)(2,1)S(1)} collective-permute-done((bf16[2,256,128]{2,1,0:T(8,128)(2,1)S(1)}, bf16[2,256,128]{2,1,0:T(8,128)(2,1)S(1)}, u32[]{:S(2)}, u32[]{:S(2)}) %collective-permute-start.5) | collective-permute-done | bytes 131104 | tf_op jit(solution)/shard_map/ppermute | solution.py:157
  18.0 9.1 %window_pairs.1 = (s16[25,16,128]{2,1,0:T(8,128)(2,1)S(1)}, s16[25,16,128]{2,1,0:T(8,128)(2,1)S(1)}, s16[25,16,128]{2,1,0:T(8,128)(2,1)S(1)}, s16[25,16,128]{2,1...) custom-call(s32[4]{0:T(128)S(1)} %copy-done.3, ...), custom_call_target="tpu_custom_call" | custom-call | tf_op jit(solution)/shard_map/window_pairs/pallas_call | solution.py:247
  27.1 2.6 %collective-permute-start.7 = (s16[25,16,128]{2,1,0:T(8,128)(2,1)S(1)}, s16[25,16,128]{2,1,0:T(8,128)(2,1)S(1)}, u32[]{:S(2)}, u32[]{:S(2)}) collective-permute-start(s16[25,16,128]{2,1,0:T(8,128)(2,1)S(1)} %get-tuple-element.33), channel_id=1, source_target_pairs={{0,24},{4,28},{8,16},{12,20},{16,8},{20,12},{24,0},{28,4},{1,25},{... | collective-permute-start | bytes 307208 | tf_op jit(solution)/shard_map/ppermute | solution.py:157
  29.7 1.4 %collective-permute-start.9 = (s16[25,16,128]{2,1,0:T(8,128)(2,1)S(1)}, s16[25,16,128]{2,1,0:T(8,128)(2,1)S(1)}, u32[]{:S(2)}, u32[]{:S(2)}) collective-permute-start(s16[25,16,128]{2,1,0:T(8,128)(2,1)S(1)} %get-tuple-element.35), channel_id=1, source_target_pairs={{0,8},{4,12},{8,0},{12,4},{16,24},{20,28},{24,16},{28,20},{1,9},{5... | collective-permute-start | bytes 307208 | tf_op jit(solution)/shard_map/ppermute | solution.py:157
  31.1 1.6 %collective-permute-start.10 = (s16[25,16,128]{2,1,0:T(8,128)(2,1)S(1)}, s16[25,16,128]{2,1,0:T(8,128)(2,1)S(1)}, u32[]{:S(2)}, u32[]{:S(2)}) collective-permute-start(s16[25,16,128]{2,1,0:T(8,128)(2,1)S(1)} %get-tuple-element.36), channel_id=1, source_target_pairs={{0,16},{4,20},{8,24},{12,28},{16,0},{20,4},{24,8},{28,12},{1,17},{... | collective-permute-start | bytes 307208 | tf_op jit(solution)/shard_map/ppermute | solution.py:157
  33.5 2.4 %collective-permute-done.8.refs_1_ = s16[25,16,128]{2,1,0:T(8,128)(2,1)S(1)} collective-permute-done((s16[25,16,128]{2,1,0:T(8,128)(2,1)S(1)}, s16[25,16,128]{2,1,0:T(8,128)(2,1)S(1)}, u32[]{:S(2)}, u32[]{:S(2)}) %collective-permute-start.8) | collective-permute-done | bytes 102432 | tf_op jit(solution)/shard_map/ppermute | solution.py:157
  35.9 2.2 %collective-permute-done.9.refs_2_ = s16[25,16,128]{2,1,0:T(8,128)(2,1)S(1)} collective-permute-done((s16[25,16,128]{2,1,0:T(8,128)(2,1)S(1)}, s16[25,16,128]{2,1,0:T(8,128)(2,1)S(1)}, u32[]{:S(2)}, u32[]{:S(2)}) %collective-permute-start.9) | collective-permute-done | bytes 102432 | tf_op jit(solution)/shard_map/ppermute | solution.py:157
  38.1 1.0 %collective-permute-done.11.refs_4_ = s16[25,16,128]{2,1,0:T(8,128)(2,1)S(1)} collective-permute-done((s16[25,16,128]{2,1,0:T(8,128)(2,1)S(1)}, s16[25,16,128]{2,1,0:T(8,128)(2,1)S(1)}, u32[]{:S(2)}, u32[]{:S(2)}) %collective-permute-start.11) | collective-permute-done | bytes 102432 | tf_op jit(solution)/shard_map/ppermute | solution.py:157
  39.1 1.0 %collective-permute-done.12.refs_5_ = s16[25,16,128]{2,1,0:T(8,128)(2,1)S(1)} collective-permute-done((s16[25,16,128]{2,1,0:T(8,128)(2,1)S(1)}, s16[25,16,128]{2,1,0:T(8,128)(2,1)S(1)}, u32[]{:S(2)}, u32[]{:S(2)}) %collective-permute-start.12) | collective-permute-done | bytes 102432 | tf_op jit(solution)/shard_map/ppermute | solution.py:157
  40.3 2.7 %collective-permute-start.14 = (f32[6,16,128]{2,1,0:T(8,128)S(1)}, f32[6,16,128]{2,1,0:T(8,128)S(1)}, u32[]{:S(2)}, u32[]{:S(2)}) collective-permute-start(f32[6,16,128]{2,1,0:T(8,128)S(1)} %get-tuple-element.41), channel_id=1, source_target_pairs={{0,2},{1,3},{2,0},{3,1},{4,6},{5,7},{6,4},{7,5},{8,10},{9,11},{10,... | collective-permute-start | bytes 147464 | tf_op jit(solution)/shard_map/ppermute | solution.py:157
  43.0 1.3 %collective-permute-start.15 = (f32[6,16,128]{2,1,0:T(8,128)S(1)}, f32[6,16,128]{2,1,0:T(8,128)S(1)}, u32[]{:S(2)}, u32[]{:S(2)}) collective-permute-start(f32[6,16,128]{2,1,0:T(8,128)S(1)} %get-tuple-element.42), channel_id=1, source_target_pairs={{0,3},{1,2},{2,1},{3,0},{4,7},{5,6},{6,5},{7,4},{8,11},{9,10},{10,... | collective-permute-start | bytes 147464 | tf_op jit(solution)/shard_map/ppermute | solution.py:157
  44.6 1.9 %collective-permute-done.14.refs_0_ = f32[6,16,128]{2,1,0:T(8,128)S(1)} collective-permute-done((f32[6,16,128]{2,1,0:T(8,128)S(1)}, f32[6,16,128]{2,1,0:T(8,128)S(1)}, u32[]{:S(2)}, u32[]{:S(2)}) %collective-permute-start.14) | collective-permute-done | bytes 49184 | tf_op jit(solution)/shard_map/ppermute | solution.py:157
  46.5 2.5 %collective-permute-done.15.refs_1_ = f32[6,16,128]{2,1,0:T(8,128)S(1)} collective-permute-done((f32[6,16,128]{2,1,0:T(8,128)S(1)}, f32[6,16,128]{2,1,0:T(8,128)S(1)}, u32[]{:S(2)}, u32[]{:S(2)}) %collective-permute-start.15) | collective-permute-done | bytes 49184 | tf_op jit(solution)/shard_map/ppermute | solution.py:157
  49.0 0.7 %stack_pairs.1 = f32[8,4,8,128]{3,2,1,0:T(8,128)S(1)} custom-call(s32[4]{0:T(128)S(1)} %copy-done.3, s32[1]{0:T(128)} %bitcast.where_ref, f32[6,16,128]{2,1,0:T(8,128)S(1)} %collective-permute-done.14.refs_0_, f32[6,16,128]{2,1,0:T(8,128)S(1)} %collective-permute-done.15.refs_1_, f32[6,16,128]{2,1,0:T(8,128)S(1)} %collective-permute-done.16.refs_2_, ...), custom_call_target="tpu_custom_call" | custom-call | tf_op jit(solution)/shard_map/stack_pairs/pallas_call | solution.py:268
  49.7 12.6 %all_to_all.5 = f32[32,8,128]{2,1,0:T(8,128)S(1)} all-to-all(f32[32,8,128]{2,1,0:T(8,128)S(1)} %bitcast.4), channel_id=1, replica_groups=mesh['chan'=8,'tm'=4] {'chan','tm'}, dimensions={0} | all-to-all | bytes 262144 | tf_op jit(solution)/shard_map/all_to_all | solution.py:277
  62.3 1.2 %place_lags.1 = f32[16,4,256]{2,1,0:T(4,128)} custom-call(f32[8,4,8,128]{3,2,1,0:T(8,128)S(1)} %bitcast.5), custom_call_target="tpu_custom_call" | custom-call | tf_op jit(solution)/shard_map/place_lags/pallas_call | solution.py:278
  (24 shorter events, 2.6 us)
Async XLA Ops:
  0.0 1.2 %copy-start = (bf16[2,8,256,128]{3,2,1,0:T(8,128)(2,1)S(1)}, bf16[2,8,256,128]{3,2,1,0:T(8,128)(2,1)}, u32[]{:S(2)}) copy-start(bf16[2,8,256,128]{3,2,1,0:T(8,128)(2,1)} %spec_ref.1) | copy-start | bytes 3145732
  1.2 16.7 %copy-start.1 = (bf16[2,8,16,2048]{3,2,1,0:T(8,128)(2,1)S(1)}, bf16[2,8,16,2048]{3,2,1,0:T(8,128)(2,1)}, u32[]{:S(2)}) copy-start(bf16[2,8,16,2048]{3,2,1,0:T(8,128)(2,1)} %constant.11.clone.refs_9_) | copy-start | bytes 3145732
  2.0 7.9 %collective-permute-start = (bf16[2,256,128]{2,1,0:T(8,128)(2,1)S(1)}, bf16[2,256,128]{2,1,0:T(8,128)(2,1)S(1)}, u32[]{:S(2)}, u32[]{:S(2)}) collective-permute-start(bf16[2,256,128]{2,1,0:T(8,128)(2,1)S(1)} %get-tuple-element.25), channel_id=1, source_target_pairs={{0,24},{4,28},{8,16},{12,20},{16,8},{20,12},{24,0},{28,4},{1,25},{... | collective-permute-start | bytes 393224 | tf_op jit(solution)/shard_map/ppermute | solution.py:157
  5.9 6.8 %collective-permute-start.1 = (bf16[2,256,128]{2,1,0:T(8,128)(2,1)S(1)}, bf16[2,256,128]{2,1,0:T(8,128)(2,1)S(1)}, u32[]{:S(2)}, u32[]{:S(2)}) collective-permute-start(bf16[2,256,128]{2,1,0:T(8,128)(2,1)S(1)} %get-tuple-element.26), channel_id=1, source_target_pairs={{0,28},{4,24},{8,20},{12,16},{16,12},{20,8},{24,4},{28,0},{1,29},{... | collective-permute-start | bytes 393224 | tf_op jit(solution)/shard_map/ppermute | solution.py:157
  5.9 10.2 %collective-permute-start.2 = (bf16[2,256,128]{2,1,0:T(8,128)(2,1)S(1)}, bf16[2,256,128]{2,1,0:T(8,128)(2,1)S(1)}, u32[]{:S(2)}, u32[]{:S(2)}) collective-permute-start(bf16[2,256,128]{2,1,0:T(8,128)(2,1)S(1)} %get-tuple-element.27), channel_id=1, source_target_pairs={{0,8},{4,12},{8,0},{12,4},{16,24},{20,28},{24,16},{28,20},{1,9},{5... | collective-permute-start | bytes 393224 | tf_op jit(solution)/shard_map/ppermute | solution.py:157
  7.1 10.9 %copy-start.2 = (s32[8,128]{1,0:T(8,128)S(1)}, s32[8,128]{1,0:T(8,128)}, u32[]{:S(2)}) copy-start(s32[8,128]{1,0:T(8,128)} %refs_8_.1) | copy-start | bytes 12292
  7.1 9.1 %collective-permute-start.3 = (bf16[2,256,128]{2,1,0:T(8,128)(2,1)S(1)}, bf16[2,256,128]{2,1,0:T(8,128)(2,1)S(1)}, u32[]{:S(2)}, u32[]{:S(2)}) collective-permute-start(bf16[2,256,128]{2,1,0:T(8,128)(2,1)S(1)} %get-tuple-element.28), channel_id=1, source_target_pairs={{0,16},{4,20},{8,24},{12,28},{16,0},{20,4},{24,8},{28,12},{1,17},{... | collective-permute-start | bytes 393224 | tf_op jit(solution)/shard_map/ppermute | solution.py:157
  8.6 8.7 %collective-permute-start.4 = (bf16[2,256,128]{2,1,0:T(8,128)(2,1)S(1)}, bf16[2,256,128]{2,1,0:T(8,128)(2,1)S(1)}, u32[]{:S(2)}, u32[]{:S(2)}) collective-permute-start(bf16[2,256,128]{2,1,0:T(8,128)(2,1)S(1)} %get-tuple-element.29), channel_id=1, source_target_pairs={{0,12},{4,8},{8,4},{12,0},{16,28},{20,24},{24,20},{28,16},{1,13},{... | collective-permute-start | bytes 393224 | tf_op jit(solution)/shard_map/ppermute | solution.py:157
  9.8 8.1 %collective-permute-start.5 = (bf16[2,256,128]{2,1,0:T(8,128)(2,1)S(1)}, bf16[2,256,128]{2,1,0:T(8,128)(2,1)S(1)}, u32[]{:S(2)}, u32[]{:S(2)}) collective-permute-start(bf16[2,256,128]{2,1,0:T(8,128)(2,1)S(1)} %get-tuple-element.30), channel_id=1, source_target_pairs={{0,20},{4,16},{8,28},{12,24},{16,4},{20,0},{24,12},{28,8},{1,21},{... | collective-permute-start | bytes 393224 | tf_op jit(solution)/shard_map/ppermute | solution.py:157
  12.7 5.3 %copy-start.3 = (s32[4]{0:T(128)S(1)}, s32[4]{0:T(128)}, u32[]{:S(2)}) copy-start(s32[4]{0:T(128)} %offs_ref.3) | copy-start | bytes 52
  12.7 5.3 %collective-permute-start.6 = (bf16[2,256,128]{2,1,0:T(8,128)(2,1)S(1)}, bf16[2,256,128]{2,1,0:T(8,128)(2,1)S(1)}, u32[]{:S(2)}, u32[]{:S(2)}) collective-permute-start(bf16[2,256,128]{2,1,0:T(8,128)(2,1)S(1)} %get-tuple-element.31), channel_id=1, source_target_pairs={{0,4},{4,0},{8,12},{12,8},{16,20},{20,16},{24,28},{28,24},{1,5},{5... | collective-permute-start | bytes 393224 | tf_op jit(solution)/shard_map/ppermute | solution.py:157
  27.1 5.9 %collective-permute-start.7 = (s16[25,16,128]{2,1,0:T(8,128)(2,1)S(1)}, s16[25,16,128]{2,1,0:T(8,128)(2,1)S(1)}, u32[]{:S(2)}, u32[]{:S(2)}) collective-permute-start(s16[25,16,128]{2,1,0:T(8,128)(2,1)S(1)} %get-tuple-element.33), channel_id=1, source_target_pairs={{0,24},{4,28},{8,16},{12,20},{16,8},{20,12},{24,0},{28,4},{1,25},{... | collective-permute-start | bytes 307208 | tf_op jit(solution)/shard_map/ppermute | solution.py:157
  29.7 6.2 %collective-permute-start.8 = (s16[25,16,128]{2,1,0:T(8,128)(2,1)S(1)}, s16[25,16,128]{2,1,0:T(8,128)(2,1)S(1)}, u32[]{:S(2)}, u32[]{:S(2)}) collective-permute-start(s16[25,16,128]{2,1,0:T(8,128)(2,1)S(1)} %get-tuple-element.34), channel_id=1, source_target_pairs={{0,28},{4,24},{8,20},{12,16},{16,12},{20,8},{24,4},{28,0},{1,29},{... | collective-permute-start | bytes 307208 | tf_op jit(solution)/shard_map/ppermute | solution.py:157
  29.7 8.4 %collective-permute-start.9 = (s16[25,16,128]{2,1,0:T(8,128)(2,1)S(1)}, s16[25,16,128]{2,1,0:T(8,128)(2,1)S(1)}, u32[]{:S(2)}, u32[]{:S(2)}) collective-permute-start(s16[25,16,128]{2,1,0:T(8,128)(2,1)S(1)} %get-tuple-element.35), channel_id=1, source_target_pairs={{0,8},{4,12},{8,0},{12,4},{16,24},{20,28},{24,16},{28,20},{1,9},{5... | collective-permute-start | bytes 307208 | tf_op jit(solution)/shard_map/ppermute | solution.py:157
  31.1 7.0 %collective-permute-start.10 = (s16[25,16,128]{2,1,0:T(8,128)(2,1)S(1)}, s16[25,16,128]{2,1,0:T(8,128)(2,1)S(1)}, u32[]{:S(2)}, u32[]{:S(2)}) collective-permute-start(s16[25,16,128]{2,1,0:T(8,128)(2,1)S(1)} %get-tuple-element.36), channel_id=1, source_target_pairs={{0,16},{4,20},{8,24},{12,28},{16,0},{20,4},{24,8},{28,12},{1,17},{... | collective-permute-start | bytes 307208 | tf_op jit(solution)/shard_map/ppermute | solution.py:157
  32.7 6.5 %collective-permute-start.11 = (s16[25,16,128]{2,1,0:T(8,128)(2,1)S(1)}, s16[25,16,128]{2,1,0:T(8,128)(2,1)S(1)}, u32[]{:S(2)}, u32[]{:S(2)}) collective-permute-start(s16[25,16,128]{2,1,0:T(8,128)(2,1)S(1)} %get-tuple-element.37), channel_id=1, source_target_pairs={{0,12},{4,8},{8,4},{12,0},{16,28},{20,24},{24,20},{28,16},{1,13},{... | collective-permute-start | bytes 307208 | tf_op jit(solution)/shard_map/ppermute | solution.py:157
  33.0 7.1 %collective-permute-start.12 = (s16[25,16,128]{2,1,0:T(8,128)(2,1)S(1)}, s16[25,16,128]{2,1,0:T(8,128)(2,1)S(1)}, u32[]{:S(2)}, u32[]{:S(2)}) collective-permute-start(s16[25,16,128]{2,1,0:T(8,128)(2,1)S(1)} %get-tuple-element.38), channel_id=1, source_target_pairs={{0,20},{4,16},{8,28},{12,24},{16,4},{20,0},{24,12},{28,8},{1,21},{... | collective-permute-start | bytes 307208 | tf_op jit(solution)/shard_map/ppermute | solution.py:157
  35.9 4.2 %collective-permute-start.13 = (s16[25,16,128]{2,1,0:T(8,128)(2,1)S(1)}, s16[25,16,128]{2,1,0:T(8,128)(2,1)S(1)}, u32[]{:S(2)}, u32[]{:S(2)}) collective-permute-start(s16[25,16,128]{2,1,0:T(8,128)(2,1)S(1)} %get-tuple-element.39), channel_id=1, source_target_pairs={{0,4},{4,0},{8,12},{12,8},{16,20},{20,16},{24,28},{28,24},{1,5},{5... | collective-permute-start | bytes 307208 | tf_op jit(solution)/shard_map/ppermute | solution.py:157
  40.3 6.1 %collective-permute-start.14 = (f32[6,16,128]{2,1,0:T(8,128)S(1)}, f32[6,16,128]{2,1,0:T(8,128)S(1)}, u32[]{:S(2)}, u32[]{:S(2)}) collective-permute-start(f32[6,16,128]{2,1,0:T(8,128)S(1)} %get-tuple-element.41), channel_id=1, source_target_pairs={{0,2},{1,3},{2,0},{3,1},{4,6},{5,7},{6,4},{7,5},{8,10},{9,11},{10,... | collective-permute-start | bytes 147464 | tf_op jit(solution)/shard_map/ppermute | solution.py:157
  43.0 6.0 %collective-permute-start.15 = (f32[6,16,128]{2,1,0:T(8,128)S(1)}, f32[6,16,128]{2,1,0:T(8,128)S(1)}, u32[]{:S(2)}, u32[]{:S(2)}) collective-permute-start(f32[6,16,128]{2,1,0:T(8,128)S(1)} %get-tuple-element.42), channel_id=1, source_target_pairs={{0,3},{1,2},{2,1},{3,0},{4,7},{5,6},{6,5},{7,4},{8,11},{9,10},{10,... | collective-permute-start | bytes 147464 | tf_op jit(solution)/shard_map/ppermute | solution.py:157
  44.3 4.6 %collective-permute-start.16 = (f32[6,16,128]{2,1,0:T(8,128)S(1)}, f32[6,16,128]{2,1,0:T(8,128)S(1)}, u32[]{:S(2)}, u32[]{:S(2)}) collective-permute-start(f32[6,16,128]{2,1,0:T(8,128)S(1)} %get-tuple-element.43), channel_id=1, source_target_pairs={{0,1},{1,0},{2,3},{3,2},{4,5},{5,4},{6,7},{7,6},{8,9},{9,8},{10,11... | collective-permute-start | bytes 147464 | tf_op jit(solution)/shard_map/ppermute | solution.py:157

commit v5 on v4

--- a/solution.py
+++ b/solution.py
@@ -21,7 +21,7 @@
 
 
 def encode(value):
-    return jnp.round(value * CODE_TOP).astype(jnp.int32).astype(jnp.int16)
+    return jnp.round(value).astype(jnp.int32).astype(jnp.int16)
 
 
 def decode(code):
@@ -59,82 +59,72 @@
 
     total = jnp.zeros((8, chans), jnp.float32)
     for partner, spec_ref in zip(order, spec_refs):
-
-        def magnitudes(index, total, spec_ref=spec_ref, base=(me ^ partner) * band):
-            rows = pl.ds(pl.multiple_of(index * step, step), step)
-            real = spec_ref[0, rows, :].astype(jnp.float32)
-            imag = spec_ref[1, rows, :].astype(jnp.float32)
-            magnitude = jnp.sqrt(real * real + imag * imag)
-            mag_ref[pl.ds(pl.multiple_of(base + index * step, step), step), :] = magnitude
-            return total + jnp.sum(magnitude.reshape(step // 8, 8, chans), axis=0)
-
-        total = lax.fori_loop(0, band // step, magnitudes, total, unroll=True)
-    level = jnp.sum(total, axis=0, keepdims=True) / freqs
+        base = (me ^ partner) * band
+        for row in range(0, band, step):
+            real = spec_ref[0, row : row + step, :].astype(jnp.float32)
+            imag = spec_ref[1, row : row + step, :].astype(jnp.float32)
+            square = real * real + imag * imag
+            magnitude = square * lax.rsqrt(jnp.maximum(square, 1e-30))
+            mag_ref[pl.ds(pl.multiple_of(base + row, step), step), :] = magnitude
+            total += jnp.sum(magnitude.reshape(step // 8, 8, chans), axis=0)
+    level = jnp.sum(total, axis=0, keepdims=True) * (1.0 / freqs)
     floor = 0.5 * (level + 1e-05)
+
+    for partner, spec_ref in zip(order, spec_refs):
+        base = (me ^ partner) * band
+        for row in range(0, band, step):
+            held = pl.ds(pl.multiple_of(base + row, step), step)
+            factor = pl.reciprocal(mag_ref[held, :] + floor, approx=True)
+            for part in range(2):
+                value = spec_ref[part, row : row + step, :].astype(jnp.float32) * factor
+                white_ref[part, held, :] = value.astype(jnp.bfloat16)
+
+    lane = lax.broadcasted_iota(jnp.int32, (1, chans), 1)
+    line = lax.broadcasted_iota(jnp.int32, (lag_rows, chans), 0)
     usable = qual_ref[pl.ds(me, 1), :].astype(jnp.float32)
-
-    for partner, spec_ref in zip(order, spec_refs):
-
-        def whiten(index, carry, spec_ref=spec_ref, base=(me ^ partner) * band):
-            rows = pl.ds(pl.multiple_of(index * step, step), step)
-            held = pl.ds(pl.multiple_of(base + index * step, step), step)
-            factor = usable / (mag_ref[held, :] + floor)
-            for part in range(2):
-                value = spec_ref[part, rows, :].astype(jnp.float32) * factor
-                white_ref[part, held, :] = value.astype(jnp.bfloat16).astype(jnp.float32)
-            return carry
-
-        lax.fori_loop(0, band // step, whiten, 0, unroll=True)
-
-    lane = lax.broadcasted_iota(jnp.int32, (1, chans), 1)
-    row = lax.broadcasted_iota(jnp.int32, (lag_rows, chans), 0)
     levels = jnp.zeros((lag_rows, chans), jnp.float32)
-    scale = 1.0 / math.sqrt(freqs)
     table = jnp.concatenate([table_ref[side, me ^ k] for side in range(2) for k in order], axis=0)
     for number in range(offset_count):
-        ahead = offs_ref[number] * (chans // chan_count)
-        turn = chans - ahead
-
-        def cross(index, carry):
-            held = pl.ds(pl.multiple_of(index * step, step), step)
-            own_real, own_imag = white_ref[0, held, :], white_ref[1, held, :]
-            far_real = pltpu.roll(own_real, turn, 1)
-            far_imag = pltpu.roll(own_imag, turn, 1)
-            cross_ref[held, pl.ds(0, chans)] = (own_real * far_real + own_imag * far_imag).astype(jnp.bfloat16)
-            cross_ref[held, pl.ds(chans, chans)] = (own_imag * far_real - own_real * far_imag).astype(jnp.bfloat16)
-            return carry
-
-        lax.fori_loop(0, freqs // step, cross, 0, unroll=4)
-        sums = jnp.dot(table, cross_ref[...], preferred_element_type=jnp.float32)
-        keep = jnp.where(lane < turn, scale, 0.0)
-        cos_real, sin_real = sums[:half, :chans] * keep, sums[half:, :chans] * keep
-        cos_imag, sin_imag = sums[:half, chans:] * keep, sums[half:, chans:] * keep
+        turn = chans - offs_ref[number] * (chans // chan_count)
+        slot = number % 2
+        for row in range(0, freqs, step):
+            own = [white_ref[part, row : row + step, :] for part in range(2)]
+            far_real, far_imag = (pltpu.roll(value, turn, 1).astype(jnp.float32) for value in own)
+            own_real, own_imag = (value.astype(jnp.float32) for value in own)
+            real = own_real * far_real + own_imag * far_imag
+            imag = own_imag * far_real - own_real * far_imag
+            cross_ref[slot, row : row + step, 0:chans] = real.astype(jnp.bfloat16)
+            cross_ref[slot, row : row + step, chans : 2 * chans] = imag.astype(jnp.bfloat16)
+        sums = jnp.dot(table, cross_ref[slot], preferred_element_type=jnp.float32)
+        cos_real, sin_real = sums[:half, :chans], sums[half:, :chans]
+        cos_imag, sin_imag = sums[:half, chans:], sums[half:, chans:]
         corr = (
             (cos_real - sin_imag, sin_real + cos_imag),
             (cos_real + sin_imag, cos_imag - sin_real),
         )
         power = [real * real + imag * imag for real, imag in corr]
-        mean_power = (jnp.sum(power[0], axis=0, keepdims=True) + jnp.sum(power[1], axis=0, keepdims=True)) / (2 * half)
-        extra = 0.25 * (mean_power + 1e-06)
+        mean_power = jnp.sum(power[0] + power[1], axis=0, keepdims=True) * (1.0 / (2 * half))
+        extra = 0.25 * (mean_power + 1e-06 * freqs)
         peak = jnp.max(jnp.maximum(jnp.abs(corr[0][0]), jnp.abs(corr[1][0])), axis=0, keepdims=True)
         code = level_code(peak)
-        levels = jnp.where(row == number, code, levels)
-        upscale = 1.0 / level_of(code)
+        levels = jnp.where(line == number, code, levels)
+        keep = jnp.where(lane < turn, usable * pltpu.roll(usable, turn, 1), 0.0) * CODE_TOP
+        upscale = keep / level_of(code)
         for side in range(2):
-            inverse = 1.0 / jnp.sqrt(power[side] + extra)
+            inverse = lax.rsqrt(power[side] + extra) * keep
             real, imag = corr[side]
             for kind, value in enumerate((real * upscale, real * inverse, imag * inverse)):
                 coded = encode(value).reshape(chan_count, lag_rows, chans)
                 for k in range(chan_count):
                     out_refs[k][6 * number + 2 * kind + side, :, :] = coded[k]
     for k in range(chan_count):
-        out_refs[k][blocks - 1, :, :] = levels.astype(jnp.int32).astype(jnp.int16)
-
-
-def sum_kernel(order, where_ref, *refs):
+        out_refs[k][blocks - 1, :, :] = encode(levels)
+
+
+def sum_kernel(order, scale, where_ref, *refs):
     code_refs, out_refs = refs[: -len(order)], refs[-len(order) :]
     blocks = code_refs[0].shape[0]
-    levels = [level_of(decode(codes_ref[blocks - 1])) / CODE_TOP for codes_ref in code_refs]
+    levels = [level_of(decode(codes_ref[blocks - 1])) * scale for codes_ref in code_refs]
     row = lax.broadcasted_iota(jnp.int32, levels[0].shape, 0)
     for k, out_ref in zip(order, out_refs):
         number = where_ref[0] ^ k
@@ -238,7 +228,7 @@
     pieces = pl.pallas_call(
         functools.partial(split_kernel, chan_order),
         out_shape=[jax.ShapeDtypeStruct((2, band, chans), spectra.dtype)] * chan_count,
-        in_specs=[smem, pl.BlockSpec(memory_space=pl.ANY)],
+        in_specs=[smem, pl.BlockSpec(memory_space=pltpu.HBM)],
         out_specs=[pl.BlockSpec(memory_space=pl.ANY)] * chan_count,
         scratch_shapes=[pltpu.SemaphoreType.DMA((chan_count,))],
         compiler_params=params,
@@ -251,14 +241,14 @@
         out_specs=[vmem] * chan_count,
         scratch_shapes=[
             pltpu.VMEM((freqs, chans), jnp.float32),
-            pltpu.VMEM((2, freqs, chans), jnp.float32),
-            pltpu.VMEM((freqs, 2 * chans), jnp.bfloat16),
+            pltpu.VMEM((2, freqs, chans), jnp.bfloat16),
+            pltpu.VMEM((2, freqs, 2 * chans), jnp.bfloat16),
         ],
         compiler_params=params,
         name="window_pairs",
     )(offsets, chan_where, *exchange(pieces, "chan"), quality, table)
     sums = pl.pallas_call(
-        functools.partial(sum_kernel, tm_order),
+        functools.partial(sum_kernel, tm_order, 1.0 / (CODE_TOP * math.sqrt(freqs))),
         out_shape=[jax.ShapeDtypeStruct((6, lag_rows, chans), jnp.float32)] * tm_count,
         in_specs=[smem] + [vmem] * chan_count,
         out_specs=[vmem] * tm_count,

time: 63.7 us -> 58.4 us (0.917)
  Pallas kernels: 12 us -> 6.78 us
    pallas_call x1, Pallas kernels: 9.13 us -> 3.87 us  [window_shards(): pl.pallas_call(functools.partial(window_kernel, chan_order), out_shape=[j...]
where the time goes in v5:
time: 58.4 us; the launch traced here: 58.2 us
  waiting for transfers between devices  19.8 us (34%)
  starting transfers between devices  17.7 us (30%)
  blocking collectives  12.6 us (22%)
  Pallas kernels  6.78 us (12%)
  local copies, waits for them, and re-layouts  1.24 us (2%)
    ppermute x17, waiting for transfers between devices, exchange(): lax.ppermute(piece, axis, [(source, source ^ k) for source in range(count)])  19.8 us
    ppermute x17, starting transfers between devices, exchange(): lax.ppermute(piece, axis, [(source, source ^ k) for source in range(count)])  17.7 us
    all_to_all x1, blocking collectives, window_shards(): lax.all_to_all(pieces.reshape(shape), ('chan', 'tm'), 0, 0, tiled=True)  12.6 us
    pallas_call x1, Pallas kernels, window_shards(): pl.pallas_call(functools.partial(window_kernel, chan_order), out_shape=[j...  3.87 us
    unnamed x8, local copies, waits for them, and re-layouts  1.24 us
    pallas_call x1, Pallas kernels, window_shards(): pl.pallas_call(place_kernel, out_shape=jax.ShapeDtypeStruct((CH_DEV, offs...  1.22 us
  transfers between devices with their start and end apart: 17, of which 12 were waited for; matrix products, arithmetic and copies ran while one was open for 0% of the time, Pallas kernels for 0%

profile of v5, /device:TPU:0, one launch (start us, length us, event | category | flops | bytes accessed | tf_op | source)
XLA Modules:
  0.0 58.2 jit_solution(8982565919811011239)
XLA Ops:
  0.0 1.2 %copy-done = bf16[2,8,256,128]{3,2,1,0:T(8,128)(2,1)S(1)} copy-done((bf16[2,8,256,128]{3,2,1,0:T(8,128)(2,1)S(1)}, bf16[2,8,256,128]{3,2,1,0:T(8,128)(2,1)}, u32[]{:S(2)}) %copy-start) | copy-done | bytes 1048600
  1.2 0.7 %split_windows.1 = (bf16[2,256,128]{2,1,0:T(8,128)(2,1)S(1)}, bf16[2,256,128]{2,1,0:T(8,128)(2,1)S(1)}, bf16[2,256,128]{2,1,0:T(8,128)(2,1)S(1)}, bf16[2,256,128...) custom-call(s32[1]{0:T(128)} %bitcast.1.where_ref, ...), custom_call_target="tpu_custom_call" | custom-call | tf_op jit(solution)/shard_map/split_windows/pallas_call | solution.py:228
  2.0 4.0 %collective-permute-start = (bf16[2,256,128]{2,1,0:T(8,128)(2,1)S(1)}, bf16[2,256,128]{2,1,0:T(8,128)(2,1)S(1)}, u32[]{:S(2)}, u32[]{:S(2)}) collective-permute-start(bf16[2,256,128]{2,1,0:T(8,128)(2,1)S(1)} %get-tuple-element.25), channel_id=1, source_target_pairs={{0,24},{4,28},{8,16},{12,20},{16,8},{20,12},{24,0},{28,4},{1,25},{... | collective-permute-start | bytes 393224 | tf_op jit(solution)/shard_map/ppermute | solution.py:147
  5.9 1.1 %collective-permute-start.2 = (bf16[2,256,128]{2,1,0:T(8,128)(2,1)S(1)}, bf16[2,256,128]{2,1,0:T(8,128)(2,1)S(1)}, u32[]{:S(2)}, u32[]{:S(2)}) collective-permute-start(bf16[2,256,128]{2,1,0:T(8,128)(2,1)S(1)} %get-tuple-element.27), channel_id=1, source_target_pairs={{0,8},{4,12},{8,0},{12,4},{16,24},{20,28},{24,16},{28,20},{1,9},{5... | collective-permute-start | bytes 393224 | tf_op jit(solution)/shard_map/ppermute | solution.py:147
  7.1 1.5 %collective-permute-start.3 = (bf16[2,256,128]{2,1,0:T(8,128)(2,1)S(1)}, bf16[2,256,128]{2,1,0:T(8,128)(2,1)S(1)}, u32[]{:S(2)}, u32[]{:S(2)}) collective-permute-start(bf16[2,256,128]{2,1,0:T(8,128)(2,1)S(1)} %get-tuple-element.28), channel_id=1, source_target_pairs={{0,16},{4,20},{8,24},{12,28},{16,0},{20,4},{24,8},{28,12},{1,17},{... | collective-permute-start | bytes 393224 | tf_op jit(solution)/shard_map/ppermute | solution.py:147
  9.8 2.8 %collective-permute-done.1.refs_1_ = bf16[2,256,128]{2,1,0:T(8,128)(2,1)S(1)} collective-permute-done((bf16[2,256,128]{2,1,0:T(8,128)(2,1)S(1)}, bf16[2,256,128]{2,1,0:T(8,128)(2,1)S(1)}, u32[]{:S(2)}, u32[]{:S(2)}) %collective-permute-start.1) | collective-permute-done | bytes 131104 | tf_op jit(solution)/shard_map/ppermute | solution.py:147
  12.7 3.4 %collective-permute-done.2.refs_2_ = bf16[2,256,128]{2,1,0:T(8,128)(2,1)S(1)} collective-permute-done((bf16[2,256,128]{2,1,0:T(8,128)(2,1)S(1)}, bf16[2,256,128]{2,1,0:T(8,128)(2,1)S(1)}, u32[]{:S(2)}, u32[]{:S(2)}) %collective-permute-start.2) | collective-permute-done | bytes 131104 | tf_op jit(solution)/shard_map/ppermute | solution.py:147
  16.1 1.1 %collective-permute-done.4.refs_4_ = bf16[2,256,128]{2,1,0:T(8,128)(2,1)S(1)} collective-permute-done((bf16[2,256,128]{2,1,0:T(8,128)(2,1)S(1)}, bf16[2,256,128]{2,1,0:T(8,128)(2,1)S(1)}, u32[]{:S(2)}, u32[]{:S(2)}) %collective-permute-start.4) | collective-permute-done | bytes 131104 | tf_op jit(solution)/shard_map/ppermute | solution.py:147
  17.3 0.7 %collective-permute-done.5.refs_5_ = bf16[2,256,128]{2,1,0:T(8,128)(2,1)S(1)} collective-permute-done((bf16[2,256,128]{2,1,0:T(8,128)(2,1)S(1)}, bf16[2,256,128]{2,1,0:T(8,128)(2,1)S(1)}, u32[]{:S(2)}, u32[]{:S(2)}) %collective-permute-start.5) | collective-permute-done | bytes 131104 | tf_op jit(solution)/shard_map/ppermute | solution.py:147
  18.0 3.9 %window_pairs.1 = (s16[25,16,128]{2,1,0:T(8,128)(2,1)S(1)}, s16[25,16,128]{2,1,0:T(8,128)(2,1)S(1)}, s16[25,16,128]{2,1,0:T(8,128)(2,1)S(1)}, s16[25,16,128]{2,1...) custom-call(s32[4]{0:T(128)S(1)} %copy-done.3, ...), custom_call_target="tpu_custom_call" | custom-call | tf_op jit(solution)/shard_map/window_pairs/pallas_call | solution.py:237
  21.9 2.6 %collective-permute-start.7 = (s16[25,16,128]{2,1,0:T(8,128)(2,1)S(1)}, s16[25,16,128]{2,1,0:T(8,128)(2,1)S(1)}, u32[]{:S(2)}, u32[]{:S(2)}) collective-permute-start(s16[25,16,128]{2,1,0:T(8,128)(2,1)S(1)} %get-tuple-element.33), channel_id=1, source_target_pairs={{0,24},{4,28},{8,16},{12,20},{16,8},{20,12},{24,0},{28,4},{1,25},{... | collective-permute-start | bytes 307208 | tf_op jit(solution)/shard_map/ppermute | solution.py:147
  24.4 1.4 %collective-permute-start.9 = (s16[25,16,128]{2,1,0:T(8,128)(2,1)S(1)}, s16[25,16,128]{2,1,0:T(8,128)(2,1)S(1)}, u32[]{:S(2)}, u32[]{:S(2)}) collective-permute-start(s16[25,16,128]{2,1,0:T(8,128)(2,1)S(1)} %get-tuple-element.35), channel_id=1, source_target_pairs={{0,8},{4,12},{8,0},{12,4},{16,24},{20,28},{24,16},{28,20},{1,9},{5... | collective-permute-start | bytes 307208 | tf_op jit(solution)/shard_map/ppermute | solution.py:147
  25.8 1.6 %collective-permute-start.10 = (s16[25,16,128]{2,1,0:T(8,128)(2,1)S(1)}, s16[25,16,128]{2,1,0:T(8,128)(2,1)S(1)}, u32[]{:S(2)}, u32[]{:S(2)}) collective-permute-start(s16[25,16,128]{2,1,0:T(8,128)(2,1)S(1)} %get-tuple-element.36), channel_id=1, source_target_pairs={{0,16},{4,20},{8,24},{12,28},{16,0},{20,4},{24,8},{28,12},{1,17},{... | collective-permute-start | bytes 307208 | tf_op jit(solution)/shard_map/ppermute | solution.py:147
  28.2 2.4 %collective-permute-done.8.refs_1_ = s16[25,16,128]{2,1,0:T(8,128)(2,1)S(1)} collective-permute-done((s16[25,16,128]{2,1,0:T(8,128)(2,1)S(1)}, s16[25,16,128]{2,1,0:T(8,128)(2,1)S(1)}, u32[]{:S(2)}, u32[]{:S(2)}) %collective-permute-start.8) | collective-permute-done | bytes 102432 | tf_op jit(solution)/shard_map/ppermute | solution.py:147
  30.6 2.2 %collective-permute-done.9.refs_2_ = s16[25,16,128]{2,1,0:T(8,128)(2,1)S(1)} collective-permute-done((s16[25,16,128]{2,1,0:T(8,128)(2,1)S(1)}, s16[25,16,128]{2,1,0:T(8,128)(2,1)S(1)}, u32[]{:S(2)}, u32[]{:S(2)}) %collective-permute-start.9) | collective-permute-done | bytes 102432 | tf_op jit(solution)/shard_map/ppermute | solution.py:147
  32.8 1.0 %collective-permute-done.11.refs_4_ = s16[25,16,128]{2,1,0:T(8,128)(2,1)S(1)} collective-permute-done((s16[25,16,128]{2,1,0:T(8,128)(2,1)S(1)}, s16[25,16,128]{2,1,0:T(8,128)(2,1)S(1)}, u32[]{:S(2)}, u32[]{:S(2)}) %collective-permute-start.11) | collective-permute-done | bytes 102432 | tf_op jit(solution)/shard_map/ppermute | solution.py:147
  33.9 1.0 %collective-permute-done.12.refs_5_ = s16[25,16,128]{2,1,0:T(8,128)(2,1)S(1)} collective-permute-done((s16[25,16,128]{2,1,0:T(8,128)(2,1)S(1)}, s16[25,16,128]{2,1,0:T(8,128)(2,1)S(1)}, u32[]{:S(2)}, u32[]{:S(2)}) %collective-permute-start.12) | collective-permute-done | bytes 102432 | tf_op jit(solution)/shard_map/ppermute | solution.py:147
  35.1 2.7 %collective-permute-start.14 = (f32[6,16,128]{2,1,0:T(8,128)S(1)}, f32[6,16,128]{2,1,0:T(8,128)S(1)}, u32[]{:S(2)}, u32[]{:S(2)}) collective-permute-start(f32[6,16,128]{2,1,0:T(8,128)S(1)} %get-tuple-element.41), channel_id=1, source_target_pairs={{0,2},{1,3},{2,0},{3,1},{4,6},{5,7},{6,4},{7,5},{8,10},{9,11},{10,... | collective-permute-start | bytes 147464 | tf_op jit(solution)/shard_map/ppermute | solution.py:147
  37.7 1.3 %collective-permute-start.15 = (f32[6,16,128]{2,1,0:T(8,128)S(1)}, f32[6,16,128]{2,1,0:T(8,128)S(1)}, u32[]{:S(2)}, u32[]{:S(2)}) collective-permute-start(f32[6,16,128]{2,1,0:T(8,128)S(1)} %get-tuple-element.42), channel_id=1, source_target_pairs={{0,3},{1,2},{2,1},{3,0},{4,7},{5,6},{6,5},{7,4},{8,11},{9,10},{10,... | collective-permute-start | bytes 147464 | tf_op jit(solution)/shard_map/ppermute | solution.py:147
  39.3 1.9 %collective-permute-done.14.refs_0_ = f32[6,16,128]{2,1,0:T(8,128)S(1)} collective-permute-done((f32[6,16,128]{2,1,0:T(8,128)S(1)}, f32[6,16,128]{2,1,0:T(8,128)S(1)}, u32[]{:S(2)}, u32[]{:S(2)}) %collective-permute-start.14) | collective-permute-done | bytes 49184 | tf_op jit(solution)/shard_map/ppermute | solution.py:147
  41.2 2.5 %collective-permute-done.15.refs_1_ = f32[6,16,128]{2,1,0:T(8,128)S(1)} collective-permute-done((f32[6,16,128]{2,1,0:T(8,128)S(1)}, f32[6,16,128]{2,1,0:T(8,128)S(1)}, u32[]{:S(2)}, u32[]{:S(2)}) %collective-permute-start.15) | collective-permute-done | bytes 49184 | tf_op jit(solution)/shard_map/ppermute | solution.py:147
  43.7 0.7 %stack_pairs.1 = f32[8,4,8,128]{3,2,1,0:T(8,128)S(1)} custom-call(s32[4]{0:T(128)S(1)} %copy-done.3, s32[1]{0:T(128)} %bitcast.where_ref, f32[6,16,128]{2,1,0:T(8,128)S(1)} %collective-permute-done.14.refs_0_, f32[6,16,128]{2,1,0:T(8,128)S(1)} %collective-permute-done.15.refs_1_, f32[6,16,128]{2,1,0:T(8,128)S(1)} %collective-permute-done.16.refs_2_, ...), custom_call_target="tpu_custom_call" | custom-call | tf_op jit(solution)/shard_map/stack_pairs/pallas_call | solution.py:258
  44.4 12.6 %all_to_all.5 = f32[32,8,128]{2,1,0:T(8,128)S(1)} all-to-all(f32[32,8,128]{2,1,0:T(8,128)S(1)} %bitcast.4), channel_id=1, replica_groups=mesh['chan'=8,'tm'=4] {'chan','tm'}, dimensions={0} | all-to-all | bytes 262144 | tf_op jit(solution)/shard_map/all_to_all | solution.py:267
  57.0 1.2 %place_lags.1 = f32[16,4,256]{2,1,0:T(4,128)} custom-call(f32[8,4,8,128]{3,2,1,0:T(8,128)S(1)} %bitcast.5), custom_call_target="tpu_custom_call" | custom-call | tf_op jit(solution)/shard_map/place_lags/pallas_call | solution.py:268
  (24 shorter events, 2.6 us)
Async XLA Ops:
  0.0 1.2 %copy-start = (bf16[2,8,256,128]{3,2,1,0:T(8,128)(2,1)S(1)}, bf16[2,8,256,128]{3,2,1,0:T(8,128)(2,1)}, u32[]{:S(2)}) copy-start(bf16[2,8,256,128]{3,2,1,0:T(8,128)(2,1)} %spec_ref.1) | copy-start | bytes 3145732
  1.2 16.7 %copy-start.1 = (bf16[2,8,16,2048]{3,2,1,0:T(8,128)(2,1)S(1)}, bf16[2,8,16,2048]{3,2,1,0:T(8,128)(2,1)}, u32[]{:S(2)}) copy-start(bf16[2,8,16,2048]{3,2,1,0:T(8,128)(2,1)} %constant.11.clone.refs_9_) | copy-start | bytes 3145732
  2.0 7.9 %collective-permute-start = (bf16[2,256,128]{2,1,0:T(8,128)(2,1)S(1)}, bf16[2,256,128]{2,1,0:T(8,128)(2,1)S(1)}, u32[]{:S(2)}, u32[]{:S(2)}) collective-permute-start(bf16[2,256,128]{2,1,0:T(8,128)(2,1)S(1)} %get-tuple-element.25), channel_id=1, source_target_pairs={{0,24},{4,28},{8,16},{12,20},{16,8},{20,12},{24,0},{28,4},{1,25},{... | collective-permute-start | bytes 393224 | tf_op jit(solution)/shard_map/ppermute | solution.py:147
  5.9 6.8 %collective-permute-start.1 = (bf16[2,256,128]{2,1,0:T(8,128)(2,1)S(1)}, bf16[2,256,128]{2,1,0:T(8,128)(2,1)S(1)}, u32[]{:S(2)}, u32[]{:S(2)}) collective-permute-start(bf16[2,256,128]{2,1,0:T(8,128)(2,1)S(1)} %get-tuple-element.26), channel_id=1, source_target_pairs={{0,28},{4,24},{8,20},{12,16},{16,12},{20,8},{24,4},{28,0},{1,29},{... | collective-permute-start | bytes 393224 | tf_op jit(solution)/shard_map/ppermute | solution.py:147
  5.9 10.2 %collective-permute-start.2 = (bf16[2,256,128]{2,1,0:T(8,128)(2,1)S(1)}, bf16[2,256,128]{2,1,0:T(8,128)(2,1)S(1)}, u32[]{:S(2)}, u32[]{:S(2)}) collective-permute-start(bf16[2,256,128]{2,1,0:T(8,128)(2,1)S(1)} %get-tuple-element.27), channel_id=1, source_target_pairs={{0,8},{4,12},{8,0},{12,4},{16,24},{20,28},{24,16},{28,20},{1,9},{5... | collective-permute-start | bytes 393224 | tf_op jit(solution)/shard_map/ppermute | solution.py:147
  7.1 10.9 %copy-start.2 = (s32[8,128]{1,0:T(8,128)S(1)}, s32[8,128]{1,0:T(8,128)}, u32[]{:S(2)}) copy-start(s32[8,128]{1,0:T(8,128)} %refs_8_.1) | copy-start | bytes 12292
  7.1 9.1 %collective-permute-start.3 = (bf16[2,256,128]{2,1,0:T(8,128)(2,1)S(1)}, bf16[2,256,128]{2,1,0:T(8,128)(2,1)S(1)}, u32[]{:S(2)}, u32[]{:S(2)}) collective-permute-start(bf16[2,256,128]{2,1,0:T(8,128)(2,1)S(1)} %get-tuple-element.28), channel_id=1, source_target_pairs={{0,16},{4,20},{8,24},{12,28},{16,0},{20,4},{24,8},{28,12},{1,17},{... | collective-permute-start | bytes 393224 | tf_op jit(solution)/shard_map/ppermute | solution.py:147
  8.6 8.7 %collective-permute-start.4 = (bf16[2,256,128]{2,1,0:T(8,128)(2,1)S(1)}, bf16[2,256,128]{2,1,0:T(8,128)(2,1)S(1)}, u32[]{:S(2)}, u32[]{:S(2)}) collective-permute-start(bf16[2,256,128]{2,1,0:T(8,128)(2,1)S(1)} %get-tuple-element.29), channel_id=1, source_target_pairs={{0,12},{4,8},{8,4},{12,0},{16,28},{20,24},{24,20},{28,16},{1,13},{... | collective-permute-start | bytes 393224 | tf_op jit(solution)/shard_map/ppermute | solution.py:147
  9.8 8.1 %collective-permute-start.5 = (bf16[2,256,128]{2,1,0:T(8,128)(2,1)S(1)}, bf16[2,256,128]{2,1,0:T(8,128)(2,1)S(1)}, u32[]{:S(2)}, u32[]{:S(2)}) collective-permute-start(bf16[2,256,128]{2,1,0:T(8,128)(2,1)S(1)} %get-tuple-element.30), channel_id=1, source_target_pairs={{0,20},{4,16},{8,28},{12,24},{16,4},{20,0},{24,12},{28,8},{1,21},{... | collective-permute-start | bytes 393224 | tf_op jit(solution)/shard_map/ppermute | solution.py:147
  12.7 5.3 %copy-start.3 = (s32[4]{0:T(128)S(1)}, s32[4]{0:T(128)}, u32[]{:S(2)}) copy-start(s32[4]{0:T(128)} %offs_ref.3) | copy-start | bytes 52
  12.7 5.3 %collective-permute-start.6 = (bf16[2,256,128]{2,1,0:T(8,128)(2,1)S(1)}, bf16[2,256,128]{2,1,0:T(8,128)(2,1)S(1)}, u32[]{:S(2)}, u32[]{:S(2)}) collective-permute-start(bf16[2,256,128]{2,1,0:T(8,128)(2,1)S(1)} %get-tuple-element.31), channel_id=1, source_target_pairs={{0,4},{4,0},{8,12},{12,8},{16,20},{20,16},{24,28},{28,24},{1,5},{5... | collective-permute-start | bytes 393224 | tf_op jit(solution)/shard_map/ppermute | solution.py:147
  21.9 5.9 %collective-permute-start.7 = (s16[25,16,128]{2,1,0:T(8,128)(2,1)S(1)}, s16[25,16,128]{2,1,0:T(8,128)(2,1)S(1)}, u32[]{:S(2)}, u32[]{:S(2)}) collective-permute-start(s16[25,16,128]{2,1,0:T(8,128)(2,1)S(1)} %get-tuple-element.33), channel_id=1, source_target_pairs={{0,24},{4,28},{8,16},{12,20},{16,8},{20,12},{24,0},{28,4},{1,25},{... | collective-permute-start | bytes 307208 | tf_op jit(solution)/shard_map/ppermute | solution.py:147
  24.4 6.2 %collective-permute-start.8 = (s16[25,16,128]{2,1,0:T(8,128)(2,1)S(1)}, s16[25,16,128]{2,1,0:T(8,128)(2,1)S(1)}, u32[]{:S(2)}, u32[]{:S(2)}) collective-permute-start(s16[25,16,128]{2,1,0:T(8,128)(2,1)S(1)} %get-tuple-element.34), channel_id=1, source_target_pairs={{0,28},{4,24},{8,20},{12,16},{16,12},{20,8},{24,4},{28,0},{1,29},{... | collective-permute-start | bytes 307208 | tf_op jit(solution)/shard_map/ppermute | solution.py:147
  24.4 8.4 %collective-permute-start.9 = (s16[25,16,128]{2,1,0:T(8,128)(2,1)S(1)}, s16[25,16,128]{2,1,0:T(8,128)(2,1)S(1)}, u32[]{:S(2)}, u32[]{:S(2)}) collective-permute-start(s16[25,16,128]{2,1,0:T(8,128)(2,1)S(1)} %get-tuple-element.35), channel_id=1, source_target_pairs={{0,8},{4,12},{8,0},{12,4},{16,24},{20,28},{24,16},{28,20},{1,9},{5... | collective-permute-start | bytes 307208 | tf_op jit(solution)/shard_map/ppermute | solution.py:147
  25.8 7.0 %collective-permute-start.10 = (s16[25,16,128]{2,1,0:T(8,128)(2,1)S(1)}, s16[25,16,128]{2,1,0:T(8,128)(2,1)S(1)}, u32[]{:S(2)}, u32[]{:S(2)}) collective-permute-start(s16[25,16,128]{2,1,0:T(8,128)(2,1)S(1)} %get-tuple-element.36), channel_id=1, source_target_pairs={{0,16},{4,20},{8,24},{12,28},{16,0},{20,4},{24,8},{28,12},{1,17},{... | collective-permute-start | bytes 307208 | tf_op jit(solution)/shard_map/ppermute | solution.py:147
  27.4 6.5 %collective-permute-start.11 = (s16[25,16,128]{2,1,0:T(8,128)(2,1)S(1)}, s16[25,16,128]{2,1,0:T(8,128)(2,1)S(1)}, u32[]{:S(2)}, u32[]{:S(2)}) collective-permute-start(s16[25,16,128]{2,1,0:T(8,128)(2,1)S(1)} %get-tuple-element.37), channel_id=1, source_target_pairs={{0,12},{4,8},{8,4},{12,0},{16,28},{20,24},{24,20},{28,16},{1,13},{... | collective-permute-start | bytes 307208 | tf_op jit(solution)/shard_map/ppermute | solution.py:147
  27.7 7.1 %collective-permute-start.12 = (s16[25,16,128]{2,1,0:T(8,128)(2,1)S(1)}, s16[25,16,128]{2,1,0:T(8,128)(2,1)S(1)}, u32[]{:S(2)}, u32[]{:S(2)}) collective-permute-start(s16[25,16,128]{2,1,0:T(8,128)(2,1)S(1)} %get-tuple-element.38), channel_id=1, source_target_pairs={{0,20},{4,16},{8,28},{12,24},{16,4},{20,0},{24,12},{28,8},{1,21},{... | collective-permute-start | bytes 307208 | tf_op jit(solution)/shard_map/ppermute | solution.py:147
  30.6 4.2 %collective-permute-start.13 = (s16[25,16,128]{2,1,0:T(8,128)(2,1)S(1)}, s16[25,16,128]{2,1,0:T(8,128)(2,1)S(1)}, u32[]{:S(2)}, u32[]{:S(2)}) collective-permute-start(s16[25,16,128]{2,1,0:T(8,128)(2,1)S(1)} %get-tuple-element.39), channel_id=1, source_target_pairs={{0,4},{4,0},{8,12},{12,8},{16,20},{20,16},{24,28},{28,24},{1,5},{5... | collective-permute-start | bytes 307208 | tf_op jit(solution)/shard_map/ppermute | solution.py:147
  35.1 6.1 %collective-permute-start.14 = (f32[6,16,128]{2,1,0:T(8,128)S(1)}, f32[6,16,128]{2,1,0:T(8,128)S(1)}, u32[]{:S(2)}, u32[]{:S(2)}) collective-permute-start(f32[6,16,128]{2,1,0:T(8,128)S(1)} %get-tuple-element.41), channel_id=1, source_target_pairs={{0,2},{1,3},{2,0},{3,1},{4,6},{5,7},{6,4},{7,5},{8,10},{9,11},{10,... | collective-permute-start | bytes 147464 | tf_op jit(solution)/shard_map/ppermute | solution.py:147
  37.7 6.0 %collective-permute-start.15 = (f32[6,16,128]{2,1,0:T(8,128)S(1)}, f32[6,16,128]{2,1,0:T(8,128)S(1)}, u32[]{:S(2)}, u32[]{:S(2)}) collective-permute-start(f32[6,16,128]{2,1,0:T(8,128)S(1)} %get-tuple-element.42), channel_id=1, source_target_pairs={{0,3},{1,2},{2,1},{3,0},{4,7},{5,6},{6,5},{7,4},{8,11},{9,10},{10,... | collective-permute-start | bytes 147464 | tf_op jit(solution)/shard_map/ppermute | solution.py:147
  39.1 4.6 %collective-permute-start.16 = (f32[6,16,128]{2,1,0:T(8,128)S(1)}, f32[6,16,128]{2,1,0:T(8,128)S(1)}, u32[]{:S(2)}, u32[]{:S(2)}) collective-permute-start(f32[6,16,128]{2,1,0:T(8,128)S(1)} %get-tuple-element.43), channel_id=1, source_target_pairs={{0,1},{1,0},{2,3},{3,2},{4,5},{5,4},{6,7},{7,6},{8,9},{9,8},{10,11... | collective-permute-start | bytes 147464 | tf_op jit(solution)/shard_map/ppermute | solution.py:147

commit v6 on v5

--- a/solution.py
+++ b/solution.py
@@ -233,7 +233,7 @@
         scratch_shapes=[pltpu.SemaphoreType.DMA((chan_count,))],
         compiler_params=params,
         name="split_windows",
-    )(chan_where, spectra)
+    )(chan_where, pltpu.with_memory_space_constraint(spectra, pltpu.HBM))
     pairs = pl.pallas_call(
         functools.partial(window_kernel, chan_order),
         out_shape=[jax.ShapeDtypeStruct((6 * offset_count + 1, lag_rows, chans), jnp.int16)] * chan_count,

time: 58.4 us -> 57.9 us (level)
  local copies, waits for them, and re-layouts: 1.24 us -> 0.01 us
  Pallas kernels: 6.78 us -> 7.47 us
    unnamed x8 -> x6, local copies, waits for them, and re-layouts: 1.24 us -> 0.01 us
    pallas_call x1, Pallas kernels: 0.74 us -> 1.43 us  [window_shards(): pl.pallas_call(functools.partial(split_kernel, chan_order), out_shape=[ja...]
where the time goes in v6:
time: 57.9 us; the launch traced here: 57.7 us
  waiting for transfers between devices  19.8 us (34%)
  starting transfers between devices  17.7 us (31%)
  blocking collectives  12.6 us (22%)
  Pallas kernels  7.47 us (13%)
    ppermute x17, waiting for transfers between devices, exchange(): lax.ppermute(piece, axis, [(source, source ^ k) for source in range(count)])  19.8 us
    ppermute x17, starting transfers between devices, exchange(): lax.ppermute(piece, axis, [(source, source ^ k) for source in range(count)])  17.7 us
    all_to_all x1, blocking collectives, window_shards(): lax.all_to_all(pieces.reshape(shape), ('chan', 'tm'), 0, 0, tiled=True)  12.6 us
    pallas_call x1, Pallas kernels, window_shards(): pl.pallas_call(functools.partial(window_kernel, chan_order), out_shape=[j...  3.87 us
    pallas_call x1, Pallas kernels, window_shards(): pl.pallas_call(functools.partial(split_kernel, chan_order), out_shape=[ja...  1.43 us
    pallas_call x1, Pallas kernels, window_shards(): pl.pallas_call(place_kernel, out_shape=jax.ShapeDtypeStruct((CH_DEV, offs...  1.22 us
  transfers between devices with their start and end apart: 17, of which 12 were waited for; matrix products, arithmetic and copies ran while one was open for 0% of the time, Pallas kernels for 0%

profile of v6, /device:TPU:0, one launch (start us, length us, event | category | flops | bytes accessed | tf_op | source)
XLA Modules:
  0.0 57.7 jit_solution(12920905328061907614)
XLA Ops:
  0.0 1.4 %split_windows.1 = (bf16[2,256,128]{2,1,0:T(8,128)(2,1)S(1)}, bf16[2,256,128]{2,1,0:T(8,128)(2,1)S(1)}, bf16[2,256,128]{2,1,0:T(8,128)(2,1)S(1)}, bf16[2,256,128...) custom-call(s32[1]{0:T(128)} %bitcast.1.where_ref, ...), custom_call_target="tpu_custom_call" | custom-call | tf_op jit(solution)/shard_map/split_windows/pallas_call | solution.py:228
  1.4 4.0 %collective-permute-start = (bf16[2,256,128]{2,1,0:T(8,128)(2,1)S(1)}, bf16[2,256,128]{2,1,0:T(8,128)(2,1)S(1)}, u32[]{:S(2)}, u32[]{:S(2)}) collective-permute-start(bf16[2,256,128]{2,1,0:T(8,128)(2,1)S(1)} %get-tuple-element.25), channel_id=1, source_target_pairs={{0,24},{4,28},{8,16},{12,20},{16,8},{20,12},{24,0},{28,4},{1,25},{... | collective-permute-start | bytes 393224 | tf_op jit(solution)/shard_map/ppermute | solution.py:147
  5.4 1.1 %collective-permute-start.2 = (bf16[2,256,128]{2,1,0:T(8,128)(2,1)S(1)}, bf16[2,256,128]{2,1,0:T(8,128)(2,1)S(1)}, u32[]{:S(2)}, u32[]{:S(2)}) collective-permute-start(bf16[2,256,128]{2,1,0:T(8,128)(2,1)S(1)} %get-tuple-element.27), channel_id=1, source_target_pairs={{0,8},{4,12},{8,0},{12,4},{16,24},{20,28},{24,16},{28,20},{1,9},{5... | collective-permute-start | bytes 393224 | tf_op jit(solution)/shard_map/ppermute | solution.py:147
  6.5 1.5 %collective-permute-start.3 = (bf16[2,256,128]{2,1,0:T(8,128)(2,1)S(1)}, bf16[2,256,128]{2,1,0:T(8,128)(2,1)S(1)}, u32[]{:S(2)}, u32[]{:S(2)}) collective-permute-start(bf16[2,256,128]{2,1,0:T(8,128)(2,1)S(1)} %get-tuple-element.28), channel_id=1, source_target_pairs={{0,16},{4,20},{8,24},{12,28},{16,0},{20,4},{24,8},{28,12},{1,17},{... | collective-permute-start | bytes 393224 | tf_op jit(solution)/shard_map/ppermute | solution.py:147
  8.6 0.7 %collective-permute-done.refs_0_ = bf16[2,256,128]{2,1,0:T(8,128)(2,1)S(1)} collective-permute-done((bf16[2,256,128]{2,1,0:T(8,128)(2,1)S(1)}, bf16[2,256,128]{2,1,0:T(8,128)(2,1)S(1)}, u32[]{:S(2)}, u32[]{:S(2)}) %collective-permute-start) | collective-permute-done | bytes 131104 | tf_op jit(solution)/shard_map/ppermute | solution.py:147
  9.3 2.8 %collective-permute-done.1.refs_1_ = bf16[2,256,128]{2,1,0:T(8,128)(2,1)S(1)} collective-permute-done((bf16[2,256,128]{2,1,0:T(8,128)(2,1)S(1)}, bf16[2,256,128]{2,1,0:T(8,128)(2,1)S(1)}, u32[]{:S(2)}, u32[]{:S(2)}) %collective-permute-start.1) | collective-permute-done | bytes 131104 | tf_op jit(solution)/shard_map/ppermute | solution.py:147
  12.2 3.4 %collective-permute-done.2.refs_2_ = bf16[2,256,128]{2,1,0:T(8,128)(2,1)S(1)} collective-permute-done((bf16[2,256,128]{2,1,0:T(8,128)(2,1)S(1)}, bf16[2,256,128]{2,1,0:T(8,128)(2,1)S(1)}, u32[]{:S(2)}, u32[]{:S(2)}) %collective-permute-start.2) | collective-permute-done | bytes 131104 | tf_op jit(solution)/shard_map/ppermute | solution.py:147
  15.6 1.1 %collective-permute-done.4.refs_4_ = bf16[2,256,128]{2,1,0:T(8,128)(2,1)S(1)} collective-permute-done((bf16[2,256,128]{2,1,0:T(8,128)(2,1)S(1)}, bf16[2,256,128]{2,1,0:T(8,128)(2,1)S(1)}, u32[]{:S(2)}, u32[]{:S(2)}) %collective-permute-start.4) | collective-permute-done | bytes 131104 | tf_op jit(solution)/shard_map/ppermute | solution.py:147
  16.7 0.7 %collective-permute-done.5.refs_5_ = bf16[2,256,128]{2,1,0:T(8,128)(2,1)S(1)} collective-permute-done((bf16[2,256,128]{2,1,0:T(8,128)(2,1)S(1)}, bf16[2,256,128]{2,1,0:T(8,128)(2,1)S(1)}, u32[]{:S(2)}, u32[]{:S(2)}) %collective-permute-start.5) | collective-permute-done | bytes 131104 | tf_op jit(solution)/shard_map/ppermute | solution.py:147
  17.4 3.9 %window_pairs.1 = (s16[25,16,128]{2,1,0:T(8,128)(2,1)S(1)}, s16[25,16,128]{2,1,0:T(8,128)(2,1)S(1)}, s16[25,16,128]{2,1,0:T(8,128)(2,1)S(1)}, s16[25,16,128]{2,1...) custom-call(s32[4]{0:T(128)S(1)} %copy-done.2, ...), custom_call_target="tpu_custom_call" | custom-call | tf_op jit(solution)/shard_map/window_pairs/pallas_call | solution.py:237
  21.3 2.6 %collective-permute-start.7 = (s16[25,16,128]{2,1,0:T(8,128)(2,1)S(1)}, s16[25,16,128]{2,1,0:T(8,128)(2,1)S(1)}, u32[]{:S(2)}, u32[]{:S(2)}) collective-permute-start(s16[25,16,128]{2,1,0:T(8,128)(2,1)S(1)} %get-tuple-element.33), channel_id=1, source_target_pairs={{0,24},{4,28},{8,16},{12,20},{16,8},{20,12},{24,0},{28,4},{1,25},{... | collective-permute-start | bytes 307208 | tf_op jit(solution)/shard_map/ppermute | solution.py:147
  23.9 1.4 %collective-permute-start.9 = (s16[25,16,128]{2,1,0:T(8,128)(2,1)S(1)}, s16[25,16,128]{2,1,0:T(8,128)(2,1)S(1)}, u32[]{:S(2)}, u32[]{:S(2)}) collective-permute-start(s16[25,16,128]{2,1,0:T(8,128)(2,1)S(1)} %get-tuple-element.35), channel_id=1, source_target_pairs={{0,8},{4,12},{8,0},{12,4},{16,24},{20,28},{24,16},{28,20},{1,9},{5... | collective-permute-start | bytes 307208 | tf_op jit(solution)/shard_map/ppermute | solution.py:147
  25.3 1.6 %collective-permute-start.10 = (s16[25,16,128]{2,1,0:T(8,128)(2,1)S(1)}, s16[25,16,128]{2,1,0:T(8,128)(2,1)S(1)}, u32[]{:S(2)}, u32[]{:S(2)}) collective-permute-start(s16[25,16,128]{2,1,0:T(8,128)(2,1)S(1)} %get-tuple-element.36), channel_id=1, source_target_pairs={{0,16},{4,20},{8,24},{12,28},{16,0},{20,4},{24,8},{28,12},{1,17},{... | collective-permute-start | bytes 307208 | tf_op jit(solution)/shard_map/ppermute | solution.py:147
  27.7 2.4 %collective-permute-done.8.refs_1_ = s16[25,16,128]{2,1,0:T(8,128)(2,1)S(1)} collective-permute-done((s16[25,16,128]{2,1,0:T(8,128)(2,1)S(1)}, s16[25,16,128]{2,1,0:T(8,128)(2,1)S(1)}, u32[]{:S(2)}, u32[]{:S(2)}) %collective-permute-start.8) | collective-permute-done | bytes 102432 | tf_op jit(solution)/shard_map/ppermute | solution.py:147
  30.1 2.2 %collective-permute-done.9.refs_2_ = s16[25,16,128]{2,1,0:T(8,128)(2,1)S(1)} collective-permute-done((s16[25,16,128]{2,1,0:T(8,128)(2,1)S(1)}, s16[25,16,128]{2,1,0:T(8,128)(2,1)S(1)}, u32[]{:S(2)}, u32[]{:S(2)}) %collective-permute-start.9) | collective-permute-done | bytes 102432 | tf_op jit(solution)/shard_map/ppermute | solution.py:147
  32.3 1.0 %collective-permute-done.11.refs_4_ = s16[25,16,128]{2,1,0:T(8,128)(2,1)S(1)} collective-permute-done((s16[25,16,128]{2,1,0:T(8,128)(2,1)S(1)}, s16[25,16,128]{2,1,0:T(8,128)(2,1)S(1)}, u32[]{:S(2)}, u32[]{:S(2)}) %collective-permute-start.11) | collective-permute-done | bytes 102432 | tf_op jit(solution)/shard_map/ppermute | solution.py:147
  33.3 1.0 %collective-permute-done.12.refs_5_ = s16[25,16,128]{2,1,0:T(8,128)(2,1)S(1)} collective-permute-done((s16[25,16,128]{2,1,0:T(8,128)(2,1)S(1)}, s16[25,16,128]{2,1,0:T(8,128)(2,1)S(1)}, u32[]{:S(2)}, u32[]{:S(2)}) %collective-permute-start.12) | collective-permute-done | bytes 102432 | tf_op jit(solution)/shard_map/ppermute | solution.py:147
  34.5 2.7 %collective-permute-start.14 = (f32[6,16,128]{2,1,0:T(8,128)S(1)}, f32[6,16,128]{2,1,0:T(8,128)S(1)}, u32[]{:S(2)}, u32[]{:S(2)}) collective-permute-start(f32[6,16,128]{2,1,0:T(8,128)S(1)} %get-tuple-element.41), channel_id=1, source_target_pairs={{0,2},{1,3},{2,0},{3,1},{4,6},{5,7},{6,4},{7,5},{8,10},{9,11},{10,... | collective-permute-start | bytes 147464 | tf_op jit(solution)/shard_map/ppermute | solution.py:147
  37.2 1.3 %collective-permute-start.15 = (f32[6,16,128]{2,1,0:T(8,128)S(1)}, f32[6,16,128]{2,1,0:T(8,128)S(1)}, u32[]{:S(2)}, u32[]{:S(2)}) collective-permute-start(f32[6,16,128]{2,1,0:T(8,128)S(1)} %get-tuple-element.42), channel_id=1, source_target_pairs={{0,3},{1,2},{2,1},{3,0},{4,7},{5,6},{6,5},{7,4},{8,11},{9,10},{10,... | collective-permute-start | bytes 147464 | tf_op jit(solution)/shard_map/ppermute | solution.py:147
  38.8 1.9 %collective-permute-done.14.refs_0_ = f32[6,16,128]{2,1,0:T(8,128)S(1)} collective-permute-done((f32[6,16,128]{2,1,0:T(8,128)S(1)}, f32[6,16,128]{2,1,0:T(8,128)S(1)}, u32[]{:S(2)}, u32[]{:S(2)}) %collective-permute-start.14) | collective-permute-done | bytes 49184 | tf_op jit(solution)/shard_map/ppermute | solution.py:147
  40.7 2.5 %collective-permute-done.15.refs_1_ = f32[6,16,128]{2,1,0:T(8,128)S(1)} collective-permute-done((f32[6,16,128]{2,1,0:T(8,128)S(1)}, f32[6,16,128]{2,1,0:T(8,128)S(1)}, u32[]{:S(2)}, u32[]{:S(2)}) %collective-permute-start.15) | collective-permute-done | bytes 49184 | tf_op jit(solution)/shard_map/ppermute | solution.py:147
  43.2 0.7 %stack_pairs.1 = f32[8,4,8,128]{3,2,1,0:T(8,128)S(1)} custom-call(s32[4]{0:T(128)S(1)} %copy-done.2, s32[1]{0:T(128)} %bitcast.where_ref, f32[6,16,128]{2,1,0:T(8,128)S(1)} %collective-permute-done.14.refs_0_, f32[6,16,128]{2,1,0:T(8,128)S(1)} %collective-permute-done.15.refs_1_, f32[6,16,128]{2,1,0:T(8,128)S(1)} %collective-permute-done.16.refs_2_, ...), custom_call_target="tpu_custom_call" | custom-call | tf_op jit(solution)/shard_map/stack_pairs/pallas_call | solution.py:258
  43.9 12.6 %all_to_all.5 = f32[32,8,128]{2,1,0:T(8,128)S(1)} all-to-all(f32[32,8,128]{2,1,0:T(8,128)S(1)} %bitcast.4), channel_id=1, replica_groups=mesh['chan'=8,'tm'=4] {'chan','tm'}, dimensions={0} | all-to-all | bytes 262144 | tf_op jit(solution)/shard_map/all_to_all | solution.py:267
  56.5 1.2 %place_lags.1 = f32[16,4,256]{2,1,0:T(4,128)} custom-call(f32[8,4,8,128]{3,2,1,0:T(8,128)S(1)} %bitcast.5), custom_call_target="tpu_custom_call" | custom-call | tf_op jit(solution)/shard_map/place_lags/pallas_call | solution.py:268
  (22 shorter events, 2.0 us)
Async XLA Ops:
  0.0 17.4 %copy-start = (bf16[2,8,16,2048]{3,2,1,0:T(8,128)(2,1)S(1)}, bf16[2,8,16,2048]{3,2,1,0:T(8,128)(2,1)}, u32[]{:S(2)}) copy-start(bf16[2,8,16,2048]{3,2,1,0:T(8,128)(2,1)} %constant.11.clone.refs_9_) | copy-start | bytes 3145732
  1.4 7.9 %collective-permute-start = (bf16[2,256,128]{2,1,0:T(8,128)(2,1)S(1)}, bf16[2,256,128]{2,1,0:T(8,128)(2,1)S(1)}, u32[]{:S(2)}, u32[]{:S(2)}) collective-permute-start(bf16[2,256,128]{2,1,0:T(8,128)(2,1)S(1)} %get-tuple-element.25), channel_id=1, source_target_pairs={{0,24},{4,28},{8,16},{12,20},{16,8},{20,12},{24,0},{28,4},{1,25},{... | collective-permute-start | bytes 393224 | tf_op jit(solution)/shard_map/ppermute | solution.py:147
  5.4 6.8 %collective-permute-start.1 = (bf16[2,256,128]{2,1,0:T(8,128)(2,1)S(1)}, bf16[2,256,128]{2,1,0:T(8,128)(2,1)S(1)}, u32[]{:S(2)}, u32[]{:S(2)}) collective-permute-start(bf16[2,256,128]{2,1,0:T(8,128)(2,1)S(1)} %get-tuple-element.26), channel_id=1, source_target_pairs={{0,28},{4,24},{8,20},{12,16},{16,12},{20,8},{24,4},{28,0},{1,29},{... | collective-permute-start | bytes 393224 | tf_op jit(solution)/shard_map/ppermute | solution.py:147
  5.4 10.2 %collective-permute-start.2 = (bf16[2,256,128]{2,1,0:T(8,128)(2,1)S(1)}, bf16[2,256,128]{2,1,0:T(8,128)(2,1)S(1)}, u32[]{:S(2)}, u32[]{:S(2)}) collective-permute-start(bf16[2,256,128]{2,1,0:T(8,128)(2,1)S(1)} %get-tuple-element.27), channel_id=1, source_target_pairs={{0,8},{4,12},{8,0},{12,4},{16,24},{20,28},{24,16},{28,20},{1,9},{5... | collective-permute-start | bytes 393224 | tf_op jit(solution)/shard_map/ppermute | solution.py:147
  6.5 10.9 %copy-start.1 = (s32[8,128]{1,0:T(8,128)S(1)}, s32[8,128]{1,0:T(8,128)}, u32[]{:S(2)}) copy-start(s32[8,128]{1,0:T(8,128)} %refs_8_.1) | copy-start | bytes 12292
  6.5 9.1 %collective-permute-start.3 = (bf16[2,256,128]{2,1,0:T(8,128)(2,1)S(1)}, bf16[2,256,128]{2,1,0:T(8,128)(2,1)S(1)}, u32[]{:S(2)}, u32[]{:S(2)}) collective-permute-start(bf16[2,256,128]{2,1,0:T(8,128)(2,1)S(1)} %get-tuple-element.28), channel_id=1, source_target_pairs={{0,16},{4,20},{8,24},{12,28},{16,0},{20,4},{24,8},{28,12},{1,17},{... | collective-permute-start | bytes 393224 | tf_op jit(solution)/shard_map/ppermute | solution.py:147
  8.1 8.7 %collective-permute-start.4 = (bf16[2,256,128]{2,1,0:T(8,128)(2,1)S(1)}, bf16[2,256,128]{2,1,0:T(8,128)(2,1)S(1)}, u32[]{:S(2)}, u32[]{:S(2)}) collective-permute-start(bf16[2,256,128]{2,1,0:T(8,128)(2,1)S(1)} %get-tuple-element.29), channel_id=1, source_target_pairs={{0,12},{4,8},{8,4},{12,0},{16,28},{20,24},{24,20},{28,16},{1,13},{... | collective-permute-start | bytes 393224 | tf_op jit(solution)/shard_map/ppermute | solution.py:147
  9.3 8.1 %collective-permute-start.5 = (bf16[2,256,128]{2,1,0:T(8,128)(2,1)S(1)}, bf16[2,256,128]{2,1,0:T(8,128)(2,1)S(1)}, u32[]{:S(2)}, u32[]{:S(2)}) collective-permute-start(bf16[2,256,128]{2,1,0:T(8,128)(2,1)S(1)} %get-tuple-element.30), channel_id=1, source_target_pairs={{0,20},{4,16},{8,28},{12,24},{16,4},{20,0},{24,12},{28,8},{1,21},{... | collective-permute-start | bytes 393224 | tf_op jit(solution)/shard_map/ppermute | solution.py:147
  12.2 5.3 %copy-start.2 = (s32[4]{0:T(128)S(1)}, s32[4]{0:T(128)}, u32[]{:S(2)}) copy-start(s32[4]{0:T(128)} %offs_ref.3) | copy-start | bytes 52
  12.2 5.3 %collective-permute-start.6 = (bf16[2,256,128]{2,1,0:T(8,128)(2,1)S(1)}, bf16[2,256,128]{2,1,0:T(8,128)(2,1)S(1)}, u32[]{:S(2)}, u32[]{:S(2)}) collective-permute-start(bf16[2,256,128]{2,1,0:T(8,128)(2,1)S(1)} %get-tuple-element.31), channel_id=1, source_target_pairs={{0,4},{4,0},{8,12},{12,8},{16,20},{20,16},{24,28},{28,24},{1,5},{5... | collective-permute-start | bytes 393224 | tf_op jit(solution)/shard_map/ppermute | solution.py:147
  21.3 5.9 %collective-permute-start.7 = (s16[25,16,128]{2,1,0:T(8,128)(2,1)S(1)}, s16[25,16,128]{2,1,0:T(8,128)(2,1)S(1)}, u32[]{:S(2)}, u32[]{:S(2)}) collective-permute-start(s16[25,16,128]{2,1,0:T(8,128)(2,1)S(1)} %get-tuple-element.33), channel_id=1, source_target_pairs={{0,24},{4,28},{8,16},{12,20},{16,8},{20,12},{24,0},{28,4},{1,25},{... | collective-permute-start | bytes 307208 | tf_op jit(solution)/shard_map/ppermute | solution.py:147
  23.9 6.2 %collective-permute-start.8 = (s16[25,16,128]{2,1,0:T(8,128)(2,1)S(1)}, s16[25,16,128]{2,1,0:T(8,128)(2,1)S(1)}, u32[]{:S(2)}, u32[]{:S(2)}) collective-permute-start(s16[25,16,128]{2,1,0:T(8,128)(2,1)S(1)} %get-tuple-element.34), channel_id=1, source_target_pairs={{0,28},{4,24},{8,20},{12,16},{16,12},{20,8},{24,4},{28,0},{1,29},{... | collective-permute-start | bytes 307208 | tf_op jit(solution)/shard_map/ppermute | solution.py:147
  23.9 8.4 %collective-permute-start.9 = (s16[25,16,128]{2,1,0:T(8,128)(2,1)S(1)}, s16[25,16,128]{2,1,0:T(8,128)(2,1)S(1)}, u32[]{:S(2)}, u32[]{:S(2)}) collective-permute-start(s16[25,16,128]{2,1,0:T(8,128)(2,1)S(1)} %get-tuple-element.35), channel_id=1, source_target_pairs={{0,8},{4,12},{8,0},{12,4},{16,24},{20,28},{24,16},{28,20},{1,9},{5... | collective-permute-start | bytes 307208 | tf_op jit(solution)/shard_map/ppermute | solution.py:147
  25.3 7.0 %collective-permute-start.10 = (s16[25,16,128]{2,1,0:T(8,128)(2,1)S(1)}, s16[25,16,128]{2,1,0:T(8,128)(2,1)S(1)}, u32[]{:S(2)}, u32[]{:S(2)}) collective-permute-start(s16[25,16,128]{2,1,0:T(8,128)(2,1)S(1)} %get-tuple-element.36), channel_id=1, source_target_pairs={{0,16},{4,20},{8,24},{12,28},{16,0},{20,4},{24,8},{28,12},{1,17},{... | collective-permute-start | bytes 307208 | tf_op jit(solution)/shard_map/ppermute | solution.py:147
  26.8 6.5 %collective-permute-start.11 = (s16[25,16,128]{2,1,0:T(8,128)(2,1)S(1)}, s16[25,16,128]{2,1,0:T(8,128)(2,1)S(1)}, u32[]{:S(2)}, u32[]{:S(2)}) collective-permute-start(s16[25,16,128]{2,1,0:T(8,128)(2,1)S(1)} %get-tuple-element.37), channel_id=1, source_target_pairs={{0,12},{4,8},{8,4},{12,0},{16,28},{20,24},{24,20},{28,16},{1,13},{... | collective-permute-start | bytes 307208 | tf_op jit(solution)/shard_map/ppermute | solution.py:147
  27.2 7.1 %collective-permute-start.12 = (s16[25,16,128]{2,1,0:T(8,128)(2,1)S(1)}, s16[25,16,128]{2,1,0:T(8,128)(2,1)S(1)}, u32[]{:S(2)}, u32[]{:S(2)}) collective-permute-start(s16[25,16,128]{2,1,0:T(8,128)(2,1)S(1)} %get-tuple-element.38), channel_id=1, source_target_pairs={{0,20},{4,16},{8,28},{12,24},{16,4},{20,0},{24,12},{28,8},{1,21},{... | collective-permute-start | bytes 307208 | tf_op jit(solution)/shard_map/ppermute | solution.py:147
  30.1 4.2 %collective-permute-start.13 = (s16[25,16,128]{2,1,0:T(8,128)(2,1)S(1)}, s16[25,16,128]{2,1,0:T(8,128)(2,1)S(1)}, u32[]{:S(2)}, u32[]{:S(2)}) collective-permute-start(s16[25,16,128]{2,1,0:T(8,128)(2,1)S(1)} %get-tuple-element.39), channel_id=1, source_target_pairs={{0,4},{4,0},{8,12},{12,8},{16,20},{20,16},{24,28},{28,24},{1,5},{5... | collective-permute-start | bytes 307208 | tf_op jit(solution)/shard_map/ppermute | solution.py:147
  34.5 6.1 %collective-permute-start.14 = (f32[6,16,128]{2,1,0:T(8,128)S(1)}, f32[6,16,128]{2,1,0:T(8,128)S(1)}, u32[]{:S(2)}, u32[]{:S(2)}) collective-permute-start(f32[6,16,128]{2,1,0:T(8,128)S(1)} %get-tuple-element.41), channel_id=1, source_target_pairs={{0,2},{1,3},{2,0},{3,1},{4,6},{5,7},{6,4},{7,5},{8,10},{9,11},{10,... | collective-permute-start | bytes 147464 | tf_op jit(solution)/shard_map/ppermute | solution.py:147
  37.2 6.0 %collective-permute-start.15 = (f32[6,16,128]{2,1,0:T(8,128)S(1)}, f32[6,16,128]{2,1,0:T(8,128)S(1)}, u32[]{:S(2)}, u32[]{:S(2)}) collective-permute-start(f32[6,16,128]{2,1,0:T(8,128)S(1)} %get-tuple-element.42), channel_id=1, source_target_pairs={{0,3},{1,2},{2,1},{3,0},{4,7},{5,6},{6,5},{7,4},{8,11},{9,10},{10,... | collective-permute-start | bytes 147464 | tf_op jit(solution)/shard_map/ppermute | solution.py:147
  38.5 4.6 %collective-permute-start.16 = (f32[6,16,128]{2,1,0:T(8,128)S(1)}, f32[6,16,128]{2,1,0:T(8,128)S(1)}, u32[]{:S(2)}, u32[]{:S(2)}) collective-permute-start(f32[6,16,128]{2,1,0:T(8,128)S(1)} %get-tuple-element.43), channel_id=1, source_target_pairs={{0,1},{1,0},{2,3},{3,2},{4,5},{5,4},{6,7},{7,6},{8,9},{9,8},{10,11... | collective-permute-start | bytes 147464 | tf_op jit(solution)/shard_map/ppermute | solution.py:147

commit v7 on v6

v7 whole, which is shorter than its diff:
```python
import functools
import math

import jax
import jax.numpy as jnp
import numpy as np
from jax import lax
from jax.experimental import pallas as pl
from jax.experimental.pallas import tpu as pltpu
from jax.sharding import PartitionSpec as P

F = 2048
LAGS = 256
NOFF = 4
CH_DEV = 16
W_DEV = 8
VMEM_LIMIT = 48 * 1024 * 1024
CODE_TOP = 32767.0
OCTAVE = 256.0
LOWEST = -110.0


def encode(value):
    return jnp.round(value).astype(jnp.int32).astype(jnp.int16)


def decode(code):
    return code.astype(jnp.int32).astype(jnp.float32)


def level_code(peak):
    return jnp.ceil(jnp.maximum(jnp.log2(jnp.maximum(peak, 1e-30)), LOWEST) * OCTAVE) + 1.0


def level_of(code):
    return jnp.exp2(code * (1.0 / OCTAVE))


def half_table(freq_count, lag_count):
    freq_index = np.arange(freq_count, dtype=np.int64)[None, :]
    double_lag = (2 * np.arange(lag_count // 2, lag_count, dtype=np.int64) - lag_count + 1)[:, None]
    turns = np.mod(freq_index * double_lag, 4 * freq_count).astype(np.float32)
    angles = turns * np.float32(2.0 * math.pi / (4 * freq_count))
    return np.concatenate([np.cos(angles), np.sin(angles)]).astype(jnp.bfloat16)


def window_kernel(order, offs_ref, where_ref, *refs):
    chan_count = len(order)
    spec_refs, (qual_ref, table_ref) = refs[:chan_count], refs[chan_count : chan_count + 2]
    out_refs = refs[chan_count + 2 : 2 * chan_count + 2]
    mag_ref, white_ref, cross_ref = refs[2 * chan_count + 2 :]
    me = where_ref[0]
    _, band, chans = spec_refs[0].shape
    freqs = chan_count * band
    blocks, block, half = out_refs[0].shape
    offset_count = offs_ref.shape[0]
    step = 64

    total = jnp.zeros((8, chans), jnp.float32)
    for number, spec_ref in enumerate(spec_refs):
        for row in range(0, band, step):
            real = spec_ref[0, row : row + step, :].astype(jnp.float32)
            imag = spec_ref[1, row : row + step, :].astype(jnp.float32)
            square = real * real + imag * imag
            magnitude = square * lax.rsqrt(jnp.maximum(square, 1e-30))
            mag_ref[number * band + row : number * band + row + step, :] = magnitude
            total += jnp.sum(magnitude.reshape(step // 8, 8, chans), axis=0)
    level = jnp.sum(total, axis=0, keepdims=True) * (1.0 / freqs)
    floor = 0.5 * (level + 1e-05)
    usable = qual_ref[pl.ds(me, 1), :].astype(jnp.float32)

    width = 128
    for number, spec_ref in enumerate(spec_refs):
        for row in range(0, band, width):
            start = number * band + row
            factor = usable * pl.reciprocal(mag_ref[start : start + width, :] + floor, approx=True)
            for part in range(2):
                value = spec_ref[part, row : row + width, :].astype(jnp.float32) * factor
                white_ref[part, 0:chans, start : start + width] = value.astype(jnp.bfloat16).T
    white_ref[:, chans:, :] = jnp.zeros((2, white_ref.shape[1] - chans, freqs), jnp.bfloat16)

    lane = lax.broadcasted_iota(jnp.int32, (1, half), 1)
    levels = jnp.zeros((chans, half), jnp.float32)
    table = jnp.concatenate([table_ref[me ^ k] for k in order], axis=0)
    span = min(512, freqs)
    for number in range(offset_count):
        slot = number % 2
        for place, k in enumerate(order):
            own_rows = pl.ds(pl.multiple_of((me ^ k) * block, block), block)
            far_rows = pl.ds(pl.multiple_of(((me ^ k) + offs_ref[number]) * block, block), block)
            for start in range(0, freqs, span):
                lanes = slice(start, start + span)
                own_real, own_imag = (white_ref[part, own_rows, lanes].astype(jnp.float32) for part in range(2))
                far_real, far_imag = (white_ref[part, far_rows, lanes].astype(jnp.float32) for part in range(2))
                real = own_real * far_real + own_imag * far_imag
                imag = own_imag * far_real - own_real * far_imag
                cross_ref[slot, place * block : (place + 1) * block, lanes] = real.astype(jnp.bfloat16)
                cross_ref[slot, chans + place * block : chans + (place + 1) * block, lanes] = imag.astype(jnp.bfloat16)
        sums = jnp.dot(cross_ref[slot], table, preferred_element_type=jnp.float32)
        cos_real, sin_real = sums[:chans, :half], sums[:chans, half:]
        cos_imag, sin_imag = sums[chans:, :half], sums[chans:, half:]
        corr = (
            (cos_real - sin_imag, sin_real + cos_imag),
            (cos_real + sin_imag, cos_imag - sin_real),
        )
        power = [real * real + imag * imag for real, imag in corr]
        mean_power = jnp.sum(power[0] + power[1], axis=1, keepdims=True) * (1.0 / (2 * half))
        extra = 0.25 * (mean_power + 1e-06 * freqs)
        peak = jnp.max(jnp.maximum(jnp.abs(corr[0][0]), jnp.abs(corr[1][0])), axis=1, keepdims=True)
        code = level_code(peak)
        levels = jnp.where(lane == number, code, levels)
        upscale = CODE_TOP / level_of(code)
        for side in range(2):
            inverse = lax.rsqrt(power[side] + extra) * CODE_TOP
            real, imag = corr[side]
            for kind, value in enumerate((real * upscale, real * inverse, imag * inverse)):
                coded = encode(value)
                for place, out_ref in enumerate(out_refs):
                    out_ref[6 * number + 2 * kind + side, :, :] = coded[place * block : (place + 1) * block]
    for place, out_ref in enumerate(out_refs):
        out_ref[blocks - 1, :, :] = encode(levels[place * block : (place + 1) * block])


def sum_kernel(order, scale, where_ref, *refs):
    code_refs, out_refs = refs[: -len(order)], refs[-len(order) :]
    blocks, _, half = code_refs[0].shape
    levels = [level_of(decode(codes_ref[blocks - 1])) * scale for codes_ref in code_refs]
    lane = lax.broadcasted_iota(jnp.int32, (1, half), 1)
    for k, out_ref in zip(order, out_refs):
        number = where_ref[0] ^ k
        own = [jnp.sum(jnp.where(lane == number, level, 0.0), axis=1, keepdims=True) for level in levels]
        linear = [
            sum(decode(codes_ref[6 * number + side]) * level for codes_ref, level in zip(code_refs, own))
            for side in range(2)
        ]
        peak = jnp.max(jnp.maximum(jnp.abs(linear[0]), jnp.abs(linear[1])), axis=1, keepdims=True)
        code = level_code(jnp.broadcast_to(peak, linear[0].shape))
        upscale = CODE_TOP / level_of(code)
        for side in range(2):
            out_ref[side, :, :] = encode(linear[side] * upscale)
        for part in range(2, 6):
            total = sum(decode(codes_ref[6 * number + part]) for codes_ref in code_refs)
            out_ref[part, :, :] = encode(total * (1.0 / len(code_refs)))
        out_ref[6, :, :] = encode(code)


def partners(count):
    return sorted(range(1, count), key=lambda k: (-(k >> 1).bit_count(), k & 1, k)) + [0]


def exchange(pieces, axis):
    count = lax.axis_size(axis)
    return [
        lax.ppermute(piece, axis, [(source, source ^ k) for source in range(count)]) if k else piece
        for k, piece in zip(partners(count), pieces)
    ]


def split_kernel(order, where_ref, spec_ref, *refs):
    out_refs, sems = refs[:-1], refs[-1]
    copies = [
        pltpu.make_async_copy(spec_ref.at[:, where_ref[0] ^ k], out_ref, sems.at[number])
        for number, (k, out_ref) in enumerate(zip(order, out_refs))
    ]
    for copy in copies:
        copy.start()
    for copy in copies:
        copy.wait()


def stack_kernel(windows, *refs):
    sums_refs, out_ref = refs[:-1], refs[-1]
    per_sum = windows // len(sums_refs)
    levels = [level_of(decode(sums_ref[6])) * (1.0 / (CODE_TOP * windows)) for sums_ref in sums_refs]
    for side in range(2):
        linear = sum(decode(sums_ref[side]) * level for sums_ref, level in zip(sums_refs, levels))
        real, imag = (
            sum(decode(sums_ref[part + side]) for sums_ref in sums_refs) * (per_sum / (CODE_TOP * windows))
            for part in (2, 4)
        )
        out_ref[side, :, :] = linear * (real * real + imag * imag)


def pair_kernel(offs_ref, where_ref, stack_ref, *refs):
    shift_refs, out_ref = refs[:-1], refs[-1]
    half = stack_ref.shape[2]
    ahead = offs_ref[where_ref[0]]
    behind = [
        sum(jnp.where(ahead == number + 1, shift_ref[side], 0.0) for number, shift_ref in enumerate(shift_refs))
        for side in range(2)
    ]
    mirror = (
        lax.broadcasted_iota(jnp.int32, (half, half), 0) + lax.broadcasted_iota(jnp.int32, (half, half), 1) == half - 1
    ).astype(jnp.float32)
    back = stack_ref[1] + behind[0]
    out_ref[:, 0:half] = jnp.dot(back, mirror, precision=lax.Precision.HIGHEST, preferred_element_type=jnp.float32)
    out_ref[:, half : 2 * half] = stack_ref[0] + behind[1]


def place_kernel(order, where_ref, *refs):
    part_refs, out_ref = refs[:-1], refs[-1]
    for number in range(out_ref.shape[1]):
        out_ref[:, number, :] = sum(
            jnp.where(where_ref[0] ^ k == number, part_ref[...], 0.0) for k, part_ref in zip(order, part_refs)
        )


def window_shards(spectra, quality, offsets):
    chan_count = lax.axis_size("chan")
    tm_count = lax.axis_size("tm")
    _, windows, band, chans = spectra.shape
    freqs = band * chan_count
    half = LAGS // 2
    block = chans // chan_count
    reach = chan_count // 2
    offset_count = offsets.shape[0]
    smem = pl.BlockSpec(memory_space=pltpu.SMEM)
    vmem = pl.BlockSpec(memory_space=pltpu.VMEM)
    params = pltpu.CompilerParams(vmem_limit_bytes=VMEM_LIMIT)
    table = jnp.asarray(half_table(freqs, LAGS).T.reshape(chan_count, band, LAGS))
    chan_where = lax.axis_index("chan").astype(jnp.int32).reshape(1)
    tm_where = lax.axis_index("tm").astype(jnp.int32).reshape(1)
    chan_order, tm_order = partners(chan_count), partners(tm_count)

    pieces = pl.pallas_call(
        functools.partial(split_kernel, chan_order),
        out_shape=[jax.ShapeDtypeStruct((2, band, chans), spectra.dtype)] * chan_count,
        in_specs=[smem, pl.BlockSpec(memory_space=pltpu.HBM)],
        out_specs=[pl.BlockSpec(memory_space=pl.ANY)] * chan_count,
        scratch_shapes=[pltpu.SemaphoreType.DMA((chan_count,))],
        compiler_params=params,
        name="split_windows",
    )(chan_where, pltpu.with_memory_space_constraint(spectra, pltpu.HBM))
    pairs = pl.pallas_call(
        functools.partial(window_kernel, chan_order),
        out_shape=[jax.ShapeDtypeStruct((6 * offset_count + 1, block, half), jnp.int16)] * chan_count,
        in_specs=[smem, smem] + [vmem] * (chan_count + 2),
        out_specs=[vmem] * chan_count,
        scratch_shapes=[
            pltpu.VMEM((freqs, chans), jnp.float32),
            pltpu.VMEM((2, chans + reach * block, freqs), jnp.bfloat16),
            pltpu.VMEM((2, 2 * chans, freqs), jnp.bfloat16),
        ],
        compiler_params=params,
        name="window_pairs",
    )(offsets, chan_where, *exchange(pieces, "chan"), quality, table)
    sums = pl.pallas_call(
        functools.partial(sum_kernel, tm_order, 1.0 / (CODE_TOP * math.sqrt(freqs))),
        out_shape=[jax.ShapeDtypeStruct((7, block, half), jnp.int16)] * tm_count,
        in_specs=[smem] + [vmem] * chan_count,
        out_specs=[vmem] * tm_count,
        compiler_params=params,
        name="sum_windows",
    )(tm_where, *exchange(pairs, "chan"))
    stacks = pl.pallas_call(
        functools.partial(stack_kernel, windows * tm_count),
        out_shape=jax.ShapeDtypeStruct((2, block, half), jnp.float32),
        in_specs=[vmem] * tm_count,
        out_specs=vmem,
        compiler_params=params,
        name="stack_pairs",
    )(*exchange(sums, "tm"))
    shifts = [shifted(stacks, "chan", steps) for steps in range(1, reach + 1)]
    gathers = pl.pallas_call(
        pair_kernel,
        out_shape=jax.ShapeDtypeStruct((block, LAGS), jnp.float32),
        in_specs=[smem, smem] + [vmem] * (reach + 1),
        out_specs=vmem,
        compiler_params=params,
        name="add_reverse",
    )(offsets, tm_where, stacks, *shifts)
    return pl.pallas_call(
        functools.partial(place_kernel, tm_order),
        out_shape=jax.ShapeDtypeStruct((block, offset_count, LAGS), jnp.float32),
        in_specs=[smem] + [vmem] * tm_count,
        out_specs=vmem,
        compiler_params=params,
        name="place_offsets",
    )(tm_where, *exchange([gathers] * tm_count, "tm"))


def shifted(value, axis, steps):
    count = lax.axis_size(axis)
    leading, last = (max(0, -steps), min(count, count - steps))
    return lax.ppermute(value, axis, [(source, source + steps) for source in range(leading, last)])


def lag_table(freq_count, lag_count):
    freq_index = jnp.arange(freq_count, dtype=jnp.int32)[:, None]
    double_lag = (2 * jnp.arange(lag_count, dtype=jnp.int32) - lag_count + 1)[None, :]
    turns = jnp.mod(freq_index * double_lag, 4 * freq_count)
    angles = turns.astype(jnp.float32) * (2.0 * math.pi / (4 * freq_count))
    cosine = jnp.cos(angles)
    sine = jnp.sin(angles)
    upper = jnp.concatenate([cosine, sine], axis=1)
    lower = jnp.concatenate([-sine, cosine], axis=1)
    return jnp.stack([upper, lower]).astype(jnp.bfloat16)


def whiten_parts(real_part, imag_part, magnitude, channel_level, usable):
    factor = usable.astype(jnp.float32)[:, None, :] / (magnitude + 0.5 * (channel_level + 1e-05))
    return jnp.stack([real_part * factor, imag_part * factor]).astype(jnp.bfloat16)


def cross_parts(own_real, own_imag, far_real, far_imag):
    own_real = own_real.astype(jnp.float32)
    own_imag = own_imag.astype(jnp.float32)
    far_real = far_real.astype(jnp.float32)
    far_imag = far_imag.astype(jnp.float32)
    return jnp.stack(
        [own_real * far_real + own_imag * far_imag, own_imag * far_real - own_real * far_imag]
    ).astype(jnp.bfloat16)


def pair_terms(corr_all):
    lag_count = corr_all.shape[-1] // 2
    real_corr = corr_all[..., :lag_count]
    imag_corr = corr_all[..., lag_count:]
    power = real_corr * real_corr + imag_corr * imag_corr
    mean_power = jnp.mean(power, axis=-1, keepdims=True)
    denominator = jnp.sqrt(power + 0.25 * (mean_power + 1e-06))
    return (
        jnp.sum(real_corr, axis=-3),
        jnp.sum(real_corr / denominator, axis=-3),
        jnp.sum(imag_corr / denominator, axis=-3),
    )


def shards(spectra, quality, offsets):
    chan_count = lax.axis_size("chan")
    tm_count = lax.axis_size("tm")
    levels = chan_count.bit_length() - 1
    table_bf = lag_table(F, LAGS)
    inv_root = 1.0 / math.sqrt(F)
    real_part = spectra[0].astype(jnp.float32)
    imag_part = spectra[1].astype(jnp.float32)
    magnitude = jnp.sqrt(real_part * real_part + imag_part * imag_part)
    band_total = lax.psum(jnp.sum(magnitude, axis=1), "chan")
    channel_level = (band_total / F)[:, None, :]
    whitened = whiten_parts(real_part, imag_part, magnitude, channel_level, quality)
    width_all = whitened.shape[3]
    padded = jnp.pad(whitened, ((0, 0), (0, 0), (0, 0), (0, width_all)))
    crossed_list = []
    for offset_index in range(NOFF):
        partner = lax.dynamic_slice_in_dim(padded, offsets[offset_index] * CH_DEV, width_all, 3)
        crossed_list.append(cross_parts(whitened[0], whitened[1], partner[0], partner[1]))
    crossed = jnp.stack(crossed_list, axis=1)
    corr_all = jnp.einsum(
        "cnwfh,cfl->nwhl",
        lax.all_to_all(crossed, "chan", split_axis=4, concat_axis=3, tiled=True),
        table_bf,
        preferred_element_type=jnp.float32,
    )
    linear_sum, real_sum, imag_sum = pair_terms(corr_all * inv_root)
    totals = lax.psum((linear_sum, real_sum, imag_sum), "tm")
    window_count = W_DEV * tm_count
    linear = totals[0] / window_count
    real_phase = totals[1] / window_count
    imag_phase = totals[2] / window_count
    stacks = jnp.transpose(linear * (real_phase * real_phase + imag_phase * imag_phase), (1, 0, 2))
    reverse_part = stacks
    for bit_index in range(levels):
        step_size = 1 << bit_index
        arrived = shifted(reverse_part, "chan", step_size)
        chosen = offsets // step_size % 2 == 1
        reverse_part = jnp.where(chosen[None, :, None], arrived, reverse_part)
    return stacks + jnp.flip(reverse_part, axis=2)


def solution(mesh):
    chan_count, tm_count = mesh.shape["chan"], mesh.shape["tm"]
    by_window = chan_count == W_DEV and tm_count == NOFF
    return jax.shard_map(
        window_shards if by_window else shards,
        mesh=mesh,
        in_specs=(P(None, "tm", "chan", None), P("tm", None), P()),
        out_specs=P("chan", None, None),
        check_vma=False,
    )
```

time: 57.9 us -> 62.1 us (1.073)
  starting transfers between devices: 17.7 us -> 30.6 us
  blocking collectives: 12.6 us -> 0 us
  waiting for transfers between devices: 19.8 us -> 24.3 us
    all_to_all x1 -> x0, blocking collectives: 12.6 us -> none  [window_shards(): lax.all_to_all(pieces.reshape(shape), ('chan', 'tm'), 0, 0, tiled=True)]
    ppermute x0 -> x4, starting transfers between devices: none -> 9.33 us  [shifted(): lax.ppermute(value, axis, [(source, source + steps) for source in range(l...]
    ppermute x17 -> x20, waiting for transfers between devices: 19.8 us -> 23.5 us  [exchange(): lax.ppermute(piece, axis, [(source, source ^ k) for source in range(count)])]
    ppermute x17 -> x20, starting transfers between devices: 17.7 us -> 21.2 us  [exchange(): lax.ppermute(piece, axis, [(source, source ^ k) for source in range(count)])]
    ppermute x0 -> x4, waiting for transfers between devices: none -> 0.8 us  [shifted(): lax.ppermute(value, axis, [(source, source + steps) for source in range(l...]
    pallas_call x1, Pallas kernels: 0.71 us -> 0.03 us  [window_shards(): pl.pallas_call(functools.partial(stack_kernel, windows * tm_count), out_s...]
    pallas_call x1 -> x2, Pallas kernels: 1.22 us -> 1.38 us  [the longest x1 0.71 us: window_shards(): pl.pallas_call(pair_kernel, out_shape=jax.ShapeDtypeStruct((block, LAGS),...]
  transfers between devices with their start and end apart: 17 -> 24, of which waited for: 12 -> 16; matrix products, arithmetic and copies ran while one was open for 0% -> 0% of each run, Pallas kernels for 0% -> 0%
where the time goes in v7:
time: 62.1 us; the launch traced here: 61.9 us
  starting transfers between devices  30.6 us (49%)
  waiting for transfers between devices  24.3 us (39%)
  Pallas kernels  6.91 us (11%)
    ppermute x20, waiting for transfers between devices, exchange(): lax.ppermute(piece, axis, [(source, source ^ k) for source in range(count)])  23.5 us
    ppermute x20, starting transfers between devices, exchange(): lax.ppermute(piece, axis, [(source, source ^ k) for source in range(count)])  21.2 us
    ppermute x4, starting transfers between devices, shifted(): lax.ppermute(value, axis, [(source, source + steps) for source in range(l...  9.33 us
    pallas_call x1, Pallas kernels, window_shards(): pl.pallas_call(functools.partial(window_kernel, chan_order), out_shape=[j...  3.75 us
    pallas_call x1, Pallas kernels, window_shards(): pl.pallas_call(functools.partial(split_kernel, chan_order), out_shape=[ja...  1.43 us
  transfers between devices with their start and end apart: 24, of which 16 were waited for; matrix products, arithmetic and copies ran while one was open for 0% of the time, Pallas kernels for 0%

profile of v7, /device:TPU:0, one launch (start us, length us, event | category | flops | bytes accessed | tf_op | source)
XLA Modules:
  0.0 61.9 jit_solution(4551634043854113580)
XLA Ops:
  0.0 1.4 %split_windows.1 = (bf16[2,256,128]{2,1,0:T(8,128)(2,1)S(1)}, bf16[2,256,128]{2,1,0:T(8,128)(2,1)S(1)}, bf16[2,256,128]{2,1,0:T(8,128)(2,1)S(1)}, bf16[2,256,128...) custom-call(s32[1]{0:T(128)} %bitcast.1.where_ref, ...), custom_call_target="tpu_custom_call" | custom-call | tf_op jit(solution)/shard_map/split_windows/pallas_call | solution.py:225
  1.4 4.0 %collective-permute-start = (bf16[2,256,128]{2,1,0:T(8,128)(2,1)S(1)}, bf16[2,256,128]{2,1,0:T(8,128)(2,1)S(1)}, u32[]{:S(2)}, u32[]{:S(2)}) collective-permute-start(bf16[2,256,128]{2,1,0:T(8,128)(2,1)S(1)} %get-tuple-element.25), channel_id=1, source_target_pairs={{0,24},{4,28},{8,16},{12,20},{16,8},{20,12},{24,0},{28,4},{1,25},{... | collective-permute-start | bytes 393224 | tf_op jit(solution)/shard_map/ppermute | solution.py:154
  5.4 1.1 %collective-permute-start.2 = (bf16[2,256,128]{2,1,0:T(8,128)(2,1)S(1)}, bf16[2,256,128]{2,1,0:T(8,128)(2,1)S(1)}, u32[]{:S(2)}, u32[]{:S(2)}) collective-permute-start(bf16[2,256,128]{2,1,0:T(8,128)(2,1)S(1)} %get-tuple-element.27), channel_id=1, source_target_pairs={{0,8},{4,12},{8,0},{12,4},{16,24},{20,28},{24,16},{28,20},{1,9},{5... | collective-permute-start | bytes 393224 | tf_op jit(solution)/shard_map/ppermute | solution.py:154
  6.5 1.5 %collective-permute-start.3 = (bf16[2,256,128]{2,1,0:T(8,128)(2,1)S(1)}, bf16[2,256,128]{2,1,0:T(8,128)(2,1)S(1)}, u32[]{:S(2)}, u32[]{:S(2)}) collective-permute-start(bf16[2,256,128]{2,1,0:T(8,128)(2,1)S(1)} %get-tuple-element.28), channel_id=1, source_target_pairs={{0,16},{4,20},{8,24},{12,28},{16,0},{20,4},{24,8},{28,12},{1,17},{... | collective-permute-start | bytes 393224 | tf_op jit(solution)/shard_map/ppermute | solution.py:154
  9.3 2.8 %collective-permute-done.1.refs_1_ = bf16[2,256,128]{2,1,0:T(8,128)(2,1)S(1)} collective-permute-done((bf16[2,256,128]{2,1,0:T(8,128)(2,1)S(1)}, bf16[2,256,128]{2,1,0:T(8,128)(2,1)S(1)}, u32[]{:S(2)}, u32[]{:S(2)}) %collective-permute-start.1) | collective-permute-done | bytes 131104 | tf_op jit(solution)/shard_map/ppermute | solution.py:154
  12.2 3.4 %collective-permute-done.2.refs_2_ = bf16[2,256,128]{2,1,0:T(8,128)(2,1)S(1)} collective-permute-done((bf16[2,256,128]{2,1,0:T(8,128)(2,1)S(1)}, bf16[2,256,128]{2,1,0:T(8,128)(2,1)S(1)}, u32[]{:S(2)}, u32[]{:S(2)}) %collective-permute-start.2) | collective-permute-done | bytes 131104 | tf_op jit(solution)/shard_map/ppermute | solution.py:154
  15.6 1.1 %collective-permute-done.4.refs_4_ = bf16[2,256,128]{2,1,0:T(8,128)(2,1)S(1)} collective-permute-done((bf16[2,256,128]{2,1,0:T(8,128)(2,1)S(1)}, bf16[2,256,128]{2,1,0:T(8,128)(2,1)S(1)}, u32[]{:S(2)}, u32[]{:S(2)}) %collective-permute-start.4) | collective-permute-done | bytes 131104 | tf_op jit(solution)/shard_map/ppermute | solution.py:154
  17.4 3.8 %window_pairs.1 = (s16[25,16,128]{2,1,0:T(8,128)(2,1)S(1)}, s16[25,16,128]{2,1,0:T(8,128)(2,1)S(1)}, s16[25,16,128]{2,1,0:T(8,128)(2,1)S(1)}, s16[25,16,128]{2,1...) custom-call(s32[4]{0:T(128)S(1)} %copy-done.2, ...), custom_call_target="tpu_custom_call" | custom-call | tf_op jit(solution)/shard_map/window_pairs/pallas_call | solution.py:234
  21.2 2.6 %collective-permute-start.7 = (s16[25,16,128]{2,1,0:T(8,128)(2,1)S(1)}, s16[25,16,128]{2,1,0:T(8,128)(2,1)S(1)}, u32[]{:S(2)}, u32[]{:S(2)}) collective-permute-start(s16[25,16,128]{2,1,0:T(8,128)(2,1)S(1)} %get-tuple-element.33), channel_id=1, source_target_pairs={{0,24},{4,28},{8,16},{12,20},{16,8},{20,12},{24,0},{28,4},{1,25},{... | collective-permute-start | bytes 307208 | tf_op jit(solution)/shard_map/ppermute | solution.py:154
  23.8 1.4 %collective-permute-start.9 = (s16[25,16,128]{2,1,0:T(8,128)(2,1)S(1)}, s16[25,16,128]{2,1,0:T(8,128)(2,1)S(1)}, u32[]{:S(2)}, u32[]{:S(2)}) collective-permute-start(s16[25,16,128]{2,1,0:T(8,128)(2,1)S(1)} %get-tuple-element.35), channel_id=1, source_target_pairs={{0,8},{4,12},{8,0},{12,4},{16,24},{20,28},{24,16},{28,20},{1,9},{5... | collective-permute-start | bytes 307208 | tf_op jit(solution)/shard_map/ppermute | solution.py:154
  25.1 1.6 %collective-permute-start.10 = (s16[25,16,128]{2,1,0:T(8,128)(2,1)S(1)}, s16[25,16,128]{2,1,0:T(8,128)(2,1)S(1)}, u32[]{:S(2)}, u32[]{:S(2)}) collective-permute-start(s16[25,16,128]{2,1,0:T(8,128)(2,1)S(1)} %get-tuple-element.36), channel_id=1, source_target_pairs={{0,16},{4,20},{8,24},{12,28},{16,0},{20,4},{24,8},{28,12},{1,17},{... | collective-permute-start | bytes 307208 | tf_op jit(solution)/shard_map/ppermute | solution.py:154
  27.6 2.4 %collective-permute-done.8.refs_1_ = s16[25,16,128]{2,1,0:T(8,128)(2,1)S(1)} collective-permute-done((s16[25,16,128]{2,1,0:T(8,128)(2,1)S(1)}, s16[25,16,128]{2,1,0:T(8,128)(2,1)S(1)}, u32[]{:S(2)}, u32[]{:S(2)}) %collective-permute-start.8) | collective-permute-done | bytes 102432 | tf_op jit(solution)/shard_map/ppermute | solution.py:154
  30.0 2.2 %collective-permute-done.9.refs_2_ = s16[25,16,128]{2,1,0:T(8,128)(2,1)S(1)} collective-permute-done((s16[25,16,128]{2,1,0:T(8,128)(2,1)S(1)}, s16[25,16,128]{2,1,0:T(8,128)(2,1)S(1)}, u32[]{:S(2)}, u32[]{:S(2)}) %collective-permute-start.9) | collective-permute-done | bytes 102432 | tf_op jit(solution)/shard_map/ppermute | solution.py:154
  32.2 1.0 %collective-permute-done.11.refs_4_ = s16[25,16,128]{2,1,0:T(8,128)(2,1)S(1)} collective-permute-done((s16[25,16,128]{2,1,0:T(8,128)(2,1)S(1)}, s16[25,16,128]{2,1,0:T(8,128)(2,1)S(1)}, u32[]{:S(2)}, u32[]{:S(2)}) %collective-permute-start.11) | collective-permute-done | bytes 102432 | tf_op jit(solution)/shard_map/ppermute | solution.py:154
  34.5 2.7 %collective-permute-start.14 = (s16[7,16,128]{2,1,0:T(8,128)(2,1)S(1)}, s16[7,16,128]{2,1,0:T(8,128)(2,1)S(1)}, u32[]{:S(2)}, u32[]{:S(2)}) collective-permute-start(s16[7,16,128]{2,1,0:T(8,128)(2,1)S(1)} %get-tuple-element.41), channel_id=1, source_target_pairs={{0,2},{1,3},{2,0},{3,1},{4,6},{5,7},{6,4},{7,5},{8,10},{9,11},{10,... | collective-permute-start | bytes 86024 | tf_op jit(solution)/shard_map/ppermute | solution.py:154
  37.2 1.3 %collective-permute-start.15 = (s16[7,16,128]{2,1,0:T(8,128)(2,1)S(1)}, s16[7,16,128]{2,1,0:T(8,128)(2,1)S(1)}, u32[]{:S(2)}, u32[]{:S(2)}) collective-permute-start(s16[7,16,128]{2,1,0:T(8,128)(2,1)S(1)} %get-tuple-element.42), channel_id=1, source_target_pairs={{0,3},{1,2},{2,1},{3,0},{4,7},{5,6},{6,5},{7,4},{8,11},{9,10},{10,... | collective-permute-start | bytes 86024 | tf_op jit(solution)/shard_map/ppermute | solution.py:154
  39.7 3.2 %collective-permute-done.15.refs_1_ = s16[7,16,128]{2,1,0:T(8,128)(2,1)S(1)} collective-permute-done((s16[7,16,128]{2,1,0:T(8,128)(2,1)S(1)}, s16[7,16,128]{2,1,0:T(8,128)(2,1)S(1)}, u32[]{:S(2)}, u32[]{:S(2)}) %collective-permute-start.15) | collective-permute-done | bytes 28704 | tf_op jit(solution)/shard_map/ppermute | solution.py:154
  42.9 2.9 %collective-permute-start.20 = (f32[2,16,128]{2,1,0:T(8,128)S(1)}, f32[2,16,128]{2,1,0:T(8,128)S(1)}, u32[]{:S(2)}, u32[]{:S(2)}) collective-permute-start(f32[2,16,128]{2,1,0:T(8,128)S(1)} %stack_pairs.1.stack_ref), channel_id=1, source_target_pairs={{0,16},{4,20},{8,24},{12,28},{1,17},{5,21},{9,25},{13,29},{2,18},{... | collective-permute-start | bytes 49160 | tf_op jit(solution)/shard_map/ppermute | solution.py:285
  45.8 1.4 %collective-permute-start.19 = (f32[2,16,128]{2,1,0:T(8,128)S(1)}, f32[2,16,128]{2,1,0:T(8,128)S(1)}, u32[]{:S(2)}, u32[]{:S(2)}) collective-permute-start(f32[2,16,128]{2,1,0:T(8,128)S(1)} %stack_pairs.1.stack_ref), channel_id=1, source_target_pairs={{0,12},{4,16},{8,20},{12,24},{16,28},{1,13},{5,17},{9,21},{13,25},... | collective-permute-start | bytes 49160 | tf_op jit(solution)/shard_map/ppermute | solution.py:285
  47.2 3.3 %collective-permute-start.18 = (f32[2,16,128]{2,1,0:T(8,128)S(1)}, f32[2,16,128]{2,1,0:T(8,128)S(1)}, u32[]{:S(2)}, u32[]{:S(2)}) collective-permute-start(f32[2,16,128]{2,1,0:T(8,128)S(1)} %stack_pairs.1.stack_ref), channel_id=1, source_target_pairs={{0,8},{4,12},{8,16},{12,20},{16,24},{20,28},{1,9},{5,13},{9,17},{1... | collective-permute-start | bytes 49160 | tf_op jit(solution)/shard_map/ppermute | solution.py:285
  50.5 1.7 %collective-permute-start.17 = (f32[2,16,128]{2,1,0:T(8,128)S(1)}, f32[2,16,128]{2,1,0:T(8,128)S(1)}, u32[]{:S(2)}, u32[]{:S(2)}) collective-permute-start(f32[2,16,128]{2,1,0:T(8,128)S(1)} %stack_pairs.1.stack_ref), channel_id=1, source_target_pairs={{0,4},{4,8},{8,12},{12,16},{16,20},{20,24},{24,28},{1,5},{5,9},{9,... | collective-permute-start | bytes 49160 | tf_op jit(solution)/shard_map/ppermute | solution.py:285
  53.8 2.7 %collective-permute-start.22 = (f32[16,256]{1,0:T(8,128)S(1)}, f32[16,256]{1,0:T(8,128)S(1)}, u32[]{:S(2)}, u32[]{:S(2)}) collective-permute-start(f32[16,256]{1,0:T(8,128)S(1)} %add_reverse.1.refs_3_), channel_id=1, source_target_pairs={{0,3},{1,2},{2,1},{3,0},{4,7},{5,6},{6,5},{7,4},{8,11},{9,10},{10,... | collective-permute-start | bytes 49160 | tf_op jit(solution)/shard_map/ppermute | solution.py:154
  57.5 1.8 %collective-permute-done.22.refs_1_ = f32[16,256]{1,0:T(8,128)S(1)} collective-permute-done((f32[16,256]{1,0:T(8,128)S(1)}, f32[16,256]{1,0:T(8,128)S(1)}, u32[]{:S(2)}, u32[]{:S(2)}) %collective-permute-start.22) | collective-permute-done | bytes 16416 | tf_op jit(solution)/shard_map/ppermute | solution.py:154
  59.4 1.8 %collective-permute-done.21.refs_0_ = f32[16,256]{1,0:T(8,128)S(1)} collective-permute-done((f32[16,256]{1,0:T(8,128)S(1)}, f32[16,256]{1,0:T(8,128)S(1)}, u32[]{:S(2)}, u32[]{:S(2)}) %collective-permute-start.21) | collective-permute-done | bytes 16416 | tf_op jit(solution)/shard_map/ppermute | solution.py:154
  (36 shorter events, 8.6 us)
Async XLA Ops:
  1.4 7.9 %collective-permute-start = (bf16[2,256,128]{2,1,0:T(8,128)(2,1)S(1)}, bf16[2,256,128]{2,1,0:T(8,128)(2,1)S(1)}, u32[]{:S(2)}, u32[]{:S(2)}) collective-permute-start(bf16[2,256,128]{2,1,0:T(8,128)(2,1)S(1)} %get-tuple-element.25), channel_id=1, source_target_pairs={{0,24},{4,28},{8,16},{12,20},{16,8},{20,12},{24,0},{28,4},{1,25},{... | collective-permute-start | bytes 393224 | tf_op jit(solution)/shard_map/ppermute | solution.py:154
  5.4 6.8 %collective-permute-start.1 = (bf16[2,256,128]{2,1,0:T(8,128)(2,1)S(1)}, bf16[2,256,128]{2,1,0:T(8,128)(2,1)S(1)}, u32[]{:S(2)}, u32[]{:S(2)}) collective-permute-start(bf16[2,256,128]{2,1,0:T(8,128)(2,1)S(1)} %get-tuple-element.26), channel_id=1, source_target_pairs={{0,28},{4,24},{8,20},{12,16},{16,12},{20,8},{24,4},{28,0},{1,29},{... | collective-permute-start | bytes 393224 | tf_op jit(solution)/shard_map/ppermute | solution.py:154
  5.4 10.2 %collective-permute-start.2 = (bf16[2,256,128]{2,1,0:T(8,128)(2,1)S(1)}, bf16[2,256,128]{2,1,0:T(8,128)(2,1)S(1)}, u32[]{:S(2)}, u32[]{:S(2)}) collective-permute-start(bf16[2,256,128]{2,1,0:T(8,128)(2,1)S(1)} %get-tuple-element.27), channel_id=1, source_target_pairs={{0,8},{4,12},{8,0},{12,4},{16,24},{20,28},{24,16},{28,20},{1,9},{5... | collective-permute-start | bytes 393224 | tf_op jit(solution)/shard_map/ppermute | solution.py:154
  6.5 9.1 %collective-permute-start.3 = (bf16[2,256,128]{2,1,0:T(8,128)(2,1)S(1)}, bf16[2,256,128]{2,1,0:T(8,128)(2,1)S(1)}, u32[]{:S(2)}, u32[]{:S(2)}) collective-permute-start(bf16[2,256,128]{2,1,0:T(8,128)(2,1)S(1)} %get-tuple-element.28), channel_id=1, source_target_pairs={{0,16},{4,20},{8,24},{12,28},{16,0},{20,4},{24,8},{28,12},{1,17},{... | collective-permute-start | bytes 393224 | tf_op jit(solution)/shard_map/ppermute | solution.py:154
  8.1 8.7 %collective-permute-start.4 = (bf16[2,256,128]{2,1,0:T(8,128)(2,1)S(1)}, bf16[2,256,128]{2,1,0:T(8,128)(2,1)S(1)}, u32[]{:S(2)}, u32[]{:S(2)}) collective-permute-start(bf16[2,256,128]{2,1,0:T(8,128)(2,1)S(1)} %get-tuple-element.29), channel_id=1, source_target_pairs={{0,12},{4,8},{8,4},{12,0},{16,28},{20,24},{24,20},{28,16},{1,13},{... | collective-permute-start | bytes 393224 | tf_op jit(solution)/shard_map/ppermute | solution.py:154
  9.3 8.1 %collective-permute-start.5 = (bf16[2,256,128]{2,1,0:T(8,128)(2,1)S(1)}, bf16[2,256,128]{2,1,0:T(8,128)(2,1)S(1)}, u32[]{:S(2)}, u32[]{:S(2)}) collective-permute-start(bf16[2,256,128]{2,1,0:T(8,128)(2,1)S(1)} %get-tuple-element.30), channel_id=1, source_target_pairs={{0,20},{4,16},{8,28},{12,24},{16,4},{20,0},{24,12},{28,8},{1,21},{... | collective-permute-start | bytes 393224 | tf_op jit(solution)/shard_map/ppermute | solution.py:154
  12.2 5.3 %collective-permute-start.6 = (bf16[2,256,128]{2,1,0:T(8,128)(2,1)S(1)}, bf16[2,256,128]{2,1,0:T(8,128)(2,1)S(1)}, u32[]{:S(2)}, u32[]{:S(2)}) collective-permute-start(bf16[2,256,128]{2,1,0:T(8,128)(2,1)S(1)} %get-tuple-element.31), channel_id=1, source_target_pairs={{0,4},{4,0},{8,12},{12,8},{16,20},{20,16},{24,28},{28,24},{1,5},{5... | collective-permute-start | bytes 393224 | tf_op jit(solution)/shard_map/ppermute | solution.py:154
  21.2 5.9 %collective-permute-start.7 = (s16[25,16,128]{2,1,0:T(8,128)(2,1)S(1)}, s16[25,16,128]{2,1,0:T(8,128)(2,1)S(1)}, u32[]{:S(2)}, u32[]{:S(2)}) collective-permute-start(s16[25,16,128]{2,1,0:T(8,128)(2,1)S(1)} %get-tuple-element.33), channel_id=1, source_target_pairs={{0,24},{4,28},{8,16},{12,20},{16,8},{20,12},{24,0},{28,4},{1,25},{... | collective-permute-start | bytes 307208 | tf_op jit(solution)/shard_map/ppermute | solution.py:154
  23.8 6.2 %collective-permute-start.8 = (s16[25,16,128]{2,1,0:T(8,128)(2,1)S(1)}, s16[25,16,128]{2,1,0:T(8,128)(2,1)S(1)}, u32[]{:S(2)}, u32[]{:S(2)}) collective-permute-start(s16[25,16,128]{2,1,0:T(8,128)(2,1)S(1)} %get-tuple-element.34), channel_id=1, source_target_pairs={{0,28},{4,24},{8,20},{12,16},{16,12},{20,8},{24,4},{28,0},{1,29},{... | collective-permute-start | bytes 307208 | tf_op jit(solution)/shard_map/ppermute | solution.py:154
  23.8 8.4 %collective-permute-start.9 = (s16[25,16,128]{2,1,0:T(8,128)(2,1)S(1)}, s16[25,16,128]{2,1,0:T(8,128)(2,1)S(1)}, u32[]{:S(2)}, u32[]{:S(2)}) collective-permute-start(s16[25,16,128]{2,1,0:T(8,128)(2,1)S(1)} %get-tuple-element.35), channel_id=1, source_target_pairs={{0,8},{4,12},{8,0},{12,4},{16,24},{20,28},{24,16},{28,20},{1,9},{5... | collective-permute-start | bytes 307208 | tf_op jit(solution)/shard_map/ppermute | solution.py:154
  25.1 7.0 %collective-permute-start.10 = (s16[25,16,128]{2,1,0:T(8,128)(2,1)S(1)}, s16[25,16,128]{2,1,0:T(8,128)(2,1)S(1)}, u32[]{:S(2)}, u32[]{:S(2)}) collective-permute-start(s16[25,16,128]{2,1,0:T(8,128)(2,1)S(1)} %get-tuple-element.36), channel_id=1, source_target_pairs={{0,16},{4,20},{8,24},{12,28},{16,0},{20,4},{24,8},{28,12},{1,17},{... | collective-permute-start | bytes 307208 | tf_op jit(solution)/shard_map/ppermute | solution.py:154
  26.7 6.5 %collective-permute-start.11 = (s16[25,16,128]{2,1,0:T(8,128)(2,1)S(1)}, s16[25,16,128]{2,1,0:T(8,128)(2,1)S(1)}, u32[]{:S(2)}, u32[]{:S(2)}) collective-permute-start(s16[25,16,128]{2,1,0:T(8,128)(2,1)S(1)} %get-tuple-element.37), channel_id=1, source_target_pairs={{0,12},{4,8},{8,4},{12,0},{16,28},{20,24},{24,20},{28,16},{1,13},{... | collective-permute-start | bytes 307208 | tf_op jit(solution)/shard_map/ppermute | solution.py:154
  27.1 7.1 %collective-permute-start.12 = (s16[25,16,128]{2,1,0:T(8,128)(2,1)S(1)}, s16[25,16,128]{2,1,0:T(8,128)(2,1)S(1)}, u32[]{:S(2)}, u32[]{:S(2)}) collective-permute-start(s16[25,16,128]{2,1,0:T(8,128)(2,1)S(1)} %get-tuple-element.38), channel_id=1, source_target_pairs={{0,20},{4,16},{8,28},{12,24},{16,4},{20,0},{24,12},{28,8},{1,21},{... | collective-permute-start | bytes 307208 | tf_op jit(solution)/shard_map/ppermute | solution.py:154
  29.9 4.2 %collective-permute-start.13 = (s16[25,16,128]{2,1,0:T(8,128)(2,1)S(1)}, s16[25,16,128]{2,1,0:T(8,128)(2,1)S(1)}, u32[]{:S(2)}, u32[]{:S(2)}) collective-permute-start(s16[25,16,128]{2,1,0:T(8,128)(2,1)S(1)} %get-tuple-element.39), channel_id=1, source_target_pairs={{0,4},{4,0},{8,12},{12,8},{16,20},{20,16},{24,28},{28,24},{1,5},{5... | collective-permute-start | bytes 307208 | tf_op jit(solution)/shard_map/ppermute | solution.py:154
  34.5 5.1 %collective-permute-start.14 = (s16[7,16,128]{2,1,0:T(8,128)(2,1)S(1)}, s16[7,16,128]{2,1,0:T(8,128)(2,1)S(1)}, u32[]{:S(2)}, u32[]{:S(2)}) collective-permute-start(s16[7,16,128]{2,1,0:T(8,128)(2,1)S(1)} %get-tuple-element.41), channel_id=1, source_target_pairs={{0,2},{1,3},{2,0},{3,1},{4,6},{5,7},{6,4},{7,5},{8,10},{9,11},{10,... | collective-permute-start | bytes 86024 | tf_op jit(solution)/shard_map/ppermute | solution.py:154
  37.2 5.7 %collective-permute-start.15 = (s16[7,16,128]{2,1,0:T(8,128)(2,1)S(1)}, s16[7,16,128]{2,1,0:T(8,128)(2,1)S(1)}, u32[]{:S(2)}, u32[]{:S(2)}) collective-permute-start(s16[7,16,128]{2,1,0:T(8,128)(2,1)S(1)} %get-tuple-element.42), channel_id=1, source_target_pairs={{0,3},{1,2},{2,1},{3,0},{4,7},{5,6},{6,5},{7,4},{8,11},{9,10},{10,... | collective-permute-start | bytes 86024 | tf_op jit(solution)/shard_map/ppermute | solution.py:154
  38.5 4.3 %collective-permute-start.16 = (s16[7,16,128]{2,1,0:T(8,128)(2,1)S(1)}, s16[7,16,128]{2,1,0:T(8,128)(2,1)S(1)}, u32[]{:S(2)}, u32[]{:S(2)}) collective-permute-start(s16[7,16,128]{2,1,0:T(8,128)(2,1)S(1)} %get-tuple-element.43), channel_id=1, source_target_pairs={{0,1},{1,0},{2,3},{3,2},{4,5},{5,4},{6,7},{7,6},{8,9},{9,8},{10,11... | collective-permute-start | bytes 86024 | tf_op jit(solution)/shard_map/ppermute | solution.py:154
  42.9 9.4 %collective-permute-start.20 = (f32[2,16,128]{2,1,0:T(8,128)S(1)}, f32[2,16,128]{2,1,0:T(8,128)S(1)}, u32[]{:S(2)}, u32[]{:S(2)}) collective-permute-start(f32[2,16,128]{2,1,0:T(8,128)S(1)} %stack_pairs.1.stack_ref), channel_id=1, source_target_pairs={{0,16},{4,20},{8,24},{12,28},{1,17},{5,21},{9,25},{13,29},{2,18},{... | collective-permute-start | bytes 49160 | tf_op jit(solution)/shard_map/ppermute | solution.py:285
  45.8 6.5 %collective-permute-start.19 = (f32[2,16,128]{2,1,0:T(8,128)S(1)}, f32[2,16,128]{2,1,0:T(8,128)S(1)}, u32[]{:S(2)}, u32[]{:S(2)}) collective-permute-start(f32[2,16,128]{2,1,0:T(8,128)S(1)} %stack_pairs.1.stack_ref), channel_id=1, source_target_pairs={{0,12},{4,16},{8,20},{12,24},{16,28},{1,13},{5,17},{9,21},{13,25},... | collective-permute-start | bytes 49160 | tf_op jit(solution)/shard_map/ppermute | solution.py:285
  47.2 5.1 %collective-permute-start.18 = (f32[2,16,128]{2,1,0:T(8,128)S(1)}, f32[2,16,128]{2,1,0:T(8,128)S(1)}, u32[]{:S(2)}, u32[]{:S(2)}) collective-permute-start(f32[2,16,128]{2,1,0:T(8,128)S(1)} %stack_pairs.1.stack_ref), channel_id=1, source_target_pairs={{0,8},{4,12},{8,16},{12,20},{16,24},{20,28},{1,9},{5,13},{9,17},{1... | collective-permute-start | bytes 49160 | tf_op jit(solution)/shard_map/ppermute | solution.py:285
  50.5 2.6 %collective-permute-start.17 = (f32[2,16,128]{2,1,0:T(8,128)S(1)}, f32[2,16,128]{2,1,0:T(8,128)S(1)}, u32[]{:S(2)}, u32[]{:S(2)}) collective-permute-start(f32[2,16,128]{2,1,0:T(8,128)S(1)} %stack_pairs.1.stack_ref), channel_id=1, source_target_pairs={{0,4},{4,8},{8,12},{12,16},{16,20},{20,24},{24,28},{1,5},{5,9},{9,... | collective-permute-start | bytes 49160 | tf_op jit(solution)/shard_map/ppermute | solution.py:285
  53.8 3.7 %collective-permute-start.23 = (f32[16,256]{1,0:T(8,128)S(1)}, f32[16,256]{1,0:T(8,128)S(1)}, u32[]{:S(2)}, u32[]{:S(2)}) collective-permute-start(f32[16,256]{1,0:T(8,128)S(1)} %add_reverse.1.refs_3_), channel_id=1, source_target_pairs={{0,1},{1,0},{2,3},{3,2},{4,5},{5,4},{6,7},{7,6},{8,9},{9,8},{10,11... | collective-permute-start | bytes 49160 | tf_op jit(solution)/shard_map/ppermute | solution.py:154
  53.8 5.6 %collective-permute-start.22 = (f32[16,256]{1,0:T(8,128)S(1)}, f32[16,256]{1,0:T(8,128)S(1)}, u32[]{:S(2)}, u32[]{:S(2)}) collective-permute-start(f32[16,256]{1,0:T(8,128)S(1)} %add_reverse.1.refs_3_), channel_id=1, source_target_pairs={{0,3},{1,2},{2,1},{3,0},{4,7},{5,6},{6,5},{7,4},{8,11},{9,10},{10,... | collective-permute-start | bytes 49160 | tf_op jit(solution)/shard_map/ppermute | solution.py:154
  56.5 4.7 %collective-permute-start.21 = (f32[16,256]{1,0:T(8,128)S(1)}, f32[16,256]{1,0:T(8,128)S(1)}, u32[]{:S(2)}, u32[]{:S(2)}) collective-permute-start(f32[16,256]{1,0:T(8,128)S(1)} %add_reverse.1.refs_3_), channel_id=1, source_target_pairs={{0,2},{1,3},{2,0},{3,1},{4,6},{5,7},{6,4},{7,5},{8,10},{9,11},{10,... | collective-permute-start | bytes 49160 | tf_op jit(solution)/shard_map/ppermute | solution.py:154
  (3 other events, 33.6 us)

commit v8 on v6

--- a/solution.py
+++ b/solution.py
@@ -125,16 +125,23 @@
     code_refs, out_refs = refs[: -len(order)], refs[-len(order) :]
     blocks = code_refs[0].shape[0]
     levels = [level_of(decode(codes_ref[blocks - 1])) * scale for codes_ref in code_refs]
-    row = lax.broadcasted_iota(jnp.int32, levels[0].shape, 0)
+    line = lax.broadcasted_iota(jnp.int32, levels[0].shape, 0)
     for k, out_ref in zip(order, out_refs):
         number = where_ref[0] ^ k
-        own = [jnp.sum(jnp.where(row == number, level, 0.0), axis=0, keepdims=True) for level in levels]
-        for block in range(6):
-            total = 0.0
-            for codes_ref, level in zip(code_refs, own):
-                value = decode(codes_ref[6 * number + block])
-                total += value * level if block < 2 else value
-            out_ref[block, :, :] = total if block < 2 else total / CODE_TOP
+        own = [jnp.sum(jnp.where(line == number, level, 0.0), axis=0, keepdims=True) for level in levels]
+        linear = [
+            sum(decode(codes_ref[6 * number + side]) * level for codes_ref, level in zip(code_refs, own))
+            for side in range(2)
+        ]
+        peak = jnp.max(jnp.maximum(jnp.abs(linear[0]), jnp.abs(linear[1])), axis=0, keepdims=True)
+        code = level_code(jnp.broadcast_to(peak, linear[0].shape))
+        upscale = CODE_TOP / level_of(code)
+        for side in range(2):
+            out_ref[side, :, :] = encode(linear[side] * upscale)
+        for part in range(2, 6):
+            total = sum(decode(codes_ref[6 * number + part]) for codes_ref in code_refs)
+            out_ref[part, :, :] = encode(total * (1.0 / len(code_refs)))
+        out_ref[6, :, :] = encode(code)
 
 
 def partners(count):
@@ -163,24 +170,34 @@
 
 def stack_kernel(windows, offs_ref, where_ref, *refs):
     sums_refs, out_ref = refs[:-1], refs[-1]
-    blocks, copies, _, _ = out_ref.shape
+    blocks, copies, rows, _ = out_ref.shape
     _, lag_rows, chans = sums_refs[0].shape
-    total = sum(sums_ref[...] for sums_ref in sums_refs) / windows
-    stacks = [
-        total[side] * (total[2 + side] * total[2 + side] + total[4 + side] * total[4 + side]) for side in range(2)
-    ]
+    per_sum = windows // len(sums_refs)
+    levels = [level_of(decode(sums_ref[6])) * (1.0 / (CODE_TOP * windows)) for sums_ref in sums_refs]
+    stacks = []
+    for side in range(2):
+        linear = sum(decode(sums_ref[side]) * level for sums_ref, level in zip(sums_refs, levels))
+        real, imag = (
+            sum(decode(sums_ref[part + side]) for sums_ref in sums_refs) * (per_sum / (CODE_TOP * windows))
+            for part in (2, 4)
+        )
+        stacks.append(linear * (real * real + imag * imag))
     ahead = offs_ref[where_ref[0]] * (chans // blocks)
     lane = lax.broadcasted_iota(jnp.int32, (1, chans), 1)
     behind = [jnp.where(lane >= ahead, pltpu.roll(stack, ahead, 1), 0.0) for stack in stacks]
-    both = jnp.concatenate([stacks[0] + behind[1], stacks[1] + behind[0]], axis=0)
+    back = stacks[1] + behind[0]
+    both = jnp.concatenate(
+        [stacks[0] + behind[1]] + [back[row : row + 1, :] for row in reversed(range(lag_rows))], axis=0
+    )
     wide = 2 * lag_rows
-    turned = jnp.concatenate([both] * (chans // wide), axis=0).T
+    parts = chans // wide
+    turned = jnp.concatenate([both] * parts, axis=0).T
     per_block = chans // blocks
-    rows = per_block // 2
     for block in range(blocks):
-        first = turned[block * per_block : block * per_block + rows, :]
-        second = turned[block * per_block + rows : (block + 1) * per_block, :]
-        piece = jnp.where(lane < wide, first, second)
+        piece = jnp.zeros((rows, chans), jnp.float32)
+        for part in range(parts):
+            begin = block * per_block + part * rows
+            piece = jnp.where(lane // wide == part, turned[begin : begin + rows, :], piece)
         for copy in range(copies):
             out_ref[block, copy, :, :] = piece
 
@@ -189,21 +206,20 @@
     groups, offset_count, rows, lanes = parts_ref.shape
     half = out_ref.shape[2] // 2
     lag_rows = half // groups
+    parts = out_ref.shape[0] // rows
     lane = lax.broadcasted_iota(jnp.int32, (1, lanes), 1)
-    mirror = (
-        lax.broadcasted_iota(jnp.int32, (half, half), 0) + lax.broadcasted_iota(jnp.int32, (half, half), 1) == half - 1
-    ).astype(jnp.float32)
     for number in range(offset_count):
-        for part in range(2):
+        for part in range(parts):
             ahead = jnp.zeros((rows, lanes), jnp.float32)
             back = jnp.zeros((rows, lanes), jnp.float32)
+            begin = part * 2 * lag_rows
             for group in range(groups):
                 piece = parts_ref[group, number]
-                here = (lane >= group * lag_rows) & (lane < (group + 1) * lag_rows)
-                begin = part * 2 * lag_rows
-                ahead = jnp.where(here, pltpu.roll(piece, (group * lag_rows - begin) % lanes, 1), ahead)
-                back = jnp.where(here, pltpu.roll(piece, (group * lag_rows - begin - lag_rows) % lanes, 1), back)
-            back = jnp.dot(back, mirror, precision=lax.Precision.HIGHEST, preferred_element_type=jnp.float32)
+                first, last = group * lag_rows, half - (group + 1) * lag_rows
+                ahead = jnp.where(lane // lag_rows == group, pltpu.roll(piece, (first - begin) % lanes, 1), ahead)
+                back = jnp.where(
+                    lane // lag_rows == groups - 1 - group, pltpu.roll(piece, (last - begin - lag_rows) % lanes, 1), back
+                )
             out_ref[part * rows : (part + 1) * rows, number, 0:half] = back
             out_ref[part * rows : (part + 1) * rows, number, half : 2 * half] = ahead
 
@@ -216,6 +232,7 @@
     half = LAGS // 2
     lag_rows = half // chan_count
     offset_count = offsets.shape[0]
+    piece_rows = 2 * lag_rows // chan_count
     smem = pl.BlockSpec(memory_space=pltpu.SMEM)
     vmem = pl.BlockSpec(memory_space=pltpu.VMEM)
     params = pltpu.CompilerParams(vmem_limit_bytes=VMEM_LIMIT)
@@ -249,7 +266,7 @@
     )(offsets, chan_where, *exchange(pieces, "chan"), quality, table)
     sums = pl.pallas_call(
         functools.partial(sum_kernel, tm_order, 1.0 / (CODE_TOP * math.sqrt(freqs))),
-        out_shape=[jax.ShapeDtypeStruct((6, lag_rows, chans), jnp.float32)] * tm_count,
+        out_shape=[jax.ShapeDtypeStruct((7, lag_rows, chans), jnp.int16)] * tm_count,
         in_specs=[smem] + [vmem] * chan_count,
         out_specs=[vmem] * tm_count,
         compiler_params=params,
@@ -257,13 +274,13 @@
     )(tm_where, *exchange(pairs, "chan"))
     pieces = pl.pallas_call(
         functools.partial(stack_kernel, windows * tm_count),
-        out_shape=jax.ShapeDtypeStruct((chan_count, tm_count, CH_DEV // 2, chans), jnp.float32),
+        out_shape=jax.ShapeDtypeStruct((chan_count, tm_count, piece_rows, chans), jnp.float32),
         in_specs=[smem, smem] + [vmem] * tm_count,
         out_specs=vmem,
         compiler_params=params,
         name="stack_pairs",
     )(offsets, tm_where, *exchange(sums, "tm"))
-    shape = (chan_count * tm_count, CH_DEV // 2, chans)
+    shape = (chan_count * tm_count, piece_rows, chans)
     arrived = lax.all_to_all(pieces.reshape(shape), ("chan", "tm"), 0, 0, tiled=True)
     return pl.pallas_call(
         place_kernel,
@@ -272,7 +289,7 @@
         out_specs=vmem,
         compiler_params=params,
         name="place_lags",
-    )(arrived.reshape(chan_count, tm_count, CH_DEV // 2, chans))
+    )(arrived.reshape(chan_count, tm_count, piece_rows, chans))
 
 
 def shifted(value, axis, steps):

time: 57.9 us -> 55.8 us (0.964)
  blocking collectives: 12.6 us -> 11.1 us
    all_to_all x1, blocking collectives: 12.6 us -> 11.1 us  [window_shards(): lax.all_to_all(pieces.reshape(shape), ('chan', 'tm'), 0, 0, tiled=True)]
where the time goes in v8:
time: 55.8 us; the launch traced here: 55.6 us
  waiting for transfers between devices  19.5 us (35%)
  starting transfers between devices  17.7 us (32%)
  blocking collectives  11.1 us (20%)
  Pallas kernels  7.2 us (13%)
    ppermute x17, waiting for transfers between devices, exchange(): lax.ppermute(piece, axis, [(source, source ^ k) for source in range(count)])  19.5 us
    ppermute x17, starting transfers between devices, exchange(): lax.ppermute(piece, axis, [(source, source ^ k) for source in range(count)])  17.7 us
    all_to_all x1, blocking collectives, window_shards(): lax.all_to_all(pieces.reshape(shape), ('chan', 'tm'), 0, 0, tiled=True)  11.1 us
    pallas_call x1, Pallas kernels, window_shards(): pl.pallas_call(functools.partial(window_kernel, chan_order), out_shape=[j...  3.87 us
    pallas_call x1, Pallas kernels, window_shards(): pl.pallas_call(functools.partial(split_kernel, chan_order), out_shape=[ja...  1.43 us
  transfers between devices with their start and end apart: 17, of which 12 were waited for; matrix products, arithmetic and copies ran while one was open for 0% of the time, Pallas kernels for 0%

profile of v8, /device:TPU:0, one launch (start us, length us, event | category | flops | bytes accessed | tf_op | source)
XLA Modules:
  0.0 55.6 jit_solution(13409245220679130991)
XLA Ops:
  0.0 1.4 %split_windows.1 = (bf16[2,256,128]{2,1,0:T(8,128)(2,1)S(1)}, bf16[2,256,128]{2,1,0:T(8,128)(2,1)S(1)}, bf16[2,256,128]{2,1,0:T(8,128)(2,1)S(1)}, bf16[2,256,128...) custom-call(s32[1]{0:T(128)} %bitcast.1.where_ref, ...), custom_call_target="tpu_custom_call" | custom-call | tf_op jit(solution)/shard_map/split_windows/pallas_call | solution.py:245
  1.4 4.0 %collective-permute-start = (bf16[2,256,128]{2,1,0:T(8,128)(2,1)S(1)}, bf16[2,256,128]{2,1,0:T(8,128)(2,1)S(1)}, u32[]{:S(2)}, u32[]{:S(2)}) collective-permute-start(bf16[2,256,128]{2,1,0:T(8,128)(2,1)S(1)} %get-tuple-element.25), channel_id=1, source_target_pairs={{0,24},{4,28},{8,16},{12,20},{16,8},{20,12},{24,0},{28,4},{1,25},{... | collective-permute-start | bytes 393224 | tf_op jit(solution)/shard_map/ppermute | solution.py:154
  5.4 1.1 %collective-permute-start.2 = (bf16[2,256,128]{2,1,0:T(8,128)(2,1)S(1)}, bf16[2,256,128]{2,1,0:T(8,128)(2,1)S(1)}, u32[]{:S(2)}, u32[]{:S(2)}) collective-permute-start(bf16[2,256,128]{2,1,0:T(8,128)(2,1)S(1)} %get-tuple-element.27), channel_id=1, source_target_pairs={{0,8},{4,12},{8,0},{12,4},{16,24},{20,28},{24,16},{28,20},{1,9},{5... | collective-permute-start | bytes 393224 | tf_op jit(solution)/shard_map/ppermute | solution.py:154
  6.5 1.5 %collective-permute-start.3 = (bf16[2,256,128]{2,1,0:T(8,128)(2,1)S(1)}, bf16[2,256,128]{2,1,0:T(8,128)(2,1)S(1)}, u32[]{:S(2)}, u32[]{:S(2)}) collective-permute-start(bf16[2,256,128]{2,1,0:T(8,128)(2,1)S(1)} %get-tuple-element.28), channel_id=1, source_target_pairs={{0,16},{4,20},{8,24},{12,28},{16,0},{20,4},{24,8},{28,12},{1,17},{... | collective-permute-start | bytes 393224 | tf_op jit(solution)/shard_map/ppermute | solution.py:154
  8.6 0.7 %collective-permute-done.refs_0_ = bf16[2,256,128]{2,1,0:T(8,128)(2,1)S(1)} collective-permute-done((bf16[2,256,128]{2,1,0:T(8,128)(2,1)S(1)}, bf16[2,256,128]{2,1,0:T(8,128)(2,1)S(1)}, u32[]{:S(2)}, u32[]{:S(2)}) %collective-permute-start) | collective-permute-done | bytes 131104 | tf_op jit(solution)/shard_map/ppermute | solution.py:154
  9.3 2.8 %collective-permute-done.1.refs_1_ = bf16[2,256,128]{2,1,0:T(8,128)(2,1)S(1)} collective-permute-done((bf16[2,256,128]{2,1,0:T(8,128)(2,1)S(1)}, bf16[2,256,128]{2,1,0:T(8,128)(2,1)S(1)}, u32[]{:S(2)}, u32[]{:S(2)}) %collective-permute-start.1) | collective-permute-done | bytes 131104 | tf_op jit(solution)/shard_map/ppermute | solution.py:154
  12.2 3.4 %collective-permute-done.2.refs_2_ = bf16[2,256,128]{2,1,0:T(8,128)(2,1)S(1)} collective-permute-done((bf16[2,256,128]{2,1,0:T(8,128)(2,1)S(1)}, bf16[2,256,128]{2,1,0:T(8,128)(2,1)S(1)}, u32[]{:S(2)}, u32[]{:S(2)}) %collective-permute-start.2) | collective-permute-done | bytes 131104 | tf_op jit(solution)/shard_map/ppermute | solution.py:154
  15.6 1.1 %collective-permute-done.4.refs_4_ = bf16[2,256,128]{2,1,0:T(8,128)(2,1)S(1)} collective-permute-done((bf16[2,256,128]{2,1,0:T(8,128)(2,1)S(1)}, bf16[2,256,128]{2,1,0:T(8,128)(2,1)S(1)}, u32[]{:S(2)}, u32[]{:S(2)}) %collective-permute-start.4) | collective-permute-done | bytes 131104 | tf_op jit(solution)/shard_map/ppermute | solution.py:154
  16.7 0.7 %collective-permute-done.5.refs_5_ = bf16[2,256,128]{2,1,0:T(8,128)(2,1)S(1)} collective-permute-done((bf16[2,256,128]{2,1,0:T(8,128)(2,1)S(1)}, bf16[2,256,128]{2,1,0:T(8,128)(2,1)S(1)}, u32[]{:S(2)}, u32[]{:S(2)}) %collective-permute-start.5) | collective-permute-done | bytes 131104 | tf_op jit(solution)/shard_map/ppermute | solution.py:154
  17.4 3.9 %window_pairs.1 = (s16[25,16,128]{2,1,0:T(8,128)(2,1)S(1)}, s16[25,16,128]{2,1,0:T(8,128)(2,1)S(1)}, s16[25,16,128]{2,1,0:T(8,128)(2,1)S(1)}, s16[25,16,128]{2,1...) custom-call(s32[4]{0:T(128)S(1)} %copy-done.2, ...), custom_call_target="tpu_custom_call" | custom-call | tf_op jit(solution)/shard_map/window_pairs/pallas_call | solution.py:254
  21.3 2.6 %collective-permute-start.7 = (s16[25,16,128]{2,1,0:T(8,128)(2,1)S(1)}, s16[25,16,128]{2,1,0:T(8,128)(2,1)S(1)}, u32[]{:S(2)}, u32[]{:S(2)}) collective-permute-start(s16[25,16,128]{2,1,0:T(8,128)(2,1)S(1)} %get-tuple-element.33), channel_id=1, source_target_pairs={{0,24},{4,28},{8,16},{12,20},{16,8},{20,12},{24,0},{28,4},{1,25},{... | collective-permute-start | bytes 307208 | tf_op jit(solution)/shard_map/ppermute | solution.py:154
  23.9 1.4 %collective-permute-start.9 = (s16[25,16,128]{2,1,0:T(8,128)(2,1)S(1)}, s16[25,16,128]{2,1,0:T(8,128)(2,1)S(1)}, u32[]{:S(2)}, u32[]{:S(2)}) collective-permute-start(s16[25,16,128]{2,1,0:T(8,128)(2,1)S(1)} %get-tuple-element.35), channel_id=1, source_target_pairs={{0,8},{4,12},{8,0},{12,4},{16,24},{20,28},{24,16},{28,20},{1,9},{5... | collective-permute-start | bytes 307208 | tf_op jit(solution)/shard_map/ppermute | solution.py:154
  25.3 1.6 %collective-permute-start.10 = (s16[25,16,128]{2,1,0:T(8,128)(2,1)S(1)}, s16[25,16,128]{2,1,0:T(8,128)(2,1)S(1)}, u32[]{:S(2)}, u32[]{:S(2)}) collective-permute-start(s16[25,16,128]{2,1,0:T(8,128)(2,1)S(1)} %get-tuple-element.36), channel_id=1, source_target_pairs={{0,16},{4,20},{8,24},{12,28},{16,0},{20,4},{24,8},{28,12},{1,17},{... | collective-permute-start | bytes 307208 | tf_op jit(solution)/shard_map/ppermute | solution.py:154
  27.7 2.4 %collective-permute-done.8.refs_1_ = s16[25,16,128]{2,1,0:T(8,128)(2,1)S(1)} collective-permute-done((s16[25,16,128]{2,1,0:T(8,128)(2,1)S(1)}, s16[25,16,128]{2,1,0:T(8,128)(2,1)S(1)}, u32[]{:S(2)}, u32[]{:S(2)}) %collective-permute-start.8) | collective-permute-done | bytes 102432 | tf_op jit(solution)/shard_map/ppermute | solution.py:154
  30.1 2.2 %collective-permute-done.9.refs_2_ = s16[25,16,128]{2,1,0:T(8,128)(2,1)S(1)} collective-permute-done((s16[25,16,128]{2,1,0:T(8,128)(2,1)S(1)}, s16[25,16,128]{2,1,0:T(8,128)(2,1)S(1)}, u32[]{:S(2)}, u32[]{:S(2)}) %collective-permute-start.9) | collective-permute-done | bytes 102432 | tf_op jit(solution)/shard_map/ppermute | solution.py:154
  32.3 1.0 %collective-permute-done.11.refs_4_ = s16[25,16,128]{2,1,0:T(8,128)(2,1)S(1)} collective-permute-done((s16[25,16,128]{2,1,0:T(8,128)(2,1)S(1)}, s16[25,16,128]{2,1,0:T(8,128)(2,1)S(1)}, u32[]{:S(2)}, u32[]{:S(2)}) %collective-permute-start.11) | collective-permute-done | bytes 102432 | tf_op jit(solution)/shard_map/ppermute | solution.py:154
  33.3 1.0 %collective-permute-done.12.refs_5_ = s16[25,16,128]{2,1,0:T(8,128)(2,1)S(1)} collective-permute-done((s16[25,16,128]{2,1,0:T(8,128)(2,1)S(1)}, s16[25,16,128]{2,1,0:T(8,128)(2,1)S(1)}, u32[]{:S(2)}, u32[]{:S(2)}) %collective-permute-start.12) | collective-permute-done | bytes 102432 | tf_op jit(solution)/shard_map/ppermute | solution.py:154
  34.6 2.7 %collective-permute-start.14 = (s16[7,16,128]{2,1,0:T(8,128)(2,1)S(1)}, s16[7,16,128]{2,1,0:T(8,128)(2,1)S(1)}, u32[]{:S(2)}, u32[]{:S(2)}) collective-permute-start(s16[7,16,128]{2,1,0:T(8,128)(2,1)S(1)} %get-tuple-element.41), channel_id=1, source_target_pairs={{0,2},{1,3},{2,0},{3,1},{4,6},{5,7},{6,4},{7,5},{8,10},{9,11},{10,... | collective-permute-start | bytes 86024 | tf_op jit(solution)/shard_map/ppermute | solution.py:154
  37.2 1.3 %collective-permute-start.15 = (s16[7,16,128]{2,1,0:T(8,128)(2,1)S(1)}, s16[7,16,128]{2,1,0:T(8,128)(2,1)S(1)}, u32[]{:S(2)}, u32[]{:S(2)}) collective-permute-start(s16[7,16,128]{2,1,0:T(8,128)(2,1)S(1)} %get-tuple-element.42), channel_id=1, source_target_pairs={{0,3},{1,2},{2,1},{3,0},{4,7},{5,6},{6,5},{7,4},{8,11},{9,10},{10,... | collective-permute-start | bytes 86024 | tf_op jit(solution)/shard_map/ppermute | solution.py:154
  38.8 0.9 %collective-permute-done.14.refs_0_ = s16[7,16,128]{2,1,0:T(8,128)(2,1)S(1)} collective-permute-done((s16[7,16,128]{2,1,0:T(8,128)(2,1)S(1)}, s16[7,16,128]{2,1,0:T(8,128)(2,1)S(1)}, u32[]{:S(2)}, u32[]{:S(2)}) %collective-permute-start.14) | collective-permute-done | bytes 28704 | tf_op jit(solution)/shard_map/ppermute | solution.py:154
  39.7 3.2 %collective-permute-done.15.refs_1_ = s16[7,16,128]{2,1,0:T(8,128)(2,1)S(1)} collective-permute-done((s16[7,16,128]{2,1,0:T(8,128)(2,1)S(1)}, s16[7,16,128]{2,1,0:T(8,128)(2,1)S(1)}, u32[]{:S(2)}, u32[]{:S(2)}) %collective-permute-start.15) | collective-permute-done | bytes 28704 | tf_op jit(solution)/shard_map/ppermute | solution.py:154
  42.9 0.7 %stack_pairs.1 = f32[8,4,4,128]{3,2,1,0:T(4,128)S(1)} custom-call(s32[4]{0:T(128)S(1)} %copy-done.2, s32[1]{0:T(128)} %bitcast.where_ref, s16[7,16,128]{2,1,0:T(8,128)(2,1)S(1)} %collective-permute-done.14.refs_0_, s16[7,16,128]{2,1,0:T(8,128)(2,1)S(1)} %collective-permute-done.15.refs_1_, s16[7,16,128]{2,1,0:T(8,128)(2,1)S(1)} %collective-permute-done.16.refs_2_, ...), custom_call_target="tpu_custom_call" | custom-call | tf_op jit(solution)/shard_map/stack_pairs/pallas_call | solution.py:275
  43.6 11.1 %all_to_all.5 = f32[32,4,128]{2,1,0:T(4,128)S(1)} all-to-all(f32[32,4,128]{2,1,0:T(4,128)S(1)} %bitcast.5), channel_id=1, replica_groups=mesh['chan'=8,'tm'=4] {'chan','tm'}, dimensions={0} | all-to-all | bytes 131072 | tf_op jit(solution)/shard_map/all_to_all | solution.py:284
  54.7 0.9 %place_lags.1 = f32[16,4,256]{2,1,0:T(4,128)} custom-call(f32[8,4,4,128]{3,2,1,0:T(4,128)S(1)} %bitcast.4), custom_call_target="tpu_custom_call" | custom-call | tf_op jit(solution)/shard_map/place_lags/pallas_call | solution.py:285
  (22 shorter events, 2.0 us)
Async XLA Ops:
  0.0 17.4 %copy-start = (bf16[2,8,16,2048]{3,2,1,0:T(8,128)(2,1)S(1)}, bf16[2,8,16,2048]{3,2,1,0:T(8,128)(2,1)}, u32[]{:S(2)}) copy-start(bf16[2,8,16,2048]{3,2,1,0:T(8,128)(2,1)} %constant.11.clone.refs_9_) | copy-start | bytes 3145732
  1.4 7.9 %collective-permute-start = (bf16[2,256,128]{2,1,0:T(8,128)(2,1)S(1)}, bf16[2,256,128]{2,1,0:T(8,128)(2,1)S(1)}, u32[]{:S(2)}, u32[]{:S(2)}) collective-permute-start(bf16[2,256,128]{2,1,0:T(8,128)(2,1)S(1)} %get-tuple-element.25), channel_id=1, source_target_pairs={{0,24},{4,28},{8,16},{12,20},{16,8},{20,12},{24,0},{28,4},{1,25},{... | collective-permute-start | bytes 393224 | tf_op jit(solution)/shard_map/ppermute | solution.py:154
  5.4 6.8 %collective-permute-start.1 = (bf16[2,256,128]{2,1,0:T(8,128)(2,1)S(1)}, bf16[2,256,128]{2,1,0:T(8,128)(2,1)S(1)}, u32[]{:S(2)}, u32[]{:S(2)}) collective-permute-start(bf16[2,256,128]{2,1,0:T(8,128)(2,1)S(1)} %get-tuple-element.26), channel_id=1, source_target_pairs={{0,28},{4,24},{8,20},{12,16},{16,12},{20,8},{24,4},{28,0},{1,29},{... | collective-permute-start | bytes 393224 | tf_op jit(solution)/shard_map/ppermute | solution.py:154
  5.4 10.2 %collective-permute-start.2 = (bf16[2,256,128]{2,1,0:T(8,128)(2,1)S(1)}, bf16[2,256,128]{2,1,0:T(8,128)(2,1)S(1)}, u32[]{:S(2)}, u32[]{:S(2)}) collective-permute-start(bf16[2,256,128]{2,1,0:T(8,128)(2,1)S(1)} %get-tuple-element.27), channel_id=1, source_target_pairs={{0,8},{4,12},{8,0},{12,4},{16,24},{20,28},{24,16},{28,20},{1,9},{5... | collective-permute-start | bytes 393224 | tf_op jit(solution)/shard_map/ppermute | solution.py:154
  6.5 10.9 %copy-start.1 = (s32[8,128]{1,0:T(8,128)S(1)}, s32[8,128]{1,0:T(8,128)}, u32[]{:S(2)}) copy-start(s32[8,128]{1,0:T(8,128)} %refs_8_.1) | copy-start | bytes 12292
  6.5 9.1 %collective-permute-start.3 = (bf16[2,256,128]{2,1,0:T(8,128)(2,1)S(1)}, bf16[2,256,128]{2,1,0:T(8,128)(2,1)S(1)}, u32[]{:S(2)}, u32[]{:S(2)}) collective-permute-start(bf16[2,256,128]{2,1,0:T(8,128)(2,1)S(1)} %get-tuple-element.28), channel_id=1, source_target_pairs={{0,16},{4,20},{8,24},{12,28},{16,0},{20,4},{24,8},{28,12},{1,17},{... | collective-permute-start | bytes 393224 | tf_op jit(solution)/shard_map/ppermute | solution.py:154
  8.1 8.7 %collective-permute-start.4 = (bf16[2,256,128]{2,1,0:T(8,128)(2,1)S(1)}, bf16[2,256,128]{2,1,0:T(8,128)(2,1)S(1)}, u32[]{:S(2)}, u32[]{:S(2)}) collective-permute-start(bf16[2,256,128]{2,1,0:T(8,128)(2,1)S(1)} %get-tuple-element.29), channel_id=1, source_target_pairs={{0,12},{4,8},{8,4},{12,0},{16,28},{20,24},{24,20},{28,16},{1,13},{... | collective-permute-start | bytes 393224 | tf_op jit(solution)/shard_map/ppermute | solution.py:154
  9.3 8.1 %collective-permute-start.5 = (bf16[2,256,128]{2,1,0:T(8,128)(2,1)S(1)}, bf16[2,256,128]{2,1,0:T(8,128)(2,1)S(1)}, u32[]{:S(2)}, u32[]{:S(2)}) collective-permute-start(bf16[2,256,128]{2,1,0:T(8,128)(2,1)S(1)} %get-tuple-element.30), channel_id=1, source_target_pairs={{0,20},{4,16},{8,28},{12,24},{16,4},{20,0},{24,12},{28,8},{1,21},{... | collective-permute-start | bytes 393224 | tf_op jit(solution)/shard_map/ppermute | solution.py:154
  12.2 5.3 %copy-start.2 = (s32[4]{0:T(128)S(1)}, s32[4]{0:T(128)}, u32[]{:S(2)}) copy-start(s32[4]{0:T(128)} %offs_ref.3) | copy-start | bytes 52
  12.2 5.3 %collective-permute-start.6 = (bf16[2,256,128]{2,1,0:T(8,128)(2,1)S(1)}, bf16[2,256,128]{2,1,0:T(8,128)(2,1)S(1)}, u32[]{:S(2)}, u32[]{:S(2)}) collective-permute-start(bf16[2,256,128]{2,1,0:T(8,128)(2,1)S(1)} %get-tuple-element.31), channel_id=1, source_target_pairs={{0,4},{4,0},{8,12},{12,8},{16,20},{20,16},{24,28},{28,24},{1,5},{5... | collective-permute-start | bytes 393224 | tf_op jit(solution)/shard_map/ppermute | solution.py:154
  21.3 5.9 %collective-permute-start.7 = (s16[25,16,128]{2,1,0:T(8,128)(2,1)S(1)}, s16[25,16,128]{2,1,0:T(8,128)(2,1)S(1)}, u32[]{:S(2)}, u32[]{:S(2)}) collective-permute-start(s16[25,16,128]{2,1,0:T(8,128)(2,1)S(1)} %get-tuple-element.33), channel_id=1, source_target_pairs={{0,24},{4,28},{8,16},{12,20},{16,8},{20,12},{24,0},{28,4},{1,25},{... | collective-permute-start | bytes 307208 | tf_op jit(solution)/shard_map/ppermute | solution.py:154
  23.9 6.2 %collective-permute-start.8 = (s16[25,16,128]{2,1,0:T(8,128)(2,1)S(1)}, s16[25,16,128]{2,1,0:T(8,128)(2,1)S(1)}, u32[]{:S(2)}, u32[]{:S(2)}) collective-permute-start(s16[25,16,128]{2,1,0:T(8,128)(2,1)S(1)} %get-tuple-element.34), channel_id=1, source_target_pairs={{0,28},{4,24},{8,20},{12,16},{16,12},{20,8},{24,4},{28,0},{1,29},{... | collective-permute-start | bytes 307208 | tf_op jit(solution)/shard_map/ppermute | solution.py:154
  23.9 8.4 %collective-permute-start.9 = (s16[25,16,128]{2,1,0:T(8,128)(2,1)S(1)}, s16[25,16,128]{2,1,0:T(8,128)(2,1)S(1)}, u32[]{:S(2)}, u32[]{:S(2)}) collective-permute-start(s16[25,16,128]{2,1,0:T(8,128)(2,1)S(1)} %get-tuple-element.35), channel_id=1, source_target_pairs={{0,8},{4,12},{8,0},{12,4},{16,24},{20,28},{24,16},{28,20},{1,9},{5... | collective-permute-start | bytes 307208 | tf_op jit(solution)/shard_map/ppermute | solution.py:154
  25.3 7.0 %collective-permute-start.10 = (s16[25,16,128]{2,1,0:T(8,128)(2,1)S(1)}, s16[25,16,128]{2,1,0:T(8,128)(2,1)S(1)}, u32[]{:S(2)}, u32[]{:S(2)}) collective-permute-start(s16[25,16,128]{2,1,0:T(8,128)(2,1)S(1)} %get-tuple-element.36), channel_id=1, source_target_pairs={{0,16},{4,20},{8,24},{12,28},{16,0},{20,4},{24,8},{28,12},{1,17},{... | collective-permute-start | bytes 307208 | tf_op jit(solution)/shard_map/ppermute | solution.py:154
  26.8 6.5 %collective-permute-start.11 = (s16[25,16,128]{2,1,0:T(8,128)(2,1)S(1)}, s16[25,16,128]{2,1,0:T(8,128)(2,1)S(1)}, u32[]{:S(2)}, u32[]{:S(2)}) collective-permute-start(s16[25,16,128]{2,1,0:T(8,128)(2,1)S(1)} %get-tuple-element.37), channel_id=1, source_target_pairs={{0,12},{4,8},{8,4},{12,0},{16,28},{20,24},{24,20},{28,16},{1,13},{... | collective-permute-start | bytes 307208 | tf_op jit(solution)/shard_map/ppermute | solution.py:154
  27.2 7.1 %collective-permute-start.12 = (s16[25,16,128]{2,1,0:T(8,128)(2,1)S(1)}, s16[25,16,128]{2,1,0:T(8,128)(2,1)S(1)}, u32[]{:S(2)}, u32[]{:S(2)}) collective-permute-start(s16[25,16,128]{2,1,0:T(8,128)(2,1)S(1)} %get-tuple-element.38), channel_id=1, source_target_pairs={{0,20},{4,16},{8,28},{12,24},{16,4},{20,0},{24,12},{28,8},{1,21},{... | collective-permute-start | bytes 307208 | tf_op jit(solution)/shard_map/ppermute | solution.py:154
  30.1 4.2 %collective-permute-start.13 = (s16[25,16,128]{2,1,0:T(8,128)(2,1)S(1)}, s16[25,16,128]{2,1,0:T(8,128)(2,1)S(1)}, u32[]{:S(2)}, u32[]{:S(2)}) collective-permute-start(s16[25,16,128]{2,1,0:T(8,128)(2,1)S(1)} %get-tuple-element.39), channel_id=1, source_target_pairs={{0,4},{4,0},{8,12},{12,8},{16,20},{20,16},{24,28},{28,24},{1,5},{5... | collective-permute-start | bytes 307208 | tf_op jit(solution)/shard_map/ppermute | solution.py:154
  34.6 5.1 %collective-permute-start.14 = (s16[7,16,128]{2,1,0:T(8,128)(2,1)S(1)}, s16[7,16,128]{2,1,0:T(8,128)(2,1)S(1)}, u32[]{:S(2)}, u32[]{:S(2)}) collective-permute-start(s16[7,16,128]{2,1,0:T(8,128)(2,1)S(1)} %get-tuple-element.41), channel_id=1, source_target_pairs={{0,2},{1,3},{2,0},{3,1},{4,6},{5,7},{6,4},{7,5},{8,10},{9,11},{10,... | collective-permute-start | bytes 86024 | tf_op jit(solution)/shard_map/ppermute | solution.py:154
  37.2 5.7 %collective-permute-start.15 = (s16[7,16,128]{2,1,0:T(8,128)(2,1)S(1)}, s16[7,16,128]{2,1,0:T(8,128)(2,1)S(1)}, u32[]{:S(2)}, u32[]{:S(2)}) collective-permute-start(s16[7,16,128]{2,1,0:T(8,128)(2,1)S(1)} %get-tuple-element.42), channel_id=1, source_target_pairs={{0,3},{1,2},{2,1},{3,0},{4,7},{5,6},{6,5},{7,4},{8,11},{9,10},{10,... | collective-permute-start | bytes 86024 | tf_op jit(solution)/shard_map/ppermute | solution.py:154
  38.6 4.3 %collective-permute-start.16 = (s16[7,16,128]{2,1,0:T(8,128)(2,1)S(1)}, s16[7,16,128]{2,1,0:T(8,128)(2,1)S(1)}, u32[]{:S(2)}, u32[]{:S(2)}) collective-permute-start(s16[7,16,128]{2,1,0:T(8,128)(2,1)S(1)} %get-tuple-element.43), channel_id=1, source_target_pairs={{0,1},{1,0},{2,3},{3,2},{4,5},{5,4},{6,7},{7,6},{8,9},{9,8},{10,11... | collective-permute-start | bytes 86024 | tf_op jit(solution)/shard_map/ppermute | solution.py:154

commit v9 on v8

--- a/solution.py
+++ b/solution.py
@@ -47,12 +47,12 @@
 def window_kernel(order, offs_ref, where_ref, *refs):
     chan_count = len(order)
     spec_refs, (qual_ref, table_ref) = refs[:chan_count], refs[chan_count : chan_count + 2]
-    out_refs = refs[chan_count + 2 : 2 * chan_count + 2]
-    mag_ref, white_ref, cross_ref = refs[2 * chan_count + 2 :]
+    out_refs = refs[chan_count + 2 : chan_count + 4]
+    mag_ref, white_ref, cross_ref = refs[chan_count + 4 :]
     me = where_ref[0]
     _, band, chans = spec_refs[0].shape
     freqs = chan_count * band
-    blocks, lag_rows, _ = out_refs[0].shape
+    chip_count, blocks, lag_rows, _ = out_refs[0].shape
     offset_count = offs_ref.shape[0]
     half = chan_count * lag_rows
     step = 64
@@ -83,7 +83,8 @@
     line = lax.broadcasted_iota(jnp.int32, (lag_rows, chans), 0)
     usable = qual_ref[pl.ds(me, 1), :].astype(jnp.float32)
     levels = jnp.zeros((lag_rows, chans), jnp.float32)
-    table = jnp.concatenate([table_ref[side, me ^ k] for side in range(2) for k in order], axis=0)
+    groups = [k ^ core for core in range(2) for k in chips(chan_count)]
+    table = jnp.concatenate([table_ref[side, me ^ k] for side in range(2) for k in groups], axis=0)
     for number in range(offset_count):
         turn = chans - offs_ref[number] * (chans // chan_count)
         slot = number % 2
@@ -115,10 +116,29 @@
             real, imag = corr[side]
             for kind, value in enumerate((real * upscale, real * inverse, imag * inverse)):
                 coded = encode(value).reshape(chan_count, lag_rows, chans)
-                for k in range(chan_count):
-                    out_refs[k][6 * number + 2 * kind + side, :, :] = coded[k]
-    for k in range(chan_count):
-        out_refs[k][blocks - 1, :, :] = encode(levels)
+                for core in range(2):
+                    rows = slice(core * chip_count, (core + 1) * chip_count)
+                    out_refs[core][:, 6 * number + 2 * kind + side, :, :] = coded[rows]
+    for out_ref in out_refs:
+        for chip in range(chip_count):
+            out_ref[chip, blocks - 1, :, :] = encode(levels)
+
+
+def merge_kernel(own_ref, far_ref, *out_refs):
+    blocks = own_ref.shape[1]
+    for chip, out_ref in enumerate(out_refs):
+        levels = [level_of(decode(ref[chip, blocks - 1])) for ref in (own_ref, far_ref)]
+        code = level_code(levels[0] + levels[1])
+        shares = [level / level_of(code) for level in levels]
+        out_ref[blocks - 1, :, :] = encode(code)
+        for block in range(blocks - 1):
+            number, part = divmod(block, 6)
+            own, far = decode(own_ref[chip, block]), decode(far_ref[chip, block])
+            if part < 2:
+                total = own * shares[0][number : number + 1, :] + far * shares[1][number : number + 1, :]
+            else:
+                total = (own + far) * 0.5
+            out_ref[block, :, :] = encode(total)
 
 
 def sum_kernel(order, scale, where_ref, *refs):
@@ -148,11 +168,15 @@
     return sorted(range(1, count), key=lambda k: (-(k >> 1).bit_count(), k & 1, k)) + [0]
 
 
-def exchange(pieces, axis):
+def chips(count):
+    return [k for k in partners(count) if k % 2 == 0]
+
+
+def exchange(pieces, axis, order):
     count = lax.axis_size(axis)
     return [
         lax.ppermute(piece, axis, [(source, source ^ k) for source in range(count)]) if k else piece
-        for k, piece in zip(partners(count), pieces)
+        for k, piece in zip(order, pieces)
     ]
 
 
@@ -251,11 +275,13 @@
         compiler_params=params,
         name="split_windows",
     )(chan_where, pltpu.with_memory_space_constraint(spectra, pltpu.HBM))
-    pairs = pl.pallas_call(
+    chip_order = chips(chan_count)
+    pair_shape = (6 * offset_count + 1, lag_rows, chans)
+    own, far = pl.pallas_call(
         functools.partial(window_kernel, chan_order),
-        out_shape=[jax.ShapeDtypeStruct((6 * offset_count + 1, lag_rows, chans), jnp.int16)] * chan_count,
+        out_shape=[jax.ShapeDtypeStruct((len(chip_order), *pair_shape), jnp.int16)] * 2,
         in_specs=[smem, smem] + [vmem] * (chan_count + 2),
-        out_specs=[vmem] * chan_count,
+        out_specs=[vmem] * 2,
         scratch_shapes=[
             pltpu.VMEM((freqs, chans), jnp.float32),
             pltpu.VMEM((2, freqs, chans), jnp.bfloat16),
@@ -263,15 +289,23 @@
         ],
         compiler_params=params,
         name="window_pairs",
-    )(offsets, chan_where, *exchange(pieces, "chan"), quality, table)
+    )(offsets, chan_where, *exchange(pieces, "chan", chan_order), quality, table)
+    pairs = pl.pallas_call(
+        merge_kernel,
+        out_shape=[jax.ShapeDtypeStruct(pair_shape, jnp.int16)] * len(chip_order),
+        in_specs=[vmem] * 2,
+        out_specs=[vmem] * len(chip_order),
+        compiler_params=params,
+        name="merge_windows",
+    )(own, *exchange([far], "chan", [1]))
     sums = pl.pallas_call(
         functools.partial(sum_kernel, tm_order, 1.0 / (CODE_TOP * math.sqrt(freqs))),
         out_shape=[jax.ShapeDtypeStruct((7, lag_rows, chans), jnp.int16)] * tm_count,
-        in_specs=[smem] + [vmem] * chan_count,
+        in_specs=[smem] + [vmem] * len(chip_order),
         out_specs=[vmem] * tm_count,
         compiler_params=params,
         name="sum_windows",
-    )(tm_where, *exchange(pairs, "chan"))
+    )(tm_where, *exchange(pairs, "chan", chip_order))
     pieces = pl.pallas_call(
         functools.partial(stack_kernel, windows * tm_count),
         out_shape=jax.ShapeDtypeStruct((chan_count, tm_count, piece_rows, chans), jnp.float32),
@@ -279,7 +313,7 @@
         out_specs=vmem,
         compiler_params=params,
         name="stack_pairs",
-    )(offsets, tm_where, *exchange(sums, "tm"))
+    )(offsets, tm_where, *exchange(sums, "tm", tm_order))
     shape = (chan_count * tm_count, piece_rows, chans)
     arrived = lax.all_to_all(pieces.reshape(shape), ("chan", "tm"), 0, 0, tiled=True)
     return pl.pallas_call(

time: 55.8 us -> 53.4 us (0.957)
  starting transfers between devices: 17.7 us -> 15.2 us
    ppermute x17 -> x14, starting transfers between devices: 17.7 us -> 15.2 us  [exchange(): lax.ppermute(piece, axis, [(source, source ^ k) for source in range(count)])]
    ppermute x17 -> x14, waiting for transfers between devices: 19.5 us -> 19.2 us  [exchange(): lax.ppermute(piece, axis, [(source, source ^ k) for source in range(count)])]
  transfers between devices with their start and end apart: 17 -> 14, of which waited for: 12 -> 10; matrix products, arithmetic and copies ran while one was open for 0% -> 0% of each run, Pallas kernels for 0% -> 0%
where the time goes in v9:
time: 53.4 us; the launch traced here: 53.2 us
  waiting for transfers between devices  19.2 us (36%)
  starting transfers between devices  15.2 us (28%)
  blocking collectives  11.5 us (22%)
  Pallas kernels  7.33 us (14%)
    ppermute x14, waiting for transfers between devices, exchange(): lax.ppermute(piece, axis, [(source, source ^ k) for source in range(count)])  19.2 us
    ppermute x14, starting transfers between devices, exchange(): lax.ppermute(piece, axis, [(source, source ^ k) for source in range(count)])  15.2 us
    all_to_all x1, blocking collectives, window_shards(): lax.all_to_all(pieces.reshape(shape), ('chan', 'tm'), 0, 0, tiled=True)  11.5 us
    pallas_call x1, Pallas kernels, window_shards(): pl.pallas_call(functools.partial(window_kernel, chan_order), out_shape=[j...  3.86 us
    pallas_call x1, Pallas kernels, window_shards(): pl.pallas_call(functools.partial(split_kernel, chan_order), out_shape=[ja...  1.43 us
  transfers between devices with their start and end apart: 14, of which 10 were waited for; matrix products, arithmetic and copies ran while one was open for 0% of the time, Pallas kernels for 0%

profile of v9, /device:TPU:0, one launch (start us, length us, event | category | flops | bytes accessed | tf_op | source)
XLA Modules:
  0.0 53.2 jit_solution(2699073385519517886)
XLA Ops:
  0.0 1.4 %split_windows.1 = (bf16[2,256,128]{2,1,0:T(8,128)(2,1)S(1)}, bf16[2,256,128]{2,1,0:T(8,128)(2,1)S(1)}, bf16[2,256,128]{2,1,0:T(8,128)(2,1)S(1)}, bf16[2,256,128...) custom-call(s32[1]{0:T(128)} %bitcast.1.where_ref, ...), custom_call_target="tpu_custom_call" | custom-call | tf_op jit(solution)/shard_map/split_windows/pallas_call | solution.py:269
  1.4 4.0 %collective-permute-start = (bf16[2,256,128]{2,1,0:T(8,128)(2,1)S(1)}, bf16[2,256,128]{2,1,0:T(8,128)(2,1)S(1)}, u32[]{:S(2)}, u32[]{:S(2)}) collective-permute-start(bf16[2,256,128]{2,1,0:T(8,128)(2,1)S(1)} %get-tuple-element.23), channel_id=1, source_target_pairs={{0,24},{4,28},{8,16},{12,20},{16,8},{20,12},{24,0},{28,4},{1,25},{... | collective-permute-start | bytes 393224 | tf_op jit(solution)/shard_map/ppermute | solution.py:178
  5.4 1.1 %collective-permute-start.2 = (bf16[2,256,128]{2,1,0:T(8,128)(2,1)S(1)}, bf16[2,256,128]{2,1,0:T(8,128)(2,1)S(1)}, u32[]{:S(2)}, u32[]{:S(2)}) collective-permute-start(bf16[2,256,128]{2,1,0:T(8,128)(2,1)S(1)} %get-tuple-element.25), channel_id=1, source_target_pairs={{0,8},{4,12},{8,0},{12,4},{16,24},{20,28},{24,16},{28,20},{1,9},{5... | collective-permute-start | bytes 393224 | tf_op jit(solution)/shard_map/ppermute | solution.py:178
  6.5 1.5 %collective-permute-start.3 = (bf16[2,256,128]{2,1,0:T(8,128)(2,1)S(1)}, bf16[2,256,128]{2,1,0:T(8,128)(2,1)S(1)}, u32[]{:S(2)}, u32[]{:S(2)}) collective-permute-start(bf16[2,256,128]{2,1,0:T(8,128)(2,1)S(1)} %get-tuple-element.26), channel_id=1, source_target_pairs={{0,16},{4,20},{8,24},{12,28},{16,0},{20,4},{24,8},{28,12},{1,17},{... | collective-permute-start | bytes 393224 | tf_op jit(solution)/shard_map/ppermute | solution.py:178
  8.1 0.6 %collective-permute-start.4 = (bf16[2,256,128]{2,1,0:T(8,128)(2,1)S(1)}, bf16[2,256,128]{2,1,0:T(8,128)(2,1)S(1)}, u32[]{:S(2)}, u32[]{:S(2)}) collective-permute-start(bf16[2,256,128]{2,1,0:T(8,128)(2,1)S(1)} %get-tuple-element.27), channel_id=1, source_target_pairs={{0,12},{4,8},{8,4},{12,0},{16,28},{20,24},{24,20},{28,16},{1,13},{... | collective-permute-start | bytes 393224 | tf_op jit(solution)/shard_map/ppermute | solution.py:178
  8.6 0.7 %collective-permute-done.refs_0_ = bf16[2,256,128]{2,1,0:T(8,128)(2,1)S(1)} collective-permute-done((bf16[2,256,128]{2,1,0:T(8,128)(2,1)S(1)}, bf16[2,256,128]{2,1,0:T(8,128)(2,1)S(1)}, u32[]{:S(2)}, u32[]{:S(2)}) %collective-permute-start) | collective-permute-done | bytes 131104 | tf_op jit(solution)/shard_map/ppermute | solution.py:178
  9.3 2.8 %collective-permute-done.1.refs_1_ = bf16[2,256,128]{2,1,0:T(8,128)(2,1)S(1)} collective-permute-done((bf16[2,256,128]{2,1,0:T(8,128)(2,1)S(1)}, bf16[2,256,128]{2,1,0:T(8,128)(2,1)S(1)}, u32[]{:S(2)}, u32[]{:S(2)}) %collective-permute-start.1) | collective-permute-done | bytes 131104 | tf_op jit(solution)/shard_map/ppermute | solution.py:178
  12.2 3.4 %collective-permute-done.2.refs_2_ = bf16[2,256,128]{2,1,0:T(8,128)(2,1)S(1)} collective-permute-done((bf16[2,256,128]{2,1,0:T(8,128)(2,1)S(1)}, bf16[2,256,128]{2,1,0:T(8,128)(2,1)S(1)}, u32[]{:S(2)}, u32[]{:S(2)}) %collective-permute-start.2) | collective-permute-done | bytes 131104 | tf_op jit(solution)/shard_map/ppermute | solution.py:178
  15.6 1.1 %collective-permute-done.4.refs_4_ = bf16[2,256,128]{2,1,0:T(8,128)(2,1)S(1)} collective-permute-done((bf16[2,256,128]{2,1,0:T(8,128)(2,1)S(1)}, bf16[2,256,128]{2,1,0:T(8,128)(2,1)S(1)}, u32[]{:S(2)}, u32[]{:S(2)}) %collective-permute-start.4) | collective-permute-done | bytes 131104 | tf_op jit(solution)/shard_map/ppermute | solution.py:178
  16.7 0.7 %collective-permute-done.5.refs_5_ = bf16[2,256,128]{2,1,0:T(8,128)(2,1)S(1)} collective-permute-done((bf16[2,256,128]{2,1,0:T(8,128)(2,1)S(1)}, bf16[2,256,128]{2,1,0:T(8,128)(2,1)S(1)}, u32[]{:S(2)}, u32[]{:S(2)}) %collective-permute-start.5) | collective-permute-done | bytes 131104 | tf_op jit(solution)/shard_map/ppermute | solution.py:178
  17.4 3.9 %window_pairs.1 = (s16[4,25,16,128]{3,2,1,0:T(8,128)(2,1)S(1)}, s16[4,25,16,128]{3,2,1,0:T(8,128)(2,1)S(1)}) custom-call(s32[4]{0:T(128)S(1)} %copy-done.2, s32[1]{0:T(128)} %bitcast.1.where_ref, bf16[2,256,128]{2,1,0:T(8,128)(2,1)S(1)} %collective-permute-done.refs_0_, bf16[2,256,128]{2,1,0:T(8,128)(2,1)S(1)} %collective-permute-done.1.refs_1_, ...), custom_call_target="tpu_custom_call" | custom-call | tf_op jit(solution)/shard_map/window_pairs/pallas_call | solution.py:280
  21.5 1.6 %collective-permute-done.7.far_ref = s16[4,25,16,128]{3,2,1,0:T(8,128)(2,1)S(1)} collective-permute-done((s16[4,25,16,128]{3,2,1,0:T(8,128)(2,1)S(1)}, s16[4,25,16,128]{3,2,1,0:T(8,128)(2,1)S(1)}, u32[]{:S(2)}, u32[]{:S(2)}) %collective-permute-start.7) | collective-permute-done | bytes 409632 | tf_op jit(solution)/shard_map/ppermute | solution.py:178
  23.4 2.6 %collective-permute-start.8 = (s16[25,16,128]{2,1,0:T(8,128)(2,1)S(1)}, s16[25,16,128]{2,1,0:T(8,128)(2,1)S(1)}, u32[]{:S(2)}, u32[]{:S(2)}) collective-permute-start(s16[25,16,128]{2,1,0:T(8,128)(2,1)S(1)} %get-tuple-element.33), channel_id=1, source_target_pairs={{0,24},{4,28},{8,16},{12,20},{16,8},{20,12},{24,0},{28,4},{1,25},{... | collective-permute-start | bytes 307208 | tf_op jit(solution)/shard_map/ppermute | solution.py:178
  25.9 0.5 %collective-permute-start.9 = (s16[25,16,128]{2,1,0:T(8,128)(2,1)S(1)}, s16[25,16,128]{2,1,0:T(8,128)(2,1)S(1)}, u32[]{:S(2)}, u32[]{:S(2)}) collective-permute-start(s16[25,16,128]{2,1,0:T(8,128)(2,1)S(1)} %get-tuple-element.34), channel_id=1, source_target_pairs={{0,8},{4,12},{8,0},{12,4},{16,24},{20,28},{24,16},{28,20},{1,9},{5... | collective-permute-start | bytes 307208 | tf_op jit(solution)/shard_map/ppermute | solution.py:178
  26.5 0.4 collective-permute-start.10
  26.9 3.1 %collective-permute-done.8.refs_0_ = s16[25,16,128]{2,1,0:T(8,128)(2,1)S(1)} collective-permute-done((s16[25,16,128]{2,1,0:T(8,128)(2,1)S(1)}, s16[25,16,128]{2,1,0:T(8,128)(2,1)S(1)}, u32[]{:S(2)}, u32[]{:S(2)}) %collective-permute-start.8) | collective-permute-done | bytes 102432 | tf_op jit(solution)/shard_map/ppermute | solution.py:178
  30.1 1.5 %collective-permute-done.9.refs_1_ = s16[25,16,128]{2,1,0:T(8,128)(2,1)S(1)} collective-permute-done((s16[25,16,128]{2,1,0:T(8,128)(2,1)S(1)}, s16[25,16,128]{2,1,0:T(8,128)(2,1)S(1)}, u32[]{:S(2)}, u32[]{:S(2)}) %collective-permute-start.9) | collective-permute-done | bytes 102432 | tf_op jit(solution)/shard_map/ppermute | solution.py:178
  31.7 2.7 %collective-permute-start.11 = (s16[7,16,128]{2,1,0:T(8,128)(2,1)S(1)}, s16[7,16,128]{2,1,0:T(8,128)(2,1)S(1)}, u32[]{:S(2)}, u32[]{:S(2)}) collective-permute-start(s16[7,16,128]{2,1,0:T(8,128)(2,1)S(1)} %get-tuple-element.37), channel_id=1, source_target_pairs={{0,2},{1,3},{2,0},{3,1},{4,6},{5,7},{6,4},{7,5},{8,10},{9,11},{10,... | collective-permute-start | bytes 86024 | tf_op jit(solution)/shard_map/ppermute | solution.py:178
  34.4 1.3 %collective-permute-start.12 = (s16[7,16,128]{2,1,0:T(8,128)(2,1)S(1)}, s16[7,16,128]{2,1,0:T(8,128)(2,1)S(1)}, u32[]{:S(2)}, u32[]{:S(2)}) collective-permute-start(s16[7,16,128]{2,1,0:T(8,128)(2,1)S(1)} %get-tuple-element.38), channel_id=1, source_target_pairs={{0,3},{1,2},{2,1},{3,0},{4,7},{5,6},{6,5},{7,4},{8,11},{9,10},{10,... | collective-permute-start | bytes 86024 | tf_op jit(solution)/shard_map/ppermute | solution.py:178
  36.0 0.6 %collective-permute-done.11.refs_0_ = s16[7,16,128]{2,1,0:T(8,128)(2,1)S(1)} collective-permute-done((s16[7,16,128]{2,1,0:T(8,128)(2,1)S(1)}, s16[7,16,128]{2,1,0:T(8,128)(2,1)S(1)}, u32[]{:S(2)}, u32[]{:S(2)}) %collective-permute-start.11) | collective-permute-done | bytes 28704 | tf_op jit(solution)/shard_map/ppermute | solution.py:178
  36.6 3.5 %collective-permute-done.12.refs_1_ = s16[7,16,128]{2,1,0:T(8,128)(2,1)S(1)} collective-permute-done((s16[7,16,128]{2,1,0:T(8,128)(2,1)S(1)}, s16[7,16,128]{2,1,0:T(8,128)(2,1)S(1)}, u32[]{:S(2)}, u32[]{:S(2)}) %collective-permute-start.12) | collective-permute-done | bytes 28704 | tf_op jit(solution)/shard_map/ppermute | solution.py:178
  40.1 0.7 %stack_pairs.1 = f32[8,4,4,128]{3,2,1,0:T(4,128)S(1)} custom-call(s32[4]{0:T(128)S(1)} %copy-done.2, s32[1]{0:T(128)} %bitcast.where_ref, s16[7,16,128]{2,1,0:T(8,128)(2,1)S(1)} %collective-permute-done.11.refs_0_, s16[7,16,128]{2,1,0:T(8,128)(2,1)S(1)} %collective-permute-done.12.refs_1_, s16[7,16,128]{2,1,0:T(8,128)(2,1)S(1)} %collective-permute-done.13.refs_2_, ...), custom_call_target="tpu_custom_call" | custom-call | tf_op jit(solution)/shard_map/stack_pairs/pallas_call | solution.py:309
  40.8 11.5 %all_to_all.5 = f32[32,4,128]{2,1,0:T(4,128)S(1)} all-to-all(f32[32,4,128]{2,1,0:T(4,128)S(1)} %bitcast.5), channel_id=1, replica_groups=mesh['chan'=8,'tm'=4] {'chan','tm'}, dimensions={0} | all-to-all | bytes 131072 | tf_op jit(solution)/shard_map/all_to_all | solution.py:318
  52.3 0.9 %place_lags.1 = f32[16,4,256]{2,1,0:T(4,128)} custom-call(f32[8,4,4,128]{3,2,1,0:T(4,128)S(1)} %bitcast.4), custom_call_target="tpu_custom_call" | custom-call | tf_op jit(solution)/shard_map/place_lags/pallas_call | solution.py:319
  (17 shorter events, 0.8 us)
Async XLA Ops:
  0.0 17.4 %copy-start = (bf16[2,8,16,2048]{3,2,1,0:T(8,128)(2,1)S(1)}, bf16[2,8,16,2048]{3,2,1,0:T(8,128)(2,1)}, u32[]{:S(2)}) copy-start(bf16[2,8,16,2048]{3,2,1,0:T(8,128)(2,1)} %constant.11.clone.refs_9_) | copy-start | bytes 3145732
  1.4 7.9 %collective-permute-start = (bf16[2,256,128]{2,1,0:T(8,128)(2,1)S(1)}, bf16[2,256,128]{2,1,0:T(8,128)(2,1)S(1)}, u32[]{:S(2)}, u32[]{:S(2)}) collective-permute-start(bf16[2,256,128]{2,1,0:T(8,128)(2,1)S(1)} %get-tuple-element.23), channel_id=1, source_target_pairs={{0,24},{4,28},{8,16},{12,20},{16,8},{20,12},{24,0},{28,4},{1,25},{... | collective-permute-start | bytes 393224 | tf_op jit(solution)/shard_map/ppermute | solution.py:178
  5.4 6.8 %collective-permute-start.1 = (bf16[2,256,128]{2,1,0:T(8,128)(2,1)S(1)}, bf16[2,256,128]{2,1,0:T(8,128)(2,1)S(1)}, u32[]{:S(2)}, u32[]{:S(2)}) collective-permute-start(bf16[2,256,128]{2,1,0:T(8,128)(2,1)S(1)} %get-tuple-element.24), channel_id=1, source_target_pairs={{0,28},{4,24},{8,20},{12,16},{16,12},{20,8},{24,4},{28,0},{1,29},{... | collective-permute-start | bytes 393224 | tf_op jit(solution)/shard_map/ppermute | solution.py:178
  5.4 10.2 %collective-permute-start.2 = (bf16[2,256,128]{2,1,0:T(8,128)(2,1)S(1)}, bf16[2,256,128]{2,1,0:T(8,128)(2,1)S(1)}, u32[]{:S(2)}, u32[]{:S(2)}) collective-permute-start(bf16[2,256,128]{2,1,0:T(8,128)(2,1)S(1)} %get-tuple-element.25), channel_id=1, source_target_pairs={{0,8},{4,12},{8,0},{12,4},{16,24},{20,28},{24,16},{28,20},{1,9},{5... | collective-permute-start | bytes 393224 | tf_op jit(solution)/shard_map/ppermute | solution.py:178
  6.5 10.9 %copy-start.1 = (s32[8,128]{1,0:T(8,128)S(1)}, s32[8,128]{1,0:T(8,128)}, u32[]{:S(2)}) copy-start(s32[8,128]{1,0:T(8,128)} %refs_8_.1) | copy-start | bytes 12292
  6.5 9.1 %collective-permute-start.3 = (bf16[2,256,128]{2,1,0:T(8,128)(2,1)S(1)}, bf16[2,256,128]{2,1,0:T(8,128)(2,1)S(1)}, u32[]{:S(2)}, u32[]{:S(2)}) collective-permute-start(bf16[2,256,128]{2,1,0:T(8,128)(2,1)S(1)} %get-tuple-element.26), channel_id=1, source_target_pairs={{0,16},{4,20},{8,24},{12,28},{16,0},{20,4},{24,8},{28,12},{1,17},{... | collective-permute-start | bytes 393224 | tf_op jit(solution)/shard_map/ppermute | solution.py:178
  8.1 8.7 %collective-permute-start.4 = (bf16[2,256,128]{2,1,0:T(8,128)(2,1)S(1)}, bf16[2,256,128]{2,1,0:T(8,128)(2,1)S(1)}, u32[]{:S(2)}, u32[]{:S(2)}) collective-permute-start(bf16[2,256,128]{2,1,0:T(8,128)(2,1)S(1)} %get-tuple-element.27), channel_id=1, source_target_pairs={{0,12},{4,8},{8,4},{12,0},{16,28},{20,24},{24,20},{28,16},{1,13},{... | collective-permute-start | bytes 393224 | tf_op jit(solution)/shard_map/ppermute | solution.py:178
  9.3 8.1 %collective-permute-start.5 = (bf16[2,256,128]{2,1,0:T(8,128)(2,1)S(1)}, bf16[2,256,128]{2,1,0:T(8,128)(2,1)S(1)}, u32[]{:S(2)}, u32[]{:S(2)}) collective-permute-start(bf16[2,256,128]{2,1,0:T(8,128)(2,1)S(1)} %get-tuple-element.28), channel_id=1, source_target_pairs={{0,20},{4,16},{8,28},{12,24},{16,4},{20,0},{24,12},{28,8},{1,21},{... | collective-permute-start | bytes 393224 | tf_op jit(solution)/shard_map/ppermute | solution.py:178
  12.2 5.3 %copy-start.2 = (s32[4]{0:T(128)S(1)}, s32[4]{0:T(128)}, u32[]{:S(2)}) copy-start(s32[4]{0:T(128)} %offs_ref.3) | copy-start | bytes 52
  12.2 5.3 %collective-permute-start.6 = (bf16[2,256,128]{2,1,0:T(8,128)(2,1)S(1)}, bf16[2,256,128]{2,1,0:T(8,128)(2,1)S(1)}, u32[]{:S(2)}, u32[]{:S(2)}) collective-permute-start(bf16[2,256,128]{2,1,0:T(8,128)(2,1)S(1)} %get-tuple-element.29), channel_id=1, source_target_pairs={{0,4},{4,0},{8,12},{12,8},{16,20},{20,16},{24,28},{28,24},{1,5},{5... | collective-permute-start | bytes 393224 | tf_op jit(solution)/shard_map/ppermute | solution.py:178
  21.3 1.8 %collective-permute-start.7 = (s16[4,25,16,128]{3,2,1,0:T(8,128)(2,1)S(1)}, s16[4,25,16,128]{3,2,1,0:T(8,128)(2,1)S(1)}, u32[]{:S(2)}, u32[]{:S(2)}) collective-permute-start(s16[4,25,16,128]{3,2,1,0:T(8,128)(2,1)S(1)} %get-tuple-element.32), channel_id=1, source_target_pairs={{0,4},{4,0},{8,12},{12,8},{16,20},{20,16},{24,28},{28,24},{1,5},{5... | collective-permute-start | bytes 1228808 | tf_op jit(solution)/shard_map/ppermute | solution.py:178
  23.4 6.7 %collective-permute-start.8 = (s16[25,16,128]{2,1,0:T(8,128)(2,1)S(1)}, s16[25,16,128]{2,1,0:T(8,128)(2,1)S(1)}, u32[]{:S(2)}, u32[]{:S(2)}) collective-permute-start(s16[25,16,128]{2,1,0:T(8,128)(2,1)S(1)} %get-tuple-element.33), channel_id=1, source_target_pairs={{0,24},{4,28},{8,16},{12,20},{16,8},{20,12},{24,0},{28,4},{1,25},{... | collective-permute-start | bytes 307208 | tf_op jit(solution)/shard_map/ppermute | solution.py:178
  25.9 5.6 %collective-permute-start.9 = (s16[25,16,128]{2,1,0:T(8,128)(2,1)S(1)}, s16[25,16,128]{2,1,0:T(8,128)(2,1)S(1)}, u32[]{:S(2)}, u32[]{:S(2)}) collective-permute-start(s16[25,16,128]{2,1,0:T(8,128)(2,1)S(1)} %get-tuple-element.34), channel_id=1, source_target_pairs={{0,8},{4,12},{8,0},{12,4},{16,24},{20,28},{24,16},{28,20},{1,9},{5... | collective-permute-start | bytes 307208 | tf_op jit(solution)/shard_map/ppermute | solution.py:178
  26.5 5.1 %collective-permute-start.10 = (s16[25,16,128]{2,1,0:T(8,128)(2,1)S(1)}, s16[25,16,128]{2,1,0:T(8,128)(2,1)S(1)}, u32[]{:S(2)}, u32[]{:S(2)}) collective-permute-start(s16[25,16,128]{2,1,0:T(8,128)(2,1)S(1)} %get-tuple-element.35), channel_id=1, source_target_pairs={{0,16},{4,20},{8,24},{12,28},{16,0},{20,4},{24,8},{28,12},{1,17},{... | collective-permute-start | bytes 307208 | tf_op jit(solution)/shard_map/ppermute | solution.py:178
  31.7 4.8 %collective-permute-start.11 = (s16[7,16,128]{2,1,0:T(8,128)(2,1)S(1)}, s16[7,16,128]{2,1,0:T(8,128)(2,1)S(1)}, u32[]{:S(2)}, u32[]{:S(2)}) collective-permute-start(s16[7,16,128]{2,1,0:T(8,128)(2,1)S(1)} %get-tuple-element.37), channel_id=1, source_target_pairs={{0,2},{1,3},{2,0},{3,1},{4,6},{5,7},{6,4},{7,5},{8,10},{9,11},{10,... | collective-permute-start | bytes 86024 | tf_op jit(solution)/shard_map/ppermute | solution.py:178
  34.4 5.7 %collective-permute-start.12 = (s16[7,16,128]{2,1,0:T(8,128)(2,1)S(1)}, s16[7,16,128]{2,1,0:T(8,128)(2,1)S(1)}, u32[]{:S(2)}, u32[]{:S(2)}) collective-permute-start(s16[7,16,128]{2,1,0:T(8,128)(2,1)S(1)} %get-tuple-element.38), channel_id=1, source_target_pairs={{0,3},{1,2},{2,1},{3,0},{4,7},{5,6},{6,5},{7,4},{8,11},{9,10},{10,... | collective-permute-start | bytes 86024 | tf_op jit(solution)/shard_map/ppermute | solution.py:178
  35.7 4.3 %collective-permute-start.13 = (s16[7,16,128]{2,1,0:T(8,128)(2,1)S(1)}, s16[7,16,128]{2,1,0:T(8,128)(2,1)S(1)}, u32[]{:S(2)}, u32[]{:S(2)}) collective-permute-start(s16[7,16,128]{2,1,0:T(8,128)(2,1)S(1)} %get-tuple-element.39), channel_id=1, source_target_pairs={{0,1},{1,0},{2,3},{3,2},{4,5},{5,4},{6,7},{7,6},{8,9},{9,8},{10,11... | collective-permute-start | bytes 86024 | tf_op jit(solution)/shard_map/ppermute | solution.py:178

commit v10 on v9

--- a/solution.py
+++ b/solution.py
@@ -266,15 +266,18 @@
     chan_where, tm_where = chan_index.reshape(1), tm_index.reshape(1)
 
     chan_order, tm_order = partners(chan_count), partners(tm_count)
-    pieces = pl.pallas_call(
-        functools.partial(split_kernel, chan_order),
-        out_shape=[jax.ShapeDtypeStruct((2, band, chans), spectra.dtype)] * chan_count,
-        in_specs=[smem, pl.BlockSpec(memory_space=pltpu.HBM)],
-        out_specs=[pl.BlockSpec(memory_space=pl.ANY)] * chan_count,
-        scratch_shapes=[pltpu.SemaphoreType.DMA((chan_count,))],
-        compiler_params=params,
-        name="split_windows",
-    )(chan_where, pltpu.with_memory_space_constraint(spectra, pltpu.HBM))
+    spectra = pltpu.with_memory_space_constraint(spectra, pltpu.HBM)
+    pieces = []
+    for part in (chan_order[:2], chan_order[2:]):
+        pieces += pl.pallas_call(
+            functools.partial(split_kernel, part),
+            out_shape=[jax.ShapeDtypeStruct((2, band, chans), spectra.dtype)] * len(part),
+            in_specs=[smem, pl.BlockSpec(memory_space=pltpu.HBM)],
+            out_specs=[pl.BlockSpec(memory_space=pl.ANY)] * len(part),
+            scratch_shapes=[pltpu.SemaphoreType.DMA((len(part),))],
+            compiler_params=params,
+            name="split_windows",
+        )(chan_where, spectra)
     chip_order = chips(chan_count)
     pair_shape = (6 * offset_count + 1, lag_rows, chans)
     own, far = pl.pallas_call(

time: 53.4 us -> 53 us (level)
  waiting for transfers between devices: 19.2 us -> 17.2 us
  Pallas kernels: 7.33 us -> 8.22 us
  starting transfers between devices: 15.2 us -> 15.8 us
    ppermute x14, waiting for transfers between devices: 19.2 us -> 17.2 us  [exchange(): lax.ppermute(piece, axis, [(source, source ^ k) for source in range(count)])]
    pallas_call x1 -> x2, Pallas kernels: 1.43 us -> 2.32 us  [window_shards(): pl.pallas_call(functools.partial(split_kernel, part), out_shape=[jax.Shap...]
    ppermute x14, starting transfers between devices: 15.2 us -> 15.8 us  [exchange(): lax.ppermute(piece, axis, [(source, source ^ k) for source in range(count)])]
  transfers between devices with their start and end apart: 14 -> 14, of which waited for: 10 -> 9; matrix products, arithmetic and copies ran while one was open for 0% -> 0% of each run, Pallas kernels for 0% -> 2%
where the time goes in v10:
time: 53 us; the launch traced here: 52.9 us
  waiting for transfers between devices  17.2 us (32%)
  starting transfers between devices  15.8 us (30%)
  blocking collectives  11.6 us (22%)
  Pallas kernels  8.22 us (16%)
    ppermute x14, waiting for transfers between devices, exchange(): lax.ppermute(piece, axis, [(source, source ^ k) for source in range(count)])  17.2 us
    ppermute x14, starting transfers between devices, exchange(): lax.ppermute(piece, axis, [(source, source ^ k) for source in range(count)])  15.8 us
    all_to_all x1, blocking collectives, window_shards(): lax.all_to_all(pieces.reshape(shape), ('chan', 'tm'), 0, 0, tiled=True)  11.6 us
    pallas_call x1, Pallas kernels, window_shards(): pl.pallas_call(functools.partial(window_kernel, chan_order), out_shape=[j...  3.86 us
    pallas_call x2, Pallas kernels, window_shards(): pl.pallas_call(functools.partial(split_kernel, part), out_shape=[jax.Shap...  2.32 us
  transfers between devices with their start and end apart: 14, of which 9 were waited for; matrix products, arithmetic and copies ran while one was open for 0% of the time, Pallas kernels for 2%

profile of v10, /device:TPU:0, one launch (start us, length us, event | category | flops | bytes accessed | tf_op | source)
XLA Modules:
  0.0 52.9 jit_solution(9425011736530384440)
XLA Ops:
  0.0 1.1 %split_windows.2 = (bf16[2,256,128]{2,1,0:T(8,128)(2,1)S(1)}, bf16[2,256,128]{2,1,0:T(8,128)(2,1)S(1)}) custom-call(s32[1]{0:T(128)} %bitcast.1.where_ref, bf16[2,8,256,128]{3,2,1,0:T(8,128)(2,1)} %spec_ref.3), custom_call_target="tpu_custom_call" | custom-call | tf_op jit(solution)/shard_map/split_windows/pallas_call | solution.py:272
  1.1 4.0 %collective-permute-start = (bf16[2,256,128]{2,1,0:T(8,128)(2,1)S(1)}, bf16[2,256,128]{2,1,0:T(8,128)(2,1)S(1)}, u32[]{:S(2)}, u32[]{:S(2)}) collective-permute-start(bf16[2,256,128]{2,1,0:T(8,128)(2,1)S(1)} %get-tuple-element.23), channel_id=1, source_target_pairs={{0,24},{4,28},{8,16},{12,20},{16,8},{20,12},{24,0},{28,4},{1,25},{... | collective-permute-start | bytes 393224 | tf_op jit(solution)/shard_map/ppermute | solution.py:178
  5.0 1.3 %split_windows.3 = (bf16[2,256,128]{2,1,0:T(8,128)(2,1)S(1)}, bf16[2,256,128]{2,1,0:T(8,128)(2,1)S(1)}, bf16[2,256,128]{2,1,0:T(8,128)(2,1)S(1)}, bf16[2,256,128...) custom-call(s32[1]{0:T(128)} %bitcast.1.where_ref, ...), custom_call_target="tpu_custom_call" | custom-call | tf_op jit(solution)/shard_map/split_windows/pallas_call | solution.py:272
  6.3 1.2 %collective-permute-start.2 = (bf16[2,256,128]{2,1,0:T(8,128)(2,1)S(1)}, bf16[2,256,128]{2,1,0:T(8,128)(2,1)S(1)}, u32[]{:S(2)}, u32[]{:S(2)}) collective-permute-start(bf16[2,256,128]{2,1,0:T(8,128)(2,1)S(1)} %get-tuple-element.25), channel_id=1, source_target_pairs={{0,8},{4,12},{8,0},{12,4},{16,24},{20,28},{24,16},{28,20},{1,9},{5... | collective-permute-start | bytes 393224 | tf_op jit(solution)/shard_map/ppermute | solution.py:178
  7.5 1.5 %collective-permute-start.3 = (bf16[2,256,128]{2,1,0:T(8,128)(2,1)S(1)}, bf16[2,256,128]{2,1,0:T(8,128)(2,1)S(1)}, u32[]{:S(2)}, u32[]{:S(2)}) collective-permute-start(bf16[2,256,128]{2,1,0:T(8,128)(2,1)S(1)} %get-tuple-element.26), channel_id=1, source_target_pairs={{0,16},{4,20},{8,24},{12,28},{16,0},{20,4},{24,8},{28,12},{1,17},{... | collective-permute-start | bytes 393224 | tf_op jit(solution)/shard_map/ppermute | solution.py:178
  9.0 0.6 %collective-permute-start.4 = (bf16[2,256,128]{2,1,0:T(8,128)(2,1)S(1)}, bf16[2,256,128]{2,1,0:T(8,128)(2,1)S(1)}, u32[]{:S(2)}, u32[]{:S(2)}) collective-permute-start(bf16[2,256,128]{2,1,0:T(8,128)(2,1)S(1)} %get-tuple-element.27), channel_id=1, source_target_pairs={{0,12},{4,8},{8,4},{12,0},{16,28},{20,24},{24,20},{28,16},{1,13},{... | collective-permute-start | bytes 393224 | tf_op jit(solution)/shard_map/ppermute | solution.py:178
  9.6 0.6 %collective-permute-start.5 = (bf16[2,256,128]{2,1,0:T(8,128)(2,1)S(1)}, bf16[2,256,128]{2,1,0:T(8,128)(2,1)S(1)}, u32[]{:S(2)}, u32[]{:S(2)}) collective-permute-start(bf16[2,256,128]{2,1,0:T(8,128)(2,1)S(1)} %get-tuple-element.28), channel_id=1, source_target_pairs={{0,20},{4,16},{8,28},{12,24},{16,4},{20,0},{24,12},{28,8},{1,21},{... | collective-permute-start | bytes 393224 | tf_op jit(solution)/shard_map/ppermute | solution.py:178
  10.2 1.6 %collective-permute-done.1.refs_1_ = bf16[2,256,128]{2,1,0:T(8,128)(2,1)S(1)} collective-permute-done((bf16[2,256,128]{2,1,0:T(8,128)(2,1)S(1)}, bf16[2,256,128]{2,1,0:T(8,128)(2,1)S(1)}, u32[]{:S(2)}, u32[]{:S(2)}) %collective-permute-start.1) | collective-permute-done | bytes 131104 | tf_op jit(solution)/shard_map/ppermute | solution.py:178
  11.8 3.5 %collective-permute-done.2.refs_2_ = bf16[2,256,128]{2,1,0:T(8,128)(2,1)S(1)} collective-permute-done((bf16[2,256,128]{2,1,0:T(8,128)(2,1)S(1)}, bf16[2,256,128]{2,1,0:T(8,128)(2,1)S(1)}, u32[]{:S(2)}, u32[]{:S(2)}) %collective-permute-start.2) | collective-permute-done | bytes 131104 | tf_op jit(solution)/shard_map/ppermute | solution.py:178
  15.2 1.1 %collective-permute-done.4.refs_4_ = bf16[2,256,128]{2,1,0:T(8,128)(2,1)S(1)} collective-permute-done((bf16[2,256,128]{2,1,0:T(8,128)(2,1)S(1)}, bf16[2,256,128]{2,1,0:T(8,128)(2,1)S(1)}, u32[]{:S(2)}, u32[]{:S(2)}) %collective-permute-start.4) | collective-permute-done | bytes 131104 | tf_op jit(solution)/shard_map/ppermute | solution.py:178
  16.4 0.7 %collective-permute-done.5.refs_5_ = bf16[2,256,128]{2,1,0:T(8,128)(2,1)S(1)} collective-permute-done((bf16[2,256,128]{2,1,0:T(8,128)(2,1)S(1)}, bf16[2,256,128]{2,1,0:T(8,128)(2,1)S(1)}, u32[]{:S(2)}, u32[]{:S(2)}) %collective-permute-start.5) | collective-permute-done | bytes 131104 | tf_op jit(solution)/shard_map/ppermute | solution.py:178
  17.1 3.9 %window_pairs.1 = (s16[4,25,16,128]{3,2,1,0:T(8,128)(2,1)S(1)}, s16[4,25,16,128]{3,2,1,0:T(8,128)(2,1)S(1)}) custom-call(s32[4]{0:T(128)S(1)} %copy-done.2, s32[1]{0:T(128)} %bitcast.1.where_ref, bf16[2,256,128]{2,1,0:T(8,128)(2,1)S(1)} %collective-permute-done.refs_0_, bf16[2,256,128]{2,1,0:T(8,128)(2,1)S(1)} %collective-permute-done.1.refs_1_, ...), custom_call_target="tpu_custom_call" | custom-call | tf_op jit(solution)/shard_map/window_pairs/pallas_call | solution.py:283
  21.1 1.6 %collective-permute-done.7.far_ref = s16[4,25,16,128]{3,2,1,0:T(8,128)(2,1)S(1)} collective-permute-done((s16[4,25,16,128]{3,2,1,0:T(8,128)(2,1)S(1)}, s16[4,25,16,128]{3,2,1,0:T(8,128)(2,1)S(1)}, u32[]{:S(2)}, u32[]{:S(2)}) %collective-permute-start.7) | collective-permute-done | bytes 409632 | tf_op jit(solution)/shard_map/ppermute | solution.py:178
  23.0 2.6 %collective-permute-start.8 = (s16[25,16,128]{2,1,0:T(8,128)(2,1)S(1)}, s16[25,16,128]{2,1,0:T(8,128)(2,1)S(1)}, u32[]{:S(2)}, u32[]{:S(2)}) collective-permute-start(s16[25,16,128]{2,1,0:T(8,128)(2,1)S(1)} %get-tuple-element.33), channel_id=1, source_target_pairs={{0,24},{4,28},{8,16},{12,20},{16,8},{20,12},{24,0},{28,4},{1,25},{... | collective-permute-start | bytes 307208 | tf_op jit(solution)/shard_map/ppermute | solution.py:178
  26.0 0.5 %collective-permute-start.10 = (s16[25,16,128]{2,1,0:T(8,128)(2,1)S(1)}, s16[25,16,128]{2,1,0:T(8,128)(2,1)S(1)}, u32[]{:S(2)}, u32[]{:S(2)}) collective-permute-start(s16[25,16,128]{2,1,0:T(8,128)(2,1)S(1)} %get-tuple-element.35), channel_id=1, source_target_pairs={{0,16},{4,20},{8,24},{12,28},{16,0},{20,4},{24,8},{28,12},{1,17},{... | collective-permute-start | bytes 307208 | tf_op jit(solution)/shard_map/ppermute | solution.py:178
  26.6 3.1 %collective-permute-done.8.refs_0_ = s16[25,16,128]{2,1,0:T(8,128)(2,1)S(1)} collective-permute-done((s16[25,16,128]{2,1,0:T(8,128)(2,1)S(1)}, s16[25,16,128]{2,1,0:T(8,128)(2,1)S(1)}, u32[]{:S(2)}, u32[]{:S(2)}) %collective-permute-start.8) | collective-permute-done | bytes 102432 | tf_op jit(solution)/shard_map/ppermute | solution.py:178
  29.7 1.4 %collective-permute-done.9.refs_1_ = s16[25,16,128]{2,1,0:T(8,128)(2,1)S(1)} collective-permute-done((s16[25,16,128]{2,1,0:T(8,128)(2,1)S(1)}, s16[25,16,128]{2,1,0:T(8,128)(2,1)S(1)}, u32[]{:S(2)}, u32[]{:S(2)}) %collective-permute-start.9) | collective-permute-done | bytes 102432 | tf_op jit(solution)/shard_map/ppermute | solution.py:178
  31.3 2.7 %collective-permute-start.11 = (s16[7,16,128]{2,1,0:T(8,128)(2,1)S(1)}, s16[7,16,128]{2,1,0:T(8,128)(2,1)S(1)}, u32[]{:S(2)}, u32[]{:S(2)}) collective-permute-start(s16[7,16,128]{2,1,0:T(8,128)(2,1)S(1)} %get-tuple-element.37), channel_id=1, source_target_pairs={{0,2},{1,3},{2,0},{3,1},{4,6},{5,7},{6,4},{7,5},{8,10},{9,11},{10,... | collective-permute-start | bytes 86024 | tf_op jit(solution)/shard_map/ppermute | solution.py:178
  34.0 1.3 %collective-permute-start.12 = (s16[7,16,128]{2,1,0:T(8,128)(2,1)S(1)}, s16[7,16,128]{2,1,0:T(8,128)(2,1)S(1)}, u32[]{:S(2)}, u32[]{:S(2)}) collective-permute-start(s16[7,16,128]{2,1,0:T(8,128)(2,1)S(1)} %get-tuple-element.38), channel_id=1, source_target_pairs={{0,3},{1,2},{2,1},{3,0},{4,7},{5,6},{6,5},{7,4},{8,11},{9,10},{10,... | collective-permute-start | bytes 86024 | tf_op jit(solution)/shard_map/ppermute | solution.py:178
  35.6 0.6 %collective-permute-done.11.refs_0_ = s16[7,16,128]{2,1,0:T(8,128)(2,1)S(1)} collective-permute-done((s16[7,16,128]{2,1,0:T(8,128)(2,1)S(1)}, s16[7,16,128]{2,1,0:T(8,128)(2,1)S(1)}, u32[]{:S(2)}, u32[]{:S(2)}) %collective-permute-start.11) | collective-permute-done | bytes 28704 | tf_op jit(solution)/shard_map/ppermute | solution.py:178
  36.1 3.5 %collective-permute-done.12.refs_1_ = s16[7,16,128]{2,1,0:T(8,128)(2,1)S(1)} collective-permute-done((s16[7,16,128]{2,1,0:T(8,128)(2,1)S(1)}, s16[7,16,128]{2,1,0:T(8,128)(2,1)S(1)}, u32[]{:S(2)}, u32[]{:S(2)}) %collective-permute-start.12) | collective-permute-done | bytes 28704 | tf_op jit(solution)/shard_map/ppermute | solution.py:178
  39.7 0.7 %stack_pairs.1 = f32[8,4,4,128]{3,2,1,0:T(4,128)S(1)} custom-call(s32[4]{0:T(128)S(1)} %copy-done.2, s32[1]{0:T(128)} %bitcast.where_ref, s16[7,16,128]{2,1,0:T(8,128)(2,1)S(1)} %collective-permute-done.11.refs_0_, s16[7,16,128]{2,1,0:T(8,128)(2,1)S(1)} %collective-permute-done.12.refs_1_, s16[7,16,128]{2,1,0:T(8,128)(2,1)S(1)} %collective-permute-done.13.refs_2_, ...), custom_call_target="tpu_custom_call" | custom-call | tf_op jit(solution)/shard_map/stack_pairs/pallas_call | solution.py:312
  40.4 11.6 %all_to_all.5 = f32[32,4,128]{2,1,0:T(4,128)S(1)} all-to-all(f32[32,4,128]{2,1,0:T(4,128)S(1)} %bitcast.5), channel_id=1, replica_groups=mesh['chan'=8,'tm'=4] {'chan','tm'}, dimensions={0} | all-to-all | bytes 131072 | tf_op jit(solution)/shard_map/all_to_all | solution.py:321
  52.0 0.9 %place_lags.1 = f32[16,4,256]{2,1,0:T(4,128)} custom-call(f32[8,4,4,128]{3,2,1,0:T(4,128)S(1)} %bitcast.4), custom_call_target="tpu_custom_call" | custom-call | tf_op jit(solution)/shard_map/place_lags/pallas_call | solution.py:322
  (18 shorter events, 1.3 us)
Async XLA Ops:
  0.0 17.1 %copy-start = (bf16[2,8,16,2048]{3,2,1,0:T(8,128)(2,1)S(1)}, bf16[2,8,16,2048]{3,2,1,0:T(8,128)(2,1)}, u32[]{:S(2)}) copy-start(bf16[2,8,16,2048]{3,2,1,0:T(8,128)(2,1)} %constant.11.clone.refs_9_) | copy-start | bytes 3145732
  1.1 8.5 %collective-permute-start = (bf16[2,256,128]{2,1,0:T(8,128)(2,1)S(1)}, bf16[2,256,128]{2,1,0:T(8,128)(2,1)S(1)}, u32[]{:S(2)}, u32[]{:S(2)}) collective-permute-start(bf16[2,256,128]{2,1,0:T(8,128)(2,1)S(1)} %get-tuple-element.23), channel_id=1, source_target_pairs={{0,24},{4,28},{8,16},{12,20},{16,8},{20,12},{24,0},{28,4},{1,25},{... | collective-permute-start | bytes 393224 | tf_op jit(solution)/shard_map/ppermute | solution.py:178
  5.0 6.7 %collective-permute-start.1 = (bf16[2,256,128]{2,1,0:T(8,128)(2,1)S(1)}, bf16[2,256,128]{2,1,0:T(8,128)(2,1)S(1)}, u32[]{:S(2)}, u32[]{:S(2)}) collective-permute-start(bf16[2,256,128]{2,1,0:T(8,128)(2,1)S(1)} %get-tuple-element.24), channel_id=1, source_target_pairs={{0,28},{4,24},{8,20},{12,16},{16,12},{20,8},{24,4},{28,0},{1,29},{... | collective-permute-start | bytes 393224 | tf_op jit(solution)/shard_map/ppermute | solution.py:178
  6.3 8.9 %collective-permute-start.2 = (bf16[2,256,128]{2,1,0:T(8,128)(2,1)S(1)}, bf16[2,256,128]{2,1,0:T(8,128)(2,1)S(1)}, u32[]{:S(2)}, u32[]{:S(2)}) collective-permute-start(bf16[2,256,128]{2,1,0:T(8,128)(2,1)S(1)} %get-tuple-element.25), channel_id=1, source_target_pairs={{0,8},{4,12},{8,0},{12,4},{16,24},{20,28},{24,16},{28,20},{1,9},{5... | collective-permute-start | bytes 393224 | tf_op jit(solution)/shard_map/ppermute | solution.py:178
  7.5 9.6 %copy-start.1 = (s32[8,128]{1,0:T(8,128)S(1)}, s32[8,128]{1,0:T(8,128)}, u32[]{:S(2)}) copy-start(s32[8,128]{1,0:T(8,128)} %refs_8_.1) | copy-start | bytes 12292
  7.5 7.7 %collective-permute-start.3 = (bf16[2,256,128]{2,1,0:T(8,128)(2,1)S(1)}, bf16[2,256,128]{2,1,0:T(8,128)(2,1)S(1)}, u32[]{:S(2)}, u32[]{:S(2)}) collective-permute-start(bf16[2,256,128]{2,1,0:T(8,128)(2,1)S(1)} %get-tuple-element.26), channel_id=1, source_target_pairs={{0,16},{4,20},{8,24},{12,28},{16,0},{20,4},{24,8},{28,12},{1,17},{... | collective-permute-start | bytes 393224 | tf_op jit(solution)/shard_map/ppermute | solution.py:178
  9.0 7.4 %collective-permute-start.4 = (bf16[2,256,128]{2,1,0:T(8,128)(2,1)S(1)}, bf16[2,256,128]{2,1,0:T(8,128)(2,1)S(1)}, u32[]{:S(2)}, u32[]{:S(2)}) collective-permute-start(bf16[2,256,128]{2,1,0:T(8,128)(2,1)S(1)} %get-tuple-element.27), channel_id=1, source_target_pairs={{0,12},{4,8},{8,4},{12,0},{16,28},{20,24},{24,20},{28,16},{1,13},{... | collective-permute-start | bytes 393224 | tf_op jit(solution)/shard_map/ppermute | solution.py:178
  9.6 7.5 %collective-permute-start.5 = (bf16[2,256,128]{2,1,0:T(8,128)(2,1)S(1)}, bf16[2,256,128]{2,1,0:T(8,128)(2,1)S(1)}, u32[]{:S(2)}, u32[]{:S(2)}) collective-permute-start(bf16[2,256,128]{2,1,0:T(8,128)(2,1)S(1)} %get-tuple-element.28), channel_id=1, source_target_pairs={{0,20},{4,16},{8,28},{12,24},{16,4},{20,0},{24,12},{28,8},{1,21},{... | collective-permute-start | bytes 393224 | tf_op jit(solution)/shard_map/ppermute | solution.py:178
  11.8 5.3 %copy-start.2 = (s32[4]{0:T(128)S(1)}, s32[4]{0:T(128)}, u32[]{:S(2)}) copy-start(s32[4]{0:T(128)} %offs_ref.3) | copy-start | bytes 52
  11.8 5.3 %collective-permute-start.6 = (bf16[2,256,128]{2,1,0:T(8,128)(2,1)S(1)}, bf16[2,256,128]{2,1,0:T(8,128)(2,1)S(1)}, u32[]{:S(2)}, u32[]{:S(2)}) collective-permute-start(bf16[2,256,128]{2,1,0:T(8,128)(2,1)S(1)} %get-tuple-element.29), channel_id=1, source_target_pairs={{0,4},{4,0},{8,12},{12,8},{16,20},{20,16},{24,28},{28,24},{1,5},{5... | collective-permute-start | bytes 393224 | tf_op jit(solution)/shard_map/ppermute | solution.py:178
  21.0 1.8 %collective-permute-start.7 = (s16[4,25,16,128]{3,2,1,0:T(8,128)(2,1)S(1)}, s16[4,25,16,128]{3,2,1,0:T(8,128)(2,1)S(1)}, u32[]{:S(2)}, u32[]{:S(2)}) collective-permute-start(s16[4,25,16,128]{3,2,1,0:T(8,128)(2,1)S(1)} %get-tuple-element.32), channel_id=1, source_target_pairs={{0,4},{4,0},{8,12},{12,8},{16,20},{20,16},{24,28},{28,24},{1,5},{5... | collective-permute-start | bytes 1228808 | tf_op jit(solution)/shard_map/ppermute | solution.py:178
  23.0 6.7 %collective-permute-start.8 = (s16[25,16,128]{2,1,0:T(8,128)(2,1)S(1)}, s16[25,16,128]{2,1,0:T(8,128)(2,1)S(1)}, u32[]{:S(2)}, u32[]{:S(2)}) collective-permute-start(s16[25,16,128]{2,1,0:T(8,128)(2,1)S(1)} %get-tuple-element.33), channel_id=1, source_target_pairs={{0,24},{4,28},{8,16},{12,20},{16,8},{20,12},{24,0},{28,4},{1,25},{... | collective-permute-start | bytes 307208 | tf_op jit(solution)/shard_map/ppermute | solution.py:178
  25.6 5.5 %collective-permute-start.9 = (s16[25,16,128]{2,1,0:T(8,128)(2,1)S(1)}, s16[25,16,128]{2,1,0:T(8,128)(2,1)S(1)}, u32[]{:S(2)}, u32[]{:S(2)}) collective-permute-start(s16[25,16,128]{2,1,0:T(8,128)(2,1)S(1)} %get-tuple-element.34), channel_id=1, source_target_pairs={{0,8},{4,12},{8,0},{12,4},{16,24},{20,28},{24,16},{28,20},{1,9},{5... | collective-permute-start | bytes 307208 | tf_op jit(solution)/shard_map/ppermute | solution.py:178
  26.0 5.1 %collective-permute-start.10 = (s16[25,16,128]{2,1,0:T(8,128)(2,1)S(1)}, s16[25,16,128]{2,1,0:T(8,128)(2,1)S(1)}, u32[]{:S(2)}, u32[]{:S(2)}) collective-permute-start(s16[25,16,128]{2,1,0:T(8,128)(2,1)S(1)} %get-tuple-element.35), channel_id=1, source_target_pairs={{0,16},{4,20},{8,24},{12,28},{16,0},{20,4},{24,8},{28,12},{1,17},{... | collective-permute-start | bytes 307208 | tf_op jit(solution)/shard_map/ppermute | solution.py:178
  31.3 4.8 %collective-permute-start.11 = (s16[7,16,128]{2,1,0:T(8,128)(2,1)S(1)}, s16[7,16,128]{2,1,0:T(8,128)(2,1)S(1)}, u32[]{:S(2)}, u32[]{:S(2)}) collective-permute-start(s16[7,16,128]{2,1,0:T(8,128)(2,1)S(1)} %get-tuple-element.37), channel_id=1, source_target_pairs={{0,2},{1,3},{2,0},{3,1},{4,6},{5,7},{6,4},{7,5},{8,10},{9,11},{10,... | collective-permute-start | bytes 86024 | tf_op jit(solution)/shard_map/ppermute | solution.py:178
  34.0 5.7 %collective-permute-start.12 = (s16[7,16,128]{2,1,0:T(8,128)(2,1)S(1)}, s16[7,16,128]{2,1,0:T(8,128)(2,1)S(1)}, u32[]{:S(2)}, u32[]{:S(2)}) collective-permute-start(s16[7,16,128]{2,1,0:T(8,128)(2,1)S(1)} %get-tuple-element.38), channel_id=1, source_target_pairs={{0,3},{1,2},{2,1},{3,0},{4,7},{5,6},{6,5},{7,4},{8,11},{9,10},{10,... | collective-permute-start | bytes 86024 | tf_op jit(solution)/shard_map/ppermute | solution.py:178
  35.3 4.3 %collective-permute-start.13 = (s16[7,16,128]{2,1,0:T(8,128)(2,1)S(1)}, s16[7,16,128]{2,1,0:T(8,128)(2,1)S(1)}, u32[]{:S(2)}, u32[]{:S(2)}) collective-permute-start(s16[7,16,128]{2,1,0:T(8,128)(2,1)S(1)} %get-tuple-element.39), channel_id=1, source_target_pairs={{0,1},{1,0},{2,3},{3,2},{4,5},{5,4},{6,7},{7,6},{8,9},{9,8},{10,11... | collective-permute-start | bytes 86024 | tf_op jit(solution)/shard_map/ppermute | solution.py:178

commit v11 on v10

--- a/solution.py
+++ b/solution.py
@@ -42,6 +42,19 @@
     turns = np.mod(freq_index * double_lag, 4 * freq_count).astype(np.float32)
     angles = turns * np.float32(2.0 * math.pi / (4 * freq_count))
     return np.concatenate([np.cos(angles), np.sin(angles)]).astype(jnp.bfloat16)
+
+
+def widest(offs_ref, reach):
+    last = offs_ref.shape[0] - 1
+    found = last
+    for number in reversed(range(last)):
+        found = jnp.where(offs_ref[number] == reach, number, found)
+    return found
+
+
+def offset_of(slot, offs_ref, reach):
+    last, wide = offs_ref.shape[0] - 1, widest(offs_ref, reach)
+    return offs_ref[jnp.where(slot == wide, last, jnp.where(slot == last, wide, slot))]
 
 
 def window_kernel(order, offs_ref, where_ref, *refs):
@@ -86,7 +99,7 @@
     groups = [k ^ core for core in range(2) for k in chips(chan_count)]
     table = jnp.concatenate([table_ref[side, me ^ k] for side in range(2) for k in groups], axis=0)
     for number in range(offset_count):
-        turn = chans - offs_ref[number] * (chans // chan_count)
+        turn = chans - offset_of(number, offs_ref, chan_count // 2) * (chans // chan_count)
         slot = number % 2
         for row in range(0, freqs, step):
             own = [white_ref[part, row : row + step, :] for part in range(2)]
@@ -108,17 +121,23 @@
         extra = 0.25 * (mean_power + 1e-06 * freqs)
         peak = jnp.max(jnp.maximum(jnp.abs(corr[0][0]), jnp.abs(corr[1][0])), axis=0, keepdims=True)
         code = level_code(peak)
-        levels = jnp.where(line == number, code, levels)
         keep = jnp.where(lane < turn, usable * pltpu.roll(usable, turn, 1), 0.0) * CODE_TOP
         upscale = keep / level_of(code)
-        for side in range(2):
-            inverse = lax.rsqrt(power[side] + extra) * keep
-            real, imag = corr[side]
-            for kind, value in enumerate((real * upscale, real * inverse, imag * inverse)):
-                coded = encode(value).reshape(chan_count, lag_rows, chans)
-                for core in range(2):
-                    rows = slice(core * chip_count, (core + 1) * chip_count)
-                    out_refs[core][:, 6 * number + 2 * kind + side, :, :] = coded[rows]
+        inverse = [lax.rsqrt(side + extra) * keep for side in power]
+        kinds = [
+            [real * upscale for real, _ in corr],
+            [real * scale for (real, _), scale in zip(corr, inverse)],
+            [imag * scale for (_, imag), scale in zip(corr, inverse)],
+        ]
+        if number == offset_count - 1:
+            code = jnp.where(lane < chans // 2, code, pltpu.roll(code, chans // 2, 1))
+            kinds = [[jnp.where(lane < chans // 2, ahead, pltpu.roll(back, chans // 2, 1))] for ahead, back in kinds]
+        levels = jnp.where(line == number, code, levels)
+        for place, value in enumerate(value for kind in kinds for value in kind):
+            coded = encode(value).reshape(chan_count, lag_rows, chans)
+            for core in range(2):
+                rows = slice(core * chip_count, (core + 1) * chip_count)
+                out_refs[core][:, 6 * number + place, :, :] = coded[rows]
     for out_ref in out_refs:
         for chip in range(chip_count):
             out_ref[chip, blocks - 1, :, :] = encode(levels)
@@ -133,8 +152,9 @@
         out_ref[blocks - 1, :, :] = encode(code)
         for block in range(blocks - 1):
             number, part = divmod(block, 6)
+            linear = part < (2 if blocks - 1 - 6 * number > 3 else 1)
             own, far = decode(own_ref[chip, block]), decode(far_ref[chip, block])
-            if part < 2:
+            if linear:
                 total = own * shares[0][number : number + 1, :] + far * shares[1][number : number + 1, :]
             else:
                 total = (own + far) * 0.5
@@ -142,26 +162,32 @@
 
 
 def sum_kernel(order, scale, where_ref, *refs):
-    code_refs, out_refs = refs[: -len(order)], refs[-len(order) :]
-    blocks = code_refs[0].shape[0]
+    code_refs, out_refs, held_ref = refs[: -len(order) - 1], refs[-len(order) - 1 : -1], refs[-1]
+    blocks, _, chans = code_refs[0].shape
+    slots = held_ref.shape[0]
     levels = [level_of(decode(codes_ref[blocks - 1])) * scale for codes_ref in code_refs]
-    line = lax.broadcasted_iota(jnp.int32, levels[0].shape, 0)
+    low = lax.broadcasted_iota(jnp.int32, (1, chans), 1) < chans // 2
+    for number in range(slots):
+        sides = 2 if number < slots - 1 else 1
+        own = [level[number : number + 1, :] for level in levels]
+        sums = []
+        for place in range(3 * sides):
+            codes = [decode(codes_ref[6 * number + place]) for codes_ref in code_refs]
+            if place < sides:
+                sums.append(sum(code * level for code, level in zip(codes, own)))
+            else:
+                sums.append(sum(codes) * (1.0 / len(code_refs)))
+        if sides == 1:
+            sums = [
+                jnp.where(low, side, 0.0) for value in sums for side in (value, pltpu.roll(value, chans // 2, 1))
+            ]
+        peak = jnp.max(jnp.maximum(jnp.abs(sums[0]), jnp.abs(sums[1])), axis=0, keepdims=True)
+        code = level_code(jnp.broadcast_to(peak, sums[0].shape))
+        upscale = CODE_TOP / level_of(code)
+        for part, value in enumerate([sums[0] * upscale, sums[1] * upscale, *sums[2:], code]):
+            held_ref[number, part, :, :] = encode(value)
     for k, out_ref in zip(order, out_refs):
-        number = where_ref[0] ^ k
-        own = [jnp.sum(jnp.where(line == number, level, 0.0), axis=0, keepdims=True) for level in levels]
-        linear = [
-            sum(decode(codes_ref[6 * number + side]) * level for codes_ref, level in zip(code_refs, own))
-            for side in range(2)
-        ]
-        peak = jnp.max(jnp.maximum(jnp.abs(linear[0]), jnp.abs(linear[1])), axis=0, keepdims=True)
-        code = level_code(jnp.broadcast_to(peak, linear[0].shape))
-        upscale = CODE_TOP / level_of(code)
-        for side in range(2):
-            out_ref[side, :, :] = encode(linear[side] * upscale)
-        for part in range(2, 6):
-            total = sum(decode(codes_ref[6 * number + part]) for codes_ref in code_refs)
-            out_ref[part, :, :] = encode(total * (1.0 / len(code_refs)))
-        out_ref[6, :, :] = encode(code)
+        out_ref[...] = held_ref[where_ref[0] ^ k]
 
 
 def partners(count):
@@ -206,7 +232,7 @@
             for part in (2, 4)
         )
         stacks.append(linear * (real * real + imag * imag))
-    ahead = offs_ref[where_ref[0]] * (chans // blocks)
+    ahead = offset_of(where_ref[0], offs_ref, blocks // 2) * (chans // blocks)
     lane = lax.broadcasted_iota(jnp.int32, (1, chans), 1)
     behind = [jnp.where(lane >= ahead, pltpu.roll(stack, ahead, 1), 0.0) for stack in stacks]
     back = stacks[1] + behind[0]
@@ -226,26 +252,33 @@
             out_ref[block, copy, :, :] = piece
 
 
-def place_kernel(parts_ref, out_ref):
+def place_kernel(offs_ref, parts_ref, out_ref):
     groups, offset_count, rows, lanes = parts_ref.shape
     half = out_ref.shape[2] // 2
     lag_rows = half // groups
     parts = out_ref.shape[0] // rows
     lane = lax.broadcasted_iota(jnp.int32, (1, lanes), 1)
-    for number in range(offset_count):
-        for part in range(parts):
+    last, wide = offset_count - 1, widest(offs_ref, groups // 2)
+    for part in range(parts):
+        begin = part * 2 * lag_rows
+        slots = []
+        for number in range(offset_count):
             ahead = jnp.zeros((rows, lanes), jnp.float32)
             back = jnp.zeros((rows, lanes), jnp.float32)
-            begin = part * 2 * lag_rows
             for group in range(groups):
                 piece = parts_ref[group, number]
-                first, last = group * lag_rows, half - (group + 1) * lag_rows
+                first, end = group * lag_rows, half - (group + 1) * lag_rows
                 ahead = jnp.where(lane // lag_rows == group, pltpu.roll(piece, (first - begin) % lanes, 1), ahead)
                 back = jnp.where(
-                    lane // lag_rows == groups - 1 - group, pltpu.roll(piece, (last - begin - lag_rows) % lanes, 1), back
+                    lane // lag_rows == groups - 1 - group, pltpu.roll(piece, (end - begin - lag_rows) % lanes, 1), back
                 )
-            out_ref[part * rows : (part + 1) * rows, number, 0:half] = back
-            out_ref[part * rows : (part + 1) * rows, number, half : 2 * half] = ahead
+            slots.append((back, ahead))
+        for number in range(offset_count):
+            for side in range(2):
+                value = slots[number][side]
+                for other in range(last) if number == last else [last]:
+                    value = jnp.where(wide == min(number, other), slots[other][side], value)
+                out_ref[part * rows : (part + 1) * rows, number, side * half : (side + 1) * half] = value
 
 
 def window_shards(spectra, quality, offsets):
@@ -279,7 +312,7 @@
             name="split_windows",
         )(chan_where, spectra)
     chip_order = chips(chan_count)
-    pair_shape = (6 * offset_count + 1, lag_rows, chans)
+    pair_shape = (6 * offset_count - 2, lag_rows, chans)
     own, far = pl.pallas_call(
         functools.partial(window_kernel, chan_order),
         out_shape=[jax.ShapeDtypeStruct((len(chip_order), *pair_shape), jnp.int16)] * 2,
@@ -306,6 +339,7 @@
         out_shape=[jax.ShapeDtypeStruct((7, lag_rows, chans), jnp.int16)] * tm_count,
         in_specs=[smem] + [vmem] * len(chip_order),
         out_specs=[vmem] * tm_count,
+        scratch_shapes=[pltpu.VMEM((offset_count, 7, lag_rows, chans), jnp.int16)],
         compiler_params=params,
         name="sum_windows",
     )(tm_where, *exchange(pairs, "chan", chip_order))
@@ -322,11 +356,11 @@
     return pl.pallas_call(
         place_kernel,
         out_shape=jax.ShapeDtypeStruct((CH_DEV, offset_count, LAGS), jnp.float32),
-        in_specs=[vmem],
+        in_specs=[smem, vmem],
         out_specs=vmem,
         compiler_params=params,
         name="place_lags",
-    )(arrived.reshape(chan_count, tm_count, piece_rows, chans))
+    )(offsets, arrived.reshape(chan_count, tm_count, piece_rows, chans))
 
 
 def shifted(value, axis, steps):

time: 53 us -> 53 us (level)
  Pallas kernels: 8.22 us -> 8.79 us
    pallas_call x1, Pallas kernels: 0.91 us -> 1.45 us  [window_shards(): pl.pallas_call(place_kernel, out_shape=jax.ShapeDtypeStruct((CH_DEV, offs...]
  transfers between devices with their start and end apart: 14 -> 14, of which waited for: 9 -> 10; matrix products, arithmetic and copies ran while one was open for 0% -> 0% of each run, Pallas kernels for 2% -> 2%
where the time goes in v11:
time: 53 us; the launch traced here: 52.8 us
  waiting for transfers between devices  16.7 us (32%)
  starting transfers between devices  15.8 us (30%)
  blocking collectives  11.4 us (22%)
  Pallas kernels  8.79 us (17%)
    ppermute x14, waiting for transfers between devices, exchange(): lax.ppermute(piece, axis, [(source, source ^ k) for source in range(count)])  16.7 us
    ppermute x14, starting transfers between devices, exchange(): lax.ppermute(piece, axis, [(source, source ^ k) for source in range(count)])  15.8 us
    all_to_all x1, blocking collectives, window_shards(): lax.all_to_all(pieces.reshape(shape), ('chan', 'tm'), 0, 0, tiled=True)  11.4 us
    pallas_call x1, Pallas kernels, window_shards(): pl.pallas_call(functools.partial(window_kernel, chan_order), out_shape=[j...  3.9 us
    pallas_call x2, Pallas kernels, window_shards(): pl.pallas_call(functools.partial(split_kernel, part), out_shape=[jax.Shap...  2.32 us
    pallas_call x1, Pallas kernels, window_shards(): pl.pallas_call(place_kernel, out_shape=jax.ShapeDtypeStruct((CH_DEV, offs...  1.45 us
  transfers between devices with their start and end apart: 14, of which 10 were waited for; matrix products, arithmetic and copies ran while one was open for 0% of the time, Pallas kernels for 2%

profile of v11, /device:TPU:0, one launch (start us, length us, event | category | flops | bytes accessed | tf_op | source)
XLA Modules:
  0.0 52.8 jit_solution(6606313222279872348)
XLA Ops:
  0.0 1.1 %split_windows.2 = (bf16[2,256,128]{2,1,0:T(8,128)(2,1)S(1)}, bf16[2,256,128]{2,1,0:T(8,128)(2,1)S(1)}) custom-call(s32[1]{0:T(128)} %bitcast.1.where_ref, bf16[2,8,256,128]{3,2,1,0:T(8,128)(2,1)} %spec_ref.3), custom_call_target="tpu_custom_call" | custom-call | tf_op jit(solution)/shard_map/split_windows/pallas_call | solution.py:305
  1.1 4.0 %collective-permute-start = (bf16[2,256,128]{2,1,0:T(8,128)(2,1)S(1)}, bf16[2,256,128]{2,1,0:T(8,128)(2,1)S(1)}, u32[]{:S(2)}, u32[]{:S(2)}) collective-permute-start(bf16[2,256,128]{2,1,0:T(8,128)(2,1)S(1)} %get-tuple-element.23), channel_id=1, source_target_pairs={{0,24},{4,28},{8,16},{12,20},{16,8},{20,12},{24,0},{28,4},{1,25},{... | collective-permute-start | bytes 393224 | tf_op jit(solution)/shard_map/ppermute | solution.py:204
  5.0 1.3 %split_windows.3 = (bf16[2,256,128]{2,1,0:T(8,128)(2,1)S(1)}, bf16[2,256,128]{2,1,0:T(8,128)(2,1)S(1)}, bf16[2,256,128]{2,1,0:T(8,128)(2,1)S(1)}, bf16[2,256,128...) custom-call(s32[1]{0:T(128)} %bitcast.1.where_ref, ...), custom_call_target="tpu_custom_call" | custom-call | tf_op jit(solution)/shard_map/split_windows/pallas_call | solution.py:305
  6.3 1.2 %collective-permute-start.2 = (bf16[2,256,128]{2,1,0:T(8,128)(2,1)S(1)}, bf16[2,256,128]{2,1,0:T(8,128)(2,1)S(1)}, u32[]{:S(2)}, u32[]{:S(2)}) collective-permute-start(bf16[2,256,128]{2,1,0:T(8,128)(2,1)S(1)} %get-tuple-element.25), channel_id=1, source_target_pairs={{0,8},{4,12},{8,0},{12,4},{16,24},{20,28},{24,16},{28,20},{1,9},{5... | collective-permute-start | bytes 393224 | tf_op jit(solution)/shard_map/ppermute | solution.py:204
  7.5 1.5 %collective-permute-start.3 = (bf16[2,256,128]{2,1,0:T(8,128)(2,1)S(1)}, bf16[2,256,128]{2,1,0:T(8,128)(2,1)S(1)}, u32[]{:S(2)}, u32[]{:S(2)}) collective-permute-start(bf16[2,256,128]{2,1,0:T(8,128)(2,1)S(1)} %get-tuple-element.26), channel_id=1, source_target_pairs={{0,16},{4,20},{8,24},{12,28},{16,0},{20,4},{24,8},{28,12},{1,17},{... | collective-permute-start | bytes 393224 | tf_op jit(solution)/shard_map/ppermute | solution.py:204
  9.0 0.6 %collective-permute-start.4 = (bf16[2,256,128]{2,1,0:T(8,128)(2,1)S(1)}, bf16[2,256,128]{2,1,0:T(8,128)(2,1)S(1)}, u32[]{:S(2)}, u32[]{:S(2)}) collective-permute-start(bf16[2,256,128]{2,1,0:T(8,128)(2,1)S(1)} %get-tuple-element.27), channel_id=1, source_target_pairs={{0,12},{4,8},{8,4},{12,0},{16,28},{20,24},{24,20},{28,16},{1,13},{... | collective-permute-start | bytes 393224 | tf_op jit(solution)/shard_map/ppermute | solution.py:204
  9.6 0.6 %collective-permute-start.5 = (bf16[2,256,128]{2,1,0:T(8,128)(2,1)S(1)}, bf16[2,256,128]{2,1,0:T(8,128)(2,1)S(1)}, u32[]{:S(2)}, u32[]{:S(2)}) collective-permute-start(bf16[2,256,128]{2,1,0:T(8,128)(2,1)S(1)} %get-tuple-element.28), channel_id=1, source_target_pairs={{0,20},{4,16},{8,28},{12,24},{16,4},{20,0},{24,12},{28,8},{1,21},{... | collective-permute-start | bytes 393224 | tf_op jit(solution)/shard_map/ppermute | solution.py:204
  10.2 1.6 %collective-permute-done.1.refs_1_ = bf16[2,256,128]{2,1,0:T(8,128)(2,1)S(1)} collective-permute-done((bf16[2,256,128]{2,1,0:T(8,128)(2,1)S(1)}, bf16[2,256,128]{2,1,0:T(8,128)(2,1)S(1)}, u32[]{:S(2)}, u32[]{:S(2)}) %collective-permute-start.1) | collective-permute-done | bytes 131104 | tf_op jit(solution)/shard_map/ppermute | solution.py:204
  11.8 3.5 %collective-permute-done.2.refs_2_ = bf16[2,256,128]{2,1,0:T(8,128)(2,1)S(1)} collective-permute-done((bf16[2,256,128]{2,1,0:T(8,128)(2,1)S(1)}, bf16[2,256,128]{2,1,0:T(8,128)(2,1)S(1)}, u32[]{:S(2)}, u32[]{:S(2)}) %collective-permute-start.2) | collective-permute-done | bytes 131104 | tf_op jit(solution)/shard_map/ppermute | solution.py:204
  15.2 1.1 %collective-permute-done.4.refs_4_ = bf16[2,256,128]{2,1,0:T(8,128)(2,1)S(1)} collective-permute-done((bf16[2,256,128]{2,1,0:T(8,128)(2,1)S(1)}, bf16[2,256,128]{2,1,0:T(8,128)(2,1)S(1)}, u32[]{:S(2)}, u32[]{:S(2)}) %collective-permute-start.4) | collective-permute-done | bytes 131104 | tf_op jit(solution)/shard_map/ppermute | solution.py:204
  16.4 0.7 %collective-permute-done.5.refs_5_ = bf16[2,256,128]{2,1,0:T(8,128)(2,1)S(1)} collective-permute-done((bf16[2,256,128]{2,1,0:T(8,128)(2,1)S(1)}, bf16[2,256,128]{2,1,0:T(8,128)(2,1)S(1)}, u32[]{:S(2)}, u32[]{:S(2)}) %collective-permute-start.5) | collective-permute-done | bytes 131104 | tf_op jit(solution)/shard_map/ppermute | solution.py:204
  17.1 3.9 %window_pairs.1 = (s16[4,22,16,128]{3,2,1,0:T(8,128)(2,1)S(1)}, s16[4,22,16,128]{3,2,1,0:T(8,128)(2,1)S(1)}) custom-call(s32[4]{0:T(128)S(1)} %copy-done.1, s32[1]{0:T(128)} %bitcast.1.where_ref, bf16[2,256,128]{2,1,0:T(8,128)(2,1)S(1)} %collective-permute-done.refs_0_, bf16[2,256,128]{2,1,0:T(8,128)(2,1)S(1)} %collective-permute-done.1.refs_1_, ...), custom_call_target="tpu_custom_call" | custom-call | tf_op jit(solution)/shard_map/window_pairs/pallas_call | solution.py:316
  21.2 1.6 %collective-permute-done.7.far_ref = s16[4,22,16,128]{3,2,1,0:T(8,128)(2,1)S(1)} collective-permute-done((s16[4,22,16,128]{3,2,1,0:T(8,128)(2,1)S(1)}, s16[4,22,16,128]{3,2,1,0:T(8,128)(2,1)S(1)}, u32[]{:S(2)}, u32[]{:S(2)}) %collective-permute-start.7) | collective-permute-done | bytes 360480 | tf_op jit(solution)/shard_map/ppermute | solution.py:204
  22.9 2.6 %collective-permute-start.8 = (s16[22,16,128]{2,1,0:T(8,128)(2,1)S(1)}, s16[22,16,128]{2,1,0:T(8,128)(2,1)S(1)}, u32[]{:S(2)}, u32[]{:S(2)}) collective-permute-start(s16[22,16,128]{2,1,0:T(8,128)(2,1)S(1)} %get-tuple-element.33), channel_id=1, source_target_pairs={{0,24},{4,28},{8,16},{12,20},{16,8},{20,12},{24,0},{28,4},{1,25},{... | collective-permute-start | bytes 270344 | tf_op jit(solution)/shard_map/ppermute | solution.py:204
  26.0 0.5 collective-permute-start.10
  26.5 2.8 %collective-permute-done.8.refs_0_ = s16[22,16,128]{2,1,0:T(8,128)(2,1)S(1)} collective-permute-done((s16[22,16,128]{2,1,0:T(8,128)(2,1)S(1)}, s16[22,16,128]{2,1,0:T(8,128)(2,1)S(1)}, u32[]{:S(2)}, u32[]{:S(2)}) %collective-permute-start.8) | collective-permute-done | bytes 90144 | tf_op jit(solution)/shard_map/ppermute | solution.py:204
  29.3 1.3 %collective-permute-done.9.refs_1_ = s16[22,16,128]{2,1,0:T(8,128)(2,1)S(1)} collective-permute-done((s16[22,16,128]{2,1,0:T(8,128)(2,1)S(1)}, s16[22,16,128]{2,1,0:T(8,128)(2,1)S(1)}, u32[]{:S(2)}, u32[]{:S(2)}) %collective-permute-start.9) | collective-permute-done | bytes 90144 | tf_op jit(solution)/shard_map/ppermute | solution.py:204
  30.8 2.7 %collective-permute-start.11 = (s16[7,16,128]{2,1,0:T(8,128)(2,1)S(1)}, s16[7,16,128]{2,1,0:T(8,128)(2,1)S(1)}, u32[]{:S(2)}, u32[]{:S(2)}) collective-permute-start(s16[7,16,128]{2,1,0:T(8,128)(2,1)S(1)} %get-tuple-element.37), channel_id=1, source_target_pairs={{0,2},{1,3},{2,0},{3,1},{4,6},{5,7},{6,4},{7,5},{8,10},{9,11},{10,... | collective-permute-start | bytes 86024 | tf_op jit(solution)/shard_map/ppermute | solution.py:204
  33.5 1.3 %collective-permute-start.12 = (s16[7,16,128]{2,1,0:T(8,128)(2,1)S(1)}, s16[7,16,128]{2,1,0:T(8,128)(2,1)S(1)}, u32[]{:S(2)}, u32[]{:S(2)}) collective-permute-start(s16[7,16,128]{2,1,0:T(8,128)(2,1)S(1)} %get-tuple-element.38), channel_id=1, source_target_pairs={{0,3},{1,2},{2,1},{3,0},{4,7},{5,6},{6,5},{7,4},{8,11},{9,10},{10,... | collective-permute-start | bytes 86024 | tf_op jit(solution)/shard_map/ppermute | solution.py:204
  35.1 0.5 %collective-permute-done.11.refs_0_ = s16[7,16,128]{2,1,0:T(8,128)(2,1)S(1)} collective-permute-done((s16[7,16,128]{2,1,0:T(8,128)(2,1)S(1)}, s16[7,16,128]{2,1,0:T(8,128)(2,1)S(1)}, u32[]{:S(2)}, u32[]{:S(2)}) %collective-permute-start.11) | collective-permute-done | bytes 28704 | tf_op jit(solution)/shard_map/ppermute | solution.py:204
  35.7 3.5 %collective-permute-done.12.refs_1_ = s16[7,16,128]{2,1,0:T(8,128)(2,1)S(1)} collective-permute-done((s16[7,16,128]{2,1,0:T(8,128)(2,1)S(1)}, s16[7,16,128]{2,1,0:T(8,128)(2,1)S(1)}, u32[]{:S(2)}, u32[]{:S(2)}) %collective-permute-start.12) | collective-permute-done | bytes 28704 | tf_op jit(solution)/shard_map/ppermute | solution.py:204
  39.2 0.7 %stack_pairs.1 = f32[8,4,4,128]{3,2,1,0:T(4,128)S(1)} custom-call(s32[4]{0:T(128)S(1)} %copy-done.1, s32[1]{0:T(128)} %bitcast.where_ref, s16[7,16,128]{2,1,0:T(8,128)(2,1)S(1)} %collective-permute-done.11.refs_0_, s16[7,16,128]{2,1,0:T(8,128)(2,1)S(1)} %collective-permute-done.12.refs_1_, s16[7,16,128]{2,1,0:T(8,128)(2,1)S(1)} %collective-permute-done.13.refs_2_, ...), custom_call_target="tpu_custom_call" | custom-call | tf_op jit(solution)/shard_map/stack_pairs/pallas_call | solution.py:346
  40.0 11.4 %all_to_all.5 = f32[32,4,128]{2,1,0:T(4,128)S(1)} all-to-all(f32[32,4,128]{2,1,0:T(4,128)S(1)} %bitcast.5), channel_id=1, replica_groups=mesh['chan'=8,'tm'=4] {'chan','tm'}, dimensions={0} | all-to-all | bytes 131072 | tf_op jit(solution)/shard_map/all_to_all | solution.py:355
  51.4 1.4 %place_lags.1 = f32[16,4,256]{2,1,0:T(4,128)} custom-call(s32[4]{0:T(128)S(1)} %copy-done.1, f32[8,4,4,128]{3,2,1,0:T(4,128)S(1)} %bitcast.4), custom_call_target="tpu_custom_call" | custom-call | tf_op jit(solution)/shard_map/place_lags/pallas_call | solution.py:356
  (18 shorter events, 1.4 us)
Async XLA Ops:
  0.0 17.1 %copy-start = (bf16[2,8,16,2048]{3,2,1,0:T(8,128)(2,1)S(1)}, bf16[2,8,16,2048]{3,2,1,0:T(8,128)(2,1)}, u32[]{:S(2)}) copy-start(bf16[2,8,16,2048]{3,2,1,0:T(8,128)(2,1)} %constant.11.clone.refs_9_) | copy-start | bytes 3145732
  1.1 8.5 %collective-permute-start = (bf16[2,256,128]{2,1,0:T(8,128)(2,1)S(1)}, bf16[2,256,128]{2,1,0:T(8,128)(2,1)S(1)}, u32[]{:S(2)}, u32[]{:S(2)}) collective-permute-start(bf16[2,256,128]{2,1,0:T(8,128)(2,1)S(1)} %get-tuple-element.23), channel_id=1, source_target_pairs={{0,24},{4,28},{8,16},{12,20},{16,8},{20,12},{24,0},{28,4},{1,25},{... | collective-permute-start | bytes 393224 | tf_op jit(solution)/shard_map/ppermute | solution.py:204
  5.0 6.7 %collective-permute-start.1 = (bf16[2,256,128]{2,1,0:T(8,128)(2,1)S(1)}, bf16[2,256,128]{2,1,0:T(8,128)(2,1)S(1)}, u32[]{:S(2)}, u32[]{:S(2)}) collective-permute-start(bf16[2,256,128]{2,1,0:T(8,128)(2,1)S(1)} %get-tuple-element.24), channel_id=1, source_target_pairs={{0,28},{4,24},{8,20},{12,16},{16,12},{20,8},{24,4},{28,0},{1,29},{... | collective-permute-start | bytes 393224 | tf_op jit(solution)/shard_map/ppermute | solution.py:204
  6.3 8.9 %collective-permute-start.2 = (bf16[2,256,128]{2,1,0:T(8,128)(2,1)S(1)}, bf16[2,256,128]{2,1,0:T(8,128)(2,1)S(1)}, u32[]{:S(2)}, u32[]{:S(2)}) collective-permute-start(bf16[2,256,128]{2,1,0:T(8,128)(2,1)S(1)} %get-tuple-element.25), channel_id=1, source_target_pairs={{0,8},{4,12},{8,0},{12,4},{16,24},{20,28},{24,16},{28,20},{1,9},{5... | collective-permute-start | bytes 393224 | tf_op jit(solution)/shard_map/ppermute | solution.py:204
  7.5 9.6 %copy-start.2 = (s32[8,128]{1,0:T(8,128)S(1)}, s32[8,128]{1,0:T(8,128)}, u32[]{:S(2)}) copy-start(s32[8,128]{1,0:T(8,128)} %refs_8_.1) | copy-start | bytes 12292
  7.5 7.7 %collective-permute-start.3 = (bf16[2,256,128]{2,1,0:T(8,128)(2,1)S(1)}, bf16[2,256,128]{2,1,0:T(8,128)(2,1)S(1)}, u32[]{:S(2)}, u32[]{:S(2)}) collective-permute-start(bf16[2,256,128]{2,1,0:T(8,128)(2,1)S(1)} %get-tuple-element.26), channel_id=1, source_target_pairs={{0,16},{4,20},{8,24},{12,28},{16,0},{20,4},{24,8},{28,12},{1,17},{... | collective-permute-start | bytes 393224 | tf_op jit(solution)/shard_map/ppermute | solution.py:204
  9.0 7.4 %collective-permute-start.4 = (bf16[2,256,128]{2,1,0:T(8,128)(2,1)S(1)}, bf16[2,256,128]{2,1,0:T(8,128)(2,1)S(1)}, u32[]{:S(2)}, u32[]{:S(2)}) collective-permute-start(bf16[2,256,128]{2,1,0:T(8,128)(2,1)S(1)} %get-tuple-element.27), channel_id=1, source_target_pairs={{0,12},{4,8},{8,4},{12,0},{16,28},{20,24},{24,20},{28,16},{1,13},{... | collective-permute-start | bytes 393224 | tf_op jit(solution)/shard_map/ppermute | solution.py:204
  9.6 7.5 %collective-permute-start.5 = (bf16[2,256,128]{2,1,0:T(8,128)(2,1)S(1)}, bf16[2,256,128]{2,1,0:T(8,128)(2,1)S(1)}, u32[]{:S(2)}, u32[]{:S(2)}) collective-permute-start(bf16[2,256,128]{2,1,0:T(8,128)(2,1)S(1)} %get-tuple-element.28), channel_id=1, source_target_pairs={{0,20},{4,16},{8,28},{12,24},{16,4},{20,0},{24,12},{28,8},{1,21},{... | collective-permute-start | bytes 393224 | tf_op jit(solution)/shard_map/ppermute | solution.py:204
  11.8 5.3 %copy-start.1 = (s32[4]{0:T(128)S(1)}, s32[4]{0:T(128)}, u32[]{:S(2)}) copy-start(s32[4]{0:T(128)} %offs_ref.5) | copy-start | bytes 52
  11.8 5.3 %collective-permute-start.6 = (bf16[2,256,128]{2,1,0:T(8,128)(2,1)S(1)}, bf16[2,256,128]{2,1,0:T(8,128)(2,1)S(1)}, u32[]{:S(2)}, u32[]{:S(2)}) collective-permute-start(bf16[2,256,128]{2,1,0:T(8,128)(2,1)S(1)} %get-tuple-element.29), channel_id=1, source_target_pairs={{0,4},{4,0},{8,12},{12,8},{16,20},{20,16},{24,28},{28,24},{1,5},{5... | collective-permute-start | bytes 393224 | tf_op jit(solution)/shard_map/ppermute | solution.py:204
  21.0 1.7 %collective-permute-start.7 = (s16[4,22,16,128]{3,2,1,0:T(8,128)(2,1)S(1)}, s16[4,22,16,128]{3,2,1,0:T(8,128)(2,1)S(1)}, u32[]{:S(2)}, u32[]{:S(2)}) collective-permute-start(s16[4,22,16,128]{3,2,1,0:T(8,128)(2,1)S(1)} %get-tuple-element.32), channel_id=1, source_target_pairs={{0,4},{4,0},{8,12},{12,8},{16,20},{20,16},{24,28},{28,24},{1,5},{5... | collective-permute-start | bytes 1081352 | tf_op jit(solution)/shard_map/ppermute | solution.py:204
  22.9 6.3 %collective-permute-start.8 = (s16[22,16,128]{2,1,0:T(8,128)(2,1)S(1)}, s16[22,16,128]{2,1,0:T(8,128)(2,1)S(1)}, u32[]{:S(2)}, u32[]{:S(2)}) collective-permute-start(s16[22,16,128]{2,1,0:T(8,128)(2,1)S(1)} %get-tuple-element.33), channel_id=1, source_target_pairs={{0,24},{4,28},{8,16},{12,20},{16,8},{20,12},{24,0},{28,4},{1,25},{... | collective-permute-start | bytes 270344 | tf_op jit(solution)/shard_map/ppermute | solution.py:204
  25.5 5.0 %collective-permute-start.9 = (s16[22,16,128]{2,1,0:T(8,128)(2,1)S(1)}, s16[22,16,128]{2,1,0:T(8,128)(2,1)S(1)}, u32[]{:S(2)}, u32[]{:S(2)}) collective-permute-start(s16[22,16,128]{2,1,0:T(8,128)(2,1)S(1)} %get-tuple-element.34), channel_id=1, source_target_pairs={{0,8},{4,12},{8,0},{12,4},{16,24},{20,28},{24,16},{28,20},{1,9},{5... | collective-permute-start | bytes 270344 | tf_op jit(solution)/shard_map/ppermute | solution.py:204
  26.0 4.7 %collective-permute-start.10 = (s16[22,16,128]{2,1,0:T(8,128)(2,1)S(1)}, s16[22,16,128]{2,1,0:T(8,128)(2,1)S(1)}, u32[]{:S(2)}, u32[]{:S(2)}) collective-permute-start(s16[22,16,128]{2,1,0:T(8,128)(2,1)S(1)} %get-tuple-element.35), channel_id=1, source_target_pairs={{0,16},{4,20},{8,24},{12,28},{16,0},{20,4},{24,8},{28,12},{1,17},{... | collective-permute-start | bytes 270344 | tf_op jit(solution)/shard_map/ppermute | solution.py:204
  30.8 4.8 %collective-permute-start.11 = (s16[7,16,128]{2,1,0:T(8,128)(2,1)S(1)}, s16[7,16,128]{2,1,0:T(8,128)(2,1)S(1)}, u32[]{:S(2)}, u32[]{:S(2)}) collective-permute-start(s16[7,16,128]{2,1,0:T(8,128)(2,1)S(1)} %get-tuple-element.37), channel_id=1, source_target_pairs={{0,2},{1,3},{2,0},{3,1},{4,6},{5,7},{6,4},{7,5},{8,10},{9,11},{10,... | collective-permute-start | bytes 86024 | tf_op jit(solution)/shard_map/ppermute | solution.py:204
  33.5 5.7 %collective-permute-start.12 = (s16[7,16,128]{2,1,0:T(8,128)(2,1)S(1)}, s16[7,16,128]{2,1,0:T(8,128)(2,1)S(1)}, u32[]{:S(2)}, u32[]{:S(2)}) collective-permute-start(s16[7,16,128]{2,1,0:T(8,128)(2,1)S(1)} %get-tuple-element.38), channel_id=1, source_target_pairs={{0,3},{1,2},{2,1},{3,0},{4,7},{5,6},{6,5},{7,4},{8,11},{9,10},{10,... | collective-permute-start | bytes 86024 | tf_op jit(solution)/shard_map/ppermute | solution.py:204
  34.9 4.3 %collective-permute-start.13 = (s16[7,16,128]{2,1,0:T(8,128)(2,1)S(1)}, s16[7,16,128]{2,1,0:T(8,128)(2,1)S(1)}, u32[]{:S(2)}, u32[]{:S(2)}) collective-permute-start(s16[7,16,128]{2,1,0:T(8,128)(2,1)S(1)} %get-tuple-element.39), channel_id=1, source_target_pairs={{0,1},{1,0},{2,3},{3,2},{4,5},{5,4},{6,7},{7,6},{8,9},{9,8},{10,11... | collective-permute-start | bytes 86024 | tf_op jit(solution)/shard_map/ppermute | solution.py:204

commit v12 on v11

--- a/solution.py
+++ b/solution.py
@@ -57,11 +57,13 @@
     return offs_ref[jnp.where(slot == wide, last, jnp.where(slot == last, wide, slot))]
 
 
-def window_kernel(order, offs_ref, where_ref, *refs):
+def window_kernel(order, offs_hbm_ref, where_ref, *refs):
     chan_count = len(order)
     spec_refs, (qual_ref, table_ref) = refs[:chan_count], refs[chan_count : chan_count + 2]
     out_refs = refs[chan_count + 2 : chan_count + 4]
-    mag_ref, white_ref, cross_ref = refs[chan_count + 4 :]
+    mag_ref, white_ref, cross_ref, offs_ref, offs_sem = refs[chan_count + 4 :]
+    fetch = pltpu.make_async_copy(offs_hbm_ref, offs_ref, offs_sem)
+    fetch.start()
     me = where_ref[0]
     _, band, chans = spec_refs[0].shape
     freqs = chan_count * band
@@ -97,6 +99,7 @@
     usable = qual_ref[pl.ds(me, 1), :].astype(jnp.float32)
     levels = jnp.zeros((lag_rows, chans), jnp.float32)
     groups = [k ^ core for core in range(2) for k in chips(chan_count)]
+    fetch.wait()
     table = jnp.concatenate([table_ref[side, me ^ k] for side in range(2) for k in groups], axis=0)
     for number in range(offset_count):
         turn = chans - offset_of(number, offs_ref, chan_count // 2) * (chans // chan_count)
@@ -138,18 +141,24 @@
             for core in range(2):
                 rows = slice(core * chip_count, (core + 1) * chip_count)
                 out_refs[core][:, 6 * number + place, :, :] = coded[rows]
+    for number in range(offset_count):
+        levels = jnp.where(line == offset_count + number, offs_ref[number].astype(jnp.float32), levels)
+    wide = widest(offs_ref, chan_count // 2).astype(jnp.float32)
+    levels = jnp.where(line == 2 * offset_count, wide, levels)
     for out_ref in out_refs:
         for chip in range(chip_count):
             out_ref[chip, blocks - 1, :, :] = encode(levels)
 
 
-def merge_kernel(own_ref, far_ref, *out_refs):
+def merge_kernel(slots, own_ref, far_ref, *out_refs):
     blocks = own_ref.shape[1]
     for chip, out_ref in enumerate(out_refs):
-        levels = [level_of(decode(ref[chip, blocks - 1])) for ref in (own_ref, far_ref)]
+        codes = [decode(ref[chip, blocks - 1]) for ref in (own_ref, far_ref)]
+        levels = [level_of(code) for code in codes]
         code = level_code(levels[0] + levels[1])
         shares = [level / level_of(code) for level in levels]
-        out_ref[blocks - 1, :, :] = encode(code)
+        line = lax.broadcasted_iota(jnp.int32, code.shape, 0)
+        out_ref[blocks - 1, :, :] = encode(jnp.where(line < slots, code, codes[0]))
         for block in range(blocks - 1):
             number, part = divmod(block, 6)
             linear = part < (2 if blocks - 1 - 6 * number > 3 else 1)
@@ -165,8 +174,12 @@
     code_refs, out_refs, held_ref = refs[: -len(order) - 1], refs[-len(order) - 1 : -1], refs[-1]
     blocks, _, chans = code_refs[0].shape
     slots = held_ref.shape[0]
-    levels = [level_of(decode(codes_ref[blocks - 1])) * scale for codes_ref in code_refs]
+    heads = [decode(codes_ref[blocks - 1]) for codes_ref in code_refs]
+    levels = [level_of(head) * scale for head in heads]
+    offsets = [heads[0][slots + number : slots + number + 1, :] for number in range(slots)]
+    wide = heads[0][2 * slots : 2 * slots + 1, :]
     low = lax.broadcasted_iota(jnp.int32, (1, chans), 1) < chans // 2
+    all_sums = []
     for number in range(slots):
         sides = 2 if number < slots - 1 else 1
         own = [level[number : number + 1, :] for level in levels]
@@ -181,10 +194,19 @@
             sums = [
                 jnp.where(low, side, 0.0) for value in sums for side in (value, pltpu.roll(value, chans // 2, 1))
             ]
+        all_sums.append(sums)
+    line = lax.broadcasted_iota(jnp.int32, levels[0].shape, 0)
+    last = slots - 1
+    for number in range(slots):
+        sums = all_sums[number]
+        for other in range(last) if number == last else [last]:
+            swap = wide == min(number, other)
+            sums = [jnp.where(swap, value, kept) for value, kept in zip(all_sums[other], sums)]
         peak = jnp.max(jnp.maximum(jnp.abs(sums[0]), jnp.abs(sums[1])), axis=0, keepdims=True)
-        code = level_code(jnp.broadcast_to(peak, sums[0].shape))
+        code = level_code(peak)
         upscale = CODE_TOP / level_of(code)
-        for part, value in enumerate([sums[0] * upscale, sums[1] * upscale, *sums[2:], code]):
+        head = jnp.where(line == 0, code, offsets[number])
+        for part, value in enumerate([sums[0] * upscale, sums[1] * upscale, *sums[2:], head]):
             held_ref[number, part, :, :] = encode(value)
     for k, out_ref in zip(order, out_refs):
         out_ref[...] = held_ref[where_ref[0] ^ k]
@@ -218,12 +240,13 @@
         copy.wait()
 
 
-def stack_kernel(windows, offs_ref, where_ref, *refs):
+def stack_kernel(windows, *refs):
     sums_refs, out_ref = refs[:-1], refs[-1]
     blocks, copies, rows, _ = out_ref.shape
     _, lag_rows, chans = sums_refs[0].shape
     per_sum = windows // len(sums_refs)
-    levels = [level_of(decode(sums_ref[6])) * (1.0 / (CODE_TOP * windows)) for sums_ref in sums_refs]
+    heads = [decode(sums_ref[6]) for sums_ref in sums_refs]
+    levels = [level_of(head[0:1, :]) * (1.0 / (CODE_TOP * windows)) for head in heads]
     stacks = []
     for side in range(2):
         linear = sum(decode(sums_ref[side]) * level for sums_ref, level in zip(sums_refs, levels))
@@ -232,9 +255,13 @@
             for part in (2, 4)
         )
         stacks.append(linear * (real * real + imag * imag))
-    ahead = offset_of(where_ref[0], offs_ref, blocks // 2) * (chans // blocks)
+    offset = heads[0][1:2, :]
     lane = lax.broadcasted_iota(jnp.int32, (1, chans), 1)
-    behind = [jnp.where(lane >= ahead, pltpu.roll(stack, ahead, 1), 0.0) for stack in stacks]
+    behind = [jnp.zeros_like(stack) for stack in stacks]
+    for steps in range(1, blocks // 2 + 1):
+        ahead = steps * (chans // blocks)
+        chosen = (offset == steps) & (lane >= ahead)
+        behind = [jnp.where(chosen, pltpu.roll(stack, ahead, 1), kept) for stack, kept in zip(stacks, behind)]
     back = stacks[1] + behind[0]
     both = jnp.concatenate(
         [stacks[0] + behind[1]] + [back[row : row + 1, :] for row in reversed(range(lag_rows))], axis=0
@@ -252,33 +279,26 @@
             out_ref[block, copy, :, :] = piece
 
 
-def place_kernel(offs_ref, parts_ref, out_ref):
+def place_kernel(parts_ref, out_ref):
     groups, offset_count, rows, lanes = parts_ref.shape
     half = out_ref.shape[2] // 2
     lag_rows = half // groups
     parts = out_ref.shape[0] // rows
     lane = lax.broadcasted_iota(jnp.int32, (1, lanes), 1)
-    last, wide = offset_count - 1, widest(offs_ref, groups // 2)
-    for part in range(parts):
-        begin = part * 2 * lag_rows
-        slots = []
-        for number in range(offset_count):
+    for number in range(offset_count):
+        for part in range(parts):
             ahead = jnp.zeros((rows, lanes), jnp.float32)
             back = jnp.zeros((rows, lanes), jnp.float32)
+            begin = part * 2 * lag_rows
             for group in range(groups):
                 piece = parts_ref[group, number]
-                first, end = group * lag_rows, half - (group + 1) * lag_rows
+                first, last = group * lag_rows, half - (group + 1) * lag_rows
                 ahead = jnp.where(lane // lag_rows == group, pltpu.roll(piece, (first - begin) % lanes, 1), ahead)
                 back = jnp.where(
-                    lane // lag_rows == groups - 1 - group, pltpu.roll(piece, (end - begin - lag_rows) % lanes, 1), back
+                    lane // lag_rows == groups - 1 - group, pltpu.roll(piece, (last - begin - lag_rows) % lanes, 1), back
                 )
-            slots.append((back, ahead))
-        for number in range(offset_count):
-            for side in range(2):
-                value = slots[number][side]
-                for other in range(last) if number == last else [last]:
-                    value = jnp.where(wide == min(number, other), slots[other][side], value)
-                out_ref[part * rows : (part + 1) * rows, number, side * half : (side + 1) * half] = value
+            out_ref[part * rows : (part + 1) * rows, number, 0:half] = back
+            out_ref[part * rows : (part + 1) * rows, number, half : 2 * half] = ahead
 
 
 def window_shards(spectra, quality, offsets):
@@ -299,13 +319,14 @@
     chan_where, tm_where = chan_index.reshape(1), tm_index.reshape(1)
 
     chan_order, tm_order = partners(chan_count), partners(tm_count)
+    kept = pl.BlockSpec(memory_space=pltpu.HBM)
     spectra = pltpu.with_memory_space_constraint(spectra, pltpu.HBM)
     pieces = []
     for part in (chan_order[:2], chan_order[2:]):
         pieces += pl.pallas_call(
             functools.partial(split_kernel, part),
             out_shape=[jax.ShapeDtypeStruct((2, band, chans), spectra.dtype)] * len(part),
-            in_specs=[smem, pl.BlockSpec(memory_space=pltpu.HBM)],
+            in_specs=[smem, kept],
             out_specs=[pl.BlockSpec(memory_space=pl.ANY)] * len(part),
             scratch_shapes=[pltpu.SemaphoreType.DMA((len(part),))],
             compiler_params=params,
@@ -316,18 +337,20 @@
     own, far = pl.pallas_call(
         functools.partial(window_kernel, chan_order),
         out_shape=[jax.ShapeDtypeStruct((len(chip_order), *pair_shape), jnp.int16)] * 2,
-        in_specs=[smem, smem] + [vmem] * (chan_count + 2),
+        in_specs=[kept, smem] + [vmem] * (chan_count + 2),
         out_specs=[vmem] * 2,
         scratch_shapes=[
             pltpu.VMEM((freqs, chans), jnp.float32),
             pltpu.VMEM((2, freqs, chans), jnp.bfloat16),
             pltpu.VMEM((2, freqs, 2 * chans), jnp.bfloat16),
+            pltpu.SMEM(offsets.shape, jnp.int32),
+            pltpu.SemaphoreType.DMA(()),
         ],
         compiler_params=params,
         name="window_pairs",
-    )(offsets, chan_where, *exchange(pieces, "chan", chan_order), quality, table)
+    )(pltpu.with_memory_space_constraint(offsets, pltpu.HBM), chan_where, *exchange(pieces, "chan", chan_order), quality, table)
     pairs = pl.pallas_call(
-        merge_kernel,
+        functools.partial(merge_kernel, offset_count),
         out_shape=[jax.ShapeDtypeStruct(pair_shape, jnp.int16)] * len(chip_order),
         in_specs=[vmem] * 2,
         out_specs=[vmem] * len(chip_order),
@@ -346,21 +369,21 @@
     pieces = pl.pallas_call(
         functools.partial(stack_kernel, windows * tm_count),
         out_shape=jax.ShapeDtypeStruct((chan_count, tm_count, piece_rows, chans), jnp.float32),
-        in_specs=[smem, smem] + [vmem] * tm_count,
+        in_specs=[vmem] * tm_count,
         out_specs=vmem,
         compiler_params=params,
         name="stack_pairs",
-    )(offsets, tm_where, *exchange(sums, "tm", tm_order))
+    )(*exchange(sums, "tm", tm_order))
     shape = (chan_count * tm_count, piece_rows, chans)
     arrived = lax.all_to_all(pieces.reshape(shape), ("chan", "tm"), 0, 0, tiled=True)
     return pl.pallas_call(
         place_kernel,
         out_shape=jax.ShapeDtypeStruct((CH_DEV, offset_count, LAGS), jnp.float32),
-        in_specs=[smem, vmem],
+        in_specs=[vmem],
         out_specs=vmem,
         compiler_params=params,
         name="place_lags",
-    )(offsets, arrived.reshape(chan_count, tm_count, piece_rows, chans))
+    )(arrived.reshape(chan_count, tm_count, piece_rows, chans))
 
 
 def shifted(value, axis, steps):

time: 53 us -> 51.4 us (0.970)
  Pallas kernels: 8.79 us -> 7.22 us
    pallas_call x1, Pallas kernels: 1.45 us -> 0.91 us  [window_shards(): pl.pallas_call(place_kernel, out_shape=jax.ShapeDtypeStruct((CH_DEV, offs...]
    pallas_call x1, Pallas kernels: 0.74 us -> 0.2 us  [window_shards(): pl.pallas_call(functools.partial(stack_kernel, windows * tm_count), out_s...]
where the time goes in v12:
time: 51.4 us; the launch traced here: 51.3 us
  waiting for transfers between devices  16.7 us (32%)
  starting transfers between devices  15.8 us (31%)
  blocking collectives  11.4 us (22%)
  Pallas kernels  7.22 us (14%)
    ppermute x14, waiting for transfers between devices, exchange(): lax.ppermute(piece, axis, [(source, source ^ k) for source in range(count)])  16.7 us
    ppermute x14, starting transfers between devices, exchange(): lax.ppermute(piece, axis, [(source, source ^ k) for source in range(count)])  15.8 us
    all_to_all x1, blocking collectives, window_shards(): lax.all_to_all(pieces.reshape(shape), ('chan', 'tm'), 0, 0, tiled=True)  11.4 us
    pallas_call x1, Pallas kernels, window_shards(): pl.pallas_call(functools.partial(window_kernel, chan_order), out_shape=[j...  3.43 us
    pallas_call x2, Pallas kernels, window_shards(): pl.pallas_call(functools.partial(split_kernel, part), out_shape=[jax.Shap...  2.32 us
  transfers between devices with their start and end apart: 14, of which 10 were waited for; matrix products, arithmetic and copies ran while one was open for 0% of the time, Pallas kernels for 2%

profile of v12, /device:TPU:0, one launch (start us, length us, event | category | flops | bytes accessed | tf_op | source)
XLA Modules:
  0.0 51.3 jit_solution(17781341031684802367)
XLA Ops:
  0.0 1.1 %split_windows.2 = (bf16[2,256,128]{2,1,0:T(8,128)(2,1)S(1)}, bf16[2,256,128]{2,1,0:T(8,128)(2,1)S(1)}) custom-call(s32[1]{0:T(128)} %bitcast.1.where_ref, bf16[2,8,256,128]{3,2,1,0:T(8,128)(2,1)} %spec_ref.3), custom_call_target="tpu_custom_call" | custom-call | tf_op jit(solution)/shard_map/split_windows/pallas_call | solution.py:326
  1.1 4.0 %collective-permute-start = (bf16[2,256,128]{2,1,0:T(8,128)(2,1)S(1)}, bf16[2,256,128]{2,1,0:T(8,128)(2,1)S(1)}, u32[]{:S(2)}, u32[]{:S(2)}) collective-permute-start(bf16[2,256,128]{2,1,0:T(8,128)(2,1)S(1)} %get-tuple-element.23), channel_id=1, source_target_pairs={{0,24},{4,28},{8,16},{12,20},{16,8},{20,12},{24,0},{28,4},{1,25},{... | collective-permute-start | bytes 393224 | tf_op jit(solution)/shard_map/ppermute | solution.py:226
  5.0 1.3 %split_windows.3 = (bf16[2,256,128]{2,1,0:T(8,128)(2,1)S(1)}, bf16[2,256,128]{2,1,0:T(8,128)(2,1)S(1)}, bf16[2,256,128]{2,1,0:T(8,128)(2,1)S(1)}, bf16[2,256,128...) custom-call(s32[1]{0:T(128)} %bitcast.1.where_ref, ...), custom_call_target="tpu_custom_call" | custom-call | tf_op jit(solution)/shard_map/split_windows/pallas_call | solution.py:326
  6.3 1.2 %collective-permute-start.2 = (bf16[2,256,128]{2,1,0:T(8,128)(2,1)S(1)}, bf16[2,256,128]{2,1,0:T(8,128)(2,1)S(1)}, u32[]{:S(2)}, u32[]{:S(2)}) collective-permute-start(bf16[2,256,128]{2,1,0:T(8,128)(2,1)S(1)} %get-tuple-element.25), channel_id=1, source_target_pairs={{0,8},{4,12},{8,0},{12,4},{16,24},{20,28},{24,16},{28,20},{1,9},{5... | collective-permute-start | bytes 393224 | tf_op jit(solution)/shard_map/ppermute | solution.py:226
  7.5 1.5 %collective-permute-start.3 = (bf16[2,256,128]{2,1,0:T(8,128)(2,1)S(1)}, bf16[2,256,128]{2,1,0:T(8,128)(2,1)S(1)}, u32[]{:S(2)}, u32[]{:S(2)}) collective-permute-start(bf16[2,256,128]{2,1,0:T(8,128)(2,1)S(1)} %get-tuple-element.26), channel_id=1, source_target_pairs={{0,16},{4,20},{8,24},{12,28},{16,0},{20,4},{24,8},{28,12},{1,17},{... | collective-permute-start | bytes 393224 | tf_op jit(solution)/shard_map/ppermute | solution.py:226
  9.0 0.6 %collective-permute-start.4 = (bf16[2,256,128]{2,1,0:T(8,128)(2,1)S(1)}, bf16[2,256,128]{2,1,0:T(8,128)(2,1)S(1)}, u32[]{:S(2)}, u32[]{:S(2)}) collective-permute-start(bf16[2,256,128]{2,1,0:T(8,128)(2,1)S(1)} %get-tuple-element.27), channel_id=1, source_target_pairs={{0,12},{4,8},{8,4},{12,0},{16,28},{20,24},{24,20},{28,16},{1,13},{... | collective-permute-start | bytes 393224 | tf_op jit(solution)/shard_map/ppermute | solution.py:226
  9.6 0.6 %collective-permute-start.5 = (bf16[2,256,128]{2,1,0:T(8,128)(2,1)S(1)}, bf16[2,256,128]{2,1,0:T(8,128)(2,1)S(1)}, u32[]{:S(2)}, u32[]{:S(2)}) collective-permute-start(bf16[2,256,128]{2,1,0:T(8,128)(2,1)S(1)} %get-tuple-element.28), channel_id=1, source_target_pairs={{0,20},{4,16},{8,28},{12,24},{16,4},{20,0},{24,12},{28,8},{1,21},{... | collective-permute-start | bytes 393224 | tf_op jit(solution)/shard_map/ppermute | solution.py:226
  10.2 1.6 %collective-permute-done.1.refs_1_ = bf16[2,256,128]{2,1,0:T(8,128)(2,1)S(1)} collective-permute-done((bf16[2,256,128]{2,1,0:T(8,128)(2,1)S(1)}, bf16[2,256,128]{2,1,0:T(8,128)(2,1)S(1)}, u32[]{:S(2)}, u32[]{:S(2)}) %collective-permute-start.1) | collective-permute-done | bytes 131104 | tf_op jit(solution)/shard_map/ppermute | solution.py:226
  11.8 3.5 %collective-permute-done.2.refs_2_ = bf16[2,256,128]{2,1,0:T(8,128)(2,1)S(1)} collective-permute-done((bf16[2,256,128]{2,1,0:T(8,128)(2,1)S(1)}, bf16[2,256,128]{2,1,0:T(8,128)(2,1)S(1)}, u32[]{:S(2)}, u32[]{:S(2)}) %collective-permute-start.2) | collective-permute-done | bytes 131104 | tf_op jit(solution)/shard_map/ppermute | solution.py:226
  15.2 1.1 %collective-permute-done.4.refs_4_ = bf16[2,256,128]{2,1,0:T(8,128)(2,1)S(1)} collective-permute-done((bf16[2,256,128]{2,1,0:T(8,128)(2,1)S(1)}, bf16[2,256,128]{2,1,0:T(8,128)(2,1)S(1)}, u32[]{:S(2)}, u32[]{:S(2)}) %collective-permute-start.4) | collective-permute-done | bytes 131104 | tf_op jit(solution)/shard_map/ppermute | solution.py:226
  16.4 0.7 %collective-permute-done.5.refs_5_ = bf16[2,256,128]{2,1,0:T(8,128)(2,1)S(1)} collective-permute-done((bf16[2,256,128]{2,1,0:T(8,128)(2,1)S(1)}, bf16[2,256,128]{2,1,0:T(8,128)(2,1)S(1)}, u32[]{:S(2)}, u32[]{:S(2)}) %collective-permute-start.5) | collective-permute-done | bytes 131104 | tf_op jit(solution)/shard_map/ppermute | solution.py:226
  17.1 3.4 %window_pairs.1 = (s16[4,22,16,128]{3,2,1,0:T(8,128)(2,1)S(1)}, s16[4,22,16,128]{3,2,1,0:T(8,128)(2,1)S(1)}) custom-call(s32[4]{0:T(128)} %offs_hbm_ref.1, s32[1]{0:T(128)} %bitcast.1.where_ref, bf16[2,256,128]{2,1,0:T(8,128)(2,1)S(1)} %collective-permute-done.refs_0_, bf16[2,256,128]{2,1,0:T(8,128)(2,1)S(1)} %collective-permute-done.1.refs_1_, ...), custom_call_target="tpu_custom_call" | custom-call | tf_op jit(solution)/shard_map/window_pairs/pallas_call | solution.py:337
  20.7 1.5 %collective-permute-done.7.far_ref = s16[4,22,16,128]{3,2,1,0:T(8,128)(2,1)S(1)} collective-permute-done((s16[4,22,16,128]{3,2,1,0:T(8,128)(2,1)S(1)}, s16[4,22,16,128]{3,2,1,0:T(8,128)(2,1)S(1)}, u32[]{:S(2)}, u32[]{:S(2)}) %collective-permute-start.7) | collective-permute-done | bytes 360480 | tf_op jit(solution)/shard_map/ppermute | solution.py:226
  22.5 2.6 %collective-permute-start.8 = (s16[22,16,128]{2,1,0:T(8,128)(2,1)S(1)}, s16[22,16,128]{2,1,0:T(8,128)(2,1)S(1)}, u32[]{:S(2)}, u32[]{:S(2)}) collective-permute-start(s16[22,16,128]{2,1,0:T(8,128)(2,1)S(1)} %get-tuple-element.33), channel_id=1, source_target_pairs={{0,24},{4,28},{8,16},{12,20},{16,8},{20,12},{24,0},{28,4},{1,25},{... | collective-permute-start | bytes 270344 | tf_op jit(solution)/shard_map/ppermute | solution.py:226
  25.0 0.4 collective-permute-start.9
  25.5 0.5 %collective-permute-start.10 = (s16[22,16,128]{2,1,0:T(8,128)(2,1)S(1)}, s16[22,16,128]{2,1,0:T(8,128)(2,1)S(1)}, u32[]{:S(2)}, u32[]{:S(2)}) collective-permute-start(s16[22,16,128]{2,1,0:T(8,128)(2,1)S(1)} %get-tuple-element.35), channel_id=1, source_target_pairs={{0,16},{4,20},{8,24},{12,28},{16,0},{20,4},{24,8},{28,12},{1,17},{... | collective-permute-start | bytes 270344 | tf_op jit(solution)/shard_map/ppermute | solution.py:226
  26.0 2.8 %collective-permute-done.8.refs_0_ = s16[22,16,128]{2,1,0:T(8,128)(2,1)S(1)} collective-permute-done((s16[22,16,128]{2,1,0:T(8,128)(2,1)S(1)}, s16[22,16,128]{2,1,0:T(8,128)(2,1)S(1)}, u32[]{:S(2)}, u32[]{:S(2)}) %collective-permute-start.8) | collective-permute-done | bytes 90144 | tf_op jit(solution)/shard_map/ppermute | solution.py:226
  28.8 1.3 %collective-permute-done.9.refs_1_ = s16[22,16,128]{2,1,0:T(8,128)(2,1)S(1)} collective-permute-done((s16[22,16,128]{2,1,0:T(8,128)(2,1)S(1)}, s16[22,16,128]{2,1,0:T(8,128)(2,1)S(1)}, u32[]{:S(2)}, u32[]{:S(2)}) %collective-permute-start.9) | collective-permute-done | bytes 90144 | tf_op jit(solution)/shard_map/ppermute | solution.py:226
  30.3 2.7 %collective-permute-start.11 = (s16[7,16,128]{2,1,0:T(8,128)(2,1)S(1)}, s16[7,16,128]{2,1,0:T(8,128)(2,1)S(1)}, u32[]{:S(2)}, u32[]{:S(2)}) collective-permute-start(s16[7,16,128]{2,1,0:T(8,128)(2,1)S(1)} %get-tuple-element.37), channel_id=1, source_target_pairs={{0,2},{1,3},{2,0},{3,1},{4,6},{5,7},{6,4},{7,5},{8,10},{9,11},{10,... | collective-permute-start | bytes 86024 | tf_op jit(solution)/shard_map/ppermute | solution.py:226
  33.0 1.3 %collective-permute-start.12 = (s16[7,16,128]{2,1,0:T(8,128)(2,1)S(1)}, s16[7,16,128]{2,1,0:T(8,128)(2,1)S(1)}, u32[]{:S(2)}, u32[]{:S(2)}) collective-permute-start(s16[7,16,128]{2,1,0:T(8,128)(2,1)S(1)} %get-tuple-element.38), channel_id=1, source_target_pairs={{0,3},{1,2},{2,1},{3,0},{4,7},{5,6},{6,5},{7,4},{8,11},{9,10},{10,... | collective-permute-start | bytes 86024 | tf_op jit(solution)/shard_map/ppermute | solution.py:226
  34.6 0.5 %collective-permute-done.11.refs_0_ = s16[7,16,128]{2,1,0:T(8,128)(2,1)S(1)} collective-permute-done((s16[7,16,128]{2,1,0:T(8,128)(2,1)S(1)}, s16[7,16,128]{2,1,0:T(8,128)(2,1)S(1)}, u32[]{:S(2)}, u32[]{:S(2)}) %collective-permute-start.11) | collective-permute-done | bytes 28704 | tf_op jit(solution)/shard_map/ppermute | solution.py:226
  35.2 3.5 %collective-permute-done.12.refs_1_ = s16[7,16,128]{2,1,0:T(8,128)(2,1)S(1)} collective-permute-done((s16[7,16,128]{2,1,0:T(8,128)(2,1)S(1)}, s16[7,16,128]{2,1,0:T(8,128)(2,1)S(1)}, u32[]{:S(2)}, u32[]{:S(2)}) %collective-permute-start.12) | collective-permute-done | bytes 28704 | tf_op jit(solution)/shard_map/ppermute | solution.py:226
  38.9 11.4 %all_to_all.5 = f32[32,4,128]{2,1,0:T(4,128)S(1)} all-to-all(f32[32,4,128]{2,1,0:T(4,128)S(1)} %bitcast.5), channel_id=1, replica_groups=mesh['chan'=8,'tm'=4] {'chan','tm'}, dimensions={0} | all-to-all | bytes 131072 | tf_op jit(solution)/shard_map/all_to_all | solution.py:378
  50.4 0.9 %place_lags.1 = f32[16,4,256]{2,1,0:T(4,128)} custom-call(f32[8,4,4,128]{3,2,1,0:T(4,128)S(1)} %bitcast.4), custom_call_target="tpu_custom_call" | custom-call | tf_op jit(solution)/shard_map/place_lags/pallas_call | solution.py:379
  (16 shorter events, 1.1 us)
Async XLA Ops:
  0.0 17.1 %copy-start = (bf16[2,8,16,2048]{3,2,1,0:T(8,128)(2,1)S(1)}, bf16[2,8,16,2048]{3,2,1,0:T(8,128)(2,1)}, u32[]{:S(2)}) copy-start(bf16[2,8,16,2048]{3,2,1,0:T(8,128)(2,1)} %constant.11.clone.refs_9_) | copy-start | bytes 3145732
  1.1 8.5 %collective-permute-start = (bf16[2,256,128]{2,1,0:T(8,128)(2,1)S(1)}, bf16[2,256,128]{2,1,0:T(8,128)(2,1)S(1)}, u32[]{:S(2)}, u32[]{:S(2)}) collective-permute-start(bf16[2,256,128]{2,1,0:T(8,128)(2,1)S(1)} %get-tuple-element.23), channel_id=1, source_target_pairs={{0,24},{4,28},{8,16},{12,20},{16,8},{20,12},{24,0},{28,4},{1,25},{... | collective-permute-start | bytes 393224 | tf_op jit(solution)/shard_map/ppermute | solution.py:226
  5.0 6.7 %collective-permute-start.1 = (bf16[2,256,128]{2,1,0:T(8,128)(2,1)S(1)}, bf16[2,256,128]{2,1,0:T(8,128)(2,1)S(1)}, u32[]{:S(2)}, u32[]{:S(2)}) collective-permute-start(bf16[2,256,128]{2,1,0:T(8,128)(2,1)S(1)} %get-tuple-element.24), channel_id=1, source_target_pairs={{0,28},{4,24},{8,20},{12,16},{16,12},{20,8},{24,4},{28,0},{1,29},{... | collective-permute-start | bytes 393224 | tf_op jit(solution)/shard_map/ppermute | solution.py:226
  6.3 8.9 %collective-permute-start.2 = (bf16[2,256,128]{2,1,0:T(8,128)(2,1)S(1)}, bf16[2,256,128]{2,1,0:T(8,128)(2,1)S(1)}, u32[]{:S(2)}, u32[]{:S(2)}) collective-permute-start(bf16[2,256,128]{2,1,0:T(8,128)(2,1)S(1)} %get-tuple-element.25), channel_id=1, source_target_pairs={{0,8},{4,12},{8,0},{12,4},{16,24},{20,28},{24,16},{28,20},{1,9},{5... | collective-permute-start | bytes 393224 | tf_op jit(solution)/shard_map/ppermute | solution.py:226
  7.5 9.6 %copy-start.1 = (s32[8,128]{1,0:T(8,128)S(1)}, s32[8,128]{1,0:T(8,128)}, u32[]{:S(2)}) copy-start(s32[8,128]{1,0:T(8,128)} %refs_8_.1) | copy-start | bytes 12292
  7.5 7.7 %collective-permute-start.3 = (bf16[2,256,128]{2,1,0:T(8,128)(2,1)S(1)}, bf16[2,256,128]{2,1,0:T(8,128)(2,1)S(1)}, u32[]{:S(2)}, u32[]{:S(2)}) collective-permute-start(bf16[2,256,128]{2,1,0:T(8,128)(2,1)S(1)} %get-tuple-element.26), channel_id=1, source_target_pairs={{0,16},{4,20},{8,24},{12,28},{16,0},{20,4},{24,8},{28,12},{1,17},{... | collective-permute-start | bytes 393224 | tf_op jit(solution)/shard_map/ppermute | solution.py:226
  9.0 7.4 %collective-permute-start.4 = (bf16[2,256,128]{2,1,0:T(8,128)(2,1)S(1)}, bf16[2,256,128]{2,1,0:T(8,128)(2,1)S(1)}, u32[]{:S(2)}, u32[]{:S(2)}) collective-permute-start(bf16[2,256,128]{2,1,0:T(8,128)(2,1)S(1)} %get-tuple-element.27), channel_id=1, source_target_pairs={{0,12},{4,8},{8,4},{12,0},{16,28},{20,24},{24,20},{28,16},{1,13},{... | collective-permute-start | bytes 393224 | tf_op jit(solution)/shard_map/ppermute | solution.py:226
  9.6 7.5 %collective-permute-start.5 = (bf16[2,256,128]{2,1,0:T(8,128)(2,1)S(1)}, bf16[2,256,128]{2,1,0:T(8,128)(2,1)S(1)}, u32[]{:S(2)}, u32[]{:S(2)}) collective-permute-start(bf16[2,256,128]{2,1,0:T(8,128)(2,1)S(1)} %get-tuple-element.28), channel_id=1, source_target_pairs={{0,20},{4,16},{8,28},{12,24},{16,4},{20,0},{24,12},{28,8},{1,21},{... | collective-permute-start | bytes 393224 | tf_op jit(solution)/shard_map/ppermute | solution.py:226
  11.8 5.3 %collective-permute-start.6 = (bf16[2,256,128]{2,1,0:T(8,128)(2,1)S(1)}, bf16[2,256,128]{2,1,0:T(8,128)(2,1)S(1)}, u32[]{:S(2)}, u32[]{:S(2)}) collective-permute-start(bf16[2,256,128]{2,1,0:T(8,128)(2,1)S(1)} %get-tuple-element.29), channel_id=1, source_target_pairs={{0,4},{4,0},{8,12},{12,8},{16,20},{20,16},{24,28},{28,24},{1,5},{5... | collective-permute-start | bytes 393224 | tf_op jit(solution)/shard_map/ppermute | solution.py:226
  20.5 1.7 %collective-permute-start.7 = (s16[4,22,16,128]{3,2,1,0:T(8,128)(2,1)S(1)}, s16[4,22,16,128]{3,2,1,0:T(8,128)(2,1)S(1)}, u32[]{:S(2)}, u32[]{:S(2)}) collective-permute-start(s16[4,22,16,128]{3,2,1,0:T(8,128)(2,1)S(1)} %get-tuple-element.32), channel_id=1, source_target_pairs={{0,4},{4,0},{8,12},{12,8},{16,20},{20,16},{24,28},{28,24},{1,5},{5... | collective-permute-start | bytes 1081352 | tf_op jit(solution)/shard_map/ppermute | solution.py:226
  22.5 6.3 %collective-permute-start.8 = (s16[22,16,128]{2,1,0:T(8,128)(2,1)S(1)}, s16[22,16,128]{2,1,0:T(8,128)(2,1)S(1)}, u32[]{:S(2)}, u32[]{:S(2)}) collective-permute-start(s16[22,16,128]{2,1,0:T(8,128)(2,1)S(1)} %get-tuple-element.33), channel_id=1, source_target_pairs={{0,24},{4,28},{8,16},{12,20},{16,8},{20,12},{24,0},{28,4},{1,25},{... | collective-permute-start | bytes 270344 | tf_op jit(solution)/shard_map/ppermute | solution.py:226
  25.0 5.0 %collective-permute-start.9 = (s16[22,16,128]{2,1,0:T(8,128)(2,1)S(1)}, s16[22,16,128]{2,1,0:T(8,128)(2,1)S(1)}, u32[]{:S(2)}, u32[]{:S(2)}) collective-permute-start(s16[22,16,128]{2,1,0:T(8,128)(2,1)S(1)} %get-tuple-element.34), channel_id=1, source_target_pairs={{0,8},{4,12},{8,0},{12,4},{16,24},{20,28},{24,16},{28,20},{1,9},{5... | collective-permute-start | bytes 270344 | tf_op jit(solution)/shard_map/ppermute | solution.py:226
  25.5 4.7 %collective-permute-start.10 = (s16[22,16,128]{2,1,0:T(8,128)(2,1)S(1)}, s16[22,16,128]{2,1,0:T(8,128)(2,1)S(1)}, u32[]{:S(2)}, u32[]{:S(2)}) collective-permute-start(s16[22,16,128]{2,1,0:T(8,128)(2,1)S(1)} %get-tuple-element.35), channel_id=1, source_target_pairs={{0,16},{4,20},{8,24},{12,28},{16,0},{20,4},{24,8},{28,12},{1,17},{... | collective-permute-start | bytes 270344 | tf_op jit(solution)/shard_map/ppermute | solution.py:226
  30.3 4.8 %collective-permute-start.11 = (s16[7,16,128]{2,1,0:T(8,128)(2,1)S(1)}, s16[7,16,128]{2,1,0:T(8,128)(2,1)S(1)}, u32[]{:S(2)}, u32[]{:S(2)}) collective-permute-start(s16[7,16,128]{2,1,0:T(8,128)(2,1)S(1)} %get-tuple-element.37), channel_id=1, source_target_pairs={{0,2},{1,3},{2,0},{3,1},{4,6},{5,7},{6,4},{7,5},{8,10},{9,11},{10,... | collective-permute-start | bytes 86024 | tf_op jit(solution)/shard_map/ppermute | solution.py:226
  33.0 5.7 %collective-permute-start.12 = (s16[7,16,128]{2,1,0:T(8,128)(2,1)S(1)}, s16[7,16,128]{2,1,0:T(8,128)(2,1)S(1)}, u32[]{:S(2)}, u32[]{:S(2)}) collective-permute-start(s16[7,16,128]{2,1,0:T(8,128)(2,1)S(1)} %get-tuple-element.38), channel_id=1, source_target_pairs={{0,3},{1,2},{2,1},{3,0},{4,7},{5,6},{6,5},{7,4},{8,11},{9,10},{10,... | collective-permute-start | bytes 86024 | tf_op jit(solution)/shard_map/ppermute | solution.py:226
  34.4 4.3 %collective-permute-start.13 = (s16[7,16,128]{2,1,0:T(8,128)(2,1)S(1)}, s16[7,16,128]{2,1,0:T(8,128)(2,1)S(1)}, u32[]{:S(2)}, u32[]{:S(2)}) collective-permute-start(s16[7,16,128]{2,1,0:T(8,128)(2,1)S(1)} %get-tuple-element.39), channel_id=1, source_target_pairs={{0,1},{1,0},{2,3},{3,2},{4,5},{5,4},{6,7},{7,6},{8,9},{9,8},{10,11... | collective-permute-start | bytes 86024 | tf_op jit(solution)/shard_map/ppermute | solution.py:226

commit v13 on v12

--- a/solution.py
+++ b/solution.py
@@ -101,18 +101,19 @@
     groups = [k ^ core for core in range(2) for k in chips(chan_count)]
     fetch.wait()
     table = jnp.concatenate([table_ref[side, me ^ k] for side in range(2) for k in groups], axis=0)
-    for number in range(offset_count):
-        turn = chans - offset_of(number, offs_ref, chan_count // 2) * (chans // chan_count)
-        slot = number % 2
+    turns = [chans - offset_of(number, offs_ref, chan_count // 2) * (chans // chan_count) for number in range(offset_count)]
+
+    def cross(number):
         for row in range(0, freqs, step):
             own = [white_ref[part, row : row + step, :] for part in range(2)]
-            far_real, far_imag = (pltpu.roll(value, turn, 1).astype(jnp.float32) for value in own)
+            far_real, far_imag = (pltpu.roll(value, turns[number], 1).astype(jnp.float32) for value in own)
             own_real, own_imag = (value.astype(jnp.float32) for value in own)
             real = own_real * far_real + own_imag * far_imag
             imag = own_imag * far_real - own_real * far_imag
-            cross_ref[slot, row : row + step, 0:chans] = real.astype(jnp.bfloat16)
-            cross_ref[slot, row : row + step, chans : 2 * chans] = imag.astype(jnp.bfloat16)
-        sums = jnp.dot(table, cross_ref[slot], preferred_element_type=jnp.float32)
+            cross_ref[number, row : row + step, 0:chans] = real.astype(jnp.bfloat16)
+            cross_ref[number, row : row + step, chans : 2 * chans] = imag.astype(jnp.bfloat16)
+
+    def code_pairs(number, sums, levels):
         cos_real, sin_real = sums[:half, :chans], sums[half:, :chans]
         cos_imag, sin_imag = sums[:half, chans:], sums[half:, chans:]
         corr = (
@@ -124,7 +125,7 @@
         extra = 0.25 * (mean_power + 1e-06 * freqs)
         peak = jnp.max(jnp.maximum(jnp.abs(corr[0][0]), jnp.abs(corr[1][0])), axis=0, keepdims=True)
         code = level_code(peak)
-        keep = jnp.where(lane < turn, usable * pltpu.roll(usable, turn, 1), 0.0) * CODE_TOP
+        keep = jnp.where(lane < turns[number], usable * pltpu.roll(usable, turns[number], 1), 0.0) * CODE_TOP
         upscale = keep / level_of(code)
         inverse = [lax.rsqrt(side + extra) * keep for side in power]
         kinds = [
@@ -135,12 +136,21 @@
         if number == offset_count - 1:
             code = jnp.where(lane < chans // 2, code, pltpu.roll(code, chans // 2, 1))
             kinds = [[jnp.where(lane < chans // 2, ahead, pltpu.roll(back, chans // 2, 1))] for ahead, back in kinds]
-        levels = jnp.where(line == number, code, levels)
         for place, value in enumerate(value for kind in kinds for value in kind):
             coded = encode(value).reshape(chan_count, lag_rows, chans)
             for core in range(2):
                 rows = slice(core * chip_count, (core + 1) * chip_count)
                 out_refs[core][:, 6 * number + place, :, :] = coded[rows]
+        return jnp.where(line == number, code, levels)
+
+    waiting = []
+    for number in range(offset_count + 2):
+        if number < offset_count:
+            cross(number)
+        if 0 < number <= offset_count:
+            waiting.append(jnp.dot(table, cross_ref[number - 1], preferred_element_type=jnp.float32))
+        if number > 1:
+            levels = code_pairs(number - 2, waiting[number - 2], levels)
     for number in range(offset_count):
         levels = jnp.where(line == offset_count + number, offs_ref[number].astype(jnp.float32), levels)
     wide = widest(offs_ref, chan_count // 2).astype(jnp.float32)
@@ -342,7 +352,7 @@
         scratch_shapes=[
             pltpu.VMEM((freqs, chans), jnp.float32),
             pltpu.VMEM((2, freqs, chans), jnp.bfloat16),
-            pltpu.VMEM((2, freqs, 2 * chans), jnp.bfloat16),
+            pltpu.VMEM((offset_count, freqs, 2 * chans), jnp.bfloat16),
             pltpu.SMEM(offsets.shape, jnp.int32),
             pltpu.SemaphoreType.DMA(()),
         ],

time: 51.4 us -> 51.4 us (level)
  no operation moved by 1% of the time
where the time goes in v13:
time: 51.4 us; the launch traced here: 51.3 us
  waiting for transfers between devices  16.7 us (32%)
  starting transfers between devices  15.8 us (31%)
  blocking collectives  11.4 us (22%)
  Pallas kernels  7.22 us (14%)
    ppermute x14, waiting for transfers between devices, exchange(): lax.ppermute(piece, axis, [(source, source ^ k) for source in range(count)])  16.7 us
    ppermute x14, starting transfers between devices, exchange(): lax.ppermute(piece, axis, [(source, source ^ k) for source in range(count)])  15.8 us
    all_to_all x1, blocking collectives, window_shards(): lax.all_to_all(pieces.reshape(shape), ('chan', 'tm'), 0, 0, tiled=True)  11.4 us
    pallas_call x1, Pallas kernels, window_shards(): pl.pallas_call(functools.partial(window_kernel, chan_order), out_shape=[j...  3.43 us
    pallas_call x2, Pallas kernels, window_shards(): pl.pallas_call(functools.partial(split_kernel, part), out_shape=[jax.Shap...  2.32 us
  transfers between devices with their start and end apart: 14, of which 10 were waited for; matrix products, arithmetic and copies ran while one was open for 0% of the time, Pallas kernels for 2%

profile of v13, /device:TPU:0, one launch (start us, length us, event | category | flops | bytes accessed | tf_op | source)
XLA Modules:
  0.0 51.3 jit_solution(9491610710172584834)
XLA Ops:
  0.0 1.1 %split_windows.2 = (bf16[2,256,128]{2,1,0:T(8,128)(2,1)S(1)}, bf16[2,256,128]{2,1,0:T(8,128)(2,1)S(1)}) custom-call(s32[1]{0:T(128)} %bitcast.1.where_ref, bf16[2,8,256,128]{3,2,1,0:T(8,128)(2,1)} %spec_ref.3), custom_call_target="tpu_custom_call" | custom-call | tf_op jit(solution)/shard_map/split_windows/pallas_call | solution.py:336
  1.1 4.0 %collective-permute-start = (bf16[2,256,128]{2,1,0:T(8,128)(2,1)S(1)}, bf16[2,256,128]{2,1,0:T(8,128)(2,1)S(1)}, u32[]{:S(2)}, u32[]{:S(2)}) collective-permute-start(bf16[2,256,128]{2,1,0:T(8,128)(2,1)S(1)} %get-tuple-element.23), channel_id=1, source_target_pairs={{0,24},{4,28},{8,16},{12,20},{16,8},{20,12},{24,0},{28,4},{1,25},{... | collective-permute-start | bytes 393224 | tf_op jit(solution)/shard_map/ppermute | solution.py:236
  5.0 1.3 %split_windows.3 = (bf16[2,256,128]{2,1,0:T(8,128)(2,1)S(1)}, bf16[2,256,128]{2,1,0:T(8,128)(2,1)S(1)}, bf16[2,256,128]{2,1,0:T(8,128)(2,1)S(1)}, bf16[2,256,128...) custom-call(s32[1]{0:T(128)} %bitcast.1.where_ref, ...), custom_call_target="tpu_custom_call" | custom-call | tf_op jit(solution)/shard_map/split_windows/pallas_call | solution.py:336
  6.3 1.2 %collective-permute-start.2 = (bf16[2,256,128]{2,1,0:T(8,128)(2,1)S(1)}, bf16[2,256,128]{2,1,0:T(8,128)(2,1)S(1)}, u32[]{:S(2)}, u32[]{:S(2)}) collective-permute-start(bf16[2,256,128]{2,1,0:T(8,128)(2,1)S(1)} %get-tuple-element.25), channel_id=1, source_target_pairs={{0,8},{4,12},{8,0},{12,4},{16,24},{20,28},{24,16},{28,20},{1,9},{5... | collective-permute-start | bytes 393224 | tf_op jit(solution)/shard_map/ppermute | solution.py:236
  7.5 1.5 %collective-permute-start.3 = (bf16[2,256,128]{2,1,0:T(8,128)(2,1)S(1)}, bf16[2,256,128]{2,1,0:T(8,128)(2,1)S(1)}, u32[]{:S(2)}, u32[]{:S(2)}) collective-permute-start(bf16[2,256,128]{2,1,0:T(8,128)(2,1)S(1)} %get-tuple-element.26), channel_id=1, source_target_pairs={{0,16},{4,20},{8,24},{12,28},{16,0},{20,4},{24,8},{28,12},{1,17},{... | collective-permute-start | bytes 393224 | tf_op jit(solution)/shard_map/ppermute | solution.py:236
  9.0 0.6 %collective-permute-start.4 = (bf16[2,256,128]{2,1,0:T(8,128)(2,1)S(1)}, bf16[2,256,128]{2,1,0:T(8,128)(2,1)S(1)}, u32[]{:S(2)}, u32[]{:S(2)}) collective-permute-start(bf16[2,256,128]{2,1,0:T(8,128)(2,1)S(1)} %get-tuple-element.27), channel_id=1, source_target_pairs={{0,12},{4,8},{8,4},{12,0},{16,28},{20,24},{24,20},{28,16},{1,13},{... | collective-permute-start | bytes 393224 | tf_op jit(solution)/shard_map/ppermute | solution.py:236
  9.6 0.6 %collective-permute-start.5 = (bf16[2,256,128]{2,1,0:T(8,128)(2,1)S(1)}, bf16[2,256,128]{2,1,0:T(8,128)(2,1)S(1)}, u32[]{:S(2)}, u32[]{:S(2)}) collective-permute-start(bf16[2,256,128]{2,1,0:T(8,128)(2,1)S(1)} %get-tuple-element.28), channel_id=1, source_target_pairs={{0,20},{4,16},{8,28},{12,24},{16,4},{20,0},{24,12},{28,8},{1,21},{... | collective-permute-start | bytes 393224 | tf_op jit(solution)/shard_map/ppermute | solution.py:236
  10.2 1.6 %collective-permute-done.1.refs_1_ = bf16[2,256,128]{2,1,0:T(8,128)(2,1)S(1)} collective-permute-done((bf16[2,256,128]{2,1,0:T(8,128)(2,1)S(1)}, bf16[2,256,128]{2,1,0:T(8,128)(2,1)S(1)}, u32[]{:S(2)}, u32[]{:S(2)}) %collective-permute-start.1) | collective-permute-done | bytes 131104 | tf_op jit(solution)/shard_map/ppermute | solution.py:236
  11.8 3.5 %collective-permute-done.2.refs_2_ = bf16[2,256,128]{2,1,0:T(8,128)(2,1)S(1)} collective-permute-done((bf16[2,256,128]{2,1,0:T(8,128)(2,1)S(1)}, bf16[2,256,128]{2,1,0:T(8,128)(2,1)S(1)}, u32[]{:S(2)}, u32[]{:S(2)}) %collective-permute-start.2) | collective-permute-done | bytes 131104 | tf_op jit(solution)/shard_map/ppermute | solution.py:236
  15.2 1.1 %collective-permute-done.4.refs_4_ = bf16[2,256,128]{2,1,0:T(8,128)(2,1)S(1)} collective-permute-done((bf16[2,256,128]{2,1,0:T(8,128)(2,1)S(1)}, bf16[2,256,128]{2,1,0:T(8,128)(2,1)S(1)}, u32[]{:S(2)}, u32[]{:S(2)}) %collective-permute-start.4) | collective-permute-done | bytes 131104 | tf_op jit(solution)/shard_map/ppermute | solution.py:236
  16.4 0.7 %collective-permute-done.5.refs_5_ = bf16[2,256,128]{2,1,0:T(8,128)(2,1)S(1)} collective-permute-done((bf16[2,256,128]{2,1,0:T(8,128)(2,1)S(1)}, bf16[2,256,128]{2,1,0:T(8,128)(2,1)S(1)}, u32[]{:S(2)}, u32[]{:S(2)}) %collective-permute-start.5) | collective-permute-done | bytes 131104 | tf_op jit(solution)/shard_map/ppermute | solution.py:236
  17.1 3.4 %window_pairs.1 = (s16[4,22,16,128]{3,2,1,0:T(8,128)(2,1)S(1)}, s16[4,22,16,128]{3,2,1,0:T(8,128)(2,1)S(1)}) custom-call(s32[4]{0:T(128)} %offs_hbm_ref.1, s32[1]{0:T(128)} %bitcast.1.where_ref, bf16[2,256,128]{2,1,0:T(8,128)(2,1)S(1)} %collective-permute-done.refs_0_, bf16[2,256,128]{2,1,0:T(8,128)(2,1)S(1)} %collective-permute-done.1.refs_1_, ...), custom_call_target="tpu_custom_call" | custom-call | tf_op jit(solution)/shard_map/window_pairs/pallas_call | solution.py:347
  20.7 1.5 %collective-permute-done.7.far_ref = s16[4,22,16,128]{3,2,1,0:T(8,128)(2,1)S(1)} collective-permute-done((s16[4,22,16,128]{3,2,1,0:T(8,128)(2,1)S(1)}, s16[4,22,16,128]{3,2,1,0:T(8,128)(2,1)S(1)}, u32[]{:S(2)}, u32[]{:S(2)}) %collective-permute-start.7) | collective-permute-done | bytes 360480 | tf_op jit(solution)/shard_map/ppermute | solution.py:236
  22.5 2.6 %collective-permute-start.8 = (s16[22,16,128]{2,1,0:T(8,128)(2,1)S(1)}, s16[22,16,128]{2,1,0:T(8,128)(2,1)S(1)}, u32[]{:S(2)}, u32[]{:S(2)}) collective-permute-start(s16[22,16,128]{2,1,0:T(8,128)(2,1)S(1)} %get-tuple-element.33), channel_id=1, source_target_pairs={{0,24},{4,28},{8,16},{12,20},{16,8},{20,12},{24,0},{28,4},{1,25},{... | collective-permute-start | bytes 270344 | tf_op jit(solution)/shard_map/ppermute | solution.py:236
  25.0 0.4 collective-permute-start.9
  25.5 0.5 %collective-permute-start.10 = (s16[22,16,128]{2,1,0:T(8,128)(2,1)S(1)}, s16[22,16,128]{2,1,0:T(8,128)(2,1)S(1)}, u32[]{:S(2)}, u32[]{:S(2)}) collective-permute-start(s16[22,16,128]{2,1,0:T(8,128)(2,1)S(1)} %get-tuple-element.35), channel_id=1, source_target_pairs={{0,16},{4,20},{8,24},{12,28},{16,0},{20,4},{24,8},{28,12},{1,17},{... | collective-permute-start | bytes 270344 | tf_op jit(solution)/shard_map/ppermute | solution.py:236
  26.0 2.8 %collective-permute-done.8.refs_0_ = s16[22,16,128]{2,1,0:T(8,128)(2,1)S(1)} collective-permute-done((s16[22,16,128]{2,1,0:T(8,128)(2,1)S(1)}, s16[22,16,128]{2,1,0:T(8,128)(2,1)S(1)}, u32[]{:S(2)}, u32[]{:S(2)}) %collective-permute-start.8) | collective-permute-done | bytes 90144 | tf_op jit(solution)/shard_map/ppermute | solution.py:236
  28.8 1.3 %collective-permute-done.9.refs_1_ = s16[22,16,128]{2,1,0:T(8,128)(2,1)S(1)} collective-permute-done((s16[22,16,128]{2,1,0:T(8,128)(2,1)S(1)}, s16[22,16,128]{2,1,0:T(8,128)(2,1)S(1)}, u32[]{:S(2)}, u32[]{:S(2)}) %collective-permute-start.9) | collective-permute-done | bytes 90144 | tf_op jit(solution)/shard_map/ppermute | solution.py:236
  30.3 2.7 %collective-permute-start.11 = (s16[7,16,128]{2,1,0:T(8,128)(2,1)S(1)}, s16[7,16,128]{2,1,0:T(8,128)(2,1)S(1)}, u32[]{:S(2)}, u32[]{:S(2)}) collective-permute-start(s16[7,16,128]{2,1,0:T(8,128)(2,1)S(1)} %get-tuple-element.37), channel_id=1, source_target_pairs={{0,2},{1,3},{2,0},{3,1},{4,6},{5,7},{6,4},{7,5},{8,10},{9,11},{10,... | collective-permute-start | bytes 86024 | tf_op jit(solution)/shard_map/ppermute | solution.py:236
  33.0 1.3 %collective-permute-start.12 = (s16[7,16,128]{2,1,0:T(8,128)(2,1)S(1)}, s16[7,16,128]{2,1,0:T(8,128)(2,1)S(1)}, u32[]{:S(2)}, u32[]{:S(2)}) collective-permute-start(s16[7,16,128]{2,1,0:T(8,128)(2,1)S(1)} %get-tuple-element.38), channel_id=1, source_target_pairs={{0,3},{1,2},{2,1},{3,0},{4,7},{5,6},{6,5},{7,4},{8,11},{9,10},{10,... | collective-permute-start | bytes 86024 | tf_op jit(solution)/shard_map/ppermute | solution.py:236
  34.6 0.5 %collective-permute-done.11.refs_0_ = s16[7,16,128]{2,1,0:T(8,128)(2,1)S(1)} collective-permute-done((s16[7,16,128]{2,1,0:T(8,128)(2,1)S(1)}, s16[7,16,128]{2,1,0:T(8,128)(2,1)S(1)}, u32[]{:S(2)}, u32[]{:S(2)}) %collective-permute-start.11) | collective-permute-done | bytes 28704 | tf_op jit(solution)/shard_map/ppermute | solution.py:236
  35.1 3.5 %collective-permute-done.12.refs_1_ = s16[7,16,128]{2,1,0:T(8,128)(2,1)S(1)} collective-permute-done((s16[7,16,128]{2,1,0:T(8,128)(2,1)S(1)}, s16[7,16,128]{2,1,0:T(8,128)(2,1)S(1)}, u32[]{:S(2)}, u32[]{:S(2)}) %collective-permute-start.12) | collective-permute-done | bytes 28704 | tf_op jit(solution)/shard_map/ppermute | solution.py:236
  38.9 11.4 %all_to_all.5 = f32[32,4,128]{2,1,0:T(4,128)S(1)} all-to-all(f32[32,4,128]{2,1,0:T(4,128)S(1)} %bitcast.5), channel_id=1, replica_groups=mesh['chan'=8,'tm'=4] {'chan','tm'}, dimensions={0} | all-to-all | bytes 131072 | tf_op jit(solution)/shard_map/all_to_all | solution.py:388
  50.4 0.9 %place_lags.1 = f32[16,4,256]{2,1,0:T(4,128)} custom-call(f32[8,4,4,128]{3,2,1,0:T(4,128)S(1)} %bitcast.4), custom_call_target="tpu_custom_call" | custom-call | tf_op jit(solution)/shard_map/place_lags/pallas_call | solution.py:389
  (16 shorter events, 1.1 us)
Async XLA Ops:
  0.0 17.1 %copy-start = (bf16[2,8,16,2048]{3,2,1,0:T(8,128)(2,1)S(1)}, bf16[2,8,16,2048]{3,2,1,0:T(8,128)(2,1)}, u32[]{:S(2)}) copy-start(bf16[2,8,16,2048]{3,2,1,0:T(8,128)(2,1)} %constant.11.clone.refs_9_) | copy-start | bytes 3145732
  1.1 8.5 %collective-permute-start = (bf16[2,256,128]{2,1,0:T(8,128)(2,1)S(1)}, bf16[2,256,128]{2,1,0:T(8,128)(2,1)S(1)}, u32[]{:S(2)}, u32[]{:S(2)}) collective-permute-start(bf16[2,256,128]{2,1,0:T(8,128)(2,1)S(1)} %get-tuple-element.23), channel_id=1, source_target_pairs={{0,24},{4,28},{8,16},{12,20},{16,8},{20,12},{24,0},{28,4},{1,25},{... | collective-permute-start | bytes 393224 | tf_op jit(solution)/shard_map/ppermute | solution.py:236
  5.0 6.7 %collective-permute-start.1 = (bf16[2,256,128]{2,1,0:T(8,128)(2,1)S(1)}, bf16[2,256,128]{2,1,0:T(8,128)(2,1)S(1)}, u32[]{:S(2)}, u32[]{:S(2)}) collective-permute-start(bf16[2,256,128]{2,1,0:T(8,128)(2,1)S(1)} %get-tuple-element.24), channel_id=1, source_target_pairs={{0,28},{4,24},{8,20},{12,16},{16,12},{20,8},{24,4},{28,0},{1,29},{... | collective-permute-start | bytes 393224 | tf_op jit(solution)/shard_map/ppermute | solution.py:236
  6.3 8.9 %collective-permute-start.2 = (bf16[2,256,128]{2,1,0:T(8,128)(2,1)S(1)}, bf16[2,256,128]{2,1,0:T(8,128)(2,1)S(1)}, u32[]{:S(2)}, u32[]{:S(2)}) collective-permute-start(bf16[2,256,128]{2,1,0:T(8,128)(2,1)S(1)} %get-tuple-element.25), channel_id=1, source_target_pairs={{0,8},{4,12},{8,0},{12,4},{16,24},{20,28},{24,16},{28,20},{1,9},{5... | collective-permute-start | bytes 393224 | tf_op jit(solution)/shard_map/ppermute | solution.py:236
  7.5 9.6 %copy-start.1 = (s32[8,128]{1,0:T(8,128)S(1)}, s32[8,128]{1,0:T(8,128)}, u32[]{:S(2)}) copy-start(s32[8,128]{1,0:T(8,128)} %refs_8_.1) | copy-start | bytes 12292
  7.5 7.7 %collective-permute-start.3 = (bf16[2,256,128]{2,1,0:T(8,128)(2,1)S(1)}, bf16[2,256,128]{2,1,0:T(8,128)(2,1)S(1)}, u32[]{:S(2)}, u32[]{:S(2)}) collective-permute-start(bf16[2,256,128]{2,1,0:T(8,128)(2,1)S(1)} %get-tuple-element.26), channel_id=1, source_target_pairs={{0,16},{4,20},{8,24},{12,28},{16,0},{20,4},{24,8},{28,12},{1,17},{... | collective-permute-start | bytes 393224 | tf_op jit(solution)/shard_map/ppermute | solution.py:236
  9.0 7.4 %collective-permute-start.4 = (bf16[2,256,128]{2,1,0:T(8,128)(2,1)S(1)}, bf16[2,256,128]{2,1,0:T(8,128)(2,1)S(1)}, u32[]{:S(2)}, u32[]{:S(2)}) collective-permute-start(bf16[2,256,128]{2,1,0:T(8,128)(2,1)S(1)} %get-tuple-element.27), channel_id=1, source_target_pairs={{0,12},{4,8},{8,4},{12,0},{16,28},{20,24},{24,20},{28,16},{1,13},{... | collective-permute-start | bytes 393224 | tf_op jit(solution)/shard_map/ppermute | solution.py:236
  9.6 7.5 %collective-permute-start.5 = (bf16[2,256,128]{2,1,0:T(8,128)(2,1)S(1)}, bf16[2,256,128]{2,1,0:T(8,128)(2,1)S(1)}, u32[]{:S(2)}, u32[]{:S(2)}) collective-permute-start(bf16[2,256,128]{2,1,0:T(8,128)(2,1)S(1)} %get-tuple-element.28), channel_id=1, source_target_pairs={{0,20},{4,16},{8,28},{12,24},{16,4},{20,0},{24,12},{28,8},{1,21},{... | collective-permute-start | bytes 393224 | tf_op jit(solution)/shard_map/ppermute | solution.py:236
  11.8 5.3 %collective-permute-start.6 = (bf16[2,256,128]{2,1,0:T(8,128)(2,1)S(1)}, bf16[2,256,128]{2,1,0:T(8,128)(2,1)S(1)}, u32[]{:S(2)}, u32[]{:S(2)}) collective-permute-start(bf16[2,256,128]{2,1,0:T(8,128)(2,1)S(1)} %get-tuple-element.29), channel_id=1, source_target_pairs={{0,4},{4,0},{8,12},{12,8},{16,20},{20,16},{24,28},{28,24},{1,5},{5... | collective-permute-start | bytes 393224 | tf_op jit(solution)/shard_map/ppermute | solution.py:236
  20.5 1.7 %collective-permute-start.7 = (s16[4,22,16,128]{3,2,1,0:T(8,128)(2,1)S(1)}, s16[4,22,16,128]{3,2,1,0:T(8,128)(2,1)S(1)}, u32[]{:S(2)}, u32[]{:S(2)}) collective-permute-start(s16[4,22,16,128]{3,2,1,0:T(8,128)(2,1)S(1)} %get-tuple-element.32), channel_id=1, source_target_pairs={{0,4},{4,0},{8,12},{12,8},{16,20},{20,16},{24,28},{28,24},{1,5},{5... | collective-permute-start | bytes 1081352 | tf_op jit(solution)/shard_map/ppermute | solution.py:236
  22.5 6.3 %collective-permute-start.8 = (s16[22,16,128]{2,1,0:T(8,128)(2,1)S(1)}, s16[22,16,128]{2,1,0:T(8,128)(2,1)S(1)}, u32[]{:S(2)}, u32[]{:S(2)}) collective-permute-start(s16[22,16,128]{2,1,0:T(8,128)(2,1)S(1)} %get-tuple-element.33), channel_id=1, source_target_pairs={{0,24},{4,28},{8,16},{12,20},{16,8},{20,12},{24,0},{28,4},{1,25},{... | collective-permute-start | bytes 270344 | tf_op jit(solution)/shard_map/ppermute | solution.py:236
  25.0 5.0 %collective-permute-start.9 = (s16[22,16,128]{2,1,0:T(8,128)(2,1)S(1)}, s16[22,16,128]{2,1,0:T(8,128)(2,1)S(1)}, u32[]{:S(2)}, u32[]{:S(2)}) collective-permute-start(s16[22,16,128]{2,1,0:T(8,128)(2,1)S(1)} %get-tuple-element.34), channel_id=1, source_target_pairs={{0,8},{4,12},{8,0},{12,4},{16,24},{20,28},{24,16},{28,20},{1,9},{5... | collective-permute-start | bytes 270344 | tf_op jit(solution)/shard_map/ppermute | solution.py:236
  25.5 4.7 %collective-permute-start.10 = (s16[22,16,128]{2,1,0:T(8,128)(2,1)S(1)}, s16[22,16,128]{2,1,0:T(8,128)(2,1)S(1)}, u32[]{:S(2)}, u32[]{:S(2)}) collective-permute-start(s16[22,16,128]{2,1,0:T(8,128)(2,1)S(1)} %get-tuple-element.35), channel_id=1, source_target_pairs={{0,16},{4,20},{8,24},{12,28},{16,0},{20,4},{24,8},{28,12},{1,17},{... | collective-permute-start | bytes 270344 | tf_op jit(solution)/shard_map/ppermute | solution.py:236
  30.3 4.8 %collective-permute-start.11 = (s16[7,16,128]{2,1,0:T(8,128)(2,1)S(1)}, s16[7,16,128]{2,1,0:T(8,128)(2,1)S(1)}, u32[]{:S(2)}, u32[]{:S(2)}) collective-permute-start(s16[7,16,128]{2,1,0:T(8,128)(2,1)S(1)} %get-tuple-element.37), channel_id=1, source_target_pairs={{0,2},{1,3},{2,0},{3,1},{4,6},{5,7},{6,4},{7,5},{8,10},{9,11},{10,... | collective-permute-start | bytes 86024 | tf_op jit(solution)/shard_map/ppermute | solution.py:236
  33.0 5.7 %collective-permute-start.12 = (s16[7,16,128]{2,1,0:T(8,128)(2,1)S(1)}, s16[7,16,128]{2,1,0:T(8,128)(2,1)S(1)}, u32[]{:S(2)}, u32[]{:S(2)}) collective-permute-start(s16[7,16,128]{2,1,0:T(8,128)(2,1)S(1)} %get-tuple-element.38), channel_id=1, source_target_pairs={{0,3},{1,2},{2,1},{3,0},{4,7},{5,6},{6,5},{7,4},{8,11},{9,10},{10,... | collective-permute-start | bytes 86024 | tf_op jit(solution)/shard_map/ppermute | solution.py:236
  34.4 4.3 %collective-permute-start.13 = (s16[7,16,128]{2,1,0:T(8,128)(2,1)S(1)}, s16[7,16,128]{2,1,0:T(8,128)(2,1)S(1)}, u32[]{:S(2)}, u32[]{:S(2)}) collective-permute-start(s16[7,16,128]{2,1,0:T(8,128)(2,1)S(1)} %get-tuple-element.39), channel_id=1, source_target_pairs={{0,1},{1,0},{2,3},{3,2},{4,5},{5,4},{6,7},{7,6},{8,9},{9,8},{10,11... | collective-permute-start | bytes 86024 | tf_op jit(solution)/shard_map/ppermute | solution.py:236

commit v14 on v12

--- a/solution.py
+++ b/solution.py
@@ -105,9 +105,8 @@
         turn = chans - offset_of(number, offs_ref, chan_count // 2) * (chans // chan_count)
         slot = number % 2
         for row in range(0, freqs, step):
-            own = [white_ref[part, row : row + step, :] for part in range(2)]
-            far_real, far_imag = (pltpu.roll(value, turn, 1).astype(jnp.float32) for value in own)
-            own_real, own_imag = (value.astype(jnp.float32) for value in own)
+            own_real, own_imag = (white_ref[part, row : row + step, :].astype(jnp.float32) for part in range(2))
+            far_real, far_imag = (pltpu.roll(value, turn, 1) for value in (own_real, own_imag))
             real = own_real * far_real + own_imag * far_imag
             imag = own_imag * far_real - own_real * far_imag
             cross_ref[slot, row : row + step, 0:chans] = real.astype(jnp.bfloat16)

time: 51.4 us -> 51.6 us (level)
  no operation moved by 1% of the time
where the time goes in v14:
time: 51.6 us; the launch traced here: 51.4 us
  waiting for transfers between devices  16.7 us (32%)
  starting transfers between devices  15.8 us (31%)
  blocking collectives  11.4 us (22%)
  Pallas kernels  7.34 us (14%)
    ppermute x14, waiting for transfers between devices, exchange(): lax.ppermute(piece, axis, [(source, source ^ k) for source in range(count)])  16.7 us
    ppermute x14, starting transfers between devices, exchange(): lax.ppermute(piece, axis, [(source, source ^ k) for source in range(count)])  15.8 us
    all_to_all x1, blocking collectives, window_shards(): lax.all_to_all(pieces.reshape(shape), ('chan', 'tm'), 0, 0, tiled=True)  11.4 us
    pallas_call x1, Pallas kernels, window_shards(): pl.pallas_call(functools.partial(window_kernel, chan_order), out_shape=[j...  3.55 us
    pallas_call x2, Pallas kernels, window_shards(): pl.pallas_call(functools.partial(split_kernel, part), out_shape=[jax.Shap...  2.32 us
  transfers between devices with their start and end apart: 14, of which 10 were waited for; matrix products, arithmetic and copies ran while one was open for 0% of the time, Pallas kernels for 2%

profile of v14, /device:TPU:0, one launch (start us, length us, event | category | flops | bytes accessed | tf_op | source)
XLA Modules:
  0.0 51.4 jit_solution(4108251898437654109)
XLA Ops:
  0.0 1.1 %split_windows.2 = (bf16[2,256,128]{2,1,0:T(8,128)(2,1)S(1)}, bf16[2,256,128]{2,1,0:T(8,128)(2,1)S(1)}) custom-call(s32[1]{0:T(128)} %bitcast.1.where_ref, bf16[2,8,256,128]{3,2,1,0:T(8,128)(2,1)} %spec_ref.3), custom_call_target="tpu_custom_call" | custom-call | tf_op jit(solution)/shard_map/split_windows/pallas_call | solution.py:325
  1.1 4.0 %collective-permute-start = (bf16[2,256,128]{2,1,0:T(8,128)(2,1)S(1)}, bf16[2,256,128]{2,1,0:T(8,128)(2,1)S(1)}, u32[]{:S(2)}, u32[]{:S(2)}) collective-permute-start(bf16[2,256,128]{2,1,0:T(8,128)(2,1)S(1)} %get-tuple-element.23), channel_id=1, source_target_pairs={{0,24},{4,28},{8,16},{12,20},{16,8},{20,12},{24,0},{28,4},{1,25},{... | collective-permute-start | bytes 393224 | tf_op jit(solution)/shard_map/ppermute | solution.py:225
  5.0 1.3 %split_windows.3 = (bf16[2,256,128]{2,1,0:T(8,128)(2,1)S(1)}, bf16[2,256,128]{2,1,0:T(8,128)(2,1)S(1)}, bf16[2,256,128]{2,1,0:T(8,128)(2,1)S(1)}, bf16[2,256,128...) custom-call(s32[1]{0:T(128)} %bitcast.1.where_ref, ...), custom_call_target="tpu_custom_call" | custom-call | tf_op jit(solution)/shard_map/split_windows/pallas_call | solution.py:325
  6.3 1.2 %collective-permute-start.2 = (bf16[2,256,128]{2,1,0:T(8,128)(2,1)S(1)}, bf16[2,256,128]{2,1,0:T(8,128)(2,1)S(1)}, u32[]{:S(2)}, u32[]{:S(2)}) collective-permute-start(bf16[2,256,128]{2,1,0:T(8,128)(2,1)S(1)} %get-tuple-element.25), channel_id=1, source_target_pairs={{0,8},{4,12},{8,0},{12,4},{16,24},{20,28},{24,16},{28,20},{1,9},{5... | collective-permute-start | bytes 393224 | tf_op jit(solution)/shard_map/ppermute | solution.py:225
  7.5 1.5 %collective-permute-start.3 = (bf16[2,256,128]{2,1,0:T(8,128)(2,1)S(1)}, bf16[2,256,128]{2,1,0:T(8,128)(2,1)S(1)}, u32[]{:S(2)}, u32[]{:S(2)}) collective-permute-start(bf16[2,256,128]{2,1,0:T(8,128)(2,1)S(1)} %get-tuple-element.26), channel_id=1, source_target_pairs={{0,16},{4,20},{8,24},{12,28},{16,0},{20,4},{24,8},{28,12},{1,17},{... | collective-permute-start | bytes 393224 | tf_op jit(solution)/shard_map/ppermute | solution.py:225
  9.0 0.6 %collective-permute-start.4 = (bf16[2,256,128]{2,1,0:T(8,128)(2,1)S(1)}, bf16[2,256,128]{2,1,0:T(8,128)(2,1)S(1)}, u32[]{:S(2)}, u32[]{:S(2)}) collective-permute-start(bf16[2,256,128]{2,1,0:T(8,128)(2,1)S(1)} %get-tuple-element.27), channel_id=1, source_target_pairs={{0,12},{4,8},{8,4},{12,0},{16,28},{20,24},{24,20},{28,16},{1,13},{... | collective-permute-start | bytes 393224 | tf_op jit(solution)/shard_map/ppermute | solution.py:225
  9.6 0.6 %collective-permute-start.5 = (bf16[2,256,128]{2,1,0:T(8,128)(2,1)S(1)}, bf16[2,256,128]{2,1,0:T(8,128)(2,1)S(1)}, u32[]{:S(2)}, u32[]{:S(2)}) collective-permute-start(bf16[2,256,128]{2,1,0:T(8,128)(2,1)S(1)} %get-tuple-element.28), channel_id=1, source_target_pairs={{0,20},{4,16},{8,28},{12,24},{16,4},{20,0},{24,12},{28,8},{1,21},{... | collective-permute-start | bytes 393224 | tf_op jit(solution)/shard_map/ppermute | solution.py:225
  10.2 1.6 %collective-permute-done.1.refs_1_ = bf16[2,256,128]{2,1,0:T(8,128)(2,1)S(1)} collective-permute-done((bf16[2,256,128]{2,1,0:T(8,128)(2,1)S(1)}, bf16[2,256,128]{2,1,0:T(8,128)(2,1)S(1)}, u32[]{:S(2)}, u32[]{:S(2)}) %collective-permute-start.1) | collective-permute-done | bytes 131104 | tf_op jit(solution)/shard_map/ppermute | solution.py:225
  11.8 3.5 %collective-permute-done.2.refs_2_ = bf16[2,256,128]{2,1,0:T(8,128)(2,1)S(1)} collective-permute-done((bf16[2,256,128]{2,1,0:T(8,128)(2,1)S(1)}, bf16[2,256,128]{2,1,0:T(8,128)(2,1)S(1)}, u32[]{:S(2)}, u32[]{:S(2)}) %collective-permute-start.2) | collective-permute-done | bytes 131104 | tf_op jit(solution)/shard_map/ppermute | solution.py:225
  15.2 1.1 %collective-permute-done.4.refs_4_ = bf16[2,256,128]{2,1,0:T(8,128)(2,1)S(1)} collective-permute-done((bf16[2,256,128]{2,1,0:T(8,128)(2,1)S(1)}, bf16[2,256,128]{2,1,0:T(8,128)(2,1)S(1)}, u32[]{:S(2)}, u32[]{:S(2)}) %collective-permute-start.4) | collective-permute-done | bytes 131104 | tf_op jit(solution)/shard_map/ppermute | solution.py:225
  16.4 0.7 %collective-permute-done.5.refs_5_ = bf16[2,256,128]{2,1,0:T(8,128)(2,1)S(1)} collective-permute-done((bf16[2,256,128]{2,1,0:T(8,128)(2,1)S(1)}, bf16[2,256,128]{2,1,0:T(8,128)(2,1)S(1)}, u32[]{:S(2)}, u32[]{:S(2)}) %collective-permute-start.5) | collective-permute-done | bytes 131104 | tf_op jit(solution)/shard_map/ppermute | solution.py:225
  17.1 3.6 %window_pairs.1 = (s16[4,22,16,128]{3,2,1,0:T(8,128)(2,1)S(1)}, s16[4,22,16,128]{3,2,1,0:T(8,128)(2,1)S(1)}) custom-call(s32[4]{0:T(128)} %offs_hbm_ref.1, s32[1]{0:T(128)} %bitcast.1.where_ref, bf16[2,256,128]{2,1,0:T(8,128)(2,1)S(1)} %collective-permute-done.refs_0_, bf16[2,256,128]{2,1,0:T(8,128)(2,1)S(1)} %collective-permute-done.1.refs_1_, ...), custom_call_target="tpu_custom_call" | custom-call | tf_op jit(solution)/shard_map/window_pairs/pallas_call | solution.py:336
  20.8 1.5 %collective-permute-done.7.far_ref = s16[4,22,16,128]{3,2,1,0:T(8,128)(2,1)S(1)} collective-permute-done((s16[4,22,16,128]{3,2,1,0:T(8,128)(2,1)S(1)}, s16[4,22,16,128]{3,2,1,0:T(8,128)(2,1)S(1)}, u32[]{:S(2)}, u32[]{:S(2)}) %collective-permute-start.7) | collective-permute-done | bytes 360480 | tf_op jit(solution)/shard_map/ppermute | solution.py:225
  22.6 2.6 %collective-permute-start.8 = (s16[22,16,128]{2,1,0:T(8,128)(2,1)S(1)}, s16[22,16,128]{2,1,0:T(8,128)(2,1)S(1)}, u32[]{:S(2)}, u32[]{:S(2)}) collective-permute-start(s16[22,16,128]{2,1,0:T(8,128)(2,1)S(1)} %get-tuple-element.33), channel_id=1, source_target_pairs={{0,24},{4,28},{8,16},{12,20},{16,8},{20,12},{24,0},{28,4},{1,25},{... | collective-permute-start | bytes 270344 | tf_op jit(solution)/shard_map/ppermute | solution.py:225
  25.2 0.5 collective-permute-start.9
  25.6 0.5 %collective-permute-start.10 = (s16[22,16,128]{2,1,0:T(8,128)(2,1)S(1)}, s16[22,16,128]{2,1,0:T(8,128)(2,1)S(1)}, u32[]{:S(2)}, u32[]{:S(2)}) collective-permute-start(s16[22,16,128]{2,1,0:T(8,128)(2,1)S(1)} %get-tuple-element.35), channel_id=1, source_target_pairs={{0,16},{4,20},{8,24},{12,28},{16,0},{20,4},{24,8},{28,12},{1,17},{... | collective-permute-start | bytes 270344 | tf_op jit(solution)/shard_map/ppermute | solution.py:225
  26.1 2.8 %collective-permute-done.8.refs_0_ = s16[22,16,128]{2,1,0:T(8,128)(2,1)S(1)} collective-permute-done((s16[22,16,128]{2,1,0:T(8,128)(2,1)S(1)}, s16[22,16,128]{2,1,0:T(8,128)(2,1)S(1)}, u32[]{:S(2)}, u32[]{:S(2)}) %collective-permute-start.8) | collective-permute-done | bytes 90144 | tf_op jit(solution)/shard_map/ppermute | solution.py:225
  28.9 1.3 %collective-permute-done.9.refs_1_ = s16[22,16,128]{2,1,0:T(8,128)(2,1)S(1)} collective-permute-done((s16[22,16,128]{2,1,0:T(8,128)(2,1)S(1)}, s16[22,16,128]{2,1,0:T(8,128)(2,1)S(1)}, u32[]{:S(2)}, u32[]{:S(2)}) %collective-permute-start.9) | collective-permute-done | bytes 90144 | tf_op jit(solution)/shard_map/ppermute | solution.py:225
  30.4 2.7 %collective-permute-start.11 = (s16[7,16,128]{2,1,0:T(8,128)(2,1)S(1)}, s16[7,16,128]{2,1,0:T(8,128)(2,1)S(1)}, u32[]{:S(2)}, u32[]{:S(2)}) collective-permute-start(s16[7,16,128]{2,1,0:T(8,128)(2,1)S(1)} %get-tuple-element.37), channel_id=1, source_target_pairs={{0,2},{1,3},{2,0},{3,1},{4,6},{5,7},{6,4},{7,5},{8,10},{9,11},{10,... | collective-permute-start | bytes 86024 | tf_op jit(solution)/shard_map/ppermute | solution.py:225
  33.2 1.3 %collective-permute-start.12 = (s16[7,16,128]{2,1,0:T(8,128)(2,1)S(1)}, s16[7,16,128]{2,1,0:T(8,128)(2,1)S(1)}, u32[]{:S(2)}, u32[]{:S(2)}) collective-permute-start(s16[7,16,128]{2,1,0:T(8,128)(2,1)S(1)} %get-tuple-element.38), channel_id=1, source_target_pairs={{0,3},{1,2},{2,1},{3,0},{4,7},{5,6},{6,5},{7,4},{8,11},{9,10},{10,... | collective-permute-start | bytes 86024 | tf_op jit(solution)/shard_map/ppermute | solution.py:225
  34.7 0.5 %collective-permute-done.11.refs_0_ = s16[7,16,128]{2,1,0:T(8,128)(2,1)S(1)} collective-permute-done((s16[7,16,128]{2,1,0:T(8,128)(2,1)S(1)}, s16[7,16,128]{2,1,0:T(8,128)(2,1)S(1)}, u32[]{:S(2)}, u32[]{:S(2)}) %collective-permute-start.11) | collective-permute-done | bytes 28704 | tf_op jit(solution)/shard_map/ppermute | solution.py:225
  35.3 3.5 %collective-permute-done.12.refs_1_ = s16[7,16,128]{2,1,0:T(8,128)(2,1)S(1)} collective-permute-done((s16[7,16,128]{2,1,0:T(8,128)(2,1)S(1)}, s16[7,16,128]{2,1,0:T(8,128)(2,1)S(1)}, u32[]{:S(2)}, u32[]{:S(2)}) %collective-permute-start.12) | collective-permute-done | bytes 28704 | tf_op jit(solution)/shard_map/ppermute | solution.py:225
  39.0 11.4 %all_to_all.5 = f32[32,4,128]{2,1,0:T(4,128)S(1)} all-to-all(f32[32,4,128]{2,1,0:T(4,128)S(1)} %bitcast.5), channel_id=1, replica_groups=mesh['chan'=8,'tm'=4] {'chan','tm'}, dimensions={0} | all-to-all | bytes 131072 | tf_op jit(solution)/shard_map/all_to_all | solution.py:377
  50.5 0.9 %place_lags.1 = f32[16,4,256]{2,1,0:T(4,128)} custom-call(f32[8,4,4,128]{3,2,1,0:T(4,128)S(1)} %bitcast.4), custom_call_target="tpu_custom_call" | custom-call | tf_op jit(solution)/shard_map/place_lags/pallas_call | solution.py:378
  (16 shorter events, 1.1 us)
Async XLA Ops:
  0.0 17.1 %copy-start = (bf16[2,8,16,2048]{3,2,1,0:T(8,128)(2,1)S(1)}, bf16[2,8,16,2048]{3,2,1,0:T(8,128)(2,1)}, u32[]{:S(2)}) copy-start(bf16[2,8,16,2048]{3,2,1,0:T(8,128)(2,1)} %constant.11.clone.refs_9_) | copy-start | bytes 3145732
  1.1 8.5 %collective-permute-start = (bf16[2,256,128]{2,1,0:T(8,128)(2,1)S(1)}, bf16[2,256,128]{2,1,0:T(8,128)(2,1)S(1)}, u32[]{:S(2)}, u32[]{:S(2)}) collective-permute-start(bf16[2,256,128]{2,1,0:T(8,128)(2,1)S(1)} %get-tuple-element.23), channel_id=1, source_target_pairs={{0,24},{4,28},{8,16},{12,20},{16,8},{20,12},{24,0},{28,4},{1,25},{... | collective-permute-start | bytes 393224 | tf_op jit(solution)/shard_map/ppermute | solution.py:225
  5.0 6.7 %collective-permute-start.1 = (bf16[2,256,128]{2,1,0:T(8,128)(2,1)S(1)}, bf16[2,256,128]{2,1,0:T(8,128)(2,1)S(1)}, u32[]{:S(2)}, u32[]{:S(2)}) collective-permute-start(bf16[2,256,128]{2,1,0:T(8,128)(2,1)S(1)} %get-tuple-element.24), channel_id=1, source_target_pairs={{0,28},{4,24},{8,20},{12,16},{16,12},{20,8},{24,4},{28,0},{1,29},{... | collective-permute-start | bytes 393224 | tf_op jit(solution)/shard_map/ppermute | solution.py:225
  6.3 8.9 %collective-permute-start.2 = (bf16[2,256,128]{2,1,0:T(8,128)(2,1)S(1)}, bf16[2,256,128]{2,1,0:T(8,128)(2,1)S(1)}, u32[]{:S(2)}, u32[]{:S(2)}) collective-permute-start(bf16[2,256,128]{2,1,0:T(8,128)(2,1)S(1)} %get-tuple-element.25), channel_id=1, source_target_pairs={{0,8},{4,12},{8,0},{12,4},{16,24},{20,28},{24,16},{28,20},{1,9},{5... | collective-permute-start | bytes 393224 | tf_op jit(solution)/shard_map/ppermute | solution.py:225
  7.5 9.6 %copy-start.1 = (s32[8,128]{1,0:T(8,128)S(1)}, s32[8,128]{1,0:T(8,128)}, u32[]{:S(2)}) copy-start(s32[8,128]{1,0:T(8,128)} %refs_8_.1) | copy-start | bytes 12292
  7.5 7.7 %collective-permute-start.3 = (bf16[2,256,128]{2,1,0:T(8,128)(2,1)S(1)}, bf16[2,256,128]{2,1,0:T(8,128)(2,1)S(1)}, u32[]{:S(2)}, u32[]{:S(2)}) collective-permute-start(bf16[2,256,128]{2,1,0:T(8,128)(2,1)S(1)} %get-tuple-element.26), channel_id=1, source_target_pairs={{0,16},{4,20},{8,24},{12,28},{16,0},{20,4},{24,8},{28,12},{1,17},{... | collective-permute-start | bytes 393224 | tf_op jit(solution)/shard_map/ppermute | solution.py:225
  9.0 7.4 %collective-permute-start.4 = (bf16[2,256,128]{2,1,0:T(8,128)(2,1)S(1)}, bf16[2,256,128]{2,1,0:T(8,128)(2,1)S(1)}, u32[]{:S(2)}, u32[]{:S(2)}) collective-permute-start(bf16[2,256,128]{2,1,0:T(8,128)(2,1)S(1)} %get-tuple-element.27), channel_id=1, source_target_pairs={{0,12},{4,8},{8,4},{12,0},{16,28},{20,24},{24,20},{28,16},{1,13},{... | collective-permute-start | bytes 393224 | tf_op jit(solution)/shard_map/ppermute | solution.py:225
  9.6 7.5 %collective-permute-start.5 = (bf16[2,256,128]{2,1,0:T(8,128)(2,1)S(1)}, bf16[2,256,128]{2,1,0:T(8,128)(2,1)S(1)}, u32[]{:S(2)}, u32[]{:S(2)}) collective-permute-start(bf16[2,256,128]{2,1,0:T(8,128)(2,1)S(1)} %get-tuple-element.28), channel_id=1, source_target_pairs={{0,20},{4,16},{8,28},{12,24},{16,4},{20,0},{24,12},{28,8},{1,21},{... | collective-permute-start | bytes 393224 | tf_op jit(solution)/shard_map/ppermute | solution.py:225
  11.8 5.3 %collective-permute-start.6 = (bf16[2,256,128]{2,1,0:T(8,128)(2,1)S(1)}, bf16[2,256,128]{2,1,0:T(8,128)(2,1)S(1)}, u32[]{:S(2)}, u32[]{:S(2)}) collective-permute-start(bf16[2,256,128]{2,1,0:T(8,128)(2,1)S(1)} %get-tuple-element.29), channel_id=1, source_target_pairs={{0,4},{4,0},{8,12},{12,8},{16,20},{20,16},{24,28},{28,24},{1,5},{5... | collective-permute-start | bytes 393224 | tf_op jit(solution)/shard_map/ppermute | solution.py:225
  20.6 1.7 %collective-permute-start.7 = (s16[4,22,16,128]{3,2,1,0:T(8,128)(2,1)S(1)}, s16[4,22,16,128]{3,2,1,0:T(8,128)(2,1)S(1)}, u32[]{:S(2)}, u32[]{:S(2)}) collective-permute-start(s16[4,22,16,128]{3,2,1,0:T(8,128)(2,1)S(1)} %get-tuple-element.32), channel_id=1, source_target_pairs={{0,4},{4,0},{8,12},{12,8},{16,20},{20,16},{24,28},{28,24},{1,5},{5... | collective-permute-start | bytes 1081352 | tf_op jit(solution)/shard_map/ppermute | solution.py:225
  22.6 6.3 %collective-permute-start.8 = (s16[22,16,128]{2,1,0:T(8,128)(2,1)S(1)}, s16[22,16,128]{2,1,0:T(8,128)(2,1)S(1)}, u32[]{:S(2)}, u32[]{:S(2)}) collective-permute-start(s16[22,16,128]{2,1,0:T(8,128)(2,1)S(1)} %get-tuple-element.33), channel_id=1, source_target_pairs={{0,24},{4,28},{8,16},{12,20},{16,8},{20,12},{24,0},{28,4},{1,25},{... | collective-permute-start | bytes 270344 | tf_op jit(solution)/shard_map/ppermute | solution.py:225
  25.2 5.0 %collective-permute-start.9 = (s16[22,16,128]{2,1,0:T(8,128)(2,1)S(1)}, s16[22,16,128]{2,1,0:T(8,128)(2,1)S(1)}, u32[]{:S(2)}, u32[]{:S(2)}) collective-permute-start(s16[22,16,128]{2,1,0:T(8,128)(2,1)S(1)} %get-tuple-element.34), channel_id=1, source_target_pairs={{0,8},{4,12},{8,0},{12,4},{16,24},{20,28},{24,16},{28,20},{1,9},{5... | collective-permute-start | bytes 270344 | tf_op jit(solution)/shard_map/ppermute | solution.py:225
  25.6 4.7 %collective-permute-start.10 = (s16[22,16,128]{2,1,0:T(8,128)(2,1)S(1)}, s16[22,16,128]{2,1,0:T(8,128)(2,1)S(1)}, u32[]{:S(2)}, u32[]{:S(2)}) collective-permute-start(s16[22,16,128]{2,1,0:T(8,128)(2,1)S(1)} %get-tuple-element.35), channel_id=1, source_target_pairs={{0,16},{4,20},{8,24},{12,28},{16,0},{20,4},{24,8},{28,12},{1,17},{... | collective-permute-start | bytes 270344 | tf_op jit(solution)/shard_map/ppermute | solution.py:225
  30.4 4.8 %collective-permute-start.11 = (s16[7,16,128]{2,1,0:T(8,128)(2,1)S(1)}, s16[7,16,128]{2,1,0:T(8,128)(2,1)S(1)}, u32[]{:S(2)}, u32[]{:S(2)}) collective-permute-start(s16[7,16,128]{2,1,0:T(8,128)(2,1)S(1)} %get-tuple-element.37), channel_id=1, source_target_pairs={{0,2},{1,3},{2,0},{3,1},{4,6},{5,7},{6,4},{7,5},{8,10},{9,11},{10,... | collective-permute-start | bytes 86024 | tf_op jit(solution)/shard_map/ppermute | solution.py:225
  33.2 5.7 %collective-permute-start.12 = (s16[7,16,128]{2,1,0:T(8,128)(2,1)S(1)}, s16[7,16,128]{2,1,0:T(8,128)(2,1)S(1)}, u32[]{:S(2)}, u32[]{:S(2)}) collective-permute-start(s16[7,16,128]{2,1,0:T(8,128)(2,1)S(1)} %get-tuple-element.38), channel_id=1, source_target_pairs={{0,3},{1,2},{2,1},{3,0},{4,7},{5,6},{6,5},{7,4},{8,11},{9,10},{10,... | collective-permute-start | bytes 86024 | tf_op jit(solution)/shard_map/ppermute | solution.py:225
  34.5 4.3 %collective-permute-start.13 = (s16[7,16,128]{2,1,0:T(8,128)(2,1)S(1)}, s16[7,16,128]{2,1,0:T(8,128)(2,1)S(1)}, u32[]{:S(2)}, u32[]{:S(2)}) collective-permute-start(s16[7,16,128]{2,1,0:T(8,128)(2,1)S(1)} %get-tuple-element.39), channel_id=1, source_target_pairs={{0,1},{1,0},{2,3},{3,2},{4,5},{5,4},{6,7},{7,6},{8,9},{9,8},{10,11... | collective-permute-start | bytes 86024 | tf_op jit(solution)/shard_map/ppermute | solution.py:225

commit v15 on v12

--- a/solution.py
+++ b/solution.py
@@ -104,14 +104,19 @@
     for number in range(offset_count):
         turn = chans - offset_of(number, offs_ref, chan_count // 2) * (chans // chan_count)
         slot = number % 2
-        for row in range(0, freqs, step):
-            own = [white_ref[part, row : row + step, :] for part in range(2)]
+
+        def cross(index, carry, slot=slot, turn=turn):
+            rows = pl.ds(pl.multiple_of(index * step, step), step)
+            own = [white_ref[part, rows, :] for part in range(2)]
             far_real, far_imag = (pltpu.roll(value, turn, 1).astype(jnp.float32) for value in own)
             own_real, own_imag = (value.astype(jnp.float32) for value in own)
             real = own_real * far_real + own_imag * far_imag
             imag = own_imag * far_real - own_real * far_imag
-            cross_ref[slot, row : row + step, 0:chans] = real.astype(jnp.bfloat16)
-            cross_ref[slot, row : row + step, chans : 2 * chans] = imag.astype(jnp.bfloat16)
+            cross_ref[slot, rows, 0:chans] = real.astype(jnp.bfloat16)
+            cross_ref[slot, rows, chans : 2 * chans] = imag.astype(jnp.bfloat16)
+            return carry
+
+        lax.fori_loop(0, freqs // step, cross, 0, unroll=4)
         sums = jnp.dot(table, cross_ref[slot], preferred_element_type=jnp.float32)
         cos_real, sin_real = sums[:half, :chans], sums[half:, :chans]
         cos_imag, sin_imag = sums[:half, chans:], sums[half:, chans:]

time: 51.4 us -> 55.9 us (1.088)
  Pallas kernels: 7.22 us -> 11.7 us
    pallas_call x1, Pallas kernels: 3.43 us -> 7.94 us  [window_shards(): pl.pallas_call(functools.partial(window_kernel, chan_order), out_shape=[j...]
where the time goes in v15:
time: 55.9 us; the launch traced here: 55.8 us
  waiting for transfers between devices  16.7 us (30%)
  starting transfers between devices  15.8 us (28%)
  Pallas kernels  11.7 us (21%)
  blocking collectives  11.4 us (20%)
    ppermute x14, waiting for transfers between devices, exchange(): lax.ppermute(piece, axis, [(source, source ^ k) for source in range(count)])  16.7 us
    ppermute x14, starting transfers between devices, exchange(): lax.ppermute(piece, axis, [(source, source ^ k) for source in range(count)])  15.8 us
    all_to_all x1, blocking collectives, window_shards(): lax.all_to_all(pieces.reshape(shape), ('chan', 'tm'), 0, 0, tiled=True)  11.4 us
    pallas_call x1, Pallas kernels, window_shards(): pl.pallas_call(functools.partial(window_kernel, chan_order), out_shape=[j...  7.94 us
    pallas_call x2, Pallas kernels, window_shards(): pl.pallas_call(functools.partial(split_kernel, part), out_shape=[jax.Shap...  2.32 us
  transfers between devices with their start and end apart: 14, of which 10 were waited for; matrix products, arithmetic and copies ran while one was open for 0% of the time, Pallas kernels for 2%

profile of v15, /device:TPU:0, one launch (start us, length us, event | category | flops | bytes accessed | tf_op | source)
XLA Modules:
  0.0 55.8 jit_solution(4421500612674509017)
XLA Ops:
  0.0 1.1 %split_windows.2 = (bf16[2,256,128]{2,1,0:T(8,128)(2,1)S(1)}, bf16[2,256,128]{2,1,0:T(8,128)(2,1)S(1)}) custom-call(s32[1]{0:T(128)} %bitcast.1.where_ref, bf16[2,8,256,128]{3,2,1,0:T(8,128)(2,1)} %spec_ref.3), custom_call_target="tpu_custom_call" | custom-call | tf_op jit(solution)/shard_map/split_windows/pallas_call | solution.py:331
  1.1 4.0 %collective-permute-start = (bf16[2,256,128]{2,1,0:T(8,128)(2,1)S(1)}, bf16[2,256,128]{2,1,0:T(8,128)(2,1)S(1)}, u32[]{:S(2)}, u32[]{:S(2)}) collective-permute-start(bf16[2,256,128]{2,1,0:T(8,128)(2,1)S(1)} %get-tuple-element.23), channel_id=1, source_target_pairs={{0,24},{4,28},{8,16},{12,20},{16,8},{20,12},{24,0},{28,4},{1,25},{... | collective-permute-start | bytes 393224 | tf_op jit(solution)/shard_map/ppermute | solution.py:231
  5.0 1.3 %split_windows.3 = (bf16[2,256,128]{2,1,0:T(8,128)(2,1)S(1)}, bf16[2,256,128]{2,1,0:T(8,128)(2,1)S(1)}, bf16[2,256,128]{2,1,0:T(8,128)(2,1)S(1)}, bf16[2,256,128...) custom-call(s32[1]{0:T(128)} %bitcast.1.where_ref, ...), custom_call_target="tpu_custom_call" | custom-call | tf_op jit(solution)/shard_map/split_windows/pallas_call | solution.py:331
  6.3 1.2 %collective-permute-start.2 = (bf16[2,256,128]{2,1,0:T(8,128)(2,1)S(1)}, bf16[2,256,128]{2,1,0:T(8,128)(2,1)S(1)}, u32[]{:S(2)}, u32[]{:S(2)}) collective-permute-start(bf16[2,256,128]{2,1,0:T(8,128)(2,1)S(1)} %get-tuple-element.25), channel_id=1, source_target_pairs={{0,8},{4,12},{8,0},{12,4},{16,24},{20,28},{24,16},{28,20},{1,9},{5... | collective-permute-start | bytes 393224 | tf_op jit(solution)/shard_map/ppermute | solution.py:231
  7.5 1.5 %collective-permute-start.3 = (bf16[2,256,128]{2,1,0:T(8,128)(2,1)S(1)}, bf16[2,256,128]{2,1,0:T(8,128)(2,1)S(1)}, u32[]{:S(2)}, u32[]{:S(2)}) collective-permute-start(bf16[2,256,128]{2,1,0:T(8,128)(2,1)S(1)} %get-tuple-element.26), channel_id=1, source_target_pairs={{0,16},{4,20},{8,24},{12,28},{16,0},{20,4},{24,8},{28,12},{1,17},{... | collective-permute-start | bytes 393224 | tf_op jit(solution)/shard_map/ppermute | solution.py:231
  9.0 0.6 %collective-permute-start.4 = (bf16[2,256,128]{2,1,0:T(8,128)(2,1)S(1)}, bf16[2,256,128]{2,1,0:T(8,128)(2,1)S(1)}, u32[]{:S(2)}, u32[]{:S(2)}) collective-permute-start(bf16[2,256,128]{2,1,0:T(8,128)(2,1)S(1)} %get-tuple-element.27), channel_id=1, source_target_pairs={{0,12},{4,8},{8,4},{12,0},{16,28},{20,24},{24,20},{28,16},{1,13},{... | collective-permute-start | bytes 393224 | tf_op jit(solution)/shard_map/ppermute | solution.py:231
  9.6 0.6 %collective-permute-start.5 = (bf16[2,256,128]{2,1,0:T(8,128)(2,1)S(1)}, bf16[2,256,128]{2,1,0:T(8,128)(2,1)S(1)}, u32[]{:S(2)}, u32[]{:S(2)}) collective-permute-start(bf16[2,256,128]{2,1,0:T(8,128)(2,1)S(1)} %get-tuple-element.28), channel_id=1, source_target_pairs={{0,20},{4,16},{8,28},{12,24},{16,4},{20,0},{24,12},{28,8},{1,21},{... | collective-permute-start | bytes 393224 | tf_op jit(solution)/shard_map/ppermute | solution.py:231
  10.2 1.6 %collective-permute-done.1.refs_1_ = bf16[2,256,128]{2,1,0:T(8,128)(2,1)S(1)} collective-permute-done((bf16[2,256,128]{2,1,0:T(8,128)(2,1)S(1)}, bf16[2,256,128]{2,1,0:T(8,128)(2,1)S(1)}, u32[]{:S(2)}, u32[]{:S(2)}) %collective-permute-start.1) | collective-permute-done | bytes 131104 | tf_op jit(solution)/shard_map/ppermute | solution.py:231
  11.8 3.5 %collective-permute-done.2.refs_2_ = bf16[2,256,128]{2,1,0:T(8,128)(2,1)S(1)} collective-permute-done((bf16[2,256,128]{2,1,0:T(8,128)(2,1)S(1)}, bf16[2,256,128]{2,1,0:T(8,128)(2,1)S(1)}, u32[]{:S(2)}, u32[]{:S(2)}) %collective-permute-start.2) | collective-permute-done | bytes 131104 | tf_op jit(solution)/shard_map/ppermute | solution.py:231
  15.2 1.1 %collective-permute-done.4.refs_4_ = bf16[2,256,128]{2,1,0:T(8,128)(2,1)S(1)} collective-permute-done((bf16[2,256,128]{2,1,0:T(8,128)(2,1)S(1)}, bf16[2,256,128]{2,1,0:T(8,128)(2,1)S(1)}, u32[]{:S(2)}, u32[]{:S(2)}) %collective-permute-start.4) | collective-permute-done | bytes 131104 | tf_op jit(solution)/shard_map/ppermute | solution.py:231
  16.4 0.7 %collective-permute-done.5.refs_5_ = bf16[2,256,128]{2,1,0:T(8,128)(2,1)S(1)} collective-permute-done((bf16[2,256,128]{2,1,0:T(8,128)(2,1)S(1)}, bf16[2,256,128]{2,1,0:T(8,128)(2,1)S(1)}, u32[]{:S(2)}, u32[]{:S(2)}) %collective-permute-start.5) | collective-permute-done | bytes 131104 | tf_op jit(solution)/shard_map/ppermute | solution.py:231
  17.1 7.9 %window_pairs.1 = (s16[4,22,16,128]{3,2,1,0:T(8,128)(2,1)S(1)}, s16[4,22,16,128]{3,2,1,0:T(8,128)(2,1)S(1)}) custom-call(s32[4]{0:T(128)} %offs_hbm_ref.1, s32[1]{0:T(128)} %bitcast.1.where_ref, bf16[2,256,128]{2,1,0:T(8,128)(2,1)S(1)} %collective-permute-done.refs_0_, bf16[2,256,128]{2,1,0:T(8,128)(2,1)S(1)} %collective-permute-done.1.refs_1_, ...), custom_call_target="tpu_custom_call" | custom-call | tf_op jit(solution)/shard_map/window_pairs/pallas_call | solution.py:342
  25.2 1.5 %collective-permute-done.7.far_ref = s16[4,22,16,128]{3,2,1,0:T(8,128)(2,1)S(1)} collective-permute-done((s16[4,22,16,128]{3,2,1,0:T(8,128)(2,1)S(1)}, s16[4,22,16,128]{3,2,1,0:T(8,128)(2,1)S(1)}, u32[]{:S(2)}, u32[]{:S(2)}) %collective-permute-start.7) | collective-permute-done | bytes 360480 | tf_op jit(solution)/shard_map/ppermute | solution.py:231
  27.0 2.6 %collective-permute-start.8 = (s16[22,16,128]{2,1,0:T(8,128)(2,1)S(1)}, s16[22,16,128]{2,1,0:T(8,128)(2,1)S(1)}, u32[]{:S(2)}, u32[]{:S(2)}) collective-permute-start(s16[22,16,128]{2,1,0:T(8,128)(2,1)S(1)} %get-tuple-element.33), channel_id=1, source_target_pairs={{0,24},{4,28},{8,16},{12,20},{16,8},{20,12},{24,0},{28,4},{1,25},{... | collective-permute-start | bytes 270344 | tf_op jit(solution)/shard_map/ppermute | solution.py:231
  29.6 0.4 collective-permute-start.9
  30.0 0.5 collective-permute-start.10
  30.5 2.8 %collective-permute-done.8.refs_0_ = s16[22,16,128]{2,1,0:T(8,128)(2,1)S(1)} collective-permute-done((s16[22,16,128]{2,1,0:T(8,128)(2,1)S(1)}, s16[22,16,128]{2,1,0:T(8,128)(2,1)S(1)}, u32[]{:S(2)}, u32[]{:S(2)}) %collective-permute-start.8) | collective-permute-done | bytes 90144 | tf_op jit(solution)/shard_map/ppermute | solution.py:231
  33.3 1.3 %collective-permute-done.9.refs_1_ = s16[22,16,128]{2,1,0:T(8,128)(2,1)S(1)} collective-permute-done((s16[22,16,128]{2,1,0:T(8,128)(2,1)S(1)}, s16[22,16,128]{2,1,0:T(8,128)(2,1)S(1)}, u32[]{:S(2)}, u32[]{:S(2)}) %collective-permute-start.9) | collective-permute-done | bytes 90144 | tf_op jit(solution)/shard_map/ppermute | solution.py:231
  34.8 2.7 %collective-permute-start.11 = (s16[7,16,128]{2,1,0:T(8,128)(2,1)S(1)}, s16[7,16,128]{2,1,0:T(8,128)(2,1)S(1)}, u32[]{:S(2)}, u32[]{:S(2)}) collective-permute-start(s16[7,16,128]{2,1,0:T(8,128)(2,1)S(1)} %get-tuple-element.37), channel_id=1, source_target_pairs={{0,2},{1,3},{2,0},{3,1},{4,6},{5,7},{6,4},{7,5},{8,10},{9,11},{10,... | collective-permute-start | bytes 86024 | tf_op jit(solution)/shard_map/ppermute | solution.py:231
  37.5 1.3 %collective-permute-start.12 = (s16[7,16,128]{2,1,0:T(8,128)(2,1)S(1)}, s16[7,16,128]{2,1,0:T(8,128)(2,1)S(1)}, u32[]{:S(2)}, u32[]{:S(2)}) collective-permute-start(s16[7,16,128]{2,1,0:T(8,128)(2,1)S(1)} %get-tuple-element.38), channel_id=1, source_target_pairs={{0,3},{1,2},{2,1},{3,0},{4,7},{5,6},{6,5},{7,4},{8,11},{9,10},{10,... | collective-permute-start | bytes 86024 | tf_op jit(solution)/shard_map/ppermute | solution.py:231
  39.1 0.5 collective-permute-done.11.refs_0_
  39.7 3.5 %collective-permute-done.12.refs_1_ = s16[7,16,128]{2,1,0:T(8,128)(2,1)S(1)} collective-permute-done((s16[7,16,128]{2,1,0:T(8,128)(2,1)S(1)}, s16[7,16,128]{2,1,0:T(8,128)(2,1)S(1)}, u32[]{:S(2)}, u32[]{:S(2)}) %collective-permute-start.12) | collective-permute-done | bytes 28704 | tf_op jit(solution)/shard_map/ppermute | solution.py:231
  43.4 11.4 %all_to_all.5 = f32[32,4,128]{2,1,0:T(4,128)S(1)} all-to-all(f32[32,4,128]{2,1,0:T(4,128)S(1)} %bitcast.5), channel_id=1, replica_groups=mesh['chan'=8,'tm'=4] {'chan','tm'}, dimensions={0} | all-to-all | bytes 131072 | tf_op jit(solution)/shard_map/all_to_all | solution.py:383
  54.9 0.9 %place_lags.1 = f32[16,4,256]{2,1,0:T(4,128)} custom-call(f32[8,4,4,128]{3,2,1,0:T(4,128)S(1)} %bitcast.4), custom_call_target="tpu_custom_call" | custom-call | tf_op jit(solution)/shard_map/place_lags/pallas_call | solution.py:384
  (16 shorter events, 1.1 us)
Async XLA Ops:
  0.0 17.1 %copy-start = (bf16[2,8,16,2048]{3,2,1,0:T(8,128)(2,1)S(1)}, bf16[2,8,16,2048]{3,2,1,0:T(8,128)(2,1)}, u32[]{:S(2)}) copy-start(bf16[2,8,16,2048]{3,2,1,0:T(8,128)(2,1)} %constant.11.clone.refs_9_) | copy-start | bytes 3145732
  1.1 8.5 %collective-permute-start = (bf16[2,256,128]{2,1,0:T(8,128)(2,1)S(1)}, bf16[2,256,128]{2,1,0:T(8,128)(2,1)S(1)}, u32[]{:S(2)}, u32[]{:S(2)}) collective-permute-start(bf16[2,256,128]{2,1,0:T(8,128)(2,1)S(1)} %get-tuple-element.23), channel_id=1, source_target_pairs={{0,24},{4,28},{8,16},{12,20},{16,8},{20,12},{24,0},{28,4},{1,25},{... | collective-permute-start | bytes 393224 | tf_op jit(solution)/shard_map/ppermute | solution.py:231
  5.0 6.7 %collective-permute-start.1 = (bf16[2,256,128]{2,1,0:T(8,128)(2,1)S(1)}, bf16[2,256,128]{2,1,0:T(8,128)(2,1)S(1)}, u32[]{:S(2)}, u32[]{:S(2)}) collective-permute-start(bf16[2,256,128]{2,1,0:T(8,128)(2,1)S(1)} %get-tuple-element.24), channel_id=1, source_target_pairs={{0,28},{4,24},{8,20},{12,16},{16,12},{20,8},{24,4},{28,0},{1,29},{... | collective-permute-start | bytes 393224 | tf_op jit(solution)/shard_map/ppermute | solution.py:231
  6.3 8.9 %collective-permute-start.2 = (bf16[2,256,128]{2,1,0:T(8,128)(2,1)S(1)}, bf16[2,256,128]{2,1,0:T(8,128)(2,1)S(1)}, u32[]{:S(2)}, u32[]{:S(2)}) collective-permute-start(bf16[2,256,128]{2,1,0:T(8,128)(2,1)S(1)} %get-tuple-element.25), channel_id=1, source_target_pairs={{0,8},{4,12},{8,0},{12,4},{16,24},{20,28},{24,16},{28,20},{1,9},{5... | collective-permute-start | bytes 393224 | tf_op jit(solution)/shard_map/ppermute | solution.py:231
  7.5 9.6 %copy-start.1 = (s32[8,128]{1,0:T(8,128)S(1)}, s32[8,128]{1,0:T(8,128)}, u32[]{:S(2)}) copy-start(s32[8,128]{1,0:T(8,128)} %refs_8_.1) | copy-start | bytes 12292
  7.5 7.7 %collective-permute-start.3 = (bf16[2,256,128]{2,1,0:T(8,128)(2,1)S(1)}, bf16[2,256,128]{2,1,0:T(8,128)(2,1)S(1)}, u32[]{:S(2)}, u32[]{:S(2)}) collective-permute-start(bf16[2,256,128]{2,1,0:T(8,128)(2,1)S(1)} %get-tuple-element.26), channel_id=1, source_target_pairs={{0,16},{4,20},{8,24},{12,28},{16,0},{20,4},{24,8},{28,12},{1,17},{... | collective-permute-start | bytes 393224 | tf_op jit(solution)/shard_map/ppermute | solution.py:231
  9.0 7.4 %collective-permute-start.4 = (bf16[2,256,128]{2,1,0:T(8,128)(2,1)S(1)}, bf16[2,256,128]{2,1,0:T(8,128)(2,1)S(1)}, u32[]{:S(2)}, u32[]{:S(2)}) collective-permute-start(bf16[2,256,128]{2,1,0:T(8,128)(2,1)S(1)} %get-tuple-element.27), channel_id=1, source_target_pairs={{0,12},{4,8},{8,4},{12,0},{16,28},{20,24},{24,20},{28,16},{1,13},{... | collective-permute-start | bytes 393224 | tf_op jit(solution)/shard_map/ppermute | solution.py:231
  9.6 7.5 %collective-permute-start.5 = (bf16[2,256,128]{2,1,0:T(8,128)(2,1)S(1)}, bf16[2,256,128]{2,1,0:T(8,128)(2,1)S(1)}, u32[]{:S(2)}, u32[]{:S(2)}) collective-permute-start(bf16[2,256,128]{2,1,0:T(8,128)(2,1)S(1)} %get-tuple-element.28), channel_id=1, source_target_pairs={{0,20},{4,16},{8,28},{12,24},{16,4},{20,0},{24,12},{28,8},{1,21},{... | collective-permute-start | bytes 393224 | tf_op jit(solution)/shard_map/ppermute | solution.py:231
  11.8 5.3 %collective-permute-start.6 = (bf16[2,256,128]{2,1,0:T(8,128)(2,1)S(1)}, bf16[2,256,128]{2,1,0:T(8,128)(2,1)S(1)}, u32[]{:S(2)}, u32[]{:S(2)}) collective-permute-start(bf16[2,256,128]{2,1,0:T(8,128)(2,1)S(1)} %get-tuple-element.29), channel_id=1, source_target_pairs={{0,4},{4,0},{8,12},{12,8},{16,20},{20,16},{24,28},{28,24},{1,5},{5... | collective-permute-start | bytes 393224 | tf_op jit(solution)/shard_map/ppermute | solution.py:231
  25.0 1.7 %collective-permute-start.7 = (s16[4,22,16,128]{3,2,1,0:T(8,128)(2,1)S(1)}, s16[4,22,16,128]{3,2,1,0:T(8,128)(2,1)S(1)}, u32[]{:S(2)}, u32[]{:S(2)}) collective-permute-start(s16[4,22,16,128]{3,2,1,0:T(8,128)(2,1)S(1)} %get-tuple-element.32), channel_id=1, source_target_pairs={{0,4},{4,0},{8,12},{12,8},{16,20},{20,16},{24,28},{28,24},{1,5},{5... | collective-permute-start | bytes 1081352 | tf_op jit(solution)/shard_map/ppermute | solution.py:231
  27.0 6.3 %collective-permute-start.8 = (s16[22,16,128]{2,1,0:T(8,128)(2,1)S(1)}, s16[22,16,128]{2,1,0:T(8,128)(2,1)S(1)}, u32[]{:S(2)}, u32[]{:S(2)}) collective-permute-start(s16[22,16,128]{2,1,0:T(8,128)(2,1)S(1)} %get-tuple-element.33), channel_id=1, source_target_pairs={{0,24},{4,28},{8,16},{12,20},{16,8},{20,12},{24,0},{28,4},{1,25},{... | collective-permute-start | bytes 270344 | tf_op jit(solution)/shard_map/ppermute | solution.py:231
  29.6 5.0 %collective-permute-start.9 = (s16[22,16,128]{2,1,0:T(8,128)(2,1)S(1)}, s16[22,16,128]{2,1,0:T(8,128)(2,1)S(1)}, u32[]{:S(2)}, u32[]{:S(2)}) collective-permute-start(s16[22,16,128]{2,1,0:T(8,128)(2,1)S(1)} %get-tuple-element.34), channel_id=1, source_target_pairs={{0,8},{4,12},{8,0},{12,4},{16,24},{20,28},{24,16},{28,20},{1,9},{5... | collective-permute-start | bytes 270344 | tf_op jit(solution)/shard_map/ppermute | solution.py:231
  30.0 4.7 %collective-permute-start.10 = (s16[22,16,128]{2,1,0:T(8,128)(2,1)S(1)}, s16[22,16,128]{2,1,0:T(8,128)(2,1)S(1)}, u32[]{:S(2)}, u32[]{:S(2)}) collective-permute-start(s16[22,16,128]{2,1,0:T(8,128)(2,1)S(1)} %get-tuple-element.35), channel_id=1, source_target_pairs={{0,16},{4,20},{8,24},{12,28},{16,0},{20,4},{24,8},{28,12},{1,17},{... | collective-permute-start | bytes 270344 | tf_op jit(solution)/shard_map/ppermute | solution.py:231
  34.8 4.8 %collective-permute-start.11 = (s16[7,16,128]{2,1,0:T(8,128)(2,1)S(1)}, s16[7,16,128]{2,1,0:T(8,128)(2,1)S(1)}, u32[]{:S(2)}, u32[]{:S(2)}) collective-permute-start(s16[7,16,128]{2,1,0:T(8,128)(2,1)S(1)} %get-tuple-element.37), channel_id=1, source_target_pairs={{0,2},{1,3},{2,0},{3,1},{4,6},{5,7},{6,4},{7,5},{8,10},{9,11},{10,... | collective-permute-start | bytes 86024 | tf_op jit(solution)/shard_map/ppermute | solution.py:231
  37.5 5.7 %collective-permute-start.12 = (s16[7,16,128]{2,1,0:T(8,128)(2,1)S(1)}, s16[7,16,128]{2,1,0:T(8,128)(2,1)S(1)}, u32[]{:S(2)}, u32[]{:S(2)}) collective-permute-start(s16[7,16,128]{2,1,0:T(8,128)(2,1)S(1)} %get-tuple-element.38), channel_id=1, source_target_pairs={{0,3},{1,2},{2,1},{3,0},{4,7},{5,6},{6,5},{7,4},{8,11},{9,10},{10,... | collective-permute-start | bytes 86024 | tf_op jit(solution)/shard_map/ppermute | solution.py:231
  38.9 4.3 %collective-permute-start.13 = (s16[7,16,128]{2,1,0:T(8,128)(2,1)S(1)}, s16[7,16,128]{2,1,0:T(8,128)(2,1)S(1)}, u32[]{:S(2)}, u32[]{:S(2)}) collective-permute-start(s16[7,16,128]{2,1,0:T(8,128)(2,1)S(1)} %get-tuple-element.39), channel_id=1, source_target_pairs={{0,1},{1,0},{2,3},{3,2},{4,5},{5,4},{6,7},{7,6},{8,9},{9,8},{10,11... | collective-permute-start | bytes 86024 | tf_op jit(solution)/shard_map/ppermute | solution.py:231

commit v16 on v12

--- a/solution.py
+++ b/solution.py
@@ -73,22 +73,20 @@
     step = 64
 
     total = jnp.zeros((8, chans), jnp.float32)
-    for partner, spec_ref in zip(order, spec_refs):
-        base = (me ^ partner) * band
+    for number, spec_ref in enumerate(spec_refs):
         for row in range(0, band, step):
-            real = spec_ref[0, row : row + step, :].astype(jnp.float32)
-            imag = spec_ref[1, row : row + step, :].astype(jnp.float32)
+            real, imag = (spec_ref[part, row : row + step, :].astype(jnp.float32) for part in range(2))
             square = real * real + imag * imag
             magnitude = square * lax.rsqrt(jnp.maximum(square, 1e-30))
-            mag_ref[pl.ds(pl.multiple_of(base + row, step), step), :] = magnitude
+            held = slice(number * band + row, number * band + row + step)
+            mag_ref[held, :] = magnitude
             total += jnp.sum(magnitude.reshape(step // 8, 8, chans), axis=0)
     level = jnp.sum(total, axis=0, keepdims=True) * (1.0 / freqs)
     floor = 0.5 * (level + 1e-05)
 
-    for partner, spec_ref in zip(order, spec_refs):
-        base = (me ^ partner) * band
+    for number, spec_ref in enumerate(spec_refs):
         for row in range(0, band, step):
-            held = pl.ds(pl.multiple_of(base + row, step), step)
+            held = slice(number * band + row, number * band + row + step)
             factor = pl.reciprocal(mag_ref[held, :] + floor, approx=True)
             for part in range(2):
                 value = spec_ref[part, row : row + step, :].astype(jnp.float32) * factor
@@ -100,7 +98,15 @@
     levels = jnp.zeros((lag_rows, chans), jnp.float32)
     groups = [k ^ core for core in range(2) for k in chips(chan_count)]
     fetch.wait()
-    table = jnp.concatenate([table_ref[side, me ^ k] for side in range(2) for k in groups], axis=0)
+    bands = [pl.ds(pl.multiple_of((me ^ k) * band, band), band) for k in order]
+    table = jnp.concatenate(
+        [
+            jnp.concatenate([table_ref[side, me ^ group, :, taken] for taken in bands], axis=1)
+            for side in range(2)
+            for group in groups
+        ],
+        axis=0,
+    )
     for number in range(offset_count):
         turn = chans - offset_of(number, offs_ref, chan_count // 2) * (chans // chan_count)
         slot = number % 2

time: 51.4 us -> 51.4 us (level)
  no operation moved by 1% of the time
where the time goes in v16:
time: 51.4 us; the launch traced here: 51.2 us
  waiting for transfers between devices  16.7 us (32%)
  starting transfers between devices  15.8 us (31%)
  blocking collectives  11.4 us (22%)
  Pallas kernels  7.21 us (14%)
    ppermute x14, waiting for transfers between devices, exchange(): lax.ppermute(piece, axis, [(source, source ^ k) for source in range(count)])  16.7 us
    ppermute x14, starting transfers between devices, exchange(): lax.ppermute(piece, axis, [(source, source ^ k) for source in range(count)])  15.8 us
    all_to_all x1, blocking collectives, window_shards(): lax.all_to_all(pieces.reshape(shape), ('chan', 'tm'), 0, 0, tiled=True)  11.4 us
    pallas_call x1, Pallas kernels, window_shards(): pl.pallas_call(functools.partial(window_kernel, chan_order), out_shape=[j...  3.42 us
    pallas_call x2, Pallas kernels, window_shards(): pl.pallas_call(functools.partial(split_kernel, part), out_shape=[jax.Shap...  2.32 us
  transfers between devices with their start and end apart: 14, of which 10 were waited for; matrix products, arithmetic and copies ran while one was open for 0% of the time, Pallas kernels for 2%

profile of v16, /device:TPU:0, one launch (start us, length us, event | category | flops | bytes accessed | tf_op | source)
XLA Modules:
  0.0 51.2 jit_solution(11456638960713088520)
XLA Ops:
  0.0 1.1 %split_windows.2 = (bf16[2,256,128]{2,1,0:T(8,128)(2,1)S(1)}, bf16[2,256,128]{2,1,0:T(8,128)(2,1)S(1)}) custom-call(s32[1]{0:T(128)} %bitcast.1.where_ref, bf16[2,8,256,128]{3,2,1,0:T(8,128)(2,1)} %spec_ref.3), custom_call_target="tpu_custom_call" | custom-call | tf_op jit(solution)/shard_map/split_windows/pallas_call | solution.py:332
  1.1 4.0 %collective-permute-start = (bf16[2,256,128]{2,1,0:T(8,128)(2,1)S(1)}, bf16[2,256,128]{2,1,0:T(8,128)(2,1)S(1)}, u32[]{:S(2)}, u32[]{:S(2)}) collective-permute-start(bf16[2,256,128]{2,1,0:T(8,128)(2,1)S(1)} %get-tuple-element.23), channel_id=1, source_target_pairs={{0,24},{4,28},{8,16},{12,20},{16,8},{20,12},{24,0},{28,4},{1,25},{... | collective-permute-start | bytes 393224 | tf_op jit(solution)/shard_map/ppermute | solution.py:232
  5.0 1.3 %split_windows.3 = (bf16[2,256,128]{2,1,0:T(8,128)(2,1)S(1)}, bf16[2,256,128]{2,1,0:T(8,128)(2,1)S(1)}, bf16[2,256,128]{2,1,0:T(8,128)(2,1)S(1)}, bf16[2,256,128...) custom-call(s32[1]{0:T(128)} %bitcast.1.where_ref, ...), custom_call_target="tpu_custom_call" | custom-call | tf_op jit(solution)/shard_map/split_windows/pallas_call | solution.py:332
  6.3 1.2 %collective-permute-start.2 = (bf16[2,256,128]{2,1,0:T(8,128)(2,1)S(1)}, bf16[2,256,128]{2,1,0:T(8,128)(2,1)S(1)}, u32[]{:S(2)}, u32[]{:S(2)}) collective-permute-start(bf16[2,256,128]{2,1,0:T(8,128)(2,1)S(1)} %get-tuple-element.25), channel_id=1, source_target_pairs={{0,8},{4,12},{8,0},{12,4},{16,24},{20,28},{24,16},{28,20},{1,9},{5... | collective-permute-start | bytes 393224 | tf_op jit(solution)/shard_map/ppermute | solution.py:232
  7.5 1.5 %collective-permute-start.3 = (bf16[2,256,128]{2,1,0:T(8,128)(2,1)S(1)}, bf16[2,256,128]{2,1,0:T(8,128)(2,1)S(1)}, u32[]{:S(2)}, u32[]{:S(2)}) collective-permute-start(bf16[2,256,128]{2,1,0:T(8,128)(2,1)S(1)} %get-tuple-element.26), channel_id=1, source_target_pairs={{0,16},{4,20},{8,24},{12,28},{16,0},{20,4},{24,8},{28,12},{1,17},{... | collective-permute-start | bytes 393224 | tf_op jit(solution)/shard_map/ppermute | solution.py:232
  9.0 0.6 %collective-permute-start.4 = (bf16[2,256,128]{2,1,0:T(8,128)(2,1)S(1)}, bf16[2,256,128]{2,1,0:T(8,128)(2,1)S(1)}, u32[]{:S(2)}, u32[]{:S(2)}) collective-permute-start(bf16[2,256,128]{2,1,0:T(8,128)(2,1)S(1)} %get-tuple-element.27), channel_id=1, source_target_pairs={{0,12},{4,8},{8,4},{12,0},{16,28},{20,24},{24,20},{28,16},{1,13},{... | collective-permute-start | bytes 393224 | tf_op jit(solution)/shard_map/ppermute | solution.py:232
  9.6 0.6 %collective-permute-start.5 = (bf16[2,256,128]{2,1,0:T(8,128)(2,1)S(1)}, bf16[2,256,128]{2,1,0:T(8,128)(2,1)S(1)}, u32[]{:S(2)}, u32[]{:S(2)}) collective-permute-start(bf16[2,256,128]{2,1,0:T(8,128)(2,1)S(1)} %get-tuple-element.28), channel_id=1, source_target_pairs={{0,20},{4,16},{8,28},{12,24},{16,4},{20,0},{24,12},{28,8},{1,21},{... | collective-permute-start | bytes 393224 | tf_op jit(solution)/shard_map/ppermute | solution.py:232
  10.2 1.6 %collective-permute-done.1.refs_1_ = bf16[2,256,128]{2,1,0:T(8,128)(2,1)S(1)} collective-permute-done((bf16[2,256,128]{2,1,0:T(8,128)(2,1)S(1)}, bf16[2,256,128]{2,1,0:T(8,128)(2,1)S(1)}, u32[]{:S(2)}, u32[]{:S(2)}) %collective-permute-start.1) | collective-permute-done | bytes 131104 | tf_op jit(solution)/shard_map/ppermute | solution.py:232
  11.8 3.5 %collective-permute-done.2.refs_2_ = bf16[2,256,128]{2,1,0:T(8,128)(2,1)S(1)} collective-permute-done((bf16[2,256,128]{2,1,0:T(8,128)(2,1)S(1)}, bf16[2,256,128]{2,1,0:T(8,128)(2,1)S(1)}, u32[]{:S(2)}, u32[]{:S(2)}) %collective-permute-start.2) | collective-permute-done | bytes 131104 | tf_op jit(solution)/shard_map/ppermute | solution.py:232
  15.2 1.1 %collective-permute-done.4.refs_4_ = bf16[2,256,128]{2,1,0:T(8,128)(2,1)S(1)} collective-permute-done((bf16[2,256,128]{2,1,0:T(8,128)(2,1)S(1)}, bf16[2,256,128]{2,1,0:T(8,128)(2,1)S(1)}, u32[]{:S(2)}, u32[]{:S(2)}) %collective-permute-start.4) | collective-permute-done | bytes 131104 | tf_op jit(solution)/shard_map/ppermute | solution.py:232
  16.4 0.7 %collective-permute-done.5.refs_5_ = bf16[2,256,128]{2,1,0:T(8,128)(2,1)S(1)} collective-permute-done((bf16[2,256,128]{2,1,0:T(8,128)(2,1)S(1)}, bf16[2,256,128]{2,1,0:T(8,128)(2,1)S(1)}, u32[]{:S(2)}, u32[]{:S(2)}) %collective-permute-start.5) | collective-permute-done | bytes 131104 | tf_op jit(solution)/shard_map/ppermute | solution.py:232
  17.1 3.4 %window_pairs.1 = (s16[4,22,16,128]{3,2,1,0:T(8,128)(2,1)S(1)}, s16[4,22,16,128]{3,2,1,0:T(8,128)(2,1)S(1)}) custom-call(s32[4]{0:T(128)} %offs_hbm_ref.1, s32[1]{0:T(128)} %bitcast.1.where_ref, bf16[2,256,128]{2,1,0:T(8,128)(2,1)S(1)} %collective-permute-done.refs_0_, bf16[2,256,128]{2,1,0:T(8,128)(2,1)S(1)} %collective-permute-done.1.refs_1_, ...), custom_call_target="tpu_custom_call" | custom-call | tf_op jit(solution)/shard_map/window_pairs/pallas_call | solution.py:343
  20.7 1.5 %collective-permute-done.7.far_ref = s16[4,22,16,128]{3,2,1,0:T(8,128)(2,1)S(1)} collective-permute-done((s16[4,22,16,128]{3,2,1,0:T(8,128)(2,1)S(1)}, s16[4,22,16,128]{3,2,1,0:T(8,128)(2,1)S(1)}, u32[]{:S(2)}, u32[]{:S(2)}) %collective-permute-start.7) | collective-permute-done | bytes 360480 | tf_op jit(solution)/shard_map/ppermute | solution.py:232
  22.5 2.6 %collective-permute-start.8 = (s16[22,16,128]{2,1,0:T(8,128)(2,1)S(1)}, s16[22,16,128]{2,1,0:T(8,128)(2,1)S(1)}, u32[]{:S(2)}, u32[]{:S(2)}) collective-permute-start(s16[22,16,128]{2,1,0:T(8,128)(2,1)S(1)} %get-tuple-element.33), channel_id=1, source_target_pairs={{0,24},{4,28},{8,16},{12,20},{16,8},{20,12},{24,0},{28,4},{1,25},{... | collective-permute-start | bytes 270344 | tf_op jit(solution)/shard_map/ppermute | solution.py:232
  25.0 0.4 collective-permute-start.9
  25.5 0.5 %collective-permute-start.10 = (s16[22,16,128]{2,1,0:T(8,128)(2,1)S(1)}, s16[22,16,128]{2,1,0:T(8,128)(2,1)S(1)}, u32[]{:S(2)}, u32[]{:S(2)}) collective-permute-start(s16[22,16,128]{2,1,0:T(8,128)(2,1)S(1)} %get-tuple-element.35), channel_id=1, source_target_pairs={{0,16},{4,20},{8,24},{12,28},{16,0},{20,4},{24,8},{28,12},{1,17},{... | collective-permute-start | bytes 270344 | tf_op jit(solution)/shard_map/ppermute | solution.py:232
  26.0 2.8 %collective-permute-done.8.refs_0_ = s16[22,16,128]{2,1,0:T(8,128)(2,1)S(1)} collective-permute-done((s16[22,16,128]{2,1,0:T(8,128)(2,1)S(1)}, s16[22,16,128]{2,1,0:T(8,128)(2,1)S(1)}, u32[]{:S(2)}, u32[]{:S(2)}) %collective-permute-start.8) | collective-permute-done | bytes 90144 | tf_op jit(solution)/shard_map/ppermute | solution.py:232
  28.8 1.3 %collective-permute-done.9.refs_1_ = s16[22,16,128]{2,1,0:T(8,128)(2,1)S(1)} collective-permute-done((s16[22,16,128]{2,1,0:T(8,128)(2,1)S(1)}, s16[22,16,128]{2,1,0:T(8,128)(2,1)S(1)}, u32[]{:S(2)}, u32[]{:S(2)}) %collective-permute-start.9) | collective-permute-done | bytes 90144 | tf_op jit(solution)/shard_map/ppermute | solution.py:232
  30.3 2.7 %collective-permute-start.11 = (s16[7,16,128]{2,1,0:T(8,128)(2,1)S(1)}, s16[7,16,128]{2,1,0:T(8,128)(2,1)S(1)}, u32[]{:S(2)}, u32[]{:S(2)}) collective-permute-start(s16[7,16,128]{2,1,0:T(8,128)(2,1)S(1)} %get-tuple-element.37), channel_id=1, source_target_pairs={{0,2},{1,3},{2,0},{3,1},{4,6},{5,7},{6,4},{7,5},{8,10},{9,11},{10,... | collective-permute-start | bytes 86024 | tf_op jit(solution)/shard_map/ppermute | solution.py:232
  33.0 1.3 %collective-permute-start.12 = (s16[7,16,128]{2,1,0:T(8,128)(2,1)S(1)}, s16[7,16,128]{2,1,0:T(8,128)(2,1)S(1)}, u32[]{:S(2)}, u32[]{:S(2)}) collective-permute-start(s16[7,16,128]{2,1,0:T(8,128)(2,1)S(1)} %get-tuple-element.38), channel_id=1, source_target_pairs={{0,3},{1,2},{2,1},{3,0},{4,7},{5,6},{6,5},{7,4},{8,11},{9,10},{10,... | collective-permute-start | bytes 86024 | tf_op jit(solution)/shard_map/ppermute | solution.py:232
  34.6 0.5 %collective-permute-done.11.refs_0_ = s16[7,16,128]{2,1,0:T(8,128)(2,1)S(1)} collective-permute-done((s16[7,16,128]{2,1,0:T(8,128)(2,1)S(1)}, s16[7,16,128]{2,1,0:T(8,128)(2,1)S(1)}, u32[]{:S(2)}, u32[]{:S(2)}) %collective-permute-start.11) | collective-permute-done | bytes 28704 | tf_op jit(solution)/shard_map/ppermute | solution.py:232
  35.1 3.5 %collective-permute-done.12.refs_1_ = s16[7,16,128]{2,1,0:T(8,128)(2,1)S(1)} collective-permute-done((s16[7,16,128]{2,1,0:T(8,128)(2,1)S(1)}, s16[7,16,128]{2,1,0:T(8,128)(2,1)S(1)}, u32[]{:S(2)}, u32[]{:S(2)}) %collective-permute-start.12) | collective-permute-done | bytes 28704 | tf_op jit(solution)/shard_map/ppermute | solution.py:232
  38.9 11.4 %all_to_all.5 = f32[32,4,128]{2,1,0:T(4,128)S(1)} all-to-all(f32[32,4,128]{2,1,0:T(4,128)S(1)} %bitcast.5), channel_id=1, replica_groups=mesh['chan'=8,'tm'=4] {'chan','tm'}, dimensions={0} | all-to-all | bytes 131072 | tf_op jit(solution)/shard_map/all_to_all | solution.py:384
  50.3 0.9 %place_lags.1 = f32[16,4,256]{2,1,0:T(4,128)} custom-call(f32[8,4,4,128]{3,2,1,0:T(4,128)S(1)} %bitcast.4), custom_call_target="tpu_custom_call" | custom-call | tf_op jit(solution)/shard_map/place_lags/pallas_call | solution.py:385
  (16 shorter events, 1.1 us)
Async XLA Ops:
  0.0 17.1 %copy-start = (bf16[2,8,16,2048]{3,2,1,0:T(8,128)(2,1)S(1)}, bf16[2,8,16,2048]{3,2,1,0:T(8,128)(2,1)}, u32[]{:S(2)}) copy-start(bf16[2,8,16,2048]{3,2,1,0:T(8,128)(2,1)} %constant.11.clone.refs_9_) | copy-start | bytes 3145732
  1.1 8.5 %collective-permute-start = (bf16[2,256,128]{2,1,0:T(8,128)(2,1)S(1)}, bf16[2,256,128]{2,1,0:T(8,128)(2,1)S(1)}, u32[]{:S(2)}, u32[]{:S(2)}) collective-permute-start(bf16[2,256,128]{2,1,0:T(8,128)(2,1)S(1)} %get-tuple-element.23), channel_id=1, source_target_pairs={{0,24},{4,28},{8,16},{12,20},{16,8},{20,12},{24,0},{28,4},{1,25},{... | collective-permute-start | bytes 393224 | tf_op jit(solution)/shard_map/ppermute | solution.py:232
  5.0 6.7 %collective-permute-start.1 = (bf16[2,256,128]{2,1,0:T(8,128)(2,1)S(1)}, bf16[2,256,128]{2,1,0:T(8,128)(2,1)S(1)}, u32[]{:S(2)}, u32[]{:S(2)}) collective-permute-start(bf16[2,256,128]{2,1,0:T(8,128)(2,1)S(1)} %get-tuple-element.24), channel_id=1, source_target_pairs={{0,28},{4,24},{8,20},{12,16},{16,12},{20,8},{24,4},{28,0},{1,29},{... | collective-permute-start | bytes 393224 | tf_op jit(solution)/shard_map/ppermute | solution.py:232
  6.3 8.9 %collective-permute-start.2 = (bf16[2,256,128]{2,1,0:T(8,128)(2,1)S(1)}, bf16[2,256,128]{2,1,0:T(8,128)(2,1)S(1)}, u32[]{:S(2)}, u32[]{:S(2)}) collective-permute-start(bf16[2,256,128]{2,1,0:T(8,128)(2,1)S(1)} %get-tuple-element.25), channel_id=1, source_target_pairs={{0,8},{4,12},{8,0},{12,4},{16,24},{20,28},{24,16},{28,20},{1,9},{5... | collective-permute-start | bytes 393224 | tf_op jit(solution)/shard_map/ppermute | solution.py:232
  7.5 9.6 %copy-start.1 = (s32[8,128]{1,0:T(8,128)S(1)}, s32[8,128]{1,0:T(8,128)}, u32[]{:S(2)}) copy-start(s32[8,128]{1,0:T(8,128)} %refs_8_.1) | copy-start | bytes 12292
  7.5 7.7 %collective-permute-start.3 = (bf16[2,256,128]{2,1,0:T(8,128)(2,1)S(1)}, bf16[2,256,128]{2,1,0:T(8,128)(2,1)S(1)}, u32[]{:S(2)}, u32[]{:S(2)}) collective-permute-start(bf16[2,256,128]{2,1,0:T(8,128)(2,1)S(1)} %get-tuple-element.26), channel_id=1, source_target_pairs={{0,16},{4,20},{8,24},{12,28},{16,0},{20,4},{24,8},{28,12},{1,17},{... | collective-permute-start | bytes 393224 | tf_op jit(solution)/shard_map/ppermute | solution.py:232
  9.0 7.4 %collective-permute-start.4 = (bf16[2,256,128]{2,1,0:T(8,128)(2,1)S(1)}, bf16[2,256,128]{2,1,0:T(8,128)(2,1)S(1)}, u32[]{:S(2)}, u32[]{:S(2)}) collective-permute-start(bf16[2,256,128]{2,1,0:T(8,128)(2,1)S(1)} %get-tuple-element.27), channel_id=1, source_target_pairs={{0,12},{4,8},{8,4},{12,0},{16,28},{20,24},{24,20},{28,16},{1,13},{... | collective-permute-start | bytes 393224 | tf_op jit(solution)/shard_map/ppermute | solution.py:232
  9.6 7.5 %collective-permute-start.5 = (bf16[2,256,128]{2,1,0:T(8,128)(2,1)S(1)}, bf16[2,256,128]{2,1,0:T(8,128)(2,1)S(1)}, u32[]{:S(2)}, u32[]{:S(2)}) collective-permute-start(bf16[2,256,128]{2,1,0:T(8,128)(2,1)S(1)} %get-tuple-element.28), channel_id=1, source_target_pairs={{0,20},{4,16},{8,28},{12,24},{16,4},{20,0},{24,12},{28,8},{1,21},{... | collective-permute-start | bytes 393224 | tf_op jit(solution)/shard_map/ppermute | solution.py:232
  11.8 5.3 %collective-permute-start.6 = (bf16[2,256,128]{2,1,0:T(8,128)(2,1)S(1)}, bf16[2,256,128]{2,1,0:T(8,128)(2,1)S(1)}, u32[]{:S(2)}, u32[]{:S(2)}) collective-permute-start(bf16[2,256,128]{2,1,0:T(8,128)(2,1)S(1)} %get-tuple-element.29), channel_id=1, source_target_pairs={{0,4},{4,0},{8,12},{12,8},{16,20},{20,16},{24,28},{28,24},{1,5},{5... | collective-permute-start | bytes 393224 | tf_op jit(solution)/shard_map/ppermute | solution.py:232
  20.5 1.7 %collective-permute-start.7 = (s16[4,22,16,128]{3,2,1,0:T(8,128)(2,1)S(1)}, s16[4,22,16,128]{3,2,1,0:T(8,128)(2,1)S(1)}, u32[]{:S(2)}, u32[]{:S(2)}) collective-permute-start(s16[4,22,16,128]{3,2,1,0:T(8,128)(2,1)S(1)} %get-tuple-element.32), channel_id=1, source_target_pairs={{0,4},{4,0},{8,12},{12,8},{16,20},{20,16},{24,28},{28,24},{1,5},{5... | collective-permute-start | bytes 1081352 | tf_op jit(solution)/shard_map/ppermute | solution.py:232
  22.5 6.3 %collective-permute-start.8 = (s16[22,16,128]{2,1,0:T(8,128)(2,1)S(1)}, s16[22,16,128]{2,1,0:T(8,128)(2,1)S(1)}, u32[]{:S(2)}, u32[]{:S(2)}) collective-permute-start(s16[22,16,128]{2,1,0:T(8,128)(2,1)S(1)} %get-tuple-element.33), channel_id=1, source_target_pairs={{0,24},{4,28},{8,16},{12,20},{16,8},{20,12},{24,0},{28,4},{1,25},{... | collective-permute-start | bytes 270344 | tf_op jit(solution)/shard_map/ppermute | solution.py:232
  25.0 5.0 %collective-permute-start.9 = (s16[22,16,128]{2,1,0:T(8,128)(2,1)S(1)}, s16[22,16,128]{2,1,0:T(8,128)(2,1)S(1)}, u32[]{:S(2)}, u32[]{:S(2)}) collective-permute-start(s16[22,16,128]{2,1,0:T(8,128)(2,1)S(1)} %get-tuple-element.34), channel_id=1, source_target_pairs={{0,8},{4,12},{8,0},{12,4},{16,24},{20,28},{24,16},{28,20},{1,9},{5... | collective-permute-start | bytes 270344 | tf_op jit(solution)/shard_map/ppermute | solution.py:232
  25.5 4.7 %collective-permute-start.10 = (s16[22,16,128]{2,1,0:T(8,128)(2,1)S(1)}, s16[22,16,128]{2,1,0:T(8,128)(2,1)S(1)}, u32[]{:S(2)}, u32[]{:S(2)}) collective-permute-start(s16[22,16,128]{2,1,0:T(8,128)(2,1)S(1)} %get-tuple-element.35), channel_id=1, source_target_pairs={{0,16},{4,20},{8,24},{12,28},{16,0},{20,4},{24,8},{28,12},{1,17},{... | collective-permute-start | bytes 270344 | tf_op jit(solution)/shard_map/ppermute | solution.py:232
  30.3 4.8 %collective-permute-start.11 = (s16[7,16,128]{2,1,0:T(8,128)(2,1)S(1)}, s16[7,16,128]{2,1,0:T(8,128)(2,1)S(1)}, u32[]{:S(2)}, u32[]{:S(2)}) collective-permute-start(s16[7,16,128]{2,1,0:T(8,128)(2,1)S(1)} %get-tuple-element.37), channel_id=1, source_target_pairs={{0,2},{1,3},{2,0},{3,1},{4,6},{5,7},{6,4},{7,5},{8,10},{9,11},{10,... | collective-permute-start | bytes 86024 | tf_op jit(solution)/shard_map/ppermute | solution.py:232
  33.0 5.7 %collective-permute-start.12 = (s16[7,16,128]{2,1,0:T(8,128)(2,1)S(1)}, s16[7,16,128]{2,1,0:T(8,128)(2,1)S(1)}, u32[]{:S(2)}, u32[]{:S(2)}) collective-permute-start(s16[7,16,128]{2,1,0:T(8,128)(2,1)S(1)} %get-tuple-element.38), channel_id=1, source_target_pairs={{0,3},{1,2},{2,1},{3,0},{4,7},{5,6},{6,5},{7,4},{8,11},{9,10},{10,... | collective-permute-start | bytes 86024 | tf_op jit(solution)/shard_map/ppermute | solution.py:232
  34.4 4.3 %collective-permute-start.13 = (s16[7,16,128]{2,1,0:T(8,128)(2,1)S(1)}, s16[7,16,128]{2,1,0:T(8,128)(2,1)S(1)}, u32[]{:S(2)}, u32[]{:S(2)}) collective-permute-start(s16[7,16,128]{2,1,0:T(8,128)(2,1)S(1)} %get-tuple-element.39), channel_id=1, source_target_pairs={{0,1},{1,0},{2,3},{3,2},{4,5},{5,4},{6,7},{7,6},{8,9},{9,8},{10,11... | collective-permute-start | bytes 86024 | tf_op jit(solution)/shard_map/ppermute | solution.py:232

commit v17 on v16

--- a/solution.py
+++ b/solution.py
@@ -107,18 +107,19 @@
         ],
         axis=0,
     )
-    for number in range(offset_count):
-        turn = chans - offset_of(number, offs_ref, chan_count // 2) * (chans // chan_count)
-        slot = number % 2
-        for row in range(0, freqs, step):
-            own = [white_ref[part, row : row + step, :] for part in range(2)]
+    turns = [chans - offset_of(number, offs_ref, chan_count // 2) * (chans // chan_count) for number in range(offset_count)]
+    for row in range(0, freqs, step):
+        own = [white_ref[part, row : row + step, :] for part in range(2)]
+        own_real, own_imag = (value.astype(jnp.float32) for value in own)
+        for number, turn in enumerate(turns):
             far_real, far_imag = (pltpu.roll(value, turn, 1).astype(jnp.float32) for value in own)
-            own_real, own_imag = (value.astype(jnp.float32) for value in own)
             real = own_real * far_real + own_imag * far_imag
             imag = own_imag * far_real - own_real * far_imag
-            cross_ref[slot, row : row + step, 0:chans] = real.astype(jnp.bfloat16)
-            cross_ref[slot, row : row + step, chans : 2 * chans] = imag.astype(jnp.bfloat16)
-        sums = jnp.dot(table, cross_ref[slot], preferred_element_type=jnp.float32)
+            cross_ref[number, row : row + step, 0:chans] = real.astype(jnp.bfloat16)
+            cross_ref[number, row : row + step, chans : 2 * chans] = imag.astype(jnp.bfloat16)
+
+    for number, turn in enumerate(turns):
+        sums = jnp.dot(table, cross_ref[number], preferred_element_type=jnp.float32)
         cos_real, sin_real = sums[:half, :chans], sums[half:, :chans]
         cos_imag, sin_imag = sums[:half, chans:], sums[half:, chans:]
         corr = (
@@ -326,18 +327,19 @@
 
     chan_order, tm_order = partners(chan_count), partners(tm_count)
     kept = pl.BlockSpec(memory_space=pltpu.HBM)
-    spectra = pltpu.with_memory_space_constraint(spectra, pltpu.HBM)
-    pieces = []
-    for part in (chan_order[:2], chan_order[2:]):
-        pieces += pl.pallas_call(
-            functools.partial(split_kernel, part),
-            out_shape=[jax.ShapeDtypeStruct((2, band, chans), spectra.dtype)] * len(part),
-            in_specs=[smem, kept],
-            out_specs=[pl.BlockSpec(memory_space=pl.ANY)] * len(part),
-            scratch_shapes=[pltpu.SemaphoreType.DMA((len(part),))],
-            compiler_params=params,
-            name="split_windows",
-        )(chan_where, spectra)
+    begun, left = chan_order[:2], chan_order[2:]
+    pieces = [
+        lax.dynamic_index_in_dim(spectra, lax.axis_index("chan").astype(jnp.int32) ^ k, 1, keepdims=False) for k in begun
+    ]
+    pieces += pl.pallas_call(
+        functools.partial(split_kernel, left),
+        out_shape=[jax.ShapeDtypeStruct((2, band, chans), spectra.dtype)] * len(left),
+        in_specs=[smem, kept],
+        out_specs=[pl.BlockSpec(memory_space=pl.ANY)] * len(left),
+        scratch_shapes=[pltpu.SemaphoreType.DMA((len(left),))],
+        compiler_params=params,
+        name="split_windows",
+    )(chan_where, pltpu.with_memory_space_constraint(spectra, pltpu.HBM))
     chip_order = chips(chan_count)
     pair_shape = (6 * offset_count - 2, lag_rows, chans)
     own, far = pl.pallas_call(
@@ -348,7 +350,7 @@
         scratch_shapes=[
             pltpu.VMEM((freqs, chans), jnp.float32),
             pltpu.VMEM((2, freqs, chans), jnp.bfloat16),
-            pltpu.VMEM((2, freqs, 2 * chans), jnp.bfloat16),
+            pltpu.VMEM((offset_count, freqs, 2 * chans), jnp.bfloat16),
             pltpu.SMEM(offsets.shape, jnp.int32),
             pltpu.SemaphoreType.DMA(()),
         ],

time: 51.4 us -> 51.8 us (level)
  Pallas kernels: 7.21 us -> 5.98 us
  local copies, waits for them, and re-layouts: 0.01 us -> 1.08 us
    squeeze x0 -> x1, local copies, waits for them, and re-layouts: none -> 1.08 us  [window_shards(): lax.dynamic_index_in_dim(spectra, lax.axis_index('chan').astype(jnp.int32...]
    pallas_call x2 -> x1, Pallas kernels: 2.32 us -> 1.25 us  [window_shards(): pl.pallas_call(functools.partial(split_kernel, left), out_shape=[jax.Shap...]
  transfers between devices with their start and end apart: 14 -> 14, of which waited for: 10 -> 9; matrix products, arithmetic and copies ran while one was open for 0% -> 0% of each run, Pallas kernels for 2% -> 2%
where the time goes in v17:
time: 51.8 us; the launch traced here: 51.6 us
  waiting for transfers between devices  17 us (33%)
  starting transfers between devices  16.1 us (31%)
  blocking collectives  11.4 us (22%)
  Pallas kernels  5.98 us (12%)
  local copies, waits for them, and re-layouts  1.08 us (2%)
    ppermute x14, waiting for transfers between devices, exchange(): lax.ppermute(piece, axis, [(source, source ^ k) for source in range(count)])  17 us
    ppermute x14, starting transfers between devices, exchange(): lax.ppermute(piece, axis, [(source, source ^ k) for source in range(count)])  16.1 us
    all_to_all x1, blocking collectives, window_shards(): lax.all_to_all(pieces.reshape(shape), ('chan', 'tm'), 0, 0, tiled=True)  11.4 us
    pallas_call x1, Pallas kernels, window_shards(): pl.pallas_call(functools.partial(window_kernel, chan_order), out_shape=[j...  3.26 us
    pallas_call x1, Pallas kernels, window_shards(): pl.pallas_call(functools.partial(split_kernel, left), out_shape=[jax.Shap...  1.25 us
    squeeze x1, local copies, waits for them, and re-layouts, window_shards(): lax.dynamic_index_in_dim(spectra, lax.axis_index('chan').astype(jnp.int32...  1.08 us
  transfers between devices with their start and end apart: 14, of which 9 were waited for; matrix products, arithmetic and copies ran while one was open for 0% of the time, Pallas kernels for 2%

profile of v17, /device:TPU:0, one launch (start us, length us, event | category | flops | bytes accessed | tf_op | source)
XLA Modules:
  0.0 51.6 jit_solution(1043330975115322734)
XLA Ops:
  0.0 1.1 %dynamic-slice_bitcast_fusion = (bf16[2,256,128]{2,1,0:T(8,128)(2,1)S(1)}, bf16[2,256,128]{2,1,0:T(8,128)(2,1)S(1)}) fusion(bf16[2,8,256,128]{3,2,1,0:T(8,128)(2,1)} %spec_ref.1, s32[]{:T(128)S(6)} %select_n.8, s32[]{:T(128)S(6)} %select_n.7), kind=kLoop, calls=%fused_computation | loop fusion | bytes 524296 | tf_op jit(solution)/shard_map/jit(dynamic_index_in_dim)/squeeze | solution.py:332
  1.1 3.4 %collective-permute-start.1 = (bf16[2,256,128]{2,1,0:T(8,128)(2,1)S(1)}, bf16[2,256,128]{2,1,0:T(8,128)(2,1)S(1)}, u32[]{:S(2)}, u32[]{:S(2)}) collective-permute-start(bf16[2,256,128]{2,1,0:T(8,128)(2,1)S(1)} %get-tuple-element.37), channel_id=1, source_target_pairs={{0,28},{4,24},{8,20},{12,16},{16,12},{20,8},{24,4},{28,0},{1,29},{... | collective-permute-start | bytes 393224 | tf_op jit(solution)/shard_map/ppermute | solution.py:233
  4.5 0.6 %collective-permute-start = (bf16[2,256,128]{2,1,0:T(8,128)(2,1)S(1)}, bf16[2,256,128]{2,1,0:T(8,128)(2,1)S(1)}, u32[]{:S(2)}, u32[]{:S(2)}) collective-permute-start(bf16[2,256,128]{2,1,0:T(8,128)(2,1)S(1)} %get-tuple-element.38), channel_id=1, source_target_pairs={{0,24},{4,28},{8,16},{12,20},{16,8},{20,12},{24,0},{28,4},{1,25},{... | collective-permute-start | bytes 393224 | tf_op jit(solution)/shard_map/ppermute | solution.py:233
  5.1 1.3 %split_windows.1 = (bf16[2,256,128]{2,1,0:T(8,128)(2,1)S(1)}, bf16[2,256,128]{2,1,0:T(8,128)(2,1)S(1)}, bf16[2,256,128]{2,1,0:T(8,128)(2,1)S(1)}, bf16[2,256,128...) custom-call(s32[1]{0:T(128)} %bitcast.1.where_ref, ...), custom_call_target="tpu_custom_call" | custom-call | tf_op jit(solution)/shard_map/split_windows/pallas_call | solution.py:334
  6.4 1.4 %collective-permute-start.2 = (bf16[2,256,128]{2,1,0:T(8,128)(2,1)S(1)}, bf16[2,256,128]{2,1,0:T(8,128)(2,1)S(1)}, u32[]{:S(2)}, u32[]{:S(2)}) collective-permute-start(bf16[2,256,128]{2,1,0:T(8,128)(2,1)S(1)} %get-tuple-element.21), channel_id=1, source_target_pairs={{0,8},{4,12},{8,0},{12,4},{16,24},{20,28},{24,16},{28,20},{1,9},{5... | collective-permute-start | bytes 393224 | tf_op jit(solution)/shard_map/ppermute | solution.py:233
  7.8 1.5 %collective-permute-start.3 = (bf16[2,256,128]{2,1,0:T(8,128)(2,1)S(1)}, bf16[2,256,128]{2,1,0:T(8,128)(2,1)S(1)}, u32[]{:S(2)}, u32[]{:S(2)}) collective-permute-start(bf16[2,256,128]{2,1,0:T(8,128)(2,1)S(1)} %get-tuple-element.22), channel_id=1, source_target_pairs={{0,16},{4,20},{8,24},{12,28},{16,0},{20,4},{24,8},{28,12},{1,17},{... | collective-permute-start | bytes 393224 | tf_op jit(solution)/shard_map/ppermute | solution.py:233
  9.3 1.2 %collective-permute-start.5 = (bf16[2,256,128]{2,1,0:T(8,128)(2,1)S(1)}, bf16[2,256,128]{2,1,0:T(8,128)(2,1)S(1)}, u32[]{:S(2)}, u32[]{:S(2)}) collective-permute-start(bf16[2,256,128]{2,1,0:T(8,128)(2,1)S(1)} %get-tuple-element.24), channel_id=1, source_target_pairs={{0,20},{4,16},{8,28},{12,24},{16,4},{20,0},{24,12},{28,8},{1,21},{... | collective-permute-start | bytes 393224 | tf_op jit(solution)/shard_map/ppermute | solution.py:233
  10.5 1.2 %collective-permute-done.refs_0_ = bf16[2,256,128]{2,1,0:T(8,128)(2,1)S(1)} collective-permute-done((bf16[2,256,128]{2,1,0:T(8,128)(2,1)S(1)}, bf16[2,256,128]{2,1,0:T(8,128)(2,1)S(1)}, u32[]{:S(2)}, u32[]{:S(2)}) %collective-permute-start) | collective-permute-done | bytes 131104 | tf_op jit(solution)/shard_map/ppermute | solution.py:233
  11.8 3.2 %collective-permute-done.2.refs_2_ = bf16[2,256,128]{2,1,0:T(8,128)(2,1)S(1)} collective-permute-done((bf16[2,256,128]{2,1,0:T(8,128)(2,1)S(1)}, bf16[2,256,128]{2,1,0:T(8,128)(2,1)S(1)}, u32[]{:S(2)}, u32[]{:S(2)}) %collective-permute-start.2) | collective-permute-done | bytes 131104 | tf_op jit(solution)/shard_map/ppermute | solution.py:233
  15.0 2.8 %collective-permute-done.4.refs_4_ = bf16[2,256,128]{2,1,0:T(8,128)(2,1)S(1)} collective-permute-done((bf16[2,256,128]{2,1,0:T(8,128)(2,1)S(1)}, bf16[2,256,128]{2,1,0:T(8,128)(2,1)S(1)}, u32[]{:S(2)}, u32[]{:S(2)}) %collective-permute-start.4) | collective-permute-done | bytes 131104 | tf_op jit(solution)/shard_map/ppermute | solution.py:233
  17.8 3.3 %window_pairs.1 = (s16[4,22,16,128]{3,2,1,0:T(8,128)(2,1)S(1)}, s16[4,22,16,128]{3,2,1,0:T(8,128)(2,1)S(1)}) custom-call(s32[4]{0:T(128)} %offs_hbm_ref.1, s32[1]{0:T(128)} %bitcast.1.where_ref, bf16[2,256,128]{2,1,0:T(8,128)(2,1)S(1)} %collective-permute-done.refs_0_, bf16[2,256,128]{2,1,0:T(8,128)(2,1)S(1)} %collective-permute-done.1.refs_1_, ...), custom_call_target="tpu_custom_call" | custom-call | tf_op jit(solution)/shard_map/window_pairs/pallas_call | solution.py:345
  21.2 1.6 %collective-permute-done.7.far_ref = s16[4,22,16,128]{3,2,1,0:T(8,128)(2,1)S(1)} collective-permute-done((s16[4,22,16,128]{3,2,1,0:T(8,128)(2,1)S(1)}, s16[4,22,16,128]{3,2,1,0:T(8,128)(2,1)S(1)}, u32[]{:S(2)}, u32[]{:S(2)}) %collective-permute-start.7) | collective-permute-done | bytes 360480 | tf_op jit(solution)/shard_map/ppermute | solution.py:233
  23.0 2.4 %collective-permute-start.8 = (s16[22,16,128]{2,1,0:T(8,128)(2,1)S(1)}, s16[22,16,128]{2,1,0:T(8,128)(2,1)S(1)}, u32[]{:S(2)}, u32[]{:S(2)}) collective-permute-start(s16[22,16,128]{2,1,0:T(8,128)(2,1)S(1)} %get-tuple-element.29), channel_id=1, source_target_pairs={{0,24},{4,28},{8,16},{12,20},{16,8},{20,12},{24,0},{28,4},{1,25},{... | collective-permute-start | bytes 270344 | tf_op jit(solution)/shard_map/ppermute | solution.py:233
  25.4 0.5 %collective-permute-start.9 = (s16[22,16,128]{2,1,0:T(8,128)(2,1)S(1)}, s16[22,16,128]{2,1,0:T(8,128)(2,1)S(1)}, u32[]{:S(2)}, u32[]{:S(2)}) collective-permute-start(s16[22,16,128]{2,1,0:T(8,128)(2,1)S(1)} %get-tuple-element.30), channel_id=1, source_target_pairs={{0,8},{4,12},{8,0},{12,4},{16,24},{20,28},{24,16},{28,20},{1,9},{5... | collective-permute-start | bytes 270344 | tf_op jit(solution)/shard_map/ppermute | solution.py:233
  25.9 0.7 %collective-permute-start.10 = (s16[22,16,128]{2,1,0:T(8,128)(2,1)S(1)}, s16[22,16,128]{2,1,0:T(8,128)(2,1)S(1)}, u32[]{:S(2)}, u32[]{:S(2)}) collective-permute-start(s16[22,16,128]{2,1,0:T(8,128)(2,1)S(1)} %get-tuple-element.31), channel_id=1, source_target_pairs={{0,16},{4,20},{8,24},{12,28},{16,0},{20,4},{24,8},{28,12},{1,17},{... | collective-permute-start | bytes 270344 | tf_op jit(solution)/shard_map/ppermute | solution.py:233
  26.6 2.8 %collective-permute-done.8.refs_0_ = s16[22,16,128]{2,1,0:T(8,128)(2,1)S(1)} collective-permute-done((s16[22,16,128]{2,1,0:T(8,128)(2,1)S(1)}, s16[22,16,128]{2,1,0:T(8,128)(2,1)S(1)}, u32[]{:S(2)}, u32[]{:S(2)}) %collective-permute-start.8) | collective-permute-done | bytes 90144 | tf_op jit(solution)/shard_map/ppermute | solution.py:233
  29.3 1.2 %collective-permute-done.9.refs_1_ = s16[22,16,128]{2,1,0:T(8,128)(2,1)S(1)} collective-permute-done((s16[22,16,128]{2,1,0:T(8,128)(2,1)S(1)}, s16[22,16,128]{2,1,0:T(8,128)(2,1)S(1)}, u32[]{:S(2)}, u32[]{:S(2)}) %collective-permute-start.9) | collective-permute-done | bytes 90144 | tf_op jit(solution)/shard_map/ppermute | solution.py:233
  30.8 2.7 %collective-permute-start.11 = (s16[7,16,128]{2,1,0:T(8,128)(2,1)S(1)}, s16[7,16,128]{2,1,0:T(8,128)(2,1)S(1)}, u32[]{:S(2)}, u32[]{:S(2)}) collective-permute-start(s16[7,16,128]{2,1,0:T(8,128)(2,1)S(1)} %get-tuple-element.33), channel_id=1, source_target_pairs={{0,2},{1,3},{2,0},{3,1},{4,6},{5,7},{6,4},{7,5},{8,10},{9,11},{10,... | collective-permute-start | bytes 86024 | tf_op jit(solution)/shard_map/ppermute | solution.py:233
  33.4 1.3 %collective-permute-start.12 = (s16[7,16,128]{2,1,0:T(8,128)(2,1)S(1)}, s16[7,16,128]{2,1,0:T(8,128)(2,1)S(1)}, u32[]{:S(2)}, u32[]{:S(2)}) collective-permute-start(s16[7,16,128]{2,1,0:T(8,128)(2,1)S(1)} %get-tuple-element.34), channel_id=1, source_target_pairs={{0,3},{1,2},{2,1},{3,0},{4,7},{5,6},{6,5},{7,4},{8,11},{9,10},{10,... | collective-permute-start | bytes 86024 | tf_op jit(solution)/shard_map/ppermute | solution.py:233
  34.8 0.2 collective-permute-start.13
  35.0 0.6 %collective-permute-done.11.refs_0_ = s16[7,16,128]{2,1,0:T(8,128)(2,1)S(1)} collective-permute-done((s16[7,16,128]{2,1,0:T(8,128)(2,1)S(1)}, s16[7,16,128]{2,1,0:T(8,128)(2,1)S(1)}, u32[]{:S(2)}, u32[]{:S(2)}) %collective-permute-start.11) | collective-permute-done | bytes 28704 | tf_op jit(solution)/shard_map/ppermute | solution.py:233
  35.6 3.5 %collective-permute-done.12.refs_1_ = s16[7,16,128]{2,1,0:T(8,128)(2,1)S(1)} collective-permute-done((s16[7,16,128]{2,1,0:T(8,128)(2,1)S(1)}, s16[7,16,128]{2,1,0:T(8,128)(2,1)S(1)}, u32[]{:S(2)}, u32[]{:S(2)}) %collective-permute-start.12) | collective-permute-done | bytes 28704 | tf_op jit(solution)/shard_map/ppermute | solution.py:233
  39.3 11.4 %all_to_all.5 = f32[32,4,128]{2,1,0:T(4,128)S(1)} all-to-all(f32[32,4,128]{2,1,0:T(4,128)S(1)} %bitcast.9), channel_id=1, replica_groups=mesh['chan'=8,'tm'=4] {'chan','tm'}, dimensions={0} | all-to-all | bytes 131072 | tf_op jit(solution)/shard_map/all_to_all | solution.py:386
  50.7 0.9 %place_lags.1 = f32[16,4,256]{2,1,0:T(4,128)} custom-call(f32[8,4,4,128]{3,2,1,0:T(4,128)S(1)} %bitcast.8), custom_call_target="tpu_custom_call" | custom-call | tf_op jit(solution)/shard_map/place_lags/pallas_call | solution.py:387
  (16 shorter events, 0.9 us)
Async XLA Ops:
  0.0 17.8 %copy-start = (bf16[2,8,16,2048]{3,2,1,0:T(8,128)(2,1)S(1)}, bf16[2,8,16,2048]{3,2,1,0:T(8,128)(2,1)}, u32[]{:S(2)}) copy-start(bf16[2,8,16,2048]{3,2,1,0:T(8,128)(2,1)} %constant.23.clone.refs_9_) | copy-start | bytes 3145732
  1.1 8.2 %collective-permute-start.1 = (bf16[2,256,128]{2,1,0:T(8,128)(2,1)S(1)}, bf16[2,256,128]{2,1,0:T(8,128)(2,1)S(1)}, u32[]{:S(2)}, u32[]{:S(2)}) collective-permute-start(bf16[2,256,128]{2,1,0:T(8,128)(2,1)S(1)} %get-tuple-element.37), channel_id=1, source_target_pairs={{0,28},{4,24},{8,20},{12,16},{16,12},{20,8},{24,4},{28,0},{1,29},{... | collective-permute-start | bytes 393224 | tf_op jit(solution)/shard_map/ppermute | solution.py:233
  4.5 7.3 %collective-permute-start = (bf16[2,256,128]{2,1,0:T(8,128)(2,1)S(1)}, bf16[2,256,128]{2,1,0:T(8,128)(2,1)S(1)}, u32[]{:S(2)}, u32[]{:S(2)}) collective-permute-start(bf16[2,256,128]{2,1,0:T(8,128)(2,1)S(1)} %get-tuple-element.38), channel_id=1, source_target_pairs={{0,24},{4,28},{8,16},{12,20},{16,8},{20,12},{24,0},{28,4},{1,25},{... | collective-permute-start | bytes 393224 | tf_op jit(solution)/shard_map/ppermute | solution.py:233
  6.4 8.6 %collective-permute-start.2 = (bf16[2,256,128]{2,1,0:T(8,128)(2,1)S(1)}, bf16[2,256,128]{2,1,0:T(8,128)(2,1)S(1)}, u32[]{:S(2)}, u32[]{:S(2)}) collective-permute-start(bf16[2,256,128]{2,1,0:T(8,128)(2,1)S(1)} %get-tuple-element.21), channel_id=1, source_target_pairs={{0,8},{4,12},{8,0},{12,4},{16,24},{20,28},{24,16},{28,20},{1,9},{5... | collective-permute-start | bytes 393224 | tf_op jit(solution)/shard_map/ppermute | solution.py:233
  7.8 10.0 %copy-start.1 = (s32[8,128]{1,0:T(8,128)S(1)}, s32[8,128]{1,0:T(8,128)}, u32[]{:S(2)}) copy-start(s32[8,128]{1,0:T(8,128)} %refs_8_.1) | copy-start | bytes 12292
  7.8 7.2 %collective-permute-start.3 = (bf16[2,256,128]{2,1,0:T(8,128)(2,1)S(1)}, bf16[2,256,128]{2,1,0:T(8,128)(2,1)S(1)}, u32[]{:S(2)}, u32[]{:S(2)}) collective-permute-start(bf16[2,256,128]{2,1,0:T(8,128)(2,1)S(1)} %get-tuple-element.22), channel_id=1, source_target_pairs={{0,16},{4,20},{8,24},{12,28},{16,0},{20,4},{24,8},{28,12},{1,17},{... | collective-permute-start | bytes 393224 | tf_op jit(solution)/shard_map/ppermute | solution.py:233
  9.3 8.5 %collective-permute-start.4 = (bf16[2,256,128]{2,1,0:T(8,128)(2,1)S(1)}, bf16[2,256,128]{2,1,0:T(8,128)(2,1)S(1)}, u32[]{:S(2)}, u32[]{:S(2)}) collective-permute-start(bf16[2,256,128]{2,1,0:T(8,128)(2,1)S(1)} %get-tuple-element.23), channel_id=1, source_target_pairs={{0,12},{4,8},{8,4},{12,0},{16,28},{20,24},{24,20},{28,16},{1,13},{... | collective-permute-start | bytes 393224 | tf_op jit(solution)/shard_map/ppermute | solution.py:233
  9.3 8.5 %collective-permute-start.5 = (bf16[2,256,128]{2,1,0:T(8,128)(2,1)S(1)}, bf16[2,256,128]{2,1,0:T(8,128)(2,1)S(1)}, u32[]{:S(2)}, u32[]{:S(2)}) collective-permute-start(bf16[2,256,128]{2,1,0:T(8,128)(2,1)S(1)} %get-tuple-element.24), channel_id=1, source_target_pairs={{0,20},{4,16},{8,28},{12,24},{16,4},{20,0},{24,12},{28,8},{1,21},{... | collective-permute-start | bytes 393224 | tf_op jit(solution)/shard_map/ppermute | solution.py:233
  11.7 6.0 %collective-permute-start.6 = (bf16[2,256,128]{2,1,0:T(8,128)(2,1)S(1)}, bf16[2,256,128]{2,1,0:T(8,128)(2,1)S(1)}, u32[]{:S(2)}, u32[]{:S(2)}) collective-permute-start(bf16[2,256,128]{2,1,0:T(8,128)(2,1)S(1)} %get-tuple-element.25), channel_id=1, source_target_pairs={{0,4},{4,0},{8,12},{12,8},{16,20},{20,16},{24,28},{28,24},{1,5},{5... | collective-permute-start | bytes 393224 | tf_op jit(solution)/shard_map/ppermute | solution.py:233
  21.1 1.7 %collective-permute-start.7 = (s16[4,22,16,128]{3,2,1,0:T(8,128)(2,1)S(1)}, s16[4,22,16,128]{3,2,1,0:T(8,128)(2,1)S(1)}, u32[]{:S(2)}, u32[]{:S(2)}) collective-permute-start(s16[4,22,16,128]{3,2,1,0:T(8,128)(2,1)S(1)} %get-tuple-element.28), channel_id=1, source_target_pairs={{0,4},{4,0},{8,12},{12,8},{16,20},{20,16},{24,28},{28,24},{1,5},{5... | collective-permute-start | bytes 1081352 | tf_op jit(solution)/shard_map/ppermute | solution.py:233
  23.0 6.3 %collective-permute-start.8 = (s16[22,16,128]{2,1,0:T(8,128)(2,1)S(1)}, s16[22,16,128]{2,1,0:T(8,128)(2,1)S(1)}, u32[]{:S(2)}, u32[]{:S(2)}) collective-permute-start(s16[22,16,128]{2,1,0:T(8,128)(2,1)S(1)} %get-tuple-element.29), channel_id=1, source_target_pairs={{0,24},{4,28},{8,16},{12,20},{16,8},{20,12},{24,0},{28,4},{1,25},{... | collective-permute-start | bytes 270344 | tf_op jit(solution)/shard_map/ppermute | solution.py:233
  25.4 5.1 %collective-permute-start.9 = (s16[22,16,128]{2,1,0:T(8,128)(2,1)S(1)}, s16[22,16,128]{2,1,0:T(8,128)(2,1)S(1)}, u32[]{:S(2)}, u32[]{:S(2)}) collective-permute-start(s16[22,16,128]{2,1,0:T(8,128)(2,1)S(1)} %get-tuple-element.30), channel_id=1, source_target_pairs={{0,8},{4,12},{8,0},{12,4},{16,24},{20,28},{24,16},{28,20},{1,9},{5... | collective-permute-start | bytes 270344 | tf_op jit(solution)/shard_map/ppermute | solution.py:233
  25.9 4.7 %collective-permute-start.10 = (s16[22,16,128]{2,1,0:T(8,128)(2,1)S(1)}, s16[22,16,128]{2,1,0:T(8,128)(2,1)S(1)}, u32[]{:S(2)}, u32[]{:S(2)}) collective-permute-start(s16[22,16,128]{2,1,0:T(8,128)(2,1)S(1)} %get-tuple-element.31), channel_id=1, source_target_pairs={{0,16},{4,20},{8,24},{12,28},{16,0},{20,4},{24,8},{28,12},{1,17},{... | collective-permute-start | bytes 270344 | tf_op jit(solution)/shard_map/ppermute | solution.py:233
  30.8 4.8 %collective-permute-start.11 = (s16[7,16,128]{2,1,0:T(8,128)(2,1)S(1)}, s16[7,16,128]{2,1,0:T(8,128)(2,1)S(1)}, u32[]{:S(2)}, u32[]{:S(2)}) collective-permute-start(s16[7,16,128]{2,1,0:T(8,128)(2,1)S(1)} %get-tuple-element.33), channel_id=1, source_target_pairs={{0,2},{1,3},{2,0},{3,1},{4,6},{5,7},{6,4},{7,5},{8,10},{9,11},{10,... | collective-permute-start | bytes 86024 | tf_op jit(solution)/shard_map/ppermute | solution.py:233
  33.4 5.7 %collective-permute-start.12 = (s16[7,16,128]{2,1,0:T(8,128)(2,1)S(1)}, s16[7,16,128]{2,1,0:T(8,128)(2,1)S(1)}, u32[]{:S(2)}, u32[]{:S(2)}) collective-permute-start(s16[7,16,128]{2,1,0:T(8,128)(2,1)S(1)} %get-tuple-element.34), channel_id=1, source_target_pairs={{0,3},{1,2},{2,1},{3,0},{4,7},{5,6},{6,5},{7,4},{8,11},{9,10},{10,... | collective-permute-start | bytes 86024 | tf_op jit(solution)/shard_map/ppermute | solution.py:233
  34.8 4.3 %collective-permute-start.13 = (s16[7,16,128]{2,1,0:T(8,128)(2,1)S(1)}, s16[7,16,128]{2,1,0:T(8,128)(2,1)S(1)}, u32[]{:S(2)}, u32[]{:S(2)}) collective-permute-start(s16[7,16,128]{2,1,0:T(8,128)(2,1)S(1)} %get-tuple-element.35), channel_id=1, source_target_pairs={{0,1},{1,0},{2,3},{3,2},{4,5},{5,4},{6,7},{7,6},{8,9},{9,8},{10,11... | collective-permute-start | bytes 86024 | tf_op jit(solution)/shard_map/ppermute | solution.py:233

commit v18 on v16

--- a/solution.py
+++ b/solution.py
@@ -107,18 +107,19 @@
         ],
         axis=0,
     )
-    for number in range(offset_count):
-        turn = chans - offset_of(number, offs_ref, chan_count // 2) * (chans // chan_count)
-        slot = number % 2
-        for row in range(0, freqs, step):
-            own = [white_ref[part, row : row + step, :] for part in range(2)]
+    turns = [chans - offset_of(number, offs_ref, chan_count // 2) * (chans // chan_count) for number in range(offset_count)]
+    for row in range(0, freqs, step):
+        own = [white_ref[part, row : row + step, :] for part in range(2)]
+        own_real, own_imag = (value.astype(jnp.float32) for value in own)
+        for number, turn in enumerate(turns):
             far_real, far_imag = (pltpu.roll(value, turn, 1).astype(jnp.float32) for value in own)
-            own_real, own_imag = (value.astype(jnp.float32) for value in own)
             real = own_real * far_real + own_imag * far_imag
             imag = own_imag * far_real - own_real * far_imag
-            cross_ref[slot, row : row + step, 0:chans] = real.astype(jnp.bfloat16)
-            cross_ref[slot, row : row + step, chans : 2 * chans] = imag.astype(jnp.bfloat16)
-        sums = jnp.dot(table, cross_ref[slot], preferred_element_type=jnp.float32)
+            cross_ref[number, row : row + step, 0:chans] = real.astype(jnp.bfloat16)
+            cross_ref[number, row : row + step, chans : 2 * chans] = imag.astype(jnp.bfloat16)
+
+    for number, turn in enumerate(turns):
+        sums = jnp.dot(table, cross_ref[number], preferred_element_type=jnp.float32)
         cos_real, sin_real = sums[:half, :chans], sums[half:, :chans]
         cos_imag, sin_imag = sums[:half, chans:], sums[half:, chans:]
         corr = (
@@ -223,7 +224,7 @@
 
 
 def chips(count):
-    return [k for k in partners(count) if k % 2 == 0]
+    return sorted(range(2, count, 2), key=lambda k: (k.bit_count(), k)) + [0]
 
 
 def exchange(pieces, axis, order):
@@ -348,7 +349,7 @@
         scratch_shapes=[
             pltpu.VMEM((freqs, chans), jnp.float32),
             pltpu.VMEM((2, freqs, chans), jnp.bfloat16),
-            pltpu.VMEM((2, freqs, 2 * chans), jnp.bfloat16),
+            pltpu.VMEM((offset_count, freqs, 2 * chans), jnp.bfloat16),
             pltpu.SMEM(offsets.shape, jnp.int32),
             pltpu.SemaphoreType.DMA(()),
         ],

time: 51.4 us -> 50.8 us (0.988)
  blocking collectives: 11.4 us -> 10.1 us
  waiting for transfers between devices: 16.7 us -> 17.6 us
    all_to_all x1, blocking collectives: 11.4 us -> 10.1 us  [window_shards(): lax.all_to_all(pieces.reshape(shape), ('chan', 'tm'), 0, 0, tiled=True)]
    ppermute x14, waiting for transfers between devices: 16.7 us -> 17.6 us  [exchange(): lax.ppermute(piece, axis, [(source, source ^ k) for source in range(count)])]
where the time goes in v18:
time: 50.8 us; the launch traced here: 50.6 us
  waiting for transfers between devices  17.6 us (35%)
  starting transfers between devices  15.8 us (31%)
  blocking collectives  10.1 us (20%)
  Pallas kernels  7.05 us (14%)
    ppermute x14, waiting for transfers between devices, exchange(): lax.ppermute(piece, axis, [(source, source ^ k) for source in range(count)])  17.6 us
    ppermute x14, starting transfers between devices, exchange(): lax.ppermute(piece, axis, [(source, source ^ k) for source in range(count)])  15.8 us
    all_to_all x1, blocking collectives, window_shards(): lax.all_to_all(pieces.reshape(shape), ('chan', 'tm'), 0, 0, tiled=True)  10.1 us
    pallas_call x1, Pallas kernels, window_shards(): pl.pallas_call(functools.partial(window_kernel, chan_order), out_shape=[j...  3.25 us
    pallas_call x2, Pallas kernels, window_shards(): pl.pallas_call(functools.partial(split_kernel, part), out_shape=[jax.Shap...  2.32 us
  transfers between devices with their start and end apart: 14, of which 10 were waited for; matrix products, arithmetic and copies ran while one was open for 0% of the time, Pallas kernels for 2%

profile of v18, /device:TPU:0, one launch (start us, length us, event | category | flops | bytes accessed | tf_op | source)
XLA Modules:
  0.0 50.6 jit_solution(1234770443473422630)
XLA Ops:
  0.0 1.1 %split_windows.2 = (bf16[2,256,128]{2,1,0:T(8,128)(2,1)S(1)}, bf16[2,256,128]{2,1,0:T(8,128)(2,1)S(1)}) custom-call(s32[1]{0:T(128)} %bitcast.1.where_ref, bf16[2,8,256,128]{3,2,1,0:T(8,128)(2,1)} %spec_ref.3), custom_call_target="tpu_custom_call" | custom-call | tf_op jit(solution)/shard_map/split_windows/pallas_call | solution.py:333
  1.1 4.0 %collective-permute-start = (bf16[2,256,128]{2,1,0:T(8,128)(2,1)S(1)}, bf16[2,256,128]{2,1,0:T(8,128)(2,1)S(1)}, u32[]{:S(2)}, u32[]{:S(2)}) collective-permute-start(bf16[2,256,128]{2,1,0:T(8,128)(2,1)S(1)} %get-tuple-element.23), channel_id=1, source_target_pairs={{0,24},{4,28},{8,16},{12,20},{16,8},{20,12},{24,0},{28,4},{1,25},{... | collective-permute-start | bytes 393224 | tf_op jit(solution)/shard_map/ppermute | solution.py:233
  5.0 1.3 %split_windows.3 = (bf16[2,256,128]{2,1,0:T(8,128)(2,1)S(1)}, bf16[2,256,128]{2,1,0:T(8,128)(2,1)S(1)}, bf16[2,256,128]{2,1,0:T(8,128)(2,1)S(1)}, bf16[2,256,128...) custom-call(s32[1]{0:T(128)} %bitcast.1.where_ref, ...), custom_call_target="tpu_custom_call" | custom-call | tf_op jit(solution)/shard_map/split_windows/pallas_call | solution.py:333
  6.3 1.2 %collective-permute-start.2 = (bf16[2,256,128]{2,1,0:T(8,128)(2,1)S(1)}, bf16[2,256,128]{2,1,0:T(8,128)(2,1)S(1)}, u32[]{:S(2)}, u32[]{:S(2)}) collective-permute-start(bf16[2,256,128]{2,1,0:T(8,128)(2,1)S(1)} %get-tuple-element.25), channel_id=1, source_target_pairs={{0,8},{4,12},{8,0},{12,4},{16,24},{20,28},{24,16},{28,20},{1,9},{5... | collective-permute-start | bytes 393224 | tf_op jit(solution)/shard_map/ppermute | solution.py:233
  7.5 1.5 %collective-permute-start.3 = (bf16[2,256,128]{2,1,0:T(8,128)(2,1)S(1)}, bf16[2,256,128]{2,1,0:T(8,128)(2,1)S(1)}, u32[]{:S(2)}, u32[]{:S(2)}) collective-permute-start(bf16[2,256,128]{2,1,0:T(8,128)(2,1)S(1)} %get-tuple-element.26), channel_id=1, source_target_pairs={{0,16},{4,20},{8,24},{12,28},{16,0},{20,4},{24,8},{28,12},{1,17},{... | collective-permute-start | bytes 393224 | tf_op jit(solution)/shard_map/ppermute | solution.py:233
  9.0 0.6 %collective-permute-start.4 = (bf16[2,256,128]{2,1,0:T(8,128)(2,1)S(1)}, bf16[2,256,128]{2,1,0:T(8,128)(2,1)S(1)}, u32[]{:S(2)}, u32[]{:S(2)}) collective-permute-start(bf16[2,256,128]{2,1,0:T(8,128)(2,1)S(1)} %get-tuple-element.27), channel_id=1, source_target_pairs={{0,12},{4,8},{8,4},{12,0},{16,28},{20,24},{24,20},{28,16},{1,13},{... | collective-permute-start | bytes 393224 | tf_op jit(solution)/shard_map/ppermute | solution.py:233
  9.6 0.6 %collective-permute-start.5 = (bf16[2,256,128]{2,1,0:T(8,128)(2,1)S(1)}, bf16[2,256,128]{2,1,0:T(8,128)(2,1)S(1)}, u32[]{:S(2)}, u32[]{:S(2)}) collective-permute-start(bf16[2,256,128]{2,1,0:T(8,128)(2,1)S(1)} %get-tuple-element.28), channel_id=1, source_target_pairs={{0,20},{4,16},{8,28},{12,24},{16,4},{20,0},{24,12},{28,8},{1,21},{... | collective-permute-start | bytes 393224 | tf_op jit(solution)/shard_map/ppermute | solution.py:233
  10.2 1.6 %collective-permute-done.1.refs_1_ = bf16[2,256,128]{2,1,0:T(8,128)(2,1)S(1)} collective-permute-done((bf16[2,256,128]{2,1,0:T(8,128)(2,1)S(1)}, bf16[2,256,128]{2,1,0:T(8,128)(2,1)S(1)}, u32[]{:S(2)}, u32[]{:S(2)}) %collective-permute-start.1) | collective-permute-done | bytes 131104 | tf_op jit(solution)/shard_map/ppermute | solution.py:233
  11.8 3.5 %collective-permute-done.2.refs_2_ = bf16[2,256,128]{2,1,0:T(8,128)(2,1)S(1)} collective-permute-done((bf16[2,256,128]{2,1,0:T(8,128)(2,1)S(1)}, bf16[2,256,128]{2,1,0:T(8,128)(2,1)S(1)}, u32[]{:S(2)}, u32[]{:S(2)}) %collective-permute-start.2) | collective-permute-done | bytes 131104 | tf_op jit(solution)/shard_map/ppermute | solution.py:233
  15.2 1.1 %collective-permute-done.4.refs_4_ = bf16[2,256,128]{2,1,0:T(8,128)(2,1)S(1)} collective-permute-done((bf16[2,256,128]{2,1,0:T(8,128)(2,1)S(1)}, bf16[2,256,128]{2,1,0:T(8,128)(2,1)S(1)}, u32[]{:S(2)}, u32[]{:S(2)}) %collective-permute-start.4) | collective-permute-done | bytes 131104 | tf_op jit(solution)/shard_map/ppermute | solution.py:233
  16.4 0.7 %collective-permute-done.5.refs_5_ = bf16[2,256,128]{2,1,0:T(8,128)(2,1)S(1)} collective-permute-done((bf16[2,256,128]{2,1,0:T(8,128)(2,1)S(1)}, bf16[2,256,128]{2,1,0:T(8,128)(2,1)S(1)}, u32[]{:S(2)}, u32[]{:S(2)}) %collective-permute-start.5) | collective-permute-done | bytes 131104 | tf_op jit(solution)/shard_map/ppermute | solution.py:233
  17.1 3.3 %window_pairs.1 = (s16[4,22,16,128]{3,2,1,0:T(8,128)(2,1)S(1)}, s16[4,22,16,128]{3,2,1,0:T(8,128)(2,1)S(1)}) custom-call(s32[4]{0:T(128)} %offs_hbm_ref.1, s32[1]{0:T(128)} %bitcast.1.where_ref, bf16[2,256,128]{2,1,0:T(8,128)(2,1)S(1)} %collective-permute-done.refs_0_, bf16[2,256,128]{2,1,0:T(8,128)(2,1)S(1)} %collective-permute-done.1.refs_1_, ...), custom_call_target="tpu_custom_call" | custom-call | tf_op jit(solution)/shard_map/window_pairs/pallas_call | solution.py:344
  20.5 1.6 %collective-permute-done.7.far_ref = s16[4,22,16,128]{3,2,1,0:T(8,128)(2,1)S(1)} collective-permute-done((s16[4,22,16,128]{3,2,1,0:T(8,128)(2,1)S(1)}, s16[4,22,16,128]{3,2,1,0:T(8,128)(2,1)S(1)}, u32[]{:S(2)}, u32[]{:S(2)}) %collective-permute-start.7) | collective-permute-done | bytes 360480 | tf_op jit(solution)/shard_map/ppermute | solution.py:233
  22.3 1.6 %collective-permute-start.8 = (s16[22,16,128]{2,1,0:T(8,128)(2,1)S(1)}, s16[22,16,128]{2,1,0:T(8,128)(2,1)S(1)}, u32[]{:S(2)}, u32[]{:S(2)}) collective-permute-start(s16[22,16,128]{2,1,0:T(8,128)(2,1)S(1)} %get-tuple-element.33), channel_id=1, source_target_pairs={{0,8},{4,12},{8,0},{12,4},{16,24},{20,28},{24,16},{28,20},{1,9},{5... | collective-permute-start | bytes 270344 | tf_op jit(solution)/shard_map/ppermute | solution.py:233
  23.9 1.6 %collective-permute-start.9 = (s16[22,16,128]{2,1,0:T(8,128)(2,1)S(1)}, s16[22,16,128]{2,1,0:T(8,128)(2,1)S(1)}, u32[]{:S(2)}, u32[]{:S(2)}) collective-permute-start(s16[22,16,128]{2,1,0:T(8,128)(2,1)S(1)} %get-tuple-element.34), channel_id=1, source_target_pairs={{0,16},{4,20},{8,24},{12,28},{16,0},{20,4},{24,8},{28,12},{1,17},{... | collective-permute-start | bytes 270344 | tf_op jit(solution)/shard_map/ppermute | solution.py:233
  25.8 1.2 %collective-permute-done.8.refs_0_ = s16[22,16,128]{2,1,0:T(8,128)(2,1)S(1)} collective-permute-done((s16[22,16,128]{2,1,0:T(8,128)(2,1)S(1)}, s16[22,16,128]{2,1,0:T(8,128)(2,1)S(1)}, u32[]{:S(2)}, u32[]{:S(2)}) %collective-permute-start.8) | collective-permute-done | bytes 90144 | tf_op jit(solution)/shard_map/ppermute | solution.py:233
  27.0 2.4 %collective-permute-done.9.refs_1_ = s16[22,16,128]{2,1,0:T(8,128)(2,1)S(1)} collective-permute-done((s16[22,16,128]{2,1,0:T(8,128)(2,1)S(1)}, s16[22,16,128]{2,1,0:T(8,128)(2,1)S(1)}, u32[]{:S(2)}, u32[]{:S(2)}) %collective-permute-start.9) | collective-permute-done | bytes 90144 | tf_op jit(solution)/shard_map/ppermute | solution.py:233
  29.4 1.5 %collective-permute-done.10.refs_2_ = s16[22,16,128]{2,1,0:T(8,128)(2,1)S(1)} collective-permute-done((s16[22,16,128]{2,1,0:T(8,128)(2,1)S(1)}, s16[22,16,128]{2,1,0:T(8,128)(2,1)S(1)}, u32[]{:S(2)}, u32[]{:S(2)}) %collective-permute-start.10) | collective-permute-done | bytes 90144 | tf_op jit(solution)/shard_map/ppermute | solution.py:233
  31.0 2.7 %collective-permute-start.11 = (s16[7,16,128]{2,1,0:T(8,128)(2,1)S(1)}, s16[7,16,128]{2,1,0:T(8,128)(2,1)S(1)}, u32[]{:S(2)}, u32[]{:S(2)}) collective-permute-start(s16[7,16,128]{2,1,0:T(8,128)(2,1)S(1)} %get-tuple-element.37), channel_id=1, source_target_pairs={{0,2},{1,3},{2,0},{3,1},{4,6},{5,7},{6,4},{7,5},{8,10},{9,11},{10,... | collective-permute-start | bytes 86024 | tf_op jit(solution)/shard_map/ppermute | solution.py:233
  33.7 1.3 %collective-permute-start.12 = (s16[7,16,128]{2,1,0:T(8,128)(2,1)S(1)}, s16[7,16,128]{2,1,0:T(8,128)(2,1)S(1)}, u32[]{:S(2)}, u32[]{:S(2)}) collective-permute-start(s16[7,16,128]{2,1,0:T(8,128)(2,1)S(1)} %get-tuple-element.38), channel_id=1, source_target_pairs={{0,3},{1,2},{2,1},{3,0},{4,7},{5,6},{6,5},{7,4},{8,11},{9,10},{10,... | collective-permute-start | bytes 86024 | tf_op jit(solution)/shard_map/ppermute | solution.py:233
  35.3 0.9 %collective-permute-done.11.refs_0_ = s16[7,16,128]{2,1,0:T(8,128)(2,1)S(1)} collective-permute-done((s16[7,16,128]{2,1,0:T(8,128)(2,1)S(1)}, s16[7,16,128]{2,1,0:T(8,128)(2,1)S(1)}, u32[]{:S(2)}, u32[]{:S(2)}) %collective-permute-start.11) | collective-permute-done | bytes 28704 | tf_op jit(solution)/shard_map/ppermute | solution.py:233
  36.1 3.2 %collective-permute-done.12.refs_1_ = s16[7,16,128]{2,1,0:T(8,128)(2,1)S(1)} collective-permute-done((s16[7,16,128]{2,1,0:T(8,128)(2,1)S(1)}, s16[7,16,128]{2,1,0:T(8,128)(2,1)S(1)}, u32[]{:S(2)}, u32[]{:S(2)}) %collective-permute-start.12) | collective-permute-done | bytes 28704 | tf_op jit(solution)/shard_map/ppermute | solution.py:233
  39.6 10.1 %all_to_all.5 = f32[32,4,128]{2,1,0:T(4,128)S(1)} all-to-all(f32[32,4,128]{2,1,0:T(4,128)S(1)} %bitcast.5), channel_id=1, replica_groups=mesh['chan'=8,'tm'=4] {'chan','tm'}, dimensions={0} | all-to-all | bytes 131072 | tf_op jit(solution)/shard_map/all_to_all | solution.py:385
  49.7 0.9 %place_lags.1 = f32[16,4,256]{2,1,0:T(4,128)} custom-call(f32[8,4,4,128]{3,2,1,0:T(4,128)S(1)} %bitcast.4), custom_call_target="tpu_custom_call" | custom-call | tf_op jit(solution)/shard_map/place_lags/pallas_call | solution.py:386
  (16 shorter events, 1.4 us)
Async XLA Ops:
  0.0 17.1 %copy-start = (bf16[2,8,16,2048]{3,2,1,0:T(8,128)(2,1)S(1)}, bf16[2,8,16,2048]{3,2,1,0:T(8,128)(2,1)}, u32[]{:S(2)}) copy-start(bf16[2,8,16,2048]{3,2,1,0:T(8,128)(2,1)} %constant.11.clone.refs_9_) | copy-start | bytes 3145732
  1.1 8.5 %collective-permute-start = (bf16[2,256,128]{2,1,0:T(8,128)(2,1)S(1)}, bf16[2,256,128]{2,1,0:T(8,128)(2,1)S(1)}, u32[]{:S(2)}, u32[]{:S(2)}) collective-permute-start(bf16[2,256,128]{2,1,0:T(8,128)(2,1)S(1)} %get-tuple-element.23), channel_id=1, source_target_pairs={{0,24},{4,28},{8,16},{12,20},{16,8},{20,12},{24,0},{28,4},{1,25},{... | collective-permute-start | bytes 393224 | tf_op jit(solution)/shard_map/ppermute | solution.py:233
  5.0 6.7 %collective-permute-start.1 = (bf16[2,256,128]{2,1,0:T(8,128)(2,1)S(1)}, bf16[2,256,128]{2,1,0:T(8,128)(2,1)S(1)}, u32[]{:S(2)}, u32[]{:S(2)}) collective-permute-start(bf16[2,256,128]{2,1,0:T(8,128)(2,1)S(1)} %get-tuple-element.24), channel_id=1, source_target_pairs={{0,28},{4,24},{8,20},{12,16},{16,12},{20,8},{24,4},{28,0},{1,29},{... | collective-permute-start | bytes 393224 | tf_op jit(solution)/shard_map/ppermute | solution.py:233
  6.3 8.9 %collective-permute-start.2 = (bf16[2,256,128]{2,1,0:T(8,128)(2,1)S(1)}, bf16[2,256,128]{2,1,0:T(8,128)(2,1)S(1)}, u32[]{:S(2)}, u32[]{:S(2)}) collective-permute-start(bf16[2,256,128]{2,1,0:T(8,128)(2,1)S(1)} %get-tuple-element.25), channel_id=1, source_target_pairs={{0,8},{4,12},{8,0},{12,4},{16,24},{20,28},{24,16},{28,20},{1,9},{5... | collective-permute-start | bytes 393224 | tf_op jit(solution)/shard_map/ppermute | solution.py:233
  7.5 9.6 %copy-start.1 = (s32[8,128]{1,0:T(8,128)S(1)}, s32[8,128]{1,0:T(8,128)}, u32[]{:S(2)}) copy-start(s32[8,128]{1,0:T(8,128)} %refs_8_.1) | copy-start | bytes 12292
  7.5 7.7 %collective-permute-start.3 = (bf16[2,256,128]{2,1,0:T(8,128)(2,1)S(1)}, bf16[2,256,128]{2,1,0:T(8,128)(2,1)S(1)}, u32[]{:S(2)}, u32[]{:S(2)}) collective-permute-start(bf16[2,256,128]{2,1,0:T(8,128)(2,1)S(1)} %get-tuple-element.26), channel_id=1, source_target_pairs={{0,16},{4,20},{8,24},{12,28},{16,0},{20,4},{24,8},{28,12},{1,17},{... | collective-permute-start | bytes 393224 | tf_op jit(solution)/shard_map/ppermute | solution.py:233
  9.0 7.4 %collective-permute-start.4 = (bf16[2,256,128]{2,1,0:T(8,128)(2,1)S(1)}, bf16[2,256,128]{2,1,0:T(8,128)(2,1)S(1)}, u32[]{:S(2)}, u32[]{:S(2)}) collective-permute-start(bf16[2,256,128]{2,1,0:T(8,128)(2,1)S(1)} %get-tuple-element.27), channel_id=1, source_target_pairs={{0,12},{4,8},{8,4},{12,0},{16,28},{20,24},{24,20},{28,16},{1,13},{... | collective-permute-start | bytes 393224 | tf_op jit(solution)/shard_map/ppermute | solution.py:233
  9.6 7.5 %collective-permute-start.5 = (bf16[2,256,128]{2,1,0:T(8,128)(2,1)S(1)}, bf16[2,256,128]{2,1,0:T(8,128)(2,1)S(1)}, u32[]{:S(2)}, u32[]{:S(2)}) collective-permute-start(bf16[2,256,128]{2,1,0:T(8,128)(2,1)S(1)} %get-tuple-element.28), channel_id=1, source_target_pairs={{0,20},{4,16},{8,28},{12,24},{16,4},{20,0},{24,12},{28,8},{1,21},{... | collective-permute-start | bytes 393224 | tf_op jit(solution)/shard_map/ppermute | solution.py:233
  11.8 5.3 %collective-permute-start.6 = (bf16[2,256,128]{2,1,0:T(8,128)(2,1)S(1)}, bf16[2,256,128]{2,1,0:T(8,128)(2,1)S(1)}, u32[]{:S(2)}, u32[]{:S(2)}) collective-permute-start(bf16[2,256,128]{2,1,0:T(8,128)(2,1)S(1)} %get-tuple-element.29), channel_id=1, source_target_pairs={{0,4},{4,0},{8,12},{12,8},{16,20},{20,16},{24,28},{28,24},{1,5},{5... | collective-permute-start | bytes 393224 | tf_op jit(solution)/shard_map/ppermute | solution.py:233
  20.3 1.7 %collective-permute-start.7 = (s16[4,22,16,128]{3,2,1,0:T(8,128)(2,1)S(1)}, s16[4,22,16,128]{3,2,1,0:T(8,128)(2,1)S(1)}, u32[]{:S(2)}, u32[]{:S(2)}) collective-permute-start(s16[4,22,16,128]{3,2,1,0:T(8,128)(2,1)S(1)} %get-tuple-element.32), channel_id=1, source_target_pairs={{0,4},{4,0},{8,12},{12,8},{16,20},{20,16},{24,28},{28,24},{1,5},{5... | collective-permute-start | bytes 1081352 | tf_op jit(solution)/shard_map/ppermute | solution.py:233
  22.3 4.7 %collective-permute-start.8 = (s16[22,16,128]{2,1,0:T(8,128)(2,1)S(1)}, s16[22,16,128]{2,1,0:T(8,128)(2,1)S(1)}, u32[]{:S(2)}, u32[]{:S(2)}) collective-permute-start(s16[22,16,128]{2,1,0:T(8,128)(2,1)S(1)} %get-tuple-element.33), channel_id=1, source_target_pairs={{0,8},{4,12},{8,0},{12,4},{16,24},{20,28},{24,16},{28,20},{1,9},{5... | collective-permute-start | bytes 270344 | tf_op jit(solution)/shard_map/ppermute | solution.py:233
  23.9 5.5 %collective-permute-start.9 = (s16[22,16,128]{2,1,0:T(8,128)(2,1)S(1)}, s16[22,16,128]{2,1,0:T(8,128)(2,1)S(1)}, u32[]{:S(2)}, u32[]{:S(2)}) collective-permute-start(s16[22,16,128]{2,1,0:T(8,128)(2,1)S(1)} %get-tuple-element.34), channel_id=1, source_target_pairs={{0,16},{4,20},{8,24},{12,28},{16,0},{20,4},{24,8},{28,12},{1,17},{... | collective-permute-start | bytes 270344 | tf_op jit(solution)/shard_map/ppermute | solution.py:233
  25.4 5.4 %collective-permute-start.10 = (s16[22,16,128]{2,1,0:T(8,128)(2,1)S(1)}, s16[22,16,128]{2,1,0:T(8,128)(2,1)S(1)}, u32[]{:S(2)}, u32[]{:S(2)}) collective-permute-start(s16[22,16,128]{2,1,0:T(8,128)(2,1)S(1)} %get-tuple-element.35), channel_id=1, source_target_pairs={{0,24},{4,28},{8,16},{12,20},{16,8},{20,12},{24,0},{28,4},{1,25},{... | collective-permute-start | bytes 270344 | tf_op jit(solution)/shard_map/ppermute | solution.py:233
  31.0 5.1 %collective-permute-start.11 = (s16[7,16,128]{2,1,0:T(8,128)(2,1)S(1)}, s16[7,16,128]{2,1,0:T(8,128)(2,1)S(1)}, u32[]{:S(2)}, u32[]{:S(2)}) collective-permute-start(s16[7,16,128]{2,1,0:T(8,128)(2,1)S(1)} %get-tuple-element.37), channel_id=1, source_target_pairs={{0,2},{1,3},{2,0},{3,1},{4,6},{5,7},{6,4},{7,5},{8,10},{9,11},{10,... | collective-permute-start | bytes 86024 | tf_op jit(solution)/shard_map/ppermute | solution.py:233
  33.7 5.7 %collective-permute-start.12 = (s16[7,16,128]{2,1,0:T(8,128)(2,1)S(1)}, s16[7,16,128]{2,1,0:T(8,128)(2,1)S(1)}, u32[]{:S(2)}, u32[]{:S(2)}) collective-permute-start(s16[7,16,128]{2,1,0:T(8,128)(2,1)S(1)} %get-tuple-element.38), channel_id=1, source_target_pairs={{0,3},{1,2},{2,1},{3,0},{4,7},{5,6},{6,5},{7,4},{8,11},{9,10},{10,... | collective-permute-start | bytes 86024 | tf_op jit(solution)/shard_map/ppermute | solution.py:233
  35.0 4.3 %collective-permute-start.13 = (s16[7,16,128]{2,1,0:T(8,128)(2,1)S(1)}, s16[7,16,128]{2,1,0:T(8,128)(2,1)S(1)}, u32[]{:S(2)}, u32[]{:S(2)}) collective-permute-start(s16[7,16,128]{2,1,0:T(8,128)(2,1)S(1)} %get-tuple-element.39), channel_id=1, source_target_pairs={{0,1},{1,0},{2,3},{3,2},{4,5},{5,4},{6,7},{7,6},{8,9},{9,8},{10,11... | collective-permute-start | bytes 86024 | tf_op jit(solution)/shard_map/ppermute | solution.py:233

commit v19 on v18

--- a/solution.py
+++ b/solution.py
@@ -220,7 +220,9 @@
 
 
 def partners(count):
-    return sorted(range(1, count), key=lambda k: (-(k >> 1).bit_count(), k & 1, k)) + [0]
+    near = [k for k in range(2, count) if k.bit_count() == 1]
+    far = [k for k in range(2, count) if k >> 1 not in (1, 2)]
+    return near + far + [k for k in range(2, count) if k not in near + far] + [1, 0]
 
 
 def chips(count):

time: 50.8 us -> 51.4 us (1.012)
  blocking collectives: 10.1 us -> 11 us
    all_to_all x1, blocking collectives: 10.1 us -> 11 us  [window_shards(): lax.all_to_all(pieces.reshape(shape), ('chan', 'tm'), 0, 0, tiled=True)]
  transfers between devices with their start and end apart: 14 -> 14, of which waited for: 10 -> 8; matrix products, arithmetic and copies ran while one was open for 0% -> 0% of each run, Pallas kernels for 2% -> 2%
where the time goes in v19:
time: 51.4 us; the launch traced here: 51.3 us
  waiting for transfers between devices  17.2 us (33%)
  starting transfers between devices  16 us (31%)
  blocking collectives  11 us (21%)
  Pallas kernels  7.05 us (14%)
    ppermute x14, waiting for transfers between devices, exchange(): lax.ppermute(piece, axis, [(source, source ^ k) for source in range(count)])  17.2 us
    ppermute x14, starting transfers between devices, exchange(): lax.ppermute(piece, axis, [(source, source ^ k) for source in range(count)])  16 us
    all_to_all x1, blocking collectives, window_shards(): lax.all_to_all(pieces.reshape(shape), ('chan', 'tm'), 0, 0, tiled=True)  11 us
    pallas_call x1, Pallas kernels, window_shards(): pl.pallas_call(functools.partial(window_kernel, chan_order), out_shape=[j...  3.25 us
    pallas_call x2, Pallas kernels, window_shards(): pl.pallas_call(functools.partial(split_kernel, part), out_shape=[jax.Shap...  2.32 us
  transfers between devices with their start and end apart: 14, of which 8 were waited for; matrix products, arithmetic and copies ran while one was open for 0% of the time, Pallas kernels for 2%

profile of v19, /device:TPU:0, one launch (start us, length us, event | category | flops | bytes accessed | tf_op | source)
XLA Modules:
  0.0 51.3 jit_solution(9216232972467581303)
XLA Ops:
  0.0 1.1 %split_windows.2 = (bf16[2,256,128]{2,1,0:T(8,128)(2,1)S(1)}, bf16[2,256,128]{2,1,0:T(8,128)(2,1)S(1)}) custom-call(s32[1]{0:T(128)} %bitcast.1.where_ref, bf16[2,8,256,128]{3,2,1,0:T(8,128)(2,1)} %spec_ref.3), custom_call_target="tpu_custom_call" | custom-call | tf_op jit(solution)/shard_map/split_windows/pallas_call | solution.py:335
  1.1 3.0 %collective-permute-start = (bf16[2,256,128]{2,1,0:T(8,128)(2,1)S(1)}, bf16[2,256,128]{2,1,0:T(8,128)(2,1)S(1)}, u32[]{:S(2)}, u32[]{:S(2)}) collective-permute-start(bf16[2,256,128]{2,1,0:T(8,128)(2,1)S(1)} %get-tuple-element.23), channel_id=1, source_target_pairs={{0,8},{4,12},{8,0},{12,4},{16,24},{20,28},{24,16},{28,20},{1,9},{5... | collective-permute-start | bytes 393224 | tf_op jit(solution)/shard_map/ppermute | solution.py:235
  4.1 1.5 %collective-permute-start.1 = (bf16[2,256,128]{2,1,0:T(8,128)(2,1)S(1)}, bf16[2,256,128]{2,1,0:T(8,128)(2,1)S(1)}, u32[]{:S(2)}, u32[]{:S(2)}) collective-permute-start(bf16[2,256,128]{2,1,0:T(8,128)(2,1)S(1)} %get-tuple-element.24), channel_id=1, source_target_pairs={{0,16},{4,20},{8,24},{12,28},{16,0},{20,4},{24,8},{28,12},{1,17},{... | collective-permute-start | bytes 393224 | tf_op jit(solution)/shard_map/ppermute | solution.py:235
  5.6 1.3 %split_windows.3 = (bf16[2,256,128]{2,1,0:T(8,128)(2,1)S(1)}, bf16[2,256,128]{2,1,0:T(8,128)(2,1)S(1)}, bf16[2,256,128]{2,1,0:T(8,128)(2,1)S(1)}, bf16[2,256,128...) custom-call(s32[1]{0:T(128)} %bitcast.1.where_ref, ...), custom_call_target="tpu_custom_call" | custom-call | tf_op jit(solution)/shard_map/split_windows/pallas_call | solution.py:335
  7.0 1.5 %collective-permute-start.3 = (bf16[2,256,128]{2,1,0:T(8,128)(2,1)S(1)}, bf16[2,256,128]{2,1,0:T(8,128)(2,1)S(1)}, u32[]{:S(2)}, u32[]{:S(2)}) collective-permute-start(bf16[2,256,128]{2,1,0:T(8,128)(2,1)S(1)} %get-tuple-element.26), channel_id=1, source_target_pairs={{0,28},{4,24},{8,20},{12,16},{16,12},{20,8},{24,4},{28,0},{1,29},{... | collective-permute-start | bytes 393224 | tf_op jit(solution)/shard_map/ppermute | solution.py:235
  8.5 1.7 %collective-permute-start.4 = (bf16[2,256,128]{2,1,0:T(8,128)(2,1)S(1)}, bf16[2,256,128]{2,1,0:T(8,128)(2,1)S(1)}, u32[]{:S(2)}, u32[]{:S(2)}) collective-permute-start(bf16[2,256,128]{2,1,0:T(8,128)(2,1)S(1)} %get-tuple-element.27), channel_id=1, source_target_pairs={{0,12},{4,8},{8,4},{12,0},{16,28},{20,24},{24,20},{28,16},{1,13},{... | collective-permute-start | bytes 393224 | tf_op jit(solution)/shard_map/ppermute | solution.py:235
  10.4 3.9 %collective-permute-done.2.refs_2_ = bf16[2,256,128]{2,1,0:T(8,128)(2,1)S(1)} collective-permute-done((bf16[2,256,128]{2,1,0:T(8,128)(2,1)S(1)}, bf16[2,256,128]{2,1,0:T(8,128)(2,1)S(1)}, u32[]{:S(2)}, u32[]{:S(2)}) %collective-permute-start.2) | collective-permute-done | bytes 131104 | tf_op jit(solution)/shard_map/ppermute | solution.py:235
  14.3 2.7 %collective-permute-done.4.refs_4_ = bf16[2,256,128]{2,1,0:T(8,128)(2,1)S(1)} collective-permute-done((bf16[2,256,128]{2,1,0:T(8,128)(2,1)S(1)}, bf16[2,256,128]{2,1,0:T(8,128)(2,1)S(1)}, u32[]{:S(2)}, u32[]{:S(2)}) %collective-permute-start.4) | collective-permute-done | bytes 131104 | tf_op jit(solution)/shard_map/ppermute | solution.py:235
  17.0 1.2 %collective-permute-done.5.refs_5_ = bf16[2,256,128]{2,1,0:T(8,128)(2,1)S(1)} collective-permute-done((bf16[2,256,128]{2,1,0:T(8,128)(2,1)S(1)}, bf16[2,256,128]{2,1,0:T(8,128)(2,1)S(1)}, u32[]{:S(2)}, u32[]{:S(2)}) %collective-permute-start.5) | collective-permute-done | bytes 131104 | tf_op jit(solution)/shard_map/ppermute | solution.py:235
  18.1 3.3 %window_pairs.1 = (s16[4,22,16,128]{3,2,1,0:T(8,128)(2,1)S(1)}, s16[4,22,16,128]{3,2,1,0:T(8,128)(2,1)S(1)}) custom-call(s32[4]{0:T(128)} %offs_hbm_ref.1, s32[1]{0:T(128)} %bitcast.1.where_ref, bf16[2,256,128]{2,1,0:T(8,128)(2,1)S(1)} %collective-permute-done.refs_0_, bf16[2,256,128]{2,1,0:T(8,128)(2,1)S(1)} %collective-permute-done.1.refs_1_, ...), custom_call_target="tpu_custom_call" | custom-call | tf_op jit(solution)/shard_map/window_pairs/pallas_call | solution.py:346
  21.6 1.6 %collective-permute-done.7.far_ref = s16[4,22,16,128]{3,2,1,0:T(8,128)(2,1)S(1)} collective-permute-done((s16[4,22,16,128]{3,2,1,0:T(8,128)(2,1)S(1)}, s16[4,22,16,128]{3,2,1,0:T(8,128)(2,1)S(1)}, u32[]{:S(2)}, u32[]{:S(2)}) %collective-permute-start.7) | collective-permute-done | bytes 360480 | tf_op jit(solution)/shard_map/ppermute | solution.py:235
  23.1 0.2 merge_windows.1
  23.4 0.9 %collective-permute-start.8 = (s16[22,16,128]{2,1,0:T(8,128)(2,1)S(1)}, s16[22,16,128]{2,1,0:T(8,128)(2,1)S(1)}, u32[]{:S(2)}, u32[]{:S(2)}) collective-permute-start(s16[22,16,128]{2,1,0:T(8,128)(2,1)S(1)} %get-tuple-element.33), channel_id=1, source_target_pairs={{0,8},{4,12},{8,0},{12,4},{16,24},{20,28},{24,16},{28,20},{1,9},{5... | collective-permute-start | bytes 270344 | tf_op jit(solution)/shard_map/ppermute | solution.py:235
  24.2 0.4 collective-permute-start.9
  24.7 2.2 %collective-permute-start.10 = (s16[22,16,128]{2,1,0:T(8,128)(2,1)S(1)}, s16[22,16,128]{2,1,0:T(8,128)(2,1)S(1)}, u32[]{:S(2)}, u32[]{:S(2)}) collective-permute-start(s16[22,16,128]{2,1,0:T(8,128)(2,1)S(1)} %get-tuple-element.35), channel_id=1, source_target_pairs={{0,24},{4,28},{8,16},{12,20},{16,8},{20,12},{24,0},{28,4},{1,25},{... | collective-permute-start | bytes 270344 | tf_op jit(solution)/shard_map/ppermute | solution.py:235
  26.9 1.4 %collective-permute-done.8.refs_0_ = s16[22,16,128]{2,1,0:T(8,128)(2,1)S(1)} collective-permute-done((s16[22,16,128]{2,1,0:T(8,128)(2,1)S(1)}, s16[22,16,128]{2,1,0:T(8,128)(2,1)S(1)}, u32[]{:S(2)}, u32[]{:S(2)}) %collective-permute-start.8) | collective-permute-done | bytes 90144 | tf_op jit(solution)/shard_map/ppermute | solution.py:235
  28.3 2.4 %collective-permute-done.9.refs_1_ = s16[22,16,128]{2,1,0:T(8,128)(2,1)S(1)} collective-permute-done((s16[22,16,128]{2,1,0:T(8,128)(2,1)S(1)}, s16[22,16,128]{2,1,0:T(8,128)(2,1)S(1)}, u32[]{:S(2)}, u32[]{:S(2)}) %collective-permute-start.9) | collective-permute-done | bytes 90144 | tf_op jit(solution)/shard_map/ppermute | solution.py:235
  30.8 2.7 %collective-permute-start.11 = (s16[7,16,128]{2,1,0:T(8,128)(2,1)S(1)}, s16[7,16,128]{2,1,0:T(8,128)(2,1)S(1)}, u32[]{:S(2)}, u32[]{:S(2)}) collective-permute-start(s16[7,16,128]{2,1,0:T(8,128)(2,1)S(1)} %get-tuple-element.37), channel_id=1, source_target_pairs={{0,2},{1,3},{2,0},{3,1},{4,6},{5,7},{6,4},{7,5},{8,10},{9,11},{10,... | collective-permute-start | bytes 86024 | tf_op jit(solution)/shard_map/ppermute | solution.py:235
  33.5 1.3 %collective-permute-start.12 = (s16[7,16,128]{2,1,0:T(8,128)(2,1)S(1)}, s16[7,16,128]{2,1,0:T(8,128)(2,1)S(1)}, u32[]{:S(2)}, u32[]{:S(2)}) collective-permute-start(s16[7,16,128]{2,1,0:T(8,128)(2,1)S(1)} %get-tuple-element.38), channel_id=1, source_target_pairs={{0,3},{1,2},{2,1},{3,0},{4,7},{5,6},{6,5},{7,4},{8,11},{9,10},{10,... | collective-permute-start | bytes 86024 | tf_op jit(solution)/shard_map/ppermute | solution.py:235
  34.9 0.2 collective-permute-start.13
  35.1 0.6 %collective-permute-done.11.refs_0_ = s16[7,16,128]{2,1,0:T(8,128)(2,1)S(1)} collective-permute-done((s16[7,16,128]{2,1,0:T(8,128)(2,1)S(1)}, s16[7,16,128]{2,1,0:T(8,128)(2,1)S(1)}, u32[]{:S(2)}, u32[]{:S(2)}) %collective-permute-start.11) | collective-permute-done | bytes 28704 | tf_op jit(solution)/shard_map/ppermute | solution.py:235
  35.7 3.5 %collective-permute-done.12.refs_1_ = s16[7,16,128]{2,1,0:T(8,128)(2,1)S(1)} collective-permute-done((s16[7,16,128]{2,1,0:T(8,128)(2,1)S(1)}, s16[7,16,128]{2,1,0:T(8,128)(2,1)S(1)}, u32[]{:S(2)}, u32[]{:S(2)}) %collective-permute-start.12) | collective-permute-done | bytes 28704 | tf_op jit(solution)/shard_map/ppermute | solution.py:235
  39.4 11.0 %all_to_all.5 = f32[32,4,128]{2,1,0:T(4,128)S(1)} all-to-all(f32[32,4,128]{2,1,0:T(4,128)S(1)} %bitcast.5), channel_id=1, replica_groups=mesh['chan'=8,'tm'=4] {'chan','tm'}, dimensions={0} | all-to-all | bytes 131072 | tf_op jit(solution)/shard_map/all_to_all | solution.py:387
  50.3 0.9 %place_lags.1 = f32[16,4,256]{2,1,0:T(4,128)} custom-call(f32[8,4,4,128]{3,2,1,0:T(4,128)S(1)} %bitcast.4), custom_call_target="tpu_custom_call" | custom-call | tf_op jit(solution)/shard_map/place_lags/pallas_call | solution.py:388
  (16 shorter events, 0.9 us)
Async XLA Ops:
  0.0 18.1 %copy-start = (bf16[2,8,16,2048]{3,2,1,0:T(8,128)(2,1)S(1)}, bf16[2,8,16,2048]{3,2,1,0:T(8,128)(2,1)}, u32[]{:S(2)}) copy-start(bf16[2,8,16,2048]{3,2,1,0:T(8,128)(2,1)} %constant.11.clone.refs_9_) | copy-start | bytes 3145732
  1.1 9.0 %collective-permute-start = (bf16[2,256,128]{2,1,0:T(8,128)(2,1)S(1)}, bf16[2,256,128]{2,1,0:T(8,128)(2,1)S(1)}, u32[]{:S(2)}, u32[]{:S(2)}) collective-permute-start(bf16[2,256,128]{2,1,0:T(8,128)(2,1)S(1)} %get-tuple-element.23), channel_id=1, source_target_pairs={{0,8},{4,12},{8,0},{12,4},{16,24},{20,28},{24,16},{28,20},{1,9},{5... | collective-permute-start | bytes 393224 | tf_op jit(solution)/shard_map/ppermute | solution.py:235
  4.1 6.1 %collective-permute-start.1 = (bf16[2,256,128]{2,1,0:T(8,128)(2,1)S(1)}, bf16[2,256,128]{2,1,0:T(8,128)(2,1)S(1)}, u32[]{:S(2)}, u32[]{:S(2)}) collective-permute-start(bf16[2,256,128]{2,1,0:T(8,128)(2,1)S(1)} %get-tuple-element.24), channel_id=1, source_target_pairs={{0,16},{4,20},{8,24},{12,28},{16,0},{20,4},{24,8},{28,12},{1,17},{... | collective-permute-start | bytes 393224 | tf_op jit(solution)/shard_map/ppermute | solution.py:235
  6.9 7.4 %collective-permute-start.2 = (bf16[2,256,128]{2,1,0:T(8,128)(2,1)S(1)}, bf16[2,256,128]{2,1,0:T(8,128)(2,1)S(1)}, u32[]{:S(2)}, u32[]{:S(2)}) collective-permute-start(bf16[2,256,128]{2,1,0:T(8,128)(2,1)S(1)} %get-tuple-element.25), channel_id=1, source_target_pairs={{0,24},{4,28},{8,16},{12,20},{16,8},{20,12},{24,0},{28,4},{1,25},{... | collective-permute-start | bytes 393224 | tf_op jit(solution)/shard_map/ppermute | solution.py:235
  7.0 11.2 %copy-start.1 = (s32[8,128]{1,0:T(8,128)S(1)}, s32[8,128]{1,0:T(8,128)}, u32[]{:S(2)}) copy-start(s32[8,128]{1,0:T(8,128)} %refs_8_.1) | copy-start | bytes 12292
  7.0 7.3 %collective-permute-start.3 = (bf16[2,256,128]{2,1,0:T(8,128)(2,1)S(1)}, bf16[2,256,128]{2,1,0:T(8,128)(2,1)S(1)}, u32[]{:S(2)}, u32[]{:S(2)}) collective-permute-start(bf16[2,256,128]{2,1,0:T(8,128)(2,1)S(1)} %get-tuple-element.26), channel_id=1, source_target_pairs={{0,28},{4,24},{8,20},{12,16},{16,12},{20,8},{24,4},{28,0},{1,29},{... | collective-permute-start | bytes 393224 | tf_op jit(solution)/shard_map/ppermute | solution.py:235
  8.5 8.5 %collective-permute-start.4 = (bf16[2,256,128]{2,1,0:T(8,128)(2,1)S(1)}, bf16[2,256,128]{2,1,0:T(8,128)(2,1)S(1)}, u32[]{:S(2)}, u32[]{:S(2)}) collective-permute-start(bf16[2,256,128]{2,1,0:T(8,128)(2,1)S(1)} %get-tuple-element.27), channel_id=1, source_target_pairs={{0,12},{4,8},{8,4},{12,0},{16,28},{20,24},{24,20},{28,16},{1,13},{... | collective-permute-start | bytes 393224 | tf_op jit(solution)/shard_map/ppermute | solution.py:235
  10.1 8.0 %collective-permute-start.5 = (bf16[2,256,128]{2,1,0:T(8,128)(2,1)S(1)}, bf16[2,256,128]{2,1,0:T(8,128)(2,1)S(1)}, u32[]{:S(2)}, u32[]{:S(2)}) collective-permute-start(bf16[2,256,128]{2,1,0:T(8,128)(2,1)S(1)} %get-tuple-element.28), channel_id=1, source_target_pairs={{0,20},{4,16},{8,28},{12,24},{16,4},{20,0},{24,12},{28,8},{1,21},{... | collective-permute-start | bytes 393224 | tf_op jit(solution)/shard_map/ppermute | solution.py:235
  10.2 8.0 %collective-permute-start.6 = (bf16[2,256,128]{2,1,0:T(8,128)(2,1)S(1)}, bf16[2,256,128]{2,1,0:T(8,128)(2,1)S(1)}, u32[]{:S(2)}, u32[]{:S(2)}) collective-permute-start(bf16[2,256,128]{2,1,0:T(8,128)(2,1)S(1)} %get-tuple-element.29), channel_id=1, source_target_pairs={{0,4},{4,0},{8,12},{12,8},{16,20},{20,16},{24,28},{28,24},{1,5},{5... | collective-permute-start | bytes 393224 | tf_op jit(solution)/shard_map/ppermute | solution.py:235
  21.4 1.7 %collective-permute-start.7 = (s16[4,22,16,128]{3,2,1,0:T(8,128)(2,1)S(1)}, s16[4,22,16,128]{3,2,1,0:T(8,128)(2,1)S(1)}, u32[]{:S(2)}, u32[]{:S(2)}) collective-permute-start(s16[4,22,16,128]{3,2,1,0:T(8,128)(2,1)S(1)} %get-tuple-element.32), channel_id=1, source_target_pairs={{0,4},{4,0},{8,12},{12,8},{16,20},{20,16},{24,28},{28,24},{1,5},{5... | collective-permute-start | bytes 1081352 | tf_op jit(solution)/shard_map/ppermute | solution.py:235
  23.4 4.9 %collective-permute-start.8 = (s16[22,16,128]{2,1,0:T(8,128)(2,1)S(1)}, s16[22,16,128]{2,1,0:T(8,128)(2,1)S(1)}, u32[]{:S(2)}, u32[]{:S(2)}) collective-permute-start(s16[22,16,128]{2,1,0:T(8,128)(2,1)S(1)} %get-tuple-element.33), channel_id=1, source_target_pairs={{0,8},{4,12},{8,0},{12,4},{16,24},{20,28},{24,16},{28,20},{1,9},{5... | collective-permute-start | bytes 270344 | tf_op jit(solution)/shard_map/ppermute | solution.py:235
  24.2 6.4 %collective-permute-start.9 = (s16[22,16,128]{2,1,0:T(8,128)(2,1)S(1)}, s16[22,16,128]{2,1,0:T(8,128)(2,1)S(1)}, u32[]{:S(2)}, u32[]{:S(2)}) collective-permute-start(s16[22,16,128]{2,1,0:T(8,128)(2,1)S(1)} %get-tuple-element.34), channel_id=1, source_target_pairs={{0,16},{4,20},{8,24},{12,28},{16,0},{20,4},{24,8},{28,12},{1,17},{... | collective-permute-start | bytes 270344 | tf_op jit(solution)/shard_map/ppermute | solution.py:235
  24.7 6.0 %collective-permute-start.10 = (s16[22,16,128]{2,1,0:T(8,128)(2,1)S(1)}, s16[22,16,128]{2,1,0:T(8,128)(2,1)S(1)}, u32[]{:S(2)}, u32[]{:S(2)}) collective-permute-start(s16[22,16,128]{2,1,0:T(8,128)(2,1)S(1)} %get-tuple-element.35), channel_id=1, source_target_pairs={{0,24},{4,28},{8,16},{12,20},{16,8},{20,12},{24,0},{28,4},{1,25},{... | collective-permute-start | bytes 270344 | tf_op jit(solution)/shard_map/ppermute | solution.py:235
  30.8 4.9 %collective-permute-start.11 = (s16[7,16,128]{2,1,0:T(8,128)(2,1)S(1)}, s16[7,16,128]{2,1,0:T(8,128)(2,1)S(1)}, u32[]{:S(2)}, u32[]{:S(2)}) collective-permute-start(s16[7,16,128]{2,1,0:T(8,128)(2,1)S(1)} %get-tuple-element.37), channel_id=1, source_target_pairs={{0,2},{1,3},{2,0},{3,1},{4,6},{5,7},{6,4},{7,5},{8,10},{9,11},{10,... | collective-permute-start | bytes 86024 | tf_op jit(solution)/shard_map/ppermute | solution.py:235
  33.5 5.7 %collective-permute-start.12 = (s16[7,16,128]{2,1,0:T(8,128)(2,1)S(1)}, s16[7,16,128]{2,1,0:T(8,128)(2,1)S(1)}, u32[]{:S(2)}, u32[]{:S(2)}) collective-permute-start(s16[7,16,128]{2,1,0:T(8,128)(2,1)S(1)} %get-tuple-element.38), channel_id=1, source_target_pairs={{0,3},{1,2},{2,1},{3,0},{4,7},{5,6},{6,5},{7,4},{8,11},{9,10},{10,... | collective-permute-start | bytes 86024 | tf_op jit(solution)/shard_map/ppermute | solution.py:235
  34.9 4.3 %collective-permute-start.13 = (s16[7,16,128]{2,1,0:T(8,128)(2,1)S(1)}, s16[7,16,128]{2,1,0:T(8,128)(2,1)S(1)}, u32[]{:S(2)}, u32[]{:S(2)}) collective-permute-start(s16[7,16,128]{2,1,0:T(8,128)(2,1)S(1)} %get-tuple-element.39), channel_id=1, source_target_pairs={{0,1},{1,0},{2,3},{3,2},{4,5},{5,4},{6,7},{7,6},{8,9},{9,8},{10,11... | collective-permute-start | bytes 86024 | tf_op jit(solution)/shard_map/ppermute | solution.py:235

commit v20 on v18

--- a/solution.py
+++ b/solution.py
@@ -235,10 +235,11 @@
     ]
 
 
-def split_kernel(order, where_ref, spec_ref, *refs):
+def split_kernel(order, spec_ref, *refs):
     out_refs, sems = refs[:-1], refs[-1]
+    me = lax.axis_index("chan").astype(jnp.int32)
     copies = [
-        pltpu.make_async_copy(spec_ref.at[:, where_ref[0] ^ k], out_ref, sems.at[number])
+        pltpu.make_async_copy(spec_ref.at[:, me ^ k], out_ref, sems.at[number])
         for number, (k, out_ref) in enumerate(zip(order, out_refs))
     ]
     for copy in copies:
@@ -333,12 +334,12 @@
         pieces += pl.pallas_call(
             functools.partial(split_kernel, part),
             out_shape=[jax.ShapeDtypeStruct((2, band, chans), spectra.dtype)] * len(part),
-            in_specs=[smem, kept],
+            in_specs=[kept],
             out_specs=[pl.BlockSpec(memory_space=pl.ANY)] * len(part),
             scratch_shapes=[pltpu.SemaphoreType.DMA((len(part),))],
             compiler_params=params,
             name="split_windows",
-        )(chan_where, spectra)
+        )(spectra)
     chip_order = chips(chan_count)
     pair_shape = (6 * offset_count - 2, lag_rows, chans)
     own, far = pl.pallas_call(

time: 50.8 us -> 50.8 us (level)
  no operation moved by 1% of the time
where the time goes in v20:
time: 50.8 us; the launch traced here: 50.6 us
  waiting for transfers between devices  17.6 us (35%)
  starting transfers between devices  15.8 us (31%)
  blocking collectives  10.1 us (20%)
  Pallas kernels  7.05 us (14%)
    ppermute x14, waiting for transfers between devices, exchange(): lax.ppermute(piece, axis, [(source, source ^ k) for source in range(count)])  17.6 us
    ppermute x14, starting transfers between devices, exchange(): lax.ppermute(piece, axis, [(source, source ^ k) for source in range(count)])  15.8 us
    all_to_all x1, blocking collectives, window_shards(): lax.all_to_all(pieces.reshape(shape), ('chan', 'tm'), 0, 0, tiled=True)  10.1 us
    pallas_call x1, Pallas kernels, window_shards(): pl.pallas_call(functools.partial(window_kernel, chan_order), out_shape=[j...  3.26 us
    pallas_call x2, Pallas kernels, window_shards(): pl.pallas_call(functools.partial(split_kernel, part), out_shape=[jax.Shap...  2.32 us
  transfers between devices with their start and end apart: 14, of which 10 were waited for; matrix products, arithmetic and copies ran while one was open for 0% of the time, Pallas kernels for 2%

profile of v20, /device:TPU:0, one launch (start us, length us, event | category | flops | bytes accessed | tf_op | source)
XLA Modules:
  0.0 50.6 jit_solution(7978220165120442801)
XLA Ops:
  0.0 1.1 %split_windows.2 = (bf16[2,256,128]{2,1,0:T(8,128)(2,1)S(1)}, bf16[2,256,128]{2,1,0:T(8,128)(2,1)S(1)}) custom-call(bf16[2,8,256,128]{3,2,1,0:T(8,128)(2,1)} %spec_ref.3), custom_call_target="tpu_custom_call" | custom-call | tf_op jit(solution)/shard_map/split_windows/pallas_call | solution.py:334
  1.1 4.0 %collective-permute-start = (bf16[2,256,128]{2,1,0:T(8,128)(2,1)S(1)}, bf16[2,256,128]{2,1,0:T(8,128)(2,1)S(1)}, u32[]{:S(2)}, u32[]{:S(2)}) collective-permute-start(bf16[2,256,128]{2,1,0:T(8,128)(2,1)S(1)} %get-tuple-element.23), channel_id=1, source_target_pairs={{0,24},{4,28},{8,16},{12,20},{16,8},{20,12},{24,0},{28,4},{1,25},{... | collective-permute-start | bytes 393224 | tf_op jit(solution)/shard_map/ppermute | solution.py:233
  5.0 1.3 %split_windows.3 = (bf16[2,256,128]{2,1,0:T(8,128)(2,1)S(1)}, bf16[2,256,128]{2,1,0:T(8,128)(2,1)S(1)}, bf16[2,256,128]{2,1,0:T(8,128)(2,1)S(1)}, bf16[2,256,128...) custom-call(bf16[2,8,256,128]{3,2,1,0:T(8,128)(2,1)} %spec_ref.3), custom_call_target="tpu_custom_call" | custom-call | tf_op jit(solution)/shard_map/split_windows/pallas_call | solution.py:334
  6.3 1.2 %collective-permute-start.2 = (bf16[2,256,128]{2,1,0:T(8,128)(2,1)S(1)}, bf16[2,256,128]{2,1,0:T(8,128)(2,1)S(1)}, u32[]{:S(2)}, u32[]{:S(2)}) collective-permute-start(bf16[2,256,128]{2,1,0:T(8,128)(2,1)S(1)} %get-tuple-element.25), channel_id=1, source_target_pairs={{0,8},{4,12},{8,0},{12,4},{16,24},{20,28},{24,16},{28,20},{1,9},{5... | collective-permute-start | bytes 393224 | tf_op jit(solution)/shard_map/ppermute | solution.py:233
  7.5 1.5 %collective-permute-start.3 = (bf16[2,256,128]{2,1,0:T(8,128)(2,1)S(1)}, bf16[2,256,128]{2,1,0:T(8,128)(2,1)S(1)}, u32[]{:S(2)}, u32[]{:S(2)}) collective-permute-start(bf16[2,256,128]{2,1,0:T(8,128)(2,1)S(1)} %get-tuple-element.26), channel_id=1, source_target_pairs={{0,16},{4,20},{8,24},{12,28},{16,0},{20,4},{24,8},{28,12},{1,17},{... | collective-permute-start | bytes 393224 | tf_op jit(solution)/shard_map/ppermute | solution.py:233
  9.0 0.6 %collective-permute-start.4 = (bf16[2,256,128]{2,1,0:T(8,128)(2,1)S(1)}, bf16[2,256,128]{2,1,0:T(8,128)(2,1)S(1)}, u32[]{:S(2)}, u32[]{:S(2)}) collective-permute-start(bf16[2,256,128]{2,1,0:T(8,128)(2,1)S(1)} %get-tuple-element.27), channel_id=1, source_target_pairs={{0,12},{4,8},{8,4},{12,0},{16,28},{20,24},{24,20},{28,16},{1,13},{... | collective-permute-start | bytes 393224 | tf_op jit(solution)/shard_map/ppermute | solution.py:233
  9.6 0.6 %collective-permute-start.5 = (bf16[2,256,128]{2,1,0:T(8,128)(2,1)S(1)}, bf16[2,256,128]{2,1,0:T(8,128)(2,1)S(1)}, u32[]{:S(2)}, u32[]{:S(2)}) collective-permute-start(bf16[2,256,128]{2,1,0:T(8,128)(2,1)S(1)} %get-tuple-element.28), channel_id=1, source_target_pairs={{0,20},{4,16},{8,28},{12,24},{16,4},{20,0},{24,12},{28,8},{1,21},{... | collective-permute-start | bytes 393224 | tf_op jit(solution)/shard_map/ppermute | solution.py:233
  10.1 1.6 %collective-permute-done.1.refs_1_ = bf16[2,256,128]{2,1,0:T(8,128)(2,1)S(1)} collective-permute-done((bf16[2,256,128]{2,1,0:T(8,128)(2,1)S(1)}, bf16[2,256,128]{2,1,0:T(8,128)(2,1)S(1)}, u32[]{:S(2)}, u32[]{:S(2)}) %collective-permute-start.1) | collective-permute-done | bytes 131104 | tf_op jit(solution)/shard_map/ppermute | solution.py:233
  11.8 3.5 %collective-permute-done.2.refs_2_ = bf16[2,256,128]{2,1,0:T(8,128)(2,1)S(1)} collective-permute-done((bf16[2,256,128]{2,1,0:T(8,128)(2,1)S(1)}, bf16[2,256,128]{2,1,0:T(8,128)(2,1)S(1)}, u32[]{:S(2)}, u32[]{:S(2)}) %collective-permute-start.2) | collective-permute-done | bytes 131104 | tf_op jit(solution)/shard_map/ppermute | solution.py:233
  15.2 1.1 %collective-permute-done.4.refs_4_ = bf16[2,256,128]{2,1,0:T(8,128)(2,1)S(1)} collective-permute-done((bf16[2,256,128]{2,1,0:T(8,128)(2,1)S(1)}, bf16[2,256,128]{2,1,0:T(8,128)(2,1)S(1)}, u32[]{:S(2)}, u32[]{:S(2)}) %collective-permute-start.4) | collective-permute-done | bytes 131104 | tf_op jit(solution)/shard_map/ppermute | solution.py:233
  16.4 0.7 %collective-permute-done.5.refs_5_ = bf16[2,256,128]{2,1,0:T(8,128)(2,1)S(1)} collective-permute-done((bf16[2,256,128]{2,1,0:T(8,128)(2,1)S(1)}, bf16[2,256,128]{2,1,0:T(8,128)(2,1)S(1)}, u32[]{:S(2)}, u32[]{:S(2)}) %collective-permute-start.5) | collective-permute-done | bytes 131104 | tf_op jit(solution)/shard_map/ppermute | solution.py:233
  17.1 3.3 %window_pairs.1 = (s16[4,22,16,128]{3,2,1,0:T(8,128)(2,1)S(1)}, s16[4,22,16,128]{3,2,1,0:T(8,128)(2,1)S(1)}) custom-call(s32[4]{0:T(128)} %offs_hbm_ref.1, s32[1]{0:T(128)} %bitcast.1.where_ref, bf16[2,256,128]{2,1,0:T(8,128)(2,1)S(1)} %collective-permute-done.refs_0_, bf16[2,256,128]{2,1,0:T(8,128)(2,1)S(1)} %collective-permute-done.1.refs_1_, ...), custom_call_target="tpu_custom_call" | custom-call | tf_op jit(solution)/shard_map/window_pairs/pallas_call | solution.py:345
  20.5 1.6 %collective-permute-done.7.far_ref = s16[4,22,16,128]{3,2,1,0:T(8,128)(2,1)S(1)} collective-permute-done((s16[4,22,16,128]{3,2,1,0:T(8,128)(2,1)S(1)}, s16[4,22,16,128]{3,2,1,0:T(8,128)(2,1)S(1)}, u32[]{:S(2)}, u32[]{:S(2)}) %collective-permute-start.7) | collective-permute-done | bytes 360480 | tf_op jit(solution)/shard_map/ppermute | solution.py:233
  22.3 1.6 %collective-permute-start.8 = (s16[22,16,128]{2,1,0:T(8,128)(2,1)S(1)}, s16[22,16,128]{2,1,0:T(8,128)(2,1)S(1)}, u32[]{:S(2)}, u32[]{:S(2)}) collective-permute-start(s16[22,16,128]{2,1,0:T(8,128)(2,1)S(1)} %get-tuple-element.33), channel_id=1, source_target_pairs={{0,8},{4,12},{8,0},{12,4},{16,24},{20,28},{24,16},{28,20},{1,9},{5... | collective-permute-start | bytes 270344 | tf_op jit(solution)/shard_map/ppermute | solution.py:233
  23.9 1.6 %collective-permute-start.9 = (s16[22,16,128]{2,1,0:T(8,128)(2,1)S(1)}, s16[22,16,128]{2,1,0:T(8,128)(2,1)S(1)}, u32[]{:S(2)}, u32[]{:S(2)}) collective-permute-start(s16[22,16,128]{2,1,0:T(8,128)(2,1)S(1)} %get-tuple-element.34), channel_id=1, source_target_pairs={{0,16},{4,20},{8,24},{12,28},{16,0},{20,4},{24,8},{28,12},{1,17},{... | collective-permute-start | bytes 270344 | tf_op jit(solution)/shard_map/ppermute | solution.py:233
  25.8 1.2 %collective-permute-done.8.refs_0_ = s16[22,16,128]{2,1,0:T(8,128)(2,1)S(1)} collective-permute-done((s16[22,16,128]{2,1,0:T(8,128)(2,1)S(1)}, s16[22,16,128]{2,1,0:T(8,128)(2,1)S(1)}, u32[]{:S(2)}, u32[]{:S(2)}) %collective-permute-start.8) | collective-permute-done | bytes 90144 | tf_op jit(solution)/shard_map/ppermute | solution.py:233
  27.0 2.4 %collective-permute-done.9.refs_1_ = s16[22,16,128]{2,1,0:T(8,128)(2,1)S(1)} collective-permute-done((s16[22,16,128]{2,1,0:T(8,128)(2,1)S(1)}, s16[22,16,128]{2,1,0:T(8,128)(2,1)S(1)}, u32[]{:S(2)}, u32[]{:S(2)}) %collective-permute-start.9) | collective-permute-done | bytes 90144 | tf_op jit(solution)/shard_map/ppermute | solution.py:233
  29.4 1.5 %collective-permute-done.10.refs_2_ = s16[22,16,128]{2,1,0:T(8,128)(2,1)S(1)} collective-permute-done((s16[22,16,128]{2,1,0:T(8,128)(2,1)S(1)}, s16[22,16,128]{2,1,0:T(8,128)(2,1)S(1)}, u32[]{:S(2)}, u32[]{:S(2)}) %collective-permute-start.10) | collective-permute-done | bytes 90144 | tf_op jit(solution)/shard_map/ppermute | solution.py:233
  31.0 2.7 %collective-permute-start.11 = (s16[7,16,128]{2,1,0:T(8,128)(2,1)S(1)}, s16[7,16,128]{2,1,0:T(8,128)(2,1)S(1)}, u32[]{:S(2)}, u32[]{:S(2)}) collective-permute-start(s16[7,16,128]{2,1,0:T(8,128)(2,1)S(1)} %get-tuple-element.37), channel_id=1, source_target_pairs={{0,2},{1,3},{2,0},{3,1},{4,6},{5,7},{6,4},{7,5},{8,10},{9,11},{10,... | collective-permute-start | bytes 86024 | tf_op jit(solution)/shard_map/ppermute | solution.py:233
  33.7 1.3 %collective-permute-start.12 = (s16[7,16,128]{2,1,0:T(8,128)(2,1)S(1)}, s16[7,16,128]{2,1,0:T(8,128)(2,1)S(1)}, u32[]{:S(2)}, u32[]{:S(2)}) collective-permute-start(s16[7,16,128]{2,1,0:T(8,128)(2,1)S(1)} %get-tuple-element.38), channel_id=1, source_target_pairs={{0,3},{1,2},{2,1},{3,0},{4,7},{5,6},{6,5},{7,4},{8,11},{9,10},{10,... | collective-permute-start | bytes 86024 | tf_op jit(solution)/shard_map/ppermute | solution.py:233
  35.2 0.9 %collective-permute-done.11.refs_0_ = s16[7,16,128]{2,1,0:T(8,128)(2,1)S(1)} collective-permute-done((s16[7,16,128]{2,1,0:T(8,128)(2,1)S(1)}, s16[7,16,128]{2,1,0:T(8,128)(2,1)S(1)}, u32[]{:S(2)}, u32[]{:S(2)}) %collective-permute-start.11) | collective-permute-done | bytes 28704 | tf_op jit(solution)/shard_map/ppermute | solution.py:233
  36.1 3.2 %collective-permute-done.12.refs_1_ = s16[7,16,128]{2,1,0:T(8,128)(2,1)S(1)} collective-permute-done((s16[7,16,128]{2,1,0:T(8,128)(2,1)S(1)}, s16[7,16,128]{2,1,0:T(8,128)(2,1)S(1)}, u32[]{:S(2)}, u32[]{:S(2)}) %collective-permute-start.12) | collective-permute-done | bytes 28704 | tf_op jit(solution)/shard_map/ppermute | solution.py:233
  39.5 10.1 %all_to_all.5 = f32[32,4,128]{2,1,0:T(4,128)S(1)} all-to-all(f32[32,4,128]{2,1,0:T(4,128)S(1)} %bitcast.5), channel_id=1, replica_groups=mesh['chan'=8,'tm'=4] {'chan','tm'}, dimensions={0} | all-to-all | bytes 131072 | tf_op jit(solution)/shard_map/all_to_all | solution.py:386
  49.7 0.9 %place_lags.1 = f32[16,4,256]{2,1,0:T(4,128)} custom-call(f32[8,4,4,128]{3,2,1,0:T(4,128)S(1)} %bitcast.4), custom_call_target="tpu_custom_call" | custom-call | tf_op jit(solution)/shard_map/place_lags/pallas_call | solution.py:387
  (16 shorter events, 1.4 us)
Async XLA Ops:
  0.0 17.1 %copy-start = (bf16[2,8,16,2048]{3,2,1,0:T(8,128)(2,1)S(1)}, bf16[2,8,16,2048]{3,2,1,0:T(8,128)(2,1)}, u32[]{:S(2)}) copy-start(bf16[2,8,16,2048]{3,2,1,0:T(8,128)(2,1)} %constant.11.clone.refs_9_) | copy-start | bytes 3145732
  1.1 8.5 %collective-permute-start = (bf16[2,256,128]{2,1,0:T(8,128)(2,1)S(1)}, bf16[2,256,128]{2,1,0:T(8,128)(2,1)S(1)}, u32[]{:S(2)}, u32[]{:S(2)}) collective-permute-start(bf16[2,256,128]{2,1,0:T(8,128)(2,1)S(1)} %get-tuple-element.23), channel_id=1, source_target_pairs={{0,24},{4,28},{8,16},{12,20},{16,8},{20,12},{24,0},{28,4},{1,25},{... | collective-permute-start | bytes 393224 | tf_op jit(solution)/shard_map/ppermute | solution.py:233
  5.0 6.7 %collective-permute-start.1 = (bf16[2,256,128]{2,1,0:T(8,128)(2,1)S(1)}, bf16[2,256,128]{2,1,0:T(8,128)(2,1)S(1)}, u32[]{:S(2)}, u32[]{:S(2)}) collective-permute-start(bf16[2,256,128]{2,1,0:T(8,128)(2,1)S(1)} %get-tuple-element.24), channel_id=1, source_target_pairs={{0,28},{4,24},{8,20},{12,16},{16,12},{20,8},{24,4},{28,0},{1,29},{... | collective-permute-start | bytes 393224 | tf_op jit(solution)/shard_map/ppermute | solution.py:233
  6.3 8.9 %collective-permute-start.2 = (bf16[2,256,128]{2,1,0:T(8,128)(2,1)S(1)}, bf16[2,256,128]{2,1,0:T(8,128)(2,1)S(1)}, u32[]{:S(2)}, u32[]{:S(2)}) collective-permute-start(bf16[2,256,128]{2,1,0:T(8,128)(2,1)S(1)} %get-tuple-element.25), channel_id=1, source_target_pairs={{0,8},{4,12},{8,0},{12,4},{16,24},{20,28},{24,16},{28,20},{1,9},{5... | collective-permute-start | bytes 393224 | tf_op jit(solution)/shard_map/ppermute | solution.py:233
  7.5 7.7 %collective-permute-start.3 = (bf16[2,256,128]{2,1,0:T(8,128)(2,1)S(1)}, bf16[2,256,128]{2,1,0:T(8,128)(2,1)S(1)}, u32[]{:S(2)}, u32[]{:S(2)}) collective-permute-start(bf16[2,256,128]{2,1,0:T(8,128)(2,1)S(1)} %get-tuple-element.26), channel_id=1, source_target_pairs={{0,16},{4,20},{8,24},{12,28},{16,0},{20,4},{24,8},{28,12},{1,17},{... | collective-permute-start | bytes 393224 | tf_op jit(solution)/shard_map/ppermute | solution.py:233
  9.0 7.4 %collective-permute-start.4 = (bf16[2,256,128]{2,1,0:T(8,128)(2,1)S(1)}, bf16[2,256,128]{2,1,0:T(8,128)(2,1)S(1)}, u32[]{:S(2)}, u32[]{:S(2)}) collective-permute-start(bf16[2,256,128]{2,1,0:T(8,128)(2,1)S(1)} %get-tuple-element.27), channel_id=1, source_target_pairs={{0,12},{4,8},{8,4},{12,0},{16,28},{20,24},{24,20},{28,16},{1,13},{... | collective-permute-start | bytes 393224 | tf_op jit(solution)/shard_map/ppermute | solution.py:233
  9.6 7.5 %collective-permute-start.5 = (bf16[2,256,128]{2,1,0:T(8,128)(2,1)S(1)}, bf16[2,256,128]{2,1,0:T(8,128)(2,1)S(1)}, u32[]{:S(2)}, u32[]{:S(2)}) collective-permute-start(bf16[2,256,128]{2,1,0:T(8,128)(2,1)S(1)} %get-tuple-element.28), channel_id=1, source_target_pairs={{0,20},{4,16},{8,28},{12,24},{16,4},{20,0},{24,12},{28,8},{1,21},{... | collective-permute-start | bytes 393224 | tf_op jit(solution)/shard_map/ppermute | solution.py:233
  11.8 5.3 %collective-permute-start.6 = (bf16[2,256,128]{2,1,0:T(8,128)(2,1)S(1)}, bf16[2,256,128]{2,1,0:T(8,128)(2,1)S(1)}, u32[]{:S(2)}, u32[]{:S(2)}) collective-permute-start(bf16[2,256,128]{2,1,0:T(8,128)(2,1)S(1)} %get-tuple-element.29), channel_id=1, source_target_pairs={{0,4},{4,0},{8,12},{12,8},{16,20},{20,16},{24,28},{28,24},{1,5},{5... | collective-permute-start | bytes 393224 | tf_op jit(solution)/shard_map/ppermute | solution.py:233
  11.8 5.3 %copy-start.1 = (s32[8,128]{1,0:T(8,128)S(1)}, s32[8,128]{1,0:T(8,128)}, u32[]{:S(2)}) copy-start(s32[8,128]{1,0:T(8,128)} %refs_8_.1) | copy-start | bytes 12292
  20.3 1.7 %collective-permute-start.7 = (s16[4,22,16,128]{3,2,1,0:T(8,128)(2,1)S(1)}, s16[4,22,16,128]{3,2,1,0:T(8,128)(2,1)S(1)}, u32[]{:S(2)}, u32[]{:S(2)}) collective-permute-start(s16[4,22,16,128]{3,2,1,0:T(8,128)(2,1)S(1)} %get-tuple-element.32), channel_id=1, source_target_pairs={{0,4},{4,0},{8,12},{12,8},{16,20},{20,16},{24,28},{28,24},{1,5},{5... | collective-permute-start | bytes 1081352 | tf_op jit(solution)/shard_map/ppermute | solution.py:233
  22.3 4.7 %collective-permute-start.8 = (s16[22,16,128]{2,1,0:T(8,128)(2,1)S(1)}, s16[22,16,128]{2,1,0:T(8,128)(2,1)S(1)}, u32[]{:S(2)}, u32[]{:S(2)}) collective-permute-start(s16[22,16,128]{2,1,0:T(8,128)(2,1)S(1)} %get-tuple-element.33), channel_id=1, source_target_pairs={{0,8},{4,12},{8,0},{12,4},{16,24},{20,28},{24,16},{28,20},{1,9},{5... | collective-permute-start | bytes 270344 | tf_op jit(solution)/shard_map/ppermute | solution.py:233
  23.9 5.5 %collective-permute-start.9 = (s16[22,16,128]{2,1,0:T(8,128)(2,1)S(1)}, s16[22,16,128]{2,1,0:T(8,128)(2,1)S(1)}, u32[]{:S(2)}, u32[]{:S(2)}) collective-permute-start(s16[22,16,128]{2,1,0:T(8,128)(2,1)S(1)} %get-tuple-element.34), channel_id=1, source_target_pairs={{0,16},{4,20},{8,24},{12,28},{16,0},{20,4},{24,8},{28,12},{1,17},{... | collective-permute-start | bytes 270344 | tf_op jit(solution)/shard_map/ppermute | solution.py:233
  25.4 5.4 %collective-permute-start.10 = (s16[22,16,128]{2,1,0:T(8,128)(2,1)S(1)}, s16[22,16,128]{2,1,0:T(8,128)(2,1)S(1)}, u32[]{:S(2)}, u32[]{:S(2)}) collective-permute-start(s16[22,16,128]{2,1,0:T(8,128)(2,1)S(1)} %get-tuple-element.35), channel_id=1, source_target_pairs={{0,24},{4,28},{8,16},{12,20},{16,8},{20,12},{24,0},{28,4},{1,25},{... | collective-permute-start | bytes 270344 | tf_op jit(solution)/shard_map/ppermute | solution.py:233
  31.0 5.1 %collective-permute-start.11 = (s16[7,16,128]{2,1,0:T(8,128)(2,1)S(1)}, s16[7,16,128]{2,1,0:T(8,128)(2,1)S(1)}, u32[]{:S(2)}, u32[]{:S(2)}) collective-permute-start(s16[7,16,128]{2,1,0:T(8,128)(2,1)S(1)} %get-tuple-element.37), channel_id=1, source_target_pairs={{0,2},{1,3},{2,0},{3,1},{4,6},{5,7},{6,4},{7,5},{8,10},{9,11},{10,... | collective-permute-start | bytes 86024 | tf_op jit(solution)/shard_map/ppermute | solution.py:233
  33.7 5.7 %collective-permute-start.12 = (s16[7,16,128]{2,1,0:T(8,128)(2,1)S(1)}, s16[7,16,128]{2,1,0:T(8,128)(2,1)S(1)}, u32[]{:S(2)}, u32[]{:S(2)}) collective-permute-start(s16[7,16,128]{2,1,0:T(8,128)(2,1)S(1)} %get-tuple-element.38), channel_id=1, source_target_pairs={{0,3},{1,2},{2,1},{3,0},{4,7},{5,6},{6,5},{7,4},{8,11},{9,10},{10,... | collective-permute-start | bytes 86024 | tf_op jit(solution)/shard_map/ppermute | solution.py:233
  35.0 4.3 %collective-permute-start.13 = (s16[7,16,128]{2,1,0:T(8,128)(2,1)S(1)}, s16[7,16,128]{2,1,0:T(8,128)(2,1)S(1)}, u32[]{:S(2)}, u32[]{:S(2)}) collective-permute-start(s16[7,16,128]{2,1,0:T(8,128)(2,1)S(1)} %get-tuple-element.39), channel_id=1, source_target_pairs={{0,1},{1,0},{2,3},{3,2},{4,5},{5,4},{6,7},{7,6},{8,9},{9,8},{10,11... | collective-permute-start | bytes 86024 | tf_op jit(solution)/shard_map/ppermute | solution.py:233

commit v21 on v20

--- a/solution.py
+++ b/solution.py
@@ -238,9 +238,17 @@
 def split_kernel(order, spec_ref, *refs):
     out_refs, sems = refs[:-1], refs[-1]
     me = lax.axis_index("chan").astype(jnp.int32)
+    chunks = sems.shape[2]
+    rows = spec_ref.shape[2] // chunks
     copies = [
-        pltpu.make_async_copy(spec_ref.at[:, me ^ k], out_ref, sems.at[number])
+        pltpu.make_async_copy(
+            spec_ref.at[part, me ^ k, pl.ds(chunk * rows, rows)],
+            out_ref.at[part, pl.ds(chunk * rows, rows)],
+            sems.at[number, part, chunk],
+        )
         for number, (k, out_ref) in enumerate(zip(order, out_refs))
+        for part in range(2)
+        for chunk in range(chunks)
     ]
     for copy in copies:
         copy.start()
@@ -336,7 +344,7 @@
             out_shape=[jax.ShapeDtypeStruct((2, band, chans), spectra.dtype)] * len(part),
             in_specs=[kept],
             out_specs=[pl.BlockSpec(memory_space=pl.ANY)] * len(part),
-            scratch_shapes=[pltpu.SemaphoreType.DMA((len(part),))],
+            scratch_shapes=[pltpu.SemaphoreType.DMA((len(part), 2, 4))],
             compiler_params=params,
             name="split_windows",
         )(spectra)

time: 50.8 us -> 51.1 us (level)
  transfers between devices with their start and end apart: 14 -> 14, of which waited for: 10 -> 10; matrix products, arithmetic and copies ran while one was open for 0% -> 0% of each run, Pallas kernels for 2% -> 3%
where the time goes in v21:
time: 51.1 us; the launch traced here: 50.6 us
  waiting for transfers between devices  17.3 us (34%)
  starting transfers between devices  15.8 us (31%)
  blocking collectives  10.2 us (20%)
  Pallas kernels  7.33 us (14%)
    ppermute x14, waiting for transfers between devices, exchange(): lax.ppermute(piece, axis, [(source, source ^ k) for source in range(count)])  17.3 us
    ppermute x14, starting transfers between devices, exchange(): lax.ppermute(piece, axis, [(source, source ^ k) for source in range(count)])  15.8 us
    all_to_all x1, blocking collectives, window_shards(): lax.all_to_all(pieces.reshape(shape), ('chan', 'tm'), 0, 0, tiled=True)  10.2 us
    pallas_call x1, Pallas kernels, window_shards(): pl.pallas_call(functools.partial(window_kernel, chan_order), out_shape=[j...  3.25 us
    pallas_call x2, Pallas kernels, window_shards(): pl.pallas_call(functools.partial(split_kernel, part), out_shape=[jax.Shap...  2.6 us
  transfers between devices with their start and end apart: 14, of which 10 were waited for; matrix products, arithmetic and copies ran while one was open for 0% of the time, Pallas kernels for 3%

profile of v21, /device:TPU:0, one launch (start us, length us, event | category | flops | bytes accessed | tf_op | source)
XLA Modules:
  0.0 50.6 jit_solution(7690884073469633439)
XLA Ops:
  0.0 1.1 %split_windows.2 = (bf16[2,256,128]{2,1,0:T(8,128)(2,1)S(1)}, bf16[2,256,128]{2,1,0:T(8,128)(2,1)S(1)}) custom-call(bf16[2,8,256,128]{3,2,1,0:T(8,128)(2,1)} %spec_ref.3), custom_call_target="tpu_custom_call" | custom-call | tf_op jit(solution)/shard_map/split_windows/pallas_call | solution.py:342
  1.1 4.0 %collective-permute-start = (bf16[2,256,128]{2,1,0:T(8,128)(2,1)S(1)}, bf16[2,256,128]{2,1,0:T(8,128)(2,1)S(1)}, u32[]{:S(2)}, u32[]{:S(2)}) collective-permute-start(bf16[2,256,128]{2,1,0:T(8,128)(2,1)S(1)} %get-tuple-element.23), channel_id=1, source_target_pairs={{0,24},{4,28},{8,16},{12,20},{16,8},{20,12},{24,0},{28,4},{1,25},{... | collective-permute-start | bytes 393224 | tf_op jit(solution)/shard_map/ppermute | solution.py:233
  5.1 1.5 %split_windows.3 = (bf16[2,256,128]{2,1,0:T(8,128)(2,1)S(1)}, bf16[2,256,128]{2,1,0:T(8,128)(2,1)S(1)}, bf16[2,256,128]{2,1,0:T(8,128)(2,1)S(1)}, bf16[2,256,128...) custom-call(bf16[2,8,256,128]{3,2,1,0:T(8,128)(2,1)} %spec_ref.3), custom_call_target="tpu_custom_call" | custom-call | tf_op jit(solution)/shard_map/split_windows/pallas_call | solution.py:342
  6.6 1.2 %collective-permute-start.2 = (bf16[2,256,128]{2,1,0:T(8,128)(2,1)S(1)}, bf16[2,256,128]{2,1,0:T(8,128)(2,1)S(1)}, u32[]{:S(2)}, u32[]{:S(2)}) collective-permute-start(bf16[2,256,128]{2,1,0:T(8,128)(2,1)S(1)} %get-tuple-element.25), channel_id=1, source_target_pairs={{0,8},{4,12},{8,0},{12,4},{16,24},{20,28},{24,16},{28,20},{1,9},{5... | collective-permute-start | bytes 393224 | tf_op jit(solution)/shard_map/ppermute | solution.py:233
  7.8 1.5 %collective-permute-start.3 = (bf16[2,256,128]{2,1,0:T(8,128)(2,1)S(1)}, bf16[2,256,128]{2,1,0:T(8,128)(2,1)S(1)}, u32[]{:S(2)}, u32[]{:S(2)}) collective-permute-start(bf16[2,256,128]{2,1,0:T(8,128)(2,1)S(1)} %get-tuple-element.26), channel_id=1, source_target_pairs={{0,16},{4,20},{8,24},{12,28},{16,0},{20,4},{24,8},{28,12},{1,17},{... | collective-permute-start | bytes 393224 | tf_op jit(solution)/shard_map/ppermute | solution.py:233
  9.3 0.6 %collective-permute-start.4 = (bf16[2,256,128]{2,1,0:T(8,128)(2,1)S(1)}, bf16[2,256,128]{2,1,0:T(8,128)(2,1)S(1)}, u32[]{:S(2)}, u32[]{:S(2)}) collective-permute-start(bf16[2,256,128]{2,1,0:T(8,128)(2,1)S(1)} %get-tuple-element.27), channel_id=1, source_target_pairs={{0,12},{4,8},{8,4},{12,0},{16,28},{20,24},{24,20},{28,16},{1,13},{... | collective-permute-start | bytes 393224 | tf_op jit(solution)/shard_map/ppermute | solution.py:233
  9.9 0.6 %collective-permute-start.5 = (bf16[2,256,128]{2,1,0:T(8,128)(2,1)S(1)}, bf16[2,256,128]{2,1,0:T(8,128)(2,1)S(1)}, u32[]{:S(2)}, u32[]{:S(2)}) collective-permute-start(bf16[2,256,128]{2,1,0:T(8,128)(2,1)S(1)} %get-tuple-element.28), channel_id=1, source_target_pairs={{0,20},{4,16},{8,28},{12,24},{16,4},{20,0},{24,12},{28,8},{1,21},{... | collective-permute-start | bytes 393224 | tf_op jit(solution)/shard_map/ppermute | solution.py:233
  10.4 1.4 %collective-permute-done.1.refs_1_ = bf16[2,256,128]{2,1,0:T(8,128)(2,1)S(1)} collective-permute-done((bf16[2,256,128]{2,1,0:T(8,128)(2,1)S(1)}, bf16[2,256,128]{2,1,0:T(8,128)(2,1)S(1)}, u32[]{:S(2)}, u32[]{:S(2)}) %collective-permute-start.1) | collective-permute-done | bytes 131104 | tf_op jit(solution)/shard_map/ppermute | solution.py:233
  11.8 3.5 %collective-permute-done.2.refs_2_ = bf16[2,256,128]{2,1,0:T(8,128)(2,1)S(1)} collective-permute-done((bf16[2,256,128]{2,1,0:T(8,128)(2,1)S(1)}, bf16[2,256,128]{2,1,0:T(8,128)(2,1)S(1)}, u32[]{:S(2)}, u32[]{:S(2)}) %collective-permute-start.2) | collective-permute-done | bytes 131104 | tf_op jit(solution)/shard_map/ppermute | solution.py:233
  15.3 1.1 %collective-permute-done.4.refs_4_ = bf16[2,256,128]{2,1,0:T(8,128)(2,1)S(1)} collective-permute-done((bf16[2,256,128]{2,1,0:T(8,128)(2,1)S(1)}, bf16[2,256,128]{2,1,0:T(8,128)(2,1)S(1)}, u32[]{:S(2)}, u32[]{:S(2)}) %collective-permute-start.4) | collective-permute-done | bytes 131104 | tf_op jit(solution)/shard_map/ppermute | solution.py:233
  16.4 0.7 %collective-permute-done.5.refs_5_ = bf16[2,256,128]{2,1,0:T(8,128)(2,1)S(1)} collective-permute-done((bf16[2,256,128]{2,1,0:T(8,128)(2,1)S(1)}, bf16[2,256,128]{2,1,0:T(8,128)(2,1)S(1)}, u32[]{:S(2)}, u32[]{:S(2)}) %collective-permute-start.5) | collective-permute-done | bytes 131104 | tf_op jit(solution)/shard_map/ppermute | solution.py:233
  17.1 3.3 %window_pairs.1 = (s16[4,22,16,128]{3,2,1,0:T(8,128)(2,1)S(1)}, s16[4,22,16,128]{3,2,1,0:T(8,128)(2,1)S(1)}) custom-call(s32[4]{0:T(128)} %offs_hbm_ref.1, s32[1]{0:T(128)} %bitcast.1.where_ref, bf16[2,256,128]{2,1,0:T(8,128)(2,1)S(1)} %collective-permute-done.refs_0_, bf16[2,256,128]{2,1,0:T(8,128)(2,1)S(1)} %collective-permute-done.1.refs_1_, ...), custom_call_target="tpu_custom_call" | custom-call | tf_op jit(solution)/shard_map/window_pairs/pallas_call | solution.py:353
  20.5 1.6 %collective-permute-done.7.far_ref = s16[4,22,16,128]{3,2,1,0:T(8,128)(2,1)S(1)} collective-permute-done((s16[4,22,16,128]{3,2,1,0:T(8,128)(2,1)S(1)}, s16[4,22,16,128]{3,2,1,0:T(8,128)(2,1)S(1)}, u32[]{:S(2)}, u32[]{:S(2)}) %collective-permute-start.7) | collective-permute-done | bytes 360480 | tf_op jit(solution)/shard_map/ppermute | solution.py:233
  22.3 1.6 %collective-permute-start.8 = (s16[22,16,128]{2,1,0:T(8,128)(2,1)S(1)}, s16[22,16,128]{2,1,0:T(8,128)(2,1)S(1)}, u32[]{:S(2)}, u32[]{:S(2)}) collective-permute-start(s16[22,16,128]{2,1,0:T(8,128)(2,1)S(1)} %get-tuple-element.33), channel_id=1, source_target_pairs={{0,8},{4,12},{8,0},{12,4},{16,24},{20,28},{24,16},{28,20},{1,9},{5... | collective-permute-start | bytes 270344 | tf_op jit(solution)/shard_map/ppermute | solution.py:233
  23.9 1.6 %collective-permute-start.9 = (s16[22,16,128]{2,1,0:T(8,128)(2,1)S(1)}, s16[22,16,128]{2,1,0:T(8,128)(2,1)S(1)}, u32[]{:S(2)}, u32[]{:S(2)}) collective-permute-start(s16[22,16,128]{2,1,0:T(8,128)(2,1)S(1)} %get-tuple-element.34), channel_id=1, source_target_pairs={{0,16},{4,20},{8,24},{12,28},{16,0},{20,4},{24,8},{28,12},{1,17},{... | collective-permute-start | bytes 270344 | tf_op jit(solution)/shard_map/ppermute | solution.py:233
  25.8 1.2 %collective-permute-done.8.refs_0_ = s16[22,16,128]{2,1,0:T(8,128)(2,1)S(1)} collective-permute-done((s16[22,16,128]{2,1,0:T(8,128)(2,1)S(1)}, s16[22,16,128]{2,1,0:T(8,128)(2,1)S(1)}, u32[]{:S(2)}, u32[]{:S(2)}) %collective-permute-start.8) | collective-permute-done | bytes 90144 | tf_op jit(solution)/shard_map/ppermute | solution.py:233
  27.0 2.4 %collective-permute-done.9.refs_1_ = s16[22,16,128]{2,1,0:T(8,128)(2,1)S(1)} collective-permute-done((s16[22,16,128]{2,1,0:T(8,128)(2,1)S(1)}, s16[22,16,128]{2,1,0:T(8,128)(2,1)S(1)}, u32[]{:S(2)}, u32[]{:S(2)}) %collective-permute-start.9) | collective-permute-done | bytes 90144 | tf_op jit(solution)/shard_map/ppermute | solution.py:233
  29.4 1.5 %collective-permute-done.10.refs_2_ = s16[22,16,128]{2,1,0:T(8,128)(2,1)S(1)} collective-permute-done((s16[22,16,128]{2,1,0:T(8,128)(2,1)S(1)}, s16[22,16,128]{2,1,0:T(8,128)(2,1)S(1)}, u32[]{:S(2)}, u32[]{:S(2)}) %collective-permute-start.10) | collective-permute-done | bytes 90144 | tf_op jit(solution)/shard_map/ppermute | solution.py:233
  31.0 2.7 %collective-permute-start.11 = (s16[7,16,128]{2,1,0:T(8,128)(2,1)S(1)}, s16[7,16,128]{2,1,0:T(8,128)(2,1)S(1)}, u32[]{:S(2)}, u32[]{:S(2)}) collective-permute-start(s16[7,16,128]{2,1,0:T(8,128)(2,1)S(1)} %get-tuple-element.37), channel_id=1, source_target_pairs={{0,2},{1,3},{2,0},{3,1},{4,6},{5,7},{6,4},{7,5},{8,10},{9,11},{10,... | collective-permute-start | bytes 86024 | tf_op jit(solution)/shard_map/ppermute | solution.py:233
  33.7 1.3 %collective-permute-start.12 = (s16[7,16,128]{2,1,0:T(8,128)(2,1)S(1)}, s16[7,16,128]{2,1,0:T(8,128)(2,1)S(1)}, u32[]{:S(2)}, u32[]{:S(2)}) collective-permute-start(s16[7,16,128]{2,1,0:T(8,128)(2,1)S(1)} %get-tuple-element.38), channel_id=1, source_target_pairs={{0,3},{1,2},{2,1},{3,0},{4,7},{5,6},{6,5},{7,4},{8,11},{9,10},{10,... | collective-permute-start | bytes 86024 | tf_op jit(solution)/shard_map/ppermute | solution.py:233
  35.3 0.9 %collective-permute-done.11.refs_0_ = s16[7,16,128]{2,1,0:T(8,128)(2,1)S(1)} collective-permute-done((s16[7,16,128]{2,1,0:T(8,128)(2,1)S(1)}, s16[7,16,128]{2,1,0:T(8,128)(2,1)S(1)}, u32[]{:S(2)}, u32[]{:S(2)}) %collective-permute-start.11) | collective-permute-done | bytes 28704 | tf_op jit(solution)/shard_map/ppermute | solution.py:233
  36.1 3.2 %collective-permute-done.12.refs_1_ = s16[7,16,128]{2,1,0:T(8,128)(2,1)S(1)} collective-permute-done((s16[7,16,128]{2,1,0:T(8,128)(2,1)S(1)}, s16[7,16,128]{2,1,0:T(8,128)(2,1)S(1)}, u32[]{:S(2)}, u32[]{:S(2)}) %collective-permute-start.12) | collective-permute-done | bytes 28704 | tf_op jit(solution)/shard_map/ppermute | solution.py:233
  39.6 10.2 %all_to_all.5 = f32[32,4,128]{2,1,0:T(4,128)S(1)} all-to-all(f32[32,4,128]{2,1,0:T(4,128)S(1)} %bitcast.5), channel_id=1, replica_groups=mesh['chan'=8,'tm'=4] {'chan','tm'}, dimensions={0} | all-to-all | bytes 131072 | tf_op jit(solution)/shard_map/all_to_all | solution.py:394
  49.7 0.9 %place_lags.1 = f32[16,4,256]{2,1,0:T(4,128)} custom-call(f32[8,4,4,128]{3,2,1,0:T(4,128)S(1)} %bitcast.4), custom_call_target="tpu_custom_call" | custom-call | tf_op jit(solution)/shard_map/place_lags/pallas_call | solution.py:395
  (16 shorter events, 1.4 us)
Async XLA Ops:
  0.0 17.1 %copy-start = (bf16[2,8,16,2048]{3,2,1,0:T(8,128)(2,1)S(1)}, bf16[2,8,16,2048]{3,2,1,0:T(8,128)(2,1)}, u32[]{:S(2)}) copy-start(bf16[2,8,16,2048]{3,2,1,0:T(8,128)(2,1)} %constant.11.clone.refs_9_) | copy-start | bytes 3145732
  1.1 8.8 %collective-permute-start = (bf16[2,256,128]{2,1,0:T(8,128)(2,1)S(1)}, bf16[2,256,128]{2,1,0:T(8,128)(2,1)S(1)}, u32[]{:S(2)}, u32[]{:S(2)}) collective-permute-start(bf16[2,256,128]{2,1,0:T(8,128)(2,1)S(1)} %get-tuple-element.23), channel_id=1, source_target_pairs={{0,24},{4,28},{8,16},{12,20},{16,8},{20,12},{24,0},{28,4},{1,25},{... | collective-permute-start | bytes 393224 | tf_op jit(solution)/shard_map/ppermute | solution.py:233
  5.1 6.7 %collective-permute-start.1 = (bf16[2,256,128]{2,1,0:T(8,128)(2,1)S(1)}, bf16[2,256,128]{2,1,0:T(8,128)(2,1)S(1)}, u32[]{:S(2)}, u32[]{:S(2)}) collective-permute-start(bf16[2,256,128]{2,1,0:T(8,128)(2,1)S(1)} %get-tuple-element.24), channel_id=1, source_target_pairs={{0,28},{4,24},{8,20},{12,16},{16,12},{20,8},{24,4},{28,0},{1,29},{... | collective-permute-start | bytes 393224 | tf_op jit(solution)/shard_map/ppermute | solution.py:233
  6.6 8.7 %collective-permute-start.2 = (bf16[2,256,128]{2,1,0:T(8,128)(2,1)S(1)}, bf16[2,256,128]{2,1,0:T(8,128)(2,1)S(1)}, u32[]{:S(2)}, u32[]{:S(2)}) collective-permute-start(bf16[2,256,128]{2,1,0:T(8,128)(2,1)S(1)} %get-tuple-element.25), channel_id=1, source_target_pairs={{0,8},{4,12},{8,0},{12,4},{16,24},{20,28},{24,16},{28,20},{1,9},{5... | collective-permute-start | bytes 393224 | tf_op jit(solution)/shard_map/ppermute | solution.py:233
  7.8 7.5 %collective-permute-start.3 = (bf16[2,256,128]{2,1,0:T(8,128)(2,1)S(1)}, bf16[2,256,128]{2,1,0:T(8,128)(2,1)S(1)}, u32[]{:S(2)}, u32[]{:S(2)}) collective-permute-start(bf16[2,256,128]{2,1,0:T(8,128)(2,1)S(1)} %get-tuple-element.26), channel_id=1, source_target_pairs={{0,16},{4,20},{8,24},{12,28},{16,0},{20,4},{24,8},{28,12},{1,17},{... | collective-permute-start | bytes 393224 | tf_op jit(solution)/shard_map/ppermute | solution.py:233
  9.3 7.1 %collective-permute-start.4 = (bf16[2,256,128]{2,1,0:T(8,128)(2,1)S(1)}, bf16[2,256,128]{2,1,0:T(8,128)(2,1)S(1)}, u32[]{:S(2)}, u32[]{:S(2)}) collective-permute-start(bf16[2,256,128]{2,1,0:T(8,128)(2,1)S(1)} %get-tuple-element.27), channel_id=1, source_target_pairs={{0,12},{4,8},{8,4},{12,0},{16,28},{20,24},{24,20},{28,16},{1,13},{... | collective-permute-start | bytes 393224 | tf_op jit(solution)/shard_map/ppermute | solution.py:233
  9.9 7.2 %collective-permute-start.5 = (bf16[2,256,128]{2,1,0:T(8,128)(2,1)S(1)}, bf16[2,256,128]{2,1,0:T(8,128)(2,1)S(1)}, u32[]{:S(2)}, u32[]{:S(2)}) collective-permute-start(bf16[2,256,128]{2,1,0:T(8,128)(2,1)S(1)} %get-tuple-element.28), channel_id=1, source_target_pairs={{0,20},{4,16},{8,28},{12,24},{16,4},{20,0},{24,12},{28,8},{1,21},{... | collective-permute-start | bytes 393224 | tf_op jit(solution)/shard_map/ppermute | solution.py:233
  11.8 5.3 %collective-permute-start.6 = (bf16[2,256,128]{2,1,0:T(8,128)(2,1)S(1)}, bf16[2,256,128]{2,1,0:T(8,128)(2,1)S(1)}, u32[]{:S(2)}, u32[]{:S(2)}) collective-permute-start(bf16[2,256,128]{2,1,0:T(8,128)(2,1)S(1)} %get-tuple-element.29), channel_id=1, source_target_pairs={{0,4},{4,0},{8,12},{12,8},{16,20},{20,16},{24,28},{28,24},{1,5},{5... | collective-permute-start | bytes 393224 | tf_op jit(solution)/shard_map/ppermute | solution.py:233
  11.8 5.3 %copy-start.1 = (s32[8,128]{1,0:T(8,128)S(1)}, s32[8,128]{1,0:T(8,128)}, u32[]{:S(2)}) copy-start(s32[8,128]{1,0:T(8,128)} %refs_8_.1) | copy-start | bytes 12292
  20.3 1.7 %collective-permute-start.7 = (s16[4,22,16,128]{3,2,1,0:T(8,128)(2,1)S(1)}, s16[4,22,16,128]{3,2,1,0:T(8,128)(2,1)S(1)}, u32[]{:S(2)}, u32[]{:S(2)}) collective-permute-start(s16[4,22,16,128]{3,2,1,0:T(8,128)(2,1)S(1)} %get-tuple-element.32), channel_id=1, source_target_pairs={{0,4},{4,0},{8,12},{12,8},{16,20},{20,16},{24,28},{28,24},{1,5},{5... | collective-permute-start | bytes 1081352 | tf_op jit(solution)/shard_map/ppermute | solution.py:233
  22.3 4.7 %collective-permute-start.8 = (s16[22,16,128]{2,1,0:T(8,128)(2,1)S(1)}, s16[22,16,128]{2,1,0:T(8,128)(2,1)S(1)}, u32[]{:S(2)}, u32[]{:S(2)}) collective-permute-start(s16[22,16,128]{2,1,0:T(8,128)(2,1)S(1)} %get-tuple-element.33), channel_id=1, source_target_pairs={{0,8},{4,12},{8,0},{12,4},{16,24},{20,28},{24,16},{28,20},{1,9},{5... | collective-permute-start | bytes 270344 | tf_op jit(solution)/shard_map/ppermute | solution.py:233
  23.9 5.5 %collective-permute-start.9 = (s16[22,16,128]{2,1,0:T(8,128)(2,1)S(1)}, s16[22,16,128]{2,1,0:T(8,128)(2,1)S(1)}, u32[]{:S(2)}, u32[]{:S(2)}) collective-permute-start(s16[22,16,128]{2,1,0:T(8,128)(2,1)S(1)} %get-tuple-element.34), channel_id=1, source_target_pairs={{0,16},{4,20},{8,24},{12,28},{16,0},{20,4},{24,8},{28,12},{1,17},{... | collective-permute-start | bytes 270344 | tf_op jit(solution)/shard_map/ppermute | solution.py:233
  25.5 5.4 %collective-permute-start.10 = (s16[22,16,128]{2,1,0:T(8,128)(2,1)S(1)}, s16[22,16,128]{2,1,0:T(8,128)(2,1)S(1)}, u32[]{:S(2)}, u32[]{:S(2)}) collective-permute-start(s16[22,16,128]{2,1,0:T(8,128)(2,1)S(1)} %get-tuple-element.35), channel_id=1, source_target_pairs={{0,24},{4,28},{8,16},{12,20},{16,8},{20,12},{24,0},{28,4},{1,25},{... | collective-permute-start | bytes 270344 | tf_op jit(solution)/shard_map/ppermute | solution.py:233
  31.0 5.1 %collective-permute-start.11 = (s16[7,16,128]{2,1,0:T(8,128)(2,1)S(1)}, s16[7,16,128]{2,1,0:T(8,128)(2,1)S(1)}, u32[]{:S(2)}, u32[]{:S(2)}) collective-permute-start(s16[7,16,128]{2,1,0:T(8,128)(2,1)S(1)} %get-tuple-element.37), channel_id=1, source_target_pairs={{0,2},{1,3},{2,0},{3,1},{4,6},{5,7},{6,4},{7,5},{8,10},{9,11},{10,... | collective-permute-start | bytes 86024 | tf_op jit(solution)/shard_map/ppermute | solution.py:233
  33.7 5.7 %collective-permute-start.12 = (s16[7,16,128]{2,1,0:T(8,128)(2,1)S(1)}, s16[7,16,128]{2,1,0:T(8,128)(2,1)S(1)}, u32[]{:S(2)}, u32[]{:S(2)}) collective-permute-start(s16[7,16,128]{2,1,0:T(8,128)(2,1)S(1)} %get-tuple-element.38), channel_id=1, source_target_pairs={{0,3},{1,2},{2,1},{3,0},{4,7},{5,6},{6,5},{7,4},{8,11},{9,10},{10,... | collective-permute-start | bytes 86024 | tf_op jit(solution)/shard_map/ppermute | solution.py:233
  35.0 4.3 %collective-permute-start.13 = (s16[7,16,128]{2,1,0:T(8,128)(2,1)S(1)}, s16[7,16,128]{2,1,0:T(8,128)(2,1)S(1)}, u32[]{:S(2)}, u32[]{:S(2)}) collective-permute-start(s16[7,16,128]{2,1,0:T(8,128)(2,1)S(1)} %get-tuple-element.39), channel_id=1, source_target_pairs={{0,1},{1,0},{2,3},{3,2},{4,5},{5,4},{6,7},{7,6},{8,9},{9,8},{10,11... | collective-permute-start | bytes 86024 | tf_op jit(solution)/shard_map/ppermute | solution.py:233

commit v22 on v20

--- a/solution.py
+++ b/solution.py
@@ -107,7 +107,8 @@
         ],
         axis=0,
     )
-    turns = [chans - offset_of(number, offs_ref, chan_count // 2) * (chans // chan_count) for number in range(offset_count)]
+    turns = [chans - offset_of(number, offs_ref, chan_count // 2) * (chans // chan_count) for number in range(offset_count - 1)]
+    low = lane < chans // 2
     for row in range(0, freqs, step):
         own = [white_ref[part, row : row + step, :] for part in range(2)]
         own_real, own_imag = (value.astype(jnp.float32) for value in own)
@@ -117,6 +118,18 @@
             imag = own_imag * far_real - own_real * far_imag
             cross_ref[number, row : row + step, 0:chans] = real.astype(jnp.bfloat16)
             cross_ref[number, row : row + step, chans : 2 * chans] = imag.astype(jnp.bfloat16)
+        far_real, far_imag = (pltpu.roll(value, chans // 2, 1).astype(jnp.float32) for value in own)
+        both = own_real * jnp.where(low, far_real, far_imag) + own_imag * jnp.where(low, far_imag, -far_real)
+        cross_ref[offset_count - 1, row : row + step, 0:chans] = both.astype(jnp.bfloat16)
+
+    def store(block, value):
+        coded = encode(value).reshape(chan_count, lag_rows, chans)
+        for core in range(2):
+            rows = slice(core * chip_count, (core + 1) * chip_count)
+            out_refs[core][:, block, :, :] = coded[rows]
+
+    def extra_of(power):
+        return 0.25 * (jnp.sum(power[0] + power[1], axis=0, keepdims=True) * (1.0 / (2 * half)) + 1e-06 * freqs)
 
     for number, turn in enumerate(turns):
         sums = jnp.dot(table, cross_ref[number], preferred_element_type=jnp.float32)
@@ -127,27 +140,36 @@
             (cos_real + sin_imag, cos_imag - sin_real),
         )
         power = [real * real + imag * imag for real, imag in corr]
-        mean_power = jnp.sum(power[0] + power[1], axis=0, keepdims=True) * (1.0 / (2 * half))
-        extra = 0.25 * (mean_power + 1e-06 * freqs)
+        extra = extra_of(power)
         peak = jnp.max(jnp.maximum(jnp.abs(corr[0][0]), jnp.abs(corr[1][0])), axis=0, keepdims=True)
         code = level_code(peak)
+        levels = jnp.where(line == number, code, levels)
         keep = jnp.where(lane < turn, usable * pltpu.roll(usable, turn, 1), 0.0) * CODE_TOP
         upscale = keep / level_of(code)
-        inverse = [lax.rsqrt(side + extra) * keep for side in power]
-        kinds = [
-            [real * upscale for real, _ in corr],
-            [real * scale for (real, _), scale in zip(corr, inverse)],
-            [imag * scale for (_, imag), scale in zip(corr, inverse)],
-        ]
-        if number == offset_count - 1:
-            code = jnp.where(lane < chans // 2, code, pltpu.roll(code, chans // 2, 1))
-            kinds = [[jnp.where(lane < chans // 2, ahead, pltpu.roll(back, chans // 2, 1))] for ahead, back in kinds]
-        levels = jnp.where(line == number, code, levels)
-        for place, value in enumerate(value for kind in kinds for value in kind):
-            coded = encode(value).reshape(chan_count, lag_rows, chans)
-            for core in range(2):
-                rows = slice(core * chip_count, (core + 1) * chip_count)
-                out_refs[core][:, 6 * number + place, :, :] = coded[rows]
+        for side in range(2):
+            inverse = lax.rsqrt(power[side] + extra) * keep
+            real, imag = corr[side]
+            for kind, value in enumerate((real * upscale, real * inverse, imag * inverse)):
+                store(6 * number + 2 * kind + side, value)
+
+    def swap(value):
+        return pltpu.roll(value, chans // 2, 1)
+
+    number = offset_count - 1
+    sums = jnp.dot(table, cross_ref[number, :, 0:chans], preferred_element_type=jnp.float32)
+    cosine, sine = sums[:half], swap(sums[half:])
+    less, more = cosine - sine, cosine + sine
+    sides = (jnp.where(low, less, more), jnp.where(low, more, less))
+    power = [value * value for value in sides]
+    power = [value + swap(value) for value in power]
+    extra = extra_of(power)
+    linear = jnp.where(low, sides[0], swap(sides[1]))
+    code = level_code(jnp.max(jnp.abs(linear), axis=0, keepdims=True))
+    levels = jnp.where(line == number, code, levels)
+    keep = usable * swap(usable) * CODE_TOP
+    store(6 * number, linear * (keep / level_of(code)))
+    for side in range(2):
+        store(6 * number + 1 + side, sides[side] * (lax.rsqrt(power[side] + extra) * keep))
     for number in range(offset_count):
         levels = jnp.where(line == offset_count + number, offs_ref[number].astype(jnp.float32), levels)
     wide = widest(offs_ref, chan_count // 2).astype(jnp.float32)
@@ -186,6 +208,10 @@
     offsets = [heads[0][slots + number : slots + number + 1, :] for number in range(slots)]
     wide = heads[0][2 * slots : 2 * slots + 1, :]
     low = lax.broadcasted_iota(jnp.int32, (1, chans), 1) < chans // 2
+
+    def swap(value):
+        return pltpu.roll(value, chans // 2, 1)
+
     all_sums = []
     for number in range(slots):
         sides = 2 if number < slots - 1 else 1
@@ -198,9 +224,9 @@
             else:
                 sums.append(sum(codes) * (1.0 / len(code_refs)))
         if sides == 1:
-            sums = [
-                jnp.where(low, side, 0.0) for value in sums for side in (value, pltpu.roll(value, chans // 2, 1))
-            ]
+            linear, ahead, back = sums
+            sums = [linear, swap(linear), ahead, back, swap(ahead), swap(back)]
+            sums = [jnp.where(low, value, 0.0) for value in sums]
         all_sums.append(sums)
     line = lax.broadcasted_iota(jnp.int32, levels[0].shape, 0)
     last = slots - 1
@@ -248,7 +274,7 @@
         copy.wait()
 
 
-def stack_kernel(windows, *refs):
+def stack_kernel(windows, where_ref, *refs):
     sums_refs, out_ref = refs[:-1], refs[-1]
     blocks, copies, rows, _ = out_ref.shape
     _, lag_rows, chans = sums_refs[0].shape
@@ -271,18 +297,21 @@
         chosen = (offset == steps) & (lane >= ahead)
         behind = [jnp.where(chosen, pltpu.roll(stack, ahead, 1), kept) for stack, kept in zip(stacks, behind)]
     back = stacks[1] + behind[0]
-    both = jnp.concatenate(
-        [stacks[0] + behind[1]] + [back[row : row + 1, :] for row in reversed(range(lag_rows))], axis=0
-    )
-    wide = 2 * lag_rows
-    parts = chans // wide
+    back = jnp.concatenate([back[row : row + 1, :] for row in reversed(range(lag_rows))], axis=0)
+    me = where_ref[0]
+    even = (me & 1) == 0
+    ahead = stacks[0] + behind[1]
+    both = jnp.concatenate([jnp.where(even, ahead, back), jnp.where(even, back, ahead)], axis=0)
+    parts = chans // (2 * lag_rows)
     turned = jnp.concatenate([both] * parts, axis=0).T
+    unit = lane // lag_rows
+    part_of = jnp.where(((unit ^ me) & 1) == 0, unit - me, unit + me + 1) % blocks // 2
     per_block = chans // blocks
     for block in range(blocks):
         piece = jnp.zeros((rows, chans), jnp.float32)
         for part in range(parts):
             begin = block * per_block + part * rows
-            piece = jnp.where(lane // wide == part, turned[begin : begin + rows, :], piece)
+            piece = jnp.where(part_of == part, turned[begin : begin + rows, :], piece)
         for copy in range(copies):
             out_ref[block, copy, :, :] = piece
 
@@ -292,21 +321,17 @@
     half = out_ref.shape[2] // 2
     lag_rows = half // groups
     parts = out_ref.shape[0] // rows
-    lane = lax.broadcasted_iota(jnp.int32, (1, lanes), 1)
+    unit = lax.broadcasted_iota(jnp.int32, (1, lanes), 1) // lag_rows
     for number in range(offset_count):
+        pieces = [parts_ref[group, number] for group in range(groups)]
         for part in range(parts):
-            ahead = jnp.zeros((rows, lanes), jnp.float32)
-            back = jnp.zeros((rows, lanes), jnp.float32)
-            begin = part * 2 * lag_rows
-            for group in range(groups):
-                piece = parts_ref[group, number]
-                first, last = group * lag_rows, half - (group + 1) * lag_rows
-                ahead = jnp.where(lane // lag_rows == group, pltpu.roll(piece, (first - begin) % lanes, 1), ahead)
-                back = jnp.where(
-                    lane // lag_rows == groups - 1 - group, pltpu.roll(piece, (last - begin - lag_rows) % lanes, 1), back
-                )
-            out_ref[part * rows : (part + 1) * rows, number, 0:half] = back
-            out_ref[part * rows : (part + 1) * rows, number, half : 2 * half] = ahead
+            sides = [jnp.zeros((rows, lanes), jnp.float32)] * 2
+            for group, piece in enumerate(pieces):
+                places = ((groups - 1 - group + 2 * part) % groups, (group + 2 * part) % groups)
+                sides = [jnp.where(unit == place, piece, side) for place, side in zip(places, sides)]
+            for side, value in enumerate(sides):
+                value = pltpu.roll(value, (lanes - 2 * part * lag_rows) % lanes, 1) if part else value
+                out_ref[part * rows : (part + 1) * rows, number, side * half : (side + 1) * half] = value
 
 
 def window_shards(spectra, quality, offsets):
@@ -377,11 +402,11 @@
     pieces = pl.pallas_call(
         functools.partial(stack_kernel, windows * tm_count),
         out_shape=jax.ShapeDtypeStruct((chan_count, tm_count, piece_rows, chans), jnp.float32),
-        in_specs=[vmem] * tm_count,
+        in_specs=[smem] + [vmem] * tm_count,
         out_specs=vmem,
         compiler_params=params,
         name="stack_pairs",
-    )(*exchange(sums, "tm", tm_order))
+    )(chan_where, *exchange(sums, "tm", tm_order))
     shape = (chan_count * tm_count, piece_rows, chans)
     arrived = lax.all_to_all(pieces.reshape(shape), ("chan", "tm"), 0, 0, tiled=True)
     return pl.pallas_call(

time: 50.8 us -> 50.8 us (level)
  no operation moved by 1% of the time
where the time goes in v22:
time: 50.8 us; the launch traced here: 50.6 us
  waiting for transfers between devices  17.6 us (35%)
  starting transfers between devices  15.8 us (31%)
  blocking collectives  10.1 us (20%)
  Pallas kernels  7.06 us (14%)
    ppermute x14, waiting for transfers between devices, exchange(): lax.ppermute(piece, axis, [(source, source ^ k) for source in range(count)])  17.6 us
    ppermute x14, starting transfers between devices, exchange(): lax.ppermute(piece, axis, [(source, source ^ k) for source in range(count)])  15.8 us
    all_to_all x1, blocking collectives, window_shards(): lax.all_to_all(pieces.reshape(shape), ('chan', 'tm'), 0, 0, tiled=True)  10.1 us
    pallas_call x1, Pallas kernels, window_shards(): pl.pallas_call(functools.partial(window_kernel, chan_order), out_shape=[j...  3.43 us
    pallas_call x2, Pallas kernels, window_shards(): pl.pallas_call(functools.partial(split_kernel, part), out_shape=[jax.Shap...  2.32 us
  transfers between devices with their start and end apart: 14, of which 10 were waited for; matrix products, arithmetic and copies ran while one was open for 0% of the time, Pallas kernels for 2%

profile of v22, /device:TPU:0, one launch (start us, length us, event | category | flops | bytes accessed | tf_op | source)
XLA Modules:
  0.0 50.6 jit_solution(4321617536965096900)
XLA Ops:
  0.0 1.1 %split_windows.2 = (bf16[2,256,128]{2,1,0:T(8,128)(2,1)S(1)}, bf16[2,256,128]{2,1,0:T(8,128)(2,1)S(1)}) custom-call(bf16[2,8,256,128]{3,2,1,0:T(8,128)(2,1)} %spec_ref.3), custom_call_target="tpu_custom_call" | custom-call | tf_op jit(solution)/shard_map/split_windows/pallas_call | solution.py:359
  1.1 4.0 %collective-permute-start = (bf16[2,256,128]{2,1,0:T(8,128)(2,1)S(1)}, bf16[2,256,128]{2,1,0:T(8,128)(2,1)S(1)}, u32[]{:S(2)}, u32[]{:S(2)}) collective-permute-start(bf16[2,256,128]{2,1,0:T(8,128)(2,1)S(1)} %get-tuple-element.23), channel_id=1, source_target_pairs={{0,24},{4,28},{8,16},{12,20},{16,8},{20,12},{24,0},{28,4},{1,25},{... | collective-permute-start | bytes 393224 | tf_op jit(solution)/shard_map/ppermute | solution.py:259
  5.0 1.3 %split_windows.3 = (bf16[2,256,128]{2,1,0:T(8,128)(2,1)S(1)}, bf16[2,256,128]{2,1,0:T(8,128)(2,1)S(1)}, bf16[2,256,128]{2,1,0:T(8,128)(2,1)S(1)}, bf16[2,256,128...) custom-call(bf16[2,8,256,128]{3,2,1,0:T(8,128)(2,1)} %spec_ref.3), custom_call_target="tpu_custom_call" | custom-call | tf_op jit(solution)/shard_map/split_windows/pallas_call | solution.py:359
  6.3 1.2 %collective-permute-start.2 = (bf16[2,256,128]{2,1,0:T(8,128)(2,1)S(1)}, bf16[2,256,128]{2,1,0:T(8,128)(2,1)S(1)}, u32[]{:S(2)}, u32[]{:S(2)}) collective-permute-start(bf16[2,256,128]{2,1,0:T(8,128)(2,1)S(1)} %get-tuple-element.25), channel_id=1, source_target_pairs={{0,8},{4,12},{8,0},{12,4},{16,24},{20,28},{24,16},{28,20},{1,9},{5... | collective-permute-start | bytes 393224 | tf_op jit(solution)/shard_map/ppermute | solution.py:259
  7.5 1.5 %collective-permute-start.3 = (bf16[2,256,128]{2,1,0:T(8,128)(2,1)S(1)}, bf16[2,256,128]{2,1,0:T(8,128)(2,1)S(1)}, u32[]{:S(2)}, u32[]{:S(2)}) collective-permute-start(bf16[2,256,128]{2,1,0:T(8,128)(2,1)S(1)} %get-tuple-element.26), channel_id=1, source_target_pairs={{0,16},{4,20},{8,24},{12,28},{16,0},{20,4},{24,8},{28,12},{1,17},{... | collective-permute-start | bytes 393224 | tf_op jit(solution)/shard_map/ppermute | solution.py:259
  9.0 0.6 %collective-permute-start.4 = (bf16[2,256,128]{2,1,0:T(8,128)(2,1)S(1)}, bf16[2,256,128]{2,1,0:T(8,128)(2,1)S(1)}, u32[]{:S(2)}, u32[]{:S(2)}) collective-permute-start(bf16[2,256,128]{2,1,0:T(8,128)(2,1)S(1)} %get-tuple-element.27), channel_id=1, source_target_pairs={{0,12},{4,8},{8,4},{12,0},{16,28},{20,24},{24,20},{28,16},{1,13},{... | collective-permute-start | bytes 393224 | tf_op jit(solution)/shard_map/ppermute | solution.py:259
  9.6 0.6 %collective-permute-start.5 = (bf16[2,256,128]{2,1,0:T(8,128)(2,1)S(1)}, bf16[2,256,128]{2,1,0:T(8,128)(2,1)S(1)}, u32[]{:S(2)}, u32[]{:S(2)}) collective-permute-start(bf16[2,256,128]{2,1,0:T(8,128)(2,1)S(1)} %get-tuple-element.28), channel_id=1, source_target_pairs={{0,20},{4,16},{8,28},{12,24},{16,4},{20,0},{24,12},{28,8},{1,21},{... | collective-permute-start | bytes 393224 | tf_op jit(solution)/shard_map/ppermute | solution.py:259
  10.1 1.6 %collective-permute-done.1.refs_1_ = bf16[2,256,128]{2,1,0:T(8,128)(2,1)S(1)} collective-permute-done((bf16[2,256,128]{2,1,0:T(8,128)(2,1)S(1)}, bf16[2,256,128]{2,1,0:T(8,128)(2,1)S(1)}, u32[]{:S(2)}, u32[]{:S(2)}) %collective-permute-start.1) | collective-permute-done | bytes 131104 | tf_op jit(solution)/shard_map/ppermute | solution.py:259
  11.8 3.5 %collective-permute-done.2.refs_2_ = bf16[2,256,128]{2,1,0:T(8,128)(2,1)S(1)} collective-permute-done((bf16[2,256,128]{2,1,0:T(8,128)(2,1)S(1)}, bf16[2,256,128]{2,1,0:T(8,128)(2,1)S(1)}, u32[]{:S(2)}, u32[]{:S(2)}) %collective-permute-start.2) | collective-permute-done | bytes 131104 | tf_op jit(solution)/shard_map/ppermute | solution.py:259
  15.2 1.1 %collective-permute-done.4.refs_4_ = bf16[2,256,128]{2,1,0:T(8,128)(2,1)S(1)} collective-permute-done((bf16[2,256,128]{2,1,0:T(8,128)(2,1)S(1)}, bf16[2,256,128]{2,1,0:T(8,128)(2,1)S(1)}, u32[]{:S(2)}, u32[]{:S(2)}) %collective-permute-start.4) | collective-permute-done | bytes 131104 | tf_op jit(solution)/shard_map/ppermute | solution.py:259
  16.4 0.7 %collective-permute-done.5.refs_5_ = bf16[2,256,128]{2,1,0:T(8,128)(2,1)S(1)} collective-permute-done((bf16[2,256,128]{2,1,0:T(8,128)(2,1)S(1)}, bf16[2,256,128]{2,1,0:T(8,128)(2,1)S(1)}, u32[]{:S(2)}, u32[]{:S(2)}) %collective-permute-start.5) | collective-permute-done | bytes 131104 | tf_op jit(solution)/shard_map/ppermute | solution.py:259
  17.1 3.4 %window_pairs.1 = (s16[4,22,16,128]{3,2,1,0:T(8,128)(2,1)S(1)}, s16[4,22,16,128]{3,2,1,0:T(8,128)(2,1)S(1)}) custom-call(s32[4]{0:T(128)} %offs_hbm_ref.1, s32[1]{0:T(128)} %bitcast.where_ref, bf16[2,256,128]{2,1,0:T(8,128)(2,1)S(1)} %collective-permute-done.refs_0_, bf16[2,256,128]{2,1,0:T(8,128)(2,1)S(1)} %collective-permute-done.1.refs_1_, ...), custom_call_target="tpu_custom_call" | custom-call | tf_op jit(solution)/shard_map/window_pairs/pallas_call | solution.py:370
  20.7 1.5 %collective-permute-done.7.far_ref = s16[4,22,16,128]{3,2,1,0:T(8,128)(2,1)S(1)} collective-permute-done((s16[4,22,16,128]{3,2,1,0:T(8,128)(2,1)S(1)}, s16[4,22,16,128]{3,2,1,0:T(8,128)(2,1)S(1)}, u32[]{:S(2)}, u32[]{:S(2)}) %collective-permute-start.7) | collective-permute-done | bytes 360480 | tf_op jit(solution)/shard_map/ppermute | solution.py:259
  22.5 1.6 %collective-permute-start.8 = (s16[22,16,128]{2,1,0:T(8,128)(2,1)S(1)}, s16[22,16,128]{2,1,0:T(8,128)(2,1)S(1)}, u32[]{:S(2)}, u32[]{:S(2)}) collective-permute-start(s16[22,16,128]{2,1,0:T(8,128)(2,1)S(1)} %get-tuple-element.33), channel_id=1, source_target_pairs={{0,8},{4,12},{8,0},{12,4},{16,24},{20,28},{24,16},{28,20},{1,9},{5... | collective-permute-start | bytes 270344 | tf_op jit(solution)/shard_map/ppermute | solution.py:259
  24.0 1.6 %collective-permute-start.9 = (s16[22,16,128]{2,1,0:T(8,128)(2,1)S(1)}, s16[22,16,128]{2,1,0:T(8,128)(2,1)S(1)}, u32[]{:S(2)}, u32[]{:S(2)}) collective-permute-start(s16[22,16,128]{2,1,0:T(8,128)(2,1)S(1)} %get-tuple-element.34), channel_id=1, source_target_pairs={{0,16},{4,20},{8,24},{12,28},{16,0},{20,4},{24,8},{28,12},{1,17},{... | collective-permute-start | bytes 270344 | tf_op jit(solution)/shard_map/ppermute | solution.py:259
  26.0 1.2 %collective-permute-done.8.refs_0_ = s16[22,16,128]{2,1,0:T(8,128)(2,1)S(1)} collective-permute-done((s16[22,16,128]{2,1,0:T(8,128)(2,1)S(1)}, s16[22,16,128]{2,1,0:T(8,128)(2,1)S(1)}, u32[]{:S(2)}, u32[]{:S(2)}) %collective-permute-start.8) | collective-permute-done | bytes 90144 | tf_op jit(solution)/shard_map/ppermute | solution.py:259
  27.2 2.4 %collective-permute-done.9.refs_1_ = s16[22,16,128]{2,1,0:T(8,128)(2,1)S(1)} collective-permute-done((s16[22,16,128]{2,1,0:T(8,128)(2,1)S(1)}, s16[22,16,128]{2,1,0:T(8,128)(2,1)S(1)}, u32[]{:S(2)}, u32[]{:S(2)}) %collective-permute-start.9) | collective-permute-done | bytes 90144 | tf_op jit(solution)/shard_map/ppermute | solution.py:259
  29.6 1.5 %collective-permute-done.10.refs_2_ = s16[22,16,128]{2,1,0:T(8,128)(2,1)S(1)} collective-permute-done((s16[22,16,128]{2,1,0:T(8,128)(2,1)S(1)}, s16[22,16,128]{2,1,0:T(8,128)(2,1)S(1)}, u32[]{:S(2)}, u32[]{:S(2)}) %collective-permute-start.10) | collective-permute-done | bytes 90144 | tf_op jit(solution)/shard_map/ppermute | solution.py:259
  31.2 2.7 %collective-permute-start.11 = (s16[7,16,128]{2,1,0:T(8,128)(2,1)S(1)}, s16[7,16,128]{2,1,0:T(8,128)(2,1)S(1)}, u32[]{:S(2)}, u32[]{:S(2)}) collective-permute-start(s16[7,16,128]{2,1,0:T(8,128)(2,1)S(1)} %get-tuple-element.37), channel_id=1, source_target_pairs={{0,2},{1,3},{2,0},{3,1},{4,6},{5,7},{6,4},{7,5},{8,10},{9,11},{10,... | collective-permute-start | bytes 86024 | tf_op jit(solution)/shard_map/ppermute | solution.py:259
  33.8 1.3 %collective-permute-start.12 = (s16[7,16,128]{2,1,0:T(8,128)(2,1)S(1)}, s16[7,16,128]{2,1,0:T(8,128)(2,1)S(1)}, u32[]{:S(2)}, u32[]{:S(2)}) collective-permute-start(s16[7,16,128]{2,1,0:T(8,128)(2,1)S(1)} %get-tuple-element.38), channel_id=1, source_target_pairs={{0,3},{1,2},{2,1},{3,0},{4,7},{5,6},{6,5},{7,4},{8,11},{9,10},{10,... | collective-permute-start | bytes 86024 | tf_op jit(solution)/shard_map/ppermute | solution.py:259
  35.4 0.9 %collective-permute-done.11.refs_0_ = s16[7,16,128]{2,1,0:T(8,128)(2,1)S(1)} collective-permute-done((s16[7,16,128]{2,1,0:T(8,128)(2,1)S(1)}, s16[7,16,128]{2,1,0:T(8,128)(2,1)S(1)}, u32[]{:S(2)}, u32[]{:S(2)}) %collective-permute-start.11) | collective-permute-done | bytes 28704 | tf_op jit(solution)/shard_map/ppermute | solution.py:259
  36.3 3.2 %collective-permute-done.12.refs_1_ = s16[7,16,128]{2,1,0:T(8,128)(2,1)S(1)} collective-permute-done((s16[7,16,128]{2,1,0:T(8,128)(2,1)S(1)}, s16[7,16,128]{2,1,0:T(8,128)(2,1)S(1)}, u32[]{:S(2)}, u32[]{:S(2)}) %collective-permute-start.12) | collective-permute-done | bytes 28704 | tf_op jit(solution)/shard_map/ppermute | solution.py:259
  39.7 10.1 %all_to_all.5 = f32[32,4,128]{2,1,0:T(4,128)S(1)} all-to-all(f32[32,4,128]{2,1,0:T(4,128)S(1)} %bitcast.5), channel_id=1, replica_groups=mesh['chan'=8,'tm'=4] {'chan','tm'}, dimensions={0} | all-to-all | bytes 131072 | tf_op jit(solution)/shard_map/all_to_all | solution.py:411
  49.9 0.8 %place_lags.1 = f32[16,4,256]{2,1,0:T(4,128)} custom-call(f32[8,4,4,128]{3,2,1,0:T(4,128)S(1)} %bitcast.4), custom_call_target="tpu_custom_call" | custom-call | tf_op jit(solution)/shard_map/place_lags/pallas_call | solution.py:412
  (16 shorter events, 1.4 us)
Async XLA Ops:
  0.0 17.1 %copy-start = (bf16[2,8,16,2048]{3,2,1,0:T(8,128)(2,1)S(1)}, bf16[2,8,16,2048]{3,2,1,0:T(8,128)(2,1)}, u32[]{:S(2)}) copy-start(bf16[2,8,16,2048]{3,2,1,0:T(8,128)(2,1)} %constant.11.clone.refs_9_) | copy-start | bytes 3145732
  1.1 8.5 %collective-permute-start = (bf16[2,256,128]{2,1,0:T(8,128)(2,1)S(1)}, bf16[2,256,128]{2,1,0:T(8,128)(2,1)S(1)}, u32[]{:S(2)}, u32[]{:S(2)}) collective-permute-start(bf16[2,256,128]{2,1,0:T(8,128)(2,1)S(1)} %get-tuple-element.23), channel_id=1, source_target_pairs={{0,24},{4,28},{8,16},{12,20},{16,8},{20,12},{24,0},{28,4},{1,25},{... | collective-permute-start | bytes 393224 | tf_op jit(solution)/shard_map/ppermute | solution.py:259
  5.0 6.7 %collective-permute-start.1 = (bf16[2,256,128]{2,1,0:T(8,128)(2,1)S(1)}, bf16[2,256,128]{2,1,0:T(8,128)(2,1)S(1)}, u32[]{:S(2)}, u32[]{:S(2)}) collective-permute-start(bf16[2,256,128]{2,1,0:T(8,128)(2,1)S(1)} %get-tuple-element.24), channel_id=1, source_target_pairs={{0,28},{4,24},{8,20},{12,16},{16,12},{20,8},{24,4},{28,0},{1,29},{... | collective-permute-start | bytes 393224 | tf_op jit(solution)/shard_map/ppermute | solution.py:259
  6.3 8.9 %collective-permute-start.2 = (bf16[2,256,128]{2,1,0:T(8,128)(2,1)S(1)}, bf16[2,256,128]{2,1,0:T(8,128)(2,1)S(1)}, u32[]{:S(2)}, u32[]{:S(2)}) collective-permute-start(bf16[2,256,128]{2,1,0:T(8,128)(2,1)S(1)} %get-tuple-element.25), channel_id=1, source_target_pairs={{0,8},{4,12},{8,0},{12,4},{16,24},{20,28},{24,16},{28,20},{1,9},{5... | collective-permute-start | bytes 393224 | tf_op jit(solution)/shard_map/ppermute | solution.py:259
  7.5 7.7 %collective-permute-start.3 = (bf16[2,256,128]{2,1,0:T(8,128)(2,1)S(1)}, bf16[2,256,128]{2,1,0:T(8,128)(2,1)S(1)}, u32[]{:S(2)}, u32[]{:S(2)}) collective-permute-start(bf16[2,256,128]{2,1,0:T(8,128)(2,1)S(1)} %get-tuple-element.26), channel_id=1, source_target_pairs={{0,16},{4,20},{8,24},{12,28},{16,0},{20,4},{24,8},{28,12},{1,17},{... | collective-permute-start | bytes 393224 | tf_op jit(solution)/shard_map/ppermute | solution.py:259
  9.0 7.4 %collective-permute-start.4 = (bf16[2,256,128]{2,1,0:T(8,128)(2,1)S(1)}, bf16[2,256,128]{2,1,0:T(8,128)(2,1)S(1)}, u32[]{:S(2)}, u32[]{:S(2)}) collective-permute-start(bf16[2,256,128]{2,1,0:T(8,128)(2,1)S(1)} %get-tuple-element.27), channel_id=1, source_target_pairs={{0,12},{4,8},{8,4},{12,0},{16,28},{20,24},{24,20},{28,16},{1,13},{... | collective-permute-start | bytes 393224 | tf_op jit(solution)/shard_map/ppermute | solution.py:259
  9.6 7.5 %collective-permute-start.5 = (bf16[2,256,128]{2,1,0:T(8,128)(2,1)S(1)}, bf16[2,256,128]{2,1,0:T(8,128)(2,1)S(1)}, u32[]{:S(2)}, u32[]{:S(2)}) collective-permute-start(bf16[2,256,128]{2,1,0:T(8,128)(2,1)S(1)} %get-tuple-element.28), channel_id=1, source_target_pairs={{0,20},{4,16},{8,28},{12,24},{16,4},{20,0},{24,12},{28,8},{1,21},{... | collective-permute-start | bytes 393224 | tf_op jit(solution)/shard_map/ppermute | solution.py:259
  11.8 5.3 %collective-permute-start.6 = (bf16[2,256,128]{2,1,0:T(8,128)(2,1)S(1)}, bf16[2,256,128]{2,1,0:T(8,128)(2,1)S(1)}, u32[]{:S(2)}, u32[]{:S(2)}) collective-permute-start(bf16[2,256,128]{2,1,0:T(8,128)(2,1)S(1)} %get-tuple-element.29), channel_id=1, source_target_pairs={{0,4},{4,0},{8,12},{12,8},{16,20},{20,16},{24,28},{28,24},{1,5},{5... | collective-permute-start | bytes 393224 | tf_op jit(solution)/shard_map/ppermute | solution.py:259
  11.8 5.3 %copy-start.1 = (s32[8,128]{1,0:T(8,128)S(1)}, s32[8,128]{1,0:T(8,128)}, u32[]{:S(2)}) copy-start(s32[8,128]{1,0:T(8,128)} %refs_8_.1) | copy-start | bytes 12292
  20.5 1.7 %collective-permute-start.7 = (s16[4,22,16,128]{3,2,1,0:T(8,128)(2,1)S(1)}, s16[4,22,16,128]{3,2,1,0:T(8,128)(2,1)S(1)}, u32[]{:S(2)}, u32[]{:S(2)}) collective-permute-start(s16[4,22,16,128]{3,2,1,0:T(8,128)(2,1)S(1)} %get-tuple-element.32), channel_id=1, source_target_pairs={{0,4},{4,0},{8,12},{12,8},{16,20},{20,16},{24,28},{28,24},{1,5},{5... | collective-permute-start | bytes 1081352 | tf_op jit(solution)/shard_map/ppermute | solution.py:259
  22.5 4.7 %collective-permute-start.8 = (s16[22,16,128]{2,1,0:T(8,128)(2,1)S(1)}, s16[22,16,128]{2,1,0:T(8,128)(2,1)S(1)}, u32[]{:S(2)}, u32[]{:S(2)}) collective-permute-start(s16[22,16,128]{2,1,0:T(8,128)(2,1)S(1)} %get-tuple-element.33), channel_id=1, source_target_pairs={{0,8},{4,12},{8,0},{12,4},{16,24},{20,28},{24,16},{28,20},{1,9},{5... | collective-permute-start | bytes 270344 | tf_op jit(solution)/shard_map/ppermute | solution.py:259
  24.0 5.5 %collective-permute-start.9 = (s16[22,16,128]{2,1,0:T(8,128)(2,1)S(1)}, s16[22,16,128]{2,1,0:T(8,128)(2,1)S(1)}, u32[]{:S(2)}, u32[]{:S(2)}) collective-permute-start(s16[22,16,128]{2,1,0:T(8,128)(2,1)S(1)} %get-tuple-element.34), channel_id=1, source_target_pairs={{0,16},{4,20},{8,24},{12,28},{16,0},{20,4},{24,8},{28,12},{1,17},{... | collective-permute-start | bytes 270344 | tf_op jit(solution)/shard_map/ppermute | solution.py:259
  25.6 5.4 %collective-permute-start.10 = (s16[22,16,128]{2,1,0:T(8,128)(2,1)S(1)}, s16[22,16,128]{2,1,0:T(8,128)(2,1)S(1)}, u32[]{:S(2)}, u32[]{:S(2)}) collective-permute-start(s16[22,16,128]{2,1,0:T(8,128)(2,1)S(1)} %get-tuple-element.35), channel_id=1, source_target_pairs={{0,24},{4,28},{8,16},{12,20},{16,8},{20,12},{24,0},{28,4},{1,25},{... | collective-permute-start | bytes 270344 | tf_op jit(solution)/shard_map/ppermute | solution.py:259
  31.2 5.1 %collective-permute-start.11 = (s16[7,16,128]{2,1,0:T(8,128)(2,1)S(1)}, s16[7,16,128]{2,1,0:T(8,128)(2,1)S(1)}, u32[]{:S(2)}, u32[]{:S(2)}) collective-permute-start(s16[7,16,128]{2,1,0:T(8,128)(2,1)S(1)} %get-tuple-element.37), channel_id=1, source_target_pairs={{0,2},{1,3},{2,0},{3,1},{4,6},{5,7},{6,4},{7,5},{8,10},{9,11},{10,... | collective-permute-start | bytes 86024 | tf_op jit(solution)/shard_map/ppermute | solution.py:259
  33.8 5.7 %collective-permute-start.12 = (s16[7,16,128]{2,1,0:T(8,128)(2,1)S(1)}, s16[7,16,128]{2,1,0:T(8,128)(2,1)S(1)}, u32[]{:S(2)}, u32[]{:S(2)}) collective-permute-start(s16[7,16,128]{2,1,0:T(8,128)(2,1)S(1)} %get-tuple-element.38), channel_id=1, source_target_pairs={{0,3},{1,2},{2,1},{3,0},{4,7},{5,6},{6,5},{7,4},{8,11},{9,10},{10,... | collective-permute-start | bytes 86024 | tf_op jit(solution)/shard_map/ppermute | solution.py:259
  35.2 4.3 %collective-permute-start.13 = (s16[7,16,128]{2,1,0:T(8,128)(2,1)S(1)}, s16[7,16,128]{2,1,0:T(8,128)(2,1)S(1)}, u32[]{:S(2)}, u32[]{:S(2)}) collective-permute-start(s16[7,16,128]{2,1,0:T(8,128)(2,1)S(1)} %get-tuple-element.39), channel_id=1, source_target_pairs={{0,1},{1,0},{2,3},{3,2},{4,5},{5,4},{6,7},{7,6},{8,9},{9,8},{10,11... | collective-permute-start | bytes 86024 | tf_op jit(solution)/shard_map/ppermute | solution.py:259

commit v23 on v22

--- a/solution.py
+++ b/solution.py
@@ -116,11 +116,13 @@
             far_real, far_imag = (pltpu.roll(value, turn, 1).astype(jnp.float32) for value in own)
             real = own_real * far_real + own_imag * far_imag
             imag = own_imag * far_real - own_real * far_imag
-            cross_ref[number, row : row + step, 0:chans] = real.astype(jnp.bfloat16)
-            cross_ref[number, row : row + step, chans : 2 * chans] = imag.astype(jnp.bfloat16)
+            begin = 2 * number * chans
+            cross_ref[row : row + step, begin : begin + chans] = real.astype(jnp.bfloat16)
+            cross_ref[row : row + step, begin + chans : begin + 2 * chans] = imag.astype(jnp.bfloat16)
         far_real, far_imag = (pltpu.roll(value, chans // 2, 1).astype(jnp.float32) for value in own)
         both = own_real * jnp.where(low, far_real, far_imag) + own_imag * jnp.where(low, far_imag, -far_real)
-        cross_ref[offset_count - 1, row : row + step, 0:chans] = both.astype(jnp.bfloat16)
+        cross_ref[row : row + step, 2 * (offset_count - 1) * chans :] = both.astype(jnp.bfloat16)
+    all_sums = jnp.dot(table, cross_ref[...], preferred_element_type=jnp.float32)
 
     def store(block, value):
         coded = encode(value).reshape(chan_count, lag_rows, chans)
@@ -132,7 +134,7 @@
         return 0.25 * (jnp.sum(power[0] + power[1], axis=0, keepdims=True) * (1.0 / (2 * half)) + 1e-06 * freqs)
 
     for number, turn in enumerate(turns):
-        sums = jnp.dot(table, cross_ref[number], preferred_element_type=jnp.float32)
+        sums = all_sums[:, 2 * number * chans : 2 * (number + 1) * chans]
         cos_real, sin_real = sums[:half, :chans], sums[half:, :chans]
         cos_imag, sin_imag = sums[:half, chans:], sums[half:, chans:]
         corr = (
@@ -156,7 +158,7 @@
         return pltpu.roll(value, chans // 2, 1)
 
     number = offset_count - 1
-    sums = jnp.dot(table, cross_ref[number, :, 0:chans], preferred_element_type=jnp.float32)
+    sums = all_sums[:, 2 * number * chans :]
     cosine, sine = sums[:half], swap(sums[half:])
     less, more = cosine - sine, cosine + sine
     sides = (jnp.where(low, less, more), jnp.where(low, more, less))
@@ -375,7 +377,7 @@
         scratch_shapes=[
             pltpu.VMEM((freqs, chans), jnp.float32),
             pltpu.VMEM((2, freqs, chans), jnp.bfloat16),
-            pltpu.VMEM((offset_count, freqs, 2 * chans), jnp.bfloat16),
+            pltpu.VMEM((freqs, (2 * offset_count - 1) * chans), jnp.bfloat16),
             pltpu.SMEM(offsets.shape, jnp.int32),
             pltpu.SemaphoreType.DMA(()),
         ],

time: 50.8 us -> 50.8 us (level)
  no operation moved by 1% of the time
where the time goes in v23:
time: 50.8 us; the launch traced here: 50.6 us
  waiting for transfers between devices  17.6 us (35%)
  starting transfers between devices  15.8 us (31%)
  blocking collectives  10.1 us (20%)
  Pallas kernels  7.07 us (14%)
    ppermute x14, waiting for transfers between devices, exchange(): lax.ppermute(piece, axis, [(source, source ^ k) for source in range(count)])  17.6 us
    ppermute x14, starting transfers between devices, exchange(): lax.ppermute(piece, axis, [(source, source ^ k) for source in range(count)])  15.8 us
    all_to_all x1, blocking collectives, window_shards(): lax.all_to_all(pieces.reshape(shape), ('chan', 'tm'), 0, 0, tiled=True)  10.1 us
    pallas_call x1, Pallas kernels, window_shards(): pl.pallas_call(functools.partial(window_kernel, chan_order), out_shape=[j...  3.43 us
    pallas_call x2, Pallas kernels, window_shards(): pl.pallas_call(functools.partial(split_kernel, part), out_shape=[jax.Shap...  2.32 us
  transfers between devices with their start and end apart: 14, of which 10 were waited for; matrix products, arithmetic and copies ran while one was open for 0% of the time, Pallas kernels for 2%

profile of v23, /device:TPU:0, one launch (start us, length us, event | category | flops | bytes accessed | tf_op | source)
XLA Modules:
  0.0 50.6 jit_solution(18100041897275460459)
XLA Ops:
  0.0 1.1 %split_windows.2 = (bf16[2,256,128]{2,1,0:T(8,128)(2,1)S(1)}, bf16[2,256,128]{2,1,0:T(8,128)(2,1)S(1)}) custom-call(bf16[2,8,256,128]{3,2,1,0:T(8,128)(2,1)} %spec_ref.3), custom_call_target="tpu_custom_call" | custom-call | tf_op jit(solution)/shard_map/split_windows/pallas_call | solution.py:361
  1.1 4.0 %collective-permute-start = (bf16[2,256,128]{2,1,0:T(8,128)(2,1)S(1)}, bf16[2,256,128]{2,1,0:T(8,128)(2,1)S(1)}, u32[]{:S(2)}, u32[]{:S(2)}) collective-permute-start(bf16[2,256,128]{2,1,0:T(8,128)(2,1)S(1)} %get-tuple-element.23), channel_id=1, source_target_pairs={{0,24},{4,28},{8,16},{12,20},{16,8},{20,12},{24,0},{28,4},{1,25},{... | collective-permute-start | bytes 393224 | tf_op jit(solution)/shard_map/ppermute | solution.py:261
  5.0 1.3 %split_windows.3 = (bf16[2,256,128]{2,1,0:T(8,128)(2,1)S(1)}, bf16[2,256,128]{2,1,0:T(8,128)(2,1)S(1)}, bf16[2,256,128]{2,1,0:T(8,128)(2,1)S(1)}, bf16[2,256,128...) custom-call(bf16[2,8,256,128]{3,2,1,0:T(8,128)(2,1)} %spec_ref.3), custom_call_target="tpu_custom_call" | custom-call | tf_op jit(solution)/shard_map/split_windows/pallas_call | solution.py:361
  6.3 1.2 %collective-permute-start.2 = (bf16[2,256,128]{2,1,0:T(8,128)(2,1)S(1)}, bf16[2,256,128]{2,1,0:T(8,128)(2,1)S(1)}, u32[]{:S(2)}, u32[]{:S(2)}) collective-permute-start(bf16[2,256,128]{2,1,0:T(8,128)(2,1)S(1)} %get-tuple-element.25), channel_id=1, source_target_pairs={{0,8},{4,12},{8,0},{12,4},{16,24},{20,28},{24,16},{28,20},{1,9},{5... | collective-permute-start | bytes 393224 | tf_op jit(solution)/shard_map/ppermute | solution.py:261
  7.5 1.5 %collective-permute-start.3 = (bf16[2,256,128]{2,1,0:T(8,128)(2,1)S(1)}, bf16[2,256,128]{2,1,0:T(8,128)(2,1)S(1)}, u32[]{:S(2)}, u32[]{:S(2)}) collective-permute-start(bf16[2,256,128]{2,1,0:T(8,128)(2,1)S(1)} %get-tuple-element.26), channel_id=1, source_target_pairs={{0,16},{4,20},{8,24},{12,28},{16,0},{20,4},{24,8},{28,12},{1,17},{... | collective-permute-start | bytes 393224 | tf_op jit(solution)/shard_map/ppermute | solution.py:261
  9.0 0.6 %collective-permute-start.4 = (bf16[2,256,128]{2,1,0:T(8,128)(2,1)S(1)}, bf16[2,256,128]{2,1,0:T(8,128)(2,1)S(1)}, u32[]{:S(2)}, u32[]{:S(2)}) collective-permute-start(bf16[2,256,128]{2,1,0:T(8,128)(2,1)S(1)} %get-tuple-element.27), channel_id=1, source_target_pairs={{0,12},{4,8},{8,4},{12,0},{16,28},{20,24},{24,20},{28,16},{1,13},{... | collective-permute-start | bytes 393224 | tf_op jit(solution)/shard_map/ppermute | solution.py:261
  9.6 0.6 %collective-permute-start.5 = (bf16[2,256,128]{2,1,0:T(8,128)(2,1)S(1)}, bf16[2,256,128]{2,1,0:T(8,128)(2,1)S(1)}, u32[]{:S(2)}, u32[]{:S(2)}) collective-permute-start(bf16[2,256,128]{2,1,0:T(8,128)(2,1)S(1)} %get-tuple-element.28), channel_id=1, source_target_pairs={{0,20},{4,16},{8,28},{12,24},{16,4},{20,0},{24,12},{28,8},{1,21},{... | collective-permute-start | bytes 393224 | tf_op jit(solution)/shard_map/ppermute | solution.py:261
  10.1 1.6 %collective-permute-done.1.refs_1_ = bf16[2,256,128]{2,1,0:T(8,128)(2,1)S(1)} collective-permute-done((bf16[2,256,128]{2,1,0:T(8,128)(2,1)S(1)}, bf16[2,256,128]{2,1,0:T(8,128)(2,1)S(1)}, u32[]{:S(2)}, u32[]{:S(2)}) %collective-permute-start.1) | collective-permute-done | bytes 131104 | tf_op jit(solution)/shard_map/ppermute | solution.py:261
  11.8 3.5 %collective-permute-done.2.refs_2_ = bf16[2,256,128]{2,1,0:T(8,128)(2,1)S(1)} collective-permute-done((bf16[2,256,128]{2,1,0:T(8,128)(2,1)S(1)}, bf16[2,256,128]{2,1,0:T(8,128)(2,1)S(1)}, u32[]{:S(2)}, u32[]{:S(2)}) %collective-permute-start.2) | collective-permute-done | bytes 131104 | tf_op jit(solution)/shard_map/ppermute | solution.py:261
  15.2 1.1 %collective-permute-done.4.refs_4_ = bf16[2,256,128]{2,1,0:T(8,128)(2,1)S(1)} collective-permute-done((bf16[2,256,128]{2,1,0:T(8,128)(2,1)S(1)}, bf16[2,256,128]{2,1,0:T(8,128)(2,1)S(1)}, u32[]{:S(2)}, u32[]{:S(2)}) %collective-permute-start.4) | collective-permute-done | bytes 131104 | tf_op jit(solution)/shard_map/ppermute | solution.py:261
  16.4 0.7 %collective-permute-done.5.refs_5_ = bf16[2,256,128]{2,1,0:T(8,128)(2,1)S(1)} collective-permute-done((bf16[2,256,128]{2,1,0:T(8,128)(2,1)S(1)}, bf16[2,256,128]{2,1,0:T(8,128)(2,1)S(1)}, u32[]{:S(2)}, u32[]{:S(2)}) %collective-permute-start.5) | collective-permute-done | bytes 131104 | tf_op jit(solution)/shard_map/ppermute | solution.py:261
  17.1 3.4 %window_pairs.1 = (s16[4,22,16,128]{3,2,1,0:T(8,128)(2,1)S(1)}, s16[4,22,16,128]{3,2,1,0:T(8,128)(2,1)S(1)}) custom-call(s32[4]{0:T(128)} %offs_hbm_ref.1, s32[1]{0:T(128)} %bitcast.where_ref, bf16[2,256,128]{2,1,0:T(8,128)(2,1)S(1)} %collective-permute-done.refs_0_, bf16[2,256,128]{2,1,0:T(8,128)(2,1)S(1)} %collective-permute-done.1.refs_1_, ...), custom_call_target="tpu_custom_call" | custom-call | tf_op jit(solution)/shard_map/window_pairs/pallas_call | solution.py:372
  20.7 1.6 %collective-permute-done.7.far_ref = s16[4,22,16,128]{3,2,1,0:T(8,128)(2,1)S(1)} collective-permute-done((s16[4,22,16,128]{3,2,1,0:T(8,128)(2,1)S(1)}, s16[4,22,16,128]{3,2,1,0:T(8,128)(2,1)S(1)}, u32[]{:S(2)}, u32[]{:S(2)}) %collective-permute-start.7) | collective-permute-done | bytes 360480 | tf_op jit(solution)/shard_map/ppermute | solution.py:261
  22.5 1.6 %collective-permute-start.8 = (s16[22,16,128]{2,1,0:T(8,128)(2,1)S(1)}, s16[22,16,128]{2,1,0:T(8,128)(2,1)S(1)}, u32[]{:S(2)}, u32[]{:S(2)}) collective-permute-start(s16[22,16,128]{2,1,0:T(8,128)(2,1)S(1)} %get-tuple-element.33), channel_id=1, source_target_pairs={{0,8},{4,12},{8,0},{12,4},{16,24},{20,28},{24,16},{28,20},{1,9},{5... | collective-permute-start | bytes 270344 | tf_op jit(solution)/shard_map/ppermute | solution.py:261
  24.0 1.6 %collective-permute-start.9 = (s16[22,16,128]{2,1,0:T(8,128)(2,1)S(1)}, s16[22,16,128]{2,1,0:T(8,128)(2,1)S(1)}, u32[]{:S(2)}, u32[]{:S(2)}) collective-permute-start(s16[22,16,128]{2,1,0:T(8,128)(2,1)S(1)} %get-tuple-element.34), channel_id=1, source_target_pairs={{0,16},{4,20},{8,24},{12,28},{16,0},{20,4},{24,8},{28,12},{1,17},{... | collective-permute-start | bytes 270344 | tf_op jit(solution)/shard_map/ppermute | solution.py:261
  26.0 1.2 %collective-permute-done.8.refs_0_ = s16[22,16,128]{2,1,0:T(8,128)(2,1)S(1)} collective-permute-done((s16[22,16,128]{2,1,0:T(8,128)(2,1)S(1)}, s16[22,16,128]{2,1,0:T(8,128)(2,1)S(1)}, u32[]{:S(2)}, u32[]{:S(2)}) %collective-permute-start.8) | collective-permute-done | bytes 90144 | tf_op jit(solution)/shard_map/ppermute | solution.py:261
  27.2 2.4 %collective-permute-done.9.refs_1_ = s16[22,16,128]{2,1,0:T(8,128)(2,1)S(1)} collective-permute-done((s16[22,16,128]{2,1,0:T(8,128)(2,1)S(1)}, s16[22,16,128]{2,1,0:T(8,128)(2,1)S(1)}, u32[]{:S(2)}, u32[]{:S(2)}) %collective-permute-start.9) | collective-permute-done | bytes 90144 | tf_op jit(solution)/shard_map/ppermute | solution.py:261
  29.6 1.5 %collective-permute-done.10.refs_2_ = s16[22,16,128]{2,1,0:T(8,128)(2,1)S(1)} collective-permute-done((s16[22,16,128]{2,1,0:T(8,128)(2,1)S(1)}, s16[22,16,128]{2,1,0:T(8,128)(2,1)S(1)}, u32[]{:S(2)}, u32[]{:S(2)}) %collective-permute-start.10) | collective-permute-done | bytes 90144 | tf_op jit(solution)/shard_map/ppermute | solution.py:261
  31.2 2.7 %collective-permute-start.11 = (s16[7,16,128]{2,1,0:T(8,128)(2,1)S(1)}, s16[7,16,128]{2,1,0:T(8,128)(2,1)S(1)}, u32[]{:S(2)}, u32[]{:S(2)}) collective-permute-start(s16[7,16,128]{2,1,0:T(8,128)(2,1)S(1)} %get-tuple-element.37), channel_id=1, source_target_pairs={{0,2},{1,3},{2,0},{3,1},{4,6},{5,7},{6,4},{7,5},{8,10},{9,11},{10,... | collective-permute-start | bytes 86024 | tf_op jit(solution)/shard_map/ppermute | solution.py:261
  33.8 1.3 %collective-permute-start.12 = (s16[7,16,128]{2,1,0:T(8,128)(2,1)S(1)}, s16[7,16,128]{2,1,0:T(8,128)(2,1)S(1)}, u32[]{:S(2)}, u32[]{:S(2)}) collective-permute-start(s16[7,16,128]{2,1,0:T(8,128)(2,1)S(1)} %get-tuple-element.38), channel_id=1, source_target_pairs={{0,3},{1,2},{2,1},{3,0},{4,7},{5,6},{6,5},{7,4},{8,11},{9,10},{10,... | collective-permute-start | bytes 86024 | tf_op jit(solution)/shard_map/ppermute | solution.py:261
  35.4 0.9 %collective-permute-done.11.refs_0_ = s16[7,16,128]{2,1,0:T(8,128)(2,1)S(1)} collective-permute-done((s16[7,16,128]{2,1,0:T(8,128)(2,1)S(1)}, s16[7,16,128]{2,1,0:T(8,128)(2,1)S(1)}, u32[]{:S(2)}, u32[]{:S(2)}) %collective-permute-start.11) | collective-permute-done | bytes 28704 | tf_op jit(solution)/shard_map/ppermute | solution.py:261
  36.3 3.2 %collective-permute-done.12.refs_1_ = s16[7,16,128]{2,1,0:T(8,128)(2,1)S(1)} collective-permute-done((s16[7,16,128]{2,1,0:T(8,128)(2,1)S(1)}, s16[7,16,128]{2,1,0:T(8,128)(2,1)S(1)}, u32[]{:S(2)}, u32[]{:S(2)}) %collective-permute-start.12) | collective-permute-done | bytes 28704 | tf_op jit(solution)/shard_map/ppermute | solution.py:261
  39.7 10.1 %all_to_all.5 = f32[32,4,128]{2,1,0:T(4,128)S(1)} all-to-all(f32[32,4,128]{2,1,0:T(4,128)S(1)} %bitcast.5), channel_id=1, replica_groups=mesh['chan'=8,'tm'=4] {'chan','tm'}, dimensions={0} | all-to-all | bytes 131072 | tf_op jit(solution)/shard_map/all_to_all | solution.py:413
  49.9 0.8 %place_lags.1 = f32[16,4,256]{2,1,0:T(4,128)} custom-call(f32[8,4,4,128]{3,2,1,0:T(4,128)S(1)} %bitcast.4), custom_call_target="tpu_custom_call" | custom-call | tf_op jit(solution)/shard_map/place_lags/pallas_call | solution.py:414
  (16 shorter events, 1.4 us)
Async XLA Ops:
  0.0 17.1 %copy-start = (bf16[2,8,16,2048]{3,2,1,0:T(8,128)(2,1)S(1)}, bf16[2,8,16,2048]{3,2,1,0:T(8,128)(2,1)}, u32[]{:S(2)}) copy-start(bf16[2,8,16,2048]{3,2,1,0:T(8,128)(2,1)} %constant.11.clone.refs_9_) | copy-start | bytes 3145732
  1.1 8.5 %collective-permute-start = (bf16[2,256,128]{2,1,0:T(8,128)(2,1)S(1)}, bf16[2,256,128]{2,1,0:T(8,128)(2,1)S(1)}, u32[]{:S(2)}, u32[]{:S(2)}) collective-permute-start(bf16[2,256,128]{2,1,0:T(8,128)(2,1)S(1)} %get-tuple-element.23), channel_id=1, source_target_pairs={{0,24},{4,28},{8,16},{12,20},{16,8},{20,12},{24,0},{28,4},{1,25},{... | collective-permute-start | bytes 393224 | tf_op jit(solution)/shard_map/ppermute | solution.py:261
  5.0 6.7 %collective-permute-start.1 = (bf16[2,256,128]{2,1,0:T(8,128)(2,1)S(1)}, bf16[2,256,128]{2,1,0:T(8,128)(2,1)S(1)}, u32[]{:S(2)}, u32[]{:S(2)}) collective-permute-start(bf16[2,256,128]{2,1,0:T(8,128)(2,1)S(1)} %get-tuple-element.24), channel_id=1, source_target_pairs={{0,28},{4,24},{8,20},{12,16},{16,12},{20,8},{24,4},{28,0},{1,29},{... | collective-permute-start | bytes 393224 | tf_op jit(solution)/shard_map/ppermute | solution.py:261
  6.3 8.9 %collective-permute-start.2 = (bf16[2,256,128]{2,1,0:T(8,128)(2,1)S(1)}, bf16[2,256,128]{2,1,0:T(8,128)(2,1)S(1)}, u32[]{:S(2)}, u32[]{:S(2)}) collective-permute-start(bf16[2,256,128]{2,1,0:T(8,128)(2,1)S(1)} %get-tuple-element.25), channel_id=1, source_target_pairs={{0,8},{4,12},{8,0},{12,4},{16,24},{20,28},{24,16},{28,20},{1,9},{5... | collective-permute-start | bytes 393224 | tf_op jit(solution)/shard_map/ppermute | solution.py:261
  7.5 7.7 %collective-permute-start.3 = (bf16[2,256,128]{2,1,0:T(8,128)(2,1)S(1)}, bf16[2,256,128]{2,1,0:T(8,128)(2,1)S(1)}, u32[]{:S(2)}, u32[]{:S(2)}) collective-permute-start(bf16[2,256,128]{2,1,0:T(8,128)(2,1)S(1)} %get-tuple-element.26), channel_id=1, source_target_pairs={{0,16},{4,20},{8,24},{12,28},{16,0},{20,4},{24,8},{28,12},{1,17},{... | collective-permute-start | bytes 393224 | tf_op jit(solution)/shard_map/ppermute | solution.py:261
  9.0 7.4 %collective-permute-start.4 = (bf16[2,256,128]{2,1,0:T(8,128)(2,1)S(1)}, bf16[2,256,128]{2,1,0:T(8,128)(2,1)S(1)}, u32[]{:S(2)}, u32[]{:S(2)}) collective-permute-start(bf16[2,256,128]{2,1,0:T(8,128)(2,1)S(1)} %get-tuple-element.27), channel_id=1, source_target_pairs={{0,12},{4,8},{8,4},{12,0},{16,28},{20,24},{24,20},{28,16},{1,13},{... | collective-permute-start | bytes 393224 | tf_op jit(solution)/shard_map/ppermute | solution.py:261
  9.6 7.5 %collective-permute-start.5 = (bf16[2,256,128]{2,1,0:T(8,128)(2,1)S(1)}, bf16[2,256,128]{2,1,0:T(8,128)(2,1)S(1)}, u32[]{:S(2)}, u32[]{:S(2)}) collective-permute-start(bf16[2,256,128]{2,1,0:T(8,128)(2,1)S(1)} %get-tuple-element.28), channel_id=1, source_target_pairs={{0,20},{4,16},{8,28},{12,24},{16,4},{20,0},{24,12},{28,8},{1,21},{... | collective-permute-start | bytes 393224 | tf_op jit(solution)/shard_map/ppermute | solution.py:261
  11.8 5.3 %collective-permute-start.6 = (bf16[2,256,128]{2,1,0:T(8,128)(2,1)S(1)}, bf16[2,256,128]{2,1,0:T(8,128)(2,1)S(1)}, u32[]{:S(2)}, u32[]{:S(2)}) collective-permute-start(bf16[2,256,128]{2,1,0:T(8,128)(2,1)S(1)} %get-tuple-element.29), channel_id=1, source_target_pairs={{0,4},{4,0},{8,12},{12,8},{16,20},{20,16},{24,28},{28,24},{1,5},{5... | collective-permute-start | bytes 393224 | tf_op jit(solution)/shard_map/ppermute | solution.py:261
  11.8 5.3 %copy-start.1 = (s32[8,128]{1,0:T(8,128)S(1)}, s32[8,128]{1,0:T(8,128)}, u32[]{:S(2)}) copy-start(s32[8,128]{1,0:T(8,128)} %refs_8_.1) | copy-start | bytes 12292
  20.5 1.7 %collective-permute-start.7 = (s16[4,22,16,128]{3,2,1,0:T(8,128)(2,1)S(1)}, s16[4,22,16,128]{3,2,1,0:T(8,128)(2,1)S(1)}, u32[]{:S(2)}, u32[]{:S(2)}) collective-permute-start(s16[4,22,16,128]{3,2,1,0:T(8,128)(2,1)S(1)} %get-tuple-element.32), channel_id=1, source_target_pairs={{0,4},{4,0},{8,12},{12,8},{16,20},{20,16},{24,28},{28,24},{1,5},{5... | collective-permute-start | bytes 1081352 | tf_op jit(solution)/shard_map/ppermute | solution.py:261
  22.5 4.7 %collective-permute-start.8 = (s16[22,16,128]{2,1,0:T(8,128)(2,1)S(1)}, s16[22,16,128]{2,1,0:T(8,128)(2,1)S(1)}, u32[]{:S(2)}, u32[]{:S(2)}) collective-permute-start(s16[22,16,128]{2,1,0:T(8,128)(2,1)S(1)} %get-tuple-element.33), channel_id=1, source_target_pairs={{0,8},{4,12},{8,0},{12,4},{16,24},{20,28},{24,16},{28,20},{1,9},{5... | collective-permute-start | bytes 270344 | tf_op jit(solution)/shard_map/ppermute | solution.py:261
  24.0 5.5 %collective-permute-start.9 = (s16[22,16,128]{2,1,0:T(8,128)(2,1)S(1)}, s16[22,16,128]{2,1,0:T(8,128)(2,1)S(1)}, u32[]{:S(2)}, u32[]{:S(2)}) collective-permute-start(s16[22,16,128]{2,1,0:T(8,128)(2,1)S(1)} %get-tuple-element.34), channel_id=1, source_target_pairs={{0,16},{4,20},{8,24},{12,28},{16,0},{20,4},{24,8},{28,12},{1,17},{... | collective-permute-start | bytes 270344 | tf_op jit(solution)/shard_map/ppermute | solution.py:261
  25.6 5.4 %collective-permute-start.10 = (s16[22,16,128]{2,1,0:T(8,128)(2,1)S(1)}, s16[22,16,128]{2,1,0:T(8,128)(2,1)S(1)}, u32[]{:S(2)}, u32[]{:S(2)}) collective-permute-start(s16[22,16,128]{2,1,0:T(8,128)(2,1)S(1)} %get-tuple-element.35), channel_id=1, source_target_pairs={{0,24},{4,28},{8,16},{12,20},{16,8},{20,12},{24,0},{28,4},{1,25},{... | collective-permute-start | bytes 270344 | tf_op jit(solution)/shard_map/ppermute | solution.py:261
  31.2 5.1 %collective-permute-start.11 = (s16[7,16,128]{2,1,0:T(8,128)(2,1)S(1)}, s16[7,16,128]{2,1,0:T(8,128)(2,1)S(1)}, u32[]{:S(2)}, u32[]{:S(2)}) collective-permute-start(s16[7,16,128]{2,1,0:T(8,128)(2,1)S(1)} %get-tuple-element.37), channel_id=1, source_target_pairs={{0,2},{1,3},{2,0},{3,1},{4,6},{5,7},{6,4},{7,5},{8,10},{9,11},{10,... | collective-permute-start | bytes 86024 | tf_op jit(solution)/shard_map/ppermute | solution.py:261
  33.8 5.7 %collective-permute-start.12 = (s16[7,16,128]{2,1,0:T(8,128)(2,1)S(1)}, s16[7,16,128]{2,1,0:T(8,128)(2,1)S(1)}, u32[]{:S(2)}, u32[]{:S(2)}) collective-permute-start(s16[7,16,128]{2,1,0:T(8,128)(2,1)S(1)} %get-tuple-element.38), channel_id=1, source_target_pairs={{0,3},{1,2},{2,1},{3,0},{4,7},{5,6},{6,5},{7,4},{8,11},{9,10},{10,... | collective-permute-start | bytes 86024 | tf_op jit(solution)/shard_map/ppermute | solution.py:261
  35.2 4.3 %collective-permute-start.13 = (s16[7,16,128]{2,1,0:T(8,128)(2,1)S(1)}, s16[7,16,128]{2,1,0:T(8,128)(2,1)S(1)}, u32[]{:S(2)}, u32[]{:S(2)}) collective-permute-start(s16[7,16,128]{2,1,0:T(8,128)(2,1)S(1)} %get-tuple-element.39), channel_id=1, source_target_pairs={{0,1},{1,0},{2,3},{3,2},{4,5},{5,4},{6,7},{7,6},{8,9},{9,8},{10,11... | collective-permute-start | bytes 86024 | tf_op jit(solution)/shard_map/ppermute | solution.py:261

commit v24 on v20

--- a/solution.py
+++ b/solution.py
@@ -98,14 +98,14 @@
     levels = jnp.zeros((lag_rows, chans), jnp.float32)
     groups = [k ^ core for core in range(2) for k in chips(chan_count)]
     fetch.wait()
-    bands = [pl.ds(pl.multiple_of((me ^ k) * band, band), band) for k in order]
+    per_band = table_ref.shape[0] // chan_count
+    chunks = [(me ^ k) * per_band + chunk for k in order for chunk in range(per_band)]
     table = jnp.concatenate(
         [
-            jnp.concatenate([table_ref[side, me ^ group, :, taken] for taken in bands], axis=1)
-            for side in range(2)
-            for group in groups
+            jnp.concatenate([table_ref[chunk, side, me ^ group] for side in range(2) for group in groups], axis=0)
+            for chunk in chunks
         ],
-        axis=0,
+        axis=1,
     )
     turns = [chans - offset_of(number, offs_ref, chan_count // 2) * (chans // chan_count) for number in range(offset_count)]
     for row in range(0, freqs, step):
@@ -115,11 +115,12 @@
             far_real, far_imag = (pltpu.roll(value, turn, 1).astype(jnp.float32) for value in own)
             real = own_real * far_real + own_imag * far_imag
             imag = own_imag * far_real - own_real * far_imag
-            cross_ref[number, row : row + step, 0:chans] = real.astype(jnp.bfloat16)
-            cross_ref[number, row : row + step, chans : 2 * chans] = imag.astype(jnp.bfloat16)
+            cross_ref[number, 0, row : row + step, :] = real.astype(jnp.bfloat16)
+            cross_ref[number, 1, row : row + step, :] = imag.astype(jnp.bfloat16)
 
     for number, turn in enumerate(turns):
-        sums = jnp.dot(table, cross_ref[number], preferred_element_type=jnp.float32)
+        both = jnp.concatenate([cross_ref[number, 0], cross_ref[number, 1]], axis=1)
+        sums = jnp.dot(table, both, preferred_element_type=jnp.float32)
         cos_real, sin_real = sums[:half, :chans], sums[half:, :chans]
         cos_imag, sin_imag = sums[:half, chans:], sums[half:, chans:]
         corr = (
@@ -248,7 +249,7 @@
         copy.wait()
 
 
-def stack_kernel(windows, *refs):
+def stack_kernel(windows, where_ref, *refs):
     sums_refs, out_ref = refs[:-1], refs[-1]
     blocks, copies, rows, _ = out_ref.shape
     _, lag_rows, chans = sums_refs[0].shape
@@ -271,18 +272,21 @@
         chosen = (offset == steps) & (lane >= ahead)
         behind = [jnp.where(chosen, pltpu.roll(stack, ahead, 1), kept) for stack, kept in zip(stacks, behind)]
     back = stacks[1] + behind[0]
-    both = jnp.concatenate(
-        [stacks[0] + behind[1]] + [back[row : row + 1, :] for row in reversed(range(lag_rows))], axis=0
-    )
-    wide = 2 * lag_rows
-    parts = chans // wide
+    back = jnp.concatenate([back[row : row + 1, :] for row in reversed(range(lag_rows))], axis=0)
+    me = where_ref[0]
+    even = (me & 1) == 0
+    ahead = stacks[0] + behind[1]
+    both = jnp.concatenate([jnp.where(even, ahead, back), jnp.where(even, back, ahead)], axis=0)
+    parts = chans // (2 * lag_rows)
     turned = jnp.concatenate([both] * parts, axis=0).T
+    unit = lane // lag_rows
+    part_of = jnp.where(((unit ^ me) & 1) == 0, unit - me, unit + me + 1) % blocks // 2
     per_block = chans // blocks
     for block in range(blocks):
         piece = jnp.zeros((rows, chans), jnp.float32)
         for part in range(parts):
             begin = block * per_block + part * rows
-            piece = jnp.where(lane // wide == part, turned[begin : begin + rows, :], piece)
+            piece = jnp.where(part_of == part, turned[begin : begin + rows, :], piece)
         for copy in range(copies):
             out_ref[block, copy, :, :] = piece
 
@@ -292,21 +296,17 @@
     half = out_ref.shape[2] // 2
     lag_rows = half // groups
     parts = out_ref.shape[0] // rows
-    lane = lax.broadcasted_iota(jnp.int32, (1, lanes), 1)
+    unit = lax.broadcasted_iota(jnp.int32, (1, lanes), 1) // lag_rows
     for number in range(offset_count):
+        pieces = [parts_ref[group, number] for group in range(groups)]
         for part in range(parts):
-            ahead = jnp.zeros((rows, lanes), jnp.float32)
-            back = jnp.zeros((rows, lanes), jnp.float32)
-            begin = part * 2 * lag_rows
-            for group in range(groups):
-                piece = parts_ref[group, number]
-                first, last = group * lag_rows, half - (group + 1) * lag_rows
-                ahead = jnp.where(lane // lag_rows == group, pltpu.roll(piece, (first - begin) % lanes, 1), ahead)
-                back = jnp.where(
-                    lane // lag_rows == groups - 1 - group, pltpu.roll(piece, (last - begin - lag_rows) % lanes, 1), back
-                )
-            out_ref[part * rows : (part + 1) * rows, number, 0:half] = back
-            out_ref[part * rows : (part + 1) * rows, number, half : 2 * half] = ahead
+            sides = [jnp.zeros((rows, lanes), jnp.float32)] * 2
+            for group, piece in enumerate(pieces):
+                places = ((groups - 1 - group + 2 * part) % groups, (group + 2 * part) % groups)
+                sides = [jnp.where(unit == place, piece, side) for place, side in zip(places, sides)]
+            for side, value in enumerate(sides):
+                value = pltpu.roll(value, (lanes - 2 * part * lag_rows) % lanes, 1) if part else value
+                out_ref[part * rows : (part + 1) * rows, number, side * half : (side + 1) * half] = value
 
 
 def window_shards(spectra, quality, offsets):
@@ -321,7 +321,8 @@
     smem = pl.BlockSpec(memory_space=pltpu.SMEM)
     vmem = pl.BlockSpec(memory_space=pltpu.VMEM)
     params = pltpu.CompilerParams(vmem_limit_bytes=VMEM_LIMIT)
-    table = jnp.asarray(half_table(freqs, LAGS).reshape(2, chan_count, lag_rows, freqs))
+    table = half_table(freqs, LAGS).reshape(2, chan_count, lag_rows, freqs // 128, 128)
+    table = jnp.asarray(np.ascontiguousarray(table.transpose(3, 0, 1, 2, 4)))
     chan_index = lax.axis_index("chan").astype(jnp.int32)
     tm_index = lax.axis_index("tm").astype(jnp.int32)
     chan_where, tm_where = chan_index.reshape(1), tm_index.reshape(1)
@@ -350,7 +351,7 @@
         scratch_shapes=[
             pltpu.VMEM((freqs, chans), jnp.float32),
             pltpu.VMEM((2, freqs, chans), jnp.bfloat16),
-            pltpu.VMEM((offset_count, freqs, 2 * chans), jnp.bfloat16),
+            pltpu.VMEM((offset_count, 2, freqs, chans), jnp.bfloat16),
             pltpu.SMEM(offsets.shape, jnp.int32),
             pltpu.SemaphoreType.DMA(()),
         ],
@@ -377,11 +378,11 @@
     pieces = pl.pallas_call(
         functools.partial(stack_kernel, windows * tm_count),
         out_shape=jax.ShapeDtypeStruct((chan_count, tm_count, piece_rows, chans), jnp.float32),
-        in_specs=[vmem] * tm_count,
+        in_specs=[smem] + [vmem] * tm_count,
         out_specs=vmem,
         compiler_params=params,
         name="stack_pairs",
-    )(*exchange(sums, "tm", tm_order))
+    )(chan_where, *exchange(sums, "tm", tm_order))
     shape = (chan_count * tm_count, piece_rows, chans)
     arrived = lax.all_to_all(pieces.reshape(shape), ("chan", "tm"), 0, 0, tiled=True)
     return pl.pallas_call(

time: 50.8 us -> 50.5 us (level)
  no operation moved by 1% of the time
where the time goes in v24:
time: 50.5 us; the launch traced here: 50.3 us
  waiting for transfers between devices  17.6 us (35%)
  starting transfers between devices  15.8 us (31%)
  blocking collectives  10.1 us (20%)
  Pallas kernels  6.77 us (13%)
    ppermute x14, waiting for transfers between devices, exchange(): lax.ppermute(piece, axis, [(source, source ^ k) for source in range(count)])  17.6 us
    ppermute x14, starting transfers between devices, exchange(): lax.ppermute(piece, axis, [(source, source ^ k) for source in range(count)])  15.8 us
    all_to_all x1, blocking collectives, window_shards(): lax.all_to_all(pieces.reshape(shape), ('chan', 'tm'), 0, 0, tiled=True)  10.1 us
    pallas_call x1, Pallas kernels, window_shards(): pl.pallas_call(functools.partial(window_kernel, chan_order), out_shape=[j...  3.14 us
    pallas_call x2, Pallas kernels, window_shards(): pl.pallas_call(functools.partial(split_kernel, part), out_shape=[jax.Shap...  2.32 us
  transfers between devices with their start and end apart: 14, of which 10 were waited for; matrix products, arithmetic and copies ran while one was open for 0% of the time, Pallas kernels for 2%

profile of v24, /device:TPU:0, one launch (start us, length us, event | category | flops | bytes accessed | tf_op | source)
XLA Modules:
  0.0 50.3 jit_solution(8496294353495334486)
XLA Ops:
  0.0 1.1 %split_windows.2 = (bf16[2,256,128]{2,1,0:T(8,128)(2,1)S(1)}, bf16[2,256,128]{2,1,0:T(8,128)(2,1)S(1)}) custom-call(bf16[2,8,256,128]{3,2,1,0:T(8,128)(2,1)} %spec_ref.3), custom_call_target="tpu_custom_call" | custom-call | tf_op jit(solution)/shard_map/split_windows/pallas_call | solution.py:335
  1.1 4.0 %collective-permute-start = (bf16[2,256,128]{2,1,0:T(8,128)(2,1)S(1)}, bf16[2,256,128]{2,1,0:T(8,128)(2,1)S(1)}, u32[]{:S(2)}, u32[]{:S(2)}) collective-permute-start(bf16[2,256,128]{2,1,0:T(8,128)(2,1)S(1)} %get-tuple-element.23), channel_id=1, source_target_pairs={{0,24},{4,28},{8,16},{12,20},{16,8},{20,12},{24,0},{28,4},{1,25},{... | collective-permute-start | bytes 393224 | tf_op jit(solution)/shard_map/ppermute | solution.py:234
  5.0 1.3 %split_windows.3 = (bf16[2,256,128]{2,1,0:T(8,128)(2,1)S(1)}, bf16[2,256,128]{2,1,0:T(8,128)(2,1)S(1)}, bf16[2,256,128]{2,1,0:T(8,128)(2,1)S(1)}, bf16[2,256,128...) custom-call(bf16[2,8,256,128]{3,2,1,0:T(8,128)(2,1)} %spec_ref.3), custom_call_target="tpu_custom_call" | custom-call | tf_op jit(solution)/shard_map/split_windows/pallas_call | solution.py:335
  6.3 1.2 %collective-permute-start.2 = (bf16[2,256,128]{2,1,0:T(8,128)(2,1)S(1)}, bf16[2,256,128]{2,1,0:T(8,128)(2,1)S(1)}, u32[]{:S(2)}, u32[]{:S(2)}) collective-permute-start(bf16[2,256,128]{2,1,0:T(8,128)(2,1)S(1)} %get-tuple-element.25), channel_id=1, source_target_pairs={{0,8},{4,12},{8,0},{12,4},{16,24},{20,28},{24,16},{28,20},{1,9},{5... | collective-permute-start | bytes 393224 | tf_op jit(solution)/shard_map/ppermute | solution.py:234
  7.5 1.5 %collective-permute-start.3 = (bf16[2,256,128]{2,1,0:T(8,128)(2,1)S(1)}, bf16[2,256,128]{2,1,0:T(8,128)(2,1)S(1)}, u32[]{:S(2)}, u32[]{:S(2)}) collective-permute-start(bf16[2,256,128]{2,1,0:T(8,128)(2,1)S(1)} %get-tuple-element.26), channel_id=1, source_target_pairs={{0,16},{4,20},{8,24},{12,28},{16,0},{20,4},{24,8},{28,12},{1,17},{... | collective-permute-start | bytes 393224 | tf_op jit(solution)/shard_map/ppermute | solution.py:234
  9.0 0.6 %collective-permute-start.4 = (bf16[2,256,128]{2,1,0:T(8,128)(2,1)S(1)}, bf16[2,256,128]{2,1,0:T(8,128)(2,1)S(1)}, u32[]{:S(2)}, u32[]{:S(2)}) collective-permute-start(bf16[2,256,128]{2,1,0:T(8,128)(2,1)S(1)} %get-tuple-element.27), channel_id=1, source_target_pairs={{0,12},{4,8},{8,4},{12,0},{16,28},{20,24},{24,20},{28,16},{1,13},{... | collective-permute-start | bytes 393224 | tf_op jit(solution)/shard_map/ppermute | solution.py:234
  9.6 0.6 %collective-permute-start.5 = (bf16[2,256,128]{2,1,0:T(8,128)(2,1)S(1)}, bf16[2,256,128]{2,1,0:T(8,128)(2,1)S(1)}, u32[]{:S(2)}, u32[]{:S(2)}) collective-permute-start(bf16[2,256,128]{2,1,0:T(8,128)(2,1)S(1)} %get-tuple-element.28), channel_id=1, source_target_pairs={{0,20},{4,16},{8,28},{12,24},{16,4},{20,0},{24,12},{28,8},{1,21},{... | collective-permute-start | bytes 393224 | tf_op jit(solution)/shard_map/ppermute | solution.py:234
  10.1 1.6 %collective-permute-done.1.refs_1_ = bf16[2,256,128]{2,1,0:T(8,128)(2,1)S(1)} collective-permute-done((bf16[2,256,128]{2,1,0:T(8,128)(2,1)S(1)}, bf16[2,256,128]{2,1,0:T(8,128)(2,1)S(1)}, u32[]{:S(2)}, u32[]{:S(2)}) %collective-permute-start.1) | collective-permute-done | bytes 131104 | tf_op jit(solution)/shard_map/ppermute | solution.py:234
  11.8 3.5 %collective-permute-done.2.refs_2_ = bf16[2,256,128]{2,1,0:T(8,128)(2,1)S(1)} collective-permute-done((bf16[2,256,128]{2,1,0:T(8,128)(2,1)S(1)}, bf16[2,256,128]{2,1,0:T(8,128)(2,1)S(1)}, u32[]{:S(2)}, u32[]{:S(2)}) %collective-permute-start.2) | collective-permute-done | bytes 131104 | tf_op jit(solution)/shard_map/ppermute | solution.py:234
  15.2 1.1 %collective-permute-done.4.refs_4_ = bf16[2,256,128]{2,1,0:T(8,128)(2,1)S(1)} collective-permute-done((bf16[2,256,128]{2,1,0:T(8,128)(2,1)S(1)}, bf16[2,256,128]{2,1,0:T(8,128)(2,1)S(1)}, u32[]{:S(2)}, u32[]{:S(2)}) %collective-permute-start.4) | collective-permute-done | bytes 131104 | tf_op jit(solution)/shard_map/ppermute | solution.py:234
  16.4 0.7 %collective-permute-done.5.refs_5_ = bf16[2,256,128]{2,1,0:T(8,128)(2,1)S(1)} collective-permute-done((bf16[2,256,128]{2,1,0:T(8,128)(2,1)S(1)}, bf16[2,256,128]{2,1,0:T(8,128)(2,1)S(1)}, u32[]{:S(2)}, u32[]{:S(2)}) %collective-permute-start.5) | collective-permute-done | bytes 131104 | tf_op jit(solution)/shard_map/ppermute | solution.py:234
  17.1 3.1 %window_pairs.1 = (s16[4,22,16,128]{3,2,1,0:T(8,128)(2,1)S(1)}, s16[4,22,16,128]{3,2,1,0:T(8,128)(2,1)S(1)}) custom-call(s32[4]{0:T(128)} %offs_hbm_ref.1, s32[1]{0:T(128)} %bitcast.where_ref, bf16[2,256,128]{2,1,0:T(8,128)(2,1)S(1)} %collective-permute-done.refs_0_, bf16[2,256,128]{2,1,0:T(8,128)(2,1)S(1)} %collective-permute-done.1.refs_1_, ...), custom_call_target="tpu_custom_call" | custom-call | tf_op jit(solution)/shard_map/window_pairs/pallas_call | solution.py:346
  20.4 1.6 %collective-permute-done.7.far_ref = s16[4,22,16,128]{3,2,1,0:T(8,128)(2,1)S(1)} collective-permute-done((s16[4,22,16,128]{3,2,1,0:T(8,128)(2,1)S(1)}, s16[4,22,16,128]{3,2,1,0:T(8,128)(2,1)S(1)}, u32[]{:S(2)}, u32[]{:S(2)}) %collective-permute-start.7) | collective-permute-done | bytes 360480 | tf_op jit(solution)/shard_map/ppermute | solution.py:234
  22.2 1.6 %collective-permute-start.8 = (s16[22,16,128]{2,1,0:T(8,128)(2,1)S(1)}, s16[22,16,128]{2,1,0:T(8,128)(2,1)S(1)}, u32[]{:S(2)}, u32[]{:S(2)}) collective-permute-start(s16[22,16,128]{2,1,0:T(8,128)(2,1)S(1)} %get-tuple-element.33), channel_id=1, source_target_pairs={{0,8},{4,12},{8,0},{12,4},{16,24},{20,28},{24,16},{28,20},{1,9},{5... | collective-permute-start | bytes 270344 | tf_op jit(solution)/shard_map/ppermute | solution.py:234
  23.7 1.6 %collective-permute-start.9 = (s16[22,16,128]{2,1,0:T(8,128)(2,1)S(1)}, s16[22,16,128]{2,1,0:T(8,128)(2,1)S(1)}, u32[]{:S(2)}, u32[]{:S(2)}) collective-permute-start(s16[22,16,128]{2,1,0:T(8,128)(2,1)S(1)} %get-tuple-element.34), channel_id=1, source_target_pairs={{0,16},{4,20},{8,24},{12,28},{16,0},{20,4},{24,8},{28,12},{1,17},{... | collective-permute-start | bytes 270344 | tf_op jit(solution)/shard_map/ppermute | solution.py:234
  25.7 1.2 %collective-permute-done.8.refs_0_ = s16[22,16,128]{2,1,0:T(8,128)(2,1)S(1)} collective-permute-done((s16[22,16,128]{2,1,0:T(8,128)(2,1)S(1)}, s16[22,16,128]{2,1,0:T(8,128)(2,1)S(1)}, u32[]{:S(2)}, u32[]{:S(2)}) %collective-permute-start.8) | collective-permute-done | bytes 90144 | tf_op jit(solution)/shard_map/ppermute | solution.py:234
  26.9 2.4 %collective-permute-done.9.refs_1_ = s16[22,16,128]{2,1,0:T(8,128)(2,1)S(1)} collective-permute-done((s16[22,16,128]{2,1,0:T(8,128)(2,1)S(1)}, s16[22,16,128]{2,1,0:T(8,128)(2,1)S(1)}, u32[]{:S(2)}, u32[]{:S(2)}) %collective-permute-start.9) | collective-permute-done | bytes 90144 | tf_op jit(solution)/shard_map/ppermute | solution.py:234
  29.3 1.5 %collective-permute-done.10.refs_2_ = s16[22,16,128]{2,1,0:T(8,128)(2,1)S(1)} collective-permute-done((s16[22,16,128]{2,1,0:T(8,128)(2,1)S(1)}, s16[22,16,128]{2,1,0:T(8,128)(2,1)S(1)}, u32[]{:S(2)}, u32[]{:S(2)}) %collective-permute-start.10) | collective-permute-done | bytes 90144 | tf_op jit(solution)/shard_map/ppermute | solution.py:234
  30.9 2.7 %collective-permute-start.11 = (s16[7,16,128]{2,1,0:T(8,128)(2,1)S(1)}, s16[7,16,128]{2,1,0:T(8,128)(2,1)S(1)}, u32[]{:S(2)}, u32[]{:S(2)}) collective-permute-start(s16[7,16,128]{2,1,0:T(8,128)(2,1)S(1)} %get-tuple-element.37), channel_id=1, source_target_pairs={{0,2},{1,3},{2,0},{3,1},{4,6},{5,7},{6,4},{7,5},{8,10},{9,11},{10,... | collective-permute-start | bytes 86024 | tf_op jit(solution)/shard_map/ppermute | solution.py:234
  33.5 1.4 %collective-permute-start.12 = (s16[7,16,128]{2,1,0:T(8,128)(2,1)S(1)}, s16[7,16,128]{2,1,0:T(8,128)(2,1)S(1)}, u32[]{:S(2)}, u32[]{:S(2)}) collective-permute-start(s16[7,16,128]{2,1,0:T(8,128)(2,1)S(1)} %get-tuple-element.38), channel_id=1, source_target_pairs={{0,3},{1,2},{2,1},{3,0},{4,7},{5,6},{6,5},{7,4},{8,11},{9,10},{10,... | collective-permute-start | bytes 86024 | tf_op jit(solution)/shard_map/ppermute | solution.py:234
  35.1 0.9 %collective-permute-done.11.refs_0_ = s16[7,16,128]{2,1,0:T(8,128)(2,1)S(1)} collective-permute-done((s16[7,16,128]{2,1,0:T(8,128)(2,1)S(1)}, s16[7,16,128]{2,1,0:T(8,128)(2,1)S(1)}, u32[]{:S(2)}, u32[]{:S(2)}) %collective-permute-start.11) | collective-permute-done | bytes 28704 | tf_op jit(solution)/shard_map/ppermute | solution.py:234
  36.0 3.2 %collective-permute-done.12.refs_1_ = s16[7,16,128]{2,1,0:T(8,128)(2,1)S(1)} collective-permute-done((s16[7,16,128]{2,1,0:T(8,128)(2,1)S(1)}, s16[7,16,128]{2,1,0:T(8,128)(2,1)S(1)}, u32[]{:S(2)}, u32[]{:S(2)}) %collective-permute-start.12) | collective-permute-done | bytes 28704 | tf_op jit(solution)/shard_map/ppermute | solution.py:234
  39.4 10.1 %all_to_all.5 = f32[32,4,128]{2,1,0:T(4,128)S(1)} all-to-all(f32[32,4,128]{2,1,0:T(4,128)S(1)} %bitcast.5), channel_id=1, replica_groups=mesh['chan'=8,'tm'=4] {'chan','tm'}, dimensions={0} | all-to-all | bytes 131072 | tf_op jit(solution)/shard_map/all_to_all | solution.py:387
  49.6 0.8 %place_lags.1 = f32[16,4,256]{2,1,0:T(4,128)} custom-call(f32[8,4,4,128]{3,2,1,0:T(4,128)S(1)} %bitcast.4), custom_call_target="tpu_custom_call" | custom-call | tf_op jit(solution)/shard_map/place_lags/pallas_call | solution.py:388
  (16 shorter events, 1.4 us)
Async XLA Ops:
  0.0 17.1 %copy-start = (bf16[16,2,8,16,128]{4,3,2,1,0:T(8,128)(2,1)S(1)}, bf16[16,2,8,16,128]{4,3,2,1,0:T(8,128)(2,1)}, u32[]{:S(2)}) copy-start(bf16[16,2,8,16,128]{4,3,2,1,0:T(8,128)(2,1)} %constant.11.clone.refs_9_) | copy-start | bytes 3145732
  1.1 8.5 %collective-permute-start = (bf16[2,256,128]{2,1,0:T(8,128)(2,1)S(1)}, bf16[2,256,128]{2,1,0:T(8,128)(2,1)S(1)}, u32[]{:S(2)}, u32[]{:S(2)}) collective-permute-start(bf16[2,256,128]{2,1,0:T(8,128)(2,1)S(1)} %get-tuple-element.23), channel_id=1, source_target_pairs={{0,24},{4,28},{8,16},{12,20},{16,8},{20,12},{24,0},{28,4},{1,25},{... | collective-permute-start | bytes 393224 | tf_op jit(solution)/shard_map/ppermute | solution.py:234
  5.0 6.7 %collective-permute-start.1 = (bf16[2,256,128]{2,1,0:T(8,128)(2,1)S(1)}, bf16[2,256,128]{2,1,0:T(8,128)(2,1)S(1)}, u32[]{:S(2)}, u32[]{:S(2)}) collective-permute-start(bf16[2,256,128]{2,1,0:T(8,128)(2,1)S(1)} %get-tuple-element.24), channel_id=1, source_target_pairs={{0,28},{4,24},{8,20},{12,16},{16,12},{20,8},{24,4},{28,0},{1,29},{... | collective-permute-start | bytes 393224 | tf_op jit(solution)/shard_map/ppermute | solution.py:234
  6.3 8.9 %collective-permute-start.2 = (bf16[2,256,128]{2,1,0:T(8,128)(2,1)S(1)}, bf16[2,256,128]{2,1,0:T(8,128)(2,1)S(1)}, u32[]{:S(2)}, u32[]{:S(2)}) collective-permute-start(bf16[2,256,128]{2,1,0:T(8,128)(2,1)S(1)} %get-tuple-element.25), channel_id=1, source_target_pairs={{0,8},{4,12},{8,0},{12,4},{16,24},{20,28},{24,16},{28,20},{1,9},{5... | collective-permute-start | bytes 393224 | tf_op jit(solution)/shard_map/ppermute | solution.py:234
  7.5 7.7 %collective-permute-start.3 = (bf16[2,256,128]{2,1,0:T(8,128)(2,1)S(1)}, bf16[2,256,128]{2,1,0:T(8,128)(2,1)S(1)}, u32[]{:S(2)}, u32[]{:S(2)}) collective-permute-start(bf16[2,256,128]{2,1,0:T(8,128)(2,1)S(1)} %get-tuple-element.26), channel_id=1, source_target_pairs={{0,16},{4,20},{8,24},{12,28},{16,0},{20,4},{24,8},{28,12},{1,17},{... | collective-permute-start | bytes 393224 | tf_op jit(solution)/shard_map/ppermute | solution.py:234
  9.0 7.4 %collective-permute-start.4 = (bf16[2,256,128]{2,1,0:T(8,128)(2,1)S(1)}, bf16[2,256,128]{2,1,0:T(8,128)(2,1)S(1)}, u32[]{:S(2)}, u32[]{:S(2)}) collective-permute-start(bf16[2,256,128]{2,1,0:T(8,128)(2,1)S(1)} %get-tuple-element.27), channel_id=1, source_target_pairs={{0,12},{4,8},{8,4},{12,0},{16,28},{20,24},{24,20},{28,16},{1,13},{... | collective-permute-start | bytes 393224 | tf_op jit(solution)/shard_map/ppermute | solution.py:234
  9.6 7.5 %collective-permute-start.5 = (bf16[2,256,128]{2,1,0:T(8,128)(2,1)S(1)}, bf16[2,256,128]{2,1,0:T(8,128)(2,1)S(1)}, u32[]{:S(2)}, u32[]{:S(2)}) collective-permute-start(bf16[2,256,128]{2,1,0:T(8,128)(2,1)S(1)} %get-tuple-element.28), channel_id=1, source_target_pairs={{0,20},{4,16},{8,28},{12,24},{16,4},{20,0},{24,12},{28,8},{1,21},{... | collective-permute-start | bytes 393224 | tf_op jit(solution)/shard_map/ppermute | solution.py:234
  11.8 5.3 %collective-permute-start.6 = (bf16[2,256,128]{2,1,0:T(8,128)(2,1)S(1)}, bf16[2,256,128]{2,1,0:T(8,128)(2,1)S(1)}, u32[]{:S(2)}, u32[]{:S(2)}) collective-permute-start(bf16[2,256,128]{2,1,0:T(8,128)(2,1)S(1)} %get-tuple-element.29), channel_id=1, source_target_pairs={{0,4},{4,0},{8,12},{12,8},{16,20},{20,16},{24,28},{28,24},{1,5},{5... | collective-permute-start | bytes 393224 | tf_op jit(solution)/shard_map/ppermute | solution.py:234
  11.8 5.3 %copy-start.1 = (s32[8,128]{1,0:T(8,128)S(1)}, s32[8,128]{1,0:T(8,128)}, u32[]{:S(2)}) copy-start(s32[8,128]{1,0:T(8,128)} %refs_8_.1) | copy-start | bytes 12292
  20.2 1.7 %collective-permute-start.7 = (s16[4,22,16,128]{3,2,1,0:T(8,128)(2,1)S(1)}, s16[4,22,16,128]{3,2,1,0:T(8,128)(2,1)S(1)}, u32[]{:S(2)}, u32[]{:S(2)}) collective-permute-start(s16[4,22,16,128]{3,2,1,0:T(8,128)(2,1)S(1)} %get-tuple-element.32), channel_id=1, source_target_pairs={{0,4},{4,0},{8,12},{12,8},{16,20},{20,16},{24,28},{28,24},{1,5},{5... | collective-permute-start | bytes 1081352 | tf_op jit(solution)/shard_map/ppermute | solution.py:234
  22.2 4.7 %collective-permute-start.8 = (s16[22,16,128]{2,1,0:T(8,128)(2,1)S(1)}, s16[22,16,128]{2,1,0:T(8,128)(2,1)S(1)}, u32[]{:S(2)}, u32[]{:S(2)}) collective-permute-start(s16[22,16,128]{2,1,0:T(8,128)(2,1)S(1)} %get-tuple-element.33), channel_id=1, source_target_pairs={{0,8},{4,12},{8,0},{12,4},{16,24},{20,28},{24,16},{28,20},{1,9},{5... | collective-permute-start | bytes 270344 | tf_op jit(solution)/shard_map/ppermute | solution.py:234
  23.7 5.5 %collective-permute-start.9 = (s16[22,16,128]{2,1,0:T(8,128)(2,1)S(1)}, s16[22,16,128]{2,1,0:T(8,128)(2,1)S(1)}, u32[]{:S(2)}, u32[]{:S(2)}) collective-permute-start(s16[22,16,128]{2,1,0:T(8,128)(2,1)S(1)} %get-tuple-element.34), channel_id=1, source_target_pairs={{0,16},{4,20},{8,24},{12,28},{16,0},{20,4},{24,8},{28,12},{1,17},{... | collective-permute-start | bytes 270344 | tf_op jit(solution)/shard_map/ppermute | solution.py:234
  25.3 5.4 %collective-permute-start.10 = (s16[22,16,128]{2,1,0:T(8,128)(2,1)S(1)}, s16[22,16,128]{2,1,0:T(8,128)(2,1)S(1)}, u32[]{:S(2)}, u32[]{:S(2)}) collective-permute-start(s16[22,16,128]{2,1,0:T(8,128)(2,1)S(1)} %get-tuple-element.35), channel_id=1, source_target_pairs={{0,24},{4,28},{8,16},{12,20},{16,8},{20,12},{24,0},{28,4},{1,25},{... | collective-permute-start | bytes 270344 | tf_op jit(solution)/shard_map/ppermute | solution.py:234
  30.9 5.1 %collective-permute-start.11 = (s16[7,16,128]{2,1,0:T(8,128)(2,1)S(1)}, s16[7,16,128]{2,1,0:T(8,128)(2,1)S(1)}, u32[]{:S(2)}, u32[]{:S(2)}) collective-permute-start(s16[7,16,128]{2,1,0:T(8,128)(2,1)S(1)} %get-tuple-element.37), channel_id=1, source_target_pairs={{0,2},{1,3},{2,0},{3,1},{4,6},{5,7},{6,4},{7,5},{8,10},{9,11},{10,... | collective-permute-start | bytes 86024 | tf_op jit(solution)/shard_map/ppermute | solution.py:234
  33.5 5.7 %collective-permute-start.12 = (s16[7,16,128]{2,1,0:T(8,128)(2,1)S(1)}, s16[7,16,128]{2,1,0:T(8,128)(2,1)S(1)}, u32[]{:S(2)}, u32[]{:S(2)}) collective-permute-start(s16[7,16,128]{2,1,0:T(8,128)(2,1)S(1)} %get-tuple-element.38), channel_id=1, source_target_pairs={{0,3},{1,2},{2,1},{3,0},{4,7},{5,6},{6,5},{7,4},{8,11},{9,10},{10,... | collective-permute-start | bytes 86024 | tf_op jit(solution)/shard_map/ppermute | solution.py:234
  34.9 4.3 %collective-permute-start.13 = (s16[7,16,128]{2,1,0:T(8,128)(2,1)S(1)}, s16[7,16,128]{2,1,0:T(8,128)(2,1)S(1)}, u32[]{:S(2)}, u32[]{:S(2)}) collective-permute-start(s16[7,16,128]{2,1,0:T(8,128)(2,1)S(1)} %get-tuple-element.39), channel_id=1, source_target_pairs={{0,1},{1,0},{2,3},{3,2},{4,5},{5,4},{6,7},{7,6},{8,9},{9,8},{10,11... | collective-permute-start | bytes 86024 | tf_op jit(solution)/shard_map/ppermute | solution.py:234

commit v25 on v24

--- a/solution.py
+++ b/solution.py
@@ -251,7 +251,7 @@
 
 def stack_kernel(windows, where_ref, *refs):
     sums_refs, out_ref = refs[:-1], refs[-1]
-    blocks, copies, rows, _ = out_ref.shape
+    copies, blocks, rows, _ = out_ref.shape
     _, lag_rows, chans = sums_refs[0].shape
     per_sum = windows // len(sums_refs)
     heads = [decode(sums_ref[6]) for sums_ref in sums_refs]
@@ -288,17 +288,17 @@
             begin = block * per_block + part * rows
             piece = jnp.where(part_of == part, turned[begin : begin + rows, :], piece)
         for copy in range(copies):
-            out_ref[block, copy, :, :] = piece
+            out_ref[copy, block, :, :] = piece
 
 
 def place_kernel(parts_ref, out_ref):
-    groups, offset_count, rows, lanes = parts_ref.shape
+    offset_count, groups, rows, lanes = parts_ref.shape
     half = out_ref.shape[2] // 2
     lag_rows = half // groups
     parts = out_ref.shape[0] // rows
     unit = lax.broadcasted_iota(jnp.int32, (1, lanes), 1) // lag_rows
     for number in range(offset_count):
-        pieces = [parts_ref[group, number] for group in range(groups)]
+        pieces = [parts_ref[number, group] for group in range(groups)]
         for part in range(parts):
             sides = [jnp.zeros((rows, lanes), jnp.float32)] * 2
             for group, piece in enumerate(pieces):
@@ -377,14 +377,14 @@
     )(tm_where, *exchange(pairs, "chan", chip_order))
     pieces = pl.pallas_call(
         functools.partial(stack_kernel, windows * tm_count),
-        out_shape=jax.ShapeDtypeStruct((chan_count, tm_count, piece_rows, chans), jnp.float32),
+        out_shape=jax.ShapeDtypeStruct((tm_count, chan_count, piece_rows, chans), jnp.float32),
         in_specs=[smem] + [vmem] * tm_count,
         out_specs=vmem,
         compiler_params=params,
         name="stack_pairs",
     )(chan_where, *exchange(sums, "tm", tm_order))
     shape = (chan_count * tm_count, piece_rows, chans)
-    arrived = lax.all_to_all(pieces.reshape(shape), ("chan", "tm"), 0, 0, tiled=True)
+    arrived = lax.all_to_all(pieces.reshape(shape), ("tm", "chan"), 0, 0, tiled=True)
     return pl.pallas_call(
         place_kernel,
         out_shape=jax.ShapeDtypeStruct((CH_DEV, offset_count, LAGS), jnp.float32),
@@ -392,7 +392,7 @@
         out_specs=vmem,
         compiler_params=params,
         name="place_lags",
-    )(arrived.reshape(chan_count, tm_count, piece_rows, chans))
+    )(arrived.reshape(tm_count, chan_count, piece_rows, chans))
 
 
 def shifted(value, axis, steps):

time: 50.5 us -> 50.4 us (level)
  no operation moved by 1% of the time
where the time goes in v25:
time: 50.4 us; the launch traced here: 50.2 us
  waiting for transfers between devices  17.6 us (35%)
  starting transfers between devices  15.8 us (31%)
  blocking collectives  10.1 us (20%)
  Pallas kernels  6.77 us (13%)
    ppermute x14, waiting for transfers between devices, exchange(): lax.ppermute(piece, axis, [(source, source ^ k) for source in range(count)])  17.6 us
    ppermute x14, starting transfers between devices, exchange(): lax.ppermute(piece, axis, [(source, source ^ k) for source in range(count)])  15.8 us
    all_to_all x1, blocking collectives, window_shards(): lax.all_to_all(pieces.reshape(shape), ('tm', 'chan'), 0, 0, tiled=True)  10.1 us
    pallas_call x1, Pallas kernels, window_shards(): pl.pallas_call(functools.partial(window_kernel, chan_order), out_shape=[j...  3.14 us
    pallas_call x2, Pallas kernels, window_shards(): pl.pallas_call(functools.partial(split_kernel, part), out_shape=[jax.Shap...  2.32 us
  transfers between devices with their start and end apart: 14, of which 10 were waited for; matrix products, arithmetic and copies ran while one was open for 0% of the time, Pallas kernels for 2%

profile of v25, /device:TPU:0, one launch (start us, length us, event | category | flops | bytes accessed | tf_op | source)
XLA Modules:
  0.0 50.2 jit_solution(1604388133197672556)
XLA Ops:
  0.0 1.1 %split_windows.2 = (bf16[2,256,128]{2,1,0:T(8,128)(2,1)S(1)}, bf16[2,256,128]{2,1,0:T(8,128)(2,1)S(1)}) custom-call(bf16[2,8,256,128]{3,2,1,0:T(8,128)(2,1)} %spec_ref.3), custom_call_target="tpu_custom_call" | custom-call | tf_op jit(solution)/shard_map/split_windows/pallas_call | solution.py:335
  1.1 4.0 %collective-permute-start = (bf16[2,256,128]{2,1,0:T(8,128)(2,1)S(1)}, bf16[2,256,128]{2,1,0:T(8,128)(2,1)S(1)}, u32[]{:S(2)}, u32[]{:S(2)}) collective-permute-start(bf16[2,256,128]{2,1,0:T(8,128)(2,1)S(1)} %get-tuple-element.23), channel_id=1, source_target_pairs={{0,24},{4,28},{8,16},{12,20},{16,8},{20,12},{24,0},{28,4},{1,25},{... | collective-permute-start | bytes 393224 | tf_op jit(solution)/shard_map/ppermute | solution.py:234
  5.0 1.3 %split_windows.3 = (bf16[2,256,128]{2,1,0:T(8,128)(2,1)S(1)}, bf16[2,256,128]{2,1,0:T(8,128)(2,1)S(1)}, bf16[2,256,128]{2,1,0:T(8,128)(2,1)S(1)}, bf16[2,256,128...) custom-call(bf16[2,8,256,128]{3,2,1,0:T(8,128)(2,1)} %spec_ref.3), custom_call_target="tpu_custom_call" | custom-call | tf_op jit(solution)/shard_map/split_windows/pallas_call | solution.py:335
  6.3 1.2 %collective-permute-start.2 = (bf16[2,256,128]{2,1,0:T(8,128)(2,1)S(1)}, bf16[2,256,128]{2,1,0:T(8,128)(2,1)S(1)}, u32[]{:S(2)}, u32[]{:S(2)}) collective-permute-start(bf16[2,256,128]{2,1,0:T(8,128)(2,1)S(1)} %get-tuple-element.25), channel_id=1, source_target_pairs={{0,8},{4,12},{8,0},{12,4},{16,24},{20,28},{24,16},{28,20},{1,9},{5... | collective-permute-start | bytes 393224 | tf_op jit(solution)/shard_map/ppermute | solution.py:234
  7.5 1.5 %collective-permute-start.3 = (bf16[2,256,128]{2,1,0:T(8,128)(2,1)S(1)}, bf16[2,256,128]{2,1,0:T(8,128)(2,1)S(1)}, u32[]{:S(2)}, u32[]{:S(2)}) collective-permute-start(bf16[2,256,128]{2,1,0:T(8,128)(2,1)S(1)} %get-tuple-element.26), channel_id=1, source_target_pairs={{0,16},{4,20},{8,24},{12,28},{16,0},{20,4},{24,8},{28,12},{1,17},{... | collective-permute-start | bytes 393224 | tf_op jit(solution)/shard_map/ppermute | solution.py:234
  9.0 0.6 %collective-permute-start.4 = (bf16[2,256,128]{2,1,0:T(8,128)(2,1)S(1)}, bf16[2,256,128]{2,1,0:T(8,128)(2,1)S(1)}, u32[]{:S(2)}, u32[]{:S(2)}) collective-permute-start(bf16[2,256,128]{2,1,0:T(8,128)(2,1)S(1)} %get-tuple-element.27), channel_id=1, source_target_pairs={{0,12},{4,8},{8,4},{12,0},{16,28},{20,24},{24,20},{28,16},{1,13},{... | collective-permute-start | bytes 393224 | tf_op jit(solution)/shard_map/ppermute | solution.py:234
  9.6 0.6 %collective-permute-start.5 = (bf16[2,256,128]{2,1,0:T(8,128)(2,1)S(1)}, bf16[2,256,128]{2,1,0:T(8,128)(2,1)S(1)}, u32[]{:S(2)}, u32[]{:S(2)}) collective-permute-start(bf16[2,256,128]{2,1,0:T(8,128)(2,1)S(1)} %get-tuple-element.28), channel_id=1, source_target_pairs={{0,20},{4,16},{8,28},{12,24},{16,4},{20,0},{24,12},{28,8},{1,21},{... | collective-permute-start | bytes 393224 | tf_op jit(solution)/shard_map/ppermute | solution.py:234
  10.1 1.6 %collective-permute-done.1.refs_1_ = bf16[2,256,128]{2,1,0:T(8,128)(2,1)S(1)} collective-permute-done((bf16[2,256,128]{2,1,0:T(8,128)(2,1)S(1)}, bf16[2,256,128]{2,1,0:T(8,128)(2,1)S(1)}, u32[]{:S(2)}, u32[]{:S(2)}) %collective-permute-start.1) | collective-permute-done | bytes 131104 | tf_op jit(solution)/shard_map/ppermute | solution.py:234
  11.8 3.5 %collective-permute-done.2.refs_2_ = bf16[2,256,128]{2,1,0:T(8,128)(2,1)S(1)} collective-permute-done((bf16[2,256,128]{2,1,0:T(8,128)(2,1)S(1)}, bf16[2,256,128]{2,1,0:T(8,128)(2,1)S(1)}, u32[]{:S(2)}, u32[]{:S(2)}) %collective-permute-start.2) | collective-permute-done | bytes 131104 | tf_op jit(solution)/shard_map/ppermute | solution.py:234
  15.2 1.1 %collective-permute-done.4.refs_4_ = bf16[2,256,128]{2,1,0:T(8,128)(2,1)S(1)} collective-permute-done((bf16[2,256,128]{2,1,0:T(8,128)(2,1)S(1)}, bf16[2,256,128]{2,1,0:T(8,128)(2,1)S(1)}, u32[]{:S(2)}, u32[]{:S(2)}) %collective-permute-start.4) | collective-permute-done | bytes 131104 | tf_op jit(solution)/shard_map/ppermute | solution.py:234
  16.4 0.7 %collective-permute-done.5.refs_5_ = bf16[2,256,128]{2,1,0:T(8,128)(2,1)S(1)} collective-permute-done((bf16[2,256,128]{2,1,0:T(8,128)(2,1)S(1)}, bf16[2,256,128]{2,1,0:T(8,128)(2,1)S(1)}, u32[]{:S(2)}, u32[]{:S(2)}) %collective-permute-start.5) | collective-permute-done | bytes 131104 | tf_op jit(solution)/shard_map/ppermute | solution.py:234
  17.1 3.1 %window_pairs.1 = (s16[4,22,16,128]{3,2,1,0:T(8,128)(2,1)S(1)}, s16[4,22,16,128]{3,2,1,0:T(8,128)(2,1)S(1)}) custom-call(s32[4]{0:T(128)} %offs_hbm_ref.1, s32[1]{0:T(128)} %bitcast.where_ref, bf16[2,256,128]{2,1,0:T(8,128)(2,1)S(1)} %collective-permute-done.refs_0_, bf16[2,256,128]{2,1,0:T(8,128)(2,1)S(1)} %collective-permute-done.1.refs_1_, ...), custom_call_target="tpu_custom_call" | custom-call | tf_op jit(solution)/shard_map/window_pairs/pallas_call | solution.py:346
  20.4 1.6 %collective-permute-done.7.far_ref = s16[4,22,16,128]{3,2,1,0:T(8,128)(2,1)S(1)} collective-permute-done((s16[4,22,16,128]{3,2,1,0:T(8,128)(2,1)S(1)}, s16[4,22,16,128]{3,2,1,0:T(8,128)(2,1)S(1)}, u32[]{:S(2)}, u32[]{:S(2)}) %collective-permute-start.7) | collective-permute-done | bytes 360480 | tf_op jit(solution)/shard_map/ppermute | solution.py:234
  22.2 1.6 %collective-permute-start.8 = (s16[22,16,128]{2,1,0:T(8,128)(2,1)S(1)}, s16[22,16,128]{2,1,0:T(8,128)(2,1)S(1)}, u32[]{:S(2)}, u32[]{:S(2)}) collective-permute-start(s16[22,16,128]{2,1,0:T(8,128)(2,1)S(1)} %get-tuple-element.33), channel_id=1, source_target_pairs={{0,8},{4,12},{8,0},{12,4},{16,24},{20,28},{24,16},{28,20},{1,9},{5... | collective-permute-start | bytes 270344 | tf_op jit(solution)/shard_map/ppermute | solution.py:234
  23.7 1.6 %collective-permute-start.9 = (s16[22,16,128]{2,1,0:T(8,128)(2,1)S(1)}, s16[22,16,128]{2,1,0:T(8,128)(2,1)S(1)}, u32[]{:S(2)}, u32[]{:S(2)}) collective-permute-start(s16[22,16,128]{2,1,0:T(8,128)(2,1)S(1)} %get-tuple-element.34), channel_id=1, source_target_pairs={{0,16},{4,20},{8,24},{12,28},{16,0},{20,4},{24,8},{28,12},{1,17},{... | collective-permute-start | bytes 270344 | tf_op jit(solution)/shard_map/ppermute | solution.py:234
  25.7 1.2 %collective-permute-done.8.refs_0_ = s16[22,16,128]{2,1,0:T(8,128)(2,1)S(1)} collective-permute-done((s16[22,16,128]{2,1,0:T(8,128)(2,1)S(1)}, s16[22,16,128]{2,1,0:T(8,128)(2,1)S(1)}, u32[]{:S(2)}, u32[]{:S(2)}) %collective-permute-start.8) | collective-permute-done | bytes 90144 | tf_op jit(solution)/shard_map/ppermute | solution.py:234
  26.9 2.4 %collective-permute-done.9.refs_1_ = s16[22,16,128]{2,1,0:T(8,128)(2,1)S(1)} collective-permute-done((s16[22,16,128]{2,1,0:T(8,128)(2,1)S(1)}, s16[22,16,128]{2,1,0:T(8,128)(2,1)S(1)}, u32[]{:S(2)}, u32[]{:S(2)}) %collective-permute-start.9) | collective-permute-done | bytes 90144 | tf_op jit(solution)/shard_map/ppermute | solution.py:234
  29.3 1.5 %collective-permute-done.10.refs_2_ = s16[22,16,128]{2,1,0:T(8,128)(2,1)S(1)} collective-permute-done((s16[22,16,128]{2,1,0:T(8,128)(2,1)S(1)}, s16[22,16,128]{2,1,0:T(8,128)(2,1)S(1)}, u32[]{:S(2)}, u32[]{:S(2)}) %collective-permute-start.10) | collective-permute-done | bytes 90144 | tf_op jit(solution)/shard_map/ppermute | solution.py:234
  30.9 2.7 %collective-permute-start.11 = (s16[7,16,128]{2,1,0:T(8,128)(2,1)S(1)}, s16[7,16,128]{2,1,0:T(8,128)(2,1)S(1)}, u32[]{:S(2)}, u32[]{:S(2)}) collective-permute-start(s16[7,16,128]{2,1,0:T(8,128)(2,1)S(1)} %get-tuple-element.37), channel_id=1, source_target_pairs={{0,2},{1,3},{2,0},{3,1},{4,6},{5,7},{6,4},{7,5},{8,10},{9,11},{10,... | collective-permute-start | bytes 86024 | tf_op jit(solution)/shard_map/ppermute | solution.py:234
  33.5 1.4 %collective-permute-start.12 = (s16[7,16,128]{2,1,0:T(8,128)(2,1)S(1)}, s16[7,16,128]{2,1,0:T(8,128)(2,1)S(1)}, u32[]{:S(2)}, u32[]{:S(2)}) collective-permute-start(s16[7,16,128]{2,1,0:T(8,128)(2,1)S(1)} %get-tuple-element.38), channel_id=1, source_target_pairs={{0,3},{1,2},{2,1},{3,0},{4,7},{5,6},{6,5},{7,4},{8,11},{9,10},{10,... | collective-permute-start | bytes 86024 | tf_op jit(solution)/shard_map/ppermute | solution.py:234
  35.1 0.9 %collective-permute-done.11.refs_0_ = s16[7,16,128]{2,1,0:T(8,128)(2,1)S(1)} collective-permute-done((s16[7,16,128]{2,1,0:T(8,128)(2,1)S(1)}, s16[7,16,128]{2,1,0:T(8,128)(2,1)S(1)}, u32[]{:S(2)}, u32[]{:S(2)}) %collective-permute-start.11) | collective-permute-done | bytes 28704 | tf_op jit(solution)/shard_map/ppermute | solution.py:234
  36.0 3.2 %collective-permute-done.12.refs_1_ = s16[7,16,128]{2,1,0:T(8,128)(2,1)S(1)} collective-permute-done((s16[7,16,128]{2,1,0:T(8,128)(2,1)S(1)}, s16[7,16,128]{2,1,0:T(8,128)(2,1)S(1)}, u32[]{:S(2)}, u32[]{:S(2)}) %collective-permute-start.12) | collective-permute-done | bytes 28704 | tf_op jit(solution)/shard_map/ppermute | solution.py:234
  39.4 10.1 %all_to_all.5 = f32[32,4,128]{2,1,0:T(4,128)S(1)} all-to-all(f32[32,4,128]{2,1,0:T(4,128)S(1)} %bitcast.5), channel_id=1, replica_groups=mesh['chan'=8,'tm'=4] {'tm','chan'}, dimensions={0} | all-to-all | bytes 131072 | tf_op jit(solution)/shard_map/all_to_all | solution.py:387
  49.5 0.8 %place_lags.1 = f32[16,4,256]{2,1,0:T(4,128)} custom-call(f32[4,8,4,128]{3,2,1,0:T(4,128)S(1)} %bitcast.4), custom_call_target="tpu_custom_call" | custom-call | tf_op jit(solution)/shard_map/place_lags/pallas_call | solution.py:388
  (16 shorter events, 1.4 us)
Async XLA Ops:
  0.0 17.1 %copy-start = (bf16[16,2,8,16,128]{4,3,2,1,0:T(8,128)(2,1)S(1)}, bf16[16,2,8,16,128]{4,3,2,1,0:T(8,128)(2,1)}, u32[]{:S(2)}) copy-start(bf16[16,2,8,16,128]{4,3,2,1,0:T(8,128)(2,1)} %constant.11.clone.refs_9_) | copy-start | bytes 3145732
  1.1 8.5 %collective-permute-start = (bf16[2,256,128]{2,1,0:T(8,128)(2,1)S(1)}, bf16[2,256,128]{2,1,0:T(8,128)(2,1)S(1)}, u32[]{:S(2)}, u32[]{:S(2)}) collective-permute-start(bf16[2,256,128]{2,1,0:T(8,128)(2,1)S(1)} %get-tuple-element.23), channel_id=1, source_target_pairs={{0,24},{4,28},{8,16},{12,20},{16,8},{20,12},{24,0},{28,4},{1,25},{... | collective-permute-start | bytes 393224 | tf_op jit(solution)/shard_map/ppermute | solution.py:234
  5.0 6.7 %collective-permute-start.1 = (bf16[2,256,128]{2,1,0:T(8,128)(2,1)S(1)}, bf16[2,256,128]{2,1,0:T(8,128)(2,1)S(1)}, u32[]{:S(2)}, u32[]{:S(2)}) collective-permute-start(bf16[2,256,128]{2,1,0:T(8,128)(2,1)S(1)} %get-tuple-element.24), channel_id=1, source_target_pairs={{0,28},{4,24},{8,20},{12,16},{16,12},{20,8},{24,4},{28,0},{1,29},{... | collective-permute-start | bytes 393224 | tf_op jit(solution)/shard_map/ppermute | solution.py:234
  6.3 8.9 %collective-permute-start.2 = (bf16[2,256,128]{2,1,0:T(8,128)(2,1)S(1)}, bf16[2,256,128]{2,1,0:T(8,128)(2,1)S(1)}, u32[]{:S(2)}, u32[]{:S(2)}) collective-permute-start(bf16[2,256,128]{2,1,0:T(8,128)(2,1)S(1)} %get-tuple-element.25), channel_id=1, source_target_pairs={{0,8},{4,12},{8,0},{12,4},{16,24},{20,28},{24,16},{28,20},{1,9},{5... | collective-permute-start | bytes 393224 | tf_op jit(solution)/shard_map/ppermute | solution.py:234
  7.5 7.7 %collective-permute-start.3 = (bf16[2,256,128]{2,1,0:T(8,128)(2,1)S(1)}, bf16[2,256,128]{2,1,0:T(8,128)(2,1)S(1)}, u32[]{:S(2)}, u32[]{:S(2)}) collective-permute-start(bf16[2,256,128]{2,1,0:T(8,128)(2,1)S(1)} %get-tuple-element.26), channel_id=1, source_target_pairs={{0,16},{4,20},{8,24},{12,28},{16,0},{20,4},{24,8},{28,12},{1,17},{... | collective-permute-start | bytes 393224 | tf_op jit(solution)/shard_map/ppermute | solution.py:234
  9.0 7.4 %collective-permute-start.4 = (bf16[2,256,128]{2,1,0:T(8,128)(2,1)S(1)}, bf16[2,256,128]{2,1,0:T(8,128)(2,1)S(1)}, u32[]{:S(2)}, u32[]{:S(2)}) collective-permute-start(bf16[2,256,128]{2,1,0:T(8,128)(2,1)S(1)} %get-tuple-element.27), channel_id=1, source_target_pairs={{0,12},{4,8},{8,4},{12,0},{16,28},{20,24},{24,20},{28,16},{1,13},{... | collective-permute-start | bytes 393224 | tf_op jit(solution)/shard_map/ppermute | solution.py:234
  9.6 7.5 %collective-permute-start.5 = (bf16[2,256,128]{2,1,0:T(8,128)(2,1)S(1)}, bf16[2,256,128]{2,1,0:T(8,128)(2,1)S(1)}, u32[]{:S(2)}, u32[]{:S(2)}) collective-permute-start(bf16[2,256,128]{2,1,0:T(8,128)(2,1)S(1)} %get-tuple-element.28), channel_id=1, source_target_pairs={{0,20},{4,16},{8,28},{12,24},{16,4},{20,0},{24,12},{28,8},{1,21},{... | collective-permute-start | bytes 393224 | tf_op jit(solution)/shard_map/ppermute | solution.py:234
  11.8 5.3 %collective-permute-start.6 = (bf16[2,256,128]{2,1,0:T(8,128)(2,1)S(1)}, bf16[2,256,128]{2,1,0:T(8,128)(2,1)S(1)}, u32[]{:S(2)}, u32[]{:S(2)}) collective-permute-start(bf16[2,256,128]{2,1,0:T(8,128)(2,1)S(1)} %get-tuple-element.29), channel_id=1, source_target_pairs={{0,4},{4,0},{8,12},{12,8},{16,20},{20,16},{24,28},{28,24},{1,5},{5... | collective-permute-start | bytes 393224 | tf_op jit(solution)/shard_map/ppermute | solution.py:234
  11.8 5.3 %copy-start.1 = (s32[8,128]{1,0:T(8,128)S(1)}, s32[8,128]{1,0:T(8,128)}, u32[]{:S(2)}) copy-start(s32[8,128]{1,0:T(8,128)} %refs_8_.1) | copy-start | bytes 12292
  20.2 1.7 %collective-permute-start.7 = (s16[4,22,16,128]{3,2,1,0:T(8,128)(2,1)S(1)}, s16[4,22,16,128]{3,2,1,0:T(8,128)(2,1)S(1)}, u32[]{:S(2)}, u32[]{:S(2)}) collective-permute-start(s16[4,22,16,128]{3,2,1,0:T(8,128)(2,1)S(1)} %get-tuple-element.32), channel_id=1, source_target_pairs={{0,4},{4,0},{8,12},{12,8},{16,20},{20,16},{24,28},{28,24},{1,5},{5... | collective-permute-start | bytes 1081352 | tf_op jit(solution)/shard_map/ppermute | solution.py:234
  22.2 4.7 %collective-permute-start.8 = (s16[22,16,128]{2,1,0:T(8,128)(2,1)S(1)}, s16[22,16,128]{2,1,0:T(8,128)(2,1)S(1)}, u32[]{:S(2)}, u32[]{:S(2)}) collective-permute-start(s16[22,16,128]{2,1,0:T(8,128)(2,1)S(1)} %get-tuple-element.33), channel_id=1, source_target_pairs={{0,8},{4,12},{8,0},{12,4},{16,24},{20,28},{24,16},{28,20},{1,9},{5... | collective-permute-start | bytes 270344 | tf_op jit(solution)/shard_map/ppermute | solution.py:234
  23.7 5.5 %collective-permute-start.9 = (s16[22,16,128]{2,1,0:T(8,128)(2,1)S(1)}, s16[22,16,128]{2,1,0:T(8,128)(2,1)S(1)}, u32[]{:S(2)}, u32[]{:S(2)}) collective-permute-start(s16[22,16,128]{2,1,0:T(8,128)(2,1)S(1)} %get-tuple-element.34), channel_id=1, source_target_pairs={{0,16},{4,20},{8,24},{12,28},{16,0},{20,4},{24,8},{28,12},{1,17},{... | collective-permute-start | bytes 270344 | tf_op jit(solution)/shard_map/ppermute | solution.py:234
  25.3 5.4 %collective-permute-start.10 = (s16[22,16,128]{2,1,0:T(8,128)(2,1)S(1)}, s16[22,16,128]{2,1,0:T(8,128)(2,1)S(1)}, u32[]{:S(2)}, u32[]{:S(2)}) collective-permute-start(s16[22,16,128]{2,1,0:T(8,128)(2,1)S(1)} %get-tuple-element.35), channel_id=1, source_target_pairs={{0,24},{4,28},{8,16},{12,20},{16,8},{20,12},{24,0},{28,4},{1,25},{... | collective-permute-start | bytes 270344 | tf_op jit(solution)/shard_map/ppermute | solution.py:234
  30.9 5.1 %collective-permute-start.11 = (s16[7,16,128]{2,1,0:T(8,128)(2,1)S(1)}, s16[7,16,128]{2,1,0:T(8,128)(2,1)S(1)}, u32[]{:S(2)}, u32[]{:S(2)}) collective-permute-start(s16[7,16,128]{2,1,0:T(8,128)(2,1)S(1)} %get-tuple-element.37), channel_id=1, source_target_pairs={{0,2},{1,3},{2,0},{3,1},{4,6},{5,7},{6,4},{7,5},{8,10},{9,11},{10,... | collective-permute-start | bytes 86024 | tf_op jit(solution)/shard_map/ppermute | solution.py:234
  33.5 5.7 %collective-permute-start.12 = (s16[7,16,128]{2,1,0:T(8,128)(2,1)S(1)}, s16[7,16,128]{2,1,0:T(8,128)(2,1)S(1)}, u32[]{:S(2)}, u32[]{:S(2)}) collective-permute-start(s16[7,16,128]{2,1,0:T(8,128)(2,1)S(1)} %get-tuple-element.38), channel_id=1, source_target_pairs={{0,3},{1,2},{2,1},{3,0},{4,7},{5,6},{6,5},{7,4},{8,11},{9,10},{10,... | collective-permute-start | bytes 86024 | tf_op jit(solution)/shard_map/ppermute | solution.py:234
  34.9 4.3 %collective-permute-start.13 = (s16[7,16,128]{2,1,0:T(8,128)(2,1)S(1)}, s16[7,16,128]{2,1,0:T(8,128)(2,1)S(1)}, u32[]{:S(2)}, u32[]{:S(2)}) collective-permute-start(s16[7,16,128]{2,1,0:T(8,128)(2,1)S(1)} %get-tuple-element.39), channel_id=1, source_target_pairs={{0,1},{1,0},{2,3},{3,2},{4,5},{5,4},{6,7},{7,6},{8,9},{9,8},{10,11... | collective-permute-start | bytes 86024 | tf_op jit(solution)/shard_map/ppermute | solution.py:234

commit v26 on v24

--- a/solution.py
+++ b/solution.py
@@ -96,7 +96,10 @@
     line = lax.broadcasted_iota(jnp.int32, (lag_rows, chans), 0)
     usable = qual_ref[pl.ds(me, 1), :].astype(jnp.float32)
     levels = jnp.zeros((lag_rows, chans), jnp.float32)
-    groups = [k ^ core for core in range(2) for k in chips(chan_count)]
+    core = me & 1
+    orders = chips(chan_count)
+    groups = [partner(orders, place, core) for place in range(chip_count)]
+    groups += [partner(orders, place, 1 - core) ^ 1 for place in range(chip_count)]
     fetch.wait()
     per_band = table_ref.shape[0] // chan_count
     chunks = [(me ^ k) * per_band + chunk for k in order for chunk in range(per_band)]
@@ -178,8 +181,9 @@
             out_ref[block, :, :] = encode(total)
 
 
-def sum_kernel(order, scale, where_ref, *refs):
-    code_refs, out_refs, held_ref = refs[: -len(order) - 1], refs[-len(order) - 1 : -1], refs[-1]
+def sum_kernel(orders, scale, where_ref, core_ref, *refs):
+    count = len(orders[0])
+    code_refs, out_refs, held_ref = refs[: -count - 1], refs[-count - 1 : -1], refs[-1]
     blocks, _, chans = code_refs[0].shape
     slots = held_ref.shape[0]
     heads = [decode(codes_ref[blocks - 1]) for codes_ref in code_refs]
@@ -216,8 +220,8 @@
         head = jnp.where(line == 0, code, offsets[number])
         for part, value in enumerate([sums[0] * upscale, sums[1] * upscale, *sums[2:], head]):
             held_ref[number, part, :, :] = encode(value)
-    for k, out_ref in zip(order, out_refs):
-        out_ref[...] = held_ref[where_ref[0] ^ k]
+    for place, out_ref in enumerate(out_refs):
+        out_ref[...] = held_ref[where_ref[0] ^ partner(orders, place, core_ref[0] & 1)]
 
 
 def partners(count):
@@ -225,15 +229,31 @@
 
 
 def chips(count):
-    return sorted(range(2, count, 2), key=lambda k: (k.bit_count(), k)) + [0]
-
-
-def exchange(pieces, axis, order):
-    count = lax.axis_size(axis)
-    return [
-        lax.ppermute(piece, axis, [(source, source ^ k) for source in range(count)]) if k else piece
-        for k, piece in zip(order, pieces)
-    ]
+    near = [k for k in range(2, count, 2) if k.bit_count() == 1]
+    far = [k for k in range(2, count, 2) if k.bit_count() > 1]
+    return near[::-1] + far + [0], near + far + [0]
+
+
+def planes(count):
+    others = partners(count)[:-1]
+    return others + [0], others[1:] + others[:1] + [0]
+
+
+def partner(orders, place, core):
+    return jnp.where(core == 0, orders[0][place], orders[1][place])
+
+
+def exchange(pieces, orders, over_tm=False):
+    chan_count, tm_count = lax.axis_size("chan"), lax.axis_size("tm")
+    arrived = []
+    for place, piece in enumerate(pieces):
+        pairs = []
+        for source in range(chan_count * tm_count):
+            k = orders[source // tm_count % 2][place]
+            pairs.append((source, source ^ k if over_tm else source ^ (k * tm_count)))
+        moved = any(source != target for source, target in pairs)
+        arrived.append(lax.ppermute(piece, ("chan", "tm"), pairs) if moved else piece)
+    return arrived
 
 
 def split_kernel(order, spec_ref, *refs):
@@ -327,7 +347,7 @@
     tm_index = lax.axis_index("tm").astype(jnp.int32)
     chan_where, tm_where = chan_index.reshape(1), tm_index.reshape(1)
 
-    chan_order, tm_order = partners(chan_count), partners(tm_count)
+    chan_order, tm_orders = partners(chan_count), planes(tm_count)
     kept = pl.BlockSpec(memory_space=pltpu.HBM)
     spectra = pltpu.with_memory_space_constraint(spectra, pltpu.HBM)
     pieces = []
@@ -341,11 +361,11 @@
             compiler_params=params,
             name="split_windows",
         )(spectra)
-    chip_order = chips(chan_count)
+    chip_count = chan_count // 2
     pair_shape = (6 * offset_count - 2, lag_rows, chans)
     own, far = pl.pallas_call(
         functools.partial(window_kernel, chan_order),
-        out_shape=[jax.ShapeDtypeStruct((len(chip_order), *pair_shape), jnp.int16)] * 2,
+        out_shape=[jax.ShapeDtypeStruct((chip_count, *pair_shape), jnp.int16)] * 2,
         in_specs=[kept, smem] + [vmem] * (chan_count + 2),
         out_specs=[vmem] * 2,
         scratch_shapes=[
@@ -357,24 +377,24 @@
         ],
         compiler_params=params,
         name="window_pairs",
-    )(pltpu.with_memory_space_constraint(offsets, pltpu.HBM), chan_where, *exchange(pieces, "chan", chan_order), quality, table)
+    )(pltpu.with_memory_space_constraint(offsets, pltpu.HBM), chan_where, *exchange(pieces, (chan_order, chan_order)), quality, table)
     pairs = pl.pallas_call(
         functools.partial(merge_kernel, offset_count),
-        out_shape=[jax.ShapeDtypeStruct(pair_shape, jnp.int16)] * len(chip_order),
+        out_shape=[jax.ShapeDtypeStruct(pair_shape, jnp.int16)] * chip_count,
         in_specs=[vmem] * 2,
-        out_specs=[vmem] * len(chip_order),
+        out_specs=[vmem] * chip_count,
         compiler_params=params,
         name="merge_windows",
-    )(own, *exchange([far], "chan", [1]))
+    )(own, *exchange([far], ([1], [1])))
     sums = pl.pallas_call(
-        functools.partial(sum_kernel, tm_order, 1.0 / (CODE_TOP * math.sqrt(freqs))),
+        functools.partial(sum_kernel, tm_orders, 1.0 / (CODE_TOP * math.sqrt(freqs))),
         out_shape=[jax.ShapeDtypeStruct((7, lag_rows, chans), jnp.int16)] * tm_count,
-        in_specs=[smem] + [vmem] * len(chip_order),
+        in_specs=[smem, smem] + [vmem] * chip_count,
         out_specs=[vmem] * tm_count,
         scratch_shapes=[pltpu.VMEM((offset_count, 7, lag_rows, chans), jnp.int16)],
         compiler_params=params,
         name="sum_windows",
-    )(tm_where, *exchange(pairs, "chan", chip_order))
+    )(tm_where, chan_where, *exchange(pairs, chips(chan_count)))
     pieces = pl.pallas_call(
         functools.partial(stack_kernel, windows * tm_count),
         out_shape=jax.ShapeDtypeStruct((chan_count, tm_count, piece_rows, chans), jnp.float32),
@@ -382,7 +402,7 @@
         out_specs=vmem,
         compiler_params=params,
         name="stack_pairs",
-    )(chan_where, *exchange(sums, "tm", tm_order))
+    )(chan_where, *exchange(sums, tm_orders, over_tm=True))
     shape = (chan_count * tm_count, piece_rows, chans)
     arrived = lax.all_to_all(pieces.reshape(shape), ("chan", "tm"), 0, 0, tiled=True)
     return pl.pallas_call(

time: 50.5 us -> 50.5 us (level)
  no operation moved by 1% of the time
where the time goes in v26:
time: 50.5 us; the launch traced here: 50.3 us
  waiting for transfers between devices  17.6 us (35%)
  starting transfers between devices  15.8 us (31%)
  blocking collectives  10.2 us (20%)
  Pallas kernels  6.77 us (13%)
    ppermute x14, waiting for transfers between devices, exchange(): lax.ppermute(piece, ('chan', 'tm'), pairs)  17.6 us
    ppermute x14, starting transfers between devices, exchange(): lax.ppermute(piece, ('chan', 'tm'), pairs)  15.8 us
    all_to_all x1, blocking collectives, window_shards(): lax.all_to_all(pieces.reshape(shape), ('chan', 'tm'), 0, 0, tiled=True)  10.2 us
    pallas_call x1, Pallas kernels, window_shards(): pl.pallas_call(functools.partial(window_kernel, chan_order), out_shape=[j...  3.14 us
    pallas_call x2, Pallas kernels, window_shards(): pl.pallas_call(functools.partial(split_kernel, part), out_shape=[jax.Shap...  2.32 us
  transfers between devices with their start and end apart: 14, of which 10 were waited for; matrix products, arithmetic and copies ran while one was open for 0% of the time, Pallas kernels for 2%

profile of v26, /device:TPU:0, one launch (start us, length us, event | category | flops | bytes accessed | tf_op | source)
XLA Modules:
  0.0 50.3 jit_solution(7061822766280543138)
XLA Ops:
  0.0 1.1 %split_windows.2 = (bf16[2,256,128]{2,1,0:T(8,128)(2,1)S(1)}, bf16[2,256,128]{2,1,0:T(8,128)(2,1)S(1)}) custom-call(bf16[2,8,256,128]{3,2,1,0:T(8,128)(2,1)} %spec_ref.3), custom_call_target="tpu_custom_call" | custom-call | tf_op jit(solution)/shard_map/split_windows/pallas_call | solution.py:355
  1.1 4.0 %collective-permute-start = (bf16[2,256,128]{2,1,0:T(8,128)(2,1)S(1)}, bf16[2,256,128]{2,1,0:T(8,128)(2,1)S(1)}, u32[]{:S(2)}, u32[]{:S(2)}) collective-permute-start(bf16[2,256,128]{2,1,0:T(8,128)(2,1)S(1)} %get-tuple-element.23), channel_id=1, source_target_pairs={{0,24},{1,25},{2,26},{3,27},{4,28},{5,29},{6,30},{7,31},{8,16},{9,... | collective-permute-start | bytes 393224 | tf_op jit(solution)/shard_map/ppermute | solution.py:255
  5.0 1.3 %split_windows.3 = (bf16[2,256,128]{2,1,0:T(8,128)(2,1)S(1)}, bf16[2,256,128]{2,1,0:T(8,128)(2,1)S(1)}, bf16[2,256,128]{2,1,0:T(8,128)(2,1)S(1)}, bf16[2,256,128...) custom-call(bf16[2,8,256,128]{3,2,1,0:T(8,128)(2,1)} %spec_ref.3), custom_call_target="tpu_custom_call" | custom-call | tf_op jit(solution)/shard_map/split_windows/pallas_call | solution.py:355
  6.3 1.2 %collective-permute-start.2 = (bf16[2,256,128]{2,1,0:T(8,128)(2,1)S(1)}, bf16[2,256,128]{2,1,0:T(8,128)(2,1)S(1)}, u32[]{:S(2)}, u32[]{:S(2)}) collective-permute-start(bf16[2,256,128]{2,1,0:T(8,128)(2,1)S(1)} %get-tuple-element.25), channel_id=1, source_target_pairs={{0,8},{1,9},{2,10},{3,11},{4,12},{5,13},{6,14},{7,15},{8,0},{9,1},... | collective-permute-start | bytes 393224 | tf_op jit(solution)/shard_map/ppermute | solution.py:255
  7.5 1.5 %collective-permute-start.3 = (bf16[2,256,128]{2,1,0:T(8,128)(2,1)S(1)}, bf16[2,256,128]{2,1,0:T(8,128)(2,1)S(1)}, u32[]{:S(2)}, u32[]{:S(2)}) collective-permute-start(bf16[2,256,128]{2,1,0:T(8,128)(2,1)S(1)} %get-tuple-element.26), channel_id=1, source_target_pairs={{0,16},{1,17},{2,18},{3,19},{4,20},{5,21},{6,22},{7,23},{8,24},{9,... | collective-permute-start | bytes 393224 | tf_op jit(solution)/shard_map/ppermute | solution.py:255
  9.0 0.6 %collective-permute-start.4 = (bf16[2,256,128]{2,1,0:T(8,128)(2,1)S(1)}, bf16[2,256,128]{2,1,0:T(8,128)(2,1)S(1)}, u32[]{:S(2)}, u32[]{:S(2)}) collective-permute-start(bf16[2,256,128]{2,1,0:T(8,128)(2,1)S(1)} %get-tuple-element.27), channel_id=1, source_target_pairs={{0,12},{1,13},{2,14},{3,15},{4,8},{5,9},{6,10},{7,11},{8,4},{9,5},... | collective-permute-start | bytes 393224 | tf_op jit(solution)/shard_map/ppermute | solution.py:255
  9.6 0.6 %collective-permute-start.5 = (bf16[2,256,128]{2,1,0:T(8,128)(2,1)S(1)}, bf16[2,256,128]{2,1,0:T(8,128)(2,1)S(1)}, u32[]{:S(2)}, u32[]{:S(2)}) collective-permute-start(bf16[2,256,128]{2,1,0:T(8,128)(2,1)S(1)} %get-tuple-element.28), channel_id=1, source_target_pairs={{0,20},{1,21},{2,22},{3,23},{4,16},{5,17},{6,18},{7,19},{8,28},{9,... | collective-permute-start | bytes 393224 | tf_op jit(solution)/shard_map/ppermute | solution.py:255
  10.1 1.6 %collective-permute-done.1.refs_1_ = bf16[2,256,128]{2,1,0:T(8,128)(2,1)S(1)} collective-permute-done((bf16[2,256,128]{2,1,0:T(8,128)(2,1)S(1)}, bf16[2,256,128]{2,1,0:T(8,128)(2,1)S(1)}, u32[]{:S(2)}, u32[]{:S(2)}) %collective-permute-start.1) | collective-permute-done | bytes 131104 | tf_op jit(solution)/shard_map/ppermute | solution.py:255
  11.8 3.5 %collective-permute-done.2.refs_2_ = bf16[2,256,128]{2,1,0:T(8,128)(2,1)S(1)} collective-permute-done((bf16[2,256,128]{2,1,0:T(8,128)(2,1)S(1)}, bf16[2,256,128]{2,1,0:T(8,128)(2,1)S(1)}, u32[]{:S(2)}, u32[]{:S(2)}) %collective-permute-start.2) | collective-permute-done | bytes 131104 | tf_op jit(solution)/shard_map/ppermute | solution.py:255
  15.2 1.1 %collective-permute-done.4.refs_4_ = bf16[2,256,128]{2,1,0:T(8,128)(2,1)S(1)} collective-permute-done((bf16[2,256,128]{2,1,0:T(8,128)(2,1)S(1)}, bf16[2,256,128]{2,1,0:T(8,128)(2,1)S(1)}, u32[]{:S(2)}, u32[]{:S(2)}) %collective-permute-start.4) | collective-permute-done | bytes 131104 | tf_op jit(solution)/shard_map/ppermute | solution.py:255
  16.4 0.7 %collective-permute-done.5.refs_5_ = bf16[2,256,128]{2,1,0:T(8,128)(2,1)S(1)} collective-permute-done((bf16[2,256,128]{2,1,0:T(8,128)(2,1)S(1)}, bf16[2,256,128]{2,1,0:T(8,128)(2,1)S(1)}, u32[]{:S(2)}, u32[]{:S(2)}) %collective-permute-start.5) | collective-permute-done | bytes 131104 | tf_op jit(solution)/shard_map/ppermute | solution.py:255
  17.1 3.1 %window_pairs.1 = (s16[4,22,16,128]{3,2,1,0:T(8,128)(2,1)S(1)}, s16[4,22,16,128]{3,2,1,0:T(8,128)(2,1)S(1)}) custom-call(s32[4]{0:T(128)} %offs_hbm_ref.1, s32[1]{0:T(128)} %bitcast.where_ref.core_ref, bf16[2,256,128]{2,1,0:T(8,128)(2,1)S(1)} %collective-permute-done.refs_0_, bf16[2,256,128]{2,1,0:T(8,128)(2,1)S(1)} %collective-permute-done.1.refs_1_, ...), custom_call_target="tpu_custom_call" | custom-call | tf_op jit(solution)/shard_map/window_pairs/pallas_call | solution.py:366
  20.4 1.6 %collective-permute-done.7.far_ref = s16[4,22,16,128]{3,2,1,0:T(8,128)(2,1)S(1)} collective-permute-done((s16[4,22,16,128]{3,2,1,0:T(8,128)(2,1)S(1)}, s16[4,22,16,128]{3,2,1,0:T(8,128)(2,1)S(1)}, u32[]{:S(2)}, u32[]{:S(2)}) %collective-permute-start.7) | collective-permute-done | bytes 360480 | tf_op jit(solution)/shard_map/ppermute | solution.py:255
  22.2 1.6 %collective-permute-start.8 = (s16[22,16,128]{2,1,0:T(8,128)(2,1)S(1)}, s16[22,16,128]{2,1,0:T(8,128)(2,1)S(1)}, u32[]{:S(2)}, u32[]{:S(2)}) collective-permute-start(s16[22,16,128]{2,1,0:T(8,128)(2,1)S(1)} %get-tuple-element.33), channel_id=1, source_target_pairs={{0,16},{1,17},{2,18},{3,19},{4,12},{5,13},{6,14},{7,15},{8,24},{9,... | collective-permute-start | bytes 270344 | tf_op jit(solution)/shard_map/ppermute | solution.py:255
  23.7 1.6 %collective-permute-start.9 = (s16[22,16,128]{2,1,0:T(8,128)(2,1)S(1)}, s16[22,16,128]{2,1,0:T(8,128)(2,1)S(1)}, u32[]{:S(2)}, u32[]{:S(2)}) collective-permute-start(s16[22,16,128]{2,1,0:T(8,128)(2,1)S(1)} %get-tuple-element.34), channel_id=1, source_target_pairs={{0,8},{1,9},{2,10},{3,11},{4,20},{5,21},{6,22},{7,23},{8,0},{9,1},... | collective-permute-start | bytes 270344 | tf_op jit(solution)/shard_map/ppermute | solution.py:255
  25.7 1.7 %collective-permute-done.8.refs_0_ = s16[22,16,128]{2,1,0:T(8,128)(2,1)S(1)} collective-permute-done((s16[22,16,128]{2,1,0:T(8,128)(2,1)S(1)}, s16[22,16,128]{2,1,0:T(8,128)(2,1)S(1)}, u32[]{:S(2)}, u32[]{:S(2)}) %collective-permute-start.8) | collective-permute-done | bytes 90144 | tf_op jit(solution)/shard_map/ppermute | solution.py:255
  27.4 1.7 %collective-permute-done.9.refs_1_ = s16[22,16,128]{2,1,0:T(8,128)(2,1)S(1)} collective-permute-done((s16[22,16,128]{2,1,0:T(8,128)(2,1)S(1)}, s16[22,16,128]{2,1,0:T(8,128)(2,1)S(1)}, u32[]{:S(2)}, u32[]{:S(2)}) %collective-permute-start.9) | collective-permute-done | bytes 90144 | tf_op jit(solution)/shard_map/ppermute | solution.py:255
  29.2 1.6 %collective-permute-done.10.refs_2_ = s16[22,16,128]{2,1,0:T(8,128)(2,1)S(1)} collective-permute-done((s16[22,16,128]{2,1,0:T(8,128)(2,1)S(1)}, s16[22,16,128]{2,1,0:T(8,128)(2,1)S(1)}, u32[]{:S(2)}, u32[]{:S(2)}) %collective-permute-start.10) | collective-permute-done | bytes 90144 | tf_op jit(solution)/shard_map/ppermute | solution.py:255
  30.9 2.7 %collective-permute-start.11 = (s16[7,16,128]{2,1,0:T(8,128)(2,1)S(1)}, s16[7,16,128]{2,1,0:T(8,128)(2,1)S(1)}, u32[]{:S(2)}, u32[]{:S(2)}) collective-permute-start(s16[7,16,128]{2,1,0:T(8,128)(2,1)S(1)} %get-tuple-element.37), channel_id=1, source_target_pairs={{0,2},{1,3},{2,0},{3,1},{4,7},{5,6},{6,5},{7,4},{8,10},{9,11},{10,... | collective-permute-start | bytes 86024 | tf_op jit(solution)/shard_map/ppermute | solution.py:255
  33.5 1.3 %collective-permute-start.12 = (s16[7,16,128]{2,1,0:T(8,128)(2,1)S(1)}, s16[7,16,128]{2,1,0:T(8,128)(2,1)S(1)}, u32[]{:S(2)}, u32[]{:S(2)}) collective-permute-start(s16[7,16,128]{2,1,0:T(8,128)(2,1)S(1)} %get-tuple-element.38), channel_id=1, source_target_pairs={{0,3},{1,2},{2,1},{3,0},{4,5},{5,4},{6,7},{7,6},{8,11},{9,10},{10,... | collective-permute-start | bytes 86024 | tf_op jit(solution)/shard_map/ppermute | solution.py:255
  35.1 0.7 %collective-permute-done.11.refs_0_ = s16[7,16,128]{2,1,0:T(8,128)(2,1)S(1)} collective-permute-done((s16[7,16,128]{2,1,0:T(8,128)(2,1)S(1)}, s16[7,16,128]{2,1,0:T(8,128)(2,1)S(1)}, u32[]{:S(2)}, u32[]{:S(2)}) %collective-permute-start.11) | collective-permute-done | bytes 28704 | tf_op jit(solution)/shard_map/ppermute | solution.py:255
  35.8 3.4 %collective-permute-done.12.refs_1_ = s16[7,16,128]{2,1,0:T(8,128)(2,1)S(1)} collective-permute-done((s16[7,16,128]{2,1,0:T(8,128)(2,1)S(1)}, s16[7,16,128]{2,1,0:T(8,128)(2,1)S(1)}, u32[]{:S(2)}, u32[]{:S(2)}) %collective-permute-start.12) | collective-permute-done | bytes 28704 | tf_op jit(solution)/shard_map/ppermute | solution.py:255
  39.4 10.2 %all_to_all.5 = f32[32,4,128]{2,1,0:T(4,128)S(1)} all-to-all(f32[32,4,128]{2,1,0:T(4,128)S(1)} %bitcast.5), channel_id=1, replica_groups=mesh['chan'=8,'tm'=4] {'chan','tm'}, dimensions={0} | all-to-all | bytes 131072 | tf_op jit(solution)/shard_map/all_to_all | solution.py:407
  49.6 0.8 %place_lags.1 = f32[16,4,256]{2,1,0:T(4,128)} custom-call(f32[8,4,4,128]{3,2,1,0:T(4,128)S(1)} %bitcast.4), custom_call_target="tpu_custom_call" | custom-call | tf_op jit(solution)/shard_map/place_lags/pallas_call | solution.py:408
  (16 shorter events, 1.4 us)
Async XLA Ops:
  0.0 17.1 %copy-start = (bf16[16,2,8,16,128]{4,3,2,1,0:T(8,128)(2,1)S(1)}, bf16[16,2,8,16,128]{4,3,2,1,0:T(8,128)(2,1)}, u32[]{:S(2)}) copy-start(bf16[16,2,8,16,128]{4,3,2,1,0:T(8,128)(2,1)} %constant.11.clone.refs_9_) | copy-start | bytes 3145732
  1.1 8.5 %collective-permute-start = (bf16[2,256,128]{2,1,0:T(8,128)(2,1)S(1)}, bf16[2,256,128]{2,1,0:T(8,128)(2,1)S(1)}, u32[]{:S(2)}, u32[]{:S(2)}) collective-permute-start(bf16[2,256,128]{2,1,0:T(8,128)(2,1)S(1)} %get-tuple-element.23), channel_id=1, source_target_pairs={{0,24},{1,25},{2,26},{3,27},{4,28},{5,29},{6,30},{7,31},{8,16},{9,... | collective-permute-start | bytes 393224 | tf_op jit(solution)/shard_map/ppermute | solution.py:255
  5.0 6.7 %collective-permute-start.1 = (bf16[2,256,128]{2,1,0:T(8,128)(2,1)S(1)}, bf16[2,256,128]{2,1,0:T(8,128)(2,1)S(1)}, u32[]{:S(2)}, u32[]{:S(2)}) collective-permute-start(bf16[2,256,128]{2,1,0:T(8,128)(2,1)S(1)} %get-tuple-element.24), channel_id=1, source_target_pairs={{0,28},{1,29},{2,30},{3,31},{4,24},{5,25},{6,26},{7,27},{8,20},{9,... | collective-permute-start | bytes 393224 | tf_op jit(solution)/shard_map/ppermute | solution.py:255
  6.3 8.9 %collective-permute-start.2 = (bf16[2,256,128]{2,1,0:T(8,128)(2,1)S(1)}, bf16[2,256,128]{2,1,0:T(8,128)(2,1)S(1)}, u32[]{:S(2)}, u32[]{:S(2)}) collective-permute-start(bf16[2,256,128]{2,1,0:T(8,128)(2,1)S(1)} %get-tuple-element.25), channel_id=1, source_target_pairs={{0,8},{1,9},{2,10},{3,11},{4,12},{5,13},{6,14},{7,15},{8,0},{9,1},... | collective-permute-start | bytes 393224 | tf_op jit(solution)/shard_map/ppermute | solution.py:255
  7.5 7.7 %collective-permute-start.3 = (bf16[2,256,128]{2,1,0:T(8,128)(2,1)S(1)}, bf16[2,256,128]{2,1,0:T(8,128)(2,1)S(1)}, u32[]{:S(2)}, u32[]{:S(2)}) collective-permute-start(bf16[2,256,128]{2,1,0:T(8,128)(2,1)S(1)} %get-tuple-element.26), channel_id=1, source_target_pairs={{0,16},{1,17},{2,18},{3,19},{4,20},{5,21},{6,22},{7,23},{8,24},{9,... | collective-permute-start | bytes 393224 | tf_op jit(solution)/shard_map/ppermute | solution.py:255
  9.0 7.4 %collective-permute-start.4 = (bf16[2,256,128]{2,1,0:T(8,128)(2,1)S(1)}, bf16[2,256,128]{2,1,0:T(8,128)(2,1)S(1)}, u32[]{:S(2)}, u32[]{:S(2)}) collective-permute-start(bf16[2,256,128]{2,1,0:T(8,128)(2,1)S(1)} %get-tuple-element.27), channel_id=1, source_target_pairs={{0,12},{1,13},{2,14},{3,15},{4,8},{5,9},{6,10},{7,11},{8,4},{9,5},... | collective-permute-start | bytes 393224 | tf_op jit(solution)/shard_map/ppermute | solution.py:255
  9.6 7.5 %collective-permute-start.5 = (bf16[2,256,128]{2,1,0:T(8,128)(2,1)S(1)}, bf16[2,256,128]{2,1,0:T(8,128)(2,1)S(1)}, u32[]{:S(2)}, u32[]{:S(2)}) collective-permute-start(bf16[2,256,128]{2,1,0:T(8,128)(2,1)S(1)} %get-tuple-element.28), channel_id=1, source_target_pairs={{0,20},{1,21},{2,22},{3,23},{4,16},{5,17},{6,18},{7,19},{8,28},{9,... | collective-permute-start | bytes 393224 | tf_op jit(solution)/shard_map/ppermute | solution.py:255
  11.8 5.3 %collective-permute-start.6 = (bf16[2,256,128]{2,1,0:T(8,128)(2,1)S(1)}, bf16[2,256,128]{2,1,0:T(8,128)(2,1)S(1)}, u32[]{:S(2)}, u32[]{:S(2)}) collective-permute-start(bf16[2,256,128]{2,1,0:T(8,128)(2,1)S(1)} %get-tuple-element.29), channel_id=1, source_target_pairs={{0,4},{1,5},{2,6},{3,7},{4,0},{5,1},{6,2},{7,3},{8,12},{9,13},{10,... | collective-permute-start | bytes 393224 | tf_op jit(solution)/shard_map/ppermute | solution.py:255
  11.8 5.3 %copy-start.1 = (s32[8,128]{1,0:T(8,128)S(1)}, s32[8,128]{1,0:T(8,128)}, u32[]{:S(2)}) copy-start(s32[8,128]{1,0:T(8,128)} %refs_8_.1) | copy-start | bytes 12292
  20.2 1.7 %collective-permute-start.7 = (s16[4,22,16,128]{3,2,1,0:T(8,128)(2,1)S(1)}, s16[4,22,16,128]{3,2,1,0:T(8,128)(2,1)S(1)}, u32[]{:S(2)}, u32[]{:S(2)}) collective-permute-start(s16[4,22,16,128]{3,2,1,0:T(8,128)(2,1)S(1)} %get-tuple-element.32), channel_id=1, source_target_pairs={{0,4},{1,5},{2,6},{3,7},{4,0},{5,1},{6,2},{7,3},{8,12},{9,13},{10,... | collective-permute-start | bytes 1081352 | tf_op jit(solution)/shard_map/ppermute | solution.py:255
  22.2 5.3 %collective-permute-start.8 = (s16[22,16,128]{2,1,0:T(8,128)(2,1)S(1)}, s16[22,16,128]{2,1,0:T(8,128)(2,1)S(1)}, u32[]{:S(2)}, u32[]{:S(2)}) collective-permute-start(s16[22,16,128]{2,1,0:T(8,128)(2,1)S(1)} %get-tuple-element.33), channel_id=1, source_target_pairs={{0,16},{1,17},{2,18},{3,19},{4,12},{5,13},{6,14},{7,15},{8,24},{9,... | collective-permute-start | bytes 270344 | tf_op jit(solution)/shard_map/ppermute | solution.py:255
  23.7 5.4 %collective-permute-start.9 = (s16[22,16,128]{2,1,0:T(8,128)(2,1)S(1)}, s16[22,16,128]{2,1,0:T(8,128)(2,1)S(1)}, u32[]{:S(2)}, u32[]{:S(2)}) collective-permute-start(s16[22,16,128]{2,1,0:T(8,128)(2,1)S(1)} %get-tuple-element.34), channel_id=1, source_target_pairs={{0,8},{1,9},{2,10},{3,11},{4,20},{5,21},{6,22},{7,23},{8,0},{9,1},... | collective-permute-start | bytes 270344 | tf_op jit(solution)/shard_map/ppermute | solution.py:255
  25.3 5.4 %collective-permute-start.10 = (s16[22,16,128]{2,1,0:T(8,128)(2,1)S(1)}, s16[22,16,128]{2,1,0:T(8,128)(2,1)S(1)}, u32[]{:S(2)}, u32[]{:S(2)}) collective-permute-start(s16[22,16,128]{2,1,0:T(8,128)(2,1)S(1)} %get-tuple-element.35), channel_id=1, source_target_pairs={{0,24},{1,25},{2,26},{3,27},{4,28},{5,29},{6,30},{7,31},{8,16},{9,... | collective-permute-start | bytes 270344 | tf_op jit(solution)/shard_map/ppermute | solution.py:255
  30.9 4.9 %collective-permute-start.11 = (s16[7,16,128]{2,1,0:T(8,128)(2,1)S(1)}, s16[7,16,128]{2,1,0:T(8,128)(2,1)S(1)}, u32[]{:S(2)}, u32[]{:S(2)}) collective-permute-start(s16[7,16,128]{2,1,0:T(8,128)(2,1)S(1)} %get-tuple-element.37), channel_id=1, source_target_pairs={{0,2},{1,3},{2,0},{3,1},{4,7},{5,6},{6,5},{7,4},{8,10},{9,11},{10,... | collective-permute-start | bytes 86024 | tf_op jit(solution)/shard_map/ppermute | solution.py:255
  33.5 5.7 %collective-permute-start.12 = (s16[7,16,128]{2,1,0:T(8,128)(2,1)S(1)}, s16[7,16,128]{2,1,0:T(8,128)(2,1)S(1)}, u32[]{:S(2)}, u32[]{:S(2)}) collective-permute-start(s16[7,16,128]{2,1,0:T(8,128)(2,1)S(1)} %get-tuple-element.38), channel_id=1, source_target_pairs={{0,3},{1,2},{2,1},{3,0},{4,5},{5,4},{6,7},{7,6},{8,11},{9,10},{10,... | collective-permute-start | bytes 86024 | tf_op jit(solution)/shard_map/ppermute | solution.py:255
  34.9 4.3 %collective-permute-start.13 = (s16[7,16,128]{2,1,0:T(8,128)(2,1)S(1)}, s16[7,16,128]{2,1,0:T(8,128)(2,1)S(1)}, u32[]{:S(2)}, u32[]{:S(2)}) collective-permute-start(s16[7,16,128]{2,1,0:T(8,128)(2,1)S(1)} %get-tuple-element.39), channel_id=1, source_target_pairs={{0,1},{1,0},{2,3},{3,2},{4,6},{5,7},{6,4},{7,5},{8,9},{9,8},{10,11... | collective-permute-start | bytes 86024 | tf_op jit(solution)/shard_map/ppermute | solution.py:255

commit v27 on v26

--- a/solution.py
+++ b/solution.py
@@ -231,7 +231,7 @@
 def chips(count):
     near = [k for k in range(2, count, 2) if k.bit_count() == 1]
     far = [k for k in range(2, count, 2) if k.bit_count() > 1]
-    return near[::-1] + far + [0], near + far + [0]
+    return far + near + [0], near + far + [0]
 
 
 def planes(count):

time: 50.5 us -> 50.5 us (level)
  no operation moved by 1% of the time
where the time goes in v27:
time: 50.5 us; the launch traced here: 50.3 us
  waiting for transfers between devices  17.3 us (34%)
  starting transfers between devices  15.8 us (31%)
  blocking collectives  10.4 us (21%)
  Pallas kernels  6.77 us (13%)
    ppermute x14, waiting for transfers between devices, exchange(): lax.ppermute(piece, ('chan', 'tm'), pairs)  17.3 us
    ppermute x14, starting transfers between devices, exchange(): lax.ppermute(piece, ('chan', 'tm'), pairs)  15.8 us
    all_to_all x1, blocking collectives, window_shards(): lax.all_to_all(pieces.reshape(shape), ('chan', 'tm'), 0, 0, tiled=True)  10.4 us
    pallas_call x1, Pallas kernels, window_shards(): pl.pallas_call(functools.partial(window_kernel, chan_order), out_shape=[j...  3.14 us
    pallas_call x2, Pallas kernels, window_shards(): pl.pallas_call(functools.partial(split_kernel, part), out_shape=[jax.Shap...  2.32 us
  transfers between devices with their start and end apart: 14, of which 10 were waited for; matrix products, arithmetic and copies ran while one was open for 0% of the time, Pallas kernels for 2%

profile of v27, /device:TPU:0, one launch (start us, length us, event | category | flops | bytes accessed | tf_op | source)
XLA Modules:
  0.0 50.3 jit_solution(7067681824009247709)
XLA Ops:
  0.0 1.1 %split_windows.2 = (bf16[2,256,128]{2,1,0:T(8,128)(2,1)S(1)}, bf16[2,256,128]{2,1,0:T(8,128)(2,1)S(1)}) custom-call(bf16[2,8,256,128]{3,2,1,0:T(8,128)(2,1)} %spec_ref.3), custom_call_target="tpu_custom_call" | custom-call | tf_op jit(solution)/shard_map/split_windows/pallas_call | solution.py:355
  1.1 4.0 %collective-permute-start = (bf16[2,256,128]{2,1,0:T(8,128)(2,1)S(1)}, bf16[2,256,128]{2,1,0:T(8,128)(2,1)S(1)}, u32[]{:S(2)}, u32[]{:S(2)}) collective-permute-start(bf16[2,256,128]{2,1,0:T(8,128)(2,1)S(1)} %get-tuple-element.23), channel_id=1, source_target_pairs={{0,24},{1,25},{2,26},{3,27},{4,28},{5,29},{6,30},{7,31},{8,16},{9,... | collective-permute-start | bytes 393224 | tf_op jit(solution)/shard_map/ppermute | solution.py:255
  5.0 1.3 %split_windows.3 = (bf16[2,256,128]{2,1,0:T(8,128)(2,1)S(1)}, bf16[2,256,128]{2,1,0:T(8,128)(2,1)S(1)}, bf16[2,256,128]{2,1,0:T(8,128)(2,1)S(1)}, bf16[2,256,128...) custom-call(bf16[2,8,256,128]{3,2,1,0:T(8,128)(2,1)} %spec_ref.3), custom_call_target="tpu_custom_call" | custom-call | tf_op jit(solution)/shard_map/split_windows/pallas_call | solution.py:355
  6.3 1.2 %collective-permute-start.2 = (bf16[2,256,128]{2,1,0:T(8,128)(2,1)S(1)}, bf16[2,256,128]{2,1,0:T(8,128)(2,1)S(1)}, u32[]{:S(2)}, u32[]{:S(2)}) collective-permute-start(bf16[2,256,128]{2,1,0:T(8,128)(2,1)S(1)} %get-tuple-element.25), channel_id=1, source_target_pairs={{0,8},{1,9},{2,10},{3,11},{4,12},{5,13},{6,14},{7,15},{8,0},{9,1},... | collective-permute-start | bytes 393224 | tf_op jit(solution)/shard_map/ppermute | solution.py:255
  7.5 1.5 %collective-permute-start.3 = (bf16[2,256,128]{2,1,0:T(8,128)(2,1)S(1)}, bf16[2,256,128]{2,1,0:T(8,128)(2,1)S(1)}, u32[]{:S(2)}, u32[]{:S(2)}) collective-permute-start(bf16[2,256,128]{2,1,0:T(8,128)(2,1)S(1)} %get-tuple-element.26), channel_id=1, source_target_pairs={{0,16},{1,17},{2,18},{3,19},{4,20},{5,21},{6,22},{7,23},{8,24},{9,... | collective-permute-start | bytes 393224 | tf_op jit(solution)/shard_map/ppermute | solution.py:255
  9.0 0.6 %collective-permute-start.4 = (bf16[2,256,128]{2,1,0:T(8,128)(2,1)S(1)}, bf16[2,256,128]{2,1,0:T(8,128)(2,1)S(1)}, u32[]{:S(2)}, u32[]{:S(2)}) collective-permute-start(bf16[2,256,128]{2,1,0:T(8,128)(2,1)S(1)} %get-tuple-element.27), channel_id=1, source_target_pairs={{0,12},{1,13},{2,14},{3,15},{4,8},{5,9},{6,10},{7,11},{8,4},{9,5},... | collective-permute-start | bytes 393224 | tf_op jit(solution)/shard_map/ppermute | solution.py:255
  9.6 0.6 %collective-permute-start.5 = (bf16[2,256,128]{2,1,0:T(8,128)(2,1)S(1)}, bf16[2,256,128]{2,1,0:T(8,128)(2,1)S(1)}, u32[]{:S(2)}, u32[]{:S(2)}) collective-permute-start(bf16[2,256,128]{2,1,0:T(8,128)(2,1)S(1)} %get-tuple-element.28), channel_id=1, source_target_pairs={{0,20},{1,21},{2,22},{3,23},{4,16},{5,17},{6,18},{7,19},{8,28},{9,... | collective-permute-start | bytes 393224 | tf_op jit(solution)/shard_map/ppermute | solution.py:255
  10.1 1.6 %collective-permute-done.1.refs_1_ = bf16[2,256,128]{2,1,0:T(8,128)(2,1)S(1)} collective-permute-done((bf16[2,256,128]{2,1,0:T(8,128)(2,1)S(1)}, bf16[2,256,128]{2,1,0:T(8,128)(2,1)S(1)}, u32[]{:S(2)}, u32[]{:S(2)}) %collective-permute-start.1) | collective-permute-done | bytes 131104 | tf_op jit(solution)/shard_map/ppermute | solution.py:255
  11.8 3.5 %collective-permute-done.2.refs_2_ = bf16[2,256,128]{2,1,0:T(8,128)(2,1)S(1)} collective-permute-done((bf16[2,256,128]{2,1,0:T(8,128)(2,1)S(1)}, bf16[2,256,128]{2,1,0:T(8,128)(2,1)S(1)}, u32[]{:S(2)}, u32[]{:S(2)}) %collective-permute-start.2) | collective-permute-done | bytes 131104 | tf_op jit(solution)/shard_map/ppermute | solution.py:255
  15.2 1.1 %collective-permute-done.4.refs_4_ = bf16[2,256,128]{2,1,0:T(8,128)(2,1)S(1)} collective-permute-done((bf16[2,256,128]{2,1,0:T(8,128)(2,1)S(1)}, bf16[2,256,128]{2,1,0:T(8,128)(2,1)S(1)}, u32[]{:S(2)}, u32[]{:S(2)}) %collective-permute-start.4) | collective-permute-done | bytes 131104 | tf_op jit(solution)/shard_map/ppermute | solution.py:255
  16.4 0.7 %collective-permute-done.5.refs_5_ = bf16[2,256,128]{2,1,0:T(8,128)(2,1)S(1)} collective-permute-done((bf16[2,256,128]{2,1,0:T(8,128)(2,1)S(1)}, bf16[2,256,128]{2,1,0:T(8,128)(2,1)S(1)}, u32[]{:S(2)}, u32[]{:S(2)}) %collective-permute-start.5) | collective-permute-done | bytes 131104 | tf_op jit(solution)/shard_map/ppermute | solution.py:255
  17.1 3.1 %window_pairs.1 = (s16[4,22,16,128]{3,2,1,0:T(8,128)(2,1)S(1)}, s16[4,22,16,128]{3,2,1,0:T(8,128)(2,1)S(1)}) custom-call(s32[4]{0:T(128)} %offs_hbm_ref.1, s32[1]{0:T(128)} %bitcast.where_ref.core_ref, bf16[2,256,128]{2,1,0:T(8,128)(2,1)S(1)} %collective-permute-done.refs_0_, bf16[2,256,128]{2,1,0:T(8,128)(2,1)S(1)} %collective-permute-done.1.refs_1_, ...), custom_call_target="tpu_custom_call" | custom-call | tf_op jit(solution)/shard_map/window_pairs/pallas_call | solution.py:366
  20.4 1.6 %collective-permute-done.7.far_ref = s16[4,22,16,128]{3,2,1,0:T(8,128)(2,1)S(1)} collective-permute-done((s16[4,22,16,128]{3,2,1,0:T(8,128)(2,1)S(1)}, s16[4,22,16,128]{3,2,1,0:T(8,128)(2,1)S(1)}, u32[]{:S(2)}, u32[]{:S(2)}) %collective-permute-start.7) | collective-permute-done | bytes 360480 | tf_op jit(solution)/shard_map/ppermute | solution.py:255
  22.2 2.6 %collective-permute-start.8 = (s16[22,16,128]{2,1,0:T(8,128)(2,1)S(1)}, s16[22,16,128]{2,1,0:T(8,128)(2,1)S(1)}, u32[]{:S(2)}, u32[]{:S(2)}) collective-permute-start(s16[22,16,128]{2,1,0:T(8,128)(2,1)S(1)} %get-tuple-element.33), channel_id=1, source_target_pairs={{0,24},{1,25},{2,26},{3,27},{4,12},{5,13},{6,14},{7,15},{8,16},{9,... | collective-permute-start | bytes 270344 | tf_op jit(solution)/shard_map/ppermute | solution.py:255
  25.2 0.5 %collective-permute-start.10 = (s16[22,16,128]{2,1,0:T(8,128)(2,1)S(1)}, s16[22,16,128]{2,1,0:T(8,128)(2,1)S(1)}, u32[]{:S(2)}, u32[]{:S(2)}) collective-permute-start(s16[22,16,128]{2,1,0:T(8,128)(2,1)S(1)} %get-tuple-element.35), channel_id=1, source_target_pairs={{0,16},{1,17},{2,18},{3,19},{4,28},{5,29},{6,30},{7,31},{8,24},{9,... | collective-permute-start | bytes 270344 | tf_op jit(solution)/shard_map/ppermute | solution.py:255
  25.7 2.2 %collective-permute-done.8.refs_0_ = s16[22,16,128]{2,1,0:T(8,128)(2,1)S(1)} collective-permute-done((s16[22,16,128]{2,1,0:T(8,128)(2,1)S(1)}, s16[22,16,128]{2,1,0:T(8,128)(2,1)S(1)}, u32[]{:S(2)}, u32[]{:S(2)}) %collective-permute-start.8) | collective-permute-done | bytes 90144 | tf_op jit(solution)/shard_map/ppermute | solution.py:255
  27.9 1.8 %collective-permute-done.9.refs_1_ = s16[22,16,128]{2,1,0:T(8,128)(2,1)S(1)} collective-permute-done((s16[22,16,128]{2,1,0:T(8,128)(2,1)S(1)}, s16[22,16,128]{2,1,0:T(8,128)(2,1)S(1)}, u32[]{:S(2)}, u32[]{:S(2)}) %collective-permute-start.9) | collective-permute-done | bytes 90144 | tf_op jit(solution)/shard_map/ppermute | solution.py:255
  29.7 0.8 %collective-permute-done.10.refs_2_ = s16[22,16,128]{2,1,0:T(8,128)(2,1)S(1)} collective-permute-done((s16[22,16,128]{2,1,0:T(8,128)(2,1)S(1)}, s16[22,16,128]{2,1,0:T(8,128)(2,1)S(1)}, u32[]{:S(2)}, u32[]{:S(2)}) %collective-permute-start.10) | collective-permute-done | bytes 90144 | tf_op jit(solution)/shard_map/ppermute | solution.py:255
  30.7 2.7 %collective-permute-start.11 = (s16[7,16,128]{2,1,0:T(8,128)(2,1)S(1)}, s16[7,16,128]{2,1,0:T(8,128)(2,1)S(1)}, u32[]{:S(2)}, u32[]{:S(2)}) collective-permute-start(s16[7,16,128]{2,1,0:T(8,128)(2,1)S(1)} %get-tuple-element.37), channel_id=1, source_target_pairs={{0,2},{1,3},{2,0},{3,1},{4,7},{5,6},{6,5},{7,4},{8,10},{9,11},{10,... | collective-permute-start | bytes 86024 | tf_op jit(solution)/shard_map/ppermute | solution.py:255
  33.3 1.3 %collective-permute-start.12 = (s16[7,16,128]{2,1,0:T(8,128)(2,1)S(1)}, s16[7,16,128]{2,1,0:T(8,128)(2,1)S(1)}, u32[]{:S(2)}, u32[]{:S(2)}) collective-permute-start(s16[7,16,128]{2,1,0:T(8,128)(2,1)S(1)} %get-tuple-element.38), channel_id=1, source_target_pairs={{0,3},{1,2},{2,1},{3,0},{4,5},{5,4},{6,7},{7,6},{8,11},{9,10},{10,... | collective-permute-start | bytes 86024 | tf_op jit(solution)/shard_map/ppermute | solution.py:255
  34.9 0.6 %collective-permute-done.11.refs_0_ = s16[7,16,128]{2,1,0:T(8,128)(2,1)S(1)} collective-permute-done((s16[7,16,128]{2,1,0:T(8,128)(2,1)S(1)}, s16[7,16,128]{2,1,0:T(8,128)(2,1)S(1)}, u32[]{:S(2)}, u32[]{:S(2)}) %collective-permute-start.11) | collective-permute-done | bytes 28704 | tf_op jit(solution)/shard_map/ppermute | solution.py:255
  35.5 3.5 %collective-permute-done.12.refs_1_ = s16[7,16,128]{2,1,0:T(8,128)(2,1)S(1)} collective-permute-done((s16[7,16,128]{2,1,0:T(8,128)(2,1)S(1)}, s16[7,16,128]{2,1,0:T(8,128)(2,1)S(1)}, u32[]{:S(2)}, u32[]{:S(2)}) %collective-permute-start.12) | collective-permute-done | bytes 28704 | tf_op jit(solution)/shard_map/ppermute | solution.py:255
  39.2 10.4 %all_to_all.5 = f32[32,4,128]{2,1,0:T(4,128)S(1)} all-to-all(f32[32,4,128]{2,1,0:T(4,128)S(1)} %bitcast.5), channel_id=1, replica_groups=mesh['chan'=8,'tm'=4] {'chan','tm'}, dimensions={0} | all-to-all | bytes 131072 | tf_op jit(solution)/shard_map/all_to_all | solution.py:407
  49.6 0.8 %place_lags.1 = f32[16,4,256]{2,1,0:T(4,128)} custom-call(f32[8,4,4,128]{3,2,1,0:T(4,128)S(1)} %bitcast.4), custom_call_target="tpu_custom_call" | custom-call | tf_op jit(solution)/shard_map/place_lags/pallas_call | solution.py:408
  (16 shorter events, 1.5 us)
Async XLA Ops:
  0.0 17.1 %copy-start = (bf16[16,2,8,16,128]{4,3,2,1,0:T(8,128)(2,1)S(1)}, bf16[16,2,8,16,128]{4,3,2,1,0:T(8,128)(2,1)}, u32[]{:S(2)}) copy-start(bf16[16,2,8,16,128]{4,3,2,1,0:T(8,128)(2,1)} %constant.11.clone.refs_9_) | copy-start | bytes 3145732
  1.1 8.5 %collective-permute-start = (bf16[2,256,128]{2,1,0:T(8,128)(2,1)S(1)}, bf16[2,256,128]{2,1,0:T(8,128)(2,1)S(1)}, u32[]{:S(2)}, u32[]{:S(2)}) collective-permute-start(bf16[2,256,128]{2,1,0:T(8,128)(2,1)S(1)} %get-tuple-element.23), channel_id=1, source_target_pairs={{0,24},{1,25},{2,26},{3,27},{4,28},{5,29},{6,30},{7,31},{8,16},{9,... | collective-permute-start | bytes 393224 | tf_op jit(solution)/shard_map/ppermute | solution.py:255
  5.0 6.7 %collective-permute-start.1 = (bf16[2,256,128]{2,1,0:T(8,128)(2,1)S(1)}, bf16[2,256,128]{2,1,0:T(8,128)(2,1)S(1)}, u32[]{:S(2)}, u32[]{:S(2)}) collective-permute-start(bf16[2,256,128]{2,1,0:T(8,128)(2,1)S(1)} %get-tuple-element.24), channel_id=1, source_target_pairs={{0,28},{1,29},{2,30},{3,31},{4,24},{5,25},{6,26},{7,27},{8,20},{9,... | collective-permute-start | bytes 393224 | tf_op jit(solution)/shard_map/ppermute | solution.py:255
  6.3 8.9 %collective-permute-start.2 = (bf16[2,256,128]{2,1,0:T(8,128)(2,1)S(1)}, bf16[2,256,128]{2,1,0:T(8,128)(2,1)S(1)}, u32[]{:S(2)}, u32[]{:S(2)}) collective-permute-start(bf16[2,256,128]{2,1,0:T(8,128)(2,1)S(1)} %get-tuple-element.25), channel_id=1, source_target_pairs={{0,8},{1,9},{2,10},{3,11},{4,12},{5,13},{6,14},{7,15},{8,0},{9,1},... | collective-permute-start | bytes 393224 | tf_op jit(solution)/shard_map/ppermute | solution.py:255
  7.5 7.7 %collective-permute-start.3 = (bf16[2,256,128]{2,1,0:T(8,128)(2,1)S(1)}, bf16[2,256,128]{2,1,0:T(8,128)(2,1)S(1)}, u32[]{:S(2)}, u32[]{:S(2)}) collective-permute-start(bf16[2,256,128]{2,1,0:T(8,128)(2,1)S(1)} %get-tuple-element.26), channel_id=1, source_target_pairs={{0,16},{1,17},{2,18},{3,19},{4,20},{5,21},{6,22},{7,23},{8,24},{9,... | collective-permute-start | bytes 393224 | tf_op jit(solution)/shard_map/ppermute | solution.py:255
  9.0 7.4 %collective-permute-start.4 = (bf16[2,256,128]{2,1,0:T(8,128)(2,1)S(1)}, bf16[2,256,128]{2,1,0:T(8,128)(2,1)S(1)}, u32[]{:S(2)}, u32[]{:S(2)}) collective-permute-start(bf16[2,256,128]{2,1,0:T(8,128)(2,1)S(1)} %get-tuple-element.27), channel_id=1, source_target_pairs={{0,12},{1,13},{2,14},{3,15},{4,8},{5,9},{6,10},{7,11},{8,4},{9,5},... | collective-permute-start | bytes 393224 | tf_op jit(solution)/shard_map/ppermute | solution.py:255
  9.6 7.5 %collective-permute-start.5 = (bf16[2,256,128]{2,1,0:T(8,128)(2,1)S(1)}, bf16[2,256,128]{2,1,0:T(8,128)(2,1)S(1)}, u32[]{:S(2)}, u32[]{:S(2)}) collective-permute-start(bf16[2,256,128]{2,1,0:T(8,128)(2,1)S(1)} %get-tuple-element.28), channel_id=1, source_target_pairs={{0,20},{1,21},{2,22},{3,23},{4,16},{5,17},{6,18},{7,19},{8,28},{9,... | collective-permute-start | bytes 393224 | tf_op jit(solution)/shard_map/ppermute | solution.py:255
  11.8 5.3 %collective-permute-start.6 = (bf16[2,256,128]{2,1,0:T(8,128)(2,1)S(1)}, bf16[2,256,128]{2,1,0:T(8,128)(2,1)S(1)}, u32[]{:S(2)}, u32[]{:S(2)}) collective-permute-start(bf16[2,256,128]{2,1,0:T(8,128)(2,1)S(1)} %get-tuple-element.29), channel_id=1, source_target_pairs={{0,4},{1,5},{2,6},{3,7},{4,0},{5,1},{6,2},{7,3},{8,12},{9,13},{10,... | collective-permute-start | bytes 393224 | tf_op jit(solution)/shard_map/ppermute | solution.py:255
  11.8 5.3 %copy-start.1 = (s32[8,128]{1,0:T(8,128)S(1)}, s32[8,128]{1,0:T(8,128)}, u32[]{:S(2)}) copy-start(s32[8,128]{1,0:T(8,128)} %refs_8_.1) | copy-start | bytes 12292
  20.2 1.7 %collective-permute-start.7 = (s16[4,22,16,128]{3,2,1,0:T(8,128)(2,1)S(1)}, s16[4,22,16,128]{3,2,1,0:T(8,128)(2,1)S(1)}, u32[]{:S(2)}, u32[]{:S(2)}) collective-permute-start(s16[4,22,16,128]{3,2,1,0:T(8,128)(2,1)S(1)} %get-tuple-element.32), channel_id=1, source_target_pairs={{0,4},{1,5},{2,6},{3,7},{4,0},{5,1},{6,2},{7,3},{8,12},{9,13},{10,... | collective-permute-start | bytes 1081352 | tf_op jit(solution)/shard_map/ppermute | solution.py:255
  22.2 5.7 %collective-permute-start.8 = (s16[22,16,128]{2,1,0:T(8,128)(2,1)S(1)}, s16[22,16,128]{2,1,0:T(8,128)(2,1)S(1)}, u32[]{:S(2)}, u32[]{:S(2)}) collective-permute-start(s16[22,16,128]{2,1,0:T(8,128)(2,1)S(1)} %get-tuple-element.33), channel_id=1, source_target_pairs={{0,24},{1,25},{2,26},{3,27},{4,12},{5,13},{6,14},{7,15},{8,16},{9,... | collective-permute-start | bytes 270344 | tf_op jit(solution)/shard_map/ppermute | solution.py:255
  24.7 4.9 %collective-permute-start.9 = (s16[22,16,128]{2,1,0:T(8,128)(2,1)S(1)}, s16[22,16,128]{2,1,0:T(8,128)(2,1)S(1)}, u32[]{:S(2)}, u32[]{:S(2)}) collective-permute-start(s16[22,16,128]{2,1,0:T(8,128)(2,1)S(1)} %get-tuple-element.34), channel_id=1, source_target_pairs={{0,8},{1,9},{2,10},{3,11},{4,20},{5,21},{6,22},{7,23},{8,0},{9,1},... | collective-permute-start | bytes 270344 | tf_op jit(solution)/shard_map/ppermute | solution.py:255
  25.2 5.3 %collective-permute-start.10 = (s16[22,16,128]{2,1,0:T(8,128)(2,1)S(1)}, s16[22,16,128]{2,1,0:T(8,128)(2,1)S(1)}, u32[]{:S(2)}, u32[]{:S(2)}) collective-permute-start(s16[22,16,128]{2,1,0:T(8,128)(2,1)S(1)} %get-tuple-element.35), channel_id=1, source_target_pairs={{0,16},{1,17},{2,18},{3,19},{4,28},{5,29},{6,30},{7,31},{8,24},{9,... | collective-permute-start | bytes 270344 | tf_op jit(solution)/shard_map/ppermute | solution.py:255
  30.7 4.8 %collective-permute-start.11 = (s16[7,16,128]{2,1,0:T(8,128)(2,1)S(1)}, s16[7,16,128]{2,1,0:T(8,128)(2,1)S(1)}, u32[]{:S(2)}, u32[]{:S(2)}) collective-permute-start(s16[7,16,128]{2,1,0:T(8,128)(2,1)S(1)} %get-tuple-element.37), channel_id=1, source_target_pairs={{0,2},{1,3},{2,0},{3,1},{4,7},{5,6},{6,5},{7,4},{8,10},{9,11},{10,... | collective-permute-start | bytes 86024 | tf_op jit(solution)/shard_map/ppermute | solution.py:255
  33.3 5.7 %collective-permute-start.12 = (s16[7,16,128]{2,1,0:T(8,128)(2,1)S(1)}, s16[7,16,128]{2,1,0:T(8,128)(2,1)S(1)}, u32[]{:S(2)}, u32[]{:S(2)}) collective-permute-start(s16[7,16,128]{2,1,0:T(8,128)(2,1)S(1)} %get-tuple-element.38), channel_id=1, source_target_pairs={{0,3},{1,2},{2,1},{3,0},{4,5},{5,4},{6,7},{7,6},{8,11},{9,10},{10,... | collective-permute-start | bytes 86024 | tf_op jit(solution)/shard_map/ppermute | solution.py:255
  34.7 4.3 %collective-permute-start.13 = (s16[7,16,128]{2,1,0:T(8,128)(2,1)S(1)}, s16[7,16,128]{2,1,0:T(8,128)(2,1)S(1)}, u32[]{:S(2)}, u32[]{:S(2)}) collective-permute-start(s16[7,16,128]{2,1,0:T(8,128)(2,1)S(1)} %get-tuple-element.39), channel_id=1, source_target_pairs={{0,1},{1,0},{2,3},{3,2},{4,6},{5,7},{6,4},{7,5},{8,9},{9,8},{10,11... | collective-permute-start | bytes 86024 | tf_op jit(solution)/shard_map/ppermute | solution.py:255

commit v28 on v26

--- a/solution.py
+++ b/solution.py
@@ -60,8 +60,8 @@
 def window_kernel(order, offs_hbm_ref, where_ref, *refs):
     chan_count = len(order)
     spec_refs, (qual_ref, table_ref) = refs[:chan_count], refs[chan_count : chan_count + 2]
-    out_refs = refs[chan_count + 2 : chan_count + 4]
-    mag_ref, white_ref, cross_ref, offs_ref, offs_sem = refs[chan_count + 4 :]
+    out_refs = refs[chan_count + 2 : chan_count + 5]
+    mag_ref, white_ref, cross_ref, offs_ref, offs_sem = refs[chan_count + 5 :]
     fetch = pltpu.make_async_copy(offs_hbm_ref, offs_ref, offs_sem)
     fetch.start()
     me = where_ref[0]
@@ -149,22 +149,24 @@
         levels = jnp.where(line == number, code, levels)
         for place, value in enumerate(value for kind in kinds for value in kind):
             coded = encode(value).reshape(chan_count, lag_rows, chans)
-            for core in range(2):
-                rows = slice(core * chip_count, (core + 1) * chip_count)
-                out_refs[core][:, 6 * number + place, :, :] = coded[rows]
+            begin = 0
+            for out_ref in out_refs:
+                out_ref[:, 6 * number + place, :, :] = coded[begin : begin + out_ref.shape[0]]
+                begin += out_ref.shape[0]
     for number in range(offset_count):
         levels = jnp.where(line == offset_count + number, offs_ref[number].astype(jnp.float32), levels)
     wide = widest(offs_ref, chan_count // 2).astype(jnp.float32)
     levels = jnp.where(line == 2 * offset_count, wide, levels)
     for out_ref in out_refs:
-        for chip in range(chip_count):
+        for chip in range(out_ref.shape[0]):
             out_ref[chip, blocks - 1, :, :] = encode(levels)
 
 
-def merge_kernel(slots, own_ref, far_ref, *out_refs):
+def merge_kernel(slots, own_ref, far_ref, more_ref, *out_refs):
     blocks = own_ref.shape[1]
     for chip, out_ref in enumerate(out_refs):
-        codes = [decode(ref[chip, blocks - 1]) for ref in (own_ref, far_ref)]
+        far, from_far = (far_ref, chip) if chip < far_ref.shape[0] else (more_ref, chip - far_ref.shape[0])
+        codes = [decode(own_ref[chip, blocks - 1]), decode(far[from_far, blocks - 1])]
         levels = [level_of(code) for code in codes]
         code = level_code(levels[0] + levels[1])
         shares = [level / level_of(code) for level in levels]
@@ -173,11 +175,11 @@
         for block in range(blocks - 1):
             number, part = divmod(block, 6)
             linear = part < (2 if blocks - 1 - 6 * number > 3 else 1)
-            own, far = decode(own_ref[chip, block]), decode(far_ref[chip, block])
+            own, other = decode(own_ref[chip, block]), decode(far[from_far, block])
             if linear:
-                total = own * shares[0][number : number + 1, :] + far * shares[1][number : number + 1, :]
+                total = own * shares[0][number : number + 1, :] + other * shares[1][number : number + 1, :]
             else:
-                total = (own + far) * 0.5
+                total = (own + other) * 0.5
             out_ref[block, :, :] = encode(total)
 
 
@@ -363,11 +365,13 @@
         )(spectra)
     chip_count = chan_count // 2
     pair_shape = (6 * offset_count - 2, lag_rows, chans)
-    own, far = pl.pallas_call(
+    own, *far = pl.pallas_call(
         functools.partial(window_kernel, chan_order),
-        out_shape=[jax.ShapeDtypeStruct((chip_count, *pair_shape), jnp.int16)] * 2,
+        out_shape=[
+            jax.ShapeDtypeStruct((chips_in, *pair_shape), jnp.int16) for chips_in in (chip_count, chip_count // 2, chip_count // 2)
+        ],
         in_specs=[kept, smem] + [vmem] * (chan_count + 2),
-        out_specs=[vmem] * 2,
+        out_specs=[vmem] * 3,
         scratch_shapes=[
             pltpu.VMEM((freqs, chans), jnp.float32),
             pltpu.VMEM((2, freqs, chans), jnp.bfloat16),
@@ -381,11 +385,11 @@
     pairs = pl.pallas_call(
         functools.partial(merge_kernel, offset_count),
         out_shape=[jax.ShapeDtypeStruct(pair_shape, jnp.int16)] * chip_count,
-        in_specs=[vmem] * 2,
+        in_specs=[vmem] * 3,
         out_specs=[vmem] * chip_count,
         compiler_params=params,
         name="merge_windows",
-    )(own, *exchange([far], ([1], [1])))
+    )(own, *exchange(far, ([1, 1], [1, 1])))
     sums = pl.pallas_call(
         functools.partial(sum_kernel, tm_orders, 1.0 / (CODE_TOP * math.sqrt(freqs))),
         out_shape=[jax.ShapeDtypeStruct((7, lag_rows, chans), jnp.int16)] * tm_count,

time: 50.5 us -> 50.6 us (level)
    ppermute x14 -> x15, waiting for transfers between devices: 17.6 us -> 17.2 us  [exchange(): lax.ppermute(piece, ('chan', 'tm'), pairs)]
    ppermute x14 -> x15, starting transfers between devices: 15.8 us -> 16.2 us  [exchange(): lax.ppermute(piece, ('chan', 'tm'), pairs)]
  transfers between devices with their start and end apart: 14 -> 15, of which waited for: 10 -> 11; matrix products, arithmetic and copies ran while one was open for 0% -> 0% of each run, Pallas kernels for 2% -> 2%
where the time goes in v28:
time: 50.6 us; the launch traced here: 50.4 us
  waiting for transfers between devices  17.2 us (34%)
  starting transfers between devices  16.2 us (32%)
  blocking collectives  10.3 us (20%)
  Pallas kernels  6.77 us (13%)
    ppermute x15, waiting for transfers between devices, exchange(): lax.ppermute(piece, ('chan', 'tm'), pairs)  17.2 us
    ppermute x15, starting transfers between devices, exchange(): lax.ppermute(piece, ('chan', 'tm'), pairs)  16.2 us
    all_to_all x1, blocking collectives, window_shards(): lax.all_to_all(pieces.reshape(shape), ('chan', 'tm'), 0, 0, tiled=True)  10.3 us
    pallas_call x1, Pallas kernels, window_shards(): pl.pallas_call(functools.partial(window_kernel, chan_order), out_shape=[j...  3.14 us
    pallas_call x2, Pallas kernels, window_shards(): pl.pallas_call(functools.partial(split_kernel, part), out_shape=[jax.Shap...  2.32 us
  transfers between devices with their start and end apart: 15, of which 11 were waited for; matrix products, arithmetic and copies ran while one was open for 0% of the time, Pallas kernels for 2%

profile of v28, /device:TPU:0, one launch (start us, length us, event | category | flops | bytes accessed | tf_op | source)
XLA Modules:
  0.0 50.4 jit_solution(10964533005127443055)
XLA Ops:
  0.0 1.1 %split_windows.2 = (bf16[2,256,128]{2,1,0:T(8,128)(2,1)S(1)}, bf16[2,256,128]{2,1,0:T(8,128)(2,1)S(1)}) custom-call(bf16[2,8,256,128]{3,2,1,0:T(8,128)(2,1)} %spec_ref.3), custom_call_target="tpu_custom_call" | custom-call | tf_op jit(solution)/shard_map/split_windows/pallas_call | solution.py:357
  1.1 4.0 %collective-permute-start = (bf16[2,256,128]{2,1,0:T(8,128)(2,1)S(1)}, bf16[2,256,128]{2,1,0:T(8,128)(2,1)S(1)}, u32[]{:S(2)}, u32[]{:S(2)}) collective-permute-start(bf16[2,256,128]{2,1,0:T(8,128)(2,1)S(1)} %get-tuple-element.24), channel_id=1, source_target_pairs={{0,24},{1,25},{2,26},{3,27},{4,28},{5,29},{6,30},{7,31},{8,16},{9,... | collective-permute-start | bytes 393224 | tf_op jit(solution)/shard_map/ppermute | solution.py:257
  5.0 1.3 %split_windows.3 = (bf16[2,256,128]{2,1,0:T(8,128)(2,1)S(1)}, bf16[2,256,128]{2,1,0:T(8,128)(2,1)S(1)}, bf16[2,256,128]{2,1,0:T(8,128)(2,1)S(1)}, bf16[2,256,128...) custom-call(bf16[2,8,256,128]{3,2,1,0:T(8,128)(2,1)} %spec_ref.3), custom_call_target="tpu_custom_call" | custom-call | tf_op jit(solution)/shard_map/split_windows/pallas_call | solution.py:357
  6.3 1.2 %collective-permute-start.2 = (bf16[2,256,128]{2,1,0:T(8,128)(2,1)S(1)}, bf16[2,256,128]{2,1,0:T(8,128)(2,1)S(1)}, u32[]{:S(2)}, u32[]{:S(2)}) collective-permute-start(bf16[2,256,128]{2,1,0:T(8,128)(2,1)S(1)} %get-tuple-element.26), channel_id=1, source_target_pairs={{0,8},{1,9},{2,10},{3,11},{4,12},{5,13},{6,14},{7,15},{8,0},{9,1},... | collective-permute-start | bytes 393224 | tf_op jit(solution)/shard_map/ppermute | solution.py:257
  7.5 1.5 %collective-permute-start.3 = (bf16[2,256,128]{2,1,0:T(8,128)(2,1)S(1)}, bf16[2,256,128]{2,1,0:T(8,128)(2,1)S(1)}, u32[]{:S(2)}, u32[]{:S(2)}) collective-permute-start(bf16[2,256,128]{2,1,0:T(8,128)(2,1)S(1)} %get-tuple-element.27), channel_id=1, source_target_pairs={{0,16},{1,17},{2,18},{3,19},{4,20},{5,21},{6,22},{7,23},{8,24},{9,... | collective-permute-start | bytes 393224 | tf_op jit(solution)/shard_map/ppermute | solution.py:257
  9.0 0.6 %collective-permute-start.4 = (bf16[2,256,128]{2,1,0:T(8,128)(2,1)S(1)}, bf16[2,256,128]{2,1,0:T(8,128)(2,1)S(1)}, u32[]{:S(2)}, u32[]{:S(2)}) collective-permute-start(bf16[2,256,128]{2,1,0:T(8,128)(2,1)S(1)} %get-tuple-element.28), channel_id=1, source_target_pairs={{0,12},{1,13},{2,14},{3,15},{4,8},{5,9},{6,10},{7,11},{8,4},{9,5},... | collective-permute-start | bytes 393224 | tf_op jit(solution)/shard_map/ppermute | solution.py:257
  9.6 0.6 %collective-permute-start.5 = (bf16[2,256,128]{2,1,0:T(8,128)(2,1)S(1)}, bf16[2,256,128]{2,1,0:T(8,128)(2,1)S(1)}, u32[]{:S(2)}, u32[]{:S(2)}) collective-permute-start(bf16[2,256,128]{2,1,0:T(8,128)(2,1)S(1)} %get-tuple-element.29), channel_id=1, source_target_pairs={{0,20},{1,21},{2,22},{3,23},{4,16},{5,17},{6,18},{7,19},{8,28},{9,... | collective-permute-start | bytes 393224 | tf_op jit(solution)/shard_map/ppermute | solution.py:257
  10.1 1.6 %collective-permute-done.1.refs_1_ = bf16[2,256,128]{2,1,0:T(8,128)(2,1)S(1)} collective-permute-done((bf16[2,256,128]{2,1,0:T(8,128)(2,1)S(1)}, bf16[2,256,128]{2,1,0:T(8,128)(2,1)S(1)}, u32[]{:S(2)}, u32[]{:S(2)}) %collective-permute-start.1) | collective-permute-done | bytes 131104 | tf_op jit(solution)/shard_map/ppermute | solution.py:257
  11.8 3.5 %collective-permute-done.2.refs_2_ = bf16[2,256,128]{2,1,0:T(8,128)(2,1)S(1)} collective-permute-done((bf16[2,256,128]{2,1,0:T(8,128)(2,1)S(1)}, bf16[2,256,128]{2,1,0:T(8,128)(2,1)S(1)}, u32[]{:S(2)}, u32[]{:S(2)}) %collective-permute-start.2) | collective-permute-done | bytes 131104 | tf_op jit(solution)/shard_map/ppermute | solution.py:257
  15.2 1.1 %collective-permute-done.4.refs_4_ = bf16[2,256,128]{2,1,0:T(8,128)(2,1)S(1)} collective-permute-done((bf16[2,256,128]{2,1,0:T(8,128)(2,1)S(1)}, bf16[2,256,128]{2,1,0:T(8,128)(2,1)S(1)}, u32[]{:S(2)}, u32[]{:S(2)}) %collective-permute-start.4) | collective-permute-done | bytes 131104 | tf_op jit(solution)/shard_map/ppermute | solution.py:257
  16.4 0.7 %collective-permute-done.5.refs_5_ = bf16[2,256,128]{2,1,0:T(8,128)(2,1)S(1)} collective-permute-done((bf16[2,256,128]{2,1,0:T(8,128)(2,1)S(1)}, bf16[2,256,128]{2,1,0:T(8,128)(2,1)S(1)}, u32[]{:S(2)}, u32[]{:S(2)}) %collective-permute-start.5) | collective-permute-done | bytes 131104 | tf_op jit(solution)/shard_map/ppermute | solution.py:257
  17.1 3.1 %window_pairs.1 = (s16[4,22,16,128]{3,2,1,0:T(8,128)(2,1)S(1)}, s16[2,22,16,128]{3,2,1,0:T(8,128)(2,1)S(1)}, s16[2,22,16,128]{3,2,1,0:T(8,128)(2,1)S(1)}) custom-call(s32[4]{0:T(128)} %offs_hbm_ref.1, s32[1]{0:T(128)} %bitcast.where_ref.core_ref, bf16[2,256,128]{2,1,0:T(8,128)(2,1)S(1)} %collective-permute-done.refs_0_, ...), custom_call_target="tpu_custom_call" | custom-call | tf_op jit(solution)/shard_map/window_pairs/pallas_call | solution.py:368
  20.8 0.9 %collective-permute-done.7.far_ref = s16[2,22,16,128]{3,2,1,0:T(8,128)(2,1)S(1)} collective-permute-done((s16[2,22,16,128]{3,2,1,0:T(8,128)(2,1)S(1)}, s16[2,22,16,128]{3,2,1,0:T(8,128)(2,1)S(1)}, u32[]{:S(2)}, u32[]{:S(2)}) %collective-permute-start.7) | collective-permute-done | bytes 180256 | tf_op jit(solution)/shard_map/ppermute | solution.py:257
  22.2 1.6 %collective-permute-start.9 = (s16[22,16,128]{2,1,0:T(8,128)(2,1)S(1)}, s16[22,16,128]{2,1,0:T(8,128)(2,1)S(1)}, u32[]{:S(2)}, u32[]{:S(2)}) collective-permute-start(s16[22,16,128]{2,1,0:T(8,128)(2,1)S(1)} %get-tuple-element.35), channel_id=1, source_target_pairs={{0,16},{1,17},{2,18},{3,19},{4,12},{5,13},{6,14},{7,15},{8,24},{9,... | collective-permute-start | bytes 270344 | tf_op jit(solution)/shard_map/ppermute | solution.py:257
  23.7 1.6 %collective-permute-start.10 = (s16[22,16,128]{2,1,0:T(8,128)(2,1)S(1)}, s16[22,16,128]{2,1,0:T(8,128)(2,1)S(1)}, u32[]{:S(2)}, u32[]{:S(2)}) collective-permute-start(s16[22,16,128]{2,1,0:T(8,128)(2,1)S(1)} %get-tuple-element.36), channel_id=1, source_target_pairs={{0,8},{1,9},{2,10},{3,11},{4,20},{5,21},{6,22},{7,23},{8,0},{9,1},... | collective-permute-start | bytes 270344 | tf_op jit(solution)/shard_map/ppermute | solution.py:257
  25.7 1.6 %collective-permute-done.9.refs_0_ = s16[22,16,128]{2,1,0:T(8,128)(2,1)S(1)} collective-permute-done((s16[22,16,128]{2,1,0:T(8,128)(2,1)S(1)}, s16[22,16,128]{2,1,0:T(8,128)(2,1)S(1)}, u32[]{:S(2)}, u32[]{:S(2)}) %collective-permute-start.9) | collective-permute-done | bytes 90144 | tf_op jit(solution)/shard_map/ppermute | solution.py:257
  27.3 1.7 %collective-permute-done.10.refs_1_ = s16[22,16,128]{2,1,0:T(8,128)(2,1)S(1)} collective-permute-done((s16[22,16,128]{2,1,0:T(8,128)(2,1)S(1)}, s16[22,16,128]{2,1,0:T(8,128)(2,1)S(1)}, u32[]{:S(2)}, u32[]{:S(2)}) %collective-permute-start.10) | collective-permute-done | bytes 90144 | tf_op jit(solution)/shard_map/ppermute | solution.py:257
  29.0 1.7 %collective-permute-done.11.refs_2_ = s16[22,16,128]{2,1,0:T(8,128)(2,1)S(1)} collective-permute-done((s16[22,16,128]{2,1,0:T(8,128)(2,1)S(1)}, s16[22,16,128]{2,1,0:T(8,128)(2,1)S(1)}, u32[]{:S(2)}, u32[]{:S(2)}) %collective-permute-start.11) | collective-permute-done | bytes 90144 | tf_op jit(solution)/shard_map/ppermute | solution.py:257
  30.9 2.7 %collective-permute-start.12 = (s16[7,16,128]{2,1,0:T(8,128)(2,1)S(1)}, s16[7,16,128]{2,1,0:T(8,128)(2,1)S(1)}, u32[]{:S(2)}, u32[]{:S(2)}) collective-permute-start(s16[7,16,128]{2,1,0:T(8,128)(2,1)S(1)} %get-tuple-element.39), channel_id=1, source_target_pairs={{0,2},{1,3},{2,0},{3,1},{4,7},{5,6},{6,5},{7,4},{8,10},{9,11},{10,... | collective-permute-start | bytes 86024 | tf_op jit(solution)/shard_map/ppermute | solution.py:257
  33.5 1.3 %collective-permute-start.13 = (s16[7,16,128]{2,1,0:T(8,128)(2,1)S(1)}, s16[7,16,128]{2,1,0:T(8,128)(2,1)S(1)}, u32[]{:S(2)}, u32[]{:S(2)}) collective-permute-start(s16[7,16,128]{2,1,0:T(8,128)(2,1)S(1)} %get-tuple-element.40), channel_id=1, source_target_pairs={{0,3},{1,2},{2,1},{3,0},{4,5},{5,4},{6,7},{7,6},{8,11},{9,10},{10,... | collective-permute-start | bytes 86024 | tf_op jit(solution)/shard_map/ppermute | solution.py:257
  35.1 0.7 %collective-permute-done.12.refs_0_ = s16[7,16,128]{2,1,0:T(8,128)(2,1)S(1)} collective-permute-done((s16[7,16,128]{2,1,0:T(8,128)(2,1)S(1)}, s16[7,16,128]{2,1,0:T(8,128)(2,1)S(1)}, u32[]{:S(2)}, u32[]{:S(2)}) %collective-permute-start.12) | collective-permute-done | bytes 28704 | tf_op jit(solution)/shard_map/ppermute | solution.py:257
  35.8 3.4 %collective-permute-done.13.refs_1_ = s16[7,16,128]{2,1,0:T(8,128)(2,1)S(1)} collective-permute-done((s16[7,16,128]{2,1,0:T(8,128)(2,1)S(1)}, s16[7,16,128]{2,1,0:T(8,128)(2,1)S(1)}, u32[]{:S(2)}, u32[]{:S(2)}) %collective-permute-start.13) | collective-permute-done | bytes 28704 | tf_op jit(solution)/shard_map/ppermute | solution.py:257
  39.4 10.3 %all_to_all.5 = f32[32,4,128]{2,1,0:T(4,128)S(1)} all-to-all(f32[32,4,128]{2,1,0:T(4,128)S(1)} %bitcast.5), channel_id=1, replica_groups=mesh['chan'=8,'tm'=4] {'chan','tm'}, dimensions={0} | all-to-all | bytes 131072 | tf_op jit(solution)/shard_map/all_to_all | solution.py:411
  49.7 0.8 %place_lags.1 = f32[16,4,256]{2,1,0:T(4,128)} custom-call(f32[8,4,4,128]{3,2,1,0:T(4,128)S(1)} %bitcast.4), custom_call_target="tpu_custom_call" | custom-call | tf_op jit(solution)/shard_map/place_lags/pallas_call | solution.py:412
  (18 shorter events, 2.1 us)
Async XLA Ops:
  0.0 17.1 %copy-start = (bf16[16,2,8,16,128]{4,3,2,1,0:T(8,128)(2,1)S(1)}, bf16[16,2,8,16,128]{4,3,2,1,0:T(8,128)(2,1)}, u32[]{:S(2)}) copy-start(bf16[16,2,8,16,128]{4,3,2,1,0:T(8,128)(2,1)} %constant.11.clone.refs_9_) | copy-start | bytes 3145732
  1.1 8.5 %collective-permute-start = (bf16[2,256,128]{2,1,0:T(8,128)(2,1)S(1)}, bf16[2,256,128]{2,1,0:T(8,128)(2,1)S(1)}, u32[]{:S(2)}, u32[]{:S(2)}) collective-permute-start(bf16[2,256,128]{2,1,0:T(8,128)(2,1)S(1)} %get-tuple-element.24), channel_id=1, source_target_pairs={{0,24},{1,25},{2,26},{3,27},{4,28},{5,29},{6,30},{7,31},{8,16},{9,... | collective-permute-start | bytes 393224 | tf_op jit(solution)/shard_map/ppermute | solution.py:257
  5.0 6.7 %collective-permute-start.1 = (bf16[2,256,128]{2,1,0:T(8,128)(2,1)S(1)}, bf16[2,256,128]{2,1,0:T(8,128)(2,1)S(1)}, u32[]{:S(2)}, u32[]{:S(2)}) collective-permute-start(bf16[2,256,128]{2,1,0:T(8,128)(2,1)S(1)} %get-tuple-element.25), channel_id=1, source_target_pairs={{0,28},{1,29},{2,30},{3,31},{4,24},{5,25},{6,26},{7,27},{8,20},{9,... | collective-permute-start | bytes 393224 | tf_op jit(solution)/shard_map/ppermute | solution.py:257
  6.3 8.9 %collective-permute-start.2 = (bf16[2,256,128]{2,1,0:T(8,128)(2,1)S(1)}, bf16[2,256,128]{2,1,0:T(8,128)(2,1)S(1)}, u32[]{:S(2)}, u32[]{:S(2)}) collective-permute-start(bf16[2,256,128]{2,1,0:T(8,128)(2,1)S(1)} %get-tuple-element.26), channel_id=1, source_target_pairs={{0,8},{1,9},{2,10},{3,11},{4,12},{5,13},{6,14},{7,15},{8,0},{9,1},... | collective-permute-start | bytes 393224 | tf_op jit(solution)/shard_map/ppermute | solution.py:257
  7.5 7.7 %collective-permute-start.3 = (bf16[2,256,128]{2,1,0:T(8,128)(2,1)S(1)}, bf16[2,256,128]{2,1,0:T(8,128)(2,1)S(1)}, u32[]{:S(2)}, u32[]{:S(2)}) collective-permute-start(bf16[2,256,128]{2,1,0:T(8,128)(2,1)S(1)} %get-tuple-element.27), channel_id=1, source_target_pairs={{0,16},{1,17},{2,18},{3,19},{4,20},{5,21},{6,22},{7,23},{8,24},{9,... | collective-permute-start | bytes 393224 | tf_op jit(solution)/shard_map/ppermute | solution.py:257
  9.0 7.4 %collective-permute-start.4 = (bf16[2,256,128]{2,1,0:T(8,128)(2,1)S(1)}, bf16[2,256,128]{2,1,0:T(8,128)(2,1)S(1)}, u32[]{:S(2)}, u32[]{:S(2)}) collective-permute-start(bf16[2,256,128]{2,1,0:T(8,128)(2,1)S(1)} %get-tuple-element.28), channel_id=1, source_target_pairs={{0,12},{1,13},{2,14},{3,15},{4,8},{5,9},{6,10},{7,11},{8,4},{9,5},... | collective-permute-start | bytes 393224 | tf_op jit(solution)/shard_map/ppermute | solution.py:257
  9.6 7.5 %collective-permute-start.5 = (bf16[2,256,128]{2,1,0:T(8,128)(2,1)S(1)}, bf16[2,256,128]{2,1,0:T(8,128)(2,1)S(1)}, u32[]{:S(2)}, u32[]{:S(2)}) collective-permute-start(bf16[2,256,128]{2,1,0:T(8,128)(2,1)S(1)} %get-tuple-element.29), channel_id=1, source_target_pairs={{0,20},{1,21},{2,22},{3,23},{4,16},{5,17},{6,18},{7,19},{8,28},{9,... | collective-permute-start | bytes 393224 | tf_op jit(solution)/shard_map/ppermute | solution.py:257
  11.8 5.3 %collective-permute-start.6 = (bf16[2,256,128]{2,1,0:T(8,128)(2,1)S(1)}, bf16[2,256,128]{2,1,0:T(8,128)(2,1)S(1)}, u32[]{:S(2)}, u32[]{:S(2)}) collective-permute-start(bf16[2,256,128]{2,1,0:T(8,128)(2,1)S(1)} %get-tuple-element.30), channel_id=1, source_target_pairs={{0,4},{1,5},{2,6},{3,7},{4,0},{5,1},{6,2},{7,3},{8,12},{9,13},{10,... | collective-permute-start | bytes 393224 | tf_op jit(solution)/shard_map/ppermute | solution.py:257
  11.8 5.3 %copy-start.1 = (s32[8,128]{1,0:T(8,128)S(1)}, s32[8,128]{1,0:T(8,128)}, u32[]{:S(2)}) copy-start(s32[8,128]{1,0:T(8,128)} %refs_8_.1) | copy-start | bytes 12292
  20.2 1.5 %collective-permute-start.7 = (s16[2,22,16,128]{3,2,1,0:T(8,128)(2,1)S(1)}, s16[2,22,16,128]{3,2,1,0:T(8,128)(2,1)S(1)}, u32[]{:S(2)}, u32[]{:S(2)}) collective-permute-start(s16[2,22,16,128]{3,2,1,0:T(8,128)(2,1)S(1)} %get-tuple-element.33), channel_id=1, source_target_pairs={{0,4},{1,5},{2,6},{3,7},{4,0},{5,1},{6,2},{7,3},{8,12},{9,13},{10,... | collective-permute-start | bytes 540680 | tf_op jit(solution)/shard_map/ppermute | solution.py:257
  20.4 1.6 %collective-permute-start.8 = (s16[2,22,16,128]{3,2,1,0:T(8,128)(2,1)S(1)}, s16[2,22,16,128]{3,2,1,0:T(8,128)(2,1)S(1)}, u32[]{:S(2)}, u32[]{:S(2)}) collective-permute-start(s16[2,22,16,128]{3,2,1,0:T(8,128)(2,1)S(1)} %get-tuple-element.34), channel_id=1, source_target_pairs={{0,4},{1,5},{2,6},{3,7},{4,0},{5,1},{6,2},{7,3},{8,12},{9,13},{10,... | collective-permute-start | bytes 540680 | tf_op jit(solution)/shard_map/ppermute | solution.py:257
  22.2 5.1 %collective-permute-start.9 = (s16[22,16,128]{2,1,0:T(8,128)(2,1)S(1)}, s16[22,16,128]{2,1,0:T(8,128)(2,1)S(1)}, u32[]{:S(2)}, u32[]{:S(2)}) collective-permute-start(s16[22,16,128]{2,1,0:T(8,128)(2,1)S(1)} %get-tuple-element.35), channel_id=1, source_target_pairs={{0,16},{1,17},{2,18},{3,19},{4,12},{5,13},{6,14},{7,15},{8,24},{9,... | collective-permute-start | bytes 270344 | tf_op jit(solution)/shard_map/ppermute | solution.py:257
  23.7 5.3 %collective-permute-start.10 = (s16[22,16,128]{2,1,0:T(8,128)(2,1)S(1)}, s16[22,16,128]{2,1,0:T(8,128)(2,1)S(1)}, u32[]{:S(2)}, u32[]{:S(2)}) collective-permute-start(s16[22,16,128]{2,1,0:T(8,128)(2,1)S(1)} %get-tuple-element.36), channel_id=1, source_target_pairs={{0,8},{1,9},{2,10},{3,11},{4,20},{5,21},{6,22},{7,23},{8,0},{9,1},... | collective-permute-start | bytes 270344 | tf_op jit(solution)/shard_map/ppermute | solution.py:257
  25.3 5.4 %collective-permute-start.11 = (s16[22,16,128]{2,1,0:T(8,128)(2,1)S(1)}, s16[22,16,128]{2,1,0:T(8,128)(2,1)S(1)}, u32[]{:S(2)}, u32[]{:S(2)}) collective-permute-start(s16[22,16,128]{2,1,0:T(8,128)(2,1)S(1)} %get-tuple-element.37), channel_id=1, source_target_pairs={{0,24},{1,25},{2,26},{3,27},{4,28},{5,29},{6,30},{7,31},{8,16},{9,... | collective-permute-start | bytes 270344 | tf_op jit(solution)/shard_map/ppermute | solution.py:257
  30.9 4.9 %collective-permute-start.12 = (s16[7,16,128]{2,1,0:T(8,128)(2,1)S(1)}, s16[7,16,128]{2,1,0:T(8,128)(2,1)S(1)}, u32[]{:S(2)}, u32[]{:S(2)}) collective-permute-start(s16[7,16,128]{2,1,0:T(8,128)(2,1)S(1)} %get-tuple-element.39), channel_id=1, source_target_pairs={{0,2},{1,3},{2,0},{3,1},{4,7},{5,6},{6,5},{7,4},{8,10},{9,11},{10,... | collective-permute-start | bytes 86024 | tf_op jit(solution)/shard_map/ppermute | solution.py:257
  33.5 5.7 %collective-permute-start.13 = (s16[7,16,128]{2,1,0:T(8,128)(2,1)S(1)}, s16[7,16,128]{2,1,0:T(8,128)(2,1)S(1)}, u32[]{:S(2)}, u32[]{:S(2)}) collective-permute-start(s16[7,16,128]{2,1,0:T(8,128)(2,1)S(1)} %get-tuple-element.40), channel_id=1, source_target_pairs={{0,3},{1,2},{2,1},{3,0},{4,5},{5,4},{6,7},{7,6},{8,11},{9,10},{10,... | collective-permute-start | bytes 86024 | tf_op jit(solution)/shard_map/ppermute | solution.py:257
  34.9 4.3 %collective-permute-start.14 = (s16[7,16,128]{2,1,0:T(8,128)(2,1)S(1)}, s16[7,16,128]{2,1,0:T(8,128)(2,1)S(1)}, u32[]{:S(2)}, u32[]{:S(2)}) collective-permute-start(s16[7,16,128]{2,1,0:T(8,128)(2,1)S(1)} %get-tuple-element.41), channel_id=1, source_target_pairs={{0,1},{1,0},{2,3},{3,2},{4,6},{5,7},{6,4},{7,5},{8,9},{9,8},{10,11... | collective-permute-start | bytes 86024 | tf_op jit(solution)/shard_map/ppermute | solution.py:257

commit v29 on v26

--- a/solution.py
+++ b/solution.py
@@ -60,14 +60,15 @@
 def window_kernel(order, offs_hbm_ref, where_ref, *refs):
     chan_count = len(order)
     spec_refs, (qual_ref, table_ref) = refs[:chan_count], refs[chan_count : chan_count + 2]
-    out_refs = refs[chan_count + 2 : chan_count + 4]
-    mag_ref, white_ref, cross_ref, offs_ref, offs_sem = refs[chan_count + 4 :]
+    out_refs = refs[chan_count + 2 : chan_count + 6]
+    mag_ref, white_ref, cross_ref, offs_ref, offs_sem = refs[chan_count + 6 :]
     fetch = pltpu.make_async_copy(offs_hbm_ref, offs_ref, offs_sem)
     fetch.start()
     me = where_ref[0]
     _, band, chans = spec_refs[0].shape
     freqs = chan_count * band
-    chip_count, blocks, lag_rows, _ = out_refs[0].shape
+    chip_count = chan_count // 2
+    _, blocks, lag_rows, _ = out_refs[0].shape
     offset_count = offs_ref.shape[0]
     half = chan_count * lag_rows
     step = 64
@@ -149,15 +150,16 @@
         levels = jnp.where(line == number, code, levels)
         for place, value in enumerate(value for kind in kinds for value in kind):
             coded = encode(value).reshape(chan_count, lag_rows, chans)
-            for core in range(2):
-                rows = slice(core * chip_count, (core + 1) * chip_count)
-                out_refs[core][:, 6 * number + place, :, :] = coded[rows]
+            begin = 0
+            for out_ref in out_refs:
+                out_ref[:, 6 * number + place, :, :] = coded[begin : begin + out_ref.shape[0]]
+                begin += out_ref.shape[0]
     for number in range(offset_count):
         levels = jnp.where(line == offset_count + number, offs_ref[number].astype(jnp.float32), levels)
     wide = widest(offs_ref, chan_count // 2).astype(jnp.float32)
     levels = jnp.where(line == 2 * offset_count, wide, levels)
     for out_ref in out_refs:
-        for chip in range(chip_count):
+        for chip in range(out_ref.shape[0]):
             out_ref[chip, blocks - 1, :, :] = encode(levels)
 
 
@@ -363,11 +365,11 @@
         )(spectra)
     chip_count = chan_count // 2
     pair_shape = (6 * offset_count - 2, lag_rows, chans)
-    own, far = pl.pallas_call(
+    first_half, second_half, *far = pl.pallas_call(
         functools.partial(window_kernel, chan_order),
-        out_shape=[jax.ShapeDtypeStruct((chip_count, *pair_shape), jnp.int16)] * 2,
+        out_shape=[jax.ShapeDtypeStruct((chip_count // 2, *pair_shape), jnp.int16)] * 4,
         in_specs=[kept, smem] + [vmem] * (chan_count + 2),
-        out_specs=[vmem] * 2,
+        out_specs=[vmem] * 4,
         scratch_shapes=[
             pltpu.VMEM((freqs, chans), jnp.float32),
             pltpu.VMEM((2, freqs, chans), jnp.bfloat16),
@@ -378,14 +380,16 @@
         compiler_params=params,
         name="window_pairs",
     )(pltpu.with_memory_space_constraint(offsets, pltpu.HBM), chan_where, *exchange(pieces, (chan_order, chan_order)), quality, table)
-    pairs = pl.pallas_call(
-        functools.partial(merge_kernel, offset_count),
-        out_shape=[jax.ShapeDtypeStruct(pair_shape, jnp.int16)] * chip_count,
-        in_specs=[vmem] * 2,
-        out_specs=[vmem] * chip_count,
-        compiler_params=params,
-        name="merge_windows",
-    )(own, *exchange([far], ([1], [1])))
+    pairs = []
+    for own, other in zip((first_half, second_half), exchange(far, ([1, 1], [1, 1]))):
+        pairs += pl.pallas_call(
+            functools.partial(merge_kernel, offset_count),
+            out_shape=[jax.ShapeDtypeStruct(pair_shape, jnp.int16)] * (chip_count // 2),
+            in_specs=[vmem] * 2,
+            out_specs=[vmem] * (chip_count // 2),
+            compiler_params=params,
+            name="merge_windows",
+        )(own, other)
     sums = pl.pallas_call(
         functools.partial(sum_kernel, tm_orders, 1.0 / (CODE_TOP * math.sqrt(freqs))),
         out_shape=[jax.ShapeDtypeStruct((7, lag_rows, chans), jnp.int16)] * tm_count,

time: 50.5 us -> 50.3 us (level)
  waiting for transfers between devices: 17.6 us -> 16.9 us
    ppermute x14 -> x15, waiting for transfers between devices: 17.6 us -> 16.9 us  [exchange(): lax.ppermute(piece, ('chan', 'tm'), pairs)]
    ppermute x14 -> x15, starting transfers between devices: 15.8 us -> 16.2 us  [exchange(): lax.ppermute(piece, ('chan', 'tm'), pairs)]
  transfers between devices with their start and end apart: 14 -> 15, of which waited for: 10 -> 10; matrix products, arithmetic and copies ran while one was open for 0% -> 0% of each run, Pallas kernels for 2% -> 3%
where the time goes in v29:
time: 50.3 us; the launch traced here: 50.2 us
  waiting for transfers between devices  16.9 us (34%)
  starting transfers between devices  16.2 us (32%)
  blocking collectives  10.2 us (20%)
  Pallas kernels  6.78 us (13%)
    ppermute x15, waiting for transfers between devices, exchange(): lax.ppermute(piece, ('chan', 'tm'), pairs)  16.9 us
    ppermute x15, starting transfers between devices, exchange(): lax.ppermute(piece, ('chan', 'tm'), pairs)  16.2 us
    all_to_all x1, blocking collectives, window_shards(): lax.all_to_all(pieces.reshape(shape), ('chan', 'tm'), 0, 0, tiled=True)  10.2 us
    pallas_call x1, Pallas kernels, window_shards(): pl.pallas_call(functools.partial(window_kernel, chan_order), out_shape=[j...  3.14 us
    pallas_call x2, Pallas kernels, window_shards(): pl.pallas_call(functools.partial(split_kernel, part), out_shape=[jax.Shap...  2.32 us
  transfers between devices with their start and end apart: 15, of which 10 were waited for; matrix products, arithmetic and copies ran while one was open for 0% of the time, Pallas kernels for 3%

profile of v29, /device:TPU:0, one launch (start us, length us, event | category | flops | bytes accessed | tf_op | source)
XLA Modules:
  0.0 50.2 jit_solution(15894601164364226565)
XLA Ops:
  0.0 1.1 %split_windows.2 = (bf16[2,256,128]{2,1,0:T(8,128)(2,1)S(1)}, bf16[2,256,128]{2,1,0:T(8,128)(2,1)S(1)}) custom-call(bf16[2,8,256,128]{3,2,1,0:T(8,128)(2,1)} %spec_ref.3), custom_call_target="tpu_custom_call" | custom-call | tf_op jit(solution)/shard_map/split_windows/pallas_call | solution.py:357
  1.1 4.0 %collective-permute-start = (bf16[2,256,128]{2,1,0:T(8,128)(2,1)S(1)}, bf16[2,256,128]{2,1,0:T(8,128)(2,1)S(1)}, u32[]{:S(2)}, u32[]{:S(2)}) collective-permute-start(bf16[2,256,128]{2,1,0:T(8,128)(2,1)S(1)} %get-tuple-element.25), channel_id=1, source_target_pairs={{0,24},{1,25},{2,26},{3,27},{4,28},{5,29},{6,30},{7,31},{8,16},{9,... | collective-permute-start | bytes 393224 | tf_op jit(solution)/shard_map/ppermute | solution.py:257
  5.0 1.3 %split_windows.3 = (bf16[2,256,128]{2,1,0:T(8,128)(2,1)S(1)}, bf16[2,256,128]{2,1,0:T(8,128)(2,1)S(1)}, bf16[2,256,128]{2,1,0:T(8,128)(2,1)S(1)}, bf16[2,256,128...) custom-call(bf16[2,8,256,128]{3,2,1,0:T(8,128)(2,1)} %spec_ref.3), custom_call_target="tpu_custom_call" | custom-call | tf_op jit(solution)/shard_map/split_windows/pallas_call | solution.py:357
  6.3 1.2 %collective-permute-start.2 = (bf16[2,256,128]{2,1,0:T(8,128)(2,1)S(1)}, bf16[2,256,128]{2,1,0:T(8,128)(2,1)S(1)}, u32[]{:S(2)}, u32[]{:S(2)}) collective-permute-start(bf16[2,256,128]{2,1,0:T(8,128)(2,1)S(1)} %get-tuple-element.27), channel_id=1, source_target_pairs={{0,8},{1,9},{2,10},{3,11},{4,12},{5,13},{6,14},{7,15},{8,0},{9,1},... | collective-permute-start | bytes 393224 | tf_op jit(solution)/shard_map/ppermute | solution.py:257
  7.5 1.5 %collective-permute-start.3 = (bf16[2,256,128]{2,1,0:T(8,128)(2,1)S(1)}, bf16[2,256,128]{2,1,0:T(8,128)(2,1)S(1)}, u32[]{:S(2)}, u32[]{:S(2)}) collective-permute-start(bf16[2,256,128]{2,1,0:T(8,128)(2,1)S(1)} %get-tuple-element.28), channel_id=1, source_target_pairs={{0,16},{1,17},{2,18},{3,19},{4,20},{5,21},{6,22},{7,23},{8,24},{9,... | collective-permute-start | bytes 393224 | tf_op jit(solution)/shard_map/ppermute | solution.py:257
  9.0 0.6 %collective-permute-start.4 = (bf16[2,256,128]{2,1,0:T(8,128)(2,1)S(1)}, bf16[2,256,128]{2,1,0:T(8,128)(2,1)S(1)}, u32[]{:S(2)}, u32[]{:S(2)}) collective-permute-start(bf16[2,256,128]{2,1,0:T(8,128)(2,1)S(1)} %get-tuple-element.29), channel_id=1, source_target_pairs={{0,12},{1,13},{2,14},{3,15},{4,8},{5,9},{6,10},{7,11},{8,4},{9,5},... | collective-permute-start | bytes 393224 | tf_op jit(solution)/shard_map/ppermute | solution.py:257
  9.6 0.6 %collective-permute-start.5 = (bf16[2,256,128]{2,1,0:T(8,128)(2,1)S(1)}, bf16[2,256,128]{2,1,0:T(8,128)(2,1)S(1)}, u32[]{:S(2)}, u32[]{:S(2)}) collective-permute-start(bf16[2,256,128]{2,1,0:T(8,128)(2,1)S(1)} %get-tuple-element.30), channel_id=1, source_target_pairs={{0,20},{1,21},{2,22},{3,23},{4,16},{5,17},{6,18},{7,19},{8,28},{9,... | collective-permute-start | bytes 393224 | tf_op jit(solution)/shard_map/ppermute | solution.py:257
  10.1 1.6 %collective-permute-done.1.refs_1_ = bf16[2,256,128]{2,1,0:T(8,128)(2,1)S(1)} collective-permute-done((bf16[2,256,128]{2,1,0:T(8,128)(2,1)S(1)}, bf16[2,256,128]{2,1,0:T(8,128)(2,1)S(1)}, u32[]{:S(2)}, u32[]{:S(2)}) %collective-permute-start.1) | collective-permute-done | bytes 131104 | tf_op jit(solution)/shard_map/ppermute | solution.py:257
  11.8 3.5 %collective-permute-done.2.refs_2_ = bf16[2,256,128]{2,1,0:T(8,128)(2,1)S(1)} collective-permute-done((bf16[2,256,128]{2,1,0:T(8,128)(2,1)S(1)}, bf16[2,256,128]{2,1,0:T(8,128)(2,1)S(1)}, u32[]{:S(2)}, u32[]{:S(2)}) %collective-permute-start.2) | collective-permute-done | bytes 131104 | tf_op jit(solution)/shard_map/ppermute | solution.py:257
  15.2 1.1 %collective-permute-done.4.refs_4_ = bf16[2,256,128]{2,1,0:T(8,128)(2,1)S(1)} collective-permute-done((bf16[2,256,128]{2,1,0:T(8,128)(2,1)S(1)}, bf16[2,256,128]{2,1,0:T(8,128)(2,1)S(1)}, u32[]{:S(2)}, u32[]{:S(2)}) %collective-permute-start.4) | collective-permute-done | bytes 131104 | tf_op jit(solution)/shard_map/ppermute | solution.py:257
  16.4 0.7 %collective-permute-done.5.refs_5_ = bf16[2,256,128]{2,1,0:T(8,128)(2,1)S(1)} collective-permute-done((bf16[2,256,128]{2,1,0:T(8,128)(2,1)S(1)}, bf16[2,256,128]{2,1,0:T(8,128)(2,1)S(1)}, u32[]{:S(2)}, u32[]{:S(2)}) %collective-permute-start.5) | collective-permute-done | bytes 131104 | tf_op jit(solution)/shard_map/ppermute | solution.py:257
  17.1 3.1 %window_pairs.1 = (s16[2,22,16,128]{3,2,1,0:T(8,128)(2,1)S(1)}, s16[2,22,16,128]{3,2,1,0:T(8,128)(2,1)S(1)}, s16[2,22,16,128]{3,2,1,0:T(8,128)(2,1)S(1)}, s16[2,22,16,128]{3,2,1,0:T(8,128)(2,1)S(1)}) custom-call(s32[4]{0:T(128)} %offs_hbm_ref.1, s32[1]{0:T(128)} %bitcast.where_ref.core_ref, bf16[2,256,128]{2,1,0:T(8,128)(2,1)S(1)} %collective-permute-done.refs_0_, ...), custom_call_target="tpu_custom_call" | custom-call | tf_op jit(solution)/shard_map/window_pairs/pallas_call | solution.py:368
  20.8 0.9 %collective-permute-done.7.far_ref = s16[2,22,16,128]{3,2,1,0:T(8,128)(2,1)S(1)} collective-permute-done((s16[2,22,16,128]{3,2,1,0:T(8,128)(2,1)S(1)}, s16[2,22,16,128]{3,2,1,0:T(8,128)(2,1)S(1)}, u32[]{:S(2)}, u32[]{:S(2)}) %collective-permute-start.7) | collective-permute-done | bytes 180256 | tf_op jit(solution)/shard_map/ppermute | solution.py:257
  21.8 1.6 %collective-permute-start.8 = (s16[22,16,128]{2,1,0:T(8,128)(2,1)S(1)}, s16[22,16,128]{2,1,0:T(8,128)(2,1)S(1)}, u32[]{:S(2)}, u32[]{:S(2)}) collective-permute-start(s16[22,16,128]{2,1,0:T(8,128)(2,1)S(1)} %get-tuple-element.35), channel_id=1, source_target_pairs={{0,16},{1,17},{2,18},{3,19},{4,12},{5,13},{6,14},{7,15},{8,24},{9,... | collective-permute-start | bytes 270344 | tf_op jit(solution)/shard_map/ppermute | solution.py:257
  23.4 1.6 %collective-permute-start.9 = (s16[22,16,128]{2,1,0:T(8,128)(2,1)S(1)}, s16[22,16,128]{2,1,0:T(8,128)(2,1)S(1)}, u32[]{:S(2)}, u32[]{:S(2)}) collective-permute-start(s16[22,16,128]{2,1,0:T(8,128)(2,1)S(1)} %get-tuple-element.36), channel_id=1, source_target_pairs={{0,8},{1,9},{2,10},{3,11},{4,20},{5,21},{6,22},{7,23},{8,0},{9,1},... | collective-permute-start | bytes 270344 | tf_op jit(solution)/shard_map/ppermute | solution.py:257
  25.6 1.5 %collective-permute-done.8.refs_0_ = s16[22,16,128]{2,1,0:T(8,128)(2,1)S(1)} collective-permute-done((s16[22,16,128]{2,1,0:T(8,128)(2,1)S(1)}, s16[22,16,128]{2,1,0:T(8,128)(2,1)S(1)}, u32[]{:S(2)}, u32[]{:S(2)}) %collective-permute-start.8) | collective-permute-done | bytes 90144 | tf_op jit(solution)/shard_map/ppermute | solution.py:257
  27.1 1.5 %collective-permute-done.9.refs_1_ = s16[22,16,128]{2,1,0:T(8,128)(2,1)S(1)} collective-permute-done((s16[22,16,128]{2,1,0:T(8,128)(2,1)S(1)}, s16[22,16,128]{2,1,0:T(8,128)(2,1)S(1)}, u32[]{:S(2)}, u32[]{:S(2)}) %collective-permute-start.9) | collective-permute-done | bytes 90144 | tf_op jit(solution)/shard_map/ppermute | solution.py:257
  28.6 1.9 %collective-permute-done.11.refs_2_ = s16[22,16,128]{2,1,0:T(8,128)(2,1)S(1)} collective-permute-done((s16[22,16,128]{2,1,0:T(8,128)(2,1)S(1)}, s16[22,16,128]{2,1,0:T(8,128)(2,1)S(1)}, u32[]{:S(2)}, u32[]{:S(2)}) %collective-permute-start.11) | collective-permute-done | bytes 90144 | tf_op jit(solution)/shard_map/ppermute | solution.py:257
  30.7 2.7 %collective-permute-start.12 = (s16[7,16,128]{2,1,0:T(8,128)(2,1)S(1)}, s16[7,16,128]{2,1,0:T(8,128)(2,1)S(1)}, u32[]{:S(2)}, u32[]{:S(2)}) collective-permute-start(s16[7,16,128]{2,1,0:T(8,128)(2,1)S(1)} %get-tuple-element.41), channel_id=1, source_target_pairs={{0,2},{1,3},{2,0},{3,1},{4,7},{5,6},{6,5},{7,4},{8,10},{9,11},{10,... | collective-permute-start | bytes 86024 | tf_op jit(solution)/shard_map/ppermute | solution.py:257
  33.4 1.3 %collective-permute-start.13 = (s16[7,16,128]{2,1,0:T(8,128)(2,1)S(1)}, s16[7,16,128]{2,1,0:T(8,128)(2,1)S(1)}, u32[]{:S(2)}, u32[]{:S(2)}) collective-permute-start(s16[7,16,128]{2,1,0:T(8,128)(2,1)S(1)} %get-tuple-element.42), channel_id=1, source_target_pairs={{0,3},{1,2},{2,1},{3,0},{4,5},{5,4},{6,7},{7,6},{8,11},{9,10},{10,... | collective-permute-start | bytes 86024 | tf_op jit(solution)/shard_map/ppermute | solution.py:257
  34.9 0.7 %collective-permute-done.12.refs_0_ = s16[7,16,128]{2,1,0:T(8,128)(2,1)S(1)} collective-permute-done((s16[7,16,128]{2,1,0:T(8,128)(2,1)S(1)}, s16[7,16,128]{2,1,0:T(8,128)(2,1)S(1)}, u32[]{:S(2)}, u32[]{:S(2)}) %collective-permute-start.12) | collective-permute-done | bytes 28704 | tf_op jit(solution)/shard_map/ppermute | solution.py:257
  35.7 3.4 %collective-permute-done.13.refs_1_ = s16[7,16,128]{2,1,0:T(8,128)(2,1)S(1)} collective-permute-done((s16[7,16,128]{2,1,0:T(8,128)(2,1)S(1)}, s16[7,16,128]{2,1,0:T(8,128)(2,1)S(1)}, u32[]{:S(2)}, u32[]{:S(2)}) %collective-permute-start.13) | collective-permute-done | bytes 28704 | tf_op jit(solution)/shard_map/ppermute | solution.py:257
  39.2 10.2 %all_to_all.5 = f32[32,4,128]{2,1,0:T(4,128)S(1)} all-to-all(f32[32,4,128]{2,1,0:T(4,128)S(1)} %bitcast.5), channel_id=1, replica_groups=mesh['chan'=8,'tm'=4] {'chan','tm'}, dimensions={0} | all-to-all | bytes 131072 | tf_op jit(solution)/shard_map/all_to_all | solution.py:411
  49.4 0.8 %place_lags.1 = f32[16,4,256]{2,1,0:T(4,128)} custom-call(f32[8,4,4,128]{3,2,1,0:T(4,128)S(1)} %bitcast.4), custom_call_target="tpu_custom_call" | custom-call | tf_op jit(solution)/shard_map/place_lags/pallas_call | solution.py:412
  (19 shorter events, 1.9 us)
Async XLA Ops:
  0.0 17.1 %copy-start = (bf16[16,2,8,16,128]{4,3,2,1,0:T(8,128)(2,1)S(1)}, bf16[16,2,8,16,128]{4,3,2,1,0:T(8,128)(2,1)}, u32[]{:S(2)}) copy-start(bf16[16,2,8,16,128]{4,3,2,1,0:T(8,128)(2,1)} %constant.11.clone.refs_9_) | copy-start | bytes 3145732
  1.1 8.5 %collective-permute-start = (bf16[2,256,128]{2,1,0:T(8,128)(2,1)S(1)}, bf16[2,256,128]{2,1,0:T(8,128)(2,1)S(1)}, u32[]{:S(2)}, u32[]{:S(2)}) collective-permute-start(bf16[2,256,128]{2,1,0:T(8,128)(2,1)S(1)} %get-tuple-element.25), channel_id=1, source_target_pairs={{0,24},{1,25},{2,26},{3,27},{4,28},{5,29},{6,30},{7,31},{8,16},{9,... | collective-permute-start | bytes 393224 | tf_op jit(solution)/shard_map/ppermute | solution.py:257
  5.0 6.7 %collective-permute-start.1 = (bf16[2,256,128]{2,1,0:T(8,128)(2,1)S(1)}, bf16[2,256,128]{2,1,0:T(8,128)(2,1)S(1)}, u32[]{:S(2)}, u32[]{:S(2)}) collective-permute-start(bf16[2,256,128]{2,1,0:T(8,128)(2,1)S(1)} %get-tuple-element.26), channel_id=1, source_target_pairs={{0,28},{1,29},{2,30},{3,31},{4,24},{5,25},{6,26},{7,27},{8,20},{9,... | collective-permute-start | bytes 393224 | tf_op jit(solution)/shard_map/ppermute | solution.py:257
  6.3 8.9 %collective-permute-start.2 = (bf16[2,256,128]{2,1,0:T(8,128)(2,1)S(1)}, bf16[2,256,128]{2,1,0:T(8,128)(2,1)S(1)}, u32[]{:S(2)}, u32[]{:S(2)}) collective-permute-start(bf16[2,256,128]{2,1,0:T(8,128)(2,1)S(1)} %get-tuple-element.27), channel_id=1, source_target_pairs={{0,8},{1,9},{2,10},{3,11},{4,12},{5,13},{6,14},{7,15},{8,0},{9,1},... | collective-permute-start | bytes 393224 | tf_op jit(solution)/shard_map/ppermute | solution.py:257
  7.5 7.7 %collective-permute-start.3 = (bf16[2,256,128]{2,1,0:T(8,128)(2,1)S(1)}, bf16[2,256,128]{2,1,0:T(8,128)(2,1)S(1)}, u32[]{:S(2)}, u32[]{:S(2)}) collective-permute-start(bf16[2,256,128]{2,1,0:T(8,128)(2,1)S(1)} %get-tuple-element.28), channel_id=1, source_target_pairs={{0,16},{1,17},{2,18},{3,19},{4,20},{5,21},{6,22},{7,23},{8,24},{9,... | collective-permute-start | bytes 393224 | tf_op jit(solution)/shard_map/ppermute | solution.py:257
  9.0 7.4 %collective-permute-start.4 = (bf16[2,256,128]{2,1,0:T(8,128)(2,1)S(1)}, bf16[2,256,128]{2,1,0:T(8,128)(2,1)S(1)}, u32[]{:S(2)}, u32[]{:S(2)}) collective-permute-start(bf16[2,256,128]{2,1,0:T(8,128)(2,1)S(1)} %get-tuple-element.29), channel_id=1, source_target_pairs={{0,12},{1,13},{2,14},{3,15},{4,8},{5,9},{6,10},{7,11},{8,4},{9,5},... | collective-permute-start | bytes 393224 | tf_op jit(solution)/shard_map/ppermute | solution.py:257
  9.6 7.5 %collective-permute-start.5 = (bf16[2,256,128]{2,1,0:T(8,128)(2,1)S(1)}, bf16[2,256,128]{2,1,0:T(8,128)(2,1)S(1)}, u32[]{:S(2)}, u32[]{:S(2)}) collective-permute-start(bf16[2,256,128]{2,1,0:T(8,128)(2,1)S(1)} %get-tuple-element.30), channel_id=1, source_target_pairs={{0,20},{1,21},{2,22},{3,23},{4,16},{5,17},{6,18},{7,19},{8,28},{9,... | collective-permute-start | bytes 393224 | tf_op jit(solution)/shard_map/ppermute | solution.py:257
  11.8 5.3 %collective-permute-start.6 = (bf16[2,256,128]{2,1,0:T(8,128)(2,1)S(1)}, bf16[2,256,128]{2,1,0:T(8,128)(2,1)S(1)}, u32[]{:S(2)}, u32[]{:S(2)}) collective-permute-start(bf16[2,256,128]{2,1,0:T(8,128)(2,1)S(1)} %get-tuple-element.31), channel_id=1, source_target_pairs={{0,4},{1,5},{2,6},{3,7},{4,0},{5,1},{6,2},{7,3},{8,12},{9,13},{10,... | collective-permute-start | bytes 393224 | tf_op jit(solution)/shard_map/ppermute | solution.py:257
  11.8 5.3 %copy-start.1 = (s32[8,128]{1,0:T(8,128)S(1)}, s32[8,128]{1,0:T(8,128)}, u32[]{:S(2)}) copy-start(s32[8,128]{1,0:T(8,128)} %refs_8_.1) | copy-start | bytes 12292
  20.2 1.5 %collective-permute-start.7 = (s16[2,22,16,128]{3,2,1,0:T(8,128)(2,1)S(1)}, s16[2,22,16,128]{3,2,1,0:T(8,128)(2,1)S(1)}, u32[]{:S(2)}, u32[]{:S(2)}) collective-permute-start(s16[2,22,16,128]{3,2,1,0:T(8,128)(2,1)S(1)} %get-tuple-element.34), channel_id=1, source_target_pairs={{0,4},{1,5},{2,6},{3,7},{4,0},{5,1},{6,2},{7,3},{8,12},{9,13},{10,... | collective-permute-start | bytes 540680 | tf_op jit(solution)/shard_map/ppermute | solution.py:257
  20.4 4.6 %collective-permute-start.10 = (s16[2,22,16,128]{3,2,1,0:T(8,128)(2,1)S(1)}, s16[2,22,16,128]{3,2,1,0:T(8,128)(2,1)S(1)}, u32[]{:S(2)}, u32[]{:S(2)}) collective-permute-start(s16[2,22,16,128]{3,2,1,0:T(8,128)(2,1)S(1)} %get-tuple-element.38), channel_id=1, source_target_pairs={{0,4},{1,5},{2,6},{3,7},{4,0},{5,1},{6,2},{7,3},{8,12},{9,13},{10,... | collective-permute-start | bytes 540680 | tf_op jit(solution)/shard_map/ppermute | solution.py:257
  21.8 5.3 %collective-permute-start.8 = (s16[22,16,128]{2,1,0:T(8,128)(2,1)S(1)}, s16[22,16,128]{2,1,0:T(8,128)(2,1)S(1)}, u32[]{:S(2)}, u32[]{:S(2)}) collective-permute-start(s16[22,16,128]{2,1,0:T(8,128)(2,1)S(1)} %get-tuple-element.35), channel_id=1, source_target_pairs={{0,16},{1,17},{2,18},{3,19},{4,12},{5,13},{6,14},{7,15},{8,24},{9,... | collective-permute-start | bytes 270344 | tf_op jit(solution)/shard_map/ppermute | solution.py:257
  23.4 5.2 %collective-permute-start.9 = (s16[22,16,128]{2,1,0:T(8,128)(2,1)S(1)}, s16[22,16,128]{2,1,0:T(8,128)(2,1)S(1)}, u32[]{:S(2)}, u32[]{:S(2)}) collective-permute-start(s16[22,16,128]{2,1,0:T(8,128)(2,1)S(1)} %get-tuple-element.36), channel_id=1, source_target_pairs={{0,8},{1,9},{2,10},{3,11},{4,20},{5,21},{6,22},{7,23},{8,0},{9,1},... | collective-permute-start | bytes 270344 | tf_op jit(solution)/shard_map/ppermute | solution.py:257
  25.1 5.5 %collective-permute-start.11 = (s16[22,16,128]{2,1,0:T(8,128)(2,1)S(1)}, s16[22,16,128]{2,1,0:T(8,128)(2,1)S(1)}, u32[]{:S(2)}, u32[]{:S(2)}) collective-permute-start(s16[22,16,128]{2,1,0:T(8,128)(2,1)S(1)} %get-tuple-element.39), channel_id=1, source_target_pairs={{0,24},{1,25},{2,26},{3,27},{4,28},{5,29},{6,30},{7,31},{8,16},{9,... | collective-permute-start | bytes 270344 | tf_op jit(solution)/shard_map/ppermute | solution.py:257
  30.7 4.9 %collective-permute-start.12 = (s16[7,16,128]{2,1,0:T(8,128)(2,1)S(1)}, s16[7,16,128]{2,1,0:T(8,128)(2,1)S(1)}, u32[]{:S(2)}, u32[]{:S(2)}) collective-permute-start(s16[7,16,128]{2,1,0:T(8,128)(2,1)S(1)} %get-tuple-element.41), channel_id=1, source_target_pairs={{0,2},{1,3},{2,0},{3,1},{4,7},{5,6},{6,5},{7,4},{8,10},{9,11},{10,... | collective-permute-start | bytes 86024 | tf_op jit(solution)/shard_map/ppermute | solution.py:257
  33.4 5.7 %collective-permute-start.13 = (s16[7,16,128]{2,1,0:T(8,128)(2,1)S(1)}, s16[7,16,128]{2,1,0:T(8,128)(2,1)S(1)}, u32[]{:S(2)}, u32[]{:S(2)}) collective-permute-start(s16[7,16,128]{2,1,0:T(8,128)(2,1)S(1)} %get-tuple-element.42), channel_id=1, source_target_pairs={{0,3},{1,2},{2,1},{3,0},{4,5},{5,4},{6,7},{7,6},{8,11},{9,10},{10,... | collective-permute-start | bytes 86024 | tf_op jit(solution)/shard_map/ppermute | solution.py:257
  34.7 4.3 %collective-permute-start.14 = (s16[7,16,128]{2,1,0:T(8,128)(2,1)S(1)}, s16[7,16,128]{2,1,0:T(8,128)(2,1)S(1)}, u32[]{:S(2)}, u32[]{:S(2)}) collective-permute-start(s16[7,16,128]{2,1,0:T(8,128)(2,1)S(1)} %get-tuple-element.43), channel_id=1, source_target_pairs={{0,1},{1,0},{2,3},{3,2},{4,6},{5,7},{6,4},{7,5},{8,9},{9,8},{10,11... | collective-permute-start | bytes 86024 | tf_op jit(solution)/shard_map/ppermute | solution.py:257

commit v30 on v29

--- a/solution.py
+++ b/solution.py
@@ -237,8 +237,8 @@
 
 
 def planes(count):
-    others = partners(count)[:-1]
-    return others + [0], others[1:] + others[:1] + [0]
+    order = list(range(1, count)) + [0]
+    return order, order
 
 
 def partner(orders, place, core):

time: 50.3 us -> 50.9 us (1.012)
  waiting for transfers between devices: 16.9 us -> 18.3 us
  blocking collectives: 10.2 us -> 9.19 us
    ppermute x15, waiting for transfers between devices: 16.9 us -> 18.3 us  [exchange(): lax.ppermute(piece, ('chan', 'tm'), pairs)]
    all_to_all x1, blocking collectives: 10.2 us -> 9.19 us  [window_shards(): lax.all_to_all(pieces.reshape(shape), ('chan', 'tm'), 0, 0, tiled=True)]
where the time goes in v30:
time: 50.9 us; the launch traced here: 50.8 us
  waiting for transfers between devices  18.3 us (36%)
  starting transfers between devices  16.4 us (32%)
  blocking collectives  9.19 us (18%)
  Pallas kernels  6.78 us (13%)
    ppermute x15, waiting for transfers between devices, exchange(): lax.ppermute(piece, ('chan', 'tm'), pairs)  18.3 us
    ppermute x15, starting transfers between devices, exchange(): lax.ppermute(piece, ('chan', 'tm'), pairs)  16.4 us
    all_to_all x1, blocking collectives, window_shards(): lax.all_to_all(pieces.reshape(shape), ('chan', 'tm'), 0, 0, tiled=True)  9.19 us
    pallas_call x1, Pallas kernels, window_shards(): pl.pallas_call(functools.partial(window_kernel, chan_order), out_shape=[j...  3.14 us
    pallas_call x2, Pallas kernels, window_shards(): pl.pallas_call(functools.partial(split_kernel, part), out_shape=[jax.Shap...  2.32 us
  transfers between devices with their start and end apart: 15, of which 10 were waited for; matrix products, arithmetic and copies ran while one was open for 0% of the time, Pallas kernels for 3%

profile of v30, /device:TPU:0, one launch (start us, length us, event | category | flops | bytes accessed | tf_op | source)
XLA Modules:
  0.0 50.8 jit_solution(441144637693864914)
XLA Ops:
  0.0 1.1 %split_windows.2 = (bf16[2,256,128]{2,1,0:T(8,128)(2,1)S(1)}, bf16[2,256,128]{2,1,0:T(8,128)(2,1)S(1)}) custom-call(bf16[2,8,256,128]{3,2,1,0:T(8,128)(2,1)} %spec_ref.3), custom_call_target="tpu_custom_call" | custom-call | tf_op jit(solution)/shard_map/split_windows/pallas_call | solution.py:357
  1.1 4.0 %collective-permute-start = (bf16[2,256,128]{2,1,0:T(8,128)(2,1)S(1)}, bf16[2,256,128]{2,1,0:T(8,128)(2,1)S(1)}, u32[]{:S(2)}, u32[]{:S(2)}) collective-permute-start(bf16[2,256,128]{2,1,0:T(8,128)(2,1)S(1)} %get-tuple-element.25), channel_id=1, source_target_pairs={{0,24},{1,25},{2,26},{3,27},{4,28},{5,29},{6,30},{7,31},{8,16},{9,... | collective-permute-start | bytes 393224 | tf_op jit(solution)/shard_map/ppermute | solution.py:257
  5.0 1.3 %split_windows.3 = (bf16[2,256,128]{2,1,0:T(8,128)(2,1)S(1)}, bf16[2,256,128]{2,1,0:T(8,128)(2,1)S(1)}, bf16[2,256,128]{2,1,0:T(8,128)(2,1)S(1)}, bf16[2,256,128...) custom-call(bf16[2,8,256,128]{3,2,1,0:T(8,128)(2,1)} %spec_ref.3), custom_call_target="tpu_custom_call" | custom-call | tf_op jit(solution)/shard_map/split_windows/pallas_call | solution.py:357
  6.3 1.2 %collective-permute-start.2 = (bf16[2,256,128]{2,1,0:T(8,128)(2,1)S(1)}, bf16[2,256,128]{2,1,0:T(8,128)(2,1)S(1)}, u32[]{:S(2)}, u32[]{:S(2)}) collective-permute-start(bf16[2,256,128]{2,1,0:T(8,128)(2,1)S(1)} %get-tuple-element.27), channel_id=1, source_target_pairs={{0,8},{1,9},{2,10},{3,11},{4,12},{5,13},{6,14},{7,15},{8,0},{9,1},... | collective-permute-start | bytes 393224 | tf_op jit(solution)/shard_map/ppermute | solution.py:257
  7.5 1.5 %collective-permute-start.3 = (bf16[2,256,128]{2,1,0:T(8,128)(2,1)S(1)}, bf16[2,256,128]{2,1,0:T(8,128)(2,1)S(1)}, u32[]{:S(2)}, u32[]{:S(2)}) collective-permute-start(bf16[2,256,128]{2,1,0:T(8,128)(2,1)S(1)} %get-tuple-element.28), channel_id=1, source_target_pairs={{0,16},{1,17},{2,18},{3,19},{4,20},{5,21},{6,22},{7,23},{8,24},{9,... | collective-permute-start | bytes 393224 | tf_op jit(solution)/shard_map/ppermute | solution.py:257
  9.0 0.6 %collective-permute-start.4 = (bf16[2,256,128]{2,1,0:T(8,128)(2,1)S(1)}, bf16[2,256,128]{2,1,0:T(8,128)(2,1)S(1)}, u32[]{:S(2)}, u32[]{:S(2)}) collective-permute-start(bf16[2,256,128]{2,1,0:T(8,128)(2,1)S(1)} %get-tuple-element.29), channel_id=1, source_target_pairs={{0,12},{1,13},{2,14},{3,15},{4,8},{5,9},{6,10},{7,11},{8,4},{9,5},... | collective-permute-start | bytes 393224 | tf_op jit(solution)/shard_map/ppermute | solution.py:257
  9.6 0.6 %collective-permute-start.5 = (bf16[2,256,128]{2,1,0:T(8,128)(2,1)S(1)}, bf16[2,256,128]{2,1,0:T(8,128)(2,1)S(1)}, u32[]{:S(2)}, u32[]{:S(2)}) collective-permute-start(bf16[2,256,128]{2,1,0:T(8,128)(2,1)S(1)} %get-tuple-element.30), channel_id=1, source_target_pairs={{0,20},{1,21},{2,22},{3,23},{4,16},{5,17},{6,18},{7,19},{8,28},{9,... | collective-permute-start | bytes 393224 | tf_op jit(solution)/shard_map/ppermute | solution.py:257
  10.1 1.6 %collective-permute-done.1.refs_1_ = bf16[2,256,128]{2,1,0:T(8,128)(2,1)S(1)} collective-permute-done((bf16[2,256,128]{2,1,0:T(8,128)(2,1)S(1)}, bf16[2,256,128]{2,1,0:T(8,128)(2,1)S(1)}, u32[]{:S(2)}, u32[]{:S(2)}) %collective-permute-start.1) | collective-permute-done | bytes 131104 | tf_op jit(solution)/shard_map/ppermute | solution.py:257
  11.8 3.5 %collective-permute-done.2.refs_2_ = bf16[2,256,128]{2,1,0:T(8,128)(2,1)S(1)} collective-permute-done((bf16[2,256,128]{2,1,0:T(8,128)(2,1)S(1)}, bf16[2,256,128]{2,1,0:T(8,128)(2,1)S(1)}, u32[]{:S(2)}, u32[]{:S(2)}) %collective-permute-start.2) | collective-permute-done | bytes 131104 | tf_op jit(solution)/shard_map/ppermute | solution.py:257
  15.2 1.1 %collective-permute-done.4.refs_4_ = bf16[2,256,128]{2,1,0:T(8,128)(2,1)S(1)} collective-permute-done((bf16[2,256,128]{2,1,0:T(8,128)(2,1)S(1)}, bf16[2,256,128]{2,1,0:T(8,128)(2,1)S(1)}, u32[]{:S(2)}, u32[]{:S(2)}) %collective-permute-start.4) | collective-permute-done | bytes 131104 | tf_op jit(solution)/shard_map/ppermute | solution.py:257
  16.4 0.7 %collective-permute-done.5.refs_5_ = bf16[2,256,128]{2,1,0:T(8,128)(2,1)S(1)} collective-permute-done((bf16[2,256,128]{2,1,0:T(8,128)(2,1)S(1)}, bf16[2,256,128]{2,1,0:T(8,128)(2,1)S(1)}, u32[]{:S(2)}, u32[]{:S(2)}) %collective-permute-start.5) | collective-permute-done | bytes 131104 | tf_op jit(solution)/shard_map/ppermute | solution.py:257
  17.1 3.1 %window_pairs.1 = (s16[2,22,16,128]{3,2,1,0:T(8,128)(2,1)S(1)}, s16[2,22,16,128]{3,2,1,0:T(8,128)(2,1)S(1)}, s16[2,22,16,128]{3,2,1,0:T(8,128)(2,1)S(1)}, s16[2,22,16,128]{3,2,1,0:T(8,128)(2,1)S(1)}) custom-call(s32[4]{0:T(128)} %offs_hbm_ref.1, s32[1]{0:T(128)} %bitcast.where_ref.core_ref, bf16[2,256,128]{2,1,0:T(8,128)(2,1)S(1)} %collective-permute-done.refs_0_, ...), custom_call_target="tpu_custom_call" | custom-call | tf_op jit(solution)/shard_map/window_pairs/pallas_call | solution.py:368
  20.8 0.9 %collective-permute-done.7.far_ref = s16[2,22,16,128]{3,2,1,0:T(8,128)(2,1)S(1)} collective-permute-done((s16[2,22,16,128]{3,2,1,0:T(8,128)(2,1)S(1)}, s16[2,22,16,128]{3,2,1,0:T(8,128)(2,1)S(1)}, u32[]{:S(2)}, u32[]{:S(2)}) %collective-permute-start.7) | collective-permute-done | bytes 180256 | tf_op jit(solution)/shard_map/ppermute | solution.py:257
  21.8 1.6 %collective-permute-start.8 = (s16[22,16,128]{2,1,0:T(8,128)(2,1)S(1)}, s16[22,16,128]{2,1,0:T(8,128)(2,1)S(1)}, u32[]{:S(2)}, u32[]{:S(2)}) collective-permute-start(s16[22,16,128]{2,1,0:T(8,128)(2,1)S(1)} %get-tuple-element.35), channel_id=1, source_target_pairs={{0,16},{1,17},{2,18},{3,19},{4,12},{5,13},{6,14},{7,15},{8,24},{9,... | collective-permute-start | bytes 270344 | tf_op jit(solution)/shard_map/ppermute | solution.py:257
  23.4 1.6 %collective-permute-start.9 = (s16[22,16,128]{2,1,0:T(8,128)(2,1)S(1)}, s16[22,16,128]{2,1,0:T(8,128)(2,1)S(1)}, u32[]{:S(2)}, u32[]{:S(2)}) collective-permute-start(s16[22,16,128]{2,1,0:T(8,128)(2,1)S(1)} %get-tuple-element.36), channel_id=1, source_target_pairs={{0,8},{1,9},{2,10},{3,11},{4,20},{5,21},{6,22},{7,23},{8,0},{9,1},... | collective-permute-start | bytes 270344 | tf_op jit(solution)/shard_map/ppermute | solution.py:257
  25.6 1.5 %collective-permute-done.8.refs_0_ = s16[22,16,128]{2,1,0:T(8,128)(2,1)S(1)} collective-permute-done((s16[22,16,128]{2,1,0:T(8,128)(2,1)S(1)}, s16[22,16,128]{2,1,0:T(8,128)(2,1)S(1)}, u32[]{:S(2)}, u32[]{:S(2)}) %collective-permute-start.8) | collective-permute-done | bytes 90144 | tf_op jit(solution)/shard_map/ppermute | solution.py:257
  27.1 1.5 %collective-permute-done.9.refs_1_ = s16[22,16,128]{2,1,0:T(8,128)(2,1)S(1)} collective-permute-done((s16[22,16,128]{2,1,0:T(8,128)(2,1)S(1)}, s16[22,16,128]{2,1,0:T(8,128)(2,1)S(1)}, u32[]{:S(2)}, u32[]{:S(2)}) %collective-permute-start.9) | collective-permute-done | bytes 90144 | tf_op jit(solution)/shard_map/ppermute | solution.py:257
  28.6 1.9 %collective-permute-done.11.refs_2_ = s16[22,16,128]{2,1,0:T(8,128)(2,1)S(1)} collective-permute-done((s16[22,16,128]{2,1,0:T(8,128)(2,1)S(1)}, s16[22,16,128]{2,1,0:T(8,128)(2,1)S(1)}, u32[]{:S(2)}, u32[]{:S(2)}) %collective-permute-start.11) | collective-permute-done | bytes 90144 | tf_op jit(solution)/shard_map/ppermute | solution.py:257
  30.7 1.6 %collective-permute-start.12 = (s16[7,16,128]{2,1,0:T(8,128)(2,1)S(1)}, s16[7,16,128]{2,1,0:T(8,128)(2,1)S(1)}, u32[]{:S(2)}, u32[]{:S(2)}) collective-permute-start(s16[7,16,128]{2,1,0:T(8,128)(2,1)S(1)} %get-tuple-element.41), channel_id=1, source_target_pairs={{0,1},{1,0},{2,3},{3,2},{4,5},{5,4},{6,7},{7,6},{8,9},{9,8},{10,11... | collective-permute-start | bytes 86024 | tf_op jit(solution)/shard_map/ppermute | solution.py:257
  32.4 2.6 %collective-permute-start.13 = (s16[7,16,128]{2,1,0:T(8,128)(2,1)S(1)}, s16[7,16,128]{2,1,0:T(8,128)(2,1)S(1)}, u32[]{:S(2)}, u32[]{:S(2)}) collective-permute-start(s16[7,16,128]{2,1,0:T(8,128)(2,1)S(1)} %get-tuple-element.42), channel_id=1, source_target_pairs={{0,2},{1,3},{2,0},{3,1},{4,6},{5,7},{6,4},{7,5},{8,10},{9,11},{10,... | collective-permute-start | bytes 86024 | tf_op jit(solution)/shard_map/ppermute | solution.py:257
  35.2 2.5 %collective-permute-done.13.refs_1_ = s16[7,16,128]{2,1,0:T(8,128)(2,1)S(1)} collective-permute-done((s16[7,16,128]{2,1,0:T(8,128)(2,1)S(1)}, s16[7,16,128]{2,1,0:T(8,128)(2,1)S(1)}, u32[]{:S(2)}, u32[]{:S(2)}) %collective-permute-start.13) | collective-permute-done | bytes 28704 | tf_op jit(solution)/shard_map/ppermute | solution.py:257
  37.6 3.0 %collective-permute-done.14.refs_2_ = s16[7,16,128]{2,1,0:T(8,128)(2,1)S(1)} collective-permute-done((s16[7,16,128]{2,1,0:T(8,128)(2,1)S(1)}, s16[7,16,128]{2,1,0:T(8,128)(2,1)S(1)}, u32[]{:S(2)}, u32[]{:S(2)}) %collective-permute-start.14) | collective-permute-done | bytes 28704 | tf_op jit(solution)/shard_map/ppermute | solution.py:257
  40.8 9.2 %all_to_all.5 = f32[32,4,128]{2,1,0:T(4,128)S(1)} all-to-all(f32[32,4,128]{2,1,0:T(4,128)S(1)} %bitcast.5), channel_id=1, replica_groups=mesh['chan'=8,'tm'=4] {'chan','tm'}, dimensions={0} | all-to-all | bytes 131072 | tf_op jit(solution)/shard_map/all_to_all | solution.py:411
  50.0 0.8 %place_lags.1 = f32[16,4,256]{2,1,0:T(4,128)} custom-call(f32[8,4,4,128]{3,2,1,0:T(4,128)S(1)} %bitcast.4), custom_call_target="tpu_custom_call" | custom-call | tf_op jit(solution)/shard_map/place_lags/pallas_call | solution.py:412
  (19 shorter events, 1.9 us)
Async XLA Ops:
  0.0 17.1 %copy-start = (bf16[16,2,8,16,128]{4,3,2,1,0:T(8,128)(2,1)S(1)}, bf16[16,2,8,16,128]{4,3,2,1,0:T(8,128)(2,1)}, u32[]{:S(2)}) copy-start(bf16[16,2,8,16,128]{4,3,2,1,0:T(8,128)(2,1)} %constant.11.clone.refs_9_) | copy-start | bytes 3145732
  1.1 8.5 %collective-permute-start = (bf16[2,256,128]{2,1,0:T(8,128)(2,1)S(1)}, bf16[2,256,128]{2,1,0:T(8,128)(2,1)S(1)}, u32[]{:S(2)}, u32[]{:S(2)}) collective-permute-start(bf16[2,256,128]{2,1,0:T(8,128)(2,1)S(1)} %get-tuple-element.25), channel_id=1, source_target_pairs={{0,24},{1,25},{2,26},{3,27},{4,28},{5,29},{6,30},{7,31},{8,16},{9,... | collective-permute-start | bytes 393224 | tf_op jit(solution)/shard_map/ppermute | solution.py:257
  5.0 6.7 %collective-permute-start.1 = (bf16[2,256,128]{2,1,0:T(8,128)(2,1)S(1)}, bf16[2,256,128]{2,1,0:T(8,128)(2,1)S(1)}, u32[]{:S(2)}, u32[]{:S(2)}) collective-permute-start(bf16[2,256,128]{2,1,0:T(8,128)(2,1)S(1)} %get-tuple-element.26), channel_id=1, source_target_pairs={{0,28},{1,29},{2,30},{3,31},{4,24},{5,25},{6,26},{7,27},{8,20},{9,... | collective-permute-start | bytes 393224 | tf_op jit(solution)/shard_map/ppermute | solution.py:257
  6.3 8.9 %collective-permute-start.2 = (bf16[2,256,128]{2,1,0:T(8,128)(2,1)S(1)}, bf16[2,256,128]{2,1,0:T(8,128)(2,1)S(1)}, u32[]{:S(2)}, u32[]{:S(2)}) collective-permute-start(bf16[2,256,128]{2,1,0:T(8,128)(2,1)S(1)} %get-tuple-element.27), channel_id=1, source_target_pairs={{0,8},{1,9},{2,10},{3,11},{4,12},{5,13},{6,14},{7,15},{8,0},{9,1},... | collective-permute-start | bytes 393224 | tf_op jit(solution)/shard_map/ppermute | solution.py:257
  7.5 7.7 %collective-permute-start.3 = (bf16[2,256,128]{2,1,0:T(8,128)(2,1)S(1)}, bf16[2,256,128]{2,1,0:T(8,128)(2,1)S(1)}, u32[]{:S(2)}, u32[]{:S(2)}) collective-permute-start(bf16[2,256,128]{2,1,0:T(8,128)(2,1)S(1)} %get-tuple-element.28), channel_id=1, source_target_pairs={{0,16},{1,17},{2,18},{3,19},{4,20},{5,21},{6,22},{7,23},{8,24},{9,... | collective-permute-start | bytes 393224 | tf_op jit(solution)/shard_map/ppermute | solution.py:257
  9.0 7.4 %collective-permute-start.4 = (bf16[2,256,128]{2,1,0:T(8,128)(2,1)S(1)}, bf16[2,256,128]{2,1,0:T(8,128)(2,1)S(1)}, u32[]{:S(2)}, u32[]{:S(2)}) collective-permute-start(bf16[2,256,128]{2,1,0:T(8,128)(2,1)S(1)} %get-tuple-element.29), channel_id=1, source_target_pairs={{0,12},{1,13},{2,14},{3,15},{4,8},{5,9},{6,10},{7,11},{8,4},{9,5},... | collective-permute-start | bytes 393224 | tf_op jit(solution)/shard_map/ppermute | solution.py:257
  9.6 7.5 %collective-permute-start.5 = (bf16[2,256,128]{2,1,0:T(8,128)(2,1)S(1)}, bf16[2,256,128]{2,1,0:T(8,128)(2,1)S(1)}, u32[]{:S(2)}, u32[]{:S(2)}) collective-permute-start(bf16[2,256,128]{2,1,0:T(8,128)(2,1)S(1)} %get-tuple-element.30), channel_id=1, source_target_pairs={{0,20},{1,21},{2,22},{3,23},{4,16},{5,17},{6,18},{7,19},{8,28},{9,... | collective-permute-start | bytes 393224 | tf_op jit(solution)/shard_map/ppermute | solution.py:257
  11.8 5.3 %collective-permute-start.6 = (bf16[2,256,128]{2,1,0:T(8,128)(2,1)S(1)}, bf16[2,256,128]{2,1,0:T(8,128)(2,1)S(1)}, u32[]{:S(2)}, u32[]{:S(2)}) collective-permute-start(bf16[2,256,128]{2,1,0:T(8,128)(2,1)S(1)} %get-tuple-element.31), channel_id=1, source_target_pairs={{0,4},{1,5},{2,6},{3,7},{4,0},{5,1},{6,2},{7,3},{8,12},{9,13},{10,... | collective-permute-start | bytes 393224 | tf_op jit(solution)/shard_map/ppermute | solution.py:257
  11.8 5.3 %copy-start.1 = (s32[8,128]{1,0:T(8,128)S(1)}, s32[8,128]{1,0:T(8,128)}, u32[]{:S(2)}) copy-start(s32[8,128]{1,0:T(8,128)} %refs_8_.1) | copy-start | bytes 12292
  20.2 1.5 %collective-permute-start.7 = (s16[2,22,16,128]{3,2,1,0:T(8,128)(2,1)S(1)}, s16[2,22,16,128]{3,2,1,0:T(8,128)(2,1)S(1)}, u32[]{:S(2)}, u32[]{:S(2)}) collective-permute-start(s16[2,22,16,128]{3,2,1,0:T(8,128)(2,1)S(1)} %get-tuple-element.34), channel_id=1, source_target_pairs={{0,4},{1,5},{2,6},{3,7},{4,0},{5,1},{6,2},{7,3},{8,12},{9,13},{10,... | collective-permute-start | bytes 540680 | tf_op jit(solution)/shard_map/ppermute | solution.py:257
  20.4 4.6 %collective-permute-start.10 = (s16[2,22,16,128]{3,2,1,0:T(8,128)(2,1)S(1)}, s16[2,22,16,128]{3,2,1,0:T(8,128)(2,1)S(1)}, u32[]{:S(2)}, u32[]{:S(2)}) collective-permute-start(s16[2,22,16,128]{3,2,1,0:T(8,128)(2,1)S(1)} %get-tuple-element.38), channel_id=1, source_target_pairs={{0,4},{1,5},{2,6},{3,7},{4,0},{5,1},{6,2},{7,3},{8,12},{9,13},{10,... | collective-permute-start | bytes 540680 | tf_op jit(solution)/shard_map/ppermute | solution.py:257
  21.8 5.3 %collective-permute-start.8 = (s16[22,16,128]{2,1,0:T(8,128)(2,1)S(1)}, s16[22,16,128]{2,1,0:T(8,128)(2,1)S(1)}, u32[]{:S(2)}, u32[]{:S(2)}) collective-permute-start(s16[22,16,128]{2,1,0:T(8,128)(2,1)S(1)} %get-tuple-element.35), channel_id=1, source_target_pairs={{0,16},{1,17},{2,18},{3,19},{4,12},{5,13},{6,14},{7,15},{8,24},{9,... | collective-permute-start | bytes 270344 | tf_op jit(solution)/shard_map/ppermute | solution.py:257
  23.4 5.2 %collective-permute-start.9 = (s16[22,16,128]{2,1,0:T(8,128)(2,1)S(1)}, s16[22,16,128]{2,1,0:T(8,128)(2,1)S(1)}, u32[]{:S(2)}, u32[]{:S(2)}) collective-permute-start(s16[22,16,128]{2,1,0:T(8,128)(2,1)S(1)} %get-tuple-element.36), channel_id=1, source_target_pairs={{0,8},{1,9},{2,10},{3,11},{4,20},{5,21},{6,22},{7,23},{8,0},{9,1},... | collective-permute-start | bytes 270344 | tf_op jit(solution)/shard_map/ppermute | solution.py:257
  25.1 5.5 %collective-permute-start.11 = (s16[22,16,128]{2,1,0:T(8,128)(2,1)S(1)}, s16[22,16,128]{2,1,0:T(8,128)(2,1)S(1)}, u32[]{:S(2)}, u32[]{:S(2)}) collective-permute-start(s16[22,16,128]{2,1,0:T(8,128)(2,1)S(1)} %get-tuple-element.39), channel_id=1, source_target_pairs={{0,24},{1,25},{2,26},{3,27},{4,28},{5,29},{6,30},{7,31},{8,16},{9,... | collective-permute-start | bytes 270344 | tf_op jit(solution)/shard_map/ppermute | solution.py:257
  30.7 4.5 %collective-permute-start.12 = (s16[7,16,128]{2,1,0:T(8,128)(2,1)S(1)}, s16[7,16,128]{2,1,0:T(8,128)(2,1)S(1)}, u32[]{:S(2)}, u32[]{:S(2)}) collective-permute-start(s16[7,16,128]{2,1,0:T(8,128)(2,1)S(1)} %get-tuple-element.41), channel_id=1, source_target_pairs={{0,1},{1,0},{2,3},{3,2},{4,5},{5,4},{6,7},{7,6},{8,9},{9,8},{10,11... | collective-permute-start | bytes 86024 | tf_op jit(solution)/shard_map/ppermute | solution.py:257
  32.4 5.3 %collective-permute-start.13 = (s16[7,16,128]{2,1,0:T(8,128)(2,1)S(1)}, s16[7,16,128]{2,1,0:T(8,128)(2,1)S(1)}, u32[]{:S(2)}, u32[]{:S(2)}) collective-permute-start(s16[7,16,128]{2,1,0:T(8,128)(2,1)S(1)} %get-tuple-element.42), channel_id=1, source_target_pairs={{0,2},{1,3},{2,0},{3,1},{4,6},{5,7},{6,4},{7,5},{8,10},{9,11},{10,... | collective-permute-start | bytes 86024 | tf_op jit(solution)/shard_map/ppermute | solution.py:257
  34.9 5.7 %collective-permute-start.14 = (s16[7,16,128]{2,1,0:T(8,128)(2,1)S(1)}, s16[7,16,128]{2,1,0:T(8,128)(2,1)S(1)}, u32[]{:S(2)}, u32[]{:S(2)}) collective-permute-start(s16[7,16,128]{2,1,0:T(8,128)(2,1)S(1)} %get-tuple-element.43), channel_id=1, source_target_pairs={{0,3},{1,2},{2,1},{3,0},{4,7},{5,6},{6,5},{7,4},{8,11},{9,10},{10,... | collective-permute-start | bytes 86024 | tf_op jit(solution)/shard_map/ppermute | solution.py:257

commit v31 on v26

--- a/solution.py
+++ b/solution.py
@@ -122,8 +122,11 @@
             cross_ref[number, 1, row : row + step, :] = imag.astype(jnp.bfloat16)
 
     for number, turn in enumerate(turns):
-        both = jnp.concatenate([cross_ref[number, 0], cross_ref[number, 1]], axis=1)
-        sums = jnp.dot(table, both, preferred_element_type=jnp.float32)
+        if number % 2 == 0:
+            taken = range(number, min(number + 2, offset_count))
+            wide = jnp.concatenate([cross_ref[each, part] for each in taken for part in range(2)], axis=1)
+            pair_sums = jnp.dot(table, wide, preferred_element_type=jnp.float32)
+        sums = pair_sums[:, number % 2 * 2 * chans : (number % 2 + 1) * 2 * chans]
         cos_real, sin_real = sums[:half, :chans], sums[half:, :chans]
         cos_imag, sin_imag = sums[:half, chans:], sums[half:, chans:]
         corr = (

time: 50.5 us -> 50.5 us (level)
  no operation moved by 1% of the time
where the time goes in v31:
time: 50.5 us; the launch traced here: 50.3 us
  waiting for transfers between devices  17.6 us (35%)
  starting transfers between devices  15.8 us (31%)
  blocking collectives  10.2 us (20%)
  Pallas kernels  6.77 us (13%)
    ppermute x14, waiting for transfers between devices, exchange(): lax.ppermute(piece, ('chan', 'tm'), pairs)  17.6 us
    ppermute x14, starting transfers between devices, exchange(): lax.ppermute(piece, ('chan', 'tm'), pairs)  15.8 us
    all_to_all x1, blocking collectives, window_shards(): lax.all_to_all(pieces.reshape(shape), ('chan', 'tm'), 0, 0, tiled=True)  10.2 us
    pallas_call x1, Pallas kernels, window_shards(): pl.pallas_call(functools.partial(window_kernel, chan_order), out_shape=[j...  3.14 us
    pallas_call x2, Pallas kernels, window_shards(): pl.pallas_call(functools.partial(split_kernel, part), out_shape=[jax.Shap...  2.32 us
  transfers between devices with their start and end apart: 14, of which 10 were waited for; matrix products, arithmetic and copies ran while one was open for 0% of the time, Pallas kernels for 2%

profile of v31, /device:TPU:0, one launch (start us, length us, event | category | flops | bytes accessed | tf_op | source)
XLA Modules:
  0.0 50.3 jit_solution(7061822766280543138)
XLA Ops:
  0.0 1.1 %split_windows.2 = (bf16[2,256,128]{2,1,0:T(8,128)(2,1)S(1)}, bf16[2,256,128]{2,1,0:T(8,128)(2,1)S(1)}) custom-call(bf16[2,8,256,128]{3,2,1,0:T(8,128)(2,1)} %spec_ref.3), custom_call_target="tpu_custom_call" | custom-call | tf_op jit(solution)/shard_map/split_windows/pallas_call | solution.py:358
  1.1 4.0 %collective-permute-start = (bf16[2,256,128]{2,1,0:T(8,128)(2,1)S(1)}, bf16[2,256,128]{2,1,0:T(8,128)(2,1)S(1)}, u32[]{:S(2)}, u32[]{:S(2)}) collective-permute-start(bf16[2,256,128]{2,1,0:T(8,128)(2,1)S(1)} %get-tuple-element.23), channel_id=1, source_target_pairs={{0,24},{1,25},{2,26},{3,27},{4,28},{5,29},{6,30},{7,31},{8,16},{9,... | collective-permute-start | bytes 393224 | tf_op jit(solution)/shard_map/ppermute | solution.py:258
  5.0 1.3 %split_windows.3 = (bf16[2,256,128]{2,1,0:T(8,128)(2,1)S(1)}, bf16[2,256,128]{2,1,0:T(8,128)(2,1)S(1)}, bf16[2,256,128]{2,1,0:T(8,128)(2,1)S(1)}, bf16[2,256,128...) custom-call(bf16[2,8,256,128]{3,2,1,0:T(8,128)(2,1)} %spec_ref.3), custom_call_target="tpu_custom_call" | custom-call | tf_op jit(solution)/shard_map/split_windows/pallas_call | solution.py:358
  6.3 1.2 %collective-permute-start.2 = (bf16[2,256,128]{2,1,0:T(8,128)(2,1)S(1)}, bf16[2,256,128]{2,1,0:T(8,128)(2,1)S(1)}, u32[]{:S(2)}, u32[]{:S(2)}) collective-permute-start(bf16[2,256,128]{2,1,0:T(8,128)(2,1)S(1)} %get-tuple-element.25), channel_id=1, source_target_pairs={{0,8},{1,9},{2,10},{3,11},{4,12},{5,13},{6,14},{7,15},{8,0},{9,1},... | collective-permute-start | bytes 393224 | tf_op jit(solution)/shard_map/ppermute | solution.py:258
  7.5 1.5 %collective-permute-start.3 = (bf16[2,256,128]{2,1,0:T(8,128)(2,1)S(1)}, bf16[2,256,128]{2,1,0:T(8,128)(2,1)S(1)}, u32[]{:S(2)}, u32[]{:S(2)}) collective-permute-start(bf16[2,256,128]{2,1,0:T(8,128)(2,1)S(1)} %get-tuple-element.26), channel_id=1, source_target_pairs={{0,16},{1,17},{2,18},{3,19},{4,20},{5,21},{6,22},{7,23},{8,24},{9,... | collective-permute-start | bytes 393224 | tf_op jit(solution)/shard_map/ppermute | solution.py:258
  9.0 0.6 %collective-permute-start.4 = (bf16[2,256,128]{2,1,0:T(8,128)(2,1)S(1)}, bf16[2,256,128]{2,1,0:T(8,128)(2,1)S(1)}, u32[]{:S(2)}, u32[]{:S(2)}) collective-permute-start(bf16[2,256,128]{2,1,0:T(8,128)(2,1)S(1)} %get-tuple-element.27), channel_id=1, source_target_pairs={{0,12},{1,13},{2,14},{3,15},{4,8},{5,9},{6,10},{7,11},{8,4},{9,5},... | collective-permute-start | bytes 393224 | tf_op jit(solution)/shard_map/ppermute | solution.py:258
  9.6 0.6 %collective-permute-start.5 = (bf16[2,256,128]{2,1,0:T(8,128)(2,1)S(1)}, bf16[2,256,128]{2,1,0:T(8,128)(2,1)S(1)}, u32[]{:S(2)}, u32[]{:S(2)}) collective-permute-start(bf16[2,256,128]{2,1,0:T(8,128)(2,1)S(1)} %get-tuple-element.28), channel_id=1, source_target_pairs={{0,20},{1,21},{2,22},{3,23},{4,16},{5,17},{6,18},{7,19},{8,28},{9,... | collective-permute-start | bytes 393224 | tf_op jit(solution)/shard_map/ppermute | solution.py:258
  10.1 1.6 %collective-permute-done.1.refs_1_ = bf16[2,256,128]{2,1,0:T(8,128)(2,1)S(1)} collective-permute-done((bf16[2,256,128]{2,1,0:T(8,128)(2,1)S(1)}, bf16[2,256,128]{2,1,0:T(8,128)(2,1)S(1)}, u32[]{:S(2)}, u32[]{:S(2)}) %collective-permute-start.1) | collective-permute-done | bytes 131104 | tf_op jit(solution)/shard_map/ppermute | solution.py:258
  11.8 3.5 %collective-permute-done.2.refs_2_ = bf16[2,256,128]{2,1,0:T(8,128)(2,1)S(1)} collective-permute-done((bf16[2,256,128]{2,1,0:T(8,128)(2,1)S(1)}, bf16[2,256,128]{2,1,0:T(8,128)(2,1)S(1)}, u32[]{:S(2)}, u32[]{:S(2)}) %collective-permute-start.2) | collective-permute-done | bytes 131104 | tf_op jit(solution)/shard_map/ppermute | solution.py:258
  15.2 1.1 %collective-permute-done.4.refs_4_ = bf16[2,256,128]{2,1,0:T(8,128)(2,1)S(1)} collective-permute-done((bf16[2,256,128]{2,1,0:T(8,128)(2,1)S(1)}, bf16[2,256,128]{2,1,0:T(8,128)(2,1)S(1)}, u32[]{:S(2)}, u32[]{:S(2)}) %collective-permute-start.4) | collective-permute-done | bytes 131104 | tf_op jit(solution)/shard_map/ppermute | solution.py:258
  16.4 0.7 %collective-permute-done.5.refs_5_ = bf16[2,256,128]{2,1,0:T(8,128)(2,1)S(1)} collective-permute-done((bf16[2,256,128]{2,1,0:T(8,128)(2,1)S(1)}, bf16[2,256,128]{2,1,0:T(8,128)(2,1)S(1)}, u32[]{:S(2)}, u32[]{:S(2)}) %collective-permute-start.5) | collective-permute-done | bytes 131104 | tf_op jit(solution)/shard_map/ppermute | solution.py:258
  17.1 3.1 %window_pairs.1 = (s16[4,22,16,128]{3,2,1,0:T(8,128)(2,1)S(1)}, s16[4,22,16,128]{3,2,1,0:T(8,128)(2,1)S(1)}) custom-call(s32[4]{0:T(128)} %offs_hbm_ref.1, s32[1]{0:T(128)} %bitcast.where_ref.core_ref, bf16[2,256,128]{2,1,0:T(8,128)(2,1)S(1)} %collective-permute-done.refs_0_, bf16[2,256,128]{2,1,0:T(8,128)(2,1)S(1)} %collective-permute-done.1.refs_1_, ...), custom_call_target="tpu_custom_call" | custom-call | tf_op jit(solution)/shard_map/window_pairs/pallas_call | solution.py:369
  20.4 1.6 %collective-permute-done.7.far_ref = s16[4,22,16,128]{3,2,1,0:T(8,128)(2,1)S(1)} collective-permute-done((s16[4,22,16,128]{3,2,1,0:T(8,128)(2,1)S(1)}, s16[4,22,16,128]{3,2,1,0:T(8,128)(2,1)S(1)}, u32[]{:S(2)}, u32[]{:S(2)}) %collective-permute-start.7) | collective-permute-done | bytes 360480 | tf_op jit(solution)/shard_map/ppermute | solution.py:258
  22.2 1.6 %collective-permute-start.8 = (s16[22,16,128]{2,1,0:T(8,128)(2,1)S(1)}, s16[22,16,128]{2,1,0:T(8,128)(2,1)S(1)}, u32[]{:S(2)}, u32[]{:S(2)}) collective-permute-start(s16[22,16,128]{2,1,0:T(8,128)(2,1)S(1)} %get-tuple-element.33), channel_id=1, source_target_pairs={{0,16},{1,17},{2,18},{3,19},{4,12},{5,13},{6,14},{7,15},{8,24},{9,... | collective-permute-start | bytes 270344 | tf_op jit(solution)/shard_map/ppermute | solution.py:258
  23.7 1.6 %collective-permute-start.9 = (s16[22,16,128]{2,1,0:T(8,128)(2,1)S(1)}, s16[22,16,128]{2,1,0:T(8,128)(2,1)S(1)}, u32[]{:S(2)}, u32[]{:S(2)}) collective-permute-start(s16[22,16,128]{2,1,0:T(8,128)(2,1)S(1)} %get-tuple-element.34), channel_id=1, source_target_pairs={{0,8},{1,9},{2,10},{3,11},{4,20},{5,21},{6,22},{7,23},{8,0},{9,1},... | collective-permute-start | bytes 270344 | tf_op jit(solution)/shard_map/ppermute | solution.py:258
  25.7 1.7 %collective-permute-done.8.refs_0_ = s16[22,16,128]{2,1,0:T(8,128)(2,1)S(1)} collective-permute-done((s16[22,16,128]{2,1,0:T(8,128)(2,1)S(1)}, s16[22,16,128]{2,1,0:T(8,128)(2,1)S(1)}, u32[]{:S(2)}, u32[]{:S(2)}) %collective-permute-start.8) | collective-permute-done | bytes 90144 | tf_op jit(solution)/shard_map/ppermute | solution.py:258
  27.4 1.7 %collective-permute-done.9.refs_1_ = s16[22,16,128]{2,1,0:T(8,128)(2,1)S(1)} collective-permute-done((s16[22,16,128]{2,1,0:T(8,128)(2,1)S(1)}, s16[22,16,128]{2,1,0:T(8,128)(2,1)S(1)}, u32[]{:S(2)}, u32[]{:S(2)}) %collective-permute-start.9) | collective-permute-done | bytes 90144 | tf_op jit(solution)/shard_map/ppermute | solution.py:258
  29.2 1.6 %collective-permute-done.10.refs_2_ = s16[22,16,128]{2,1,0:T(8,128)(2,1)S(1)} collective-permute-done((s16[22,16,128]{2,1,0:T(8,128)(2,1)S(1)}, s16[22,16,128]{2,1,0:T(8,128)(2,1)S(1)}, u32[]{:S(2)}, u32[]{:S(2)}) %collective-permute-start.10) | collective-permute-done | bytes 90144 | tf_op jit(solution)/shard_map/ppermute | solution.py:258
  30.9 2.7 %collective-permute-start.11 = (s16[7,16,128]{2,1,0:T(8,128)(2,1)S(1)}, s16[7,16,128]{2,1,0:T(8,128)(2,1)S(1)}, u32[]{:S(2)}, u32[]{:S(2)}) collective-permute-start(s16[7,16,128]{2,1,0:T(8,128)(2,1)S(1)} %get-tuple-element.37), channel_id=1, source_target_pairs={{0,2},{1,3},{2,0},{3,1},{4,7},{5,6},{6,5},{7,4},{8,10},{9,11},{10,... | collective-permute-start | bytes 86024 | tf_op jit(solution)/shard_map/ppermute | solution.py:258
  33.5 1.3 %collective-permute-start.12 = (s16[7,16,128]{2,1,0:T(8,128)(2,1)S(1)}, s16[7,16,128]{2,1,0:T(8,128)(2,1)S(1)}, u32[]{:S(2)}, u32[]{:S(2)}) collective-permute-start(s16[7,16,128]{2,1,0:T(8,128)(2,1)S(1)} %get-tuple-element.38), channel_id=1, source_target_pairs={{0,3},{1,2},{2,1},{3,0},{4,5},{5,4},{6,7},{7,6},{8,11},{9,10},{10,... | collective-permute-start | bytes 86024 | tf_op jit(solution)/shard_map/ppermute | solution.py:258
  35.1 0.7 %collective-permute-done.11.refs_0_ = s16[7,16,128]{2,1,0:T(8,128)(2,1)S(1)} collective-permute-done((s16[7,16,128]{2,1,0:T(8,128)(2,1)S(1)}, s16[7,16,128]{2,1,0:T(8,128)(2,1)S(1)}, u32[]{:S(2)}, u32[]{:S(2)}) %collective-permute-start.11) | collective-permute-done | bytes 28704 | tf_op jit(solution)/shard_map/ppermute | solution.py:258
  35.8 3.4 %collective-permute-done.12.refs_1_ = s16[7,16,128]{2,1,0:T(8,128)(2,1)S(1)} collective-permute-done((s16[7,16,128]{2,1,0:T(8,128)(2,1)S(1)}, s16[7,16,128]{2,1,0:T(8,128)(2,1)S(1)}, u32[]{:S(2)}, u32[]{:S(2)}) %collective-permute-start.12) | collective-permute-done | bytes 28704 | tf_op jit(solution)/shard_map/ppermute | solution.py:258
  39.4 10.2 %all_to_all.5 = f32[32,4,128]{2,1,0:T(4,128)S(1)} all-to-all(f32[32,4,128]{2,1,0:T(4,128)S(1)} %bitcast.5), channel_id=1, replica_groups=mesh['chan'=8,'tm'=4] {'chan','tm'}, dimensions={0} | all-to-all | bytes 131072 | tf_op jit(solution)/shard_map/all_to_all | solution.py:410
  49.6 0.8 %place_lags.1 = f32[16,4,256]{2,1,0:T(4,128)} custom-call(f32[8,4,4,128]{3,2,1,0:T(4,128)S(1)} %bitcast.4), custom_call_target="tpu_custom_call" | custom-call | tf_op jit(solution)/shard_map/place_lags/pallas_call | solution.py:411
  (16 shorter events, 1.4 us)
Async XLA Ops:
  0.0 17.1 %copy-start = (bf16[16,2,8,16,128]{4,3,2,1,0:T(8,128)(2,1)S(1)}, bf16[16,2,8,16,128]{4,3,2,1,0:T(8,128)(2,1)}, u32[]{:S(2)}) copy-start(bf16[16,2,8,16,128]{4,3,2,1,0:T(8,128)(2,1)} %constant.11.clone.refs_9_) | copy-start | bytes 3145732
  1.1 8.5 %collective-permute-start = (bf16[2,256,128]{2,1,0:T(8,128)(2,1)S(1)}, bf16[2,256,128]{2,1,0:T(8,128)(2,1)S(1)}, u32[]{:S(2)}, u32[]{:S(2)}) collective-permute-start(bf16[2,256,128]{2,1,0:T(8,128)(2,1)S(1)} %get-tuple-element.23), channel_id=1, source_target_pairs={{0,24},{1,25},{2,26},{3,27},{4,28},{5,29},{6,30},{7,31},{8,16},{9,... | collective-permute-start | bytes 393224 | tf_op jit(solution)/shard_map/ppermute | solution.py:258
  5.0 6.7 %collective-permute-start.1 = (bf16[2,256,128]{2,1,0:T(8,128)(2,1)S(1)}, bf16[2,256,128]{2,1,0:T(8,128)(2,1)S(1)}, u32[]{:S(2)}, u32[]{:S(2)}) collective-permute-start(bf16[2,256,128]{2,1,0:T(8,128)(2,1)S(1)} %get-tuple-element.24), channel_id=1, source_target_pairs={{0,28},{1,29},{2,30},{3,31},{4,24},{5,25},{6,26},{7,27},{8,20},{9,... | collective-permute-start | bytes 393224 | tf_op jit(solution)/shard_map/ppermute | solution.py:258
  6.3 8.9 %collective-permute-start.2 = (bf16[2,256,128]{2,1,0:T(8,128)(2,1)S(1)}, bf16[2,256,128]{2,1,0:T(8,128)(2,1)S(1)}, u32[]{:S(2)}, u32[]{:S(2)}) collective-permute-start(bf16[2,256,128]{2,1,0:T(8,128)(2,1)S(1)} %get-tuple-element.25), channel_id=1, source_target_pairs={{0,8},{1,9},{2,10},{3,11},{4,12},{5,13},{6,14},{7,15},{8,0},{9,1},... | collective-permute-start | bytes 393224 | tf_op jit(solution)/shard_map/ppermute | solution.py:258
  7.5 7.7 %collective-permute-start.3 = (bf16[2,256,128]{2,1,0:T(8,128)(2,1)S(1)}, bf16[2,256,128]{2,1,0:T(8,128)(2,1)S(1)}, u32[]{:S(2)}, u32[]{:S(2)}) collective-permute-start(bf16[2,256,128]{2,1,0:T(8,128)(2,1)S(1)} %get-tuple-element.26), channel_id=1, source_target_pairs={{0,16},{1,17},{2,18},{3,19},{4,20},{5,21},{6,22},{7,23},{8,24},{9,... | collective-permute-start | bytes 393224 | tf_op jit(solution)/shard_map/ppermute | solution.py:258
  9.0 7.4 %collective-permute-start.4 = (bf16[2,256,128]{2,1,0:T(8,128)(2,1)S(1)}, bf16[2,256,128]{2,1,0:T(8,128)(2,1)S(1)}, u32[]{:S(2)}, u32[]{:S(2)}) collective-permute-start(bf16[2,256,128]{2,1,0:T(8,128)(2,1)S(1)} %get-tuple-element.27), channel_id=1, source_target_pairs={{0,12},{1,13},{2,14},{3,15},{4,8},{5,9},{6,10},{7,11},{8,4},{9,5},... | collective-permute-start | bytes 393224 | tf_op jit(solution)/shard_map/ppermute | solution.py:258
  9.6 7.5 %collective-permute-start.5 = (bf16[2,256,128]{2,1,0:T(8,128)(2,1)S(1)}, bf16[2,256,128]{2,1,0:T(8,128)(2,1)S(1)}, u32[]{:S(2)}, u32[]{:S(2)}) collective-permute-start(bf16[2,256,128]{2,1,0:T(8,128)(2,1)S(1)} %get-tuple-element.28), channel_id=1, source_target_pairs={{0,20},{1,21},{2,22},{3,23},{4,16},{5,17},{6,18},{7,19},{8,28},{9,... | collective-permute-start | bytes 393224 | tf_op jit(solution)/shard_map/ppermute | solution.py:258
  11.8 5.3 %collective-permute-start.6 = (bf16[2,256,128]{2,1,0:T(8,128)(2,1)S(1)}, bf16[2,256,128]{2,1,0:T(8,128)(2,1)S(1)}, u32[]{:S(2)}, u32[]{:S(2)}) collective-permute-start(bf16[2,256,128]{2,1,0:T(8,128)(2,1)S(1)} %get-tuple-element.29), channel_id=1, source_target_pairs={{0,4},{1,5},{2,6},{3,7},{4,0},{5,1},{6,2},{7,3},{8,12},{9,13},{10,... | collective-permute-start | bytes 393224 | tf_op jit(solution)/shard_map/ppermute | solution.py:258
  11.8 5.3 %copy-start.1 = (s32[8,128]{1,0:T(8,128)S(1)}, s32[8,128]{1,0:T(8,128)}, u32[]{:S(2)}) copy-start(s32[8,128]{1,0:T(8,128)} %refs_8_.1) | copy-start | bytes 12292
  20.2 1.7 %collective-permute-start.7 = (s16[4,22,16,128]{3,2,1,0:T(8,128)(2,1)S(1)}, s16[4,22,16,128]{3,2,1,0:T(8,128)(2,1)S(1)}, u32[]{:S(2)}, u32[]{:S(2)}) collective-permute-start(s16[4,22,16,128]{3,2,1,0:T(8,128)(2,1)S(1)} %get-tuple-element.32), channel_id=1, source_target_pairs={{0,4},{1,5},{2,6},{3,7},{4,0},{5,1},{6,2},{7,3},{8,12},{9,13},{10,... | collective-permute-start | bytes 1081352 | tf_op jit(solution)/shard_map/ppermute | solution.py:258
  22.2 5.3 %collective-permute-start.8 = (s16[22,16,128]{2,1,0:T(8,128)(2,1)S(1)}, s16[22,16,128]{2,1,0:T(8,128)(2,1)S(1)}, u32[]{:S(2)}, u32[]{:S(2)}) collective-permute-start(s16[22,16,128]{2,1,0:T(8,128)(2,1)S(1)} %get-tuple-element.33), channel_id=1, source_target_pairs={{0,16},{1,17},{2,18},{3,19},{4,12},{5,13},{6,14},{7,15},{8,24},{9,... | collective-permute-start | bytes 270344 | tf_op jit(solution)/shard_map/ppermute | solution.py:258
  23.7 5.4 %collective-permute-start.9 = (s16[22,16,128]{2,1,0:T(8,128)(2,1)S(1)}, s16[22,16,128]{2,1,0:T(8,128)(2,1)S(1)}, u32[]{:S(2)}, u32[]{:S(2)}) collective-permute-start(s16[22,16,128]{2,1,0:T(8,128)(2,1)S(1)} %get-tuple-element.34), channel_id=1, source_target_pairs={{0,8},{1,9},{2,10},{3,11},{4,20},{5,21},{6,22},{7,23},{8,0},{9,1},... | collective-permute-start | bytes 270344 | tf_op jit(solution)/shard_map/ppermute | solution.py:258
  25.3 5.4 %collective-permute-start.10 = (s16[22,16,128]{2,1,0:T(8,128)(2,1)S(1)}, s16[22,16,128]{2,1,0:T(8,128)(2,1)S(1)}, u32[]{:S(2)}, u32[]{:S(2)}) collective-permute-start(s16[22,16,128]{2,1,0:T(8,128)(2,1)S(1)} %get-tuple-element.35), channel_id=1, source_target_pairs={{0,24},{1,25},{2,26},{3,27},{4,28},{5,29},{6,30},{7,31},{8,16},{9,... | collective-permute-start | bytes 270344 | tf_op jit(solution)/shard_map/ppermute | solution.py:258
  30.9 4.9 %collective-permute-start.11 = (s16[7,16,128]{2,1,0:T(8,128)(2,1)S(1)}, s16[7,16,128]{2,1,0:T(8,128)(2,1)S(1)}, u32[]{:S(2)}, u32[]{:S(2)}) collective-permute-start(s16[7,16,128]{2,1,0:T(8,128)(2,1)S(1)} %get-tuple-element.37), channel_id=1, source_target_pairs={{0,2},{1,3},{2,0},{3,1},{4,7},{5,6},{6,5},{7,4},{8,10},{9,11},{10,... | collective-permute-start | bytes 86024 | tf_op jit(solution)/shard_map/ppermute | solution.py:258
  33.5 5.7 %collective-permute-start.12 = (s16[7,16,128]{2,1,0:T(8,128)(2,1)S(1)}, s16[7,16,128]{2,1,0:T(8,128)(2,1)S(1)}, u32[]{:S(2)}, u32[]{:S(2)}) collective-permute-start(s16[7,16,128]{2,1,0:T(8,128)(2,1)S(1)} %get-tuple-element.38), channel_id=1, source_target_pairs={{0,3},{1,2},{2,1},{3,0},{4,5},{5,4},{6,7},{7,6},{8,11},{9,10},{10,... | collective-permute-start | bytes 86024 | tf_op jit(solution)/shard_map/ppermute | solution.py:258
  34.9 4.3 %collective-permute-start.13 = (s16[7,16,128]{2,1,0:T(8,128)(2,1)S(1)}, s16[7,16,128]{2,1,0:T(8,128)(2,1)S(1)}, u32[]{:S(2)}, u32[]{:S(2)}) collective-permute-start(s16[7,16,128]{2,1,0:T(8,128)(2,1)S(1)} %get-tuple-element.39), channel_id=1, source_target_pairs={{0,1},{1,0},{2,3},{3,2},{4,6},{5,7},{6,4},{7,5},{8,9},{9,8},{10,11... | collective-permute-start | bytes 86024 | tf_op jit(solution)/shard_map/ppermute | solution.py:258

commit v32 on v31

--- a/solution.py
+++ b/solution.py
@@ -44,6 +44,11 @@
     return np.concatenate([np.cos(angles), np.sin(angles)]).astype(jnp.bfloat16)
 
 
+def magnitude_of(real, imag):
+    square = real * real + imag * imag
+    return square * lax.rsqrt(jnp.maximum(square, 1e-30))
+
+
 def widest(offs_ref, reach):
     last = offs_ref.shape[0] - 1
     found = last
@@ -61,7 +66,7 @@
     chan_count = len(order)
     spec_refs, (qual_ref, table_ref) = refs[:chan_count], refs[chan_count : chan_count + 2]
     out_refs = refs[chan_count + 2 : chan_count + 4]
-    mag_ref, white_ref, cross_ref, offs_ref, offs_sem = refs[chan_count + 4 :]
+    white_ref, cross_ref, offs_ref, offs_sem = refs[chan_count + 4 :]
     fetch = pltpu.make_async_copy(offs_hbm_ref, offs_ref, offs_sem)
     fetch.start()
     me = where_ref[0]
@@ -76,21 +81,17 @@
     for number, spec_ref in enumerate(spec_refs):
         for row in range(0, band, step):
             real, imag = (spec_ref[part, row : row + step, :].astype(jnp.float32) for part in range(2))
-            square = real * real + imag * imag
-            magnitude = square * lax.rsqrt(jnp.maximum(square, 1e-30))
-            held = slice(number * band + row, number * band + row + step)
-            mag_ref[held, :] = magnitude
-            total += jnp.sum(magnitude.reshape(step // 8, 8, chans), axis=0)
+            total += jnp.sum(magnitude_of(real, imag).reshape(step // 8, 8, chans), axis=0)
     level = jnp.sum(total, axis=0, keepdims=True) * (1.0 / freqs)
     floor = 0.5 * (level + 1e-05)
 
     for number, spec_ref in enumerate(spec_refs):
         for row in range(0, band, step):
             held = slice(number * band + row, number * band + row + step)
-            factor = pl.reciprocal(mag_ref[held, :] + floor, approx=True)
-            for part in range(2):
-                value = spec_ref[part, row : row + step, :].astype(jnp.float32) * factor
-                white_ref[part, held, :] = value.astype(jnp.bfloat16)
+            values = [spec_ref[part, row : row + step, :].astype(jnp.float32) for part in range(2)]
+            factor = pl.reciprocal(magnitude_of(*values) + floor, approx=True)
+            for part, value in enumerate(values):
+                white_ref[part, held, :] = (value * factor).astype(jnp.bfloat16)
 
     lane = lax.broadcasted_iota(jnp.int32, (1, chans), 1)
     line = lax.broadcasted_iota(jnp.int32, (lag_rows, chans), 0)
@@ -372,7 +373,6 @@
         in_specs=[kept, smem] + [vmem] * (chan_count + 2),
         out_specs=[vmem] * 2,
         scratch_shapes=[
-            pltpu.VMEM((freqs, chans), jnp.float32),
             pltpu.VMEM((2, freqs, chans), jnp.bfloat16),
             pltpu.VMEM((offset_count, 2, freqs, chans), jnp.bfloat16),
             pltpu.SMEM(offsets.shape, jnp.int32),

time: 50.5 us -> 50.6 us (level)
  no operation moved by 1% of the time
where the time goes in v32:
time: 50.6 us; the launch traced here: 50.4 us
  waiting for transfers between devices  17.6 us (35%)
  starting transfers between devices  15.8 us (31%)
  blocking collectives  10.2 us (20%)
  Pallas kernels  6.86 us (14%)
    ppermute x14, waiting for transfers between devices, exchange(): lax.ppermute(piece, ('chan', 'tm'), pairs)  17.6 us
    ppermute x14, starting transfers between devices, exchange(): lax.ppermute(piece, ('chan', 'tm'), pairs)  15.8 us
    all_to_all x1, blocking collectives, window_shards(): lax.all_to_all(pieces.reshape(shape), ('chan', 'tm'), 0, 0, tiled=True)  10.2 us
    pallas_call x1, Pallas kernels, window_shards(): pl.pallas_call(functools.partial(window_kernel, chan_order), out_shape=[j...  3.22 us
    pallas_call x2, Pallas kernels, window_shards(): pl.pallas_call(functools.partial(split_kernel, part), out_shape=[jax.Shap...  2.32 us
  transfers between devices with their start and end apart: 14, of which 10 were waited for; matrix products, arithmetic and copies ran while one was open for 0% of the time, Pallas kernels for 2%

profile of v32, /device:TPU:0, one launch (start us, length us, event | category | flops | bytes accessed | tf_op | source)
XLA Modules:
  0.0 50.4 jit_solution(17381356550166822880)
XLA Ops:
  0.0 1.1 %split_windows.2 = (bf16[2,256,128]{2,1,0:T(8,128)(2,1)S(1)}, bf16[2,256,128]{2,1,0:T(8,128)(2,1)S(1)}) custom-call(bf16[2,8,256,128]{3,2,1,0:T(8,128)(2,1)} %spec_ref.3), custom_call_target="tpu_custom_call" | custom-call | tf_op jit(solution)/shard_map/split_windows/pallas_call | solution.py:359
  1.1 4.0 %collective-permute-start = (bf16[2,256,128]{2,1,0:T(8,128)(2,1)S(1)}, bf16[2,256,128]{2,1,0:T(8,128)(2,1)S(1)}, u32[]{:S(2)}, u32[]{:S(2)}) collective-permute-start(bf16[2,256,128]{2,1,0:T(8,128)(2,1)S(1)} %get-tuple-element.23), channel_id=1, source_target_pairs={{0,24},{1,25},{2,26},{3,27},{4,28},{5,29},{6,30},{7,31},{8,16},{9,... | collective-permute-start | bytes 393224 | tf_op jit(solution)/shard_map/ppermute | solution.py:259
  5.0 1.3 %split_windows.3 = (bf16[2,256,128]{2,1,0:T(8,128)(2,1)S(1)}, bf16[2,256,128]{2,1,0:T(8,128)(2,1)S(1)}, bf16[2,256,128]{2,1,0:T(8,128)(2,1)S(1)}, bf16[2,256,128...) custom-call(bf16[2,8,256,128]{3,2,1,0:T(8,128)(2,1)} %spec_ref.3), custom_call_target="tpu_custom_call" | custom-call | tf_op jit(solution)/shard_map/split_windows/pallas_call | solution.py:359
  6.3 1.2 %collective-permute-start.2 = (bf16[2,256,128]{2,1,0:T(8,128)(2,1)S(1)}, bf16[2,256,128]{2,1,0:T(8,128)(2,1)S(1)}, u32[]{:S(2)}, u32[]{:S(2)}) collective-permute-start(bf16[2,256,128]{2,1,0:T(8,128)(2,1)S(1)} %get-tuple-element.25), channel_id=1, source_target_pairs={{0,8},{1,9},{2,10},{3,11},{4,12},{5,13},{6,14},{7,15},{8,0},{9,1},... | collective-permute-start | bytes 393224 | tf_op jit(solution)/shard_map/ppermute | solution.py:259
  7.5 1.5 %collective-permute-start.3 = (bf16[2,256,128]{2,1,0:T(8,128)(2,1)S(1)}, bf16[2,256,128]{2,1,0:T(8,128)(2,1)S(1)}, u32[]{:S(2)}, u32[]{:S(2)}) collective-permute-start(bf16[2,256,128]{2,1,0:T(8,128)(2,1)S(1)} %get-tuple-element.26), channel_id=1, source_target_pairs={{0,16},{1,17},{2,18},{3,19},{4,20},{5,21},{6,22},{7,23},{8,24},{9,... | collective-permute-start | bytes 393224 | tf_op jit(solution)/shard_map/ppermute | solution.py:259
  9.0 0.6 %collective-permute-start.4 = (bf16[2,256,128]{2,1,0:T(8,128)(2,1)S(1)}, bf16[2,256,128]{2,1,0:T(8,128)(2,1)S(1)}, u32[]{:S(2)}, u32[]{:S(2)}) collective-permute-start(bf16[2,256,128]{2,1,0:T(8,128)(2,1)S(1)} %get-tuple-element.27), channel_id=1, source_target_pairs={{0,12},{1,13},{2,14},{3,15},{4,8},{5,9},{6,10},{7,11},{8,4},{9,5},... | collective-permute-start | bytes 393224 | tf_op jit(solution)/shard_map/ppermute | solution.py:259
  9.6 0.6 %collective-permute-start.5 = (bf16[2,256,128]{2,1,0:T(8,128)(2,1)S(1)}, bf16[2,256,128]{2,1,0:T(8,128)(2,1)S(1)}, u32[]{:S(2)}, u32[]{:S(2)}) collective-permute-start(bf16[2,256,128]{2,1,0:T(8,128)(2,1)S(1)} %get-tuple-element.28), channel_id=1, source_target_pairs={{0,20},{1,21},{2,22},{3,23},{4,16},{5,17},{6,18},{7,19},{8,28},{9,... | collective-permute-start | bytes 393224 | tf_op jit(solution)/shard_map/ppermute | solution.py:259
  10.1 1.6 %collective-permute-done.1.refs_1_ = bf16[2,256,128]{2,1,0:T(8,128)(2,1)S(1)} collective-permute-done((bf16[2,256,128]{2,1,0:T(8,128)(2,1)S(1)}, bf16[2,256,128]{2,1,0:T(8,128)(2,1)S(1)}, u32[]{:S(2)}, u32[]{:S(2)}) %collective-permute-start.1) | collective-permute-done | bytes 131104 | tf_op jit(solution)/shard_map/ppermute | solution.py:259
  11.8 3.5 %collective-permute-done.2.refs_2_ = bf16[2,256,128]{2,1,0:T(8,128)(2,1)S(1)} collective-permute-done((bf16[2,256,128]{2,1,0:T(8,128)(2,1)S(1)}, bf16[2,256,128]{2,1,0:T(8,128)(2,1)S(1)}, u32[]{:S(2)}, u32[]{:S(2)}) %collective-permute-start.2) | collective-permute-done | bytes 131104 | tf_op jit(solution)/shard_map/ppermute | solution.py:259
  15.2 1.1 %collective-permute-done.4.refs_4_ = bf16[2,256,128]{2,1,0:T(8,128)(2,1)S(1)} collective-permute-done((bf16[2,256,128]{2,1,0:T(8,128)(2,1)S(1)}, bf16[2,256,128]{2,1,0:T(8,128)(2,1)S(1)}, u32[]{:S(2)}, u32[]{:S(2)}) %collective-permute-start.4) | collective-permute-done | bytes 131104 | tf_op jit(solution)/shard_map/ppermute | solution.py:259
  16.4 0.7 %collective-permute-done.5.refs_5_ = bf16[2,256,128]{2,1,0:T(8,128)(2,1)S(1)} collective-permute-done((bf16[2,256,128]{2,1,0:T(8,128)(2,1)S(1)}, bf16[2,256,128]{2,1,0:T(8,128)(2,1)S(1)}, u32[]{:S(2)}, u32[]{:S(2)}) %collective-permute-start.5) | collective-permute-done | bytes 131104 | tf_op jit(solution)/shard_map/ppermute | solution.py:259
  17.1 3.2 %window_pairs.1 = (s16[4,22,16,128]{3,2,1,0:T(8,128)(2,1)S(1)}, s16[4,22,16,128]{3,2,1,0:T(8,128)(2,1)S(1)}) custom-call(s32[4]{0:T(128)} %offs_hbm_ref.1, s32[1]{0:T(128)} %bitcast.where_ref.core_ref, bf16[2,256,128]{2,1,0:T(8,128)(2,1)S(1)} %collective-permute-done.refs_0_, bf16[2,256,128]{2,1,0:T(8,128)(2,1)S(1)} %collective-permute-done.1.refs_1_, ...), custom_call_target="tpu_custom_call" | custom-call | tf_op jit(solution)/shard_map/window_pairs/pallas_call | solution.py:370
  20.5 1.5 %collective-permute-done.7.far_ref = s16[4,22,16,128]{3,2,1,0:T(8,128)(2,1)S(1)} collective-permute-done((s16[4,22,16,128]{3,2,1,0:T(8,128)(2,1)S(1)}, s16[4,22,16,128]{3,2,1,0:T(8,128)(2,1)S(1)}, u32[]{:S(2)}, u32[]{:S(2)}) %collective-permute-start.7) | collective-permute-done | bytes 360480 | tf_op jit(solution)/shard_map/ppermute | solution.py:259
  22.3 1.6 %collective-permute-start.8 = (s16[22,16,128]{2,1,0:T(8,128)(2,1)S(1)}, s16[22,16,128]{2,1,0:T(8,128)(2,1)S(1)}, u32[]{:S(2)}, u32[]{:S(2)}) collective-permute-start(s16[22,16,128]{2,1,0:T(8,128)(2,1)S(1)} %get-tuple-element.33), channel_id=1, source_target_pairs={{0,16},{1,17},{2,18},{3,19},{4,12},{5,13},{6,14},{7,15},{8,24},{9,... | collective-permute-start | bytes 270344 | tf_op jit(solution)/shard_map/ppermute | solution.py:259
  23.8 1.6 %collective-permute-start.9 = (s16[22,16,128]{2,1,0:T(8,128)(2,1)S(1)}, s16[22,16,128]{2,1,0:T(8,128)(2,1)S(1)}, u32[]{:S(2)}, u32[]{:S(2)}) collective-permute-start(s16[22,16,128]{2,1,0:T(8,128)(2,1)S(1)} %get-tuple-element.34), channel_id=1, source_target_pairs={{0,8},{1,9},{2,10},{3,11},{4,20},{5,21},{6,22},{7,23},{8,0},{9,1},... | collective-permute-start | bytes 270344 | tf_op jit(solution)/shard_map/ppermute | solution.py:259
  25.8 1.7 %collective-permute-done.8.refs_0_ = s16[22,16,128]{2,1,0:T(8,128)(2,1)S(1)} collective-permute-done((s16[22,16,128]{2,1,0:T(8,128)(2,1)S(1)}, s16[22,16,128]{2,1,0:T(8,128)(2,1)S(1)}, u32[]{:S(2)}, u32[]{:S(2)}) %collective-permute-start.8) | collective-permute-done | bytes 90144 | tf_op jit(solution)/shard_map/ppermute | solution.py:259
  27.5 1.7 %collective-permute-done.9.refs_1_ = s16[22,16,128]{2,1,0:T(8,128)(2,1)S(1)} collective-permute-done((s16[22,16,128]{2,1,0:T(8,128)(2,1)S(1)}, s16[22,16,128]{2,1,0:T(8,128)(2,1)S(1)}, u32[]{:S(2)}, u32[]{:S(2)}) %collective-permute-start.9) | collective-permute-done | bytes 90144 | tf_op jit(solution)/shard_map/ppermute | solution.py:259
  29.2 1.6 %collective-permute-done.10.refs_2_ = s16[22,16,128]{2,1,0:T(8,128)(2,1)S(1)} collective-permute-done((s16[22,16,128]{2,1,0:T(8,128)(2,1)S(1)}, s16[22,16,128]{2,1,0:T(8,128)(2,1)S(1)}, u32[]{:S(2)}, u32[]{:S(2)}) %collective-permute-start.10) | collective-permute-done | bytes 90144 | tf_op jit(solution)/shard_map/ppermute | solution.py:259
  31.0 2.7 %collective-permute-start.11 = (s16[7,16,128]{2,1,0:T(8,128)(2,1)S(1)}, s16[7,16,128]{2,1,0:T(8,128)(2,1)S(1)}, u32[]{:S(2)}, u32[]{:S(2)}) collective-permute-start(s16[7,16,128]{2,1,0:T(8,128)(2,1)S(1)} %get-tuple-element.37), channel_id=1, source_target_pairs={{0,2},{1,3},{2,0},{3,1},{4,7},{5,6},{6,5},{7,4},{8,10},{9,11},{10,... | collective-permute-start | bytes 86024 | tf_op jit(solution)/shard_map/ppermute | solution.py:259
  33.6 1.3 %collective-permute-start.12 = (s16[7,16,128]{2,1,0:T(8,128)(2,1)S(1)}, s16[7,16,128]{2,1,0:T(8,128)(2,1)S(1)}, u32[]{:S(2)}, u32[]{:S(2)}) collective-permute-start(s16[7,16,128]{2,1,0:T(8,128)(2,1)S(1)} %get-tuple-element.38), channel_id=1, source_target_pairs={{0,3},{1,2},{2,1},{3,0},{4,5},{5,4},{6,7},{7,6},{8,11},{9,10},{10,... | collective-permute-start | bytes 86024 | tf_op jit(solution)/shard_map/ppermute | solution.py:259
  35.2 0.7 %collective-permute-done.11.refs_0_ = s16[7,16,128]{2,1,0:T(8,128)(2,1)S(1)} collective-permute-done((s16[7,16,128]{2,1,0:T(8,128)(2,1)S(1)}, s16[7,16,128]{2,1,0:T(8,128)(2,1)S(1)}, u32[]{:S(2)}, u32[]{:S(2)}) %collective-permute-start.11) | collective-permute-done | bytes 28704 | tf_op jit(solution)/shard_map/ppermute | solution.py:259
  35.9 3.4 %collective-permute-done.12.refs_1_ = s16[7,16,128]{2,1,0:T(8,128)(2,1)S(1)} collective-permute-done((s16[7,16,128]{2,1,0:T(8,128)(2,1)S(1)}, s16[7,16,128]{2,1,0:T(8,128)(2,1)S(1)}, u32[]{:S(2)}, u32[]{:S(2)}) %collective-permute-start.12) | collective-permute-done | bytes 28704 | tf_op jit(solution)/shard_map/ppermute | solution.py:259
  39.5 10.2 %all_to_all.5 = f32[32,4,128]{2,1,0:T(4,128)S(1)} all-to-all(f32[32,4,128]{2,1,0:T(4,128)S(1)} %bitcast.5), channel_id=1, replica_groups=mesh['chan'=8,'tm'=4] {'chan','tm'}, dimensions={0} | all-to-all | bytes 131072 | tf_op jit(solution)/shard_map/all_to_all | solution.py:410
  49.7 0.8 %place_lags.1 = f32[16,4,256]{2,1,0:T(4,128)} custom-call(f32[8,4,4,128]{3,2,1,0:T(4,128)S(1)} %bitcast.4), custom_call_target="tpu_custom_call" | custom-call | tf_op jit(solution)/shard_map/place_lags/pallas_call | solution.py:411
  (16 shorter events, 1.4 us)
Async XLA Ops:
  0.0 17.1 %copy-start = (bf16[16,2,8,16,128]{4,3,2,1,0:T(8,128)(2,1)S(1)}, bf16[16,2,8,16,128]{4,3,2,1,0:T(8,128)(2,1)}, u32[]{:S(2)}) copy-start(bf16[16,2,8,16,128]{4,3,2,1,0:T(8,128)(2,1)} %constant.11.clone.refs_9_) | copy-start | bytes 3145732
  1.1 8.5 %collective-permute-start = (bf16[2,256,128]{2,1,0:T(8,128)(2,1)S(1)}, bf16[2,256,128]{2,1,0:T(8,128)(2,1)S(1)}, u32[]{:S(2)}, u32[]{:S(2)}) collective-permute-start(bf16[2,256,128]{2,1,0:T(8,128)(2,1)S(1)} %get-tuple-element.23), channel_id=1, source_target_pairs={{0,24},{1,25},{2,26},{3,27},{4,28},{5,29},{6,30},{7,31},{8,16},{9,... | collective-permute-start | bytes 393224 | tf_op jit(solution)/shard_map/ppermute | solution.py:259
  5.0 6.7 %collective-permute-start.1 = (bf16[2,256,128]{2,1,0:T(8,128)(2,1)S(1)}, bf16[2,256,128]{2,1,0:T(8,128)(2,1)S(1)}, u32[]{:S(2)}, u32[]{:S(2)}) collective-permute-start(bf16[2,256,128]{2,1,0:T(8,128)(2,1)S(1)} %get-tuple-element.24), channel_id=1, source_target_pairs={{0,28},{1,29},{2,30},{3,31},{4,24},{5,25},{6,26},{7,27},{8,20},{9,... | collective-permute-start | bytes 393224 | tf_op jit(solution)/shard_map/ppermute | solution.py:259
  6.3 8.9 %collective-permute-start.2 = (bf16[2,256,128]{2,1,0:T(8,128)(2,1)S(1)}, bf16[2,256,128]{2,1,0:T(8,128)(2,1)S(1)}, u32[]{:S(2)}, u32[]{:S(2)}) collective-permute-start(bf16[2,256,128]{2,1,0:T(8,128)(2,1)S(1)} %get-tuple-element.25), channel_id=1, source_target_pairs={{0,8},{1,9},{2,10},{3,11},{4,12},{5,13},{6,14},{7,15},{8,0},{9,1},... | collective-permute-start | bytes 393224 | tf_op jit(solution)/shard_map/ppermute | solution.py:259
  7.5 7.7 %collective-permute-start.3 = (bf16[2,256,128]{2,1,0:T(8,128)(2,1)S(1)}, bf16[2,256,128]{2,1,0:T(8,128)(2,1)S(1)}, u32[]{:S(2)}, u32[]{:S(2)}) collective-permute-start(bf16[2,256,128]{2,1,0:T(8,128)(2,1)S(1)} %get-tuple-element.26), channel_id=1, source_target_pairs={{0,16},{1,17},{2,18},{3,19},{4,20},{5,21},{6,22},{7,23},{8,24},{9,... | collective-permute-start | bytes 393224 | tf_op jit(solution)/shard_map/ppermute | solution.py:259
  9.0 7.4 %collective-permute-start.4 = (bf16[2,256,128]{2,1,0:T(8,128)(2,1)S(1)}, bf16[2,256,128]{2,1,0:T(8,128)(2,1)S(1)}, u32[]{:S(2)}, u32[]{:S(2)}) collective-permute-start(bf16[2,256,128]{2,1,0:T(8,128)(2,1)S(1)} %get-tuple-element.27), channel_id=1, source_target_pairs={{0,12},{1,13},{2,14},{3,15},{4,8},{5,9},{6,10},{7,11},{8,4},{9,5},... | collective-permute-start | bytes 393224 | tf_op jit(solution)/shard_map/ppermute | solution.py:259
  9.6 7.5 %collective-permute-start.5 = (bf16[2,256,128]{2,1,0:T(8,128)(2,1)S(1)}, bf16[2,256,128]{2,1,0:T(8,128)(2,1)S(1)}, u32[]{:S(2)}, u32[]{:S(2)}) collective-permute-start(bf16[2,256,128]{2,1,0:T(8,128)(2,1)S(1)} %get-tuple-element.28), channel_id=1, source_target_pairs={{0,20},{1,21},{2,22},{3,23},{4,16},{5,17},{6,18},{7,19},{8,28},{9,... | collective-permute-start | bytes 393224 | tf_op jit(solution)/shard_map/ppermute | solution.py:259
  11.8 5.3 %collective-permute-start.6 = (bf16[2,256,128]{2,1,0:T(8,128)(2,1)S(1)}, bf16[2,256,128]{2,1,0:T(8,128)(2,1)S(1)}, u32[]{:S(2)}, u32[]{:S(2)}) collective-permute-start(bf16[2,256,128]{2,1,0:T(8,128)(2,1)S(1)} %get-tuple-element.29), channel_id=1, source_target_pairs={{0,4},{1,5},{2,6},{3,7},{4,0},{5,1},{6,2},{7,3},{8,12},{9,13},{10,... | collective-permute-start | bytes 393224 | tf_op jit(solution)/shard_map/ppermute | solution.py:259
  11.8 5.3 %copy-start.1 = (s32[8,128]{1,0:T(8,128)S(1)}, s32[8,128]{1,0:T(8,128)}, u32[]{:S(2)}) copy-start(s32[8,128]{1,0:T(8,128)} %refs_8_.1) | copy-start | bytes 12292
  20.3 1.7 %collective-permute-start.7 = (s16[4,22,16,128]{3,2,1,0:T(8,128)(2,1)S(1)}, s16[4,22,16,128]{3,2,1,0:T(8,128)(2,1)S(1)}, u32[]{:S(2)}, u32[]{:S(2)}) collective-permute-start(s16[4,22,16,128]{3,2,1,0:T(8,128)(2,1)S(1)} %get-tuple-element.32), channel_id=1, source_target_pairs={{0,4},{1,5},{2,6},{3,7},{4,0},{5,1},{6,2},{7,3},{8,12},{9,13},{10,... | collective-permute-start | bytes 1081352 | tf_op jit(solution)/shard_map/ppermute | solution.py:259
  22.3 5.3 %collective-permute-start.8 = (s16[22,16,128]{2,1,0:T(8,128)(2,1)S(1)}, s16[22,16,128]{2,1,0:T(8,128)(2,1)S(1)}, u32[]{:S(2)}, u32[]{:S(2)}) collective-permute-start(s16[22,16,128]{2,1,0:T(8,128)(2,1)S(1)} %get-tuple-element.33), channel_id=1, source_target_pairs={{0,16},{1,17},{2,18},{3,19},{4,12},{5,13},{6,14},{7,15},{8,24},{9,... | collective-permute-start | bytes 270344 | tf_op jit(solution)/shard_map/ppermute | solution.py:259
  23.8 5.4 %collective-permute-start.9 = (s16[22,16,128]{2,1,0:T(8,128)(2,1)S(1)}, s16[22,16,128]{2,1,0:T(8,128)(2,1)S(1)}, u32[]{:S(2)}, u32[]{:S(2)}) collective-permute-start(s16[22,16,128]{2,1,0:T(8,128)(2,1)S(1)} %get-tuple-element.34), channel_id=1, source_target_pairs={{0,8},{1,9},{2,10},{3,11},{4,20},{5,21},{6,22},{7,23},{8,0},{9,1},... | collective-permute-start | bytes 270344 | tf_op jit(solution)/shard_map/ppermute | solution.py:259
  25.4 5.4 %collective-permute-start.10 = (s16[22,16,128]{2,1,0:T(8,128)(2,1)S(1)}, s16[22,16,128]{2,1,0:T(8,128)(2,1)S(1)}, u32[]{:S(2)}, u32[]{:S(2)}) collective-permute-start(s16[22,16,128]{2,1,0:T(8,128)(2,1)S(1)} %get-tuple-element.35), channel_id=1, source_target_pairs={{0,24},{1,25},{2,26},{3,27},{4,28},{5,29},{6,30},{7,31},{8,16},{9,... | collective-permute-start | bytes 270344 | tf_op jit(solution)/shard_map/ppermute | solution.py:259
  31.0 4.9 %collective-permute-start.11 = (s16[7,16,128]{2,1,0:T(8,128)(2,1)S(1)}, s16[7,16,128]{2,1,0:T(8,128)(2,1)S(1)}, u32[]{:S(2)}, u32[]{:S(2)}) collective-permute-start(s16[7,16,128]{2,1,0:T(8,128)(2,1)S(1)} %get-tuple-element.37), channel_id=1, source_target_pairs={{0,2},{1,3},{2,0},{3,1},{4,7},{5,6},{6,5},{7,4},{8,10},{9,11},{10,... | collective-permute-start | bytes 86024 | tf_op jit(solution)/shard_map/ppermute | solution.py:259
  33.6 5.7 %collective-permute-start.12 = (s16[7,16,128]{2,1,0:T(8,128)(2,1)S(1)}, s16[7,16,128]{2,1,0:T(8,128)(2,1)S(1)}, u32[]{:S(2)}, u32[]{:S(2)}) collective-permute-start(s16[7,16,128]{2,1,0:T(8,128)(2,1)S(1)} %get-tuple-element.38), channel_id=1, source_target_pairs={{0,3},{1,2},{2,1},{3,0},{4,5},{5,4},{6,7},{7,6},{8,11},{9,10},{10,... | collective-permute-start | bytes 86024 | tf_op jit(solution)/shard_map/ppermute | solution.py:259
  35.0 4.3 %collective-permute-start.13 = (s16[7,16,128]{2,1,0:T(8,128)(2,1)S(1)}, s16[7,16,128]{2,1,0:T(8,128)(2,1)S(1)}, u32[]{:S(2)}, u32[]{:S(2)}) collective-permute-start(s16[7,16,128]{2,1,0:T(8,128)(2,1)S(1)} %get-tuple-element.39), channel_id=1, source_target_pairs={{0,1},{1,0},{2,3},{3,2},{4,6},{5,7},{6,4},{7,5},{8,9},{9,8},{10,11... | collective-permute-start | bytes 86024 | tf_op jit(solution)/shard_map/ppermute | solution.py:259

commit v33 on v29

--- a/solution.py
+++ b/solution.py
@@ -123,8 +123,11 @@
             cross_ref[number, 1, row : row + step, :] = imag.astype(jnp.bfloat16)
 
     for number, turn in enumerate(turns):
-        both = jnp.concatenate([cross_ref[number, 0], cross_ref[number, 1]], axis=1)
-        sums = jnp.dot(table, both, preferred_element_type=jnp.float32)
+        if number % 2 == 0:
+            taken = range(number, min(number + 2, offset_count))
+            wide = jnp.concatenate([cross_ref[each, part] for each in taken for part in range(2)], axis=1)
+            pair_sums = jnp.dot(table, wide, preferred_element_type=jnp.float32)
+        sums = pair_sums[:, number % 2 * 2 * chans : (number % 2 + 1) * 2 * chans]
         cos_real, sin_real = sums[:half, :chans], sums[half:, :chans]
         cos_imag, sin_imag = sums[:half, chans:], sums[half:, chans:]
         corr = (

time: 50.3 us -> 50.3 us (level)
  no operation moved by 1% of the time
where the time goes in v33:
time: 50.3 us; the launch traced here: 50.2 us
  waiting for transfers between devices  16.9 us (34%)
  starting transfers between devices  16.2 us (32%)
  blocking collectives  10.2 us (20%)
  Pallas kernels  6.78 us (13%)
    ppermute x15, waiting for transfers between devices, exchange(): lax.ppermute(piece, ('chan', 'tm'), pairs)  16.9 us
    ppermute x15, starting transfers between devices, exchange(): lax.ppermute(piece, ('chan', 'tm'), pairs)  16.2 us
    all_to_all x1, blocking collectives, window_shards(): lax.all_to_all(pieces.reshape(shape), ('chan', 'tm'), 0, 0, tiled=True)  10.2 us
    pallas_call x1, Pallas kernels, window_shards(): pl.pallas_call(functools.partial(window_kernel, chan_order), out_shape=[j...  3.14 us
    pallas_call x2, Pallas kernels, window_shards(): pl.pallas_call(functools.partial(split_kernel, part), out_shape=[jax.Shap...  2.32 us
  transfers between devices with their start and end apart: 15, of which 10 were waited for; matrix products, arithmetic and copies ran while one was open for 0% of the time, Pallas kernels for 3%

profile of v33, /device:TPU:0, one launch (start us, length us, event | category | flops | bytes accessed | tf_op | source)
XLA Modules:
  0.0 50.2 jit_solution(15894601164364226565)
XLA Ops:
  0.0 1.1 %split_windows.2 = (bf16[2,256,128]{2,1,0:T(8,128)(2,1)S(1)}, bf16[2,256,128]{2,1,0:T(8,128)(2,1)S(1)}) custom-call(bf16[2,8,256,128]{3,2,1,0:T(8,128)(2,1)} %spec_ref.3), custom_call_target="tpu_custom_call" | custom-call | tf_op jit(solution)/shard_map/split_windows/pallas_call | solution.py:360
  1.1 4.0 %collective-permute-start = (bf16[2,256,128]{2,1,0:T(8,128)(2,1)S(1)}, bf16[2,256,128]{2,1,0:T(8,128)(2,1)S(1)}, u32[]{:S(2)}, u32[]{:S(2)}) collective-permute-start(bf16[2,256,128]{2,1,0:T(8,128)(2,1)S(1)} %get-tuple-element.25), channel_id=1, source_target_pairs={{0,24},{1,25},{2,26},{3,27},{4,28},{5,29},{6,30},{7,31},{8,16},{9,... | collective-permute-start | bytes 393224 | tf_op jit(solution)/shard_map/ppermute | solution.py:260
  5.0 1.3 %split_windows.3 = (bf16[2,256,128]{2,1,0:T(8,128)(2,1)S(1)}, bf16[2,256,128]{2,1,0:T(8,128)(2,1)S(1)}, bf16[2,256,128]{2,1,0:T(8,128)(2,1)S(1)}, bf16[2,256,128...) custom-call(bf16[2,8,256,128]{3,2,1,0:T(8,128)(2,1)} %spec_ref.3), custom_call_target="tpu_custom_call" | custom-call | tf_op jit(solution)/shard_map/split_windows/pallas_call | solution.py:360
  6.3 1.2 %collective-permute-start.2 = (bf16[2,256,128]{2,1,0:T(8,128)(2,1)S(1)}, bf16[2,256,128]{2,1,0:T(8,128)(2,1)S(1)}, u32[]{:S(2)}, u32[]{:S(2)}) collective-permute-start(bf16[2,256,128]{2,1,0:T(8,128)(2,1)S(1)} %get-tuple-element.27), channel_id=1, source_target_pairs={{0,8},{1,9},{2,10},{3,11},{4,12},{5,13},{6,14},{7,15},{8,0},{9,1},... | collective-permute-start | bytes 393224 | tf_op jit(solution)/shard_map/ppermute | solution.py:260
  7.5 1.5 %collective-permute-start.3 = (bf16[2,256,128]{2,1,0:T(8,128)(2,1)S(1)}, bf16[2,256,128]{2,1,0:T(8,128)(2,1)S(1)}, u32[]{:S(2)}, u32[]{:S(2)}) collective-permute-start(bf16[2,256,128]{2,1,0:T(8,128)(2,1)S(1)} %get-tuple-element.28), channel_id=1, source_target_pairs={{0,16},{1,17},{2,18},{3,19},{4,20},{5,21},{6,22},{7,23},{8,24},{9,... | collective-permute-start | bytes 393224 | tf_op jit(solution)/shard_map/ppermute | solution.py:260
  9.0 0.6 %collective-permute-start.4 = (bf16[2,256,128]{2,1,0:T(8,128)(2,1)S(1)}, bf16[2,256,128]{2,1,0:T(8,128)(2,1)S(1)}, u32[]{:S(2)}, u32[]{:S(2)}) collective-permute-start(bf16[2,256,128]{2,1,0:T(8,128)(2,1)S(1)} %get-tuple-element.29), channel_id=1, source_target_pairs={{0,12},{1,13},{2,14},{3,15},{4,8},{5,9},{6,10},{7,11},{8,4},{9,5},... | collective-permute-start | bytes 393224 | tf_op jit(solution)/shard_map/ppermute | solution.py:260
  9.6 0.6 %collective-permute-start.5 = (bf16[2,256,128]{2,1,0:T(8,128)(2,1)S(1)}, bf16[2,256,128]{2,1,0:T(8,128)(2,1)S(1)}, u32[]{:S(2)}, u32[]{:S(2)}) collective-permute-start(bf16[2,256,128]{2,1,0:T(8,128)(2,1)S(1)} %get-tuple-element.30), channel_id=1, source_target_pairs={{0,20},{1,21},{2,22},{3,23},{4,16},{5,17},{6,18},{7,19},{8,28},{9,... | collective-permute-start | bytes 393224 | tf_op jit(solution)/shard_map/ppermute | solution.py:260
  10.1 1.6 %collective-permute-done.1.refs_1_ = bf16[2,256,128]{2,1,0:T(8,128)(2,1)S(1)} collective-permute-done((bf16[2,256,128]{2,1,0:T(8,128)(2,1)S(1)}, bf16[2,256,128]{2,1,0:T(8,128)(2,1)S(1)}, u32[]{:S(2)}, u32[]{:S(2)}) %collective-permute-start.1) | collective-permute-done | bytes 131104 | tf_op jit(solution)/shard_map/ppermute | solution.py:260
  11.8 3.5 %collective-permute-done.2.refs_2_ = bf16[2,256,128]{2,1,0:T(8,128)(2,1)S(1)} collective-permute-done((bf16[2,256,128]{2,1,0:T(8,128)(2,1)S(1)}, bf16[2,256,128]{2,1,0:T(8,128)(2,1)S(1)}, u32[]{:S(2)}, u32[]{:S(2)}) %collective-permute-start.2) | collective-permute-done | bytes 131104 | tf_op jit(solution)/shard_map/ppermute | solution.py:260
  15.2 1.1 %collective-permute-done.4.refs_4_ = bf16[2,256,128]{2,1,0:T(8,128)(2,1)S(1)} collective-permute-done((bf16[2,256,128]{2,1,0:T(8,128)(2,1)S(1)}, bf16[2,256,128]{2,1,0:T(8,128)(2,1)S(1)}, u32[]{:S(2)}, u32[]{:S(2)}) %collective-permute-start.4) | collective-permute-done | bytes 131104 | tf_op jit(solution)/shard_map/ppermute | solution.py:260
  16.4 0.7 %collective-permute-done.5.refs_5_ = bf16[2,256,128]{2,1,0:T(8,128)(2,1)S(1)} collective-permute-done((bf16[2,256,128]{2,1,0:T(8,128)(2,1)S(1)}, bf16[2,256,128]{2,1,0:T(8,128)(2,1)S(1)}, u32[]{:S(2)}, u32[]{:S(2)}) %collective-permute-start.5) | collective-permute-done | bytes 131104 | tf_op jit(solution)/shard_map/ppermute | solution.py:260
  17.1 3.1 %window_pairs.1 = (s16[2,22,16,128]{3,2,1,0:T(8,128)(2,1)S(1)}, s16[2,22,16,128]{3,2,1,0:T(8,128)(2,1)S(1)}, s16[2,22,16,128]{3,2,1,0:T(8,128)(2,1)S(1)}, s16[2,22,16,128]{3,2,1,0:T(8,128)(2,1)S(1)}) custom-call(s32[4]{0:T(128)} %offs_hbm_ref.1, s32[1]{0:T(128)} %bitcast.where_ref.core_ref, bf16[2,256,128]{2,1,0:T(8,128)(2,1)S(1)} %collective-permute-done.refs_0_, ...), custom_call_target="tpu_custom_call" | custom-call | tf_op jit(solution)/shard_map/window_pairs/pallas_call | solution.py:371
  20.8 0.9 %collective-permute-done.7.far_ref = s16[2,22,16,128]{3,2,1,0:T(8,128)(2,1)S(1)} collective-permute-done((s16[2,22,16,128]{3,2,1,0:T(8,128)(2,1)S(1)}, s16[2,22,16,128]{3,2,1,0:T(8,128)(2,1)S(1)}, u32[]{:S(2)}, u32[]{:S(2)}) %collective-permute-start.7) | collective-permute-done | bytes 180256 | tf_op jit(solution)/shard_map/ppermute | solution.py:260
  21.8 1.6 %collective-permute-start.8 = (s16[22,16,128]{2,1,0:T(8,128)(2,1)S(1)}, s16[22,16,128]{2,1,0:T(8,128)(2,1)S(1)}, u32[]{:S(2)}, u32[]{:S(2)}) collective-permute-start(s16[22,16,128]{2,1,0:T(8,128)(2,1)S(1)} %get-tuple-element.35), channel_id=1, source_target_pairs={{0,16},{1,17},{2,18},{3,19},{4,12},{5,13},{6,14},{7,15},{8,24},{9,... | collective-permute-start | bytes 270344 | tf_op jit(solution)/shard_map/ppermute | solution.py:260
  23.4 1.6 %collective-permute-start.9 = (s16[22,16,128]{2,1,0:T(8,128)(2,1)S(1)}, s16[22,16,128]{2,1,0:T(8,128)(2,1)S(1)}, u32[]{:S(2)}, u32[]{:S(2)}) collective-permute-start(s16[22,16,128]{2,1,0:T(8,128)(2,1)S(1)} %get-tuple-element.36), channel_id=1, source_target_pairs={{0,8},{1,9},{2,10},{3,11},{4,20},{5,21},{6,22},{7,23},{8,0},{9,1},... | collective-permute-start | bytes 270344 | tf_op jit(solution)/shard_map/ppermute | solution.py:260
  25.6 1.5 %collective-permute-done.8.refs_0_ = s16[22,16,128]{2,1,0:T(8,128)(2,1)S(1)} collective-permute-done((s16[22,16,128]{2,1,0:T(8,128)(2,1)S(1)}, s16[22,16,128]{2,1,0:T(8,128)(2,1)S(1)}, u32[]{:S(2)}, u32[]{:S(2)}) %collective-permute-start.8) | collective-permute-done | bytes 90144 | tf_op jit(solution)/shard_map/ppermute | solution.py:260
  27.1 1.5 %collective-permute-done.9.refs_1_ = s16[22,16,128]{2,1,0:T(8,128)(2,1)S(1)} collective-permute-done((s16[22,16,128]{2,1,0:T(8,128)(2,1)S(1)}, s16[22,16,128]{2,1,0:T(8,128)(2,1)S(1)}, u32[]{:S(2)}, u32[]{:S(2)}) %collective-permute-start.9) | collective-permute-done | bytes 90144 | tf_op jit(solution)/shard_map/ppermute | solution.py:260
  28.6 1.9 %collective-permute-done.11.refs_2_ = s16[22,16,128]{2,1,0:T(8,128)(2,1)S(1)} collective-permute-done((s16[22,16,128]{2,1,0:T(8,128)(2,1)S(1)}, s16[22,16,128]{2,1,0:T(8,128)(2,1)S(1)}, u32[]{:S(2)}, u32[]{:S(2)}) %collective-permute-start.11) | collective-permute-done | bytes 90144 | tf_op jit(solution)/shard_map/ppermute | solution.py:260
  30.7 2.7 %collective-permute-start.12 = (s16[7,16,128]{2,1,0:T(8,128)(2,1)S(1)}, s16[7,16,128]{2,1,0:T(8,128)(2,1)S(1)}, u32[]{:S(2)}, u32[]{:S(2)}) collective-permute-start(s16[7,16,128]{2,1,0:T(8,128)(2,1)S(1)} %get-tuple-element.41), channel_id=1, source_target_pairs={{0,2},{1,3},{2,0},{3,1},{4,7},{5,6},{6,5},{7,4},{8,10},{9,11},{10,... | collective-permute-start | bytes 86024 | tf_op jit(solution)/shard_map/ppermute | solution.py:260
  33.4 1.3 %collective-permute-start.13 = (s16[7,16,128]{2,1,0:T(8,128)(2,1)S(1)}, s16[7,16,128]{2,1,0:T(8,128)(2,1)S(1)}, u32[]{:S(2)}, u32[]{:S(2)}) collective-permute-start(s16[7,16,128]{2,1,0:T(8,128)(2,1)S(1)} %get-tuple-element.42), channel_id=1, source_target_pairs={{0,3},{1,2},{2,1},{3,0},{4,5},{5,4},{6,7},{7,6},{8,11},{9,10},{10,... | collective-permute-start | bytes 86024 | tf_op jit(solution)/shard_map/ppermute | solution.py:260
  34.9 0.7 %collective-permute-done.12.refs_0_ = s16[7,16,128]{2,1,0:T(8,128)(2,1)S(1)} collective-permute-done((s16[7,16,128]{2,1,0:T(8,128)(2,1)S(1)}, s16[7,16,128]{2,1,0:T(8,128)(2,1)S(1)}, u32[]{:S(2)}, u32[]{:S(2)}) %collective-permute-start.12) | collective-permute-done | bytes 28704 | tf_op jit(solution)/shard_map/ppermute | solution.py:260
  35.7 3.4 %collective-permute-done.13.refs_1_ = s16[7,16,128]{2,1,0:T(8,128)(2,1)S(1)} collective-permute-done((s16[7,16,128]{2,1,0:T(8,128)(2,1)S(1)}, s16[7,16,128]{2,1,0:T(8,128)(2,1)S(1)}, u32[]{:S(2)}, u32[]{:S(2)}) %collective-permute-start.13) | collective-permute-done | bytes 28704 | tf_op jit(solution)/shard_map/ppermute | solution.py:260
  39.2 10.2 %all_to_all.5 = f32[32,4,128]{2,1,0:T(4,128)S(1)} all-to-all(f32[32,4,128]{2,1,0:T(4,128)S(1)} %bitcast.5), channel_id=1, replica_groups=mesh['chan'=8,'tm'=4] {'chan','tm'}, dimensions={0} | all-to-all | bytes 131072 | tf_op jit(solution)/shard_map/all_to_all | solution.py:414
  49.4 0.8 %place_lags.1 = f32[16,4,256]{2,1,0:T(4,128)} custom-call(f32[8,4,4,128]{3,2,1,0:T(4,128)S(1)} %bitcast.4), custom_call_target="tpu_custom_call" | custom-call | tf_op jit(solution)/shard_map/place_lags/pallas_call | solution.py:415
  (19 shorter events, 1.9 us)
Async XLA Ops:
  0.0 17.1 %copy-start = (bf16[16,2,8,16,128]{4,3,2,1,0:T(8,128)(2,1)S(1)}, bf16[16,2,8,16,128]{4,3,2,1,0:T(8,128)(2,1)}, u32[]{:S(2)}) copy-start(bf16[16,2,8,16,128]{4,3,2,1,0:T(8,128)(2,1)} %constant.11.clone.refs_9_) | copy-start | bytes 3145732
  1.1 8.5 %collective-permute-start = (bf16[2,256,128]{2,1,0:T(8,128)(2,1)S(1)}, bf16[2,256,128]{2,1,0:T(8,128)(2,1)S(1)}, u32[]{:S(2)}, u32[]{:S(2)}) collective-permute-start(bf16[2,256,128]{2,1,0:T(8,128)(2,1)S(1)} %get-tuple-element.25), channel_id=1, source_target_pairs={{0,24},{1,25},{2,26},{3,27},{4,28},{5,29},{6,30},{7,31},{8,16},{9,... | collective-permute-start | bytes 393224 | tf_op jit(solution)/shard_map/ppermute | solution.py:260
  5.0 6.7 %collective-permute-start.1 = (bf16[2,256,128]{2,1,0:T(8,128)(2,1)S(1)}, bf16[2,256,128]{2,1,0:T(8,128)(2,1)S(1)}, u32[]{:S(2)}, u32[]{:S(2)}) collective-permute-start(bf16[2,256,128]{2,1,0:T(8,128)(2,1)S(1)} %get-tuple-element.26), channel_id=1, source_target_pairs={{0,28},{1,29},{2,30},{3,31},{4,24},{5,25},{6,26},{7,27},{8,20},{9,... | collective-permute-start | bytes 393224 | tf_op jit(solution)/shard_map/ppermute | solution.py:260
  6.3 8.9 %collective-permute-start.2 = (bf16[2,256,128]{2,1,0:T(8,128)(2,1)S(1)}, bf16[2,256,128]{2,1,0:T(8,128)(2,1)S(1)}, u32[]{:S(2)}, u32[]{:S(2)}) collective-permute-start(bf16[2,256,128]{2,1,0:T(8,128)(2,1)S(1)} %get-tuple-element.27), channel_id=1, source_target_pairs={{0,8},{1,9},{2,10},{3,11},{4,12},{5,13},{6,14},{7,15},{8,0},{9,1},... | collective-permute-start | bytes 393224 | tf_op jit(solution)/shard_map/ppermute | solution.py:260
  7.5 7.7 %collective-permute-start.3 = (bf16[2,256,128]{2,1,0:T(8,128)(2,1)S(1)}, bf16[2,256,128]{2,1,0:T(8,128)(2,1)S(1)}, u32[]{:S(2)}, u32[]{:S(2)}) collective-permute-start(bf16[2,256,128]{2,1,0:T(8,128)(2,1)S(1)} %get-tuple-element.28), channel_id=1, source_target_pairs={{0,16},{1,17},{2,18},{3,19},{4,20},{5,21},{6,22},{7,23},{8,24},{9,... | collective-permute-start | bytes 393224 | tf_op jit(solution)/shard_map/ppermute | solution.py:260
  9.0 7.4 %collective-permute-start.4 = (bf16[2,256,128]{2,1,0:T(8,128)(2,1)S(1)}, bf16[2,256,128]{2,1,0:T(8,128)(2,1)S(1)}, u32[]{:S(2)}, u32[]{:S(2)}) collective-permute-start(bf16[2,256,128]{2,1,0:T(8,128)(2,1)S(1)} %get-tuple-element.29), channel_id=1, source_target_pairs={{0,12},{1,13},{2,14},{3,15},{4,8},{5,9},{6,10},{7,11},{8,4},{9,5},... | collective-permute-start | bytes 393224 | tf_op jit(solution)/shard_map/ppermute | solution.py:260
  9.6 7.5 %collective-permute-start.5 = (bf16[2,256,128]{2,1,0:T(8,128)(2,1)S(1)}, bf16[2,256,128]{2,1,0:T(8,128)(2,1)S(1)}, u32[]{:S(2)}, u32[]{:S(2)}) collective-permute-start(bf16[2,256,128]{2,1,0:T(8,128)(2,1)S(1)} %get-tuple-element.30), channel_id=1, source_target_pairs={{0,20},{1,21},{2,22},{3,23},{4,16},{5,17},{6,18},{7,19},{8,28},{9,... | collective-permute-start | bytes 393224 | tf_op jit(solution)/shard_map/ppermute | solution.py:260
  11.8 5.3 %collective-permute-start.6 = (bf16[2,256,128]{2,1,0:T(8,128)(2,1)S(1)}, bf16[2,256,128]{2,1,0:T(8,128)(2,1)S(1)}, u32[]{:S(2)}, u32[]{:S(2)}) collective-permute-start(bf16[2,256,128]{2,1,0:T(8,128)(2,1)S(1)} %get-tuple-element.31), channel_id=1, source_target_pairs={{0,4},{1,5},{2,6},{3,7},{4,0},{5,1},{6,2},{7,3},{8,12},{9,13},{10,... | collective-permute-start | bytes 393224 | tf_op jit(solution)/shard_map/ppermute | solution.py:260
  11.8 5.3 %copy-start.1 = (s32[8,128]{1,0:T(8,128)S(1)}, s32[8,128]{1,0:T(8,128)}, u32[]{:S(2)}) copy-start(s32[8,128]{1,0:T(8,128)} %refs_8_.1) | copy-start | bytes 12292
  20.2 1.5 %collective-permute-start.7 = (s16[2,22,16,128]{3,2,1,0:T(8,128)(2,1)S(1)}, s16[2,22,16,128]{3,2,1,0:T(8,128)(2,1)S(1)}, u32[]{:S(2)}, u32[]{:S(2)}) collective-permute-start(s16[2,22,16,128]{3,2,1,0:T(8,128)(2,1)S(1)} %get-tuple-element.34), channel_id=1, source_target_pairs={{0,4},{1,5},{2,6},{3,7},{4,0},{5,1},{6,2},{7,3},{8,12},{9,13},{10,... | collective-permute-start | bytes 540680 | tf_op jit(solution)/shard_map/ppermute | solution.py:260
  20.4 4.6 %collective-permute-start.10 = (s16[2,22,16,128]{3,2,1,0:T(8,128)(2,1)S(1)}, s16[2,22,16,128]{3,2,1,0:T(8,128)(2,1)S(1)}, u32[]{:S(2)}, u32[]{:S(2)}) collective-permute-start(s16[2,22,16,128]{3,2,1,0:T(8,128)(2,1)S(1)} %get-tuple-element.38), channel_id=1, source_target_pairs={{0,4},{1,5},{2,6},{3,7},{4,0},{5,1},{6,2},{7,3},{8,12},{9,13},{10,... | collective-permute-start | bytes 540680 | tf_op jit(solution)/shard_map/ppermute | solution.py:260
  21.8 5.3 %collective-permute-start.8 = (s16[22,16,128]{2,1,0:T(8,128)(2,1)S(1)}, s16[22,16,128]{2,1,0:T(8,128)(2,1)S(1)}, u32[]{:S(2)}, u32[]{:S(2)}) collective-permute-start(s16[22,16,128]{2,1,0:T(8,128)(2,1)S(1)} %get-tuple-element.35), channel_id=1, source_target_pairs={{0,16},{1,17},{2,18},{3,19},{4,12},{5,13},{6,14},{7,15},{8,24},{9,... | collective-permute-start | bytes 270344 | tf_op jit(solution)/shard_map/ppermute | solution.py:260
  23.4 5.2 %collective-permute-start.9 = (s16[22,16,128]{2,1,0:T(8,128)(2,1)S(1)}, s16[22,16,128]{2,1,0:T(8,128)(2,1)S(1)}, u32[]{:S(2)}, u32[]{:S(2)}) collective-permute-start(s16[22,16,128]{2,1,0:T(8,128)(2,1)S(1)} %get-tuple-element.36), channel_id=1, source_target_pairs={{0,8},{1,9},{2,10},{3,11},{4,20},{5,21},{6,22},{7,23},{8,0},{9,1},... | collective-permute-start | bytes 270344 | tf_op jit(solution)/shard_map/ppermute | solution.py:260
  25.1 5.5 %collective-permute-start.11 = (s16[22,16,128]{2,1,0:T(8,128)(2,1)S(1)}, s16[22,16,128]{2,1,0:T(8,128)(2,1)S(1)}, u32[]{:S(2)}, u32[]{:S(2)}) collective-permute-start(s16[22,16,128]{2,1,0:T(8,128)(2,1)S(1)} %get-tuple-element.39), channel_id=1, source_target_pairs={{0,24},{1,25},{2,26},{3,27},{4,28},{5,29},{6,30},{7,31},{8,16},{9,... | collective-permute-start | bytes 270344 | tf_op jit(solution)/shard_map/ppermute | solution.py:260
  30.7 4.9 %collective-permute-start.12 = (s16[7,16,128]{2,1,0:T(8,128)(2,1)S(1)}, s16[7,16,128]{2,1,0:T(8,128)(2,1)S(1)}, u32[]{:S(2)}, u32[]{:S(2)}) collective-permute-start(s16[7,16,128]{2,1,0:T(8,128)(2,1)S(1)} %get-tuple-element.41), channel_id=1, source_target_pairs={{0,2},{1,3},{2,0},{3,1},{4,7},{5,6},{6,5},{7,4},{8,10},{9,11},{10,... | collective-permute-start | bytes 86024 | tf_op jit(solution)/shard_map/ppermute | solution.py:260
  33.4 5.7 %collective-permute-start.13 = (s16[7,16,128]{2,1,0:T(8,128)(2,1)S(1)}, s16[7,16,128]{2,1,0:T(8,128)(2,1)S(1)}, u32[]{:S(2)}, u32[]{:S(2)}) collective-permute-start(s16[7,16,128]{2,1,0:T(8,128)(2,1)S(1)} %get-tuple-element.42), channel_id=1, source_target_pairs={{0,3},{1,2},{2,1},{3,0},{4,5},{5,4},{6,7},{7,6},{8,11},{9,10},{10,... | collective-permute-start | bytes 86024 | tf_op jit(solution)/shard_map/ppermute | solution.py:260
  34.7 4.3 %collective-permute-start.14 = (s16[7,16,128]{2,1,0:T(8,128)(2,1)S(1)}, s16[7,16,128]{2,1,0:T(8,128)(2,1)S(1)}, u32[]{:S(2)}, u32[]{:S(2)}) collective-permute-start(s16[7,16,128]{2,1,0:T(8,128)(2,1)S(1)} %get-tuple-element.43), channel_id=1, source_target_pairs={{0,1},{1,0},{2,3},{3,2},{4,6},{5,7},{6,4},{7,5},{8,9},{9,8},{10,11... | collective-permute-start | bytes 86024 | tf_op jit(solution)/shard_map/ppermute | solution.py:260
